TPU v7x, 32 devices: a whole 2x2x4 slice. The times are simulated.
32 devices in a mesh: fsdp: 4 (over z), ctx: 4 (over x, core), tp: 2 (over y).
Axes of the slice: x: 2, y: 2, z: 4, core: 2. Of those that a mesh axis runs over, the one named last changes fastest.
Arguments:
- inputs: float32 [4, 640, 1024], P('fsdp', 'ctx'), may hold values from -6 to 6
- lengths: int32 [4, 4], P('fsdp'), may hold values from 1 to 160, 513 in all within a row
- cotangent: float32 [4, 640, 1024], P('fsdp', 'ctx'), may hold values from -6 to 6
- norm_gains: bfloat16 [2, 2, 1024], P(None, None, 'fsdp'), may hold values from 0.5 to 1.5
- shifts: bfloat16 [2, 4, 1024], P(None, None, 'fsdp'), may hold values from -2 to 2
- qv_bias: bfloat16 [2, 2, 16, 64], P(None, None, 'tp', 'fsdp'), may hold values from -3 to 3
- fc1_bias: bfloat16 [2, 2, 2048], P(None, 'tp', 'fsdp'), may hold values from -3 to 3
- w_qkv: bfloat16 [2, 3, 1024, 1024], P(None, None, 'fsdp', 'tp'), may hold values from -1 to 1
- w_out: bfloat16 [2, 1024, 1024], P(None, 'tp', 'fsdp'), may hold values from -0.375 to 0.375
- w_fc1: bfloat16 [2, 1024, 4096], P(None, 'fsdp', 'tp'), may hold values from -0.1875 to 0.1875
- w_fc2: bfloat16 [2, 4096, 1024], P(None, 'tp', 'fsdp'), may hold values from -0.09375 to 0.09375
Outputs:
- outputs: float32 [4, 640, 1024], P('fsdp', 'ctx')
- grad_inputs: float32 [4, 640, 1024], P('fsdp', 'ctx')
- grad_gains: float32 [2, 2, 1024], P(None, None, 'fsdp')
- grad_shifts: float32 [2, 4, 1024], P(None, None, 'fsdp')
- grad_qv_bias: float32 [2, 2, 16, 64], P(None, None, 'tp', 'fsdp')
- grad_fc1_bias: float32 [2, 2, 2048], P(None, 'tp', 'fsdp')
- grad_w_qkv: float32 [2, 3, 1024, 1024], P(None, None, 'fsdp', 'tp')
- grad_w_out: float32 [2, 1024, 1024], P(None, 'tp', 'fsdp')
- grad_w_fc1: float32 [2, 1024, 4096], P(None, 'fsdp', 'tp')
- grad_w_fc2: float32 [2, 4096, 1024], P(None, 'tp', 'fsdp')
Inputs may be any that keep to these rules, and one draw needn't show every extreme that they name: Each image's 4 block lengths sum to 513; block c holds the image's next tokens in order, the class token first in block 0; rows of a block past its length are padding; some block of every image holds exactly 160.
All inputs are finite; a program needn't handle non-finite values.
Results may differ from a plain program's by a relative error of at most 0.017.
Values may be sent and summed in bfloat16 or wider, within the bound.
No kernel may reach another device: no remote copies, remote signals or barrier semaphores. Data moves between devices by JAX's collectives and lax.ppermute only.
A program may use at most 256 MiB of HBM per device.

v0:
```python
import math

import jax
import jax.numpy as jnp
from jax import lax
from jax.sharding import PartitionSpec as P

NORM_EPSILON = 1e-06
MASK_FILL = -1e30
ROOT_HALF = 0.7071067811865476
INV_ROOT_TAU = 0.3989422804014327


def norm_forward(values, gain, shift):
    center = values - jnp.mean(values, axis=-1, keepdims=True)
    inverse = lax.rsqrt(jnp.mean(center * center, axis=-1, keepdims=True) + NORM_EPSILON)
    normed = center * inverse
    return (normed * gain + shift, normed, inverse)


def norm_backward(upstream, normed, inverse, gain):
    scaled = upstream * gain
    result = inverse * (
        scaled
        - jnp.mean(scaled, axis=-1, keepdims=True)
        - normed * jnp.mean(scaled * normed, axis=-1, keepdims=True)
    )
    return (result, jnp.sum(upstream * normed, axis=0), jnp.sum(upstream, axis=0))


def gelu_parts(hidden):
    normal_cdf = 0.5 * (1.0 + lax.erf(hidden * ROOT_HALF))
    density = jnp.exp(-0.5 * hidden * hidden) * INV_ROOT_TAU
    return (hidden * normal_cdf, normal_cdf + hidden * density)


def pick_block(local_rows):
    for factor in (4, 2, 1):
        return factor * local_rows
    return local_rows


def per_device(
    inputs, lengths, cotangent, norm_gains, shifts, qv_bias, fc1_bias, w_qkv, w_out, w_fc1, w_fc2
):
    bf16 = jnp.bfloat16
    f32 = jnp.float32
    depth = w_qkv.shape[0]
    local_rows = inputs.shape[1]
    heads_here = qv_bias.shape[2]
    head_dim = qv_bias.shape[3] * lax.axis_size("fsdp")
    score_scale = 1.0 / math.sqrt(head_dim)
    ctx_count = lax.axis_size("ctx")
    block_lens = lengths[0]
    place = lax.axis_index("ctx")
    ctx_ids = jnp.arange(ctx_count, dtype=jnp.int32)
    own_length = jnp.sum(jnp.where(ctx_ids == place, block_lens, 0))
    row_mask = (jnp.arange(local_rows, dtype=jnp.int32) < own_length).astype(f32)[:, None]
    stream = inputs[0]

    def key_usable(first_row, row_count):
        positions = first_row + jnp.arange(row_count, dtype=jnp.int32)
        source = positions // local_rows
        bounds = jnp.sum(
            jnp.where(source[:, None] == ctx_ids[None, :], block_lens[None, :], 0), axis=1
        )
        return positions - source * local_rows < bounds

    def split_heads(matrix):
        return matrix.reshape(local_rows, heads_here, head_dim).transpose(1, 0, 2)

    def join_heads(tensor):
        return tensor.transpose(1, 0, 2).reshape(local_rows, heads_here * head_dim)

    saved_all = []
    for layer_index in range(depth):
        params = (
            lax.all_gather(norm_gains[layer_index], "fsdp", axis=1, tiled=True),
            lax.all_gather(shifts[layer_index], "fsdp", axis=1, tiled=True),
            lax.all_gather(qv_bias[layer_index], "fsdp", axis=2, tiled=True),
            lax.all_gather(fc1_bias[layer_index], "fsdp", axis=1, tiled=True),
            lax.all_gather(w_qkv[layer_index], "fsdp", axis=1, tiled=True),
            lax.all_gather(w_out[layer_index], "fsdp", axis=1, tiled=True),
            lax.all_gather(w_fc1[layer_index], "fsdp", axis=0, tiled=True),
            lax.all_gather(w_fc2[layer_index], "fsdp", axis=1, tiled=True),
        )
        gain_pair = params[0].astype(f32)
        shift_set = params[1].astype(f32)
        qv_pair = params[2].astype(f32).reshape(2, -1)
        fc1_row = params[3].astype(f32)[0]
        weights = params[4]
        out_proj = params[5]
        fc1_proj = params[6]
        fc2_proj = params[7]
        first, normed_one, inverse_one = norm_forward(stream, gain_pair[0], shift_set[0])
        first_b = first.astype(bf16)
        queries = (jnp.dot(first_b, weights[0], preferred_element_type=f32) + qv_pair[0]).astype(
            bf16
        )
        keys_here = jnp.dot(first_b, weights[1], preferred_element_type=f32).astype(bf16)
        values_here = (
            jnp.dot(first_b, weights[2], preferred_element_type=f32) + qv_pair[1]
        ).astype(bf16)
        query_heads = split_heads(queries)

        def tile_scores(key_tile, first_row, key_block):
            usable = key_usable(first_row, key_block)
            scores = (
                jnp.einsum("hqd,khd->hqk", query_heads, key_tile, preferred_element_type=f32)
                * score_scale
            )
            return jnp.where(usable[None, None, :], scores, MASK_FILL)

        def fold_stats(running, key_piece):
            row_count = key_piece.shape[0]
            key_block = pick_block(local_rows)
            block_count = row_count // key_block
            key_tiles = key_piece.reshape(block_count, key_block, heads_here, head_dim)

            def fold_one_tile(state, element):
                key_tile, tile_number = element
                highest, denominator = state
                scores = tile_scores(key_tile, tile_number * key_block, key_block)
                new_high = jnp.maximum(highest, jnp.max(scores, axis=-1))
                denominator = denominator * jnp.exp(highest - new_high) + jnp.sum(
                    jnp.exp(scores - new_high[..., None]), axis=-1
                )
                return ((new_high, denominator), None)

            running, _ = lax.scan(
                fold_one_tile, running, (key_tiles, jnp.arange(block_count, dtype=jnp.int32))
            )
            return running

        def make_fold_out(log_norm, weighted, pieces):
            key_piece, value_piece = pieces
            row_count = key_piece.shape[0]
            key_block = pick_block(local_rows)
            block_count = row_count // key_block
            key_tiles = key_piece.reshape(block_count, key_block, heads_here, head_dim)
            value_tiles = value_piece.reshape(block_count, key_block, heads_here, head_dim)

            def make_one_tile(state, element):
                key_tile, value_tile, tile_number = element
                scores = tile_scores(key_tile, tile_number * key_block, key_block)
                soft = jnp.exp(scores - log_norm[..., None]).astype(bf16)
                state = state + jnp.einsum(
                    "hqk,khd->hqd", soft, value_tile, preferred_element_type=f32
                )
                return (state, None)

            weighted, _ = lax.scan(
                make_one_tile,
                weighted,
                (key_tiles, value_tiles, jnp.arange(block_count, dtype=jnp.int32)),
            )
            return weighted

        start_stats = (
            jnp.full((heads_here, local_rows), MASK_FILL, f32),
            jnp.zeros((heads_here, local_rows), f32),
        )
        start_weighted = jnp.zeros((heads_here, local_rows, head_dim), f32)
        highest, denominator = fold_stats(
            start_stats, lax.all_gather(keys_here, "ctx", axis=0, tiled=True)
        )
        log_norm = highest + jnp.log(denominator)
        weighted = make_fold_out(
            log_norm,
            start_weighted,
            (
                lax.all_gather(keys_here, "ctx", axis=0, tiled=True),
                lax.all_gather(values_here, "ctx", axis=0, tiled=True),
            ),
        )
        attended_b = join_heads(weighted).astype(bf16)
        middle = (
            stream
            + lax.psum(jnp.dot(attended_b, out_proj, preferred_element_type=f32), "tp")
            + shift_set[2]
        )
        second, normed_two, inverse_two = norm_forward(middle, gain_pair[1], shift_set[1])
        second_b = second.astype(bf16)
        pre = jnp.dot(second_b, fc1_proj, preferred_element_type=f32) + fc1_row
        activated, slope = gelu_parts(pre)
        activated_b = activated.astype(bf16)
        output = (
            middle
            + lax.psum(jnp.dot(activated_b, fc2_proj, preferred_element_type=f32), "tp")
            + shift_set[3]
        )
        saved = (
            params,
            normed_one,
            inverse_one,
            first_b,
            queries,
            keys_here,
            values_here,
            None,
            attended_b,
            log_norm,
            normed_two,
            inverse_two,
            second_b,
            slope,
            activated_b,
        )
        stream, saved = (output, saved)
        saved_all.append(saved)
    outputs = (stream * row_mask)[None]
    upstream = cotangent[0] * row_mask
    grads_all = [None] * depth
    for layer_index in reversed(range(depth)):
        (
            backward_params,
            backward_normed_one,
            backward_inverse_one,
            backward_first_b,
            backward_queries,
            backward_keys_here,
            backward_values_here,
            backward_kept_keys,
            backward_attended_b,
            backward_log_norm,
            backward_normed_two,
            backward_inverse_two,
            backward_second_b,
            backward_slope,
            backward_activated_b,
        ) = saved_all[layer_index]
        backward_gain_pair = backward_params[0].astype(f32)
        backward_weights = backward_params[4]
        backward_out_proj = backward_params[5]
        backward_fc1_proj = backward_params[6]
        backward_fc2_proj = backward_params[7]
        upstream_b = upstream.astype(bf16)
        grad_fc2 = jnp.dot(backward_activated_b.T, upstream_b, preferred_element_type=f32)
        grad_c2 = jnp.sum(upstream, axis=0)
        grad_pre = (
            jnp.dot(upstream_b, backward_fc2_proj.T, preferred_element_type=f32) * backward_slope
        )
        grad_pre_b = grad_pre.astype(bf16)
        grad_fc1 = jnp.dot(backward_second_b.T, grad_pre_b, preferred_element_type=f32)
        grad_c1 = jnp.sum(grad_pre, axis=0)[None, :]
        grad_second = lax.psum(
            jnp.dot(grad_pre_b, backward_fc1_proj.T, preferred_element_type=f32), "tp"
        )
        back_two, grad_g2, grad_b2 = norm_backward(
            grad_second, backward_normed_two, backward_inverse_two, backward_gain_pair[1]
        )
        grad_middle = upstream + back_two
        middle_b = grad_middle.astype(bf16)
        grad_wo = jnp.dot(backward_attended_b.T, middle_b, preferred_element_type=f32)
        grad_bo = jnp.sum(grad_middle, axis=0)
        backward_grad_attended = jnp.dot(
            middle_b, backward_out_proj.T, preferred_element_type=f32
        ).astype(bf16)
        backward_row_dots = jnp.sum(
            split_heads(backward_grad_attended).astype(f32)
            * split_heads(backward_attended_b).astype(f32),
            axis=-1,
        )
        backward_keys_all = lax.all_gather(backward_keys_here, "ctx", axis=0, tiled=True)
        backward_values_all = lax.all_gather(backward_values_here, "ctx", axis=0, tiled=True)
        attention_log_norm = backward_log_norm
        row_dots = backward_row_dots
        row_total = backward_keys_all.shape[0]
        attention_key_block = pick_block(local_rows)
        attention_block_count = row_total // attention_key_block
        attention_key_tiles = backward_keys_all.reshape(
            attention_block_count, attention_key_block, heads_here, head_dim
        )
        attention_value_tiles = backward_values_all.reshape(
            attention_block_count, attention_key_block, heads_here, head_dim
        )
        attention_query_heads = split_heads(backward_queries)
        grad_heads = split_heads(backward_grad_attended)

        def attention_one_tile(grad_query, element):
            key_tile, value_tile, tile_number = element
            usable = key_usable(tile_number * attention_key_block, attention_key_block)
            scores = (
                jnp.einsum(
                    "hqd,khd->hqk", attention_query_heads, key_tile, preferred_element_type=f32
                )
                * score_scale
            )
            scores = jnp.where(usable[None, None, :], scores, MASK_FILL)
            soft_f = jnp.exp(scores - attention_log_norm[..., None])
            grad_soft = jnp.einsum(
                "hqd,khd->hqk", grad_heads, value_tile, preferred_element_type=f32
            )
            grad_scores = (soft_f * (grad_soft - row_dots[..., None])).astype(bf16)
            grad_query = (
                grad_query
                + jnp.einsum("hqk,khd->hqd", grad_scores, key_tile, preferred_element_type=f32)
                * score_scale
            )
            grad_value_tile = jnp.einsum(
                "hqk,hqd->khd", soft_f.astype(bf16), grad_heads, preferred_element_type=f32
            )
            grad_key_tile = (
                jnp.einsum(
                    "hqk,hqd->khd", grad_scores, attention_query_heads, preferred_element_type=f32
                )
                * score_scale
            )
            return (
                grad_query,
                (
                    grad_key_tile.reshape(attention_key_block, -1),
                    grad_value_tile.reshape(attention_key_block, -1),
                ),
            )

        grad_query, tiles_out = lax.scan(
            attention_one_tile,
            jnp.zeros((heads_here, local_rows, head_dim), f32),
            (
                attention_key_tiles,
                attention_value_tiles,
                jnp.arange(attention_block_count, dtype=jnp.int32),
            ),
        )
        grad_q = join_heads(grad_query)
        grad_key_all = tiles_out[0].reshape(row_total, -1)
        grad_value_all = tiles_out[1].reshape(row_total, -1)
        grad_k = lax.psum_scatter(grad_key_all, "ctx", scatter_dimension=0, tiled=True)
        grad_v = lax.psum_scatter(grad_value_all, "ctx", scatter_dimension=0, tiled=True)
        grad_q_b = grad_q.astype(bf16)
        grad_k_b = grad_k.astype(bf16)
        grad_v_b = grad_v.astype(bf16)
        grad_qkv = jnp.stack(
            [
                jnp.dot(backward_first_b.T, grad_q_b, preferred_element_type=f32),
                jnp.dot(backward_first_b.T, grad_k_b, preferred_element_type=f32),
                jnp.dot(backward_first_b.T, grad_v_b, preferred_element_type=f32),
            ]
        )
        grad_first = lax.psum(
            jnp.dot(grad_q_b, backward_weights[0].T, preferred_element_type=f32)
            + jnp.dot(grad_k_b, backward_weights[1].T, preferred_element_type=f32)
            + jnp.dot(grad_v_b, backward_weights[2].T, preferred_element_type=f32),
            "tp",
        )
        back_one, grad_g1, grad_b1 = norm_backward(
            grad_first, backward_normed_one, backward_inverse_one, backward_gain_pair[0]
        )
        grad_qv = jnp.stack([jnp.sum(grad_q, axis=0), jnp.sum(grad_v, axis=0)]).reshape(
            2, heads_here, head_dim
        )
        grads = (
            jnp.stack([grad_g1, grad_g2]),
            jnp.stack([grad_b1, grad_b2, grad_bo, grad_c2]),
            grad_qv,
            grad_c1,
            grad_qkv,
            grad_wo,
            grad_fc1,
            grad_fc2,
        )
        upstream = grad_middle + back_one
        grads_all[layer_index] = grads
    grad_inputs = (upstream * row_mask)[None]
    stacked = tuple(
        (
            jnp.stack([grads_all[layer_index][member] for layer_index in range(depth)])
            for member in range(8)
        )
    )
    owned_all = (
        lax.psum_scatter(stacked[0], "fsdp", scatter_dimension=2, tiled=True),
        lax.psum_scatter(stacked[1], "fsdp", scatter_dimension=2, tiled=True),
        lax.psum_scatter(stacked[2], "fsdp", scatter_dimension=3, tiled=True),
        lax.psum_scatter(stacked[3], "fsdp", scatter_dimension=2, tiled=True),
        lax.psum_scatter(stacked[4], "fsdp", scatter_dimension=2, tiled=True),
        lax.psum_scatter(stacked[5], "fsdp", scatter_dimension=2, tiled=True),
        lax.psum_scatter(stacked[6], "fsdp", scatter_dimension=1, tiled=True),
        lax.psum_scatter(stacked[7], "fsdp", scatter_dimension=2, tiled=True),
    )
    reduced = lax.psum(owned_all, "ctx")
    return (
        outputs,
        grad_inputs,
        reduced[0],
        reduced[1],
        reduced[2],
        reduced[3],
        reduced[4],
        reduced[5],
        reduced[6],
        reduced[7],
    )


def solution(mesh):
    placed = (
        P("fsdp", "ctx", None),
        P("fsdp", None),
        P("fsdp", "ctx", None),
        P(None, None, "fsdp"),
        P(None, None, "fsdp"),
        P(None, None, "tp", "fsdp"),
        P(None, "tp", "fsdp"),
        P(None, None, "fsdp", "tp"),
        P(None, "tp", "fsdp"),
        P(None, "fsdp", "tp"),
        P(None, "tp", "fsdp"),
    )
    return jax.shard_map(
        per_device,
        mesh=mesh,
        in_specs=placed,
        out_specs=(
            P("fsdp", "ctx", None),
            P("fsdp", "ctx", None),
            P(None, None, "fsdp"),
            P(None, None, "fsdp"),
            P(None, None, "tp", "fsdp"),
            P(None, "tp", "fsdp"),
            P(None, None, "fsdp", "tp"),
            P(None, "tp", "fsdp"),
            P(None, "fsdp", "tp"),
            P(None, "tp", "fsdp"),
        ),
        check_vma=False,
    )
```

profile of v0, /device:TPU:9, one launch (start us, length us, event | category | flops | bytes accessed | tf_op | source)
XLA Modules:
  0.0 2141.7 jit_solution(5475744276707945433)
XLA Ops:
  11.1 9.5 all-gather.1
  21.8 6.5 all-gather
  29.4 10.5 all-gather.3
  40.6 32.4 %all-gather.25.cloned.1.call-done = bf16[1,3,1024,512]{3,2,1,0:T(8,128)(2,1)} async-done(((bf16[1,3,256,512]{3,2,1,0:T(8,128)(2,1)}), bf16[1,3,1024,512]{3,2,1,0:T(8,128)(2,1)}) %all-gather.25.cloned.1.call-update) | async-done | bytes 3145744 | tf_op jit(solution)/shard_map/all_gather | solution.py:82
  74.6 8.5 all_gather.71
  87.4 8.0 all_gather.70
  112.3 10.2 all-gather.6
  122.5 16.6 all-reduce.12.cloned.1.call-done
  140.6 78.9 %all-gather.29.cloned.1.call-done = bf16[1,1024,2048]{2,1,0:T(8,128)(2,1)} async-done(((bf16[1,256,2048]{2,1,0:T(8,128)(2,1)}), bf16[1,1024,2048]{2,1,0:T(8,128)(2,1)}) %all-gather.29.cloned.1.call-update) | async-done | bytes 4194320 | tf_op jit(solution)/shard_map/all_gather | solution.py:84
  222.6 77.7 %all-gather.31.cloned.1.call-done = bf16[1,2048,1024]{2,1,0:T(8,128)(2,1)} async-done(((bf16[1,2048,256]{2,1,0:T(8,128)(2,1)}), bf16[1,2048,1024]{2,1,0:T(8,128)(2,1)}) %all-gather.31.cloned.1.call-update) | async-done | bytes 4194320 | tf_op jit(solution)/shard_map/all_gather | solution.py:85
  305.8 10.3 all-gather.9
  316.7 8.4 all-gather.8
  325.3 9.1 all-gather.11
  339.0 60.6 %all-gather.33.cloned.1.call-done = bf16[1,3,1024,512]{3,2,1,0:T(8,128)(2,1)} async-done(((bf16[1,3,256,512]{3,2,1,0:T(8,128)(2,1)}), bf16[1,3,1024,512]{3,2,1,0:T(8,128)(2,1)}) %all-gather.33.cloned.1.call-update) | async-done | bytes 3145744 | tf_op jit(solution)/shard_map/all_gather | solution.py:82
  401.1 8.5 all_gather.81
  415.0 8.5 all_gather.80
  433.4 9.9 all-gather.14
  445.8 20.0 all-reduce.16.cloned.1.call-done
  468.4 77.7 %all-gather.37.cloned.1.call-done = bf16[1,1024,2048]{2,1,0:T(8,128)(2,1)} async-done(((bf16[1,256,2048]{2,1,0:T(8,128)(2,1)}), bf16[1,1024,2048]{2,1,0:T(8,128)(2,1)}) %all-gather.37.cloned.1.call-update) | async-done | bytes 4194320 | tf_op jit(solution)/shard_map/all_gather | solution.py:84
  546.1 4.2 fusion.24
  550.2 76.3 %all-gather.39.cloned.1.call-done = bf16[1,2048,1024]{2,1,0:T(8,128)(2,1)} async-done(((bf16[1,2048,256]{2,1,0:T(8,128)(2,1)}), bf16[1,2048,1024]{2,1,0:T(8,128)(2,1)}) %all-gather.39.cloned.1.call-update) | async-done | bytes 4194320 | tf_op jit(solution)/shard_map/all_gather | solution.py:85
  626.5 5.1 fusion.121
  634.9 32.6 %all-reduce.18.cloned.1.call-done = f32[160,1024]{1,0:T(8,128)} async-done(((f32[160,1024]{1,0:T(8,128)}), f32[160,1024]{1,0:T(8,128)}) %all-reduce.18.cloned.1.call-update) | async-done | bytes 655376 | tf_op jit(solution)/shard_map/psum | solution.py:246
  683.8 3.9 fusion.77
  697.3 13.3 reduce-scatter.37.cloned.1.call-done
  712.3 27.9 %reduce-scatter.39.cloned.1.call-done = f32[160,512]{1,0:T(8,128)} async-done(((f32[640,512]{1,0:T(8,128)}), f32[160,512]{1,0:T(8,128)}) %reduce-scatter.39.cloned.1.call-update) | async-done | bytes 327696
  746.7 31.6 %all-reduce.20.cloned.1.call-done = f32[160,1024]{1,0:T(8,128)} async-done(((f32[160,1024]{1,0:T(8,128)}), f32[160,1024]{1,0:T(8,128)}) %all-reduce.20.cloned.1.call-update) | async-done | bytes 655376 | tf_op jit(solution)/shard_map/psum | solution.py:341
  782.5 4.8 fusion.122
  790.6 31.5 %all-reduce.22.cloned.1.call-done = f32[160,1024]{1,0:T(8,128)} async-done(((f32[160,1024]{1,0:T(8,128)}), f32[160,1024]{1,0:T(8,128)}) %all-reduce.22.cloned.1.call-update) | async-done | bytes 655376 | tf_op jit(solution)/shard_map/psum | solution.py:246
  833.9 3.9 fusion.80
  840.8 4.4 fusion.2
  849.0 11.6 reduce-scatter.41.cloned.1.call-done
  862.4 27.9 %reduce-scatter.43.cloned.1.call-done = f32[160,512]{1,0:T(8,128)} async-done(((f32[640,512]{1,0:T(8,128)}), f32[160,512]{1,0:T(8,128)}) %reduce-scatter.43.cloned.1.call-update) | async-done | bytes 327696
  911.9 12.1 pad_maximum_fusion.2
  928.0 6.0 pad_maximum_fusion
  938.9 6.1 pad_maximum_fusion.1
  948.4 5.6 bitcast_reduce_fusion
  961.1 61.4 %reduce-scatter.31.cloned.1.call-done = f32[2,512,256]{2,1,0:T(8,128)} async-done(((f32[2,512,1024]{2,1,0:T(8,128)}), f32[2,512,256]{2,1,0:T(8,128)}) %reduce-scatter.31.cloned.1.call-update) | async-done | bytes 1048592 | tf_op jit(solution)/shard_map/reduce_scatter | solution.py:378
  1022.5 214.8 %reduce-scatter.29.cloned.1.call-done = f32[2,3,256,512]{3,2,1,0:T(8,128)} async-done(((f32[2,3,1024,512]{3,2,1,0:T(8,128)}), f32[2,3,256,512]{3,2,1,0:T(8,128)}) %reduce-scatter.29.cloned.1.call-update) | async-done | bytes 3145744 | tf_op jit(solution)/shard_map/reduce_scatter | solution.py:377
  1237.3 280.6 %reduce-scatter.33.cloned.1.call-done = f32[2,256,2048]{2,1,0:T(8,128)} async-done(((f32[2,1024,2048]{2,1,0:T(8,128)}), f32[2,256,2048]{2,1,0:T(8,128)}) %reduce-scatter.33.cloned.1.call-update) | async-done | bytes 4194320 | tf_op jit(solution)/shard_map/reduce_scatter | solution.py:379
  1517.9 283.6 %reduce-scatter.35.cloned.1.call-done = f32[2,2048,256]{2,1,0:T(8,128)} async-done(((f32[2,2048,1024]{2,1,0:T(8,128)}), f32[2,2048,256]{2,1,0:T(8,128)}) %reduce-scatter.35.cloned.1.call-update) | async-done | bytes 4194320 | tf_op jit(solution)/shard_map/reduce_scatter | solution.py:380
  1801.5 31.6 %reduce-scatter.51.cloned.1.call-done = f32[512,2]{1,0:T(8,128)} async-done(((f32[2048,2]{1,0:T(8,128)}), f32[512,2]{1,0:T(8,128)}) %reduce-scatter.51.cloned.1.call-update) | async-done | bytes 4112
  1834.9 16.4 reduce-scatter.49.cloned.1.call-done
  1854.6 19.7 reduce-scatter.45.cloned.1.call-done
  1875.5 21.4 reduce-scatter.47.cloned.1.call-done
  1898.1 11.9 all-reduce
  1910.1 213.4 %all-reduce.24.cloned.1.call-done = (f32[2,3,256,512]{3,2,1,0:T(8,128)}, f32[2,512,256]{2,1,0:T(8,128)}, f32[2,256,2048]{2,1,0:T(8,128)}, f32[2,2048,256]{2,1,0:T(8,128)}) async-done(((f32[2,3,256,512]{3,2,1,0:T(8,128)}, f32[2,512,256]{2,1,0:T(8,128)}, f32[2,256,2048]{2,1,0:T(8,128)}, f32[2,2048,256]{2,1,0:T(8,128)}), (f32[2,3,256,512]{3,2,1,0:T(8,128)}, f32[2,512,256]{2,1,0:T(8,128)}, ...) | async-done | bytes 12582928 | tf_op jit(solution)/shard_map/psum | solution.py:382
  2123.5 4.3 copy.119
  (441 shorter events, 185.9 us)
Async XLA Ops:
  7.2 65.8 %all-gather.25.cloned.1.call-start = ((), (), s32[]{:S(2)}) async-start(), calls=%async_computation.22 | async-start | bytes 3932160 | tf_op jit(solution)/shard_map/all_gather | solution.py:82
  10.1 92.8 %all-gather.27.cloned.1.call-start = ((), (), s32[]{:S(2)}) async-start(), calls=%async_computation.23 | async-start | bytes 1310720 | tf_op jit(solution)/shard_map/all_gather | solution.py:83
  11.0 128.1 %all-reduce.12.cloned.1.call-start = ((), (), s32[]{:S(2)}) async-start(), calls=%async_computation.12 | async-start | bytes 1310720 | tf_op jit(solution)/shard_map/psum | solution.py:179
  28.3 55.1 %copy-start.57 = (f32[1,1,1024]{2,1,0:T(1,128)}, f32[1,1,1024]{2,1,0:T(1,128)S(1)}, u32[]{:S(2)}) copy-start(f32[1,1,1024]{2,1,0:T(1,128)S(1)} %get-tuple-element.240) | copy-start | bytes 12292
  40.2 57.4 %copy-start.69 = (pred[640]{0:T(1024)(128)(4,1)}, pred[640]{0:T(1024)(128)(4,1)S(1)}, u32[]{:S(2)}) copy-start(pred[640]{0:T(1024)(128)(4,1)S(1)} %fusion.85) | copy-start | bytes 1924
  40.6 45.1 %copy-start.46 = (bf16[160,1024]{1,0:T(8,128)(2,1)}, bf16[160,1024]{1,0:T(8,128)(2,1)S(1)}, u32[]{:S(2)}) copy-start(bf16[160,1024]{1,0:T(8,128)(2,1)S(1)} %fusion.58) | copy-start | bytes 983044
  105.4 114.1 %all-gather.29.cloned.1.call-start = ((), (), s32[]{:S(2)}) async-start(), calls=%async_computation.24 | async-start | bytes 5242880 | tf_op jit(solution)/shard_map/all_gather | solution.py:84
  108.6 191.8 %all-gather.31.cloned.1.call-start = ((), (), s32[]{:S(2)}) async-start(), calls=%async_computation.25 | async-start | bytes 5242880 | tf_op jit(solution)/shard_map/all_gather | solution.py:85
  111.6 225.2 %all-reduce.14.cloned.1.call-start = ((), (), s32[]{:S(2)}) async-start(), calls=%async_computation.13 | async-start | bytes 1310720 | tf_op jit(solution)/shard_map/psum | solution.py:189
  140.4 82.2 %copy-start.64 = (f32[160]{0:T(256)}, f32[160]{0:T(256)S(1)}, u32[]{:S(2)}) copy-start(f32[160]{0:T(256)S(1)} %broadcast_multiply_fusion.10) | copy-start | bytes 1924
  140.6 163.6 %copy-start.73 = (f32[160]{0:T(256)}, f32[160]{0:T(256)S(1)}, u32[]{:S(2)}) copy-start(f32[160]{0:T(256)S(1)} %add_rsqrt_fusion.2) | copy-start | bytes 1924
  222.6 81.7 %copy-start.3 = (f32[160,2048]{1,0:T(8,128)}, f32[160,2048]{1,0:T(8,128)S(1)}, u32[]{:S(2)}) copy-start(f32[160,2048]{1,0:T(8,128)S(1)} %fusion.18) | copy-start | bytes 3932164
  222.6 94.1 %copy-start.102 = (bf16[1,2,256]{2,1,0:T(2,128)(2,1)S(1)}, bf16[1,2,256]{2,1,0:T(2,128)(2,1)}, u32[]{:S(2)}) copy-start(bf16[1,2,256]{2,1,0:T(2,128)(2,1)} %get-tuple-element.245) | copy-start | bytes 3076
  222.6 102.5 %copy-start.87 = (bf16[1,2,8,16]{3,2,1,0:T(8,128)(2,1)S(1)}, bf16[1,2,8,16]{3,2,1,0:T(8,128)(2,1)}, u32[]{:S(2)}) copy-start(bf16[1,2,8,16]{3,2,1,0:T(8,128)(2,1)} %get-tuple-element.231) | copy-start | bytes 1540
  222.6 114.3 %copy-start.85 = (f32[1,1,1024]{2,1,0:T(1,128)S(1)}, f32[1,1,1024]{2,1,0:T(1,128)}, u32[]{:S(2)}) copy-start(f32[1,1,1024]{2,1,0:T(1,128)} %get-tuple-element.236) | copy-start | bytes 12292
  304.3 95.3 %all-gather.33.cloned.1.call-start = ((), (), s32[]{:S(2)}) async-start(), calls=%async_computation.26 | async-start | bytes 3932160 | tf_op jit(solution)/shard_map/all_gather | solution.py:82
  305.0 124.5 %all-gather.35.cloned.1.call-start = ((), (), s32[]{:S(2)}) async-start(), calls=%async_computation.27 | async-start | bytes 1310720 | tf_op jit(solution)/shard_map/all_gather | solution.py:83
  305.8 160.0 %all-reduce.16.cloned.1.call-start = ((), (), s32[]{:S(2)}) async-start(), calls=%async_computation.14 | async-start | bytes 1310720 | tf_op jit(solution)/shard_map/psum | solution.py:179
  339.0 74.5 %copy-start.17 = (bf16[160,1024]{1,0:T(8,128)(2,1)}, bf16[160,1024]{1,0:T(8,128)(2,1)S(1)}, u32[]{:S(2)}) copy-start(bf16[160,1024]{1,0:T(8,128)(2,1)S(1)} %add_convert_fusion.2) | copy-start | bytes 983044
  428.5 37.2 %copy-start.34 = (bf16[8,160,64]{1,2,0:T(8,128)(2,1)}, bf16[8,160,64]{1,2,0:T(8,128)(2,1)S(1)}, u32[]{:S(2)}) copy-start(bf16[8,160,64]{1,2,0:T(8,128)(2,1)S(1)} %convolution_convert_fusion) | copy-start | bytes 491524
  428.5 37.2 %copy-start.86 = (f32[1,1,1024]{2,1,0:T(1,128)S(1)}, f32[1,1,1024]{2,1,0:T(1,128)}, u32[]{:S(2)}) copy-start(f32[1,1,1024]{2,1,0:T(1,128)} %get-tuple-element.229) | copy-start | bytes 12292
  432.0 114.1 %all-gather.37.cloned.1.call-start = ((), (), s32[]{:S(2)}) async-start(), calls=%async_computation.28 | async-start | bytes 5242880 | tf_op jit(solution)/shard_map/all_gather | solution.py:84
  432.6 194.0 %all-gather.39.cloned.1.call-start = ((), (), s32[]{:S(2)}) async-start(), calls=%async_computation.29 | async-start | bytes 5242880 | tf_op jit(solution)/shard_map/all_gather | solution.py:85
  433.3 234.2 %all-reduce.18.cloned.1.call-start = ((), (), s32[]{:S(2)}) async-start(), calls=%async_computation.15 | async-start | bytes 1310720 | tf_op jit(solution)/shard_map/psum | solution.py:246
  467.8 158.8 %copy-start.23 = (f32[1,160,1024]{2,1,0:T(8,128)S(1)}, f32[1,160,1024]{2,1,0:T(8,128)}, u32[]{:S(2)}) copy-start(f32[1,160,1024]{2,1,0:T(8,128)} %param.13) | copy-start | bytes 1966084
  631.6 35.9 %copy-start.75 = (f32[160]{0:T(256)S(1)}, f32[160]{0:T(256)}, u32[]{:S(2)}) copy-start(f32[160]{0:T(256)} %add_rsqrt_fusion) | copy-start | bytes 1924
  634.9 75.6 %reduce-scatter.37.cloned.1.call-start = ((), (), s32[]{:S(2)}) async-start(), calls=%async_computation.30 | async-start | bytes 1638400
  671.9 108.6 %copy-start.9 = (f32[160,1024]{1,0:T(8,128)}, f32[160,1024]{1,0:T(8,128)S(1)}, u32[]{:S(2)}) copy-start(f32[160,1024]{1,0:T(8,128)S(1)} %get-tuple-element.179) | copy-start | bytes 1966084
  683.8 56.4 %reduce-scatter.39.cloned.1.call-start = ((), (), s32[]{:S(2)}) async-start(), calls=%async_computation.31 | async-start | bytes 1638400
  690.5 87.8 %all-reduce.20.cloned.1.call-start = ((), (), s32[]{:S(2)}) async-start(), calls=%async_computation.16 | async-start | bytes 1310720 | tf_op jit(solution)/shard_map/psum | solution.py:341
  746.7 75.4 %all-reduce.22.cloned.1.call-start = ((), (), s32[]{:S(2)}) async-start(), calls=%async_computation.17 | async-start | bytes 1310720 | tf_op jit(solution)/shard_map/psum | solution.py:246
  788.1 36.2 %copy-start.15 = (f32[160,1024]{1,0:T(8,128)S(1)}, f32[160,1024]{1,0:T(8,128)}, u32[]{:S(2)}) copy-start(f32[160,1024]{1,0:T(8,128)} %copy-done.14) | copy-start | bytes 1966084
  790.5 37.9 %copy-start.54 = (bf16[640,512]{0,1:T(8,128)(2,1)S(1)}, bf16[640,512]{0,1:T(8,128)(2,1)}, u32[]{:S(2)}) copy-start(bf16[640,512]{0,1:T(8,128)(2,1)} %copy-done.53) | copy-start | bytes 1966084
  790.5 70.0 %reduce-scatter.41.cloned.1.call-start = ((), (), s32[]{:S(2)}) async-start(), calls=%async_computation.32 | async-start | bytes 1638400
  833.8 56.4 %reduce-scatter.43.cloned.1.call-start = ((), (), s32[]{:S(2)}) async-start(), calls=%async_computation.33 | async-start | bytes 1638400
  840.7 114.7 %all-reduce.26.cloned.1.call-start = ((), (), s32[]{:S(2)}) async-start(), calls=%async_computation.39 | async-start | bytes 2621440 | tf_op jit(solution)/shard_map/psum | solution.py:189
  896.7 125.8 %reduce-scatter.31.cloned.1.call-start = ((), (), s32[]{:S(2)}) async-start(), calls=%async_computation.19 | async-start | bytes 5242880 | tf_op jit(solution)/shard_map/reduce_scatter | solution.py:378
  900.9 336.3 %reduce-scatter.29.cloned.1.call-start = ((), (), s32[]{:S(2)}) async-start(), calls=%async_computation.18 | async-start | bytes 15728640 | tf_op jit(solution)/shard_map/reduce_scatter | solution.py:377
  924.1 593.8 %reduce-scatter.33.cloned.1.call-start = ((), (), s32[]{:S(2)}) async-start(), calls=%async_computation.20 | async-start | bytes 20971520 | tf_op jit(solution)/shard_map/reduce_scatter | solution.py:379
  934.1 867.4 %reduce-scatter.35.cloned.1.call-start = ((), (), s32[]{:S(2)}) async-start(), calls=%async_computation.21 | async-start | bytes 20971520 | tf_op jit(solution)/shard_map/reduce_scatter | solution.py:380
  945.0 888.1 %reduce-scatter.51.cloned.1.call-start = ((), (), s32[]{:S(2)}) async-start(), calls=%async_computation.37 | async-start | bytes 1310720
  954.1 897.1 %reduce-scatter.49.cloned.1.call-start = ((), (), s32[]{:S(2)}) async-start(), calls=%async_computation.36 | async-start | bytes 40960
  955.3 919.0 %reduce-scatter.45.cloned.1.call-start = ((), (), s32[]{:S(2)}) async-start(), calls=%async_computation.34 | async-start | bytes 655360
  958.9 938.0 %reduce-scatter.47.cloned.1.call-start = ((), (), s32[]{:S(2)}) async-start(), calls=%async_computation.35 | async-start | bytes 655360
  961.0 1162.5 %all-reduce.24.cloned.1.call-start = ((), (), s32[]{:S(2)}) async-start(), calls=%async_computation.38 | async-start | bytes 25165824 | tf_op jit(solution)/shard_map/psum | solution.py:382
  1801.5 50.6 %copy-start.13 = (f32[160,1024]{1,0:T(8,128)S(1)}, f32[160,1024]{1,0:T(8,128)}, u32[]{:S(2)}) copy-start(f32[160,1024]{1,0:T(8,128)} %copy-done.11) | copy-start | bytes 1966084
  1801.5 50.6 %copy-start.31 = (f32[160,1024]{1,0:T(8,128)S(1)}, f32[160,1024]{1,0:T(8,128)}, u32[]{:S(2)}) copy-start(f32[160,1024]{1,0:T(8,128)} %get-tuple-element.173) | copy-start | bytes 1966084
  1801.5 50.6 %copy-start.94 = (f32[1,1,1024]{2,1,0:T(1,128)S(1)}, f32[1,1,1024]{2,1,0:T(1,128)}, u32[]{:S(2)}) copy-start(f32[1,1,1024]{2,1,0:T(1,128)} %get-tuple-element.227) | copy-start | bytes 12292
  (88 other events, 480.6 us)
Sparse Core Ops, SparseCore 0:
  10.2 62.7 all-gather.24
  75.2 27.7 all-gather.26
  105.8 33.2 all-reduce.11
  141.2 78.2 all-gather.28
  221.5 78.7 all-gather.30
  304.4 32.4 all-reduce.13
  338.5 61.0 all-gather.32
  401.7 27.7 all-gather.34
  432.4 33.2 all-reduce.15
  467.8 78.2 all-gather.36
  547.7 78.7 all-gather.38
  635.0 32.4 all-reduce.17
  683.9 26.5 reduce-scatter.36
  713.6 26.5 reduce-scatter.38
  746.8 31.4 all-reduce.19
  790.6 31.4 all-reduce.21
  834.0 26.5 reduce-scatter.40
  863.7 26.5 reduce-scatter.42
  896.8 45.9 all-reduce.25
  945.6 76.8 reduce-scatter.30
  1024.9 212.3 reduce-scatter.28
  1239.6 278.2 reduce-scatter.32
  1520.4 281.0 reduce-scatter.34
  1804.2 28.8 reduce-scatter.50
  1836.0 15.1 reduce-scatter.48
  1853.9 20.3 reduce-scatter.44
  1877.0 19.8 reduce-scatter.46
  1899.7 223.7 all-reduce.23
where the time goes:
time: 2150 us; the launch traced here: 2140 us
  waiting for transfers between devices  1770 us (82%)
  blocking collectives  120 us (6%)
  matrix products  97 us (5%)
  local copies, waits for them, and re-layouts  75.8 us (4%)
  other arithmetic  61.7 us (3%)
    reduce_scatter x1, waiting for transfers between devices, per_device(): lax.psum_scatter(stacked[7], 'fsdp', scatter_dimension=2, tiled=True)  284 us
    reduce_scatter x1, waiting for transfers between devices, per_device(): lax.psum_scatter(stacked[6], 'fsdp', scatter_dimension=1, tiled=True)  281 us
    reduce_scatter x1, waiting for transfers between devices, per_device(): lax.psum_scatter(stacked[4], 'fsdp', scatter_dimension=2, tiled=True)  215 us
    psum x1, waiting for transfers between devices, per_device(): reduced = lax.psum(owned_all, 'ctx')  213 us
    unnamed x36, waiting for transfers between devices  173 us
    all_gather x2, waiting for transfers between devices, per_device(): lax.all_gather(w_fc1[layer_index], 'fsdp', axis=0, tiled=True)  157 us
    all_gather x2, waiting for transfers between devices, per_device(): lax.all_gather(w_fc2[layer_index], 'fsdp', axis=1, tiled=True)  154 us
    all_gather x2, waiting for transfers between devices, per_device(): lax.all_gather(w_qkv[layer_index], 'fsdp', axis=1, tiled=True)  93 us
  transfers between devices with their start and end apart: 28, of which 27 were waited for; matrix products, arithmetic and copies ran while one was open for 7% of the time, Pallas kernels for 0%

commit v1 on v0

v1 whole, which is shorter than its diff:
```python
import math

import jax
import jax.numpy as jnp
from jax import lax
from jax.sharding import PartitionSpec as P

NORM_EPSILON = 1e-06
MASK_FILL = -1e30
ROOT_HALF = 0.7071067811865476
INV_ROOT_TAU = 0.3989422804014327
GROUP = 4
ORDER = (0, 1, 4, 5, 2, 3, 6, 7)

bf16 = jnp.bfloat16
f32 = jnp.float32


def dot(a, b):
    return lax.dot_general(a, b, (((1,), (0,)), ((), ())), preferred_element_type=f32)


def dot_nt(a, b):
    return lax.dot_general(a, b, (((1,), (1,)), ((), ())), preferred_element_type=f32)


def dot_tn(a, b):
    return lax.dot_general(a, b, (((0,), (0,)), ((), ())), preferred_element_type=f32)


def norm_forward(values, gain, shift):
    center = values - jnp.mean(values, axis=-1, keepdims=True)
    inverse = lax.rsqrt(jnp.mean(center * center, axis=-1, keepdims=True) + NORM_EPSILON)
    normed = center * inverse
    return (normed * gain + shift, normed, inverse)


def norm_backward(upstream, normed, inverse, gain):
    scaled = upstream * gain
    result = inverse * (
        scaled
        - jnp.mean(scaled, axis=-1, keepdims=True)
        - normed * jnp.mean(scaled * normed, axis=-1, keepdims=True)
    )
    return (result, jnp.sum(upstream * normed, axis=0), jnp.sum(upstream, axis=0))


def gelu_parts(hidden):
    normal_cdf = 0.5 * (1.0 + lax.erf(hidden * ROOT_HALF))
    density = jnp.exp(-0.5 * hidden * hidden) * INV_ROOT_TAU
    return (hidden * normal_cdf, normal_cdf + hidden * density)


def per_device(
    inputs, lengths, cotangent, norm_gains, shifts, qv_bias, fc1_bias, w_qkv, w_out, w_fc1, w_fc2
):
    depth = w_qkv.shape[0]
    width_own = w_qkv.shape[2]
    local_rows = inputs.shape[1]
    fsdp = lax.axis_size("fsdp")
    tp = lax.axis_size("tp")
    ctx = lax.axis_size("ctx")
    outer = ctx // GROUP
    own_rows = local_rows // tp
    all_rows = own_rows * tp * GROUP
    half_rows = all_rows // 2
    head_dim = qv_bias.shape[3] * fsdp
    heads = qv_bias.shape[2] // GROUP
    feats = heads * head_dim
    hidden = w_fc1.shape[2] // GROUP
    score_scale = 1.0 / math.sqrt(head_dim)
    c = lax.axis_index("ctx")
    t = lax.axis_index("tp")
    f = lax.axis_index("fsdp")
    ci = c % GROUP
    place = ci * tp + t

    def swap_core(value):
        return lax.ppermute(value, "ctx", [(i, i ^ 1) for i in range(ctx)])

    def swap_x(value):
        return lax.ppermute(value, "ctx", [(i, i ^ 2) for i in range(ctx)])

    def swap_y(value):
        return lax.ppermute(value, "tp", [(i, i ^ 1) for i in range(tp)])

    def swap_xy(value):
        pairs = [
            (i * tp + k, (i ^ 2) * tp + (k ^ 1)) for i in range(ctx) for k in range(tp)
        ]
        return lax.ppermute(value, ("ctx", "tp"), pairs)

    outer_groups = [[o * GROUP + i for o in range(outer)] for i in range(GROUP)]

    def gather_rows(own):
        near = jnp.concatenate([own, swap_y(own), swap_x(own), swap_xy(own)], axis=0)
        return jnp.concatenate([near, swap_core(near)], axis=0)

    def reduce_rows(partial):
        far = swap_core(partial[half_rows:].astype(bf16))
        near = partial[:half_rows] + far.astype(f32)
        near_b = near[own_rows:].astype(bf16)
        got_y = swap_y(near_b[:own_rows])
        got_x = swap_x(near_b[own_rows : 2 * own_rows])
        got_xy = swap_xy(near_b[2 * own_rows :])
        return near[:own_rows] + got_y.astype(f32) + got_x.astype(f32) + got_xy.astype(f32)

    offsets = jnp.arange(own_rows, dtype=jnp.int32)
    marks = []
    for o in range(outer):
        for d in ORDER:
            source = place ^ d
            length = lax.dynamic_index_in_dim(
                lengths[0], o * GROUP + source // tp, 0, keepdims=False
            )
            marks.append((source % tp) * own_rows + offsets < length)
    usable = jnp.concatenate(marks)
    own_length = lax.dynamic_index_in_dim(lengths[0], c, 0, keepdims=False)
    own_first = t * own_rows
    row_mask = (own_first + offsets < own_length).astype(f32)[:, None]

    def own_part(block):
        return lax.dynamic_slice_in_dim(block[0], own_first, own_rows, axis=0)

    def gather_small(value, axis):
        return lax.all_gather(value, "fsdp", axis=axis, tiled=True)

    small = jnp.concatenate([norm_gains, shifts], axis=1)
    small = gather_small(small, 2).astype(f32)
    gains_all, shifts_all = small[:, :2], small[:, 2:]
    qv_own = lax.dynamic_slice_in_dim(qv_bias, ci * heads, heads, axis=2)
    qv_all = gather_small(qv_own, 3).astype(f32).reshape(depth, 2, feats)
    fc1_all = gather_small(fc1_bias, 2)[:, 0]
    fc1_all = lax.dynamic_slice_in_dim(fc1_all, ci * hidden, hidden, axis=1).astype(f32)

    attn_w = []
    mlp_w = []
    for l in range(depth):
        qkv = lax.dynamic_slice_in_dim(w_qkv[l], ci * feats, feats, axis=2)
        out = lax.dynamic_slice_in_dim(w_out[l], ci * feats, feats, axis=0)
        fc1 = lax.dynamic_slice_in_dim(w_fc1[l], ci * hidden, hidden, axis=1)
        fc2 = lax.dynamic_slice_in_dim(w_fc2[l], ci * hidden, hidden, axis=0)
        attn_w.append(gather_small(jnp.concatenate([qkv[0], qkv[1], qkv[2], out.T], axis=1), 0))
        mlp_w.append(gather_small(jnp.concatenate([fc1, fc2.T], axis=1), 0))

    stream = own_part(inputs)
    upstream = own_part(cotangent) * row_mask
    upstream_all = gather_rows(upstream.astype(bf16))

    saved_all = []
    for l in range(depth):
        w_in = attn_w[l][:, : 3 * feats]
        w_o = attn_w[l][:, 3 * feats :]
        w_1 = mlp_w[l][:, :hidden]
        w_2 = mlp_w[l][:, hidden:]
        first, normed_one, inverse_one = norm_forward(stream, gains_all[l, 0], shifts_all[l, 0])
        first_all = gather_rows(first.astype(bf16))
        qkv = dot(first_all, w_in)
        queries = (qkv[:, :feats] + qv_all[l, 0]).astype(bf16)
        keys = qkv[:, feats : 2 * feats].astype(bf16)
        values = (qkv[:, 2 * feats :] + qv_all[l, 1]).astype(bf16)
        if outer > 1:
            keys, values = (
                lax.all_gather(v, "ctx", axis=0, tiled=True, axis_index_groups=outer_groups)
                for v in (keys, values)
            )
        attended = []
        norms = []
        for h in range(heads):
            cols = slice(h * head_dim, (h + 1) * head_dim)
            scores = dot_nt(queries[:, cols], keys[:, cols]) * score_scale
            scores = jnp.where(usable[None, :], scores, MASK_FILL)
            highest = jnp.max(scores, axis=-1, keepdims=True)
            log_norm = highest + jnp.log(
                jnp.sum(jnp.exp(scores - highest), axis=-1, keepdims=True)
            )
            soft = jnp.exp(scores - log_norm).astype(bf16)
            attended.append(dot(soft, values[:, cols]).astype(bf16))
            norms.append(log_norm)
        attended = jnp.concatenate(attended, axis=1)
        middle = stream + reduce_rows(dot_nt(attended, w_o)) + shifts_all[l, 2]
        second, normed_two, inverse_two = norm_forward(middle, gains_all[l, 1], shifts_all[l, 1])
        second_all = gather_rows(second.astype(bf16))
        pre = dot(second_all, w_1) + fc1_all[l]
        activated, slope = gelu_parts(pre)
        activated = activated.astype(bf16)
        stream = middle + reduce_rows(dot_nt(activated, w_2)) + shifts_all[l, 3]
        saved_all.append(
            (
                normed_one,
                inverse_one,
                first_all,
                queries,
                keys,
                values,
                attended,
                norms,
                normed_two,
                inverse_two,
                second_all,
                slope,
                activated,
            )
        )
    outputs_own = stream * row_mask

    small_grads = [None] * depth
    owned = [None] * depth
    for l in reversed(range(depth)):
        (
            normed_one,
            inverse_one,
            first_all,
            queries,
            keys,
            values,
            attended,
            norms,
            normed_two,
            inverse_two,
            second_all,
            slope,
            activated,
        ) = saved_all[l]
        w_in = attn_w[l][:, : 3 * feats]
        w_o = attn_w[l][:, 3 * feats :]
        w_1 = mlp_w[l][:, :hidden]
        w_2 = mlp_w[l][:, hidden:]
        grad_c2 = jnp.sum(upstream, axis=0)
        grad_pre = dot(upstream_all, w_2) * slope
        grad_pre_b = grad_pre.astype(bf16)
        grad_second = reduce_rows(dot_nt(grad_pre_b, w_1))
        grad_c1 = jnp.sum(grad_pre, axis=0)
        mlp_grad = jnp.concatenate(
            [
                dot_tn(second_all, grad_pre_b).astype(bf16),
                dot_tn(upstream_all, activated).astype(bf16),
            ],
            axis=1,
        )
        back_two, grad_g2, grad_b2 = norm_backward(
            grad_second, normed_two, inverse_two, gains_all[l, 1]
        )
        grad_middle = upstream + back_two
        grad_bo = jnp.sum(grad_middle, axis=0)
        middle_all = gather_rows(grad_middle.astype(bf16))
        grad_attended = dot(middle_all, w_o).astype(bf16)
        row_products = grad_attended.astype(f32) * attended.astype(f32)
        grad_q = []
        grad_k = []
        grad_v = []
        for h in range(heads):
            cols = slice(h * head_dim, (h + 1) * head_dim)
            row_dots = jnp.sum(row_products[:, cols], axis=-1, keepdims=True)
            scores = dot_nt(queries[:, cols], keys[:, cols]) * score_scale
            scores = jnp.where(usable[None, :], scores, MASK_FILL)
            soft_f = jnp.exp(scores - norms[h])
            grad_soft = dot_nt(grad_attended[:, cols], values[:, cols])
            grad_scores = (soft_f * (grad_soft - row_dots)).astype(bf16)
            grad_q.append(dot(grad_scores, keys[:, cols]) * score_scale)
            grad_k.append(dot_tn(grad_scores, queries[:, cols]) * score_scale)
            grad_v.append(dot_tn(soft_f.astype(bf16), grad_attended[:, cols]))
        grad_q = jnp.concatenate(grad_q, axis=1)
        grad_k = jnp.concatenate(grad_k, axis=1)
        grad_v = jnp.concatenate(grad_v, axis=1)
        if outer > 1:
            grad_k, grad_v = (
                lax.psum_scatter(
                    v, "ctx", scatter_dimension=0, tiled=True, axis_index_groups=outer_groups
                )
                for v in (grad_k, grad_v)
            )
        grad_qkv = jnp.concatenate([grad_q, grad_k, grad_v], axis=1).astype(bf16)
        grad_first = reduce_rows(dot_nt(grad_qkv, w_in))
        attn_grad = jnp.concatenate(
            [
                dot_tn(first_all, grad_qkv).astype(bf16),
                dot_tn(middle_all, attended).astype(bf16),
            ],
            axis=1,
        )
        grad_qv = jnp.stack([jnp.sum(grad_q, axis=0), jnp.sum(grad_v, axis=0)])
        back_one, grad_g1, grad_b1 = norm_backward(
            grad_first, normed_one, inverse_one, gains_all[l, 0]
        )
        upstream = grad_middle + back_one
        if l > 0:
            upstream_all = gather_rows(upstream.astype(bf16))
        owned_l = []
        for grad in (mlp_grad, attn_grad):
            part = lax.psum_scatter(grad, "fsdp", scatter_dimension=0, tiled=True)
            if outer > 1:
                part = lax.psum(part, "ctx", axis_index_groups=outer_groups)
                inner_groups = [[o * GROUP + i for i in range(GROUP)] for o in range(outer)]
                part = lax.all_gather(part, "ctx", axis=0, axis_index_groups=inner_groups)
            else:
                part = lax.all_gather(part, "ctx", axis=0)
            owned_l.append(part.astype(f32))
        owned[l] = owned_l
        small_grads[l] = (grad_g1, grad_g2, grad_b1, grad_b2, grad_bo, grad_c2, grad_qv, grad_c1)

    grad_inputs_own = upstream * row_mask

    def both_halves(own):
        other = swap_y(own)
        return jnp.where(
            t == 0,
            jnp.concatenate([own, other], axis=0),
            jnp.concatenate([other, own], axis=0),
        )[None]

    outputs = both_halves(outputs_own)
    grad_inputs = both_halves(grad_inputs_own)

    width = width_own * fsdp
    qv_full = jnp.zeros((depth, 2, tp * GROUP, feats), f32)
    qv_full = lax.dynamic_update_slice_in_dim(
        qv_full,
        jnp.stack([small_grads[l][6] for l in range(depth)])[:, :, None, :],
        t * GROUP + ci,
        axis=2,
    )
    c1_full = jnp.zeros((depth, tp * GROUP, hidden), f32)
    c1_full = lax.dynamic_update_slice_in_dim(
        c1_full,
        jnp.stack([small_grads[l][7] for l in range(depth)])[:, None, :],
        t * GROUP + ci,
        axis=1,
    )
    rows = jnp.stack([small_grads[l][k] for l in range(depth) for k in range(6)])
    packed = jnp.concatenate(
        [rows, qv_full.reshape(-1, width), c1_full.reshape(-1, width)], axis=0
    )
    packed = lax.psum(packed, ("fsdp", "ctx", "tp"))
    cut = 6 * depth
    rows = lax.dynamic_slice_in_dim(packed[:cut], f * width_own, width_own, axis=1)
    rows = rows.reshape(depth, 6, width_own)
    qv_count = qv_full.size // width
    qv_full = packed[cut : cut + qv_count].reshape(depth, 2, tp, GROUP * heads, head_dim)
    qv_full = lax.dynamic_index_in_dim(qv_full, t, 2, keepdims=False)
    grad_qv_bias = lax.dynamic_slice_in_dim(
        qv_full, f * (head_dim // fsdp), head_dim // fsdp, axis=3
    )
    c1_full = packed[cut + qv_count :].reshape(depth, tp, GROUP * hidden)
    c1_full = lax.dynamic_slice_in_dim(c1_full, t, 1, axis=1)
    c1_own = GROUP * hidden // fsdp
    grad_fc1_bias = lax.dynamic_slice_in_dim(c1_full, f * c1_own, c1_own, axis=2)

    def weight(l, kind, first, count):
        return owned[l][kind][:, :, first : first + count]

    grad_qkv = []
    grad_out = []
    grad_fc1 = []
    grad_fc2 = []
    for l in range(depth):
        piece = weight(l, 1, 0, 3 * feats).reshape(GROUP, width_own, 3, feats)
        grad_qkv.append(piece.transpose(2, 1, 0, 3).reshape(3, width_own, GROUP * feats))
        piece = weight(l, 1, 3 * feats, feats)
        grad_out.append(piece.transpose(0, 2, 1).reshape(GROUP * feats, width_own))
        piece = weight(l, 0, 0, hidden)
        grad_fc1.append(piece.transpose(1, 0, 2).reshape(width_own, GROUP * hidden))
        piece = weight(l, 0, hidden, hidden)
        grad_fc2.append(piece.transpose(0, 2, 1).reshape(GROUP * hidden, width_own))
    return (
        outputs,
        grad_inputs,
        rows[:, :2],
        rows[:, 2:],
        grad_qv_bias,
        grad_fc1_bias,
        jnp.stack(grad_qkv),
        jnp.stack(grad_out),
        jnp.stack(grad_fc1),
        jnp.stack(grad_fc2),
    )


def solution(mesh):
    rows = P("fsdp", "ctx", None)
    params = (
        P(None, None, "fsdp"),
        P(None, None, "fsdp"),
        P(None, None, "tp", "fsdp"),
        P(None, "tp", "fsdp"),
        P(None, None, "fsdp", "tp"),
        P(None, "tp", "fsdp"),
        P(None, "fsdp", "tp"),
        P(None, "tp", "fsdp"),
    )
    return jax.shard_map(
        per_device,
        mesh=mesh,
        in_specs=(rows, P("fsdp", None), rows) + params,
        out_specs=(rows, rows) + params,
        check_vma=False,
    )
```

time: 2150 us -> 731 us (0.34)
  waiting for transfers between devices: 1770 us -> 345 us
  blocking collectives: 120 us -> 31 us
  starting transfers between devices: 1.79 us -> 84.8 us
  local copies, waits for them, and re-layouts: 75.8 us -> 124 us
  matrix products: 97 us -> 55.1 us
    reduce_scatter x4, waiting for transfers between devices: 840 us -> 75.5 us  [per_device(): part = lax.psum_scatter(grad, 'fsdp', scatter_dimension=0, tiled=True)]
    all_gather x8, waiting for transfers between devices: 408 us -> 61.7 us  [the longest x4 43.9 us: per_device(): part = lax.all_gather(part, 'ctx', axis=0)]
    psum x8 -> x1, waiting for transfers between devices: 348 us -> 115 us  [per_device(): packed = lax.psum(packed, ('fsdp', 'ctx', 'tp'))]
    unnamed x36 -> x13, waiting for transfers between devices: 173 us -> 0.21 us
    ppermute x0 -> x66, waiting for transfers between devices: none -> 92.8 us  [the longest x18 51.5 us: swap_y(): return lax.ppermute(value, 'tp', [(i, i ^ 1) for i in range(tp)])]
    all_gather x12 -> x3, blocking collectives: 108 us -> 31 us  [gather_small(): return lax.all_gather(value, 'fsdp', axis=axis, tiled=True)]
    ppermute x0 -> x66, starting transfers between devices: none -> 72.5 us  [the longest x16 27 us: swap_core(): return lax.ppermute(value, 'ctx', [(i, i ^ 1) for i in range(ctx)])]
    dot_general x48, matrix products: 97 us -> 55.1 us  [the longest x16 24.8 us: dot(): lax.dot_general(a, b, (((1,), (0,)), ((), ())), preferred_element_type=f32)]
  transfers between devices with their start and end apart: 28 -> 79, of which waited for: 27 -> 47; matrix products, arithmetic and copies ran while one was open for 7% -> 22% of each run, Pallas kernels for 0% -> 0%
where the time goes in v1:
time: 731 us; the launch traced here: 720 us
  waiting for transfers between devices  345 us (47%)
  local copies, waits for them, and re-layouts  124 us (17%)
  starting transfers between devices  84.8 us (12%)
  other arithmetic  63.1 us (9%)
  matrix products  55.1 us (8%)
  blocking collectives  31 us (4%)
  between operations  16.5 us (2%)
    psum x1, waiting for transfers between devices, per_device(): packed = lax.psum(packed, ('fsdp', 'ctx', 'tp'))  115 us
    reduce_scatter x4, waiting for transfers between devices, per_device(): part = lax.psum_scatter(grad, 'fsdp', scatter_dimension=0, tiled=True)  75.5 us
    ppermute x18, waiting for transfers between devices, swap_y(): return lax.ppermute(value, 'tp', [(i, i ^ 1) for i in range(tp)])  51.5 us
    all_gather x4, waiting for transfers between devices, per_device(): part = lax.all_gather(part, 'ctx', axis=0)  43.9 us
    unnamed x259, local copies, waits for them, and re-layouts  34.4 us
    all_gather x3, blocking collectives, gather_small(): return lax.all_gather(value, 'fsdp', axis=axis, tiled=True)  31 us
    ppermute x16, starting transfers between devices, swap_core(): return lax.ppermute(value, 'ctx', [(i, i ^ 1) for i in range(ctx)])  27 us
    dot_general x16, matrix products, dot(): lax.dot_general(a, b, (((1,), (0,)), ((), ())), preferred_element_type=f32)  24.8 us
  transfers between devices with their start and end apart: 79, of which 47 were waited for; matrix products, arithmetic and copies ran while one was open for 22% of the time, Pallas kernels for 0%

profile of v1, /device:TPU:9, one launch (start us, length us, event | category | flops | bytes accessed | tf_op | source)
XLA Modules:
  0.0 719.9 jit_solution(17320928590538390528)
XLA Ops:
  10.4 10.5 %all_gather.45 = bf16[2,6,1024]{2,1,0:T(8,128)(2,1)S(1)} all-gather(bf16[2,6,256]{2,1,0:T(8,128)(2,1)S(1)} %pad_maximum_fusion.26), channel_id=1, replica_groups=mesh['fsdp'=4,'ctx'=4,'tp'=2] {'fsdp'}, dimensions={2}, use_global_device_ids=true | all-gather | bytes 30720 | tf_op jit(solution)/shard_map/all_gather | solution.py:126
  41.5 11.0 %all_gather.47 = bf16[2,2,2,64]{2,1,0,3:T(2,128)(2,1)S(1)} all-gather(bf16[2,2,2,16]{2,1,0,3:T(2,128)(2,1)S(1)} %copy.116), channel_id=1, replica_groups=mesh['fsdp'=4,'ctx'=4,'tp'=2] {'fsdp'}, dimensions={3}, use_global_device_ids=true | all-gather | bytes 1280 | tf_op jit(solution)/shard_map/all_gather | solution.py:126
  55.1 6.9 collective-permute-start.3
  92.0 6.8 collective-permute-done.5
  104.2 9.6 %all_gather.49 = bf16[2,1,2048]{2,0,1:T(2,128)(2,1)S(1)} all-gather(bf16[2,1,512]{2,0,1:T(2,128)(2,1)S(1)} %copy-done.110), channel_id=1, replica_groups=mesh['fsdp'=4,'ctx'=4,'tp'=2] {'fsdp'}, dimensions={2}, use_global_device_ids=true | all-gather | bytes 10240 | tf_op jit(solution)/shard_map/all_gather | solution.py:126
  113.8 3.8 collective-permute-start.11
  121.1 10.0 %all-gather.15.cloned.1.call-done = bf16[1024,1024]{1,0:T(8,128)(2,1)} async-done(((bf16[256,1024]{1,0:T(8,128)(2,1)}), bf16[1024,1024]{1,0:T(8,128)(2,1)}) %all-gather.15.cloned.1.call-update) | async-done | bytes 2097168 | tf_op jit(solution)/shard_map/all_gather | solution.py:126
  131.2 3.9 multiply_convert_fusion.5
  151.4 11.6 %all-gather.19.cloned.1.call-start = ((), (), s32[]{:S(2)}) async-start(), calls=%async_computation.7 | async-start | bytes 2621440 | tf_op jit(solution)/shard_map/all_gather | solution.py:126
  168.8 2.7 collective-permute-done.18
  171.5 3.5 collective-permute-done.17
  190.3 4.2 collective-permute-start.20
  202.6 2.6 collective-permute-start.33
  210.0 3.4 collective-permute-done.33
  214.1 6.1 collective-permute-done.21
  224.6 3.7 collective-permute-done.26
  236.2 5.5 all-gather.19.cloned.1.call-done
  241.7 2.7 multiply_convert_fusion.4
  255.8 2.9 collective-permute-done.38
  261.0 4.7 collective-permute-done.29
  271.6 2.4 collective-permute-done.43
  274.1 3.6 collective-permute-done.42
  298.2 5.8 collective-permute-done.46
  309.8 2.4 collective-permute-done.51
  312.2 3.5 collective-permute-done.50
  337.3 4.0 collective-permute-done.54
  350.9 3.8 collective-permute-done.58
  388.8 5.5 collective-permute-done.62
  400.5 29.1 %reduce-scatter.5.cloned.1.call-done = bf16[256,512]{0,1:T(8,128)(2,1)} async-done(((bf16[1024,512]{0,1:T(8,128)(2,1)}), bf16[256,512]{0,1:T(8,128)(2,1)}) %reduce-scatter.5.cloned.1.call-update) | async-done | bytes 262160 | tf_op jit(solution)/shard_map/reduce_scatter | solution.py:291
  429.6 45.1 %reduce-scatter.9.cloned.1.call-done = bf16[256,1024]{0,1:T(8,128)(2,1)} async-done(((bf16[1024,1024]{0,1:T(8,128)(2,1)}), bf16[256,1024]{0,1:T(8,128)(2,1)}) %reduce-scatter.9.cloned.1.call-update) | async-done | bytes 524304 | tf_op jit(solution)/shard_map/reduce_scatter | solution.py:291
  476.0 7.2 %collective-permute-done.32 = f32[80,1024]{1,0:T(8,128)S(1)} collective-permute-done((f32[80,1024]{1,0:T(8,128)S(1)}, f32[80,1024]{1,0:T(8,128)S(1)}, u32[]{:S(2)}, u32[]{:S(2)}) %collective-permute-start.32) | collective-permute-done | bytes 327712 | tf_op jit(solution)/shard_map/ppermute | solution.py:85
  484.1 11.1 %all-gather.23.cloned.1.call-done = bf16[1024,512]{0,1:T(8,128)(2,1)} async-done(((bf16[256,512]{0,1:T(8,128)(2,1)}), bf16[1024,512]{0,1:T(8,128)(2,1)}) %all-gather.23.cloned.1.call-update) | async-done | bytes 1048592 | tf_op jit(solution)/shard_map/all_gather | solution.py:297
  498.7 2.6 copy.100
  501.2 2.8 stack_reshape.25
  506.7 114.7 %all-reduce.2.cloned.1.call-done = f32[24,1024]{1,0:T(8,128)} async-done(((f32[24,1024]{1,0:T(8,128)}), f32[24,1024]{1,0:T(8,128)}) %all-reduce.2.cloned.1.call-update) | async-done | bytes 98320 | tf_op jit(solution)/shard_map/psum | solution.py:334
  627.3 19.8 %all-gather.27.cloned.1.call-done = bf16[1024,1024]{0,1:T(8,128)(2,1)} async-done(((bf16[256,1024]{0,1:T(8,128)(2,1)}), bf16[1024,1024]{0,1:T(8,128)(2,1)}) %all-gather.27.cloned.1.call-update) | async-done | bytes 2097168 | tf_op jit(solution)/shard_map/all_gather | solution.py:297
  647.1 5.0 reshape.365
  652.1 4.3 slice_bitcast_fusion
  658.1 2.9 copy.104
  661.0 2.4 stack_reshape.29
  668.8 2.6 copy.99
  671.4 2.8 stack_reshape.24
  678.9 11.0 %all-gather.25.cloned.1.call-done = bf16[1024,1024]{0,1:T(8,128)(2,1)} async-done(((bf16[256,1024]{0,1:T(8,128)(2,1)}), bf16[1024,1024]{0,1:T(8,128)(2,1)}) %all-gather.25.cloned.1.call-update) | async-done | bytes 2097168 | tf_op jit(solution)/shard_map/all_gather | solution.py:297
  689.8 5.0 reshape.364
  694.8 4.3 slice_bitcast_fusion.1
  700.8 2.9 copy.103
  703.7 2.5 stack_reshape.28
  706.2 4.7 pad_maximum_fusion.1
  (615 shorter events, 273.7 us)
Async XLA Ops:
  7.2 61.7 %all-gather.13.cloned.1.call-start = ((), (), s32[]{:S(2)}) async-start(), calls=%async_computation.4 | async-start | bytes 1310720 | tf_op jit(solution)/shard_map/all_gather | solution.py:126
  23.3 30.6 %collective-permute-start.2 = (bf16[80,1024]{1,0:T(8,128)(2,1)}, bf16[80,1024]{1,0:T(8,128)(2,1)}, u32[]{:S(2)}, u32[]{:S(2)}) collective-permute-start(bf16[80,1024]{1,0:T(8,128)(2,1)} %get-tuple-element.77), channel_id=1, source_target_pairs={{0,5},{1,4},{2,7},{3,6},{4,1},{5,0},{6,3},{7,2},{8,13},{9,12},{10,... | collective-permute-start | bytes 491528 | tf_op jit(solution)/shard_map/ppermute | solution.py:91
  25.5 28.4 %collective-permute-start.1 = (bf16[80,1024]{1,0:T(8,128)(2,1)}, bf16[80,1024]{1,0:T(8,128)(2,1)}, u32[]{:S(2)}, u32[]{:S(2)}) collective-permute-start(bf16[80,1024]{1,0:T(8,128)(2,1)} %get-tuple-element.77), channel_id=1, source_target_pairs={{0,4},{2,6},{4,0},{6,2},{1,5},{3,7},{5,1},{7,3},{8,12},{10,14},{12... | collective-permute-start | bytes 491528 | tf_op jit(solution)/shard_map/ppermute | solution.py:82
  25.7 28.2 %collective-permute-start = (bf16[80,1024]{1,0:T(8,128)(2,1)}, bf16[80,1024]{1,0:T(8,128)(2,1)}, u32[]{:S(2)}, u32[]{:S(2)}) collective-permute-start(bf16[80,1024]{1,0:T(8,128)(2,1)} %get-tuple-element.77), channel_id=1, source_target_pairs={{0,1},{1,0},{2,3},{3,2},{4,5},{5,4},{6,7},{7,6},{8,9},{9,8},{10,11... | collective-permute-start | bytes 491528 | tf_op jit(solution)/shard_map/ppermute | solution.py:85
  35.3 95.9 %all-gather.15.cloned.1.call-start = ((), (), s32[]{:S(2)}) async-start(), calls=%async_computation.5 | async-start | bytes 2621440 | tf_op jit(solution)/shard_map/all_gather | solution.py:126
  55.1 11.5 %collective-permute-start.3 = (bf16[320,1024]{1,0:T(8,128)(2,1)S(1)}, bf16[320,1024]{1,0:T(8,128)(2,1)S(1)}, u32[]{:S(2)}, u32[]{:S(2)}) collective-permute-start(bf16[320,1024]{1,0:T(8,128)(2,1)S(1)} %pad_maximum_fusion.8), channel_id=1, source_target_pairs={{0,2},{2,0},{4,6},{6,4},{1,3},{3,1},{5,7},{7,5},{8,10},{10,8},{12,... | collective-permute-start | bytes 1966088 | tf_op jit(solution)/shard_map/ppermute | solution.py:79
  78.2 9.2 %collective-permute-start.4 = (bf16[320,1024]{1,0:T(8,128)(2,1)}, bf16[320,1024]{1,0:T(8,128)(2,1)}, u32[]{:S(2)}, u32[]{:S(2)}) collective-permute-start(bf16[320,1024]{1,0:T(8,128)(2,1)} %slice.928), channel_id=1, source_target_pairs={{0,2},{2,0},{4,6},{6,4},{1,3},{3,1},{5,7},{7,5},{8,10},{10,8},{12,... | collective-permute-start | bytes 1966088 | tf_op jit(solution)/shard_map/ppermute | solution.py:79
  87.4 92.9 %all-gather.17.cloned.1.call-start = ((), (), s32[]{:S(2)}) async-start(), calls=%async_computation.6 | async-start | bytes 1310720 | tf_op jit(solution)/shard_map/all_gather | solution.py:126
  89.3 9.5 %collective-permute-start.5 = (bf16[80,1024]{1,0:T(8,128)(2,1)S(1)}, bf16[80,1024]{1,0:T(8,128)(2,1)S(1)}, u32[]{:S(2)}, u32[]{:S(2)}) collective-permute-start(bf16[80,1024]{1,0:T(8,128)(2,1)S(1)} %get-tuple-element.120), channel_id=1, source_target_pairs={{0,1},{1,0},{2,3},{3,2},{4,5},{5,4},{6,7},{7,6},{8,9},{9,8},{10,11... | collective-permute-start | bytes 491528 | tf_op jit(solution)/shard_map/ppermute | solution.py:85
  90.6 8.3 %collective-permute-start.7 = (bf16[80,1024]{1,0:T(8,128)(2,1)S(1)}, bf16[80,1024]{1,0:T(8,128)(2,1)S(1)}, u32[]{:S(2)}, u32[]{:S(2)}) collective-permute-start(bf16[80,1024]{1,0:T(8,128)(2,1)S(1)} %get-tuple-element.121), channel_id=1, source_target_pairs={{0,5},{1,4},{2,7},{3,6},{4,1},{5,0},{6,3},{7,2},{8,13},{9,12},{10,... | collective-permute-start | bytes 491528 | tf_op jit(solution)/shard_map/ppermute | solution.py:91
  91.8 8.0 %collective-permute-start.6 = (bf16[80,1024]{1,0:T(8,128)(2,1)S(1)}, bf16[80,1024]{1,0:T(8,128)(2,1)S(1)}, u32[]{:S(2)}, u32[]{:S(2)}) collective-permute-start(bf16[80,1024]{1,0:T(8,128)(2,1)S(1)} %get-tuple-element.122), channel_id=1, source_target_pairs={{0,4},{2,6},{4,0},{6,2},{1,5},{3,7},{5,1},{7,3},{8,12},{10,14},{12... | collective-permute-start | bytes 491528 | tf_op jit(solution)/shard_map/ppermute | solution.py:82
  101.5 12.2 %collective-permute-start.10 = (bf16[80,1024]{1,0:T(8,128)(2,1)S(1)}, bf16[80,1024]{1,0:T(8,128)(2,1)S(1)}, u32[]{:S(2)}, u32[]{:S(2)}) collective-permute-start(bf16[80,1024]{1,0:T(8,128)(2,1)S(1)} %get-tuple-element.71), channel_id=1, source_target_pairs={{0,5},{1,4},{2,7},{3,6},{4,1},{5,0},{6,3},{7,2},{8,13},{9,12},{10,... | collective-permute-start | bytes 491528 | tf_op jit(solution)/shard_map/ppermute | solution.py:91
  103.6 10.1 %collective-permute-start.9 = (bf16[80,1024]{1,0:T(8,128)(2,1)S(1)}, bf16[80,1024]{1,0:T(8,128)(2,1)S(1)}, u32[]{:S(2)}, u32[]{:S(2)}) collective-permute-start(bf16[80,1024]{1,0:T(8,128)(2,1)S(1)} %get-tuple-element.71), channel_id=1, source_target_pairs={{0,4},{2,6},{4,0},{6,2},{1,5},{3,7},{5,1},{7,3},{8,12},{10,14},{12... | collective-permute-start | bytes 491528 | tf_op jit(solution)/shard_map/ppermute | solution.py:82
  103.9 9.8 %collective-permute-start.8 = (bf16[80,1024]{1,0:T(8,128)(2,1)S(1)}, bf16[80,1024]{1,0:T(8,128)(2,1)S(1)}, u32[]{:S(2)}, u32[]{:S(2)}) collective-permute-start(bf16[80,1024]{1,0:T(8,128)(2,1)S(1)} %get-tuple-element.71), channel_id=1, source_target_pairs={{0,1},{1,0},{2,3},{3,2},{4,5},{5,4},{6,7},{7,6},{8,9},{9,8},{10,11... | collective-permute-start | bytes 491528 | tf_op jit(solution)/shard_map/ppermute | solution.py:85
  140.9 22.2 %collective-permute-start.13 = (bf16[80,1024]{1,0:T(8,128)(2,1)}, bf16[80,1024]{1,0:T(8,128)(2,1)}, u32[]{:S(2)}, u32[]{:S(2)}) collective-permute-start(bf16[80,1024]{1,0:T(8,128)(2,1)} %get-tuple-element.117), channel_id=1, source_target_pairs={{0,1},{1,0},{2,3},{3,2},{4,5},{5,4},{6,7},{7,6},{8,9},{9,8},{10,11... | collective-permute-start | bytes 491528 | tf_op jit(solution)/shard_map/ppermute | solution.py:85
  142.1 21.0 %collective-permute-start.15 = (bf16[80,1024]{1,0:T(8,128)(2,1)}, bf16[80,1024]{1,0:T(8,128)(2,1)}, u32[]{:S(2)}, u32[]{:S(2)}) collective-permute-start(bf16[80,1024]{1,0:T(8,128)(2,1)} %get-tuple-element.118), channel_id=1, source_target_pairs={{0,5},{1,4},{2,7},{3,6},{4,1},{5,0},{6,3},{7,2},{8,13},{9,12},{10,... | collective-permute-start | bytes 491528 | tf_op jit(solution)/shard_map/ppermute | solution.py:91
  143.3 19.8 %collective-permute-start.14 = (bf16[80,1024]{1,0:T(8,128)(2,1)}, bf16[80,1024]{1,0:T(8,128)(2,1)}, u32[]{:S(2)}, u32[]{:S(2)}) collective-permute-start(bf16[80,1024]{1,0:T(8,128)(2,1)} %get-tuple-element.119), channel_id=1, source_target_pairs={{0,4},{2,6},{4,0},{6,2},{1,5},{3,7},{5,1},{7,3},{8,12},{10,14},{12... | collective-permute-start | bytes 491528 | tf_op jit(solution)/shard_map/ppermute | solution.py:82
  151.4 90.3 %all-gather.19.cloned.1.call-start = ((), (), s32[]{:S(2)}) async-start(), calls=%async_computation.7 | async-start | bytes 2621440 | tf_op jit(solution)/shard_map/all_gather | solution.py:126
  190.3 14.9 %collective-permute-start.20 = (bf16[320,1024]{1,0:T(8,128)(2,1)}, bf16[320,1024]{1,0:T(8,128)(2,1)}, u32[]{:S(2)}, u32[]{:S(2)}) collective-permute-start(bf16[320,1024]{1,0:T(8,128)(2,1)} %slice.926), channel_id=1, source_target_pairs={{0,2},{2,0},{4,6},{6,4},{1,3},{3,1},{5,7},{7,5},{8,10},{10,8},{12,... | collective-permute-start | bytes 1966088 | tf_op jit(solution)/shard_map/ppermute | solution.py:79
  200.7 181.1 %reduce-scatter.7.cloned.1.call-start = ((), (), s32[]{:S(2)}) async-start(), calls=%async_computation.10 | async-start | bytes 1310720 | tf_op jit(solution)/shard_map/reduce_scatter | solution.py:291
  202.6 10.8 %collective-permute-start.33 = (bf16[80,1024]{1,0:T(8,128)(2,1)S(1)}, bf16[80,1024]{1,0:T(8,128)(2,1)S(1)}, u32[]{:S(2)}, u32[]{:S(2)}) collective-permute-start(bf16[80,1024]{1,0:T(8,128)(2,1)S(1)} %get-tuple-element.55), channel_id=1, source_target_pairs={{0,1},{1,0},{2,3},{3,2},{4,5},{5,4},{6,7},{7,6},{8,9},{9,8},{10,11... | collective-permute-start | bytes 491528 | tf_op jit(solution)/shard_map/ppermute | solution.py:85
  207.1 13.1 %collective-permute-start.21 = (bf16[80,1024]{1,0:T(8,128)(2,1)S(1)}, bf16[80,1024]{1,0:T(8,128)(2,1)S(1)}, u32[]{:S(2)}, u32[]{:S(2)}) collective-permute-start(bf16[80,1024]{1,0:T(8,128)(2,1)S(1)} %get-tuple-element.114), channel_id=1, source_target_pairs={{0,1},{1,0},{2,3},{3,2},{4,5},{5,4},{6,7},{7,6},{8,9},{9,8},{10,11... | collective-permute-start | bytes 491528 | tf_op jit(solution)/shard_map/ppermute | solution.py:85
  207.2 13.0 %collective-permute-start.23 = (bf16[80,1024]{1,0:T(8,128)(2,1)S(1)}, bf16[80,1024]{1,0:T(8,128)(2,1)S(1)}, u32[]{:S(2)}, u32[]{:S(2)}) collective-permute-start(bf16[80,1024]{1,0:T(8,128)(2,1)S(1)} %get-tuple-element.115), channel_id=1, source_target_pairs={{0,5},{1,4},{2,7},{3,6},{4,1},{5,0},{6,3},{7,2},{8,13},{9,12},{10,... | collective-permute-start | bytes 491528 | tf_op jit(solution)/shard_map/ppermute | solution.py:91
  209.3 10.9 %collective-permute-start.22 = (bf16[80,1024]{1,0:T(8,128)(2,1)S(1)}, bf16[80,1024]{1,0:T(8,128)(2,1)S(1)}, u32[]{:S(2)}, u32[]{:S(2)}) collective-permute-start(bf16[80,1024]{1,0:T(8,128)(2,1)S(1)} %get-tuple-element.116), channel_id=1, source_target_pairs={{0,4},{2,6},{4,0},{6,2},{1,5},{3,7},{5,1},{7,3},{8,12},{10,14},{12... | collective-permute-start | bytes 491528 | tf_op jit(solution)/shard_map/ppermute | solution.py:82
  213.5 19.6 %collective-permute-start.36 = (bf16[320,1024]{1,0:T(8,128)(2,1)S(1)}, bf16[320,1024]{1,0:T(8,128)(2,1)S(1)}, u32[]{:S(2)}, u32[]{:S(2)}) collective-permute-start(bf16[320,1024]{1,0:T(8,128)(2,1)S(1)} %pad_maximum_fusion.12), channel_id=1, source_target_pairs={{0,2},{2,0},{4,6},{6,4},{1,3},{3,1},{5,7},{7,5},{8,10},{10,8},{12,... | collective-permute-start | bytes 1966088 | tf_op jit(solution)/shard_map/ppermute | solution.py:79
  222.0 8.4 %collective-permute-start.25 = (bf16[80,1024]{1,0:T(8,128)(2,1)S(1)}, bf16[80,1024]{1,0:T(8,128)(2,1)S(1)}, u32[]{:S(2)}, u32[]{:S(2)}) collective-permute-start(bf16[80,1024]{1,0:T(8,128)(2,1)S(1)} %get-tuple-element.59), channel_id=1, source_target_pairs={{0,4},{2,6},{4,0},{6,2},{1,5},{3,7},{5,1},{7,3},{8,12},{10,14},{12... | collective-permute-start | bytes 491528 | tf_op jit(solution)/shard_map/ppermute | solution.py:82
  223.2 9.4 %collective-permute-start.24 = (bf16[80,1024]{1,0:T(8,128)(2,1)S(1)}, bf16[80,1024]{1,0:T(8,128)(2,1)S(1)}, u32[]{:S(2)}, u32[]{:S(2)}) collective-permute-start(bf16[80,1024]{1,0:T(8,128)(2,1)S(1)} %get-tuple-element.59), channel_id=1, source_target_pairs={{0,1},{1,0},{2,3},{3,2},{4,5},{5,4},{6,7},{7,6},{8,9},{9,8},{10,11... | collective-permute-start | bytes 491528 | tf_op jit(solution)/shard_map/ppermute | solution.py:85
  250.3 8.5 %collective-permute-start.38 = (bf16[80,1024]{1,0:T(8,128)(2,1)S(1)}, bf16[80,1024]{1,0:T(8,128)(2,1)S(1)}, u32[]{:S(2)}, u32[]{:S(2)}) collective-permute-start(bf16[80,1024]{1,0:T(8,128)(2,1)S(1)} %get-tuple-element.108), channel_id=1, source_target_pairs={{0,1},{1,0},{2,3},{3,2},{4,5},{5,4},{6,7},{7,6},{8,9},{9,8},{10,11... | collective-permute-start | bytes 491528 | tf_op jit(solution)/shard_map/ppermute | solution.py:85
  251.5 8.4 %collective-permute-start.40 = (bf16[80,1024]{1,0:T(8,128)(2,1)S(1)}, bf16[80,1024]{1,0:T(8,128)(2,1)S(1)}, u32[]{:S(2)}, u32[]{:S(2)}) collective-permute-start(bf16[80,1024]{1,0:T(8,128)(2,1)S(1)} %get-tuple-element.109), channel_id=1, source_target_pairs={{0,5},{1,4},{2,7},{3,6},{4,1},{5,0},{6,3},{7,2},{8,13},{9,12},{10,... | collective-permute-start | bytes 491528 | tf_op jit(solution)/shard_map/ppermute | solution.py:91
  253.4 12.3 %collective-permute-start.29 = (bf16[80,1024]{1,0:T(8,128)(2,1)S(1)}, bf16[80,1024]{1,0:T(8,128)(2,1)S(1)}, u32[]{:S(2)}, u32[]{:S(2)}) collective-permute-start(bf16[80,1024]{1,0:T(8,128)(2,1)S(1)} %get-tuple-element.111), channel_id=1, source_target_pairs={{0,1},{1,0},{2,3},{3,2},{4,5},{5,4},{6,7},{7,6},{8,9},{9,8},{10,11... | collective-permute-start | bytes 491528 | tf_op jit(solution)/shard_map/ppermute | solution.py:85
  254.6 11.1 %collective-permute-start.31 = (bf16[80,1024]{1,0:T(8,128)(2,1)S(1)}, bf16[80,1024]{1,0:T(8,128)(2,1)S(1)}, u32[]{:S(2)}, u32[]{:S(2)}) collective-permute-start(bf16[80,1024]{1,0:T(8,128)(2,1)S(1)} %get-tuple-element.112), channel_id=1, source_target_pairs={{0,5},{1,4},{2,7},{3,6},{4,1},{5,0},{6,3},{7,2},{8,13},{9,12},{10,... | collective-permute-start | bytes 491528 | tf_op jit(solution)/shard_map/ppermute | solution.py:91
  258.7 8.5 %collective-permute-start.30 = (bf16[80,1024]{1,0:T(8,128)(2,1)S(1)}, bf16[80,1024]{1,0:T(8,128)(2,1)S(1)}, u32[]{:S(2)}, u32[]{:S(2)}) collective-permute-start(bf16[80,1024]{1,0:T(8,128)(2,1)S(1)} %get-tuple-element.113), channel_id=1, source_target_pairs={{0,4},{2,6},{4,0},{6,2},{1,5},{3,7},{5,1},{7,3},{8,12},{10,14},{12... | collective-permute-start | bytes 491528 | tf_op jit(solution)/shard_map/ppermute | solution.py:82
  295.5 8.5 %collective-permute-start.46 = (bf16[80,1024]{1,0:T(8,128)(2,1)S(1)}, bf16[80,1024]{1,0:T(8,128)(2,1)S(1)}, u32[]{:S(2)}, u32[]{:S(2)}) collective-permute-start(bf16[80,1024]{1,0:T(8,128)(2,1)S(1)} %get-tuple-element.105), channel_id=1, source_target_pairs={{0,1},{1,0},{2,3},{3,2},{4,5},{5,4},{6,7},{7,6},{8,9},{9,8},{10,11... | collective-permute-start | bytes 491528 | tf_op jit(solution)/shard_map/ppermute | solution.py:85
  330.3 70.1 %reduce-scatter.11.cloned.1.call-start = ((), (), s32[]{:S(2)}) async-start(), calls=%async_computation.12 | async-start | bytes 2621440 | tf_op jit(solution)/shard_map/reduce_scatter | solution.py:291
  332.2 9.0 %collective-permute-start.54 = (bf16[80,1024]{1,0:T(8,128)(2,1)S(1)}, bf16[80,1024]{1,0:T(8,128)(2,1)S(1)}, u32[]{:S(2)}, u32[]{:S(2)}) collective-permute-start(bf16[80,1024]{1,0:T(8,128)(2,1)S(1)} %get-tuple-element.102), channel_id=1, source_target_pairs={{0,1},{1,0},{2,3},{3,2},{4,5},{5,4},{6,7},{7,6},{8,9},{9,8},{10,11... | collective-permute-start | bytes 491528 | tf_op jit(solution)/shard_map/ppermute | solution.py:85
  333.5 7.8 %collective-permute-start.56 = (bf16[80,1024]{1,0:T(8,128)(2,1)S(1)}, bf16[80,1024]{1,0:T(8,128)(2,1)S(1)}, u32[]{:S(2)}, u32[]{:S(2)}) collective-permute-start(bf16[80,1024]{1,0:T(8,128)(2,1)S(1)} %get-tuple-element.103), channel_id=1, source_target_pairs={{0,5},{1,4},{2,7},{3,6},{4,1},{5,0},{6,3},{7,2},{8,13},{9,12},{10,... | collective-permute-start | bytes 491528 | tf_op jit(solution)/shard_map/ppermute | solution.py:91
  334.7 7.7 %collective-permute-start.55 = (bf16[80,1024]{1,0:T(8,128)(2,1)S(1)}, bf16[80,1024]{1,0:T(8,128)(2,1)S(1)}, u32[]{:S(2)}, u32[]{:S(2)}) collective-permute-start(bf16[80,1024]{1,0:T(8,128)(2,1)S(1)} %get-tuple-element.104), channel_id=1, source_target_pairs={{0,4},{2,6},{4,0},{6,2},{1,5},{3,7},{5,1},{7,3},{8,12},{10,14},{12... | collective-permute-start | bytes 491528 | tf_op jit(solution)/shard_map/ppermute | solution.py:82
  347.9 7.5 %collective-permute-start.57 = (bf16[80,1024]{1,0:T(8,128)(2,1)}, bf16[80,1024]{1,0:T(8,128)(2,1)}, u32[]{:S(2)}, u32[]{:S(2)}) collective-permute-start(bf16[80,1024]{1,0:T(8,128)(2,1)} %get-tuple-element.40), channel_id=1, source_target_pairs={{0,1},{1,0},{2,3},{3,2},{4,5},{5,4},{6,7},{7,6},{8,9},{9,8},{10,11... | collective-permute-start | bytes 491528 | tf_op jit(solution)/shard_map/ppermute | solution.py:85
  349.7 79.9 %reduce-scatter.5.cloned.1.call-start = ((), (), s32[]{:S(2)}) async-start(), calls=%async_computation.9 | async-start | bytes 1310720 | tf_op jit(solution)/shard_map/reduce_scatter | solution.py:291
  372.0 102.7 %reduce-scatter.9.cloned.1.call-start = ((), (), s32[]{:S(2)}) async-start(), calls=%async_computation.11 | async-start | bytes 2621440 | tf_op jit(solution)/shard_map/reduce_scatter | solution.py:291
  377.7 117.6 %all-gather.23.cloned.1.call-start = ((), (), s32[]{:S(2)}) async-start(), calls=%async_computation.14 | async-start | bytes 1310720 | tf_op jit(solution)/shard_map/all_gather | solution.py:297
  381.8 239.6 %all-reduce.2.cloned.1.call-start = ((), (), s32[]{:S(2)}) async-start(), calls=%async_computation.8 | async-start | bytes 196608 | tf_op jit(solution)/shard_map/psum | solution.py:334
  386.0 8.3 %collective-permute-start.62 = (bf16[80,1024]{1,0:T(8,128)(2,1)S(1)}, bf16[80,1024]{1,0:T(8,128)(2,1)S(1)}, u32[]{:S(2)}, u32[]{:S(2)}) collective-permute-start(bf16[80,1024]{1,0:T(8,128)(2,1)S(1)} %get-tuple-element.99), channel_id=1, source_target_pairs={{0,1},{1,0},{2,3},{3,2},{4,5},{5,4},{6,7},{7,6},{8,9},{9,8},{10,11... | collective-permute-start | bytes 491528 | tf_op jit(solution)/shard_map/ppermute | solution.py:85
  399.0 248.1 %all-gather.27.cloned.1.call-start = ((), (), s32[]{:S(2)}) async-start(), calls=%async_computation.16 | async-start | bytes 2621440 | tf_op jit(solution)/shard_map/all_gather | solution.py:297
  400.4 265.0 %all-gather.21.cloned.1.call-start = ((), (), s32[]{:S(2)}) async-start(), calls=%async_computation.13 | async-start | bytes 1310720 | tf_op jit(solution)/shard_map/all_gather | solution.py:297
  429.6 260.3 %all-gather.25.cloned.1.call-start = ((), (), s32[]{:S(2)}) async-start(), calls=%async_computation.15 | async-start | bytes 2621440 | tf_op jit(solution)/shard_map/all_gather | solution.py:297
  474.7 8.5 %collective-permute-start.32 = (f32[80,1024]{1,0:T(8,128)S(1)}, f32[80,1024]{1,0:T(8,128)S(1)}, u32[]{:S(2)}, u32[]{:S(2)}) collective-permute-start(f32[80,1024]{1,0:T(8,128)S(1)} %copy-done.52), channel_id=1, source_target_pairs={{0,1},{1,0},{2,3},{3,2},{4,5},{5,4},{6,7},{7,6},{8,9},{9,8},{10,11... | collective-permute-start | bytes 983048 | tf_op jit(solution)/shard_map/ppermute | solution.py:85
  505.4 121.1 %collective-permute-start.65 = (f32[80,1024]{1,0:T(8,128)S(1)}, f32[80,1024]{1,0:T(8,128)S(1)}, u32[]{:S(2)}, u32[]{:S(2)}) collective-permute-start(f32[80,1024]{1,0:T(8,128)S(1)} %add_multiply_fusion.2), channel_id=1, source_target_pairs={{0,1},{1,0},{2,3},{3,2},{4,5},{5,4},{6,7},{7,6},{8,9},{9,8},{10,11... | collective-permute-start | bytes 983048 | tf_op jit(solution)/shard_map/ppermute | solution.py:85
  (145 other events, 990.2 us)
Sparse Core Ops, SparseCore 0:
  35.4 33.4 all-gather.12
  87.5 43.6 all-gather.14
  151.5 27.6 all-gather.16
  200.8 40.7 all-gather.18
  330.4 24.9 reduce-scatter.6
  358.2 42.1 reduce-scatter.10
  402.7 26.8 reduce-scatter.4
  432.5 42.1 reduce-scatter.8
  476.3 18.9 all-gather.22
  501.3 120.0 all-reduce.1
  622.9 24.1 all-gather.26
  648.5 16.8 all-gather.20
  667.0 22.8 all-gather.24

commit v2 on v1

v2 whole, which is shorter than its diff:
```python
import functools
import math

import jax
import jax.numpy as jnp
from jax import lax
from jax.experimental import pallas as pl
from jax.experimental.pallas import tpu as pltpu
from jax.sharding import PartitionSpec as P

NORM_EPSILON = 1e-06
MASK_FILL = -1e30
ROOT_HALF = 0.7071067811865476
INV_ROOT_TAU = 0.3989422804014327
GROUP = 4
ORDER = (0, 1, 4, 5, 2, 3, 6, 7)
CHIPS = 4

bf16 = jnp.bfloat16
f32 = jnp.float32
VMEM = pl.BlockSpec(memory_space=pltpu.VMEM)
ANY = pl.BlockSpec(memory_space=pl.ANY)


def dot(a, b):
    return lax.dot_general(a, b, (((1,), (0,)), ((), ())), preferred_element_type=f32)


def dot_nt(a, b):
    return lax.dot_general(a, b, (((1,), (1,)), ((), ())), preferred_element_type=f32)


def dot_tn(a, b):
    return lax.dot_general(a, b, (((0,), (0,)), ((), ())), preferred_element_type=f32)


def kernel_call(body, outs, *args, name, flops=0, limit=16, scratch=(), specs=None):
    moved = sum(a.size * a.dtype.itemsize for a in args)
    moved += sum(math.prod(s) * jnp.dtype(d).itemsize for s, d in outs)
    return pl.pallas_call(
        body,
        out_shape=[jax.ShapeDtypeStruct(s, d) for s, d in outs],
        in_specs=[VMEM] * len(args) if specs is None else specs,
        out_specs=[VMEM] * len(outs),
        scratch_shapes=list(scratch),
        compiler_params=pltpu.CompilerParams(vmem_limit_bytes=limit << 20),
        cost_estimate=pl.CostEstimate(flops=flops, bytes_accessed=moved, transcendentals=0),
        name=name,
    )(*args)


def row_mean(value):
    return jnp.mean(value, axis=-1, keepdims=True)


def normalize(values):
    center = values - row_mean(values)
    inverse = lax.rsqrt(row_mean(center * center) + NORM_EPSILON)
    return center * inverse, inverse


def lanes_of(head, head_dim, width):
    lane = lax.broadcasted_iota(jnp.int32, (1, width), 1)
    return (lane >= head * head_dim) & (lane < (head + 1) * head_dim)


def assemble(chunks, target):
    rows = chunks[0].shape[0]
    for k, chunk in enumerate(chunks):
        target[k * rows : (k + 1) * rows, :] = chunk[...]


def pack_kernel(layer, feats, hidden, qkv_hbm, out_hbm, fc1_hbm, fc2_hbm, attn_ref, mlp_ref,
                qkv, out, fc1, fc2, sems):
    ci = lax.rem(lax.axis_index("ctx"), GROUP)
    head_cols = pl.ds(pl.multiple_of(ci * feats, feats), feats)
    hidden_cols = pl.ds(pl.multiple_of(ci * hidden, hidden), hidden)
    copies = [
        pltpu.make_async_copy(qkv_hbm.at[layer, :, :, head_cols], qkv, sems.at[0]),
        pltpu.make_async_copy(out_hbm.at[layer, head_cols, :], out, sems.at[1]),
        pltpu.make_async_copy(fc1_hbm.at[layer, :, hidden_cols], fc1, sems.at[2]),
        pltpu.make_async_copy(fc2_hbm.at[layer, hidden_cols, :], fc2, sems.at[3]),
    ]
    for copy in copies:
        copy.start()
    copies[0].wait()
    for k in range(3):
        attn_ref[:, k * feats : (k + 1) * feats] = qkv[k]
    copies[1].wait()
    attn_ref[:, 3 * feats :] = out[...].T
    copies[2].wait()
    mlp_ref[:, :hidden] = fc1[...]
    copies[3].wait()
    mlp_ref[:, hidden:] = fc2[...].T


def prep_kernel(tp, outer, rows, lengths, inputs, cotangent, vecs,
                stream_ref, first_ref, upstream_ref, upstream_b_ref, usable_ref, mask_ref):
    c = lax.axis_index("ctx")
    t = lax.axis_index("tp")
    place = lax.rem(c, GROUP) * tp + t
    start = pl.multiple_of(t * rows, rows)
    stream = inputs[0, pl.ds(start, rows), :]
    stream_ref[...] = stream
    normed, _ = normalize(stream)
    first_ref[...] = (normed * vecs[0:1, :] + vecs[4:5, :]).astype(bf16)
    row = lax.broadcasted_iota(jnp.int32, (rows, 128), 0)
    mask = jnp.where(row + start < lengths[0, c], 1.0, 0.0)
    mask_ref[...] = mask
    upstream = cotangent[0, pl.ds(start, rows), :] * mask[:, 0:1]
    upstream_ref[...] = upstream
    upstream_b_ref[...] = upstream.astype(bf16)
    lane = lax.broadcasted_iota(jnp.int32, usable_ref.shape, 1)
    limit = jnp.zeros(usable_ref.shape, jnp.int32)
    for o in range(outer):
        for k, d in enumerate(ORDER):
            source = place ^ d
            first_lane = (o * len(ORDER) + k) * rows
            count = lengths[0, o * GROUP + lax.div(source, tp)] - lax.rem(source, tp) * rows
            limit = jnp.where(lane >= first_lane, first_lane + count, limit)
            limit = jnp.where(lane >= first_lane + rows, 0, limit)
    usable_ref[...] = jnp.where(lane < limit, 1.0, 0.0)


def qkv_kernel(feats, c0, c1, c2, c3, w, bias, qkv_ref, x):
    assemble((c0, c1, c2, c3), x)
    qkv = dot(x[...], w[:, : 3 * feats])
    qkv_ref[:, :feats] = (qkv[:, :feats] + bias[0:1, :]).astype(bf16)
    qkv_ref[:, feats : 2 * feats] = qkv[:, feats : 2 * feats].astype(bf16)
    qkv_ref[:, 2 * feats :] = (qkv[:, 2 * feats :] + bias[1:2, :]).astype(bf16)


def load_keys(parts, feats, keys, values):
    first = 0
    for part in parts:
        rows, width = part.shape
        keys[first : first + rows, :] = part[:, width - 2 * feats : width - feats]
        values[first : first + rows, :] = part[:, width - feats :]
        first += rows


def attn_kernel(feats, heads, part_count, tile, *refs):
    q_ref, *rest = refs
    parts = rest[:part_count]
    w, usable, attended_ref, norm_ref, partial_ref, keys, values = rest[part_count:]
    head_dim = feats // heads
    scale = 1.0 / math.sqrt(head_dim)
    load_keys(parts, feats, keys, values)
    keep = usable[...] > 0.5
    rows = q_ref.shape[0]
    for first in range(0, rows, tile):
        span = slice(first, first + tile)
        q = q_ref[span, :feats]
        attended = None
        for h in range(heads):
            own = lanes_of(h, head_dim, feats)
            scores = dot_nt(jnp.where(own, q, jnp.zeros_like(q)), keys[...]) * scale
            scores = jnp.where(keep, scores, MASK_FILL)
            highest = jnp.max(scores, axis=-1, keepdims=True)
            raised = jnp.exp(scores - highest)
            total = jnp.sum(raised, axis=-1, keepdims=True)
            soft = (raised * (1.0 / total)).astype(bf16)
            result = dot(soft, values[...])
            log_norm = jnp.broadcast_to(highest + jnp.log(total), (tile, feats))
            if attended is None:
                attended, norms = result, log_norm
            else:
                attended = jnp.where(own, result, attended)
                norms = jnp.where(own, log_norm, norms)
        attended_ref[span, :] = attended.astype(bf16)
        norm_ref[span, :] = norms
    partial_ref[...] = dot_nt(attended_ref[...], w[:, 3 * feats :]).astype(bf16)


def core_sum_kernel(near, far, own_ref, y_ref, x_ref, xy_ref):
    rows = own_ref.shape[0]
    for k, ref in enumerate((own_ref, y_ref, x_ref, xy_ref)):
        span = slice(k * rows, (k + 1) * rows)
        ref[...] = (near[span, :].astype(f32) + far[span, :].astype(f32)).astype(ref.dtype)


def total_of(own, y, x, xy):
    return own[...] + y[...].astype(f32) + x[...].astype(f32) + xy[...].astype(f32)


def sum_norm_kernel(bias_row, gain_row, shift_row, own, y, x, xy, residual, vecs,
                    stream_ref, normed_ref):
    stream = residual[...] + total_of(own, y, x, xy) + vecs[bias_row : bias_row + 1, :]
    stream_ref[...] = stream
    normed, _ = normalize(stream)
    gain = vecs[gain_row : gain_row + 1, :]
    normed_ref[...] = (normed * gain + vecs[shift_row : shift_row + 1, :]).astype(bf16)


def sum_out_kernel(bias_row, own, y, x, xy, residual, vecs, mask, out_ref):
    stream = residual[...] + total_of(own, y, x, xy) + vecs[bias_row : bias_row + 1, :]
    out_ref[...] = stream * mask[:, 0:1]


def mlp_kernel(hidden, c0, c1, c2, c3, w, bias, partial_ref, act_ref, slope_ref, x):
    assemble((c0, c1, c2, c3), x)
    pre = dot(x[...], w[:, :hidden]) + bias[...]
    cdf = 0.5 * (1.0 + lax.erf(pre * ROOT_HALF))
    density = jnp.exp(-0.5 * pre * pre) * INV_ROOT_TAU
    slope_ref[...] = cdf + pre * density
    act_ref[...] = (pre * cdf).astype(bf16)
    partial_ref[...] = dot_nt(act_ref[...], w[:, hidden:]).astype(bf16)


def mlp_back_kernel(hidden, c0, c1, c2, c3, w, slope, partial_ref, grad_ref, sum_ref, x):
    assemble((c0, c1, c2, c3), x)
    grad = dot(x[...], w[:, hidden:]) * slope[...]
    grad_ref[...] = grad.astype(bf16)
    sum_ref[...] = jnp.sum(grad, axis=0, keepdims=True)
    partial_ref[...] = dot_nt(grad_ref[...], w[:, :hidden]).astype(bf16)


def grad_kernel(width, *refs):
    left_one, left_two = refs[0:8], refs[8:16]
    one_near, one_far, two_near, two_far, out_ref, x, z = refs[16:]
    rows = one_near.shape[0]
    assemble(left_one, x)
    z[:rows, :width] = one_near[...]
    z[rows:, :width] = one_far[...]
    out_ref[:, :width] = dot_tn(x[...], z[:, :width]).astype(bf16)
    assemble(left_two, x)
    rest = out_ref.shape[1] - width
    z[:rows, :rest] = two_near[...]
    z[rows:, :rest] = two_far[...]
    out_ref[:, width:] = dot_tn(x[...], z[:, :rest]).astype(bf16)


def norm_back(upstream, values, gain):
    normed, inverse = normalize(values)
    scaled = upstream * gain
    back = inverse * (scaled - row_mean(scaled) - normed * row_mean(scaled * normed))
    gain_grad = jnp.sum(upstream * normed, axis=0, keepdims=True)
    return back, gain_grad, jnp.sum(upstream, axis=0, keepdims=True)


def norm_back_two_kernel(gain_row, own, y, x, xy, values, upstream, vecs,
                         grad_ref, grad_b_ref, sums_ref):
    up = upstream[...]
    back, gain_grad, shift_grad = norm_back(
        total_of(own, y, x, xy), values[...], vecs[gain_row : gain_row + 1, :]
    )
    grad = up + back
    grad_ref[...] = grad
    grad_b_ref[...] = grad.astype(bf16)
    sums_ref[0:1, :] = gain_grad
    sums_ref[1:2, :] = shift_grad
    sums_ref[2:3, :] = jnp.sum(grad, axis=0, keepdims=True)
    sums_ref[3:4, :] = jnp.sum(up, axis=0, keepdims=True)


def norm_back_one_kernel(gain_row, own, y, x, xy, values, upstream, vecs, mask,
                         grad_ref, grad_b_ref, sums_ref):
    back, gain_grad, shift_grad = norm_back(
        total_of(own, y, x, xy), values[...], vecs[gain_row : gain_row + 1, :]
    )
    grad = upstream[...] + back
    if mask is not None:
        grad = grad * mask[:, 0:1]
    grad_ref[...] = grad
    if grad_b_ref is not None:
        grad_b_ref[...] = grad.astype(bf16)
    sums_ref[0:1, :] = gain_grad
    sums_ref[1:2, :] = shift_grad


def attn_back_kernel(feats, heads, part_count, tile, carried, *refs):
    c0, c1, c2, c3, w, q_ref, attended, norms, usable, *rest = refs
    parts = rest[:part_count]
    rest = rest[part_count:]
    if carried:
        keys_before, values_before, *rest = rest
    grad_q, grad_k, grad_v, x, keys, values, grad_att = rest
    head_dim = feats // heads
    scale = 1.0 / math.sqrt(head_dim)
    assemble((c0, c1, c2, c3), x)
    load_keys(parts, feats, keys, values)
    grad_att[...] = dot(x[...], w[:, 3 * feats :]).astype(bf16)
    keep = usable[...] > 0.5
    rows = q_ref.shape[0]
    if carried:
        sum_k, sum_v = keys_before[...], values_before[...]
    else:
        sum_k = jnp.zeros(grad_k.shape, f32)
        sum_v = jnp.zeros(grad_v.shape, f32)
    for first in range(0, rows, tile):
        span = slice(first, first + tile)
        q = q_ref[span, :feats]
        ga = grad_att[span, :]
        products = ga.astype(f32) * attended[span, :].astype(f32)
        gq = None
        for h in range(heads):
            own = lanes_of(h, head_dim, feats)
            own_f = jnp.where(own, 1.0, 0.0)
            q_h = jnp.where(own, q, jnp.zeros_like(q))
            ga_h = jnp.where(own, ga, jnp.zeros_like(ga))
            row_dots = jnp.sum(products * own_f, axis=-1, keepdims=True)
            scores = dot_nt(q_h, keys[...]) * scale
            scores = jnp.where(keep, scores, MASK_FILL)
            soft = jnp.exp(scores - norms[span, h * head_dim : h * head_dim + 1])
            grad_soft = dot_nt(ga_h, values[...])
            grad_scores = (soft * (grad_soft - row_dots)).astype(bf16)
            part = dot(grad_scores, keys[...])
            gq = part if gq is None else jnp.where(own, part, gq)
            sum_k = sum_k + dot_tn(grad_scores, q_h) * scale
            sum_v = sum_v + dot_tn(soft.astype(bf16), ga_h)
        grad_q[span, :] = gq * scale
    grad_k[...] = sum_k
    grad_v[...] = sum_v


def project_kernel(feats, first, gq, gk, gv, w, packed_ref, partial_ref, sums_ref):
    rows = gq.shape[0]
    span = slice(first, first + rows)
    packed_ref[:, :feats] = gq[...].astype(bf16)
    packed_ref[:, feats : 2 * feats] = gk[span, :].astype(bf16)
    packed_ref[:, 2 * feats :] = gv[span, :].astype(bf16)
    sums_ref[0:1, :] = jnp.sum(gq[...], axis=0, keepdims=True)
    sums_ref[1:2, :] = jnp.sum(gv[span, :], axis=0, keepdims=True)
    partial_ref[...] = dot_nt(packed_ref[...], w[:, : 3 * feats]).astype(bf16)


def place_mlp_kernel(layer, hidden, p0, p1, p2, p3, *refs):
    fc1_hbm, fc2_hbm, fc1, fc2, sems = refs[-5:]
    ci = lax.rem(lax.axis_index("ctx"), GROUP)
    copies = []
    for k, piece in enumerate((p0, p1, p2, p3)):
        span = pl.ds(pl.multiple_of((ci ^ k) * hidden, hidden), hidden)
        fc1[k] = piece[:, :hidden].astype(f32)
        copies.append(
            pltpu.make_async_copy(fc1.at[k], fc1_hbm.at[layer, :, span], sems.at[2 * k])
        )
        copies[-1].start()
        fc2[k] = piece[:, hidden:].astype(f32).T
        copies.append(
            pltpu.make_async_copy(fc2.at[k], fc2_hbm.at[layer, span, :], sems.at[2 * k + 1])
        )
        copies[-1].start()
    for copy in copies:
        copy.wait()


def place_attn_kernel(layer, feats, p0, p1, p2, p3, *refs):
    qkv_hbm, out_hbm, qkv, out, sems = refs[-5:]
    ci = lax.rem(lax.axis_index("ctx"), GROUP)
    copies = []
    for k, piece in enumerate((p0, p1, p2, p3)):
        span = pl.ds(pl.multiple_of((ci ^ k) * feats, feats), feats)
        for j in range(3):
            qkv[k, j] = piece[:, j * feats : (j + 1) * feats].astype(f32)
        copies.append(
            pltpu.make_async_copy(qkv.at[k], qkv_hbm.at[layer, :, :, span], sems.at[2 * k])
        )
        copies[-1].start()
        out[k] = piece[:, 3 * feats :].astype(f32).T
        copies.append(
            pltpu.make_async_copy(out.at[k], out_hbm.at[layer, span, :], sems.at[2 * k + 1])
        )
        copies[-1].start()
    for copy in copies:
        copy.wait()


def place_call(body, pieces, before, outs, scratch, name):
    aliases = {} if before is None else {4: 0, 5: 1}
    extra = () if before is None else tuple(before)
    return pl.pallas_call(
        body,
        out_shape=[jax.ShapeDtypeStruct(s, f32) for s in outs],
        in_specs=[VMEM] * 4 + [ANY] * len(extra),
        out_specs=[ANY] * 2,
        scratch_shapes=[pltpu.VMEM(s, f32) for s in scratch] + [pltpu.SemaphoreType.DMA((8,))],
        input_output_aliases=aliases,
        compiler_params=pltpu.CompilerParams(vmem_limit_bytes=16 << 20),
        cost_estimate=pl.CostEstimate(
            flops=0, bytes_accessed=12 * pieces[0].size * 4, transcendentals=0
        ),
        name=name,
    )(*pieces, *extra)


def per_device(
    inputs, lengths, cotangent, norm_gains, shifts, qv_bias, fc1_bias, w_qkv, w_out, w_fc1, w_fc2
):
    depth = w_qkv.shape[0]
    width_own = w_qkv.shape[2]
    fsdp = lax.axis_size("fsdp")
    tp = lax.axis_size("tp")
    ctx = lax.axis_size("ctx")
    outer = ctx // GROUP
    rows = inputs.shape[1] // tp
    half = rows * CHIPS
    all_rows = 2 * half
    head_own = qv_bias.shape[3]
    head_dim = head_own * fsdp
    heads = qv_bias.shape[2] // GROUP
    feats = heads * head_dim
    hidden = w_fc1.shape[2] // GROUP
    width = width_own * fsdp
    t = lax.axis_index("tp")
    f = lax.axis_index("fsdp")
    ci = lax.axis_index("ctx") % GROUP
    tile = half // 2

    def swap_core(value):
        return lax.ppermute(value, "ctx", [(i, i ^ 1) for i in range(ctx)])

    def swap_x(value):
        return lax.ppermute(value, "ctx", [(i, i ^ 2) for i in range(ctx)])

    def swap_y(value):
        return lax.ppermute(value, "tp", [(i, i ^ 1) for i in range(tp)])

    def swap_xy(value):
        pairs = [
            (i * tp + k, (i ^ 2) * tp + (k ^ 1)) for i in range(ctx) for k in range(tp)
        ]
        return lax.ppermute(value, ("ctx", "tp"), pairs)

    outer_groups = [[o * GROUP + i for o in range(outer)] for i in range(GROUP)]

    def gather_rows(own):
        near = (own, swap_y(own), swap_x(own), swap_xy(own))
        return near, tuple(swap_core(chunk) for chunk in near)

    def reduce_rows(near, far):
        own, y, x, xy = kernel_call(
            core_sum_kernel,
            [((rows, width), f32)] + [((rows, width), bf16)] * 3,
            near,
            swap_core(far),
            name="core_sum",
        )
        return own, swap_y(y), swap_x(x), swap_xy(xy)

    attn_w = []
    mlp_w = []
    for l in range(depth):
        attn_own, mlp_own = kernel_call(
            functools.partial(pack_kernel, l, feats, hidden),
            [((width_own, 4 * feats), bf16), ((width_own, 2 * hidden), bf16)],
            w_qkv,
            w_out,
            w_fc1,
            w_fc2,
            name="pack",
            specs=[ANY] * 4,
            scratch=[
                pltpu.VMEM((3, width_own, feats), bf16),
                pltpu.VMEM((feats, width_own), bf16),
                pltpu.VMEM((width_own, hidden), bf16),
                pltpu.VMEM((hidden, width_own), bf16),
                pltpu.SemaphoreType.DMA((4,)),
            ],
        )
        attn_w.append(lax.all_gather(attn_own, "fsdp", axis=0, tiled=True))
        mlp_w.append(lax.all_gather(mlp_own, "fsdp", axis=0, tiled=True))

    qv_own = lax.dynamic_slice_in_dim(qv_bias, ci * heads, heads, axis=2)
    vec_rows = depth * 6
    c1_rows = depth * fc1_bias.shape[2] // width_own
    qv_own = qv_own.reshape(1, -1)
    small_own = jnp.concatenate(
        [
            norm_gains.reshape(-1, width_own),
            shifts.reshape(-1, width_own),
            fc1_bias.reshape(-1, width_own),
            jnp.pad(qv_own, ((0, 0), (0, width_own - qv_own.shape[1]))),
        ],
        axis=0,
    )
    shifted = [small_own] + [
        lax.ppermute(small_own, "fsdp", [(i, (i + d) % fsdp) for i in range(fsdp)])
        for d in range(1, fsdp)
    ]

    def shard(a):
        picked = shifted[0]
        for d in range(1, fsdp):
            picked = jnp.where((f - d) % fsdp == a, shifted[d], picked)
        return picked.astype(f32)

    shards = [shard(a) for a in range(fsdp)]
    vecs = jnp.concatenate([s[:vec_rows] for s in shards], axis=1)
    fc1_all = shard(ci)[vec_rows : vec_rows + c1_rows].reshape(depth, 1, hidden)
    qv_all = jnp.stack(
        [s[vec_rows + c1_rows, : qv_own.shape[1]].reshape(depth, 2, heads, head_own) for s in shards],
        axis=3,
    ).reshape(depth, 2, feats)

    def gain_row(l, i):
        return 2 * l + i

    def shift_row(l, i):
        return 2 * depth + 4 * l + i

    key_rows = outer * all_rows
    stream, first, upstream, upstream_b, usable, mask = kernel_call(
        functools.partial(prep_kernel, tp, outer, rows),
        [
            ((rows, width), f32),
            ((rows, width), bf16),
            ((rows, width), f32),
            ((rows, width), bf16),
            ((1, key_rows), f32),
            ((rows, 128), f32),
        ],
        lengths,
        inputs,
        cotangent,
        vecs,
        name="prep",
        specs=[pl.BlockSpec(memory_space=pltpu.SMEM), VMEM, VMEM, VMEM],
    )
    first_chunks = gather_rows(first)
    upstream_chunks = gather_rows(upstream_b)

    chunk_scratch = pltpu.VMEM((half, width), bf16)
    key_scratch = pltpu.VMEM((key_rows, feats), bf16)
    partial_out = ((half, width), bf16)
    saved_all = []
    for l in range(depth):
        qkv = [
            kernel_call(
                functools.partial(qkv_kernel, feats),
                [((half, 3 * feats), bf16)],
                *chunks,
                attn_w[l],
                qv_all[l],
                name="qkv",
                flops=2 * half * width * 3 * feats,
                scratch=[chunk_scratch],
            )[0]
            for chunks in first_chunks
        ]
        if outer > 1:
            pairs = jnp.concatenate([part[:, feats:] for part in qkv], axis=0)
            pairs = lax.all_gather(
                pairs, "ctx", axis=0, tiled=True, axis_index_groups=outer_groups
            )
            key_parts = (pairs,)
        else:
            key_parts = tuple(qkv)
        attn = [
            kernel_call(
                functools.partial(attn_kernel, feats, heads, len(key_parts), tile),
                [((half, feats), bf16), ((half, feats), f32), partial_out],
                qkv[side],
                *key_parts,
                attn_w[l],
                usable,
                name="attn",
                flops=2 * half * (width * feats + 4 * heads * key_rows * feats),
                scratch=[key_scratch, key_scratch],
            )
            for side in (1, 0)
        ][::-1]
        sums = reduce_rows(attn[0][2], attn[1][2])
        middle, second = kernel_call(
            functools.partial(sum_norm_kernel, shift_row(l, 2), gain_row(l, 1), shift_row(l, 1)),
            [((rows, width), f32), ((rows, width), bf16)],
            *sums,
            stream,
            vecs,
            name="sum_norm",
        )
        second_chunks = gather_rows(second)
        mlp = [
            kernel_call(
                functools.partial(mlp_kernel, hidden),
                [partial_out, ((half, hidden), bf16), ((half, hidden), f32)],
                *second_chunks[side],
                mlp_w[l],
                fc1_all[l],
                name="mlp",
                flops=4 * half * width * hidden,
                scratch=[chunk_scratch],
            )
            for side in (1, 0)
        ][::-1]
        sums = reduce_rows(mlp[0][0], mlp[1][0])
        saved_all.append(
            (stream, first_chunks, qkv, key_parts, attn, middle, second_chunks, mlp)
        )
        if l + 1 < depth:
            stream, first = kernel_call(
                functools.partial(
                    sum_norm_kernel, shift_row(l, 3), gain_row(l + 1, 0), shift_row(l + 1, 0)
                ),
                [((rows, width), f32), ((rows, width), bf16)],
                *sums,
                middle,
                vecs,
                name="sum_norm",
            )
            first_chunks = gather_rows(first)
        else:
            outputs_own = kernel_call(
                functools.partial(sum_out_kernel, shift_row(l, 3)),
                [((rows, width), f32)],
                *sums,
                middle,
                vecs,
                mask,
                name="sum_out",
            )[0]

    def both_halves(own):
        other = swap_y(own)
        return jnp.where(
            t == 0,
            jnp.concatenate([own, other], axis=0),
            jnp.concatenate([other, own], axis=0),
        )[None]

    outputs = both_halves(outputs_own)

    def reduce_grads(grad):
        part = lax.psum_scatter(grad, "fsdp", scatter_dimension=0, tiled=True)
        if outer > 1:
            part = lax.psum(part, "ctx", axis_index_groups=outer_groups)
        other = swap_x(part)
        return part, swap_core(part), other, swap_core(other)

    row_sums = [None] * depth
    unit_sums = [None] * depth
    head_sums = [None] * depth
    placed_mlp = None
    placed_attn = None
    for l in reversed(range(depth)):
        stream, first_chunks, qkv, key_parts, attn, middle, second_chunks, mlp = saved_all[l]
        back = [
            kernel_call(
                functools.partial(mlp_back_kernel, hidden),
                [partial_out, ((half, hidden), bf16), ((1, hidden), f32)],
                *upstream_chunks[side],
                mlp_w[l],
                mlp[side][2],
                name="mlp_back",
                flops=4 * half * width * hidden,
                scratch=[chunk_scratch],
            )
            for side in (1, 0)
        ][::-1]
        sums = reduce_rows(back[0][0], back[1][0])
        mlp_grad = kernel_call(
            functools.partial(grad_kernel, hidden),
            [((width, 2 * hidden), bf16)],
            *second_chunks[0],
            *second_chunks[1],
            *upstream_chunks[0],
            *upstream_chunks[1],
            back[0][1],
            back[1][1],
            mlp[0][1],
            mlp[1][1],
            name="mlp_grad",
            flops=4 * all_rows * width * hidden,
            scratch=[pltpu.VMEM((all_rows, width), bf16), pltpu.VMEM((all_rows, hidden), bf16)],
        )[0]
        pieces = reduce_grads(mlp_grad)
        placed_mlp = place_call(
            functools.partial(place_mlp_kernel, l, hidden),
            pieces,
            placed_mlp,
            [w_fc1.shape, w_fc2.shape],
            [(GROUP, width_own, hidden), (GROUP, hidden, width_own)],
            "place_mlp",
        )
        unit_sums[l] = back[0][2] + back[1][2]
        grad_middle, middle_b, sums_two = kernel_call(
            functools.partial(norm_back_two_kernel, gain_row(l, 1)),
            [((rows, width), f32), ((rows, width), bf16), ((4, width), f32)],
            *sums,
            middle,
            upstream,
            vecs,
            name="norm_back_two",
        )
        middle_chunks = gather_rows(middle_b)
        grad_q = [None, None]
        carried = ()
        for side in (0, 1):
            grad_q[side], *carried = kernel_call(
                functools.partial(
                    attn_back_kernel, feats, heads, len(key_parts), tile, len(carried) > 0
                ),
                [((half, feats), f32), ((key_rows, feats), f32), ((key_rows, feats), f32)],
                *middle_chunks[side],
                attn_w[l],
                qkv[side],
                attn[side][0],
                attn[side][1],
                usable,
                *key_parts,
                *carried,
                name="attn_back",
                flops=2 * half * (width * feats + 10 * heads * key_rows * feats),
                scratch=[chunk_scratch, key_scratch, key_scratch, pltpu.VMEM((half, feats), bf16)],
                limit=32,
            )
        grad_k, grad_v = carried
        if outer > 1:
            grad_k, grad_v = (
                lax.psum_scatter(
                    v, "ctx", scatter_dimension=0, tiled=True, axis_index_groups=outer_groups
                )
                for v in (grad_k, grad_v)
            )
        project = [
            kernel_call(
                functools.partial(project_kernel, feats, side * half),
                [((half, 3 * feats), bf16), partial_out, ((2, feats), f32)],
                grad_q[side],
                grad_k,
                grad_v,
                attn_w[l],
                name="project",
                flops=2 * half * width * 3 * feats,
            )
            for side in (1, 0)
        ][::-1]
        sums = reduce_rows(project[0][1], project[1][1])
        attn_grad = kernel_call(
            functools.partial(grad_kernel, 3 * feats),
            [((width, 4 * feats), bf16)],
            *first_chunks[0],
            *first_chunks[1],
            *middle_chunks[0],
            *middle_chunks[1],
            project[0][0],
            project[1][0],
            attn[0][0],
            attn[1][0],
            name="attn_grad",
            flops=2 * all_rows * width * 4 * feats,
            scratch=[
                pltpu.VMEM((all_rows, width), bf16),
                pltpu.VMEM((all_rows, 3 * feats), bf16),
            ],
        )[0]
        pieces = reduce_grads(attn_grad)
        placed_attn = place_call(
            functools.partial(place_attn_kernel, l, feats),
            pieces,
            placed_attn,
            [w_qkv.shape, w_out.shape],
            [(GROUP, 3, width_own, feats), (GROUP, feats, width_own)],
            "place_attn",
        )
        head_sums[l] = project[0][2] + project[1][2]
        back_outs = [((rows, width), f32), ((rows, width), bf16), ((2, width), f32)]
        if l > 0:
            upstream, upstream_b, sums_one = kernel_call(
                lambda *refs, row=gain_row(l, 0): norm_back_one_kernel(
                    row, *refs[:7], None, *refs[7:]
                ),
                back_outs,
                *sums,
                stream,
                grad_middle,
                vecs,
                name="norm_back_one",
            )[:3]
            upstream_chunks = gather_rows(upstream_b)
        else:
            grad_inputs_own, sums_one = kernel_call(
                lambda *refs, row=gain_row(l, 0): norm_back_one_kernel(
                    row, *refs[:8], refs[8], None, refs[9]
                ),
                [back_outs[0], back_outs[2]],
                *sums,
                stream,
                grad_middle,
                vecs,
                mask,
                name="norm_back_one",
            )
        row_sums[l] = (sums_one, sums_two)

    grad_inputs = both_halves(grad_inputs_own)

    vec_part = jnp.concatenate(
        [
            piece
            for l in range(depth)
            for piece in (
                row_sums[l][0][0:1],
                row_sums[l][1][0:1],
                row_sums[l][0][1:2],
                row_sums[l][1][1:4],
            )
        ],
        axis=0,
    )
    unit_part = jnp.concatenate(unit_sums, axis=0)
    head_part = jnp.concatenate(head_sums, axis=0)
    unit_lines = unit_part.reshape(-1, width)
    head_lines = head_part.reshape(1, -1)
    head_lines = jnp.pad(head_lines, ((0, 0), (0, width - head_lines.shape[1])))
    packed = jnp.concatenate([vec_part, unit_lines, head_lines], axis=0)
    if outer > 1:
        packed = lax.psum(packed, "ctx", axis_index_groups=outer_groups)
    step = 1
    while step < fsdp:
        packed = packed + lax.ppermute(packed, "fsdp", [(i, i ^ step) for i in range(fsdp)])
        step *= 2
    vec_sum = lax.dynamic_slice_in_dim(packed[:vec_rows], f * width_own, width_own, axis=1)
    rest = packed[vec_rows:]
    vec_sum = vec_sum + swap_y(vec_sum)
    rest_core = swap_core(rest)
    vec_sum = vec_sum + swap_core(vec_sum)
    rest_two = jnp.stack([rest, rest_core])
    vec_sum = vec_sum + swap_x(vec_sum)
    rest_four = jnp.concatenate([rest_two, swap_x(rest_two)], axis=0)
    vec_sum = vec_sum.reshape(depth, 6, width_own)
    unit_count = unit_lines.shape[0]

    def of_place(c):
        return lax.dynamic_index_in_dim(rest_four, ci ^ c, 0, keepdims=False)

    grad_fc1_bias = of_place(f)[:unit_count].reshape(depth, 1, hidden)
    grad_qv_bias = jnp.stack(
        [
            lax.dynamic_slice_in_dim(
                of_place(c)[unit_count, : head_part.size].reshape(depth, 2, heads, head_dim),
                f * head_own,
                head_own,
                axis=3,
            )
            for c in range(GROUP)
        ],
        axis=2,
    ).reshape(qv_bias.shape)
    return (
        outputs,
        grad_inputs,
        vec_sum[:, :2],
        vec_sum[:, 2:],
        grad_qv_bias,
        grad_fc1_bias,
        placed_attn[0],
        placed_attn[1],
        placed_mlp[0],
        placed_mlp[1],
    )


def solution(mesh):
    rows = P("fsdp", "ctx", None)
    params = (
        P(None, None, "fsdp"),
        P(None, None, "fsdp"),
        P(None, None, "tp", "fsdp"),
        P(None, "tp", "fsdp"),
        P(None, None, "fsdp", "tp"),
        P(None, "tp", "fsdp"),
        P(None, "fsdp", "tp"),
        P(None, "tp", "fsdp"),
    )
    return jax.shard_map(
        per_device,
        mesh=mesh,
        in_specs=(rows, P("fsdp", None), rows) + params,
        out_specs=(rows, rows) + params,
        check_vma=False,
    )
```

time: 731 us -> 419 us (0.57)
  waiting for transfers between devices: 345 us -> 97.7 us
  Pallas kernels: 0 us -> 70.9 us
  other arithmetic: 63.1 us -> 5.72 us
  matrix products: 55.1 us -> 0 us
  starting transfers between devices: 84.8 us -> 132 us
  local copies, waits for them, and re-layouts: 124 us -> 90.1 us
  blocking collectives: 31 us -> 0 us
    psum x1 -> x0, waiting for transfers between devices: 115 us -> none  [per_device(): packed = lax.psum(packed, ('fsdp', 'ctx', 'tp'))]
    reduce_scatter x4, waiting for transfers between devices: 75.5 us -> 0.05 us  [reduce_grads(): part = lax.psum_scatter(grad, 'fsdp', scatter_dimension=0, tiled=True)]
    pallas_call x0 -> x51, Pallas kernels: none -> 70.9 us  [the longest x47 60.5 us: kernel_call(): pl.pallas_call(body, out_shape=[jax.ShapeDtypeStruct(s, d) for s, d in ou...]
    dot_general x48 -> x0, matrix products: 55.1 us -> none  [the longest x16 24.8 us: dot(): lax.dot_general(a, b, (((1,), (0,)), ((), ())), preferred_element_type=f32)]
    all_gather x8 -> x4, waiting for transfers between devices: 61.7 us -> 11.6 us  [the longest x2 11.5 us: per_device(): mlp_w.append(lax.all_gather(mlp_own, 'fsdp', axis=0, tiled=True))]
    unnamed x259 -> x419, local copies, waits for them, and re-layouts: 34.4 us -> 83.2 us
    ppermute x16 -> x50, starting transfers between devices: 27 us -> 73.1 us  [swap_core(): return lax.ppermute(value, 'ctx', [(i, i ^ 1) for i in range(ctx)])]
    all_gather x3 -> x0, blocking collectives: 31 us -> none  [gather_small(): return lax.all_gather(value, 'fsdp', axis=axis, tiled=True)]
  transfers between devices with their start and end apart: 79 -> 120, of which waited for: 47 -> 42; matrix products, arithmetic and copies ran while one was open for 22% -> 3% of each run, Pallas kernels for 0% -> 14%
where the time goes in v2:
time: 419 us; the launch traced here: 413 us
  starting transfers between devices  132 us (32%)
  waiting for transfers between devices  97.7 us (23%)
  local copies, waits for them, and re-layouts  90.1 us (22%)
  Pallas kernels  70.9 us (17%)
  between operations  16.7 us (4%)
  other arithmetic  5.72 us (1%)
    unnamed x419, local copies, waits for them, and re-layouts  83.2 us
    ppermute x50, starting transfers between devices, swap_core(): return lax.ppermute(value, 'ctx', [(i, i ^ 1) for i in range(ctx)])  73.1 us
    pallas_call x47, Pallas kernels, kernel_call(): pl.pallas_call(body, out_shape=[jax.ShapeDtypeStruct(s, d) for s, d in ou...  60.5 us
    ppermute x16, waiting for transfers between devices, swap_xy(): return lax.ppermute(value, ('ctx', 'tp'), pairs)  31.9 us
    ppermute x19, waiting for transfers between devices, swap_y(): return lax.ppermute(value, 'tp', [(i, i ^ 1) for i in range(tp)])  23.5 us
    ppermute x22, waiting for transfers between devices, swap_x(): return lax.ppermute(value, 'ctx', [(i, i ^ 2) for i in range(ctx)])  20.9 us
    ppermute x16, starting transfers between devices, swap_xy(): return lax.ppermute(value, ('ctx', 'tp'), pairs)  20.7 us
    ppermute x22, starting transfers between devices, swap_x(): return lax.ppermute(value, 'ctx', [(i, i ^ 2) for i in range(ctx)])  15.7 us
  transfers between devices with their start and end apart: 120, of which 42 were waited for; matrix products, arithmetic and copies ran while one was open for 3% of the time, Pallas kernels for 14%

profile of v2, /device:TPU:9, one launch (start us, length us, event | category | flops | bytes accessed | tf_op | source)
XLA Modules:
  0.0 412.6 jit_solution(3559805463416068132)
XLA Ops:
  34.2 3.7 collective-permute-done.5.c3.refs_3_
  39.1 2.5 collective-permute-done.4.c2.refs_2_
  46.1 3.0 attn.5
  56.6 3.3 collective-permute-done.11.y
  60.7 3.5 collective-permute-done.13.xy
  70.8 3.5 collective-permute-start.20
  80.8 8.4 %all-gather.7.cloned.1.call-done.w = bf16[1024,1024]{1,0:T(8,128)(2,1)} async-done(((bf16[256,1024]{1,0:T(8,128)(2,1)}), bf16[1024,1024]{1,0:T(8,128)(2,1)}) %all-gather.7.cloned.1.call-update) | async-done | bytes 2097168 | tf_op jit(solution)/shard_map/all_gather | solution.py:461
  102.2 3.1 collective-permute-done.22.y
  106.0 3.6 collective-permute-done.24.xy
  117.0 3.9 collective-permute-start.31
  139.2 4.3 %collective-permute-done.35.xy = bf16[80,1024]{1,0:T(8,128)(2,1)S(1)} collective-permute-done((bf16[80,1024]{1,0:T(8,128)(2,1)S(1)}, bf16[80,1024]{1,0:T(8,128)(2,1)S(1)}, u32[]{:S(2)}, u32[]{:S(2)}) %collective-permute-start.35) | collective-permute-done | bytes 163872 | tf_op jit(solution)/shard_map/ppermute | solution.py:422
  149.6 2.9 collective-permute-start.39
  162.3 3.1 all-gather.11.cloned.1.call-done.w
  169.7 2.5 mlp.7
  173.8 2.2 mlp_back.5
  185.9 3.1 collective-permute-done.56.y
  189.9 3.5 collective-permute-done.58.xy
  200.0 3.7 collective-permute-start.65
  205.7 2.5 attn_back.4
  208.2 2.5 attn_back.5
  213.2 2.7 attn_grad.3
  226.4 3.3 mlp_grad.3
  237.6 2.9 collective-permute-done.67.refs_1_
  241.3 3.4 collective-permute-done.69.refs_3_
  251.0 2.4 collective-permute-start.73
  253.5 4.2 %collective-permute-start.76 = (bf16[80,1024]{1,0:T(8,128)(2,1)S(1)}, bf16[80,1024]{1,0:T(8,128)(2,1)S(1)}, u32[]{:S(2)}, u32[]{:S(2)}) collective-permute-start(bf16[80,1024]{1,0:T(8,128)(2,1)S(1)} %collective-permute-done.72.c3.refs_11_), channel_id=1, source_target_pairs={{0,2},{2,0},{4,6},{6,4},{1,3},{3,1},{5,7},{7,5},{8,10},{10,8},{12,... | collective-permute-start | bytes 491528 | tf_op jit(solution)/shard_map/ppermute | solution.py:410
  264.4 3.2 mlp_grad.2
  277.0 3.3 collective-permute-done.80.xy
  280.8 2.2 collective-permute-start.83
  283.5 2.4 collective-permute-start.84
  285.9 4.2 %collective-permute-start.87 = (bf16[80,1024]{1,0:T(8,128)(2,1)S(1)}, bf16[80,1024]{1,0:T(8,128)(2,1)S(1)}, u32[]{:S(2)}, u32[]{:S(2)}) collective-permute-start(bf16[80,1024]{1,0:T(8,128)(2,1)S(1)} %collective-permute-done.83.refs_3_.refs_11_), channel_id=1, source_target_pairs={{0,2},{2,0},{4,6},{6,4},{1,3},{3,1},{5,7},{7,5},{8,10},{10,8},{12,... | collective-permute-start | bytes 491528 | tf_op jit(solution)/shard_map/ppermute | solution.py:410
  293.9 2.5 attn_back.6
  296.6 2.5 attn_back.7
  308.4 3.4 collective-permute-done.46.xy
  329.7 2.3 attn_grad.2
  336.2 2.7 collective-permute-start.103
  339.0 3.4 collective-permute-start.105
  344.7 3.9 collective-permute-done.93
  352.6 2.4 place_attn.2
  355.8 3.8 collective-permute-start.109
  362.4 7.0 %collective-permute-done.95 = f32[12,256]{1,0:T(8,128)S(1)} collective-permute-done((f32[12,256]{1,0:T(8,128)S(1)}, f32[12,256]{1,0:T(8,128)S(1)}, u32[]{:S(2)}, u32[]{:S(2)}) %collective-permute-start.95) | collective-permute-done | bytes 12320 | tf_op jit(solution)/shard_map/ppermute | solution.py:416
  377.3 7.6 %collective-permute-done.107.p2 = bf16[256,1024]{1,0:T(8,128)(2,1)S(1)} collective-permute-done((bf16[256,1024]{1,0:T(8,128)(2,1)}, bf16[256,1024]{1,0:T(8,128)(2,1)S(1)}, u32[]{:S(2)}, u32[]{:S(2)}) %collective-permute-start.107) | collective-permute-done | bytes 524320 | tf_op jit(solution)/shard_map/ppermute | solution.py:413
  384.9 2.6 collective-permute-start.108
  387.6 3.0 collective-permute-done.101.p2
  395.2 2.2 maximum_select_fusion.1
  397.5 3.2 place_mlp.2
  400.7 2.6 place_attn.3
  403.4 2.2 place_mlp.3
  (740 shorter events, 236.0 us)
Async XLA Ops:
  7.2 36.0 %all-gather.5.cloned.1.call-start = ((), (), s32[]{:S(2)}) async-start(), calls=%async_computation.4 | async-start | bytes 1310720 | tf_op jit(solution)/shard_map/all_gather | solution.py:460
  14.2 75.1 %all-gather.7.cloned.1.call-start = ((), (), s32[]{:S(2)}) async-start(), calls=%async_computation.5 | async-start | bytes 2621440 | tf_op jit(solution)/shard_map/all_gather | solution.py:461
  14.9 107.8 %all-gather.9.cloned.1.call-start = ((), (), s32[]{:S(2)}) async-start(), calls=%async_computation.6 | async-start | bytes 1310720 | tf_op jit(solution)/shard_map/all_gather | solution.py:460
  15.2 9.3 %collective-permute-start.2 = (bf16[17,256]{1,0:T(8,128)(2,1)S(1)}, bf16[17,256]{1,0:T(8,128)(2,1)S(1)}, u32[]{:S(2)}, u32[]{:S(2)}) collective-permute-start(bf16[17,256]{1,0:T(8,128)(2,1)S(1)} %fusion.1), channel_id=1, source_target_pairs={{0,8},{8,16},{16,24},{24,0},{1,9},{9,17},{17,25},{25,1},{2,10},{10... | collective-permute-start | bytes 26120 | tf_op jit(solution)/shard_map/ppermute | solution.py:477
  24.4 141.0 %all-gather.11.cloned.1.call-start = ((), (), s32[]{:S(2)}) async-start(), calls=%async_computation.7 | async-start | bytes 2621440 | tf_op jit(solution)/shard_map/all_gather | solution.py:461
  29.6 15.3 %collective-permute-start.6 = (bf16[80,1024]{1,0:T(8,128)(2,1)S(1)}, bf16[80,1024]{1,0:T(8,128)(2,1)S(1)}, u32[]{:S(2)}, u32[]{:S(2)}) collective-permute-start(bf16[80,1024]{1,0:T(8,128)(2,1)S(1)} %get-tuple-element.137.c0.refs_0_), channel_id=1, source_target_pairs={{0,2},{2,0},{4,6},{6,4},{1,3},{3,1},{5,7},{7,5},{8,10},{10,8},{12,... | collective-permute-start | bytes 491528 | tf_op jit(solution)/shard_map/ppermute | solution.py:410
  33.6 8.7 %collective-permute-start.3 = (bf16[80,1024]{1,0:T(8,128)(2,1)S(1)}, bf16[80,1024]{1,0:T(8,128)(2,1)S(1)}, u32[]{:S(2)}, u32[]{:S(2)}) collective-permute-start(bf16[80,1024]{1,0:T(8,128)(2,1)S(1)} %get-tuple-element.137.c0.refs_0_), channel_id=1, source_target_pairs={{0,1},{1,0},{2,3},{3,2},{4,5},{5,4},{6,7},{7,6},{8,9},{9,8},{10,11... | collective-permute-start | bytes 491528 | tf_op jit(solution)/shard_map/ppermute | solution.py:416
  50.7 262.6 %reduce-scatter.7.cloned.1.call-start = ((), (), s32[]{:S(2)}) async-start(), calls=%async_computation.9 | async-start | bytes 1310720 | tf_op jit(solution)/shard_map/reduce_scatter | solution.py:623
  67.6 9.3 %collective-permute-start.14 = (bf16[80,1024]{1,0:T(8,128)(2,1)S(1)}, bf16[80,1024]{1,0:T(8,128)(2,1)S(1)}, u32[]{:S(2)}, u32[]{:S(2)}) collective-permute-start(bf16[80,1024]{1,0:T(8,128)(2,1)S(1)} %get-tuple-element.147.c0.refs_0_), channel_id=1, source_target_pairs={{0,1},{1,0},{2,3},{3,2},{4,5},{5,4},{6,7},{7,6},{8,9},{9,8},{10,11... | collective-permute-start | bytes 491528 | tf_op jit(solution)/shard_map/ppermute | solution.py:416
  67.9 10.3 %collective-permute-start.17 = (bf16[80,1024]{1,0:T(8,128)(2,1)S(1)}, bf16[80,1024]{1,0:T(8,128)(2,1)S(1)}, u32[]{:S(2)}, u32[]{:S(2)}) collective-permute-start(bf16[80,1024]{1,0:T(8,128)(2,1)S(1)} %get-tuple-element.147.c0.refs_0_), channel_id=1, source_target_pairs={{0,2},{2,0},{4,6},{6,4},{1,3},{3,1},{5,7},{7,5},{8,10},{10,8},{12,... | collective-permute-start | bytes 491528 | tf_op jit(solution)/shard_map/ppermute | solution.py:410
  113.7 9.0 %collective-permute-start.25 = (bf16[80,1024]{1,0:T(8,128)(2,1)}, bf16[80,1024]{1,0:T(8,128)(2,1)}, u32[]{:S(2)}, u32[]{:S(2)}) collective-permute-start(bf16[80,1024]{1,0:T(8,128)(2,1)} %get-tuple-element.156.c0.refs_0_), channel_id=1, source_target_pairs={{0,1},{1,0},{2,3},{3,2},{4,5},{5,4},{6,7},{7,6},{8,9},{9,8},{10,11... | collective-permute-start | bytes 491528 | tf_op jit(solution)/shard_map/ppermute | solution.py:416
  114.0 11.8 %collective-permute-start.28 = (bf16[80,1024]{1,0:T(8,128)(2,1)}, bf16[80,1024]{1,0:T(8,128)(2,1)}, u32[]{:S(2)}, u32[]{:S(2)}) collective-permute-start(bf16[80,1024]{1,0:T(8,128)(2,1)} %get-tuple-element.156.c0.refs_0_), channel_id=1, source_target_pairs={{0,2},{2,0},{4,6},{6,4},{1,3},{3,1},{5,7},{7,5},{8,10},{10,8},{12,... | collective-permute-start | bytes 491528 | tf_op jit(solution)/shard_map/ppermute | solution.py:410
  117.0 8.8 %collective-permute-start.31 = (bf16[80,1024]{1,0:T(8,128)(2,1)}, bf16[80,1024]{1,0:T(8,128)(2,1)}, u32[]{:S(2)}, u32[]{:S(2)}) collective-permute-start(bf16[80,1024]{1,0:T(8,128)(2,1)} %collective-permute-done.27.c3.refs_3_), channel_id=1, source_target_pairs={{0,2},{2,0},{4,6},{6,4},{1,3},{3,1},{5,7},{7,5},{8,10},{10,8},{12,... | collective-permute-start | bytes 491528 | tf_op jit(solution)/shard_map/ppermute | solution.py:410
  136.0 11.2 %collective-permute-start.50 = (bf16[80,1024]{1,0:T(8,128)(2,1)}, bf16[80,1024]{1,0:T(8,128)(2,1)}, u32[]{:S(2)}, u32[]{:S(2)}) collective-permute-start(bf16[80,1024]{1,0:T(8,128)(2,1)} %get-tuple-element.175.c0.refs_8_), channel_id=1, source_target_pairs={{0,5},{1,4},{2,7},{3,6},{4,1},{5,0},{6,3},{7,2},{8,13},{9,12},{10,... | collective-permute-start | bytes 491528 | tf_op jit(solution)/shard_map/ppermute | solution.py:422
  137.6 12.0 %collective-permute-start.49 = (bf16[80,1024]{1,0:T(8,128)(2,1)}, bf16[80,1024]{1,0:T(8,128)(2,1)}, u32[]{:S(2)}, u32[]{:S(2)}) collective-permute-start(bf16[80,1024]{1,0:T(8,128)(2,1)} %get-tuple-element.175.c0.refs_8_), channel_id=1, source_target_pairs={{0,4},{2,6},{4,0},{6,2},{1,5},{3,7},{5,1},{7,3},{8,12},{10,14},{12... | collective-permute-start | bytes 491528 | tf_op jit(solution)/shard_map/ppermute | solution.py:413
  144.5 9.6 %collective-permute-start.38 = (bf16[80,1024]{1,0:T(8,128)(2,1)S(1)}, bf16[80,1024]{1,0:T(8,128)(2,1)S(1)}, u32[]{:S(2)}, u32[]{:S(2)}) collective-permute-start(bf16[80,1024]{1,0:T(8,128)(2,1)S(1)} %get-tuple-element.165.c0.refs_0_), channel_id=1, source_target_pairs={{0,5},{1,4},{2,7},{3,6},{4,1},{5,0},{6,3},{7,2},{8,13},{9,12},{10,... | collective-permute-start | bytes 491528 | tf_op jit(solution)/shard_map/ppermute | solution.py:422
  145.7 11.0 %collective-permute-start.37 = (bf16[80,1024]{1,0:T(8,128)(2,1)S(1)}, bf16[80,1024]{1,0:T(8,128)(2,1)S(1)}, u32[]{:S(2)}, u32[]{:S(2)}) collective-permute-start(bf16[80,1024]{1,0:T(8,128)(2,1)S(1)} %get-tuple-element.165.c0.refs_0_), channel_id=1, source_target_pairs={{0,4},{2,6},{4,0},{6,2},{1,5},{3,7},{5,1},{7,3},{8,12},{10,14},{12... | collective-permute-start | bytes 491528 | tf_op jit(solution)/shard_map/ppermute | solution.py:413
  146.0 12.9 %collective-permute-start.36 = (bf16[80,1024]{1,0:T(8,128)(2,1)S(1)}, bf16[80,1024]{1,0:T(8,128)(2,1)}, u32[]{:S(2)}, u32[]{:S(2)}) collective-permute-start(bf16[80,1024]{1,0:T(8,128)(2,1)S(1)} %get-tuple-element.165.c0.refs_0_), channel_id=1, source_target_pairs={{0,1},{1,0},{2,3},{3,2},{4,5},{5,4},{6,7},{7,6},{8,9},{9,8},{10,11... | collective-permute-start | bytes 491528 | tf_op jit(solution)/shard_map/ppermute | solution.py:416
  147.2 11.7 %collective-permute-start.48 = (bf16[80,1024]{1,0:T(8,128)(2,1)}, bf16[80,1024]{1,0:T(8,128)(2,1)}, u32[]{:S(2)}, u32[]{:S(2)}) collective-permute-start(bf16[80,1024]{1,0:T(8,128)(2,1)} %get-tuple-element.175.c0.refs_8_), channel_id=1, source_target_pairs={{0,1},{1,0},{2,3},{3,2},{4,5},{5,4},{6,7},{7,6},{8,9},{9,8},{10,11... | collective-permute-start | bytes 491528 | tf_op jit(solution)/shard_map/ppermute | solution.py:416
  149.6 10.1 %collective-permute-start.39 = (bf16[80,1024]{1,0:T(8,128)(2,1)S(1)}, bf16[80,1024]{1,0:T(8,128)(2,1)S(1)}, u32[]{:S(2)}, u32[]{:S(2)}) collective-permute-start(bf16[80,1024]{1,0:T(8,128)(2,1)S(1)} %get-tuple-element.165.c0.refs_0_), channel_id=1, source_target_pairs={{0,2},{2,0},{4,6},{6,4},{1,3},{3,1},{5,7},{7,5},{8,10},{10,8},{12,... | collective-permute-start | bytes 491528 | tf_op jit(solution)/shard_map/ppermute | solution.py:410
  158.9 14.9 %collective-permute-start.51 = (bf16[80,1024]{1,0:T(8,128)(2,1)}, bf16[80,1024]{1,0:T(8,128)(2,1)}, u32[]{:S(2)}, u32[]{:S(2)}) collective-permute-start(bf16[80,1024]{1,0:T(8,128)(2,1)} %get-tuple-element.175.c0.refs_8_), channel_id=1, source_target_pairs={{0,2},{2,0},{4,6},{6,4},{1,3},{3,1},{5,7},{7,5},{8,10},{10,8},{12,... | collective-permute-start | bytes 491528 | tf_op jit(solution)/shard_map/ppermute | solution.py:410
  160.4 13.4 %collective-permute-start.54 = (bf16[80,1024]{1,0:T(8,128)(2,1)}, bf16[80,1024]{1,0:T(8,128)(2,1)}, u32[]{:S(2)}, u32[]{:S(2)}) collective-permute-start(bf16[80,1024]{1,0:T(8,128)(2,1)} %collective-permute-done.50.c3.refs_11_), channel_id=1, source_target_pairs={{0,2},{2,0},{4,6},{6,4},{1,3},{3,1},{5,7},{7,5},{8,10},{10,8},{12,... | collective-permute-start | bytes 491528 | tf_op jit(solution)/shard_map/ppermute | solution.py:410
  161.1 12.7 %collective-permute-start.53 = (bf16[80,1024]{1,0:T(8,128)(2,1)}, bf16[80,1024]{1,0:T(8,128)(2,1)}, u32[]{:S(2)}, u32[]{:S(2)}) collective-permute-start(bf16[80,1024]{1,0:T(8,128)(2,1)} %collective-permute-done.49.c2.refs_10_), channel_id=1, source_target_pairs={{0,2},{2,0},{4,6},{6,4},{1,3},{3,1},{5,7},{7,5},{8,10},{10,8},{12,... | collective-permute-start | bytes 491528 | tf_op jit(solution)/shard_map/ppermute | solution.py:410
  162.3 11.6 %collective-permute-start.52 = (bf16[80,1024]{1,0:T(8,128)(2,1)}, bf16[80,1024]{1,0:T(8,128)(2,1)}, u32[]{:S(2)}, u32[]{:S(2)}) collective-permute-start(bf16[80,1024]{1,0:T(8,128)(2,1)} %collective-permute-done.48.c1.refs_9_), channel_id=1, source_target_pairs={{0,2},{2,0},{4,6},{6,4},{1,3},{3,1},{5,7},{7,5},{8,10},{10,8},{12,... | collective-permute-start | bytes 491528 | tf_op jit(solution)/shard_map/ppermute | solution.py:410
  197.2 11.0 %collective-permute-start.62 = (bf16[80,1024]{1,0:T(8,128)(2,1)S(1)}, bf16[80,1024]{1,0:T(8,128)(2,1)S(1)}, u32[]{:S(2)}, u32[]{:S(2)}) collective-permute-start(bf16[80,1024]{1,0:T(8,128)(2,1)S(1)} %get-tuple-element.185.refs_0_.refs_8_), channel_id=1, source_target_pairs={{0,2},{2,0},{4,6},{6,4},{1,3},{3,1},{5,7},{7,5},{8,10},{10,8},{12,... | collective-permute-start | bytes 491528 | tf_op jit(solution)/shard_map/ppermute | solution.py:410
  216.9 138.1 %reduce-scatter.11.cloned.1.call-start = ((), (), s32[]{:S(2)}) async-start(), calls=%async_computation.11 | async-start | bytes 2621440 | tf_op jit(solution)/shard_map/reduce_scatter | solution.py:623
  231.0 140.8 %reduce-scatter.9.cloned.1.call-start = ((), (), s32[]{:S(2)}) async-start(), calls=%async_computation.10 | async-start | bytes 2621440 | tf_op jit(solution)/shard_map/reduce_scatter | solution.py:623
  251.0 10.9 %collective-permute-start.73 = (bf16[80,1024]{1,0:T(8,128)(2,1)S(1)}, bf16[80,1024]{1,0:T(8,128)(2,1)S(1)}, u32[]{:S(2)}, u32[]{:S(2)}) collective-permute-start(bf16[80,1024]{1,0:T(8,128)(2,1)S(1)} %get-tuple-element.203.c0.refs_8_), channel_id=1, source_target_pairs={{0,2},{2,0},{4,6},{6,4},{1,3},{3,1},{5,7},{7,5},{8,10},{10,8},{12,... | collective-permute-start | bytes 491528 | tf_op jit(solution)/shard_map/ppermute | solution.py:410
  267.6 105.9 %reduce-scatter.5.cloned.1.call-start = ((), (), s32[]{:S(2)}) async-start(), calls=%async_computation.8 | async-start | bytes 1310720 | tf_op jit(solution)/shard_map/reduce_scatter | solution.py:623
  273.2 28.5 %collective-permute-start.43 = (bf16[320,1024]{1,0:T(8,128)(2,1)}, bf16[320,1024]{1,0:T(8,128)(2,1)S(1)}, u32[]{:S(2)}, u32[]{:S(2)}) collective-permute-start(bf16[320,1024]{1,0:T(8,128)(2,1)} %copy-done.184), channel_id=1, source_target_pairs={{0,2},{2,0},{4,6},{6,4},{1,3},{3,1},{5,7},{7,5},{8,10},{10,8},{12,... | collective-permute-start | bytes 1966088 | tf_op jit(solution)/shard_map/ppermute | solution.py:410
  283.5 13.0 %collective-permute-start.84 = (bf16[80,1024]{1,0:T(8,128)(2,1)S(1)}, bf16[80,1024]{1,0:T(8,128)(2,1)S(1)}, u32[]{:S(2)}, u32[]{:S(2)}) collective-permute-start(bf16[80,1024]{1,0:T(8,128)(2,1)S(1)} %get-tuple-element.213.refs_0_.refs_8_), channel_id=1, source_target_pairs={{0,2},{2,0},{4,6},{6,4},{1,3},{3,1},{5,7},{7,5},{8,10},{10,8},{12,... | collective-permute-start | bytes 491528 | tf_op jit(solution)/shard_map/ppermute | solution.py:410
  285.9 10.6 %collective-permute-start.87 = (bf16[80,1024]{1,0:T(8,128)(2,1)S(1)}, bf16[80,1024]{1,0:T(8,128)(2,1)S(1)}, u32[]{:S(2)}, u32[]{:S(2)}) collective-permute-start(bf16[80,1024]{1,0:T(8,128)(2,1)S(1)} %collective-permute-done.83.refs_3_.refs_11_), channel_id=1, source_target_pairs={{0,2},{2,0},{4,6},{6,4},{1,3},{3,1},{5,7},{7,5},{8,10},{10,8},{12,... | collective-permute-start | bytes 491528 | tf_op jit(solution)/shard_map/ppermute | solution.py:410
  301.3 30.8 %collective-permute-start.88 = (bf16[320,1024]{1,0:T(8,128)(2,1)}, bf16[320,1024]{1,0:T(8,128)(2,1)}, u32[]{:S(2)}, u32[]{:S(2)}) collective-permute-start(bf16[320,1024]{1,0:T(8,128)(2,1)} %get-tuple-element.225), channel_id=1, source_target_pairs={{0,2},{2,0},{4,6},{6,4},{1,3},{3,1},{5,7},{7,5},{8,10},{10,8},{12,... | collective-permute-start | bytes 1966088 | tf_op jit(solution)/shard_map/ppermute | solution.py:410
  311.9 38.7 %collective-permute-start.47 = (f32[80,1024]{1,0:T(8,128)S(1)}, f32[80,1024]{1,0:T(8,128)}, u32[]{:S(2)}, u32[]{:S(2)}) collective-permute-start(f32[80,1024]{1,0:T(8,128)S(1)} %sum_out.1), channel_id=1, source_target_pairs={{0,1},{1,0},{2,3},{3,2},{4,5},{5,4},{6,7},{7,6},{8,9},{9,8},{10,11... | collective-permute-start | bytes 983048 | tf_op jit(solution)/shard_map/ppermute | solution.py:416
  313.3 22.9 %collective-permute-start.104 = (bf16[256,512]{1,0:T(8,128)(2,1)}, bf16[256,512]{1,0:T(8,128)(2,1)}, u32[]{:S(2)}, u32[]{:S(2)}) collective-permute-start(bf16[256,512]{1,0:T(8,128)(2,1)} %reduce-scatter.7.cloned.1.call-done.p0), channel_id=1, source_target_pairs={{0,4},{2,6},{4,0},{6,2},{1,5},{3,7},{5,1},{7,3},{8,12},{10,14},{12... | collective-permute-start | bytes 786440 | tf_op jit(solution)/shard_map/ppermute | solution.py:413
  336.2 16.4 %collective-permute-start.103 = (bf16[256,512]{1,0:T(8,128)(2,1)S(1)}, bf16[256,512]{1,0:T(8,128)(2,1)S(1)}, u32[]{:S(2)}, u32[]{:S(2)}) collective-permute-start(bf16[256,512]{1,0:T(8,128)(2,1)S(1)} %copy-done.124), channel_id=1, source_target_pairs={{0,2},{2,0},{4,6},{6,4},{1,3},{3,1},{5,7},{7,5},{8,10},{10,8},{12,... | collective-permute-start | bytes 786440 | tf_op jit(solution)/shard_map/ppermute | solution.py:410
  339.0 13.6 %collective-permute-start.105 = (bf16[256,512]{1,0:T(8,128)(2,1)}, bf16[256,512]{1,0:T(8,128)(2,1)S(1)}, u32[]{:S(2)}, u32[]{:S(2)}) collective-permute-start(bf16[256,512]{1,0:T(8,128)(2,1)} %collective-permute-done.104.p2), channel_id=1, source_target_pairs={{0,2},{2,0},{4,6},{6,4},{1,3},{3,1},{5,7},{7,5},{8,10},{10,8},{12,... | collective-permute-start | bytes 786440 | tf_op jit(solution)/shard_map/ppermute | solution.py:410
  348.6 12.0 %collective-permute-start.94 = (f32[14,1024]{1,0:T(8,128)S(1)}, f32[14,1024]{1,0:T(8,128)S(1)}, u32[]{:S(2)}, u32[]{:S(2)}) collective-permute-start(f32[14,1024]{1,0:T(8,128)S(1)} %add.104), channel_id=1, source_target_pairs={{0,16},{8,24},{16,0},{24,8},{1,17},{9,25},{17,1},{25,9},{2,18},{10... | collective-permute-start | bytes 172040 | tf_op jit(solution)/shard_map/ppermute | solution.py:810
  355.0 20.2 %collective-permute-start.110 = (bf16[256,1024]{1,0:T(8,128)(2,1)}, bf16[256,1024]{1,0:T(8,128)(2,1)S(1)}, u32[]{:S(2)}, u32[]{:S(2)}) collective-permute-start(bf16[256,1024]{1,0:T(8,128)(2,1)} %reduce-scatter.11.cloned.1.call-done.p0), channel_id=1, source_target_pairs={{0,4},{2,6},{4,0},{6,2},{1,5},{3,7},{5,1},{7,3},{8,12},{10,14},{12... | collective-permute-start | bytes 1572872 | tf_op jit(solution)/shard_map/ppermute | solution.py:413
  355.8 31.8 %collective-permute-start.109 = (bf16[256,1024]{1,0:T(8,128)(2,1)}, bf16[256,1024]{1,0:T(8,128)(2,1)S(1)}, u32[]{:S(2)}, u32[]{:S(2)}) collective-permute-start(bf16[256,1024]{1,0:T(8,128)(2,1)} %reduce-scatter.11.cloned.1.call-done.p0), channel_id=1, source_target_pairs={{0,2},{2,0},{4,6},{6,4},{1,3},{3,1},{5,7},{7,5},{8,10},{10,8},{12,... | collective-permute-start | bytes 1572872 | tf_op jit(solution)/shard_map/ppermute | solution.py:410
  359.6 17.6 %collective-permute-start.92 = (f32[80,1024]{1,0:T(8,128)S(1)}, f32[80,1024]{1,0:T(8,128)}, u32[]{:S(2)}, u32[]{:S(2)}) collective-permute-start(f32[80,1024]{1,0:T(8,128)S(1)} %get-tuple-element.231), channel_id=1, source_target_pairs={{0,1},{1,0},{2,3},{3,2},{4,5},{5,4},{6,7},{7,6},{8,9},{9,8},{10,11... | collective-permute-start | bytes 983048 | tf_op jit(solution)/shard_map/ppermute | solution.py:416
  371.8 13.1 %collective-permute-start.107 = (bf16[256,1024]{1,0:T(8,128)(2,1)}, bf16[256,1024]{1,0:T(8,128)(2,1)S(1)}, u32[]{:S(2)}, u32[]{:S(2)}) collective-permute-start(bf16[256,1024]{1,0:T(8,128)(2,1)} %reduce-scatter.9.cloned.1.call-done.p0), channel_id=1, source_target_pairs={{0,4},{2,6},{4,0},{6,2},{1,5},{3,7},{5,1},{7,3},{8,12},{10,14},{12... | collective-permute-start | bytes 1572872 | tf_op jit(solution)/shard_map/ppermute | solution.py:413
  373.5 17.1 %collective-permute-start.101 = (bf16[256,512]{1,0:T(8,128)(2,1)}, bf16[256,512]{1,0:T(8,128)(2,1)}, u32[]{:S(2)}, u32[]{:S(2)}) collective-permute-start(bf16[256,512]{1,0:T(8,128)(2,1)} %reduce-scatter.5.cloned.1.call-done.p0), channel_id=1, source_target_pairs={{0,4},{2,6},{4,0},{6,2},{1,5},{3,7},{5,1},{7,3},{8,12},{10,14},{12... | collective-permute-start | bytes 786440 | tf_op jit(solution)/shard_map/ppermute | solution.py:413
  375.2 22.2 %collective-permute-start.111 = (bf16[256,1024]{1,0:T(8,128)(2,1)S(1)}, bf16[256,1024]{1,0:T(8,128)(2,1)}, u32[]{:S(2)}, u32[]{:S(2)}) collective-permute-start(bf16[256,1024]{1,0:T(8,128)(2,1)S(1)} %collective-permute-done.110.p2), channel_id=1, source_target_pairs={{0,2},{2,0},{4,6},{6,4},{1,3},{3,1},{5,7},{7,5},{8,10},{10,8},{12,... | collective-permute-start | bytes 1572872 | tf_op jit(solution)/shard_map/ppermute | solution.py:410
  377.2 26.2 %collective-permute-start.106 = (bf16[256,1024]{1,0:T(8,128)(2,1)}, bf16[256,1024]{1,0:T(8,128)(2,1)S(1)}, u32[]{:S(2)}, u32[]{:S(2)}) collective-permute-start(bf16[256,1024]{1,0:T(8,128)(2,1)} %reduce-scatter.9.cloned.1.call-done.p0), channel_id=1, source_target_pairs={{0,2},{2,0},{4,6},{6,4},{1,3},{3,1},{5,7},{7,5},{8,10},{10,8},{12,... | collective-permute-start | bytes 1572872 | tf_op jit(solution)/shard_map/ppermute | solution.py:410
  384.9 18.5 %collective-permute-start.108 = (bf16[256,1024]{1,0:T(8,128)(2,1)S(1)}, bf16[256,1024]{1,0:T(8,128)(2,1)S(1)}, u32[]{:S(2)}, u32[]{:S(2)}) collective-permute-start(bf16[256,1024]{1,0:T(8,128)(2,1)S(1)} %collective-permute-done.107.p2), channel_id=1, source_target_pairs={{0,2},{2,0},{4,6},{6,4},{1,3},{3,1},{5,7},{7,5},{8,10},{10,8},{12,... | collective-permute-start | bytes 1572872 | tf_op jit(solution)/shard_map/ppermute | solution.py:410
  387.6 13.1 %collective-permute-start.100 = (bf16[256,512]{1,0:T(8,128)(2,1)}, bf16[256,512]{1,0:T(8,128)(2,1)}, u32[]{:S(2)}, u32[]{:S(2)}) collective-permute-start(bf16[256,512]{1,0:T(8,128)(2,1)} %reduce-scatter.5.cloned.1.call-done.p0), channel_id=1, source_target_pairs={{0,2},{2,0},{4,6},{6,4},{1,3},{3,1},{5,7},{7,5},{8,10},{10,8},{12,... | collective-permute-start | bytes 786440 | tf_op jit(solution)/shard_map/ppermute | solution.py:410
  390.6 10.1 %collective-permute-start.102 = (bf16[256,512]{1,0:T(8,128)(2,1)}, bf16[256,512]{1,0:T(8,128)(2,1)}, u32[]{:S(2)}, u32[]{:S(2)}) collective-permute-start(bf16[256,512]{1,0:T(8,128)(2,1)} %collective-permute-done.101.p2), channel_id=1, source_target_pairs={{0,2},{2,0},{4,6},{6,4},{1,3},{3,1},{5,7},{7,5},{8,10},{10,8},{12,... | collective-permute-start | bytes 786440 | tf_op jit(solution)/shard_map/ppermute | solution.py:410
  (278 other events, 1728.5 us)
Sparse Core Ops, SparseCore 0:
  14.3 28.8 all-gather.4
  45.3 43.8 all-gather.6
  91.4 28.1 all-gather.8
  121.5 43.8 all-gather.10
  217.0 24.7 reduce-scatter.6
  244.7 42.0 reduce-scatter.10
  289.7 43.1 reduce-scatter.8
  335.3 30.9 reduce-scatter.4

commit v3 on v2

v3 whole, which is shorter than its diff:
```python
import functools
import math

import jax
import jax.numpy as jnp
from jax import lax
from jax.experimental import pallas as pl
from jax.experimental.pallas import tpu as pltpu
from jax.sharding import PartitionSpec as P

NORM_EPSILON = 1e-06
MASK_FILL = -1e30
ROOT_HALF = 0.7071067811865476
INV_ROOT_TAU = 0.3989422804014327
GROUP = 4
ORDER = (0, 1, 4, 5, 2, 3, 6, 7)
CHIPS = 4

bf16 = jnp.bfloat16
f32 = jnp.float32
VMEM = pl.BlockSpec(memory_space=pltpu.VMEM)
SMEM = pl.BlockSpec(memory_space=pltpu.SMEM)
HBM = pl.BlockSpec(memory_space=pltpu.HBM)
DMA = pltpu.SemaphoreType.DMA
TOKEN = ((8, 128), f32)


def dot(a, b):
    return lax.dot_general(a, b, (((1,), (0,)), ((), ())), preferred_element_type=f32)


def dot_nt(a, b):
    return lax.dot_general(a, b, (((1,), (1,)), ((), ())), preferred_element_type=f32)


def dot_tn(a, b):
    return lax.dot_general(a, b, (((0,), (0,)), ((), ())), preferred_element_type=f32)


class Far:
    def __init__(self, value):
        self.value = value


class Scalars:
    def __init__(self, value):
        self.value = value


def saved(shape, dtype):
    return pltpu.HBM(shape, dtype)


def kernel_call(body, outs, *args, name, limit=12, scratch=(), after=(), aliases=None):
    values, specs = [], []
    for arg in (*args, *after):
        if isinstance(arg, Far):
            values.append(pltpu.with_memory_space_constraint(arg.value, pltpu.HBM))
            specs.append(HBM)
        elif isinstance(arg, Scalars):
            values.append(arg.value)
            specs.append(SMEM)
        else:
            values.append(arg)
            specs.append(VMEM)
    first, last = len(args), len(args) + len(after)

    def run(*refs):
        body(*refs[:first], *refs[last:])

    out_shape, out_specs = [], []
    for out in outs:
        if isinstance(out, tuple):
            out_shape.append(jax.ShapeDtypeStruct(*out))
            out_specs.append(VMEM)
        else:
            out_shape.append(out)
            out_specs.append(HBM)
    return pl.pallas_call(
        run,
        out_shape=out_shape,
        in_specs=specs,
        out_specs=out_specs,
        scratch_shapes=list(scratch),
        input_output_aliases=aliases or {},
        compiler_params=pltpu.CompilerParams(vmem_limit_bytes=limit << 20),
        cost_estimate=pl.CostEstimate(flops=0, bytes_accessed=0, transcendentals=0),
        name=name,
    )(*values)


def start_copies(pairs, sems):
    copies = [
        pltpu.make_async_copy(source, target, sems.at[k])
        for k, (source, target) in enumerate(pairs)
    ]
    for copy in copies:
        copy.start()
    return copies


def row_mean(value):
    return jnp.mean(value, axis=-1, keepdims=True)


def normalize(values):
    center = values - row_mean(values)
    inverse = lax.rsqrt(row_mean(center * center) + NORM_EPSILON)
    return center * inverse, inverse


def lanes_of(head, head_dim, width):
    lane = lax.broadcasted_iota(jnp.int32, (1, width), 1)
    return (lane >= head * head_dim) & (lane < (head + 1) * head_dim)


def assemble(chunks, target):
    rows = chunks[0].shape[0]
    for k, chunk in enumerate(chunks):
        target[k * rows : (k + 1) * rows, :] = chunk[...]


def only(flag, value):
    return jnp.where(flag, value, jnp.zeros_like(value))


def shards(weights):
    if len(weights) == 1:
        rows = weights[0].shape[0]
        return [(pl.ds(0, rows), weights[0])]
    count = len(weights)
    rows = weights[0].shape[0]
    f = lax.axis_index("fsdp")
    found = []
    for d, ref in enumerate(weights):
        place = lax.rem(f + (count - d), count)
        found.append((pl.ds(pl.multiple_of(place * rows, rows), rows), ref))
    return found


def pack_attn_kernel(layer, feats, qkv_hbm, out_hbm, packed_ref, qkv, out, sems):
    ci = lax.rem(lax.axis_index("ctx"), GROUP)
    span = pl.ds(pl.multiple_of(ci * feats, feats), feats)
    copies = start_copies(
        [(qkv_hbm.at[layer, :, :, span], qkv), (out_hbm.at[layer, span, :], out)], sems
    )
    copies[0].wait()
    for k in range(3):
        packed_ref[:, k * feats : (k + 1) * feats] = qkv[k]
    copies[1].wait()
    packed_ref[:, 3 * feats :] = out[...].T


def pack_mlp_kernel(layer, hidden, fc1_hbm, fc2_hbm, packed_ref, fc1, fc2, sems):
    ci = lax.rem(lax.axis_index("ctx"), GROUP)
    span = pl.ds(pl.multiple_of(ci * hidden, hidden), hidden)
    copies = start_copies(
        [(fc1_hbm.at[layer, :, span], fc1), (fc2_hbm.at[layer, span, :], fc2)], sems
    )
    copies[0].wait()
    packed_ref[:, :hidden] = fc1[...]
    copies[1].wait()
    packed_ref[:, hidden:] = fc2[...].T


def prep_upstream_kernel(tp, outer, lengths, cotangent_hbm,
                         upstream_ref, upstream_b_ref, usable_ref, mask_ref, rows_in, sems):
    rows = rows_in.shape[0]
    c = lax.axis_index("ctx")
    t = lax.axis_index("tp")
    place = lax.rem(c, GROUP) * tp + t
    start = pl.multiple_of(t * rows, rows)
    copies = start_copies([(cotangent_hbm.at[0, pl.ds(start, rows), :], rows_in)], sems)
    lane = lax.broadcasted_iota(jnp.int32, usable_ref.shape, 1)
    limit = jnp.zeros(usable_ref.shape, jnp.int32)
    for o in range(outer):
        for k, d in enumerate(ORDER):
            source = place ^ d
            first_lane = (o * len(ORDER) + k) * rows
            count = lengths[0, o * GROUP + lax.div(source, tp)] - lax.rem(source, tp) * rows
            limit = jnp.where(lane >= first_lane, first_lane + jnp.clip(count, 0, rows), limit)
    usable_ref[...] = jnp.where(lane < limit, 1.0, 0.0)
    row = lax.broadcasted_iota(jnp.int32, mask_ref.shape, 0)
    mask = jnp.where(row + start < lengths[0, c], 1.0, 0.0)
    mask_ref[...] = mask
    copies[0].wait()
    upstream = rows_in[...] * mask[:, 0:1]
    upstream_ref[...] = upstream
    upstream_b_ref[...] = upstream.astype(bf16)


def prep_first_kernel(depth, inputs_hbm, vecs, stream_ref, first_ref, sems):
    rows = stream_ref.shape[0]
    start = pl.multiple_of(lax.axis_index("tp") * rows, rows)
    copies = start_copies([(inputs_hbm.at[0, pl.ds(start, rows), :], stream_ref)], sems)
    copies[0].wait()
    normed, _ = normalize(stream_ref[...])
    shift = vecs[2 * depth : 2 * depth + 1, :]
    first_ref[...] = (normed * vecs[0:1, :] + shift).astype(bf16)


def keep_rows_kernel(*refs):
    chunks, (near_hbm, far_hbm, token, near, far, sems) = refs[:8], refs[8:]
    assemble(chunks[:4], near)
    assemble(chunks[4:], far)
    for copy in start_copies([(near, near_hbm), (far, far_hbm)], sems):
        copy.wait()
    token[...] = jnp.zeros_like(token)


def qkv_kernel(feats, weight_count, *refs):
    c0, c1, c2, c3, *rest = refs
    weights = rest[:weight_count]
    bias, qkv_ref, x = rest[weight_count:]
    assemble((c0, c1, c2, c3), x)
    qkv = sum(dot(x[:, span], w[:, : 3 * feats]) for span, w in shards(weights))
    qkv_ref[:, :feats] = (qkv[:, :feats] + bias[0:1, :]).astype(bf16)
    qkv_ref[:, feats : 2 * feats] = qkv[:, feats : 2 * feats].astype(bf16)
    qkv_ref[:, 2 * feats :] = (qkv[:, 2 * feats :] + bias[1:2, :]).astype(bf16)


def attn_kernel(feats, heads, weight_count, part_count, keep_count, tile, *refs):
    q_ref, *rest = refs
    parts = rest[:part_count]
    weights = rest[part_count : part_count + weight_count]
    rest = rest[part_count + weight_count :]
    usable, *rest = rest
    kept, rest = rest[:keep_count], rest[keep_count:]
    partial_ref, attended_hbm, norm_hbm, *rest = rest
    kept_hbm, rest = rest[:keep_count], rest[keep_count:]
    keys, values, attended_ref, norm_ref, sems = rest
    head_dim = feats // heads
    scale = 1.0 / math.sqrt(head_dim)
    copies = start_copies(list(zip(kept, kept_hbm)), sems)
    first = 0
    for part in parts:
        rows, width = part.shape
        keys[first : first + rows, :] = part[:, width - 2 * feats : width - feats]
        values[first : first + rows, :] = part[:, width - feats :]
        first += rows
    keep = usable[...] > 0.5
    rows = q_ref.shape[0]
    for first in range(0, rows, tile):
        span = slice(first, first + tile)
        q = q_ref[span, :feats]
        attended = None
        for h in range(heads):
            own = lanes_of(h, head_dim, feats)
            scores = dot_nt(only(own, q), keys[...]) * scale
            scores = jnp.where(keep, scores, MASK_FILL)
            highest = jnp.max(scores, axis=-1, keepdims=True)
            raised = jnp.exp(scores - highest)
            total = jnp.sum(raised, axis=-1, keepdims=True)
            soft = (raised * (1.0 / total)).astype(bf16)
            result = dot(soft, values[...])
            log_norm = jnp.broadcast_to(highest + jnp.log(total), (tile, feats))
            if attended is None:
                attended, norms = result, log_norm
            else:
                attended = jnp.where(own, result, attended)
                norms = jnp.where(own, log_norm, norms)
        attended_ref[span, :] = attended.astype(bf16)
        norm_ref[span, :] = norms
    copies += start_copies(
        [(attended_ref, attended_hbm), (norm_ref, norm_hbm)],
        sems.at[pl.ds(keep_count, 2)],
    )
    for span, w in shards(weights):
        partial_ref[:, span] = dot_nt(attended_ref[...], w[:, 3 * feats :]).astype(bf16)
    for copy in copies:
        copy.wait()


def core_sum_kernel(near, far, own_ref, y_ref, x_ref, xy_ref):
    rows = own_ref.shape[0]
    for k, ref in enumerate((own_ref, y_ref, x_ref, xy_ref)):
        span = slice(k * rows, (k + 1) * rows)
        ref[...] = (near[span, :].astype(f32) + far[span, :].astype(f32)).astype(ref.dtype)


def total_of(own, y, x, xy):
    return own[...] + y[...].astype(f32) + x[...].astype(f32) + xy[...].astype(f32)


def sum_norm_kernel(bias_row, gain_row, shift_row, own, y, x, xy, residual, vecs,
                    stream_ref, normed_ref):
    stream = residual[...] + total_of(own, y, x, xy) + vecs[bias_row : bias_row + 1, :]
    stream_ref[...] = stream
    normed, _ = normalize(stream)
    gain = vecs[gain_row : gain_row + 1, :]
    normed_ref[...] = (normed * gain + vecs[shift_row : shift_row + 1, :]).astype(bf16)


def sum_out_kernel(bias_row, own, y, x, xy, residual, vecs, mask, out_ref):
    stream = residual[...] + total_of(own, y, x, xy) + vecs[bias_row : bias_row + 1, :]
    out_ref[...] = stream * mask[:, 0:1]


def mlp_kernel(hidden, keep_count, c0, c1, c2, c3, w, bias, *refs):
    kept, rest = refs[:keep_count], refs[keep_count:]
    partial_ref, x_hbm, act_hbm, slope_hbm, *rest = rest
    kept_hbm, (x, act_ref, slope_ref, sems) = rest[:keep_count], rest[keep_count:]
    assemble((c0, c1, c2, c3), x)
    copies = start_copies([(x, x_hbm), *zip(kept, kept_hbm)], sems)
    block = hidden // 2
    for k in range(2):
        span = slice(k * block, (k + 1) * block)
        pre = dot(x[...], w[:, span]) + bias[:, span]
        cdf = 0.5 * (1.0 + lax.erf(pre * ROOT_HALF))
        density = jnp.exp(-0.5 * pre * pre) * INV_ROOT_TAU
        slope_ref[k] = cdf + pre * density
        act_ref[:, span] = (pre * cdf).astype(bf16)
        copies += start_copies(
            [(slope_ref.at[k], slope_hbm.at[k])], sems.at[pl.ds(1 + keep_count + k, 1)]
        )
    copies += start_copies([(act_ref, act_hbm)], sems.at[pl.ds(3 + keep_count, 1)])
    partial_ref[...] = dot_nt(act_ref[...], w[:, hidden:]).astype(bf16)
    for copy in copies:
        copy.wait()


def mlp_back_kernel(hidden, chunk_count, *refs):
    chunks, (w, slope_hbm, *rest) = refs[:chunk_count], refs[chunk_count:]
    partial_ref, grad_ref, sum_ref, x, slope, sems = rest
    copies = start_copies([(slope_hbm, slope)], sems)
    if chunk_count == 1:
        copies += start_copies([(chunks[0], x)], sems.at[pl.ds(1, 1)])
        copies[1].wait()
    else:
        assemble(chunks, x)
    grad = dot(x[...], w[:, hidden:])
    copies[0].wait()
    block = hidden // 2
    for k in range(2):
        span = slice(k * block, (k + 1) * block)
        part = grad[:, span] * slope[k]
        grad_ref[:, span] = part.astype(bf16)
        sum_ref[:, span] = jnp.sum(part, axis=0, keepdims=True)
    partial_ref[...] = dot_nt(grad_ref[...], w[:, :hidden]).astype(bf16)


def mlp_grad_kernel(hidden, second_near, second_far, act_near, act_far, up_near, up_far,
                    grad_near, grad_far, out_ref, token, second, act, up, grad, sems):
    rows = up_near.shape[0]
    near, far = pl.ds(0, rows), pl.ds(rows, rows)
    copies = start_copies(
        [
            (second_near, second.at[near]),
            (second_far, second.at[far]),
            (act_near, act.at[near]),
            (act_far, act.at[far]),
        ],
        sems,
    )
    up[:rows, :] = up_near[...]
    up[rows:, :] = up_far[...]
    grad[:rows, :] = grad_near[...]
    grad[rows:, :] = grad_far[...]
    for copy in copies:
        copy.wait()
    out_ref[:, hidden:] = dot_tn(up[...], act[...]).astype(bf16)
    out_ref[:, :hidden] = dot_tn(second[...], grad[...]).astype(bf16)
    token[...] = jnp.zeros_like(token)


def norm_back(upstream, values, gain):
    normed, inverse = normalize(values)
    scaled = upstream * gain
    back = inverse * (scaled - row_mean(scaled) - normed * row_mean(scaled * normed))
    gain_grad = jnp.sum(upstream * normed, axis=0, keepdims=True)
    return back, gain_grad, jnp.sum(upstream, axis=0, keepdims=True)


def norm_back_two_kernel(gain_row, own, y, x, xy, values_hbm, upstream, vecs,
                         grad_ref, grad_b_ref, sums_ref, values, sems):
    copies = start_copies([(values_hbm, values)], sems)
    up = upstream[...]
    total = total_of(own, y, x, xy)
    copies[0].wait()
    back, gain_grad, shift_grad = norm_back(
        total, values[...], vecs[gain_row : gain_row + 1, :]
    )
    grad = up + back
    grad_ref[...] = grad
    grad_b_ref[...] = grad.astype(bf16)
    sums_ref[0:1, :] = gain_grad
    sums_ref[1:2, :] = shift_grad
    sums_ref[2:3, :] = jnp.sum(grad, axis=0, keepdims=True)
    sums_ref[3:4, :] = jnp.sum(up, axis=0, keepdims=True)


def norm_back_one_kernel(gain_row, own, y, x, xy, values_hbm, upstream, vecs, mask,
                         grad_ref, grad_b_ref, sums_ref, values, sems):
    copies = start_copies([(values_hbm, values)], sems)
    total = total_of(own, y, x, xy)
    copies[0].wait()
    back, gain_grad, shift_grad = norm_back(
        total, values[...], vecs[gain_row : gain_row + 1, :]
    )
    grad = upstream[...] + back
    if mask is not None:
        grad = grad * mask[:, 0:1]
    grad_ref[...] = grad
    grad_b_ref[...] = grad.astype(bf16)
    sums_ref[0:1, :] = gain_grad
    sums_ref[1:2, :] = shift_grad


def attn_back_kernel(feats, heads, weight_count, part_count, tile, carried, *refs):
    c0, c1, c2, c3, *rest = refs
    weights, rest = rest[:weight_count], rest[weight_count:]
    usable, q_hbm, attended_hbm, norm_hbm, *rest = rest
    parts, rest = rest[:part_count], rest[part_count:]
    if carried:
        keys_before, values_before, *rest = rest
    x, grad_q, grad_k, grad_v, pairs, q_ref, attended, norms, grad_att, sems = rest
    head_dim = feats // heads
    scale = 1.0 / math.sqrt(head_dim)
    moves = [(q_hbm.at[:, pl.ds(0, feats)], q_ref), (attended_hbm, attended), (norm_hbm, norms)]
    first = 0
    for part in parts:
        rows, width = part.shape
        moves.append(
            (part.at[:, pl.ds(width - 2 * feats, 2 * feats)], pairs.at[pl.ds(first, rows)])
        )
        first += rows
    copies = start_copies(moves, sems)
    assemble((c0, c1, c2, c3), x)
    grad_att[...] = sum(
        dot(x[:, span], w[:, 3 * feats :]) for span, w in shards(weights)
    ).astype(bf16)
    keep = usable[...] > 0.5
    rows = q_ref.shape[0]
    if carried:
        sum_k, sum_v = keys_before[...], values_before[...]
    else:
        sum_k = jnp.zeros(grad_k.shape, f32)
        sum_v = jnp.zeros(grad_v.shape, f32)
    for copy in copies:
        copy.wait()
    keys, values = pairs[:, :feats], pairs[:, feats:]
    for first in range(0, rows, tile):
        span = slice(first, first + tile)
        q = q_ref[span, :]
        ga = grad_att[span, :]
        products = ga.astype(f32) * attended[span, :].astype(f32)
        gq = None
        for h in range(heads):
            own = lanes_of(h, head_dim, feats)
            q_h = only(own, q)
            ga_h = only(own, ga)
            row_dots = jnp.sum(only(own, products), axis=-1, keepdims=True)
            scores = dot_nt(q_h, keys) * scale
            scores = jnp.where(keep, scores, MASK_FILL)
            soft = jnp.exp(scores - norms[span, h * head_dim : h * head_dim + 1])
            grad_soft = dot_nt(ga_h, values)
            grad_scores = (soft * (grad_soft - row_dots)).astype(bf16)
            part = dot(grad_scores, keys)
            gq = part if gq is None else jnp.where(own, part, gq)
            sum_k = sum_k + dot_tn(grad_scores, q_h) * scale
            sum_v = sum_v + dot_tn(soft.astype(bf16), ga_h)
        grad_q[span, :] = gq * scale
    grad_k[...] = sum_k
    grad_v[...] = sum_v


def project_kernel(feats, first, weight_count, gq, gk, gv, *refs):
    weights, (partial_ref, packed) = refs[:weight_count], refs[weight_count:]
    rows = gq.shape[0]
    span = slice(first, first + rows)
    packed[:, :feats] = gq[...].astype(bf16)
    packed[:, feats : 2 * feats] = gk[span, :].astype(bf16)
    packed[:, 2 * feats :] = gv[span, :].astype(bf16)
    for columns, w in shards(weights):
        partial_ref[:, columns] = dot_nt(packed[...], w[:, : 3 * feats]).astype(bf16)


def attn_grad_kernel(feats, count, first_near, first_far, att_near, att_far, up_near, up_far,
                     gq_near, gq_far, gk, gv, *refs):
    outs = refs[:count]
    sums_ref, token, first, att, up, packed, sems = refs[count:]
    rows = up_near.shape[0]
    width_own = outs[0].shape[0]
    near, far = pl.ds(0, rows), pl.ds(rows, rows)
    copies = start_copies(
        [
            (first_near, first.at[near]),
            (first_far, first.at[far]),
            (att_near, att.at[near]),
            (att_far, att.at[far]),
        ],
        sems,
    )
    up[:rows, :] = up_near[...]
    up[rows:, :] = up_far[...]
    packed[:rows, :feats] = gq_near[...].astype(bf16)
    packed[rows:, :feats] = gq_far[...].astype(bf16)
    packed[:, feats : 2 * feats] = gk[...].astype(bf16)
    packed[:, 2 * feats :] = gv[...].astype(bf16)
    sums_ref[0:1, :] = jnp.sum(gq_near[...], axis=0, keepdims=True) + jnp.sum(
        gq_far[...], axis=0, keepdims=True
    )
    sums_ref[1:2, :] = jnp.sum(gv[...], axis=0, keepdims=True)
    f = lax.axis_index("fsdp")
    for copy in copies:
        copy.wait()
    for d in reversed(range(count)):
        place = lax.rem(f + d, count)
        span = pl.ds(pl.multiple_of(place * width_own, width_own), width_own)
        dtype = outs[d].dtype
        outs[d][:, : 3 * feats] = dot_tn(first[:, span], packed[...]).astype(dtype)
        outs[d][:, 3 * feats :] = dot_tn(up[:, span], att[...]).astype(dtype)
    token[...] = jnp.zeros_like(token)


def shard_sum_kernel(own, *refs):
    *others, out_ref, token = refs
    total = own[...]
    for other in others:
        total = total + other[...].astype(f32)
    out_ref[...] = total.astype(bf16)
    token[...] = jnp.zeros_like(token)


def place_mlp_kernel(layer, hidden, p0, p1, p2, p3, *refs):
    fc1_hbm, fc2_hbm, token, fc1, fc2, sems = refs[-6:]
    ci = lax.rem(lax.axis_index("ctx"), GROUP)
    copies = []
    for k, piece in enumerate((p0, p1, p2, p3)):
        span = pl.ds(pl.multiple_of((ci ^ k) * hidden, hidden), hidden)
        fc1[k] = piece[:, :hidden].astype(f32)
        copies += start_copies(
            [(fc1.at[k], fc1_hbm.at[layer, :, span])], sems.at[pl.ds(2 * k, 1)]
        )
        fc2[k] = piece[:, hidden:].astype(f32).T
        copies += start_copies(
            [(fc2.at[k], fc2_hbm.at[layer, span, :])], sems.at[pl.ds(2 * k + 1, 1)]
        )
    token[...] = jnp.zeros_like(token)
    for copy in copies:
        copy.wait()


def place_attn_kernel(layer, feats, p0, p1, p2, p3, *refs):
    qkv_hbm, out_hbm, token, qkv, out, sems = refs[-6:]
    ci = lax.rem(lax.axis_index("ctx"), GROUP)
    copies = []
    for k, piece in enumerate((p0, p1, p2, p3)):
        span = pl.ds(pl.multiple_of((ci ^ k) * feats, feats), feats)
        for j in range(3):
            qkv[k, j] = piece[:, j * feats : (j + 1) * feats].astype(f32)
        copies += start_copies(
            [(qkv.at[k], qkv_hbm.at[layer, :, :, span])], sems.at[pl.ds(2 * k, 1)]
        )
        out[k] = piece[:, 3 * feats :].astype(f32).T
        copies += start_copies(
            [(out.at[k], out_hbm.at[layer, span, :])], sems.at[pl.ds(2 * k + 1, 1)]
        )
    token[...] = jnp.zeros_like(token)
    for copy in copies:
        copy.wait()


def place_call(body, pieces, before, outs, scratch, name):
    extra = () if before is None else (Far(before[0]), Far(before[1]))
    return kernel_call(
        body,
        [saved(s, f32) for s in outs] + [TOKEN],
        *pieces,
        *extra,
        name=name,
        scratch=[pltpu.VMEM(s, f32) for s in scratch] + [DMA((8,))],
        aliases={} if before is None else {4: 0, 5: 1},
    )


def place_rows_kernel(own, other, out_hbm, sems):
    rows = own.shape[0]
    start = pl.multiple_of(lax.axis_index("tp") * rows, rows)
    copies = start_copies(
        [
            (own, out_hbm.at[0, pl.ds(start, rows), :]),
            (other, out_hbm.at[0, pl.ds(pl.multiple_of(rows - start, rows), rows), :]),
        ],
        sems,
    )
    for copy in copies:
        copy.wait()


def per_device(
    inputs, lengths, cotangent, norm_gains, shifts, qv_bias, fc1_bias, w_qkv, w_out, w_fc1, w_fc2
):
    depth = w_qkv.shape[0]
    width_own = w_qkv.shape[2]
    fsdp = lax.axis_size("fsdp")
    tp = lax.axis_size("tp")
    ctx = lax.axis_size("ctx")
    outer = ctx // GROUP
    rows = inputs.shape[1] // tp
    half = rows * CHIPS
    all_rows = 2 * half
    head_own = qv_bias.shape[3]
    head_dim = head_own * fsdp
    heads = qv_bias.shape[2] // GROUP
    feats = heads * head_dim
    hidden = w_fc1.shape[2] // GROUP
    width = width_own * fsdp
    t = lax.axis_index("tp")
    f = lax.axis_index("fsdp")
    ci = lax.axis_index("ctx") % GROUP
    tile = half // 2
    attn_limit = 12 if outer == 1 else 48

    def swap_core(value):
        return lax.ppermute(value, "ctx", [(i, i ^ 1) for i in range(ctx)])

    def swap_x(value):
        return lax.ppermute(value, "ctx", [(i, i ^ 2) for i in range(ctx)])

    def swap_y(value):
        return lax.ppermute(value, "tp", [(i, i ^ 1) for i in range(tp)])

    def swap_xy(value):
        pairs = [
            (i * tp + k, (i ^ 2) * tp + (k ^ 1)) for i in range(ctx) for k in range(tp)
        ]
        return lax.ppermute(value, ("ctx", "tp"), pairs)

    def shift_z(value, d):
        return lax.ppermute(value, "fsdp", [(i, (i + d) % fsdp) for i in range(fsdp)])

    outer_groups = [[o * GROUP + i for o in range(outer)] for i in range(GROUP)]

    def gather_rows(own):
        near = (own, swap_y(own), swap_x(own), swap_xy(own))
        return near, tuple(swap_core(chunk) for chunk in near)

    def reduce_rows(near, far):
        own, y, x, xy = kernel_call(
            core_sum_kernel,
            [((rows, width), f32)] + [((rows, width), bf16)] * 3,
            near,
            swap_core(far),
            name="core_sum",
        )
        return own, swap_y(y), swap_x(x), swap_xy(xy)

    def pack_attn(l, after=()):
        return kernel_call(
            functools.partial(pack_attn_kernel, l, feats),
            [((width_own, 4 * feats), bf16)],
            Far(w_qkv),
            Far(w_out),
            name="pack_attn",
            scratch=[
                pltpu.VMEM((3, width_own, feats), bf16),
                pltpu.VMEM((feats, width_own), bf16),
                DMA((2,)),
            ],
        )[0]

    def pack_mlp(l):
        return kernel_call(
            functools.partial(pack_mlp_kernel, l, hidden),
            [((width_own, 2 * hidden), bf16)],
            Far(w_fc1),
            Far(w_fc2),
            name="pack_mlp",
            scratch=[
                pltpu.VMEM((width_own, hidden), bf16),
                pltpu.VMEM((hidden, width_own), bf16),
                DMA((2,)),
            ],
        )[0]

    attn_w = []
    mlp_w = []
    for l in range(depth):
        own = pack_attn(l)
        if l == 0:
            attn_w.append((own,) + tuple(shift_z(own, d) for d in range(1, fsdp)))
        else:
            attn_w.append((lax.all_gather(own, "fsdp", axis=0, tiled=True),))
        mlp_w.append(lax.all_gather(pack_mlp(l), "fsdp", axis=0, tiled=True))

    qv_own = lax.dynamic_slice_in_dim(qv_bias, ci * heads, heads, axis=2)
    vec_rows = depth * 6
    c1_rows = depth * fc1_bias.shape[2] // width_own
    qv_own = qv_own.reshape(1, -1)
    small_own = jnp.concatenate(
        [
            norm_gains.reshape(-1, width_own),
            shifts.reshape(-1, width_own),
            fc1_bias.reshape(-1, width_own),
            jnp.pad(qv_own, ((0, 0), (0, width_own - qv_own.shape[1]))),
        ],
        axis=0,
    )
    shifted = [small_own] + [shift_z(small_own, d) for d in range(1, fsdp)]

    def shard(a):
        picked = shifted[0]
        for d in range(1, fsdp):
            picked = jnp.where((f - d) % fsdp == a, shifted[d], picked)
        return picked.astype(f32)

    small = [shard(a) for a in range(fsdp)]
    vecs = jnp.concatenate([s[:vec_rows] for s in small], axis=1)
    fc1_all = shard(ci)[vec_rows : vec_rows + c1_rows].reshape(depth, 1, hidden)
    qv_all = jnp.stack(
        [s[vec_rows + c1_rows, : qv_own.shape[1]].reshape(depth, 2, heads, head_own) for s in small],
        axis=3,
    ).reshape(depth, 2, feats)

    def gain_row(l, i):
        return 2 * l + i

    def shift_row(l, i):
        return 2 * depth + 4 * l + i

    key_rows = outer * all_rows
    row_f32 = ((rows, width), f32)
    row_bf16 = ((rows, width), bf16)
    upstream, upstream_b, usable, mask = kernel_call(
        functools.partial(prep_upstream_kernel, tp, outer),
        [row_f32, row_bf16, ((1, key_rows), f32), ((rows, 128), f32)],
        Scalars(lengths),
        Far(cotangent),
        name="prep_upstream",
        scratch=[pltpu.VMEM((rows, width), f32), DMA((1,))],
    )
    near, far = gather_rows(upstream_b)
    half_x = pltpu.VMEM((half, width), bf16)
    *upstream_rows, upstream_token = kernel_call(
        keep_rows_kernel,
        [saved((half, width), bf16)] * 2 + [TOKEN],
        *near,
        *far,
        name="keep_rows",
        scratch=[half_x, half_x, DMA((2,))],
    )
    upstream_chunks = [(Far(x),) for x in upstream_rows]
    stream, first = kernel_call(
        functools.partial(prep_first_kernel, depth),
        [row_f32, row_bf16],
        Far(inputs),
        vecs,
        name="prep_first",
        scratch=[DMA((1,))],
    )
    first_chunks = gather_rows(first)

    partial_out = ((half, width), bf16)
    saved_all = []
    for l in range(depth):
        qkv = []
        first_x = []
        for side in (0, 1):
            qkv_half, x_half = kernel_call(
                functools.partial(qkv_kernel, feats, len(attn_w[l])),
                [((half, 3 * feats), bf16), ((half, width), bf16)],
                *first_chunks[side],
                *attn_w[l],
                qv_all[l],
                name="qkv",
                after=(upstream_token,) if l == 0 and side == 0 else (),
            )
            qkv.append(qkv_half)
            first_x.append(x_half)
        if outer > 1:
            pairs = jnp.concatenate([part[:, feats:] for part in qkv], axis=0)
            pairs = lax.all_gather(
                pairs, "ctx", axis=0, tiled=True, axis_index_groups=outer_groups
            )
            key_parts = (pairs,)
        else:
            key_parts = tuple(qkv)
        attn = [None, None]
        for side in (1, 0):
            kept = (first_x[side], qkv[side]) + ((stream,) if side == 1 else ())
            attn[side] = kernel_call(
                functools.partial(
                    attn_kernel, feats, heads, len(attn_w[l]), len(key_parts), len(kept), tile
                ),
                [partial_out, saved((half, feats), bf16), saved((half, feats), f32)]
                + [saved(k.shape, k.dtype) for k in kept],
                qkv[side],
                *key_parts,
                *attn_w[l],
                usable,
                *kept,
                name="attn",
                limit=attn_limit,
                scratch=[
                    pltpu.VMEM((key_rows, feats), bf16),
                    pltpu.VMEM((key_rows, feats), bf16),
                    pltpu.VMEM((half, feats), bf16),
                    pltpu.VMEM((half, feats), f32),
                    DMA((len(kept) + 2,)),
                ],
            )
        sums = reduce_rows(attn[0][0], attn[1][0])
        middle, second = kernel_call(
            functools.partial(sum_norm_kernel, shift_row(l, 2), gain_row(l, 1), shift_row(l, 1)),
            [row_f32, row_bf16],
            *sums,
            stream,
            vecs,
            name="sum_norm",
        )
        second_chunks = gather_rows(second)
        mlp = [None, None]
        for side in (1, 0):
            kept = (middle,) if side == 1 else ()
            mlp[side] = kernel_call(
                functools.partial(mlp_kernel, hidden, len(kept)),
                [
                    partial_out,
                    saved((half, width), bf16),
                    saved((half, hidden), bf16),
                    saved((2, half, hidden // 2), f32),
                ]
                + [saved(k.shape, k.dtype) for k in kept],
                *second_chunks[side],
                mlp_w[l],
                fc1_all[l],
                *kept,
                name="mlp",
                scratch=[
                    half_x,
                    pltpu.VMEM((half, hidden), bf16),
                    pltpu.VMEM((2, half, hidden // 2), f32),
                    DMA((4 + len(kept),)),
                ],
            )
        sums = reduce_rows(mlp[0][0], mlp[1][0])
        saved_all.append((attn, pairs if outer > 1 else None, mlp))
        if l + 1 < depth:
            stream, first = kernel_call(
                functools.partial(
                    sum_norm_kernel, shift_row(l, 3), gain_row(l + 1, 0), shift_row(l + 1, 0)
                ),
                [row_f32, row_bf16],
                *sums,
                middle,
                vecs,
                name="sum_norm",
            )
            first_chunks = gather_rows(first)
        else:
            outputs_own = kernel_call(
                functools.partial(sum_out_kernel, shift_row(l, 3)),
                [row_f32],
                *sums,
                middle,
                vecs,
                mask,
                name="sum_out",
            )[0]

    def both_halves(own):
        return kernel_call(
            place_rows_kernel,
            [saved(inputs.shape, f32)],
            own,
            swap_y(own),
            name="place_rows",
            scratch=[DMA((2,))],
        )[0]

    outputs = both_halves(outputs_own)

    def spread_grads(part):
        if outer > 1:
            part = lax.psum(part, "ctx", axis_index_groups=outer_groups)
        other = swap_x(part)
        return part, swap_core(part), other, swap_core(other)

    row_sums = [None] * depth
    unit_sums = [None] * depth
    head_sums = [None] * depth
    placed_mlp = None
    placed_attn = None
    shard_token = ()
    mlp_token = ()
    for l in reversed(range(depth)):
        attn, pairs, mlp = saved_all[l]
        back = [None, None]
        for side in (1, 0):
            back[side] = kernel_call(
                functools.partial(mlp_back_kernel, hidden, len(upstream_chunks[side])),
                [partial_out, ((half, hidden), bf16), ((1, hidden), f32), ((half, width), bf16)],
                *upstream_chunks[side],
                mlp_w[l],
                Far(mlp[side][3]),
                name="mlp_back",
                scratch=[pltpu.VMEM((2, half, hidden // 2), f32), DMA((2,))],
            )
        sums = reduce_rows(back[0][0], back[1][0])
        mlp_grad, grad_token = kernel_call(
            functools.partial(mlp_grad_kernel, hidden),
            [((width, 2 * hidden), bf16), TOKEN],
            Far(mlp[0][1]),
            Far(mlp[1][1]),
            Far(mlp[0][2]),
            Far(mlp[1][2]),
            back[0][3],
            back[1][3],
            back[0][1],
            back[1][1],
            name="mlp_grad",
            after=(sums[0],),
            scratch=[
                pltpu.VMEM((all_rows, width), bf16),
                pltpu.VMEM((all_rows, hidden), bf16),
                pltpu.VMEM((all_rows, width), bf16),
                pltpu.VMEM((all_rows, hidden), bf16),
                DMA((4,)),
            ],
            limit=16,
        )
        mlp_part = lax.psum_scatter(mlp_grad, "fsdp", scatter_dimension=0, tiled=True)
        placed_mlp = place_call(
            functools.partial(place_mlp_kernel, l, hidden),
            spread_grads(mlp_part),
            placed_mlp,
            [w_fc1.shape, w_fc2.shape],
            [(GROUP, width_own, hidden), (GROUP, hidden, width_own)],
            "place_mlp",
        )
        unit_sums[l] = back[0][2] + back[1][2]
        grad_middle, middle_b, sums_two = kernel_call(
            functools.partial(norm_back_two_kernel, gain_row(l, 1)),
            [row_f32, row_bf16, ((4, width), f32)],
            *sums,
            Far(mlp[1][4]),
            upstream,
            vecs,
            name="norm_back_two",
            after=(grad_token, *shard_token),
            scratch=[pltpu.VMEM((rows, width), f32), DMA((1,))],
        )
        middle_chunks = gather_rows(middle_b)
        grad_q = [None, None]
        middle_x = [None, None]
        carried = ()
        for side in (0, 1):
            key_parts = (pairs,) if outer > 1 else (attn[0][4], attn[1][4])
            middle_x[side], grad_q[side], *carried = kernel_call(
                functools.partial(
                    attn_back_kernel,
                    feats,
                    heads,
                    len(attn_w[l]),
                    len(key_parts),
                    tile,
                    len(carried) > 0,
                ),
                [
                    ((half, width), bf16),
                    ((half, feats), f32),
                    ((key_rows, feats), f32),
                    ((key_rows, feats), f32),
                ],
                *middle_chunks[side],
                *attn_w[l],
                usable,
                Far(attn[side][4]),
                Far(attn[side][1]),
                Far(attn[side][2]),
                *[Far(part) for part in key_parts],
                *carried,
                name="attn_back",
                scratch=[
                    pltpu.VMEM((key_rows, 2 * feats), bf16),
                    pltpu.VMEM((half, feats), bf16),
                    pltpu.VMEM((half, feats), bf16),
                    pltpu.VMEM((half, feats), f32),
                    pltpu.VMEM((half, feats), bf16),
                    DMA((3 + len(key_parts),)),
                ],
                limit=attn_limit,
            )
        grad_k, grad_v = carried
        if outer > 1:
            grad_k, grad_v = (
                lax.psum_scatter(
                    v, "ctx", scatter_dimension=0, tiled=True, axis_index_groups=outer_groups
                )
                for v in (grad_k, grad_v)
            )

        def project(side, after):
            return kernel_call(
                functools.partial(project_kernel, feats, side * half, len(attn_w[l])),
                [partial_out],
                grad_q[side],
                grad_k,
                grad_v,
                *attn_w[l],
                name="project",
                after=after,
                scratch=[pltpu.VMEM((half, 3 * feats), bf16)],
            )[0]

        def weight_grad(after):
            *parts, head_sum, token = kernel_call(
                functools.partial(attn_grad_kernel, feats, fsdp),
                [((width_own, 4 * feats), f32)]
                + [((width_own, 4 * feats), bf16)] * (fsdp - 1)
                + [((2, feats), f32), TOKEN],
                Far(attn[0][3]),
                Far(attn[1][3]),
                Far(attn[0][1]),
                Far(attn[1][1]),
                *middle_x,
                *grad_q,
                grad_k,
                grad_v,
                name="attn_grad",
                after=after,
                scratch=[
                    pltpu.VMEM((all_rows, width), bf16),
                    pltpu.VMEM((all_rows, feats), bf16),
                    pltpu.VMEM((all_rows, width), bf16),
                    pltpu.VMEM((all_rows, 3 * feats), bf16),
                    DMA((4,)),
                ],
            )
            return parts, head_sum, token

        if l > 0:
            far_part = project(1, ())
            near_part = project(0, ())
            sums = reduce_rows(near_part, far_part)
            parts, head_sums[l], grad_token = weight_grad((sums[0],))
            one_after = (grad_token,)
        else:
            parts, head_sums[l], grad_token = weight_grad(mlp_token)
            far_part = project(1, (grad_token,))
            near_part = project(0, ())
            sums = reduce_rows(near_part, far_part)
            one_after = ()
        attn_part, token = kernel_call(
            shard_sum_kernel,
            [((width_own, 4 * feats), bf16), TOKEN],
            parts[0],
            *[shift_z(parts[d], d) for d in range(1, fsdp)],
            name="shard_sum",
        )
        shard_token = (token,)
        placed_attn = place_call(
            functools.partial(place_attn_kernel, l, feats),
            spread_grads(attn_part),
            placed_attn,
            [w_qkv.shape, w_out.shape],
            [(GROUP, 3, width_own, feats), (GROUP, feats, width_own)],
            "place_attn",
        )
        mlp_token = (placed_mlp[2],)
        body = functools.partial(norm_back_one_kernel, gain_row(l, 0))
        if l > 0:
            masked = ()
            body = lambda *refs, body=body: body(*refs[:7], None, *refs[7:])
        else:
            masked = (mask,)
        upstream, upstream_b, sums_one = kernel_call(
            body,
            [row_f32, row_bf16, ((2, width), f32)],
            *sums,
            Far(attn[1][5]),
            grad_middle,
            vecs,
            *masked,
            name="norm_back_one",
            after=one_after,
            scratch=[pltpu.VMEM((rows, width), f32), DMA((1,))],
        )
        if l > 0:
            upstream_chunks = gather_rows(upstream_b)
        row_sums[l] = (sums_one, sums_two)

    grad_inputs = both_halves(upstream)

    vec_part = jnp.concatenate(
        [
            piece
            for l in range(depth)
            for piece in (
                row_sums[l][0][0:1],
                row_sums[l][1][0:1],
                row_sums[l][0][1:2],
                row_sums[l][1][1:4],
            )
        ],
        axis=0,
    )
    unit_part = jnp.concatenate(unit_sums, axis=0)
    head_part = jnp.concatenate(head_sums, axis=0)
    unit_lines = unit_part.reshape(-1, width)
    head_lines = head_part.reshape(1, -1)
    head_lines = jnp.pad(head_lines, ((0, 0), (0, width - head_lines.shape[1])))
    packed = jnp.concatenate([vec_part, unit_lines, head_lines], axis=0)
    if outer > 1:
        packed = lax.psum(packed, "ctx", axis_index_groups=outer_groups)
    step = 1
    while step < fsdp:
        packed = packed + lax.ppermute(packed, "fsdp", [(i, i ^ step) for i in range(fsdp)])
        step *= 2
    vec_sum = lax.dynamic_slice_in_dim(packed[:vec_rows], f * width_own, width_own, axis=1)
    rest = packed[vec_rows:]
    vec_sum = vec_sum + swap_y(vec_sum)
    rest_core = swap_core(rest)
    vec_sum = vec_sum + swap_core(vec_sum)
    rest_two = jnp.stack([rest, rest_core])
    vec_sum = vec_sum + swap_x(vec_sum)
    rest_four = jnp.concatenate([rest_two, swap_x(rest_two)], axis=0)
    vec_sum = vec_sum.reshape(depth, 6, width_own)
    unit_count = unit_lines.shape[0]

    def of_place(c):
        return lax.dynamic_index_in_dim(rest_four, ci ^ c, 0, keepdims=False)

    grad_fc1_bias = of_place(f)[:unit_count].reshape(depth, 1, hidden)
    grad_qv_bias = jnp.stack(
        [
            lax.dynamic_slice_in_dim(
                of_place(c)[unit_count, : head_part.size].reshape(depth, 2, heads, head_dim),
                f * head_own,
                head_own,
                axis=3,
            )
            for c in range(GROUP)
        ],
        axis=2,
    ).reshape(qv_bias.shape)
    return (
        outputs,
        grad_inputs,
        vec_sum[:, :2],
        vec_sum[:, 2:],
        grad_qv_bias,
        grad_fc1_bias,
        placed_attn[0],
        placed_attn[1],
        placed_mlp[0],
        placed_mlp[1],
    )


def solution(mesh):
    rows = P("fsdp", "ctx", None)
    params = (
        P(None, None, "fsdp"),
        P(None, None, "fsdp"),
        P(None, None, "tp", "fsdp"),
        P(None, "tp", "fsdp"),
        P(None, None, "fsdp", "tp"),
        P(None, "tp", "fsdp"),
        P(None, "fsdp", "tp"),
        P(None, "tp", "fsdp"),
    )
    return jax.shard_map(
        per_device,
        mesh=mesh,
        in_specs=(rows, P("fsdp", None), rows) + params,
        out_specs=(rows, rows) + params,
        check_vma=False,
    )
```

time: 419 us -> 455 us (1.086)
  waiting for transfers between devices: 97.7 us -> 168 us
  local copies, waits for them, and re-layouts: 90.1 us -> 26.7 us
  Pallas kernels: 70.9 us -> 100 us
  starting transfers between devices: 132 us -> 138 us
  other arithmetic: 5.72 us -> 0.18 us
    ppermute x3 -> x12, waiting for transfers between devices: 0.01 us -> 89.1 us  [shift_z(): lax.ppermute(value, 'fsdp', [(i, (i + d) % fsdp) for i in range(fsdp)])]
    unnamed x419 -> x123, local copies, waits for them, and re-layouts: 83.2 us -> 22.8 us
    pallas_call x51 -> x59, Pallas kernels: 70.9 us -> 100 us  [kernel_call(): pl.pallas_call(run, out_shape=out_shape, in_specs=specs, out_specs=out_sp...]
    all_gather x4 -> x3, waiting for transfers between devices: 11.6 us -> 0.01 us  [the longest x2 0.01 us: per_device(): mlp_w.append(lax.all_gather(pack_mlp(l), 'fsdp', axis=0, tiled=True))]
    ppermute x3 -> x12, starting transfers between devices: 3.83 us -> 12.7 us  [shift_z(): lax.ppermute(value, 'fsdp', [(i, (i + d) % fsdp) for i in range(fsdp)])]
  transfers between devices with their start and end apart: 120 -> 126, of which waited for: 42 -> 43; matrix products, arithmetic and copies ran while one was open for 3% -> 1% of each run, Pallas kernels for 14% -> 19%
where the time goes in v3:
time: 455 us; the launch traced here: 449 us
  waiting for transfers between devices  168 us (37%)
  starting transfers between devices  138 us (30%)
  Pallas kernels  100 us (22%)
  local copies, waits for them, and re-layouts  26.7 us (6%)
  between operations  15.7 us (3%)
    pallas_call x59, Pallas kernels, kernel_call(): pl.pallas_call(run, out_shape=out_shape, in_specs=specs, out_specs=out_sp...  100 us
    ppermute x12, waiting for transfers between devices, shift_z(): lax.ppermute(value, 'fsdp', [(i, (i + d) % fsdp) for i in range(fsdp)])  89.1 us
    ppermute x50, starting transfers between devices, swap_core(): return lax.ppermute(value, 'ctx', [(i, i ^ 1) for i in range(ctx)])  74 us
    ppermute x16, waiting for transfers between devices, swap_xy(): return lax.ppermute(value, ('ctx', 'tp'), pairs)  33.5 us
    unnamed x123, local copies, waits for them, and re-layouts  22.8 us
    ppermute x19, waiting for transfers between devices, swap_y(): return lax.ppermute(value, 'tp', [(i, i ^ 1) for i in range(tp)])  20.8 us
    ppermute x22, waiting for transfers between devices, swap_x(): return lax.ppermute(value, 'ctx', [(i, i ^ 2) for i in range(ctx)])  20.4 us
    ppermute x16, starting transfers between devices, swap_xy(): return lax.ppermute(value, ('ctx', 'tp'), pairs)  20.1 us
  transfers between devices with their start and end apart: 126, of which 43 were waited for; matrix products, arithmetic and copies ran while one was open for 1% of the time, Pallas kernels for 19%

profile of v3, /device:TPU:9, one launch (start us, length us, event | category | flops | bytes accessed | tf_op | source)
XLA Modules:
  0.0 449.0 jit_solution(12530289714627808162)
XLA Ops:
  31.7 3.7 collective-permute-start.15
  37.4 11.1 %collective-permute-done.8.refs_7_.refs_6_ = bf16[256,512]{1,0:T(8,128)(2,1)S(1)} collective-permute-done((bf16[256,512]{1,0:T(8,128)(2,1)S(1)}, bf16[256,512]{1,0:T(8,128)(2,1)S(1)}, u32[]{:S(2)}, u32[]{:S(2)}) %collective-permute-start.8) | collective-permute-done | bytes 262176 | tf_op jit(solution)/shard_map/ppermute | solution.py:631
  48.5 8.3 %collective-permute-done.7.refs_6_.refs_5_ = bf16[256,512]{1,0:T(8,128)(2,1)S(1)} collective-permute-done((bf16[256,512]{1,0:T(8,128)(2,1)S(1)}, bf16[256,512]{1,0:T(8,128)(2,1)S(1)}, u32[]{:S(2)}, u32[]{:S(2)}) %collective-permute-start.7) | collective-permute-done | bytes 262176 | tf_op jit(solution)/shard_map/ppermute | solution.py:631
  61.9 11.8 %collective-permute-done.6.refs_5_.refs_4_ = bf16[256,512]{1,0:T(8,128)(2,1)S(1)} collective-permute-done((bf16[256,512]{1,0:T(8,128)(2,1)S(1)}, bf16[256,512]{1,0:T(8,128)(2,1)S(1)}, u32[]{:S(2)}, u32[]{:S(2)}) %collective-permute-start.6) | collective-permute-done | bytes 262176 | tf_op jit(solution)/shard_map/ppermute | solution.py:631
  75.9 3.9 attn.5
  83.3 2.8 attn.4
  89.0 3.3 collective-permute-done.21.refs_1_
  93.2 3.4 collective-permute-done.23.refs_3_
  102.5 3.5 collective-permute-start.30
  123.1 2.6 collective-permute-done.32.refs_1_
  127.2 3.0 collective-permute-done.34.refs_3_
  131.8 2.6 collective-permute-start.37
  137.5 4.2 collective-permute-start.41
  148.6 2.6 attn.7
  151.8 2.6 attn.6
  157.2 3.2 collective-permute-done.43.refs_1_
  160.4 4.4 collective-permute-done.45.refs_3_
  172.3 3.7 collective-permute-start.52
  181.8 3.5 mlp.7
  189.0 2.9 mlp.6
  197.2 3.4 mlp_grad.2
  204.8 3.2 collective-permute-done.59.refs_1_
  208.1 4.3 collective-permute-done.61.refs_3_
  221.0 4.1 collective-permute-start.68
  226.8 3.6 attn_back.4
  230.5 3.6 attn_back.5
  239.7 3.2 attn_grad.2
  242.9 4.1 collective-permute-done.72.refs_3_
  253.6 4.1 collective-permute-start.79
  265.8 4.9 %mlp_grad.3 = (bf16[1024,1024]{1,0:T(8,128)(2,1)}, f32[8,128]{1,0:T(8,128)S(1)}) custom-call(bf16[320,1024]{1,0:T(8,128)(2,1)} %get-tuple-element.276.refs_0_, bf16[320,1024]{1,0:T(8,128)(2,1)} %get-tuple-element.277.refs_1_, bf16[320,512]{1,0:T(8,128)(2,1)} %get-tuple-element.278.refs_2_, bf16[320,512]{1,0:T(8,128)(2,1)} %get-tuple-element.279.refs_3_, ...), custom_call_target="tpu_custom_call" | custom-call | tf_op jit(solution)/shard_map/mlp_grad/pallas_call | solution.py:79
  272.1 3.2 collective-permute-start.84
  275.2 4.2 collective-permute-start.85
  280.0 7.9 %collective-permute-done.84.refs_1_ = bf16[256,512]{1,0:T(8,128)(2,1)S(1)} collective-permute-done((bf16[256,512]{1,0:T(8,128)(2,1)}, bf16[256,512]{1,0:T(8,128)(2,1)S(1)}, u32[]{:S(2)}, u32[]{:S(2)}) %collective-permute-start.84) | collective-permute-done | bytes 262176 | tf_op jit(solution)/shard_map/ppermute | solution.py:631
  287.9 25.0 %collective-permute-done.85.refs_2_ = bf16[256,512]{1,0:T(8,128)(2,1)S(1)} collective-permute-done((bf16[256,512]{1,0:T(8,128)(2,1)}, bf16[256,512]{1,0:T(8,128)(2,1)S(1)}, u32[]{:S(2)}, u32[]{:S(2)}) %collective-permute-start.85) | collective-permute-done | bytes 262176 | tf_op jit(solution)/shard_map/ppermute | solution.py:631
  312.9 12.3 %collective-permute-done.86.refs_3_ = bf16[256,512]{1,0:T(8,128)(2,1)S(1)} collective-permute-done((bf16[256,512]{1,0:T(8,128)(2,1)S(1)}, bf16[256,512]{1,0:T(8,128)(2,1)S(1)}, u32[]{:S(2)}, u32[]{:S(2)}) %collective-permute-start.86) | collective-permute-done | bytes 262176 | tf_op jit(solution)/shard_map/ppermute | solution.py:631
  326.7 5.8 %collective-permute-start.90 = (bf16[80,1024]{1,0:T(8,128)(2,1)S(1)}, bf16[80,1024]{1,0:T(8,128)(2,1)S(1)}, u32[]{:S(2)}, u32[]{:S(2)}) collective-permute-start(bf16[80,1024]{1,0:T(8,128)(2,1)S(1)} %get-tuple-element.290.refs_0_), channel_id=1, source_target_pairs={{0,2},{2,0},{4,6},{6,4},{1,3},{3,1},{5,7},{7,5},{8,10},{10,8},{12,... | collective-permute-start | bytes 491528 | tf_op jit(solution)/shard_map/ppermute | solution.py:616
  335.4 4.2 collective-permute-done.89.refs_3_
  346.3 3.6 attn_back.6
  349.9 3.5 attn_back.7
  355.7 2.7 attn_grad.3
  362.5 2.7 collective-permute-done.54.refs_1_
  365.5 4.1 collective-permute-done.56.refs_3_
  373.6 12.9 %collective-permute-done.110.refs_2_ = bf16[256,512]{1,0:T(8,128)(2,1)S(1)} collective-permute-done((bf16[256,512]{1,0:T(8,128)(2,1)S(1)}, bf16[256,512]{1,0:T(8,128)(2,1)S(1)}, u32[]{:S(2)}, u32[]{:S(2)}) %collective-permute-start.110) | collective-permute-done | bytes 262176 | tf_op jit(solution)/shard_map/ppermute | solution.py:631
  393.9 3.1 collective-permute-start.117
  401.3 3.2 collective-permute-start.103
  412.9 5.5 %collective-permute-done.104 = f32[12,256]{1,0:T(8,128)S(1)} collective-permute-done((f32[12,256]{1,0:T(8,128)S(1)}, f32[12,256]{1,0:T(8,128)S(1)}, u32[]{:S(2)}, u32[]{:S(2)}) %collective-permute-start.104) | collective-permute-done | bytes 12320 | tf_op jit(solution)/shard_map/ppermute | solution.py:622
  422.8 11.1 %collective-permute-done.119.refs_2_ = bf16[256,1024]{1,0:T(8,128)(2,1)S(1)} collective-permute-done((bf16[256,1024]{1,0:T(8,128)(2,1)}, bf16[256,1024]{1,0:T(8,128)(2,1)S(1)}, u32[]{:S(2)}, u32[]{:S(2)}) %collective-permute-start.119) | collective-permute-done | bytes 524320 | tf_op jit(solution)/shard_map/ppermute | solution.py:619
  439.5 2.8 place_mlp.3
  (457 shorter events, 190.3 us)
Async XLA Ops:
  7.2 103.6 %all-gather.4.cloned.1.call-start = ((), (), s32[]{:S(2)}) async-start(), calls=%async_computation.2 | async-start | bytes 2621440 | tf_op jit(solution)/shard_map/all_gather | solution.py:685
  9.3 134.5 %all-gather.6.cloned.1.call-start = ((), (), s32[]{:S(2)}) async-start(), calls=%async_computation.3 | async-start | bytes 1310720 | tf_op jit(solution)/shard_map/all_gather | solution.py:684
  9.6 13.5 %collective-permute-start.2 = (bf16[17,256]{1,0:T(8,128)(2,1)S(1)}, bf16[17,256]{1,0:T(8,128)(2,1)S(1)}, u32[]{:S(2)}, u32[]{:S(2)}) collective-permute-start(bf16[17,256]{1,0:T(8,128)(2,1)S(1)} %fusion.1), channel_id=1, source_target_pairs={{0,8},{8,16},{16,24},{24,0},{1,9},{9,17},{17,25},{25,1},{2,10},{10... | collective-permute-start | bytes 26120 | tf_op jit(solution)/shard_map/ppermute | solution.py:631
  10.9 12.4 %collective-permute-start.1 = (bf16[17,256]{1,0:T(8,128)(2,1)S(1)}, bf16[17,256]{1,0:T(8,128)(2,1)S(1)}, u32[]{:S(2)}, u32[]{:S(2)}) collective-permute-start(bf16[17,256]{1,0:T(8,128)(2,1)S(1)} %fusion.1), channel_id=1, source_target_pairs={{0,16},{8,24},{16,0},{24,8},{1,17},{9,25},{17,1},{25,9},{2,18},{10... | collective-permute-start | bytes 26120 | tf_op jit(solution)/shard_map/ppermute | solution.py:631
  12.0 11.6 %collective-permute-start = (bf16[17,256]{1,0:T(8,128)(2,1)S(1)}, bf16[17,256]{1,0:T(8,128)(2,1)S(1)}, u32[]{:S(2)}, u32[]{:S(2)}) collective-permute-start(bf16[17,256]{1,0:T(8,128)(2,1)S(1)} %fusion.1), channel_id=1, source_target_pairs={{0,24},{8,0},{16,8},{24,16},{1,25},{9,1},{17,9},{25,17},{2,26},{10... | collective-permute-start | bytes 26120 | tf_op jit(solution)/shard_map/ppermute | solution.py:631
  16.3 9.8 %collective-permute-start.12 = (bf16[80,1024]{1,0:T(8,128)(2,1)S(1)}, bf16[80,1024]{1,0:T(8,128)(2,1)S(1)}, u32[]{:S(2)}, u32[]{:S(2)}) collective-permute-start(bf16[80,1024]{1,0:T(8,128)(2,1)S(1)} %get-tuple-element.177.refs_0_), channel_id=1, source_target_pairs={{0,2},{2,0},{4,6},{6,4},{1,3},{3,1},{5,7},{7,5},{8,10},{10,8},{12,... | collective-permute-start | bytes 491528 | tf_op jit(solution)/shard_map/ppermute | solution.py:616
  17.8 10.5 %collective-permute-start.11 = (bf16[80,1024]{1,0:T(8,128)(2,1)S(1)}, bf16[80,1024]{1,0:T(8,128)(2,1)S(1)}, u32[]{:S(2)}, u32[]{:S(2)}) collective-permute-start(bf16[80,1024]{1,0:T(8,128)(2,1)S(1)} %get-tuple-element.177.refs_0_), channel_id=1, source_target_pairs={{0,5},{1,4},{2,7},{3,6},{4,1},{5,0},{6,3},{7,2},{8,13},{9,12},{10,... | collective-permute-start | bytes 491528 | tf_op jit(solution)/shard_map/ppermute | solution.py:628
  21.8 156.0 %all-gather.8.cloned.1.call-start = ((), (), s32[]{:S(2)}) async-start(), calls=%async_computation.4 | async-start | bytes 2621440 | tf_op jit(solution)/shard_map/all_gather | solution.py:685
  23.6 24.8 %collective-permute-start.8 = (bf16[256,512]{1,0:T(8,128)(2,1)S(1)}, bf16[256,512]{1,0:T(8,128)(2,1)S(1)}, u32[]{:S(2)}, u32[]{:S(2)}) collective-permute-start(bf16[256,512]{1,0:T(8,128)(2,1)S(1)} %pack_attn.2.refs_4_.refs_3_), channel_id=1, source_target_pairs={{0,24},{8,0},{16,8},{24,16},{1,25},{9,1},{17,9},{25,17},{2,26},{10... | collective-permute-start | bytes 786440 | tf_op jit(solution)/shard_map/ppermute | solution.py:631
  29.0 27.7 %collective-permute-start.7 = (bf16[256,512]{1,0:T(8,128)(2,1)S(1)}, bf16[256,512]{1,0:T(8,128)(2,1)S(1)}, u32[]{:S(2)}, u32[]{:S(2)}) collective-permute-start(bf16[256,512]{1,0:T(8,128)(2,1)S(1)} %pack_attn.2.refs_4_.refs_3_), channel_id=1, source_target_pairs={{0,16},{8,24},{16,0},{24,8},{1,17},{9,25},{17,1},{25,9},{2,18},{10... | collective-permute-start | bytes 786440 | tf_op jit(solution)/shard_map/ppermute | solution.py:631
  31.7 27.4 %collective-permute-start.15 = (bf16[80,1024]{1,0:T(8,128)(2,1)S(1)}, bf16[80,1024]{1,0:T(8,128)(2,1)S(1)}, u32[]{:S(2)}, u32[]{:S(2)}) collective-permute-start(bf16[80,1024]{1,0:T(8,128)(2,1)S(1)} %collective-permute-done.11.refs_3_), channel_id=1, source_target_pairs={{0,2},{2,0},{4,6},{6,4},{1,3},{3,1},{5,7},{7,5},{8,10},{10,8},{12,... | collective-permute-start | bytes 491528 | tf_op jit(solution)/shard_map/ppermute | solution.py:616
  35.4 23.8 %collective-permute-start.14 = (bf16[80,1024]{1,0:T(8,128)(2,1)S(1)}, bf16[80,1024]{1,0:T(8,128)(2,1)S(1)}, u32[]{:S(2)}, u32[]{:S(2)}) collective-permute-start(bf16[80,1024]{1,0:T(8,128)(2,1)S(1)} %collective-permute-done.10.refs_2_), channel_id=1, source_target_pairs={{0,2},{2,0},{4,6},{6,4},{1,3},{3,1},{5,7},{7,5},{8,10},{10,8},{12,... | collective-permute-start | bytes 491528 | tf_op jit(solution)/shard_map/ppermute | solution.py:616
  37.3 22.4 %collective-permute-start.13 = (bf16[80,1024]{1,0:T(8,128)(2,1)S(1)}, bf16[80,1024]{1,0:T(8,128)(2,1)}, u32[]{:S(2)}, u32[]{:S(2)}) collective-permute-start(bf16[80,1024]{1,0:T(8,128)(2,1)S(1)} %collective-permute-done.9.refs_1_), channel_id=1, source_target_pairs={{0,2},{2,0},{4,6},{6,4},{1,3},{3,1},{5,7},{7,5},{8,10},{10,8},{12,... | collective-permute-start | bytes 491528 | tf_op jit(solution)/shard_map/ppermute | solution.py:616
  48.4 25.2 %collective-permute-start.6 = (bf16[256,512]{1,0:T(8,128)(2,1)S(1)}, bf16[256,512]{1,0:T(8,128)(2,1)S(1)}, u32[]{:S(2)}, u32[]{:S(2)}) collective-permute-start(bf16[256,512]{1,0:T(8,128)(2,1)S(1)} %pack_attn.2.refs_4_.refs_3_), channel_id=1, source_target_pairs={{0,8},{8,16},{16,24},{24,0},{1,9},{9,17},{17,25},{25,1},{2,10},{10... | collective-permute-start | bytes 786440 | tf_op jit(solution)/shard_map/ppermute | solution.py:631
  56.7 17.5 %collective-permute-start.16 = (bf16[80,1024]{1,0:T(8,128)(2,1)S(1)}, bf16[80,1024]{1,0:T(8,128)(2,1)S(1)}, u32[]{:S(2)}, u32[]{:S(2)}) collective-permute-start(bf16[80,1024]{1,0:T(8,128)(2,1)S(1)} %get-tuple-element.176.refs_0_), channel_id=1, source_target_pairs={{0,2},{2,0},{4,6},{6,4},{1,3},{3,1},{5,7},{7,5},{8,10},{10,8},{12,... | collective-permute-start | bytes 491528 | tf_op jit(solution)/shard_map/ppermute | solution.py:616
  59.1 15.1 %collective-permute-start.19 = (bf16[80,1024]{1,0:T(8,128)(2,1)S(1)}, bf16[80,1024]{1,0:T(8,128)(2,1)}, u32[]{:S(2)}, u32[]{:S(2)}) collective-permute-start(bf16[80,1024]{1,0:T(8,128)(2,1)S(1)} %collective-permute-done.5.refs_3_), channel_id=1, source_target_pairs={{0,2},{2,0},{4,6},{6,4},{1,3},{3,1},{5,7},{7,5},{8,10},{10,8},{12,... | collective-permute-start | bytes 491528 | tf_op jit(solution)/shard_map/ppermute | solution.py:616
  59.2 15.0 %collective-permute-start.18 = (bf16[80,1024]{1,0:T(8,128)(2,1)S(1)}, bf16[80,1024]{1,0:T(8,128)(2,1)}, u32[]{:S(2)}, u32[]{:S(2)}) collective-permute-start(bf16[80,1024]{1,0:T(8,128)(2,1)S(1)} %collective-permute-done.4.refs_2_), channel_id=1, source_target_pairs={{0,2},{2,0},{4,6},{6,4},{1,3},{3,1},{5,7},{7,5},{8,10},{10,8},{12,... | collective-permute-start | bytes 491528 | tf_op jit(solution)/shard_map/ppermute | solution.py:616
  59.7 14.6 %collective-permute-start.17 = (bf16[80,1024]{1,0:T(8,128)(2,1)S(1)}, bf16[80,1024]{1,0:T(8,128)(2,1)}, u32[]{:S(2)}, u32[]{:S(2)}) collective-permute-start(bf16[80,1024]{1,0:T(8,128)(2,1)S(1)} %collective-permute-done.3.refs_1_), channel_id=1, source_target_pairs={{0,2},{2,0},{4,6},{6,4},{1,3},{3,1},{5,7},{7,5},{8,10},{10,8},{12,... | collective-permute-start | bytes 491528 | tf_op jit(solution)/shard_map/ppermute | solution.py:616
  83.0 187.8 %reduce-scatter.3.cloned.1.call-start = ((), (), s32[]{:S(2)}) async-start(), calls=%async_computation.5 | async-start | bytes 2621440 | tf_op jit(solution)/shard_map/reduce_scatter | solution.py:923
  134.8 12.1 %collective-permute-start.38 = (bf16[80,1024]{1,0:T(8,128)(2,1)}, bf16[80,1024]{1,0:T(8,128)(2,1)}, u32[]{:S(2)}, u32[]{:S(2)}) collective-permute-start(bf16[80,1024]{1,0:T(8,128)(2,1)} %get-tuple-element.199.refs_0_), channel_id=1, source_target_pairs={{0,2},{2,0},{4,6},{6,4},{1,3},{3,1},{5,7},{7,5},{8,10},{10,8},{12,... | collective-permute-start | bytes 491528 | tf_op jit(solution)/shard_map/ppermute | solution.py:616
  202.1 218.0 %reduce-scatter.5.cloned.1.call-start = ((), (), s32[]{:S(2)}) async-start(), calls=%async_computation.6 | async-start | bytes 2621440 | tf_op jit(solution)/shard_map/reduce_scatter | solution.py:923
  218.5 12.0 %collective-permute-start.65 = (bf16[80,1024]{1,0:T(8,128)(2,1)S(1)}, bf16[80,1024]{1,0:T(8,128)(2,1)S(1)}, u32[]{:S(2)}, u32[]{:S(2)}) collective-permute-start(bf16[80,1024]{1,0:T(8,128)(2,1)S(1)} %get-tuple-element.241.refs_0_), channel_id=1, source_target_pairs={{0,2},{2,0},{4,6},{6,4},{1,3},{3,1},{5,7},{7,5},{8,10},{10,8},{12,... | collective-permute-start | bytes 491528 | tf_op jit(solution)/shard_map/ppermute | solution.py:616
  221.0 9.5 %collective-permute-start.68 = (bf16[80,1024]{1,0:T(8,128)(2,1)S(1)}, bf16[80,1024]{1,0:T(8,128)(2,1)S(1)}, u32[]{:S(2)}, u32[]{:S(2)}) collective-permute-start(bf16[80,1024]{1,0:T(8,128)(2,1)S(1)} %collective-permute-done.64.refs_3_), channel_id=1, source_target_pairs={{0,2},{2,0},{4,6},{6,4},{1,3},{3,1},{5,7},{7,5},{8,10},{10,8},{12,... | collective-permute-start | bytes 491528 | tf_op jit(solution)/shard_map/ppermute | solution.py:616
  270.8 61.8 %collective-permute-start.95 = (bf16[256,1024]{1,0:T(8,128)(2,1)}, bf16[256,1024]{1,0:T(8,128)(2,1)S(1)}, u32[]{:S(2)}, u32[]{:S(2)}) collective-permute-start(bf16[256,1024]{1,0:T(8,128)(2,1)} %reduce-scatter.3.cloned.1.call-done.refs_0_), channel_id=1, source_target_pairs={{0,4},{2,6},{4,0},{6,2},{1,5},{3,7},{5,1},{7,3},{8,12},{10,14},{12... | collective-permute-start | bytes 1572872 | tf_op jit(solution)/shard_map/ppermute | solution.py:619
  272.1 15.8 %collective-permute-start.84 = (bf16[256,512]{1,0:T(8,128)(2,1)}, bf16[256,512]{1,0:T(8,128)(2,1)S(1)}, u32[]{:S(2)}, u32[]{:S(2)}) collective-permute-start(bf16[256,512]{1,0:T(8,128)(2,1)} %get-tuple-element.286), channel_id=1, source_target_pairs={{0,8},{8,16},{16,24},{24,0},{1,9},{9,17},{17,25},{25,1},{2,10},{10... | collective-permute-start | bytes 786440 | tf_op jit(solution)/shard_map/ppermute | solution.py:631
  275.2 37.6 %collective-permute-start.85 = (bf16[256,512]{1,0:T(8,128)(2,1)}, bf16[256,512]{1,0:T(8,128)(2,1)S(1)}, u32[]{:S(2)}, u32[]{:S(2)}) collective-permute-start(bf16[256,512]{1,0:T(8,128)(2,1)} %get-tuple-element.287), channel_id=1, source_target_pairs={{0,16},{8,24},{16,0},{24,8},{1,17},{9,25},{17,1},{25,9},{2,18},{10... | collective-permute-start | bytes 786440 | tf_op jit(solution)/shard_map/ppermute | solution.py:631
  279.5 45.7 %collective-permute-start.86 = (bf16[256,512]{1,0:T(8,128)(2,1)S(1)}, bf16[256,512]{1,0:T(8,128)(2,1)S(1)}, u32[]{:S(2)}, u32[]{:S(2)}) collective-permute-start(bf16[256,512]{1,0:T(8,128)(2,1)S(1)} %copy-done.51), channel_id=1, source_target_pairs={{0,24},{8,0},{16,8},{24,16},{1,25},{9,1},{17,9},{25,17},{2,26},{10... | collective-permute-start | bytes 786440 | tf_op jit(solution)/shard_map/ppermute | solution.py:631
  279.5 45.8 %collective-permute-start.81 = (bf16[80,1024]{1,0:T(8,128)(2,1)}, bf16[80,1024]{1,0:T(8,128)(2,1)S(1)}, u32[]{:S(2)}, u32[]{:S(2)}) collective-permute-start(bf16[80,1024]{1,0:T(8,128)(2,1)} %get-tuple-element.271), channel_id=1, source_target_pairs={{0,1},{1,0},{2,3},{3,2},{4,5},{5,4},{6,7},{7,6},{8,9},{9,8},{10,11... | collective-permute-start | bytes 491528 | tf_op jit(solution)/shard_map/ppermute | solution.py:622
  287.9 37.4 %collective-permute-start.82 = (bf16[80,1024]{1,0:T(8,128)(2,1)}, bf16[80,1024]{1,0:T(8,128)(2,1)S(1)}, u32[]{:S(2)}, u32[]{:S(2)}) collective-permute-start(bf16[80,1024]{1,0:T(8,128)(2,1)} %get-tuple-element.272), channel_id=1, source_target_pairs={{0,4},{2,6},{4,0},{6,2},{1,5},{3,7},{5,1},{7,3},{8,12},{10,14},{12... | collective-permute-start | bytes 491528 | tf_op jit(solution)/shard_map/ppermute | solution.py:619
  312.9 12.4 %collective-permute-start.83 = (bf16[80,1024]{1,0:T(8,128)(2,1)}, bf16[80,1024]{1,0:T(8,128)(2,1)S(1)}, u32[]{:S(2)}, u32[]{:S(2)}) collective-permute-start(bf16[80,1024]{1,0:T(8,128)(2,1)} %get-tuple-element.273), channel_id=1, source_target_pairs={{0,5},{1,4},{2,7},{3,6},{4,1},{5,0},{6,3},{7,2},{8,13},{9,12},{10,... | collective-permute-start | bytes 491528 | tf_op jit(solution)/shard_map/ppermute | solution.py:628
  332.5 21.0 %collective-permute-start.94 = (bf16[256,1024]{1,0:T(8,128)(2,1)S(1)}, bf16[256,1024]{1,0:T(8,128)(2,1)S(1)}, u32[]{:S(2)}, u32[]{:S(2)}) collective-permute-start(bf16[256,1024]{1,0:T(8,128)(2,1)S(1)} %copy-done.25), channel_id=1, source_target_pairs={{0,2},{2,0},{4,6},{6,4},{1,3},{3,1},{5,7},{7,5},{8,10},{10,8},{12,... | collective-permute-start | bytes 1572872 | tf_op jit(solution)/shard_map/ppermute | solution.py:616
  332.6 20.9 %collective-permute-start.96 = (bf16[256,1024]{1,0:T(8,128)(2,1)S(1)}, bf16[256,1024]{1,0:T(8,128)(2,1)S(1)}, u32[]{:S(2)}, u32[]{:S(2)}) collective-permute-start(bf16[256,1024]{1,0:T(8,128)(2,1)S(1)} %collective-permute-done.95.refs_2_), channel_id=1, source_target_pairs={{0,2},{2,0},{4,6},{6,4},{1,3},{3,1},{5,7},{7,5},{8,10},{10,8},{12,... | collective-permute-start | bytes 1572872 | tf_op jit(solution)/shard_map/ppermute | solution.py:616
  334.8 24.8 %collective-permute-start.53 = (bf16[320,1024]{1,0:T(8,128)(2,1)}, bf16[320,1024]{1,0:T(8,128)(2,1)S(1)}, u32[]{:S(2)}, u32[]{:S(2)}) collective-permute-start(bf16[320,1024]{1,0:T(8,128)(2,1)} %copy-done.49), channel_id=1, source_target_pairs={{0,2},{2,0},{4,6},{6,4},{1,3},{3,1},{5,7},{7,5},{8,10},{10,8},{12,... | collective-permute-start | bytes 1966088 | tf_op jit(solution)/shard_map/ppermute | solution.py:616
  359.0 11.6 %collective-permute-start.97 = (bf16[320,1024]{1,0:T(8,128)(2,1)S(1)}, bf16[320,1024]{1,0:T(8,128)(2,1)S(1)}, u32[]{:S(2)}, u32[]{:S(2)}) collective-permute-start(bf16[320,1024]{1,0:T(8,128)(2,1)S(1)} %project.7), channel_id=1, source_target_pairs={{0,2},{2,0},{4,6},{6,4},{1,3},{3,1},{5,7},{7,5},{8,10},{10,8},{12,... | collective-permute-start | bytes 1966088 | tf_op jit(solution)/shard_map/ppermute | solution.py:616
  369.7 16.8 %collective-permute-start.110 = (bf16[256,512]{1,0:T(8,128)(2,1)S(1)}, bf16[256,512]{1,0:T(8,128)(2,1)S(1)}, u32[]{:S(2)}, u32[]{:S(2)}) collective-permute-start(bf16[256,512]{1,0:T(8,128)(2,1)S(1)} %get-tuple-element.329), channel_id=1, source_target_pairs={{0,16},{8,24},{16,0},{24,8},{1,17},{9,25},{17,1},{25,9},{2,18},{10... | collective-permute-start | bytes 786440 | tf_op jit(solution)/shard_map/ppermute | solution.py:631
  369.8 17.2 %collective-permute-start.111 = (bf16[256,512]{1,0:T(8,128)(2,1)S(1)}, bf16[256,512]{1,0:T(8,128)(2,1)S(1)}, u32[]{:S(2)}, u32[]{:S(2)}) collective-permute-start(bf16[256,512]{1,0:T(8,128)(2,1)S(1)} %get-tuple-element.330), channel_id=1, source_target_pairs={{0,24},{8,0},{16,8},{24,16},{1,25},{9,1},{17,9},{25,17},{2,26},{10... | collective-permute-start | bytes 786440 | tf_op jit(solution)/shard_map/ppermute | solution.py:631
  370.8 17.1 %collective-permute-start.98 = (bf16[80,1024]{1,0:T(8,128)(2,1)S(1)}, bf16[80,1024]{1,0:T(8,128)(2,1)S(1)}, u32[]{:S(2)}, u32[]{:S(2)}) collective-permute-start(bf16[80,1024]{1,0:T(8,128)(2,1)S(1)} %get-tuple-element.311), channel_id=1, source_target_pairs={{0,1},{1,0},{2,3},{3,2},{4,5},{5,4},{6,7},{7,6},{8,9},{9,8},{10,11... | collective-permute-start | bytes 491528 | tf_op jit(solution)/shard_map/ppermute | solution.py:622
  371.5 17.6 %collective-permute-start.99 = (bf16[80,1024]{1,0:T(8,128)(2,1)S(1)}, bf16[80,1024]{1,0:T(8,128)(2,1)S(1)}, u32[]{:S(2)}, u32[]{:S(2)}) collective-permute-start(bf16[80,1024]{1,0:T(8,128)(2,1)S(1)} %get-tuple-element.312), channel_id=1, source_target_pairs={{0,4},{2,6},{4,0},{6,2},{1,5},{3,7},{5,1},{7,3},{8,12},{10,14},{12... | collective-permute-start | bytes 491528 | tf_op jit(solution)/shard_map/ppermute | solution.py:619
  371.8 17.3 %collective-permute-start.100 = (bf16[80,1024]{1,0:T(8,128)(2,1)S(1)}, bf16[80,1024]{1,0:T(8,128)(2,1)S(1)}, u32[]{:S(2)}, u32[]{:S(2)}) collective-permute-start(bf16[80,1024]{1,0:T(8,128)(2,1)S(1)} %get-tuple-element.313), channel_id=1, source_target_pairs={{0,5},{1,4},{2,7},{3,6},{4,1},{5,0},{6,3},{7,2},{8,13},{9,12},{10,... | collective-permute-start | bytes 491528 | tf_op jit(solution)/shard_map/ppermute | solution.py:628
  386.5 14.9 %collective-permute-start.57 = (f32[80,1024]{1,0:T(8,128)S(1)}, f32[80,1024]{1,0:T(8,128)S(1)}, u32[]{:S(2)}, u32[]{:S(2)}) collective-permute-start(f32[80,1024]{1,0:T(8,128)S(1)} %sum_out.1.refs_0_), channel_id=1, source_target_pairs={{0,1},{1,0},{2,3},{3,2},{4,5},{5,4},{6,7},{7,6},{8,9},{9,8},{10,11... | collective-permute-start | bytes 983048 | tf_op jit(solution)/shard_map/ppermute | solution.py:622
  387.9 11.7 %collective-permute-start.113 = (bf16[256,512]{1,0:T(8,128)(2,1)S(1)}, bf16[256,512]{1,0:T(8,128)(2,1)S(1)}, u32[]{:S(2)}, u32[]{:S(2)}) collective-permute-start(bf16[256,512]{1,0:T(8,128)(2,1)S(1)} %get-tuple-element.331.refs_0_), channel_id=1, source_target_pairs={{0,4},{2,6},{4,0},{6,2},{1,5},{3,7},{5,1},{7,3},{8,12},{10,14},{12... | collective-permute-start | bytes 786440 | tf_op jit(solution)/shard_map/ppermute | solution.py:619
  391.2 10.1 %collective-permute-start.102 = (f32[14,1024]{1,0:T(8,128)S(1)}, f32[14,1024]{1,0:T(8,128)S(1)}, u32[]{:S(2)}, u32[]{:S(2)}) collective-permute-start(f32[14,1024]{1,0:T(8,128)S(1)} %concatenate.23), channel_id=1, source_target_pairs={{0,8},{8,0},{16,24},{24,16},{1,9},{9,1},{17,25},{25,17},{2,10},{10... | collective-permute-start | bytes 172040 | tf_op jit(solution)/shard_map/ppermute | solution.py:1109
  391.3 14.0 %collective-permute-start.115 = (bf16[256,512]{1,0:T(8,128)(2,1)S(1)}, bf16[256,512]{1,0:T(8,128)(2,1)S(1)}, u32[]{:S(2)}, u32[]{:S(2)}) collective-permute-start(bf16[256,512]{1,0:T(8,128)(2,1)S(1)} %get-tuple-element.332.refs_0_), channel_id=1, source_target_pairs={{0,2},{2,0},{4,6},{6,4},{1,3},{3,1},{5,7},{7,5},{8,10},{10,8},{12,... | collective-permute-start | bytes 786440 | tf_op jit(solution)/shard_map/ppermute | solution.py:616
  393.9 11.4 %collective-permute-start.117 = (bf16[256,512]{1,0:T(8,128)(2,1)S(1)}, bf16[256,512]{1,0:T(8,128)(2,1)S(1)}, u32[]{:S(2)}, u32[]{:S(2)}) collective-permute-start(bf16[256,512]{1,0:T(8,128)(2,1)S(1)} %collective-permute-done.116.refs_2_), channel_id=1, source_target_pairs={{0,2},{2,0},{4,6},{6,4},{1,3},{3,1},{5,7},{7,5},{8,10},{10,8},{12,... | collective-permute-start | bytes 786440 | tf_op jit(solution)/shard_map/ppermute | solution.py:616
  409.5 28.1 %collective-permute-start.101 = (f32[80,1024]{1,0:T(8,128)S(1)}, f32[80,1024]{1,0:T(8,128)S(1)}, u32[]{:S(2)}, u32[]{:S(2)}) collective-permute-start(f32[80,1024]{1,0:T(8,128)S(1)} %get-tuple-element.316.refs_0_), channel_id=1, source_target_pairs={{0,1},{1,0},{2,3},{3,2},{4,5},{5,4},{6,7},{7,6},{8,9},{9,8},{10,11... | collective-permute-start | bytes 983048 | tf_op jit(solution)/shard_map/ppermute | solution.py:622
  420.1 13.8 %collective-permute-start.119 = (bf16[256,1024]{1,0:T(8,128)(2,1)}, bf16[256,1024]{1,0:T(8,128)(2,1)S(1)}, u32[]{:S(2)}, u32[]{:S(2)}) collective-permute-start(bf16[256,1024]{1,0:T(8,128)(2,1)} %reduce-scatter.5.cloned.1.call-done.refs_0_), channel_id=1, source_target_pairs={{0,4},{2,6},{4,0},{6,2},{1,5},{3,7},{5,1},{7,3},{8,12},{10,14},{12... | collective-permute-start | bytes 1572872 | tf_op jit(solution)/shard_map/ppermute | solution.py:619
  420.9 15.5 %collective-permute-start.106 = (f32[12,256]{1,0:T(8,128)S(1)}, f32[12,256]{1,0:T(8,128)S(1)}, u32[]{:S(2)}, u32[]{:S(2)}) collective-permute-start(f32[12,256]{1,0:T(8,128)S(1)} %add.96), channel_id=1, source_target_pairs={{0,4},{2,6},{4,0},{6,2},{1,5},{3,7},{5,1},{7,3},{8,12},{10,14},{12... | collective-permute-start | bytes 36872 | tf_op jit(solution)/shard_map/ppermute | solution.py:619
  422.2 16.2 %collective-permute-start.118 = (bf16[256,1024]{1,0:T(8,128)(2,1)}, bf16[256,1024]{1,0:T(8,128)(2,1)S(1)}, u32[]{:S(2)}, u32[]{:S(2)}) collective-permute-start(bf16[256,1024]{1,0:T(8,128)(2,1)} %reduce-scatter.5.cloned.1.call-done.refs_0_), channel_id=1, source_target_pairs={{0,2},{2,0},{4,6},{6,4},{1,3},{3,1},{5,7},{7,5},{8,10},{10,8},{12,... | collective-permute-start | bytes 1572872 | tf_op jit(solution)/shard_map/ppermute | solution.py:616
  (136 other events, 1021.1 us)
Sparse Core Ops, SparseCore 0:
  10.2 66.0 all-gather.3
  77.8 29.7 all-gather.5
  109.2 43.8 all-gather.7
  202.2 43.6 reduce-scatter.2
  270.9 66.4 reduce-scatter.4

commit v4 on v3

--- a/solution.py
+++ b/solution.py
@@ -51,7 +51,7 @@
     return pltpu.HBM(shape, dtype)
 
 
-def kernel_call(body, outs, *args, name, limit=12, scratch=(), after=(), aliases=None):
+def kernel_call(body, outs, *args, name, limit=12, scratch=(), after=(), aliases=None, us=0):
     values, specs = [], []
     for arg in (*args, *after):
         if isinstance(arg, Far):
@@ -84,7 +84,7 @@
         scratch_shapes=list(scratch),
         input_output_aliases=aliases or {},
         compiler_params=pltpu.CompilerParams(vmem_limit_bytes=limit << 20),
-        cost_estimate=pl.CostEstimate(flops=0, bytes_accessed=0, transcendentals=0),
+        cost_estimate=pl.CostEstimate(flops=us * 10**9, bytes_accessed=0, transcendentals=0),
         name=name,
     )(*values)
 
@@ -138,7 +138,7 @@
     return found
 
 
-def pack_attn_kernel(layer, feats, qkv_hbm, out_hbm, packed_ref, qkv, out, sems):
+def pack_attn_kernel(layer, feats, qkv_hbm, out_hbm, packed_ref, token, qkv, out, sems):
     ci = lax.rem(lax.axis_index("ctx"), GROUP)
     span = pl.ds(pl.multiple_of(ci * feats, feats), feats)
     copies = start_copies(
@@ -149,9 +149,10 @@
         packed_ref[:, k * feats : (k + 1) * feats] = qkv[k]
     copies[1].wait()
     packed_ref[:, 3 * feats :] = out[...].T
-
-
-def pack_mlp_kernel(layer, hidden, fc1_hbm, fc2_hbm, packed_ref, fc1, fc2, sems):
+    token[...] = jnp.zeros_like(token)
+
+
+def pack_mlp_kernel(layer, hidden, fc1_hbm, fc2_hbm, packed_ref, token, fc1, fc2, sems):
     ci = lax.rem(lax.axis_index("ctx"), GROUP)
     span = pl.ds(pl.multiple_of(ci * hidden, hidden), hidden)
     copies = start_copies(
@@ -161,6 +162,7 @@
     packed_ref[:, :hidden] = fc1[...]
     copies[1].wait()
     packed_ref[:, hidden:] = fc2[...].T
+    token[...] = jnp.zeros_like(token)
 
 
 def prep_upstream_kernel(tp, outer, lengths, cotangent_hbm,
@@ -282,9 +284,12 @@
     return own[...] + y[...].astype(f32) + x[...].astype(f32) + xy[...].astype(f32)
 
 
-def sum_norm_kernel(bias_row, gain_row, shift_row, own, y, x, xy, residual, vecs,
-                    stream_ref, normed_ref):
-    stream = residual[...] + total_of(own, y, x, xy) + vecs[bias_row : bias_row + 1, :]
+def sum_norm_kernel(bias_row, gain_row, shift_row, own, y, x, xy, residual_hbm, vecs,
+                    stream_ref, normed_ref, residual, sems):
+    copies = start_copies([(residual_hbm, residual)], sems)
+    total = total_of(own, y, x, xy) + vecs[bias_row : bias_row + 1, :]
+    copies[0].wait()
+    stream = residual[...] + total
     stream_ref[...] = stream
     normed, _ = normalize(stream)
     gain = vecs[gain_row : gain_row + 1, :]
@@ -475,12 +480,10 @@
         partial_ref[:, columns] = dot_nt(packed[...], w[:, : 3 * feats]).astype(bf16)
 
 
-def attn_grad_kernel(feats, count, first_near, first_far, att_near, att_far, up_near, up_far,
-                     gq_near, gq_far, gk, gv, *refs):
-    outs = refs[:count]
-    sums_ref, token, first, att, up, packed, sems = refs[count:]
+def attn_grad_kernel(feats, first_near, first_far, att_near, att_far, up_near, up_far,
+                     gq_near, gq_far, gk, gv, out_ref, sums_ref, token,
+                     first, att, up, packed, sems):
     rows = up_near.shape[0]
-    width_own = outs[0].shape[0]
     near, far = pl.ds(0, rows), pl.ds(rows, rows)
     copies = start_copies(
         [
@@ -501,24 +504,10 @@
         gq_far[...], axis=0, keepdims=True
     )
     sums_ref[1:2, :] = jnp.sum(gv[...], axis=0, keepdims=True)
-    f = lax.axis_index("fsdp")
     for copy in copies:
         copy.wait()
-    for d in reversed(range(count)):
-        place = lax.rem(f + d, count)
-        span = pl.ds(pl.multiple_of(place * width_own, width_own), width_own)
-        dtype = outs[d].dtype
-        outs[d][:, : 3 * feats] = dot_tn(first[:, span], packed[...]).astype(dtype)
-        outs[d][:, 3 * feats :] = dot_tn(up[:, span], att[...]).astype(dtype)
-    token[...] = jnp.zeros_like(token)
-
-
-def shard_sum_kernel(own, *refs):
-    *others, out_ref, token = refs
-    total = own[...]
-    for other in others:
-        total = total + other[...].astype(f32)
-    out_ref[...] = total.astype(bf16)
+    out_ref[:, : 3 * feats] = dot_tn(first[...], packed[...]).astype(bf16)
+    out_ref[:, 3 * feats :] = dot_tn(up[...], att[...]).astype(bf16)
     token[...] = jnp.zeros_like(token)
 
 
@@ -644,45 +633,49 @@
             swap_core(far),
             name="core_sum",
         )
-        return own, swap_y(y), swap_x(x), swap_xy(xy)
-
-    def pack_attn(l, after=()):
+        xy, x, y = swap_xy(xy), swap_x(x), swap_y(y)
+        return own, y, x, xy
+
+    def pack_attn(l, after):
         return kernel_call(
             functools.partial(pack_attn_kernel, l, feats),
-            [((width_own, 4 * feats), bf16)],
+            [((width_own, 4 * feats), bf16), TOKEN],
             Far(w_qkv),
             Far(w_out),
             name="pack_attn",
+            after=after,
             scratch=[
                 pltpu.VMEM((3, width_own, feats), bf16),
                 pltpu.VMEM((feats, width_own), bf16),
                 DMA((2,)),
             ],
-        )[0]
-
-    def pack_mlp(l):
+        )
+
+    def pack_mlp(l, after):
         return kernel_call(
             functools.partial(pack_mlp_kernel, l, hidden),
-            [((width_own, 2 * hidden), bf16)],
+            [((width_own, 2 * hidden), bf16), TOKEN],
             Far(w_fc1),
             Far(w_fc2),
             name="pack_mlp",
+            after=after,
             scratch=[
                 pltpu.VMEM((width_own, hidden), bf16),
                 pltpu.VMEM((hidden, width_own), bf16),
                 DMA((2,)),
             ],
-        )[0]
+        )
 
     attn_w = []
     mlp_w = []
+    token = None
     for l in range(depth):
-        own = pack_attn(l)
+        own, token = pack_attn(l, () if token is None else (token,))
+        attn_w.append((lax.all_gather(own, "fsdp", axis=0, tiled=True),))
+        own, token = pack_mlp(l, (token,))
+        mlp_w.append(lax.all_gather(own, "fsdp", axis=0, tiled=True))
         if l == 0:
-            attn_w.append((own,) + tuple(shift_z(own, d) for d in range(1, fsdp)))
-        else:
-            attn_w.append((lax.all_gather(own, "fsdp", axis=0, tiled=True),))
-        mlp_w.append(lax.all_gather(pack_mlp(l), "fsdp", axis=0, tiled=True))
+            pack_token = token
 
     qv_own = lax.dynamic_slice_in_dim(qv_bias, ci * heads, heads, axis=2)
     vec_rows = depth * 6
@@ -728,6 +721,7 @@
         Scalars(lengths),
         Far(cotangent),
         name="prep_upstream",
+        after=(pack_token,),
         scratch=[pltpu.VMEM((rows, width), f32), DMA((1,))],
     )
     near, far = gather_rows(upstream_b)
@@ -805,9 +799,10 @@
             functools.partial(sum_norm_kernel, shift_row(l, 2), gain_row(l, 1), shift_row(l, 1)),
             [row_f32, row_bf16],
             *sums,
-            stream,
+            Far(attn[1][5]),
             vecs,
             name="sum_norm",
+            scratch=[pltpu.VMEM((rows, width), f32), DMA((1,))],
         )
         second_chunks = gather_rows(second)
         mlp = [None, None]
@@ -843,9 +838,10 @@
                 ),
                 [row_f32, row_bf16],
                 *sums,
-                middle,
+                Far(mlp[1][4]),
                 vecs,
                 name="sum_norm",
+                scratch=[pltpu.VMEM((rows, width), f32), DMA((1,))],
             )
             first_chunks = gather_rows(first)
         else:
@@ -882,7 +878,6 @@
     head_sums = [None] * depth
     placed_mlp = None
     placed_attn = None
-    shard_token = ()
     mlp_token = ()
     for l in reversed(range(depth)):
         attn, pairs, mlp = saved_all[l]
@@ -919,6 +914,7 @@
                 DMA((4,)),
             ],
             limit=16,
+            us=3,
         )
         mlp_part = lax.psum_scatter(mlp_grad, "fsdp", scatter_dimension=0, tiled=True)
         placed_mlp = place_call(
@@ -938,7 +934,7 @@
             upstream,
             vecs,
             name="norm_back_two",
-            after=(grad_token, *shard_token),
+            after=(grad_token,),
             scratch=[pltpu.VMEM((rows, width), f32), DMA((1,))],
         )
         middle_chunks = gather_rows(middle_b)
@@ -1005,11 +1001,9 @@
             )[0]
 
         def weight_grad(after):
-            *parts, head_sum, token = kernel_call(
-                functools.partial(attn_grad_kernel, feats, fsdp),
-                [((width_own, 4 * feats), f32)]
-                + [((width_own, 4 * feats), bf16)] * (fsdp - 1)
-                + [((2, feats), f32), TOKEN],
+            return kernel_call(
+                functools.partial(attn_grad_kernel, feats),
+                [((width, 4 * feats), bf16), ((2, feats), f32), TOKEN],
                 Far(attn[0][3]),
                 Far(attn[1][3]),
                 Far(attn[0][1]),
@@ -1027,29 +1021,22 @@
                     pltpu.VMEM((all_rows, 3 * feats), bf16),
                     DMA((4,)),
                 ],
+                us=3,
             )
-            return parts, head_sum, token
 
         if l > 0:
             far_part = project(1, ())
             near_part = project(0, ())
             sums = reduce_rows(near_part, far_part)
-            parts, head_sums[l], grad_token = weight_grad((sums[0],))
+            attn_grad, head_sums[l], grad_token = weight_grad((sums[0],))
             one_after = (grad_token,)
         else:
-            parts, head_sums[l], grad_token = weight_grad(mlp_token)
+            attn_grad, head_sums[l], grad_token = weight_grad(mlp_token)
             far_part = project(1, (grad_token,))
             near_part = project(0, ())
             sums = reduce_rows(near_part, far_part)
             one_after = ()
-        attn_part, token = kernel_call(
-            shard_sum_kernel,
-            [((width_own, 4 * feats), bf16), TOKEN],
-            parts[0],
-            *[shift_z(parts[d], d) for d in range(1, fsdp)],
-            name="shard_sum",
-        )
-        shard_token = (token,)
+        attn_part = lax.psum_scatter(attn_grad, "fsdp", scatter_dimension=0, tiled=True)
         placed_attn = place_call(
             functools.partial(place_attn_kernel, l, feats),
             spread_grads(attn_part),

time: 455 us -> 404 us (0.89)
  waiting for transfers between devices: 168 us -> 118 us
    ppermute x12 -> x3, waiting for transfers between devices: 89.1 us -> 0.01 us  [shift_z(): lax.ppermute(value, 'fsdp', [(i, (i + d) % fsdp) for i in range(fsdp)])]
    all_gather x2, waiting for transfers between devices: 0.01 us -> 20.1 us  [per_device(): mlp_w.append(lax.all_gather(own, 'fsdp', axis=0, tiled=True))]
    ppermute x22, waiting for transfers between devices: 20.4 us -> 34 us  [swap_x(): return lax.ppermute(value, 'ctx', [(i, i ^ 2) for i in range(ctx)])]
    ppermute x12 -> x3, starting transfers between devices: 12.7 us -> 3.83 us  [shift_z(): lax.ppermute(value, 'fsdp', [(i, (i + d) % fsdp) for i in range(fsdp)])]
    pallas_call x59 -> x57, Pallas kernels: 100 us -> 103 us  [kernel_call(): pl.pallas_call(run, out_shape=out_shape, in_specs=specs, out_specs=out_sp...]
    unnamed x123 -> x111, local copies, waits for them, and re-layouts: 22.8 us -> 20.6 us
  transfers between devices with their start and end apart: 126 -> 120, of which waited for: 43 -> 44; matrix products, arithmetic and copies ran while one was open for 1% -> 1% of each run, Pallas kernels for 19% -> 22%
where the time goes in v4:
time: 404 us; the launch traced here: 398 us
  starting transfers between devices  136 us (34%)
  waiting for transfers between devices  118 us (29%)
  Pallas kernels  103 us (25%)
  local copies, waits for them, and re-layouts  24.5 us (6%)
  between operations  15.9 us (4%)
    pallas_call x57, Pallas kernels, kernel_call(): pl.pallas_call(run, out_shape=out_shape, in_specs=specs, out_specs=out_sp...  103 us
    ppermute x50, starting transfers between devices, swap_core(): return lax.ppermute(value, 'ctx', [(i, i ^ 1) for i in range(ctx)])  75.7 us
    ppermute x22, waiting for transfers between devices, swap_x(): return lax.ppermute(value, 'ctx', [(i, i ^ 2) for i in range(ctx)])  34 us
    ppermute x16, waiting for transfers between devices, swap_xy(): return lax.ppermute(value, ('ctx', 'tp'), pairs)  33.2 us
    ppermute x16, starting transfers between devices, swap_xy(): return lax.ppermute(value, ('ctx', 'tp'), pairs)  21.7 us
    ppermute x19, waiting for transfers between devices, swap_y(): return lax.ppermute(value, 'tp', [(i, i ^ 1) for i in range(tp)])  21.1 us
    unnamed x111, local copies, waits for them, and re-layouts  20.6 us
    all_gather x2, waiting for transfers between devices, per_device(): mlp_w.append(lax.all_gather(own, 'fsdp', axis=0, tiled=True))  20.1 us
  transfers between devices with their start and end apart: 120, of which 44 were waited for; matrix products, arithmetic and copies ran while one was open for 1% of the time, Pallas kernels for 22%

profile of v4, /device:TPU:9, one launch (start us, length us, event | category | flops | bytes accessed | tf_op | source)
XLA Modules:
  0.0 397.8 jit_solution(16018479775150148479)
XLA Ops:
  30.4 2.5 collective-permute-start.11
  44.2 3.5 attn.5
  50.4 2.6 attn.4
  55.9 3.2 collective-permute-done.18.refs_1_
  60.0 3.4 collective-permute-done.20.refs_3_
  70.2 3.7 collective-permute-start.27
  77.1 8.5 %all-gather.7.cloned.1.call-done.refs_4_ = bf16[1024,1024]{1,0:T(8,128)(2,1)} async-done(((bf16[256,1024]{1,0:T(8,128)(2,1)}), bf16[1024,1024]{1,0:T(8,128)(2,1)}) %all-gather.7.cloned.1.call-update) | async-done | bytes 2097168 | tf_op jit(solution)/shard_map/all_gather | solution.py:676
  94.5 2.7 collective-permute-done.29.refs_1_
  98.0 3.6 collective-permute-done.31.refs_3_
  108.3 3.9 collective-permute-start.38
  119.9 2.6 attn.7
  123.5 2.6 attn.6
  129.0 3.3 collective-permute-done.40.refs_1_
  133.0 3.5 collective-permute-done.42.refs_3_
  143.4 3.6 collective-permute-start.49
  149.0 11.6 %all-gather.11.cloned.1.call-done.refs_4_.refs_1_ = bf16[1024,1024]{1,0:T(8,128)(2,1)} async-done(((bf16[256,1024]{1,0:T(8,128)(2,1)}), bf16[1024,1024]{1,0:T(8,128)(2,1)}) %all-gather.11.cloned.1.call-update) | async-done | bytes 2097168 | tf_op jit(solution)/shard_map/all_gather | solution.py:676
  162.2 3.1 mlp.7
  165.3 3.0 mlp_back.5
  169.3 2.7 mlp.6
  176.8 3.3 mlp_grad.2
  184.3 3.4 collective-permute-done.56.refs_1_
  188.5 3.5 collective-permute-done.58.refs_3_
  200.2 3.7 collective-permute-start.65
  205.7 3.6 attn_back.4
  209.4 3.6 attn_back.5
  218.0 2.8 attn_grad.2
  224.6 2.9 collective-permute-done.67.refs_1_
  228.5 3.4 collective-permute-done.69.refs_3_
  241.6 4.2 %collective-permute-start.76 = (bf16[80,1024]{1,0:T(8,128)(2,1)S(1)}, bf16[80,1024]{1,0:T(8,128)(2,1)S(1)}, u32[]{:S(2)}, u32[]{:S(2)}) collective-permute-start(bf16[80,1024]{1,0:T(8,128)(2,1)S(1)} %collective-permute-done.72.refs_3_), channel_id=1, source_target_pairs={{0,2},{2,0},{4,6},{6,4},{1,3},{3,1},{5,7},{7,5},{8,10},{10,8},{12,... | collective-permute-start | bytes 491528 | tf_op jit(solution)/shard_map/ppermute | solution.py:605
  253.9 4.7 %mlp_grad.3 = (bf16[1024,1024]{1,0:T(8,128)(2,1)}, f32[8,128]{1,0:T(8,128)S(1)}) custom-call(bf16[320,1024]{1,0:T(8,128)(2,1)} %get-tuple-element.282.refs_0_, bf16[320,1024]{1,0:T(8,128)(2,1)} %get-tuple-element.283.refs_1_, bf16[320,512]{1,0:T(8,128)(2,1)} %get-tuple-element.284.refs_2_, bf16[320,512]{1,0:T(8,128)(2,1)} %get-tuple-element.285.refs_3_, ...), custom_call_target="tpu_custom_call" | custom-call | flops 3000000000 | tf_op jit(solution)/shard_map/mlp_grad/pallas_call | solution.py:79
  264.2 8.3 %collective-permute-done.89.refs_2_ = bf16[256,1024]{1,0:T(8,128)(2,1)S(1)} collective-permute-done((bf16[256,1024]{1,0:T(8,128)(2,1)}, bf16[256,1024]{1,0:T(8,128)(2,1)S(1)}, u32[]{:S(2)}, u32[]{:S(2)}) %collective-permute-start.89) | collective-permute-done | bytes 524320 | tf_op jit(solution)/shard_map/ppermute | solution.py:608
  276.0 4.2 %collective-permute-done.80.refs_3_ = bf16[80,1024]{1,0:T(8,128)(2,1)S(1)} collective-permute-done((bf16[80,1024]{1,0:T(8,128)(2,1)S(1)}, bf16[80,1024]{1,0:T(8,128)(2,1)S(1)}, u32[]{:S(2)}, u32[]{:S(2)}) %collective-permute-start.80) | collective-permute-done | bytes 163872 | tf_op jit(solution)/shard_map/ppermute | solution.py:617
  285.9 4.1 %collective-permute-done.83.refs_3_ = bf16[80,1024]{1,0:T(8,128)(2,1)S(1)} collective-permute-done((bf16[80,1024]{1,0:T(8,128)(2,1)S(1)}, bf16[80,1024]{1,0:T(8,128)(2,1)S(1)}, u32[]{:S(2)}, u32[]{:S(2)}) %collective-permute-start.83) | collective-permute-done | bytes 163872 | tf_op jit(solution)/shard_map/ppermute | solution.py:617
  294.4 3.6 attn_back.6
  298.1 3.6 attn_back.7
  303.9 3.7 attn_grad.3
  312.4 3.0 collective-permute-done.51.refs_1_
  315.5 4.4 %collective-permute-done.53.refs_3_ = bf16[80,1024]{1,0:T(8,128)(2,1)S(1)} collective-permute-done((bf16[80,1024]{1,0:T(8,128)(2,1)S(1)}, bf16[80,1024]{1,0:T(8,128)(2,1)S(1)}, u32[]{:S(2)}, u32[]{:S(2)}) %collective-permute-start.53) | collective-permute-done | bytes 163872 | tf_op jit(solution)/shard_map/ppermute | solution.py:617
  326.6 4.2 %collective-permute-start.106 = (bf16[256,512]{1,0:T(8,128)(2,1)}, bf16[256,512]{1,0:T(8,128)(2,1)S(1)}, u32[]{:S(2)}, u32[]{:S(2)}) collective-permute-start(bf16[256,512]{1,0:T(8,128)(2,1)} %reduce-scatter.9.cloned.1.call-done.refs_0_), channel_id=1, source_target_pairs={{0,2},{2,0},{4,6},{6,4},{1,3},{3,1},{5,7},{7,5},{8,10},{10,8},{12,... | collective-permute-start | bytes 786440 | tf_op jit(solution)/shard_map/ppermute | solution.py:605
  331.9 3.5 collective-permute-start.108
  339.5 3.8 collective-permute-done.96
  343.3 2.9 collective-permute-start.97
  347.1 3.1 place_attn.2
  350.3 3.2 collective-permute-start.101
  357.2 3.5 collective-permute-start.99
  365.0 9.7 %collective-permute-done.110.refs_2_ = bf16[256,1024]{1,0:T(8,128)(2,1)S(1)} collective-permute-done((bf16[256,1024]{1,0:T(8,128)(2,1)}, bf16[256,1024]{1,0:T(8,128)(2,1)S(1)}, u32[]{:S(2)}, u32[]{:S(2)}) %collective-permute-start.110) | collective-permute-done | bytes 524320 | tf_op jit(solution)/shard_map/ppermute | solution.py:608
  376.2 4.4 %collective-permute-done.104.refs_2_ = bf16[256,512]{1,0:T(8,128)(2,1)S(1)} collective-permute-done((bf16[256,512]{1,0:T(8,128)(2,1)}, bf16[256,512]{1,0:T(8,128)(2,1)S(1)}, u32[]{:S(2)}, u32[]{:S(2)}) %collective-permute-start.104) | collective-permute-done | bytes 262176 | tf_op jit(solution)/shard_map/ppermute | solution.py:608
  385.9 2.8 place_mlp.3
  (434 shorter events, 193.4 us)
Async XLA Ops:
  7.2 32.3 %all-gather.5.cloned.1.call-start = ((), (), s32[]{:S(2)}) async-start(), calls=%async_computation.4 | async-start | bytes 1310720 | tf_op jit(solution)/shard_map/all_gather | solution.py:674
  9.0 76.6 %all-gather.7.cloned.1.call-start = ((), (), s32[]{:S(2)}) async-start(), calls=%async_computation.5 | async-start | bytes 2621440 | tf_op jit(solution)/shard_map/all_gather | solution.py:676
  11.2 104.1 %all-gather.9.cloned.1.call-start = ((), (), s32[]{:S(2)}) async-start(), calls=%async_computation.6 | async-start | bytes 1310720 | tf_op jit(solution)/shard_map/all_gather | solution.py:674
  11.4 11.6 %collective-permute-start.2 = (bf16[17,256]{1,0:T(8,128)(2,1)S(1)}, bf16[17,256]{1,0:T(8,128)(2,1)S(1)}, u32[]{:S(2)}, u32[]{:S(2)}) collective-permute-start(bf16[17,256]{1,0:T(8,128)(2,1)S(1)} %fusion.1), channel_id=1, source_target_pairs={{0,8},{8,16},{16,24},{24,0},{1,9},{9,17},{17,25},{25,1},{2,10},{10... | collective-permute-start | bytes 26120 | tf_op jit(solution)/shard_map/ppermute | solution.py:620
  12.8 10.6 %collective-permute-start.1 = (bf16[17,256]{1,0:T(8,128)(2,1)S(1)}, bf16[17,256]{1,0:T(8,128)(2,1)S(1)}, u32[]{:S(2)}, u32[]{:S(2)}) collective-permute-start(bf16[17,256]{1,0:T(8,128)(2,1)S(1)} %fusion.1), channel_id=1, source_target_pairs={{0,16},{8,24},{16,0},{24,8},{1,17},{9,25},{17,1},{25,9},{2,18},{10... | collective-permute-start | bytes 26120 | tf_op jit(solution)/shard_map/ppermute | solution.py:620
  13.9 9.8 %collective-permute-start = (bf16[17,256]{1,0:T(8,128)(2,1)S(1)}, bf16[17,256]{1,0:T(8,128)(2,1)S(1)}, u32[]{:S(2)}, u32[]{:S(2)}) collective-permute-start(bf16[17,256]{1,0:T(8,128)(2,1)S(1)} %fusion.1), channel_id=1, source_target_pairs={{0,24},{8,0},{16,8},{24,16},{1,25},{9,1},{17,9},{25,17},{2,26},{10... | collective-permute-start | bytes 26120 | tf_op jit(solution)/shard_map/ppermute | solution.py:620
  17.4 10.1 %collective-permute-start.9 = (bf16[80,1024]{1,0:T(8,128)(2,1)S(1)}, bf16[80,1024]{1,0:T(8,128)(2,1)S(1)}, u32[]{:S(2)}, u32[]{:S(2)}) collective-permute-start(bf16[80,1024]{1,0:T(8,128)(2,1)S(1)} %get-tuple-element.178.refs_0_), channel_id=1, source_target_pairs={{0,2},{2,0},{4,6},{6,4},{1,3},{3,1},{5,7},{7,5},{8,10},{10,8},{12,... | collective-permute-start | bytes 491528 | tf_op jit(solution)/shard_map/ppermute | solution.py:605
  18.9 8.8 %collective-permute-start.8 = (bf16[80,1024]{1,0:T(8,128)(2,1)S(1)}, bf16[80,1024]{1,0:T(8,128)(2,1)S(1)}, u32[]{:S(2)}, u32[]{:S(2)}) collective-permute-start(bf16[80,1024]{1,0:T(8,128)(2,1)S(1)} %get-tuple-element.178.refs_0_), channel_id=1, source_target_pairs={{0,5},{1,4},{2,7},{3,6},{4,1},{5,0},{6,3},{7,2},{8,13},{9,12},{10,... | collective-permute-start | bytes 491528 | tf_op jit(solution)/shard_map/ppermute | solution.py:617
  22.9 137.7 %all-gather.11.cloned.1.call-start = ((), (), s32[]{:S(2)}) async-start(), calls=%async_computation.7 | async-start | bytes 2621440 | tf_op jit(solution)/shard_map/all_gather | solution.py:676
  27.8 9.4 %collective-permute-start.3 = (bf16[80,1024]{1,0:T(8,128)(2,1)S(1)}, bf16[80,1024]{1,0:T(8,128)(2,1)}, u32[]{:S(2)}, u32[]{:S(2)}) collective-permute-start(bf16[80,1024]{1,0:T(8,128)(2,1)S(1)} %get-tuple-element.174.refs_0_), channel_id=1, source_target_pairs={{0,1},{1,0},{2,3},{3,2},{4,5},{5,4},{6,7},{7,6},{8,9},{9,8},{10,11... | collective-permute-start | bytes 491528 | tf_op jit(solution)/shard_map/ppermute | solution.py:611
  33.0 9.4 %collective-permute-start.13 = (bf16[80,1024]{1,0:T(8,128)(2,1)S(1)}, bf16[80,1024]{1,0:T(8,128)(2,1)}, u32[]{:S(2)}, u32[]{:S(2)}) collective-permute-start(bf16[80,1024]{1,0:T(8,128)(2,1)S(1)} %get-tuple-element.174.refs_0_), channel_id=1, source_target_pairs={{0,2},{2,0},{4,6},{6,4},{1,3},{3,1},{5,7},{7,5},{8,10},{10,8},{12,... | collective-permute-start | bytes 491528 | tf_op jit(solution)/shard_map/ppermute | solution.py:605
  50.1 208.8 %reduce-scatter.5.cloned.1.call-start = ((), (), s32[]{:S(2)}) async-start(), calls=%async_computation.8 | async-start | bytes 2621440 | tf_op jit(solution)/shard_map/reduce_scatter | solution.py:919
  67.1 8.7 %collective-permute-start.21 = (bf16[80,1024]{1,0:T(8,128)(2,1)S(1)}, bf16[80,1024]{1,0:T(8,128)(2,1)S(1)}, u32[]{:S(2)}, u32[]{:S(2)}) collective-permute-start(bf16[80,1024]{1,0:T(8,128)(2,1)S(1)} %get-tuple-element.193.refs_0_), channel_id=1, source_target_pairs={{0,1},{1,0},{2,3},{3,2},{4,5},{5,4},{6,7},{7,6},{8,9},{9,8},{10,11... | collective-permute-start | bytes 491528 | tf_op jit(solution)/shard_map/ppermute | solution.py:611
  105.1 8.8 %collective-permute-start.32 = (bf16[80,1024]{1,0:T(8,128)(2,1)S(1)}, bf16[80,1024]{1,0:T(8,128)(2,1)}, u32[]{:S(2)}, u32[]{:S(2)}) collective-permute-start(bf16[80,1024]{1,0:T(8,128)(2,1)S(1)} %get-tuple-element.203.refs_0_), channel_id=1, source_target_pairs={{0,1},{1,0},{2,3},{3,2},{4,5},{5,4},{6,7},{7,6},{8,9},{9,8},{10,11... | collective-permute-start | bytes 491528 | tf_op jit(solution)/shard_map/ppermute | solution.py:611
  105.5 12.7 %collective-permute-start.35 = (bf16[80,1024]{1,0:T(8,128)(2,1)S(1)}, bf16[80,1024]{1,0:T(8,128)(2,1)}, u32[]{:S(2)}, u32[]{:S(2)}) collective-permute-start(bf16[80,1024]{1,0:T(8,128)(2,1)S(1)} %get-tuple-element.203.refs_0_), channel_id=1, source_target_pairs={{0,2},{2,0},{4,6},{6,4},{1,3},{3,1},{5,7},{7,5},{8,10},{10,8},{12,... | collective-permute-start | bytes 491528 | tf_op jit(solution)/shard_map/ppermute | solution.py:605
  108.3 9.9 %collective-permute-start.38 = (bf16[80,1024]{1,0:T(8,128)(2,1)}, bf16[80,1024]{1,0:T(8,128)(2,1)}, u32[]{:S(2)}, u32[]{:S(2)}) collective-permute-start(bf16[80,1024]{1,0:T(8,128)(2,1)} %collective-permute-done.34.refs_3_), channel_id=1, source_target_pairs={{0,2},{2,0},{4,6},{6,4},{1,3},{3,1},{5,7},{7,5},{8,10},{10,8},{12,... | collective-permute-start | bytes 491528 | tf_op jit(solution)/shard_map/ppermute | solution.py:605
  140.2 8.7 %collective-permute-start.43 = (bf16[80,1024]{1,0:T(8,128)(2,1)S(1)}, bf16[80,1024]{1,0:T(8,128)(2,1)}, u32[]{:S(2)}, u32[]{:S(2)}) collective-permute-start(bf16[80,1024]{1,0:T(8,128)(2,1)S(1)} %get-tuple-element.217.refs_0_), channel_id=1, source_target_pairs={{0,1},{1,0},{2,3},{3,2},{4,5},{5,4},{6,7},{7,6},{8,9},{9,8},{10,11... | collective-permute-start | bytes 491528 | tf_op jit(solution)/shard_map/ppermute | solution.py:611
  140.5 20.1 %collective-permute-start.46 = (bf16[80,1024]{1,0:T(8,128)(2,1)S(1)}, bf16[80,1024]{1,0:T(8,128)(2,1)}, u32[]{:S(2)}, u32[]{:S(2)}) collective-permute-start(bf16[80,1024]{1,0:T(8,128)(2,1)S(1)} %get-tuple-element.217.refs_0_), channel_id=1, source_target_pairs={{0,2},{2,0},{4,6},{6,4},{1,3},{3,1},{5,7},{7,5},{8,10},{10,8},{12,... | collective-permute-start | bytes 491528 | tf_op jit(solution)/shard_map/ppermute | solution.py:605
  143.4 17.2 %collective-permute-start.49 = (bf16[80,1024]{1,0:T(8,128)(2,1)S(1)}, bf16[80,1024]{1,0:T(8,128)(2,1)}, u32[]{:S(2)}, u32[]{:S(2)}) collective-permute-start(bf16[80,1024]{1,0:T(8,128)(2,1)S(1)} %collective-permute-done.45.refs_3_), channel_id=1, source_target_pairs={{0,2},{2,0},{4,6},{6,4},{1,3},{3,1},{5,7},{7,5},{8,10},{10,8},{12,... | collective-permute-start | bytes 491528 | tf_op jit(solution)/shard_map/ppermute | solution.py:605
  147.0 13.6 %collective-permute-start.48 = (bf16[80,1024]{1,0:T(8,128)(2,1)S(1)}, bf16[80,1024]{1,0:T(8,128)(2,1)}, u32[]{:S(2)}, u32[]{:S(2)}) collective-permute-start(bf16[80,1024]{1,0:T(8,128)(2,1)S(1)} %collective-permute-done.44.refs_2_), channel_id=1, source_target_pairs={{0,2},{2,0},{4,6},{6,4},{1,3},{3,1},{5,7},{7,5},{8,10},{10,8},{12,... | collective-permute-start | bytes 491528 | tf_op jit(solution)/shard_map/ppermute | solution.py:605
  148.8 11.7 %collective-permute-start.47 = (bf16[80,1024]{1,0:T(8,128)(2,1)}, bf16[80,1024]{1,0:T(8,128)(2,1)}, u32[]{:S(2)}, u32[]{:S(2)}) collective-permute-start(bf16[80,1024]{1,0:T(8,128)(2,1)} %collective-permute-done.43.refs_1_), channel_id=1, source_target_pairs={{0,2},{2,0},{4,6},{6,4},{1,3},{3,1},{5,7},{7,5},{8,10},{10,8},{12,... | collective-permute-start | bytes 491528 | tf_op jit(solution)/shard_map/ppermute | solution.py:605
  181.5 138.7 %reduce-scatter.9.cloned.1.call-start = ((), (), s32[]{:S(2)}) async-start(), calls=%async_computation.10 | async-start | bytes 1310720 | tf_op jit(solution)/shard_map/reduce_scatter | solution.py:1039
  197.4 12.0 %collective-permute-start.62 = (bf16[80,1024]{1,0:T(8,128)(2,1)S(1)}, bf16[80,1024]{1,0:T(8,128)(2,1)S(1)}, u32[]{:S(2)}, u32[]{:S(2)}) collective-permute-start(bf16[80,1024]{1,0:T(8,128)(2,1)S(1)} %get-tuple-element.249.refs_0_), channel_id=1, source_target_pairs={{0,2},{2,0},{4,6},{6,4},{1,3},{3,1},{5,7},{7,5},{8,10},{10,8},{12,... | collective-permute-start | bytes 491528 | tf_op jit(solution)/shard_map/ppermute | solution.py:605
  200.2 9.2 %collective-permute-start.65 = (bf16[80,1024]{1,0:T(8,128)(2,1)S(1)}, bf16[80,1024]{1,0:T(8,128)(2,1)S(1)}, u32[]{:S(2)}, u32[]{:S(2)}) collective-permute-start(bf16[80,1024]{1,0:T(8,128)(2,1)S(1)} %collective-permute-done.61.refs_3_), channel_id=1, source_target_pairs={{0,2},{2,0},{4,6},{6,4},{1,3},{3,1},{5,7},{7,5},{8,10},{10,8},{12,... | collective-permute-start | bytes 491528 | tf_op jit(solution)/shard_map/ppermute | solution.py:605
  221.8 139.0 %reduce-scatter.11.cloned.1.call-start = ((), (), s32[]{:S(2)}) async-start(), calls=%async_computation.11 | async-start | bytes 2621440 | tf_op jit(solution)/shard_map/reduce_scatter | solution.py:919
  258.6 104.2 %reduce-scatter.7.cloned.1.call-start = ((), (), s32[]{:S(2)}) async-start(), calls=%async_computation.9 | async-start | bytes 1310720 | tf_op jit(solution)/shard_map/reduce_scatter | solution.py:1039
  258.9 13.6 %collective-permute-start.89 = (bf16[256,1024]{1,0:T(8,128)(2,1)}, bf16[256,1024]{1,0:T(8,128)(2,1)S(1)}, u32[]{:S(2)}, u32[]{:S(2)}) collective-permute-start(bf16[256,1024]{1,0:T(8,128)(2,1)} %reduce-scatter.5.cloned.1.call-done.refs_0_), channel_id=1, source_target_pairs={{0,4},{2,6},{4,0},{6,2},{1,5},{3,7},{5,1},{7,3},{8,12},{10,14},{12... | collective-permute-start | bytes 1572872 | tf_op jit(solution)/shard_map/ppermute | solution.py:608
  260.2 14.1 %collective-permute-start.78 = (bf16[80,1024]{1,0:T(8,128)(2,1)S(1)}, bf16[80,1024]{1,0:T(8,128)(2,1)S(1)}, u32[]{:S(2)}, u32[]{:S(2)}) collective-permute-start(bf16[80,1024]{1,0:T(8,128)(2,1)S(1)} %get-tuple-element.278), channel_id=1, source_target_pairs={{0,1},{1,0},{2,3},{3,2},{4,5},{5,4},{6,7},{7,6},{8,9},{9,8},{10,11... | collective-permute-start | bytes 491528 | tf_op jit(solution)/shard_map/ppermute | solution.py:611
  261.1 14.9 %collective-permute-start.79 = (bf16[80,1024]{1,0:T(8,128)(2,1)S(1)}, bf16[80,1024]{1,0:T(8,128)(2,1)S(1)}, u32[]{:S(2)}, u32[]{:S(2)}) collective-permute-start(bf16[80,1024]{1,0:T(8,128)(2,1)S(1)} %get-tuple-element.279), channel_id=1, source_target_pairs={{0,4},{2,6},{4,0},{6,2},{1,5},{3,7},{5,1},{7,3},{8,12},{10,14},{12... | collective-permute-start | bytes 491528 | tf_op jit(solution)/shard_map/ppermute | solution.py:608
  261.4 18.9 %collective-permute-start.80 = (bf16[80,1024]{1,0:T(8,128)(2,1)S(1)}, bf16[80,1024]{1,0:T(8,128)(2,1)S(1)}, u32[]{:S(2)}, u32[]{:S(2)}) collective-permute-start(bf16[80,1024]{1,0:T(8,128)(2,1)S(1)} %get-tuple-element.280), channel_id=1, source_target_pairs={{0,5},{1,4},{2,7},{3,6},{4,1},{5,0},{6,3},{7,2},{8,13},{9,12},{10,... | collective-permute-start | bytes 491528 | tf_op jit(solution)/shard_map/ppermute | solution.py:617
  262.8 38.9 %collective-permute-start.88 = (bf16[256,1024]{1,0:T(8,128)(2,1)}, bf16[256,1024]{1,0:T(8,128)(2,1)S(1)}, u32[]{:S(2)}, u32[]{:S(2)}) collective-permute-start(bf16[256,1024]{1,0:T(8,128)(2,1)} %reduce-scatter.5.cloned.1.call-done.refs_0_), channel_id=1, source_target_pairs={{0,2},{2,0},{4,6},{6,4},{1,3},{3,1},{5,7},{7,5},{8,10},{10,8},{12,... | collective-permute-start | bytes 1572872 | tf_op jit(solution)/shard_map/ppermute | solution.py:605
  272.5 29.2 %collective-permute-start.90 = (bf16[256,1024]{1,0:T(8,128)(2,1)S(1)}, bf16[256,1024]{1,0:T(8,128)(2,1)S(1)}, u32[]{:S(2)}, u32[]{:S(2)}) collective-permute-start(bf16[256,1024]{1,0:T(8,128)(2,1)S(1)} %collective-permute-done.89.refs_2_), channel_id=1, source_target_pairs={{0,2},{2,0},{4,6},{6,4},{1,3},{3,1},{5,7},{7,5},{8,10},{10,8},{12,... | collective-permute-start | bytes 1572872 | tf_op jit(solution)/shard_map/ppermute | solution.py:605
  285.0 8.9 %collective-permute-start.81 = (bf16[80,1024]{1,0:T(8,128)(2,1)S(1)}, bf16[80,1024]{1,0:T(8,128)(2,1)S(1)}, u32[]{:S(2)}, u32[]{:S(2)}) collective-permute-start(bf16[80,1024]{1,0:T(8,128)(2,1)S(1)} %get-tuple-element.291.refs_0_), channel_id=1, source_target_pairs={{0,1},{1,0},{2,3},{3,2},{4,5},{5,4},{6,7},{7,6},{8,9},{9,8},{10,11... | collective-permute-start | bytes 491528 | tf_op jit(solution)/shard_map/ppermute | solution.py:611
  294.3 15.2 %collective-permute-start.50 = (bf16[320,1024]{1,0:T(8,128)(2,1)}, bf16[320,1024]{1,0:T(8,128)(2,1)S(1)}, u32[]{:S(2)}, u32[]{:S(2)}) collective-permute-start(bf16[320,1024]{1,0:T(8,128)(2,1)} %copy-done.43), channel_id=1, source_target_pairs={{0,2},{2,0},{4,6},{6,4},{1,3},{3,1},{5,7},{7,5},{8,10},{10,8},{12,... | collective-permute-start | bytes 1966088 | tf_op jit(solution)/shard_map/ppermute | solution.py:605
  309.1 13.9 %collective-permute-start.91 = (bf16[320,1024]{1,0:T(8,128)(2,1)}, bf16[320,1024]{1,0:T(8,128)(2,1)S(1)}, u32[]{:S(2)}, u32[]{:S(2)}) collective-permute-start(bf16[320,1024]{1,0:T(8,128)(2,1)} %project.7), channel_id=1, source_target_pairs={{0,2},{2,0},{4,6},{6,4},{1,3},{3,1},{5,7},{7,5},{8,10},{10,8},{12,... | collective-permute-start | bytes 1966088 | tf_op jit(solution)/shard_map/ppermute | solution.py:605
  319.9 26.3 %collective-permute-start.54 = (f32[80,1024]{1,0:T(8,128)S(1)}, f32[80,1024]{1,0:T(8,128)S(1)}, u32[]{:S(2)}, u32[]{:S(2)}) collective-permute-start(f32[80,1024]{1,0:T(8,128)S(1)} %sum_out.1.refs_0_), channel_id=1, source_target_pairs={{0,1},{1,0},{2,3},{3,2},{4,5},{5,4},{6,7},{7,6},{8,9},{9,8},{10,11... | collective-permute-start | bytes 983048 | tf_op jit(solution)/shard_map/ppermute | solution.py:611
  323.2 8.8 %collective-permute-start.92 = (bf16[80,1024]{1,0:T(8,128)(2,1)S(1)}, bf16[80,1024]{1,0:T(8,128)(2,1)S(1)}, u32[]{:S(2)}, u32[]{:S(2)}) collective-permute-start(bf16[80,1024]{1,0:T(8,128)(2,1)S(1)} %get-tuple-element.312), channel_id=1, source_target_pairs={{0,1},{1,0},{2,3},{3,2},{4,5},{5,4},{6,7},{7,6},{8,9},{9,8},{10,11... | collective-permute-start | bytes 491528 | tf_op jit(solution)/shard_map/ppermute | solution.py:611
  324.5 10.9 %collective-permute-start.93 = (bf16[80,1024]{1,0:T(8,128)(2,1)S(1)}, bf16[80,1024]{1,0:T(8,128)(2,1)S(1)}, u32[]{:S(2)}, u32[]{:S(2)}) collective-permute-start(bf16[80,1024]{1,0:T(8,128)(2,1)S(1)} %get-tuple-element.313), channel_id=1, source_target_pairs={{0,4},{2,6},{4,0},{6,2},{1,5},{3,7},{5,1},{7,3},{8,12},{10,14},{12... | collective-permute-start | bytes 491528 | tf_op jit(solution)/shard_map/ppermute | solution.py:608
  324.8 10.7 %collective-permute-start.94 = (bf16[80,1024]{1,0:T(8,128)(2,1)S(1)}, bf16[80,1024]{1,0:T(8,128)(2,1)S(1)}, u32[]{:S(2)}, u32[]{:S(2)}) collective-permute-start(bf16[80,1024]{1,0:T(8,128)(2,1)S(1)} %get-tuple-element.314), channel_id=1, source_target_pairs={{0,5},{1,4},{2,7},{3,6},{4,1},{5,0},{6,3},{7,2},{8,13},{9,12},{10,... | collective-permute-start | bytes 491528 | tf_op jit(solution)/shard_map/ppermute | solution.py:617
  326.6 20.5 %collective-permute-start.106 = (bf16[256,512]{1,0:T(8,128)(2,1)}, bf16[256,512]{1,0:T(8,128)(2,1)S(1)}, u32[]{:S(2)}, u32[]{:S(2)}) collective-permute-start(bf16[256,512]{1,0:T(8,128)(2,1)} %reduce-scatter.9.cloned.1.call-done.refs_0_), channel_id=1, source_target_pairs={{0,2},{2,0},{4,6},{6,4},{1,3},{3,1},{5,7},{7,5},{8,10},{10,8},{12,... | collective-permute-start | bytes 786440 | tf_op jit(solution)/shard_map/ppermute | solution.py:605
  331.9 15.2 %collective-permute-start.108 = (bf16[256,512]{1,0:T(8,128)(2,1)}, bf16[256,512]{1,0:T(8,128)(2,1)S(1)}, u32[]{:S(2)}, u32[]{:S(2)}) collective-permute-start(bf16[256,512]{1,0:T(8,128)(2,1)} %collective-permute-done.107.refs_2_), channel_id=1, source_target_pairs={{0,2},{2,0},{4,6},{6,4},{1,3},{3,1},{5,7},{7,5},{8,10},{10,8},{12,... | collective-permute-start | bytes 786440 | tf_op jit(solution)/shard_map/ppermute | solution.py:605
  350.2 33.7 %collective-permute-start.95 = (f32[80,1024]{1,0:T(8,128)S(1)}, f32[80,1024]{1,0:T(8,128)S(1)}, u32[]{:S(2)}, u32[]{:S(2)}) collective-permute-start(f32[80,1024]{1,0:T(8,128)S(1)} %get-tuple-element.316.refs_0_), channel_id=1, source_target_pairs={{0,1},{1,0},{2,3},{3,2},{4,5},{5,4},{6,7},{7,6},{8,9},{9,8},{10,11... | collective-permute-start | bytes 983048 | tf_op jit(solution)/shard_map/ppermute | solution.py:611
  360.8 13.8 %collective-permute-start.110 = (bf16[256,1024]{1,0:T(8,128)(2,1)}, bf16[256,1024]{1,0:T(8,128)(2,1)S(1)}, u32[]{:S(2)}, u32[]{:S(2)}) collective-permute-start(bf16[256,1024]{1,0:T(8,128)(2,1)} %reduce-scatter.11.cloned.1.call-done.refs_0_), channel_id=1, source_target_pairs={{0,4},{2,6},{4,0},{6,2},{1,5},{3,7},{5,1},{7,3},{8,12},{10,14},{12... | collective-permute-start | bytes 1572872 | tf_op jit(solution)/shard_map/ppermute | solution.py:608
  362.3 13.8 %collective-permute-start.100 = (f32[12,256]{1,0:T(8,128)S(1)}, f32[12,256]{1,0:T(8,128)S(1)}, u32[]{:S(2)}, u32[]{:S(2)}) collective-permute-start(f32[12,256]{1,0:T(8,128)S(1)} %add.100), channel_id=1, source_target_pairs={{0,4},{2,6},{4,0},{6,2},{1,5},{3,7},{5,1},{7,3},{8,12},{10,14},{12... | collective-permute-start | bytes 36872 | tf_op jit(solution)/shard_map/ppermute | solution.py:608
  362.9 17.8 %collective-permute-start.104 = (bf16[256,512]{1,0:T(8,128)(2,1)}, bf16[256,512]{1,0:T(8,128)(2,1)S(1)}, u32[]{:S(2)}, u32[]{:S(2)}) collective-permute-start(bf16[256,512]{1,0:T(8,128)(2,1)} %reduce-scatter.7.cloned.1.call-done.refs_0_), channel_id=1, source_target_pairs={{0,4},{2,6},{4,0},{6,2},{1,5},{3,7},{5,1},{7,3},{8,12},{10,14},{12... | collective-permute-start | bytes 786440 | tf_op jit(solution)/shard_map/ppermute | solution.py:608
  364.1 20.7 %collective-permute-start.109 = (bf16[256,1024]{1,0:T(8,128)(2,1)}, bf16[256,1024]{1,0:T(8,128)(2,1)S(1)}, u32[]{:S(2)}, u32[]{:S(2)}) collective-permute-start(bf16[256,1024]{1,0:T(8,128)(2,1)} %reduce-scatter.11.cloned.1.call-done.refs_0_), channel_id=1, source_target_pairs={{0,2},{2,0},{4,6},{6,4},{1,3},{3,1},{5,7},{7,5},{8,10},{10,8},{12,... | collective-permute-start | bytes 1572872 | tf_op jit(solution)/shard_map/ppermute | solution.py:605
  374.7 10.1 %collective-permute-start.111 = (bf16[256,1024]{1,0:T(8,128)(2,1)S(1)}, bf16[256,1024]{1,0:T(8,128)(2,1)S(1)}, u32[]{:S(2)}, u32[]{:S(2)}) collective-permute-start(bf16[256,1024]{1,0:T(8,128)(2,1)S(1)} %collective-permute-done.110.refs_2_), channel_id=1, source_target_pairs={{0,2},{2,0},{4,6},{6,4},{1,3},{3,1},{5,7},{7,5},{8,10},{10,8},{12,... | collective-permute-start | bytes 1572872 | tf_op jit(solution)/shard_map/ppermute | solution.py:605
  376.1 12.6 %collective-permute-start.103 = (bf16[256,512]{1,0:T(8,128)(2,1)}, bf16[256,512]{1,0:T(8,128)(2,1)S(1)}, u32[]{:S(2)}, u32[]{:S(2)}) collective-permute-start(bf16[256,512]{1,0:T(8,128)(2,1)} %reduce-scatter.7.cloned.1.call-done.refs_0_), channel_id=1, source_target_pairs={{0,2},{2,0},{4,6},{6,4},{1,3},{3,1},{5,7},{7,5},{8,10},{10,8},{12,... | collective-permute-start | bytes 786440 | tf_op jit(solution)/shard_map/ppermute | solution.py:605
  (124 other events, 622.2 us)
Sparse Core Ops, SparseCore 0:
  10.2 28.8 all-gather.4
  41.2 44.3 all-gather.6
  87.2 28.0 all-gather.8
  116.7 43.8 all-gather.10
  181.6 41.2 reduce-scatter.4
  225.7 26.8 reduce-scatter.8
  258.8 41.2 reduce-scatter.10
  321.6 25.7 reduce-scatter.6

commit v5 on v4

--- a/solution.py
+++ b/solution.py
@@ -13,7 +13,7 @@
 ROOT_HALF = 0.7071067811865476
 INV_ROOT_TAU = 0.3989422804014327
 GROUP = 4
-ORDER = (0, 1, 4, 5, 2, 3, 6, 7)
+ORDER = (0, 5, 4, 1, 2, 7, 6, 3)
 CHIPS = 4
 
 bf16 = jnp.bfloat16
@@ -273,21 +273,50 @@
         copy.wait()
 
 
-def core_sum_kernel(near, far, own_ref, y_ref, x_ref, xy_ref):
-    rows = own_ref.shape[0]
-    for k, ref in enumerate((own_ref, y_ref, x_ref, xy_ref)):
-        span = slice(k * rows, (k + 1) * rows)
-        ref[...] = (near[span, :].astype(f32) + far[span, :].astype(f32)).astype(ref.dtype)
-
-
-def total_of(own, y, x, xy):
-    return own[...] + y[...].astype(f32) + x[...].astype(f32) + xy[...].astype(f32)
-
-
-def sum_norm_kernel(bias_row, gain_row, shift_row, own, y, x, xy, residual_hbm, vecs,
+def touch_kernel(source, token):
+    token[...] = jnp.zeros_like(token)
+
+
+def vector_sum_kernel(*refs):
+    *terms, out_ref, token = refs
+    total = terms[0][...]
+    for term in terms[1:]:
+        total = total + term[...]
+    out_ref[...] = total
+    token[...] = jnp.zeros_like(token)
+
+
+def copy_kernel(source, target):
+    target[...] = source[...]
+
+
+def core_sum_kernel(count, *refs):
+    pairs, owns = refs[: 2 * count], refs[2 * count : 3 * count]
+    peers = refs[3 * count :]
+    rows = owns[0].shape[0]
+    for j in range(count):
+        near, far = pairs[2 * j], pairs[2 * j + 1]
+        for k in range(1 + len(peers)):
+            span = slice(k * rows, (k + 1) * rows)
+            total = near[span, :].astype(f32) + far[span, :].astype(f32)
+            if k == 0:
+                owns[j][...] = total
+            else:
+                peers[k - 1][j * rows : (j + 1) * rows, :] = total.astype(bf16)
+
+
+def total_of(own, xy, x, y, part=0):
+    rows = own.shape[0]
+    span = slice(part * rows, (part + 1) * rows)
+    return (
+        own[...] + y[span, :].astype(f32) + x[span, :].astype(f32) + xy[span, :].astype(f32)
+    )
+
+
+def sum_norm_kernel(bias_row, gain_row, shift_row, own, xy, x, y, residual_hbm, vecs,
                     stream_ref, normed_ref, residual, sems):
     copies = start_copies([(residual_hbm, residual)], sems)
-    total = total_of(own, y, x, xy) + vecs[bias_row : bias_row + 1, :]
+    total = total_of(own, xy, x, y) + vecs[bias_row : bias_row + 1, :]
     copies[0].wait()
     stream = residual[...] + total
     stream_ref[...] = stream
@@ -296,17 +325,26 @@
     normed_ref[...] = (normed * gain + vecs[shift_row : shift_row + 1, :]).astype(bf16)
 
 
-def sum_out_kernel(bias_row, own, y, x, xy, residual, vecs, mask, out_ref):
-    stream = residual[...] + total_of(own, y, x, xy) + vecs[bias_row : bias_row + 1, :]
-    out_ref[...] = stream * mask[:, 0:1]
-
-
-def mlp_kernel(hidden, keep_count, c0, c1, c2, c3, w, bias, *refs):
+def sum_out_kernel(bias_row, own, xy, x, y, residual_hbm, vecs, mask, out_ref, residual, sems):
+    copies = start_copies([(residual_hbm, residual)], sems)
+    total = total_of(own, xy, x, y, 1) + vecs[bias_row : bias_row + 1, :]
+    copies[0].wait()
+    out_ref[...] = (residual[...] + total) * mask[:, 0:1]
+
+
+def mlp_kernel(hidden, keep_count, saves, c0, c1, c2, c3, w, bias, *refs):
     kept, rest = refs[:keep_count], refs[keep_count:]
-    partial_ref, x_hbm, act_hbm, slope_hbm, *rest = rest
-    kept_hbm, (x, act_ref, slope_ref, sems) = rest[:keep_count], rest[keep_count:]
+    partial_ref, x_out, act_out, slope_out, *rest = rest
+    kept_hbm, rest = rest[:keep_count], rest[keep_count:]
+    if saves:
+        x, act_ref, slope_ref, sems = rest
+    else:
+        x, act_ref, slope_ref = x_out, act_out, slope_out
+        (sems,) = rest
+    copies = start_copies(list(zip(kept, kept_hbm)), sems)
     assemble((c0, c1, c2, c3), x)
-    copies = start_copies([(x, x_hbm), *zip(kept, kept_hbm)], sems)
+    if saves:
+        copies += start_copies([(x, x_out)], sems.at[pl.ds(keep_count, 1)])
     block = hidden // 2
     for k in range(2):
         span = slice(k * block, (k + 1) * block)
@@ -315,10 +353,12 @@
         density = jnp.exp(-0.5 * pre * pre) * INV_ROOT_TAU
         slope_ref[k] = cdf + pre * density
         act_ref[:, span] = (pre * cdf).astype(bf16)
-        copies += start_copies(
-            [(slope_ref.at[k], slope_hbm.at[k])], sems.at[pl.ds(1 + keep_count + k, 1)]
-        )
-    copies += start_copies([(act_ref, act_hbm)], sems.at[pl.ds(3 + keep_count, 1)])
+        if saves:
+            copies += start_copies(
+                [(slope_ref.at[k], slope_out.at[k])], sems.at[pl.ds(1 + keep_count + k, 1)]
+            )
+    if saves:
+        copies += start_copies([(act_ref, act_out)], sems.at[pl.ds(3 + keep_count, 1)])
     partial_ref[...] = dot_nt(act_ref[...], w[:, hidden:]).astype(bf16)
     for copy in copies:
         copy.wait()
@@ -376,11 +416,11 @@
     return back, gain_grad, jnp.sum(upstream, axis=0, keepdims=True)
 
 
-def norm_back_two_kernel(gain_row, own, y, x, xy, values_hbm, upstream, vecs,
+def norm_back_two_kernel(gain_row, own, xy, x, y, values_hbm, upstream, vecs,
                          grad_ref, grad_b_ref, sums_ref, values, sems):
     copies = start_copies([(values_hbm, values)], sems)
     up = upstream[...]
-    total = total_of(own, y, x, xy)
+    total = total_of(own, xy, x, y)
     copies[0].wait()
     back, gain_grad, shift_grad = norm_back(
         total, values[...], vecs[gain_row : gain_row + 1, :]
@@ -394,10 +434,10 @@
     sums_ref[3:4, :] = jnp.sum(up, axis=0, keepdims=True)
 
 
-def norm_back_one_kernel(gain_row, own, y, x, xy, values_hbm, upstream, vecs, mask,
+def norm_back_one_kernel(gain_row, own, xy, x, y, values_hbm, upstream, vecs, mask,
                          grad_ref, grad_b_ref, sums_ref, values, sems):
     copies = start_copies([(values_hbm, values)], sems)
-    total = total_of(own, y, x, xy)
+    total = total_of(own, xy, x, y)
     copies[0].wait()
     back, gain_grad, shift_grad = norm_back(
         total, values[...], vecs[gain_row : gain_row + 1, :]
@@ -481,8 +521,8 @@
 
 
 def attn_grad_kernel(feats, first_near, first_far, att_near, att_far, up_near, up_far,
-                     gq_near, gq_far, gk, gv, out_ref, sums_ref, token,
-                     first, att, up, packed, sems):
+                     gq_near, gq_far, gk, gv, *refs):
+    *outs, sums_ref, token, first, att, up, packed, sems = refs
     rows = up_near.shape[0]
     near, far = pl.ds(0, rows), pl.ds(rows, rows)
     copies = start_copies(
@@ -506,9 +546,20 @@
     sums_ref[1:2, :] = jnp.sum(gv[...], axis=0, keepdims=True)
     for copy in copies:
         copy.wait()
-    out_ref[:, : 3 * feats] = dot_tn(first[...], packed[...]).astype(bf16)
-    out_ref[:, 3 * feats :] = dot_tn(up[...], att[...]).astype(bf16)
+    width_own = outs[0].shape[0]
+    for d, out_ref in enumerate(outs):
+        place = lax.rem(lax.axis_index("fsdp") + d, len(outs)) if len(outs) > 1 else 0
+        span = pl.ds(place * width_own, width_own)
+        if len(outs) > 1:
+            span = pl.ds(pl.multiple_of(place * width_own, width_own), width_own)
+        out_ref[:, : 3 * feats] = dot_tn(first[:, span], packed[...]).astype(bf16)
+        out_ref[:, 3 * feats :] = dot_tn(up[:, span], att[...]).astype(bf16)
     token[...] = jnp.zeros_like(token)
+
+
+def shard_sum_kernel(*refs):
+    *terms, out_ref = refs
+    out_ref[...] = sum(term[...].astype(f32) for term in terms).astype(out_ref.dtype)
 
 
 def place_mlp_kernel(layer, hidden, p0, p1, p2, p3, *refs):
@@ -622,19 +673,28 @@
     outer_groups = [[o * GROUP + i for o in range(outer)] for i in range(GROUP)]
 
     def gather_rows(own):
-        near = (own, swap_y(own), swap_x(own), swap_xy(own))
+        near = (own, swap_xy(own), swap_x(own), swap_y(own))
         return near, tuple(swap_core(chunk) for chunk in near)
 
-    def reduce_rows(near, far):
-        own, y, x, xy = kernel_call(
-            core_sum_kernel,
-            [((rows, width), f32)] + [((rows, width), bf16)] * 3,
-            near,
-            swap_core(far),
+    def gate(value, after):
+        return kernel_call(
+            copy_kernel, [(value.shape, value.dtype)], value, name="gate", after=after
+        )[0]
+
+    def touch(value):
+        return kernel_call(touch_kernel, [TOKEN], value, name="touch")[0]
+
+    def reduce_rows(*pairs, after=()):
+        count = len(pairs)
+        *owns, xy, x, y = kernel_call(
+            functools.partial(core_sum_kernel, count),
+            [((rows, width), f32)] * count + [((count * rows, width), bf16)] * 3,
+            *[v for near, far in pairs for v in (near, swap_core(far))],
             name="core_sum",
+            after=after,
         )
-        xy, x, y = swap_xy(xy), swap_x(x), swap_y(y)
-        return own, y, x, xy
+        peers = (swap_xy(xy), swap_x(x), swap_y(y))
+        return [(own, *peers) for own in owns]
 
     def pack_attn(l, after):
         return kernel_call(
@@ -794,7 +854,7 @@
                     DMA((len(kept) + 2,)),
                 ],
             )
-        sums = reduce_rows(attn[0][0], attn[1][0])
+        (sums,) = reduce_rows((attn[0][0], attn[1][0]))
         middle, second = kernel_call(
             functools.partial(sum_norm_kernel, shift_row(l, 2), gain_row(l, 1), shift_row(l, 1)),
             [row_f32, row_bf16],
@@ -808,30 +868,30 @@
         mlp = [None, None]
         for side in (1, 0):
             kept = (middle,) if side == 1 else ()
+            saves = l + 1 < depth
+            shapes = [
+                ((half, width), bf16),
+                ((half, hidden), bf16),
+                ((2, half, hidden // 2), f32),
+            ]
             mlp[side] = kernel_call(
-                functools.partial(mlp_kernel, hidden, len(kept)),
-                [
-                    partial_out,
-                    saved((half, width), bf16),
-                    saved((half, hidden), bf16),
-                    saved((2, half, hidden // 2), f32),
-                ]
+                functools.partial(mlp_kernel, hidden, len(kept), saves),
+                [partial_out]
+                + [saved(*shape) if saves else shape for shape in shapes]
                 + [saved(k.shape, k.dtype) for k in kept],
                 *second_chunks[side],
                 mlp_w[l],
                 fc1_all[l],
                 *kept,
                 name="mlp",
-                scratch=[
-                    half_x,
-                    pltpu.VMEM((half, hidden), bf16),
-                    pltpu.VMEM((2, half, hidden // 2), f32),
-                    DMA((4 + len(kept),)),
-                ],
-            )
-        sums = reduce_rows(mlp[0][0], mlp[1][0])
+                scratch=[pltpu.VMEM(*shape) for shape in shapes if saves]
+                + [DMA((4 + len(kept),))],
+            )
+            if saves:
+                mlp[side] = [mlp[side][0], *[Far(v) for v in mlp[side][1:4]], *mlp[side][4:]]
         saved_all.append((attn, pairs if outer > 1 else None, mlp))
         if l + 1 < depth:
+            (sums,) = reduce_rows((mlp[0][0], mlp[1][0]))
             stream, first = kernel_call(
                 functools.partial(
                     sum_norm_kernel, shift_row(l, 3), gain_row(l + 1, 0), shift_row(l + 1, 0)
@@ -844,41 +904,18 @@
                 scratch=[pltpu.VMEM((rows, width), f32), DMA((1,))],
             )
             first_chunks = gather_rows(first)
-        else:
-            outputs_own = kernel_call(
-                functools.partial(sum_out_kernel, shift_row(l, 3)),
-                [row_f32],
-                *sums,
-                middle,
-                vecs,
-                mask,
-                name="sum_out",
-            )[0]
-
-    def both_halves(own):
-        return kernel_call(
-            place_rows_kernel,
-            [saved(inputs.shape, f32)],
-            own,
-            swap_y(own),
-            name="place_rows",
-            scratch=[DMA((2,))],
-        )[0]
-
-    outputs = both_halves(outputs_own)
-
-    def spread_grads(part):
+
+    def scatter_grads(grad):
+        part = lax.psum_scatter(grad, "fsdp", scatter_dimension=0, tiled=True)
         if outer > 1:
             part = lax.psum(part, "ctx", axis_index_groups=outer_groups)
-        other = swap_x(part)
-        return part, swap_core(part), other, swap_core(other)
+        return part
 
     row_sums = [None] * depth
     unit_sums = [None] * depth
     head_sums = [None] * depth
-    placed_mlp = None
-    placed_attn = None
-    mlp_token = ()
+    mlp_parts = [None] * depth
+    attn_parts = [None] * depth
     for l in reversed(range(depth)):
         attn, pairs, mlp = saved_all[l]
         back = [None, None]
@@ -888,24 +925,23 @@
                 [partial_out, ((half, hidden), bf16), ((1, hidden), f32), ((half, width), bf16)],
                 *upstream_chunks[side],
                 mlp_w[l],
-                Far(mlp[side][3]),
+                mlp[side][3],
                 name="mlp_back",
                 scratch=[pltpu.VMEM((2, half, hidden // 2), f32), DMA((2,))],
             )
-        sums = reduce_rows(back[0][0], back[1][0])
         mlp_grad, grad_token = kernel_call(
             functools.partial(mlp_grad_kernel, hidden),
             [((width, 2 * hidden), bf16), TOKEN],
-            Far(mlp[0][1]),
-            Far(mlp[1][1]),
-            Far(mlp[0][2]),
-            Far(mlp[1][2]),
+            mlp[0][1],
+            mlp[1][1],
+            mlp[0][2],
+            mlp[1][2],
             back[0][3],
             back[1][3],
             back[0][1],
             back[1][1],
             name="mlp_grad",
-            after=(sums[0],),
+            after=() if l + 1 == depth else (touch(mlp_parts[l + 1]),),
             scratch=[
                 pltpu.VMEM((all_rows, width), bf16),
                 pltpu.VMEM((all_rows, hidden), bf16),
@@ -914,17 +950,14 @@
                 DMA((4,)),
             ],
             limit=16,
-            us=3,
         )
-        mlp_part = lax.psum_scatter(mlp_grad, "fsdp", scatter_dimension=0, tiled=True)
-        placed_mlp = place_call(
-            functools.partial(place_mlp_kernel, l, hidden),
-            spread_grads(mlp_part),
-            placed_mlp,
-            [w_fc1.shape, w_fc2.shape],
-            [(GROUP, width_own, hidden), (GROUP, hidden, width_own)],
-            "place_mlp",
-        )
+        pairs_now = [(back[0][0], back[1][0])]
+        if l + 1 == depth:
+            pairs_now.append((mlp[0][0], mlp[1][0]))
+        sums, *output_sums = reduce_rows(*pairs_now, after=(grad_token,))
+        if l + 1 == depth:
+            output_term = output_sums[0]
+        mlp_parts[l] = scatter_grads(mlp_grad)
         unit_sums[l] = back[0][2] + back[1][2]
         grad_middle, middle_b, sums_two = kernel_call(
             functools.partial(norm_back_two_kernel, gain_row(l, 1)),
@@ -934,7 +967,6 @@
             upstream,
             vecs,
             name="norm_back_two",
-            after=(grad_token,),
             scratch=[pltpu.VMEM((rows, width), f32), DMA((1,))],
         )
         middle_chunks = gather_rows(middle_b)
@@ -1000,10 +1032,11 @@
                 scratch=[pltpu.VMEM((half, 3 * feats), bf16)],
             )[0]
 
-        def weight_grad(after):
-            return kernel_call(
+        def weight_grad(after=()):
+            count = 1 if l > 0 else fsdp
+            *parts, head_sum, token = kernel_call(
                 functools.partial(attn_grad_kernel, feats),
-                [((width, 4 * feats), bf16), ((2, feats), f32), TOKEN],
+                [((width // count, 4 * feats), bf16)] * count + [((2, feats), f32), TOKEN],
                 Far(attn[0][3]),
                 Far(attn[1][3]),
                 Far(attn[0][1]),
@@ -1021,31 +1054,18 @@
                     pltpu.VMEM((all_rows, 3 * feats), bf16),
                     DMA((4,)),
                 ],
-                us=3,
-            )
-
+            )
+
+            return parts, head_sum, token
+
+        far_part = project(1, ())
+        near_part = project(0, ())
+        attn_grads, head_sums[l], grad_token = weight_grad(
+            () if l + 1 == depth else (touch(attn_parts[l + 1]),)
+        )
+        (sums,) = reduce_rows((near_part, far_part), after=(grad_token,))
         if l > 0:
-            far_part = project(1, ())
-            near_part = project(0, ())
-            sums = reduce_rows(near_part, far_part)
-            attn_grad, head_sums[l], grad_token = weight_grad((sums[0],))
-            one_after = (grad_token,)
-        else:
-            attn_grad, head_sums[l], grad_token = weight_grad(mlp_token)
-            far_part = project(1, (grad_token,))
-            near_part = project(0, ())
-            sums = reduce_rows(near_part, far_part)
-            one_after = ()
-        attn_part = lax.psum_scatter(attn_grad, "fsdp", scatter_dimension=0, tiled=True)
-        placed_attn = place_call(
-            functools.partial(place_attn_kernel, l, feats),
-            spread_grads(attn_part),
-            placed_attn,
-            [w_qkv.shape, w_out.shape],
-            [(GROUP, 3, width_own, feats), (GROUP, feats, width_own)],
-            "place_attn",
-        )
-        mlp_token = (placed_mlp[2],)
+            attn_parts[l] = scatter_grads(attn_grads[0])
         body = functools.partial(norm_back_one_kernel, gain_row(l, 0))
         if l > 0:
             masked = ()
@@ -1061,14 +1081,11 @@
             vecs,
             *masked,
             name="norm_back_one",
-            after=one_after,
             scratch=[pltpu.VMEM((rows, width), f32), DMA((1,))],
         )
         if l > 0:
             upstream_chunks = gather_rows(upstream_b)
         row_sums[l] = (sums_one, sums_two)
-
-    grad_inputs = both_halves(upstream)
 
     vec_part = jnp.concatenate(
         [
@@ -1091,19 +1108,60 @@
     packed = jnp.concatenate([vec_part, unit_lines, head_lines], axis=0)
     if outer > 1:
         packed = lax.psum(packed, "ctx", axis_index_groups=outer_groups)
-    step = 1
-    while step < fsdp:
-        packed = packed + lax.ppermute(packed, "fsdp", [(i, i ^ step) for i in range(fsdp)])
-        step *= 2
+    early = [(l, kind) for l in range(depth) for kind in (0, 1) if (l, kind) != (0, 1)]
+    parts = {key: gate((mlp_parts, attn_parts)[key[1]][key[0]], (sums_one,)) for key in early}
+    outputs_own = kernel_call(
+        functools.partial(sum_out_kernel, shift_row(depth - 1, 3)),
+        [row_f32],
+        *output_term,
+        Far(saved_all[depth - 1][2][1][4]),
+        vecs,
+        mask,
+        name="sum_out",
+        after=(sums_one,),
+        scratch=[pltpu.VMEM((rows, width), f32), DMA((1,))],
+    )[0]
+    last_terms = (attn_grads[0], *[shift_z(attn_grads[d], d) for d in range(1, fsdp)])
+    crossed = {key: swap_x(parts[key]) for key in early}
+    others = (swap_y(upstream), swap_y(outputs_own))
+    packed, hub_token = kernel_call(
+        vector_sum_kernel,
+        [(packed.shape, f32), TOKEN],
+        packed,
+        *[shift_z(packed, d) for d in range(1, fsdp)],
+        name="vector_sum",
+        after=(*crossed.values(), *others, *last_terms[1:]),
+    )
+    grad_inputs, outputs = (
+        kernel_call(
+            place_rows_kernel,
+            [saved(inputs.shape, f32)],
+            own,
+            other,
+            name="place_rows",
+            scratch=[DMA((2,))],
+        )[0]
+        for own, other in zip((upstream, outputs_own), others)
+    )
     vec_sum = lax.dynamic_slice_in_dim(packed[:vec_rows], f * width_own, width_own, axis=1)
+    vec_sum = vec_sum.reshape(-1, width)
+    vec_lines = vec_sum.shape[0]
     rest = packed[vec_rows:]
-    vec_sum = vec_sum + swap_y(vec_sum)
-    rest_core = swap_core(rest)
-    vec_sum = vec_sum + swap_core(vec_sum)
-    rest_two = jnp.stack([rest, rest_core])
-    vec_sum = vec_sum + swap_x(vec_sum)
-    rest_four = jnp.concatenate([rest_two, swap_x(rest_two)], axis=0)
-    vec_sum = vec_sum.reshape(depth, 6, width_own)
+    mine = jnp.concatenate([vec_sum, rest], axis=0)
+    from_x = swap_x(mine)
+    vec_sum = vec_sum + swap_xy(vec_sum) + from_x[:vec_lines] + swap_y(vec_sum)
+    mine = jnp.concatenate([vec_sum, rest, from_x[vec_lines:]], axis=0)
+    from_core = swap_core(mine)
+    vec_sum = (vec_sum + from_core[:vec_lines]).reshape(depth, 6, width_own)
+    count = rest.shape[0]
+    rest_four = jnp.stack(
+        [
+            rest,
+            from_core[vec_lines : vec_lines + count],
+            mine[vec_lines + count :],
+            from_core[vec_lines + count :],
+        ]
+    )
     unit_count = unit_lines.shape[0]
 
     def of_place(c):
@@ -1122,6 +1180,40 @@
         ],
         axis=2,
     ).reshape(qv_bias.shape)
+    placed = [None, None]
+    for l, kind in early + [(0, 1)]:
+        if (l, kind) in parts:
+            part, other = parts[l, kind], crossed[l, kind]
+        else:
+            part = kernel_call(
+                shard_sum_kernel,
+                [((width_own, 4 * feats), bf16)],
+                *last_terms,
+                name="shard_sum",
+                after=(hub_token,),
+            )[0]
+            if outer > 1:
+                part = lax.psum(part, "ctx", axis_index_groups=outer_groups)
+            other = swap_x(part)
+        pieces = (part, swap_core(part), other, swap_core(other))
+        if kind == 0:
+            placed[0] = place_call(
+                functools.partial(place_mlp_kernel, l, hidden),
+                pieces,
+                placed[0],
+                [w_fc1.shape, w_fc2.shape],
+                [(GROUP, width_own, hidden), (GROUP, hidden, width_own)],
+                "place_mlp",
+            )
+        else:
+            placed[1] = place_call(
+                functools.partial(place_attn_kernel, l, feats),
+                pieces,
+                placed[1],
+                [w_qkv.shape, w_out.shape],
+                [(GROUP, 3, width_own, feats), (GROUP, feats, width_own)],
+                "place_attn",
+            )
     return (
         outputs,
         grad_inputs,
@@ -1129,10 +1221,10 @@
         vec_sum[:, 2:],
         grad_qv_bias,
         grad_fc1_bias,
-        placed_attn[0],
-        placed_attn[1],
-        placed_mlp[0],
-        placed_mlp[1],
+        placed[1][0],
+        placed[1][1],
+        placed[0][0],
+        placed[0][1],
     )
 
 

time: 404 us -> 422 us (1.045)
  starting transfers between devices: 136 us -> 114 us
  local copies, waits for them, and re-layouts: 24.5 us -> 42.6 us
  waiting for transfers between devices: 118 us -> 134 us
  Pallas kernels: 103 us -> 108 us
    ppermute x50 -> x49, starting transfers between devices: 75.7 us -> 49.8 us  [swap_core(): return lax.ppermute(value, 'ctx', [(i, i ^ 1) for i in range(ctx)])]
    unnamed x111 -> x165, local copies, waits for them, and re-layouts: 20.6 us -> 37.4 us
    ppermute x19 -> x18, waiting for transfers between devices: 21.1 us -> 8.24 us  [swap_y(): return lax.ppermute(value, 'tp', [(i, i ^ 1) for i in range(tp)])]
    ppermute x22 -> x20, waiting for transfers between devices: 34 us -> 45.6 us  [swap_x(): return lax.ppermute(value, 'ctx', [(i, i ^ 2) for i in range(ctx)])]
    ppermute x3 -> x9, waiting for transfers between devices: 0.01 us -> 11.5 us  [shift_z(): lax.ppermute(value, 'fsdp', [(i, (i + d) % fsdp) for i in range(fsdp)])]
    ppermute x3 -> x9, starting transfers between devices: 3.83 us -> 15 us  [shift_z(): lax.ppermute(value, 'fsdp', [(i, (i + d) % fsdp) for i in range(fsdp)])]
    ppermute x16, waiting for transfers between devices: 33.2 us -> 43.4 us  [swap_xy(): return lax.ppermute(value, ('ctx', 'tp'), pairs)]
    ppermute x16, starting transfers between devices: 21.7 us -> 30.7 us  [swap_xy(): return lax.ppermute(value, ('ctx', 'tp'), pairs)]
  transfers between devices with their start and end apart: 120 -> 119, of which waited for: 44 -> 50; matrix products, arithmetic and copies ran while one was open for 1% -> 1% of each run, Pallas kernels for 22% -> 23%
where the time goes in v5:
time: 422 us; the launch traced here: 416 us
  waiting for transfers between devices  134 us (32%)
  starting transfers between devices  114 us (27%)
  Pallas kernels  108 us (26%)
  local copies, waits for them, and re-layouts  42.6 us (10%)
  between operations  16.2 us (4%)
    pallas_call x63, Pallas kernels, kernel_call(): pl.pallas_call(run, out_shape=out_shape, in_specs=specs, out_specs=out_sp...  108 us
    ppermute x49, starting transfers between devices, swap_core(): return lax.ppermute(value, 'ctx', [(i, i ^ 1) for i in range(ctx)])  49.8 us
    ppermute x20, waiting for transfers between devices, swap_x(): return lax.ppermute(value, 'ctx', [(i, i ^ 2) for i in range(ctx)])  45.6 us
    ppermute x16, waiting for transfers between devices, swap_xy(): return lax.ppermute(value, ('ctx', 'tp'), pairs)  43.4 us
    unnamed x165, local copies, waits for them, and re-layouts  37.4 us
    ppermute x16, starting transfers between devices, swap_xy(): return lax.ppermute(value, ('ctx', 'tp'), pairs)  30.7 us
    all_gather x2, waiting for transfers between devices, per_device(): mlp_w.append(lax.all_gather(own, 'fsdp', axis=0, tiled=True))  17.7 us
    ppermute x9, starting transfers between devices, shift_z(): lax.ppermute(value, 'fsdp', [(i, (i + d) % fsdp) for i in range(fsdp)])  15 us
  transfers between devices with their start and end apart: 119, of which 50 were waited for; matrix products, arithmetic and copies ran while one was open for 1% of the time, Pallas kernels for 23%

profile of v5, /device:TPU:9, one launch (start us, length us, event | category | flops | bytes accessed | tf_op | source)
XLA Modules:
  0.0 415.9 jit_solution(15878524461975402886)
XLA Ops:
  11.5 2.5 collective-permute-start.8
  23.1 2.4 collective-permute-start.3
  31.0 3.0 collective-permute-done.10.refs_1_
  35.2 2.4 collective-permute-done.11.refs_2_
  45.4 3.4 attn.5
  51.8 2.6 attn.4
  57.3 3.9 collective-permute-done.18.refs_1_
  61.2 2.4 collective-permute-done.19.refs_2_
  70.4 2.6 collective-permute-done.21.refs_1_
  78.6 6.5 %all-gather.9.cloned.1.call-done.refs_4_ = bf16[1024,1024]{1,0:T(8,128)(2,1)} async-done(((bf16[256,1024]{1,0:T(8,128)(2,1)}), bf16[1024,1024]{1,0:T(8,128)(2,1)}) %all-gather.9.cloned.1.call-update) | async-done | bytes 2097168 | tf_op jit(solution)/shard_map/all_gather | solution.py:736
  94.0 3.6 collective-permute-done.29.refs_1_
  97.6 3.6 collective-permute-done.30.refs_2_
  119.4 2.6 attn.7
  123.0 2.6 attn.6
  128.5 4.1 collective-permute-done.40.refs_1_
  132.6 3.7 collective-permute-done.41.refs_2_
  149.0 11.2 %all-gather.5.cloned.1.call-done.refs_4_.refs_1_ = bf16[1024,1024]{1,0:T(8,128)(2,1)} async-done(((bf16[256,1024]{1,0:T(8,128)(2,1)}), bf16[1024,1024]{1,0:T(8,128)(2,1)}) %all-gather.5.cloned.1.call-update) | async-done | bytes 2097168 | tf_op jit(solution)/shard_map/all_gather | solution.py:736
  164.2 2.5 mlp_back.4
  167.6 2.7 mlp.7
  171.1 2.4 mlp_back.5
  174.9 2.6 mlp_grad.2
  185.8 7.2 %collective-permute-done.52.refs_1_ = bf16[160,1024]{1,0:T(8,128)(2,1)S(1)} collective-permute-done((bf16[160,1024]{1,0:T(8,128)(2,1)S(1)}, bf16[160,1024]{1,0:T(8,128)(2,1)S(1)}, u32[]{:S(2)}, u32[]{:S(2)}) %collective-permute-start.52) | collective-permute-done | bytes 327712 | tf_op jit(solution)/shard_map/ppermute | solution.py:668
  193.0 7.1 %collective-permute-done.53.refs_2_ = bf16[160,1024]{1,0:T(8,128)(2,1)S(1)} collective-permute-done((bf16[160,1024]{1,0:T(8,128)(2,1)S(1)}, bf16[160,1024]{1,0:T(8,128)(2,1)S(1)}, u32[]{:S(2)}, u32[]{:S(2)}) %collective-permute-start.53) | collective-permute-done | bytes 327712 | tf_op jit(solution)/shard_map/ppermute | solution.py:659
  214.0 3.6 attn_back.4
  217.7 3.6 attn_back.5
  221.3 2.7 attn_grad.2
  231.9 3.7 collective-permute-done.63.refs_1_
  235.6 3.7 collective-permute-done.64.refs_2_
  245.8 2.4 collective-permute-done.66.refs_1_
  262.5 4.6 %mlp_grad.3 = (bf16[1024,1024]{1,0:T(8,128)(2,1)}, f32[8,128]{1,0:T(8,128)S(1)}) custom-call(bf16[320,1024]{1,0:T(8,128)(2,1)} %get-tuple-element.275.refs_0_, bf16[320,1024]{1,0:T(8,128)(2,1)} %get-tuple-element.276.refs_1_, bf16[320,512]{1,0:T(8,128)(2,1)} %get-tuple-element.277.refs_2_, bf16[320,512]{1,0:T(8,128)(2,1)} %get-tuple-element.278.refs_3_, ...), custom_call_target="tpu_custom_call" | custom-call | tf_op jit(solution)/shard_map/mlp_grad/pallas_call | solution.py:79
  273.2 3.7 collective-permute-done.74.refs_1_
  276.9 3.7 collective-permute-done.75.refs_2_
  287.2 2.4 collective-permute-done.77.refs_1_
  294.3 3.6 attn_back.6
  298.8 3.6 attn_back.7
  309.9 3.7 attn_grad.3
  318.7 2.6 collective-permute-start.97
  332.4 8.8 %collective-permute-done.97.refs_10_.refs_2_ = bf16[256,512]{1,0:T(8,128)(2,1)} collective-permute-done((bf16[256,512]{1,0:T(8,128)(2,1)}, bf16[256,512]{1,0:T(8,128)(2,1)}, u32[]{:S(2)}, u32[]{:S(2)}) %collective-permute-start.97) | collective-permute-done | bytes 262176 | tf_op jit(solution)/shard_map/ppermute | solution.py:671
  341.2 3.1 collective-permute-start.91
  349.4 2.7 collective-permute-done.92.refs_3_
  353.9 4.5 %collective-permute-done.95.refs_6_.refs_2_ = bf16[256,512]{1,0:T(8,128)(2,1)S(1)} collective-permute-done((bf16[256,512]{1,0:T(8,128)(2,1)}, bf16[256,512]{1,0:T(8,128)(2,1)S(1)}, u32[]{:S(2)}, u32[]{:S(2)}) %collective-permute-start.95) | collective-permute-done | bytes 262176 | tf_op jit(solution)/shard_map/ppermute | solution.py:659
  368.5 4.7 %collective-permute-start.106 = (bf16[256,512]{1,0:T(8,128)(2,1)}, bf16[256,512]{1,0:T(8,128)(2,1)}, u32[]{:S(2)}, u32[]{:S(2)}) collective-permute-start(bf16[256,512]{1,0:T(8,128)(2,1)} %gate.5.refs_0_), channel_id=1, source_target_pairs={{0,2},{2,0},{4,6},{6,4},{1,3},{3,1},{5,7},{7,5},{8,10},{10,8},{12,... | collective-permute-start | bytes 786440 | tf_op jit(solution)/shard_map/ppermute | solution.py:656
  373.3 3.5 collective-permute-start.102
  380.1 3.1 place_attn.2
  386.3 5.7 %collective-permute-done.104.refs_2_ = bf16[256,512]{1,0:T(8,128)(2,1)S(1)} collective-permute-done((bf16[256,512]{1,0:T(8,128)(2,1)S(1)}, bf16[256,512]{1,0:T(8,128)(2,1)S(1)}, u32[]{:S(2)}, u32[]{:S(2)}) %collective-permute-start.104) | collective-permute-done | bytes 262176 | tf_op jit(solution)/shard_map/ppermute | solution.py:659
  397.7 3.8 place_mlp.2
  401.5 4.0 place_mlp.3
  405.5 3.1 place_attn.3
  (492 shorter events, 217.7 us)
Async XLA Ops:
  7.2 33.5 %all-gather.7.cloned.1.call-start = ((), (), s32[]{:S(2)}) async-start(), calls=%async_computation.4 | async-start | bytes 1310720 | tf_op jit(solution)/shard_map/all_gather | solution.py:734
  9.0 76.0 %all-gather.9.cloned.1.call-start = ((), (), s32[]{:S(2)}) async-start(), calls=%async_computation.5 | async-start | bytes 2621440 | tf_op jit(solution)/shard_map/all_gather | solution.py:736
  11.2 103.8 %all-gather.11.cloned.1.call-start = ((), (), s32[]{:S(2)}) async-start(), calls=%async_computation.6 | async-start | bytes 1310720 | tf_op jit(solution)/shard_map/all_gather | solution.py:734
  11.4 11.4 %collective-permute-start.7 = (bf16[17,256]{1,0:T(8,128)(2,1)S(1)}, bf16[17,256]{1,0:T(8,128)(2,1)S(1)}, u32[]{:S(2)}, u32[]{:S(2)}) collective-permute-start(bf16[17,256]{1,0:T(8,128)(2,1)S(1)} %fusion.2), channel_id=1, source_target_pairs={{0,24},{8,0},{16,8},{24,16},{1,25},{9,1},{17,9},{25,17},{2,26},{10... | collective-permute-start | bytes 26120 | tf_op jit(solution)/shard_map/ppermute | solution.py:671
  11.5 11.6 %collective-permute-start.8 = (bf16[17,256]{1,0:T(8,128)(2,1)S(1)}, bf16[17,256]{1,0:T(8,128)(2,1)S(1)}, u32[]{:S(2)}, u32[]{:S(2)}) collective-permute-start(bf16[17,256]{1,0:T(8,128)(2,1)S(1)} %fusion.2), channel_id=1, source_target_pairs={{0,16},{8,24},{16,0},{24,8},{1,17},{9,25},{17,1},{25,9},{2,18},{10... | collective-permute-start | bytes 26120 | tf_op jit(solution)/shard_map/ppermute | solution.py:671
  13.9 11.5 %collective-permute-start.9 = (bf16[17,256]{1,0:T(8,128)(2,1)S(1)}, bf16[17,256]{1,0:T(8,128)(2,1)S(1)}, u32[]{:S(2)}, u32[]{:S(2)}) collective-permute-start(bf16[17,256]{1,0:T(8,128)(2,1)S(1)} %fusion.2), channel_id=1, source_target_pairs={{0,8},{8,16},{16,24},{24,0},{1,9},{9,17},{17,25},{25,1},{2,10},{10... | collective-permute-start | bytes 26120 | tf_op jit(solution)/shard_map/ppermute | solution.py:671
  18.4 10.9 %collective-permute-start = (bf16[80,1024]{1,0:T(8,128)(2,1)S(1)}, bf16[80,1024]{1,0:T(8,128)(2,1)S(1)}, u32[]{:S(2)}, u32[]{:S(2)}) collective-permute-start(bf16[80,1024]{1,0:T(8,128)(2,1)S(1)} %get-tuple-element.177.refs_0_), channel_id=1, source_target_pairs={{0,5},{1,4},{2,7},{3,6},{4,1},{5,0},{6,3},{7,2},{8,13},{9,12},{10,... | collective-permute-start | bytes 491528 | tf_op jit(solution)/shard_map/ppermute | solution.py:668
  20.6 9.0 %collective-permute-start.1 = (bf16[80,1024]{1,0:T(8,128)(2,1)S(1)}, bf16[80,1024]{1,0:T(8,128)(2,1)S(1)}, u32[]{:S(2)}, u32[]{:S(2)}) collective-permute-start(bf16[80,1024]{1,0:T(8,128)(2,1)S(1)} %get-tuple-element.177.refs_0_), channel_id=1, source_target_pairs={{0,4},{2,6},{4,0},{6,2},{1,5},{3,7},{5,1},{7,3},{8,12},{10,14},{12... | collective-permute-start | bytes 491528 | tf_op jit(solution)/shard_map/ppermute | solution.py:659
  22.6 137.6 %all-gather.5.cloned.1.call-start = ((), (), s32[]{:S(2)}) async-start(), calls=%async_computation.3 | async-start | bytes 2621440 | tf_op jit(solution)/shard_map/all_gather | solution.py:736
  29.6 8.8 %collective-permute-start.12 = (bf16[80,1024]{1,0:T(8,128)(2,1)S(1)}, bf16[80,1024]{1,0:T(8,128)(2,1)}, u32[]{:S(2)}, u32[]{:S(2)}) collective-permute-start(bf16[80,1024]{1,0:T(8,128)(2,1)S(1)} %get-tuple-element.181.refs_0_), channel_id=1, source_target_pairs={{0,1},{1,0},{2,3},{3,2},{4,5},{5,4},{6,7},{7,6},{8,9},{9,8},{10,11... | collective-permute-start | bytes 491528 | tf_op jit(solution)/shard_map/ppermute | solution.py:662
  34.0 9.6 %collective-permute-start.13 = (bf16[80,1024]{1,0:T(8,128)(2,1)S(1)}, bf16[80,1024]{1,0:T(8,128)(2,1)}, u32[]{:S(2)}, u32[]{:S(2)}) collective-permute-start(bf16[80,1024]{1,0:T(8,128)(2,1)S(1)} %get-tuple-element.181.refs_0_), channel_id=1, source_target_pairs={{0,2},{2,0},{4,6},{6,4},{1,3},{3,1},{5,7},{7,5},{8,10},{10,8},{12,... | collective-permute-start | bytes 491528 | tf_op jit(solution)/shard_map/ppermute | solution.py:656
  51.3 208.1 %reduce-scatter.4.cloned.1.call-start = ((), (), s32[]{:S(2)}) async-start(), calls=%async_computation.7 | async-start | bytes 2621440 | tf_op jit(solution)/shard_map/reduce_scatter | solution.py:909
  56.1 9.1 %collective-permute-start.20 = (bf16[80,1024]{1,0:T(8,128)(2,1)S(1)}, bf16[80,1024]{1,0:T(8,128)(2,1)S(1)}, u32[]{:S(2)}, u32[]{:S(2)}) collective-permute-start(bf16[80,1024]{1,0:T(8,128)(2,1)S(1)} %get-tuple-element.195), channel_id=1, source_target_pairs={{0,1},{1,0},{2,3},{3,2},{4,5},{5,4},{6,7},{7,6},{8,9},{9,8},{10,11... | collective-permute-start | bytes 491528 | tf_op jit(solution)/shard_map/ppermute | solution.py:662
  68.0 9.0 %collective-permute-start.23 = (bf16[80,1024]{1,0:T(8,128)(2,1)S(1)}, bf16[80,1024]{1,0:T(8,128)(2,1)S(1)}, u32[]{:S(2)}, u32[]{:S(2)}) collective-permute-start(bf16[80,1024]{1,0:T(8,128)(2,1)S(1)} %get-tuple-element.197.refs_0_), channel_id=1, source_target_pairs={{0,1},{1,0},{2,3},{3,2},{4,5},{5,4},{6,7},{7,6},{8,9},{9,8},{10,11... | collective-permute-start | bytes 491528 | tf_op jit(solution)/shard_map/ppermute | solution.py:662
  105.7 8.8 %collective-permute-start.34 = (bf16[80,1024]{1,0:T(8,128)(2,1)S(1)}, bf16[80,1024]{1,0:T(8,128)(2,1)}, u32[]{:S(2)}, u32[]{:S(2)}) collective-permute-start(bf16[80,1024]{1,0:T(8,128)(2,1)S(1)} %get-tuple-element.207.refs_0_), channel_id=1, source_target_pairs={{0,1},{1,0},{2,3},{3,2},{4,5},{5,4},{6,7},{7,6},{8,9},{9,8},{10,11... | collective-permute-start | bytes 491528 | tf_op jit(solution)/shard_map/ppermute | solution.py:662
  105.9 11.9 %collective-permute-start.35 = (bf16[80,1024]{1,0:T(8,128)(2,1)S(1)}, bf16[80,1024]{1,0:T(8,128)(2,1)S(1)}, u32[]{:S(2)}, u32[]{:S(2)}) collective-permute-start(bf16[80,1024]{1,0:T(8,128)(2,1)S(1)} %get-tuple-element.207.refs_0_), channel_id=1, source_target_pairs={{0,2},{2,0},{4,6},{6,4},{1,3},{3,1},{5,7},{7,5},{8,10},{10,8},{12,... | collective-permute-start | bytes 491528 | tf_op jit(solution)/shard_map/ppermute | solution.py:656
  140.2 8.8 %collective-permute-start.45 = (bf16[80,1024]{1,0:T(8,128)(2,1)S(1)}, bf16[80,1024]{1,0:T(8,128)(2,1)}, u32[]{:S(2)}, u32[]{:S(2)}) collective-permute-start(bf16[80,1024]{1,0:T(8,128)(2,1)S(1)} %get-tuple-element.221.refs_0_), channel_id=1, source_target_pairs={{0,1},{1,0},{2,3},{3,2},{4,5},{5,4},{6,7},{7,6},{8,9},{9,8},{10,11... | collective-permute-start | bytes 491528 | tf_op jit(solution)/shard_map/ppermute | solution.py:662
  140.4 27.1 %collective-permute-start.46 = (bf16[80,1024]{1,0:T(8,128)(2,1)S(1)}, bf16[80,1024]{1,0:T(8,128)(2,1)}, u32[]{:S(2)}, u32[]{:S(2)}) collective-permute-start(bf16[80,1024]{1,0:T(8,128)(2,1)S(1)} %get-tuple-element.221.refs_0_), channel_id=1, source_target_pairs={{0,2},{2,0},{4,6},{6,4},{1,3},{3,1},{5,7},{7,5},{8,10},{10,8},{12,... | collective-permute-start | bytes 491528 | tf_op jit(solution)/shard_map/ppermute | solution.py:656
  144.0 23.5 %collective-permute-start.47 = (bf16[80,1024]{1,0:T(8,128)(2,1)S(1)}, bf16[80,1024]{1,0:T(8,128)(2,1)}, u32[]{:S(2)}, u32[]{:S(2)}) collective-permute-start(bf16[80,1024]{1,0:T(8,128)(2,1)S(1)} %collective-permute-done.43.refs_1_), channel_id=1, source_target_pairs={{0,2},{2,0},{4,6},{6,4},{1,3},{3,1},{5,7},{7,5},{8,10},{10,8},{12,... | collective-permute-start | bytes 491528 | tf_op jit(solution)/shard_map/ppermute | solution.py:656
  147.7 19.8 %collective-permute-start.48 = (bf16[80,1024]{1,0:T(8,128)(2,1)}, bf16[80,1024]{1,0:T(8,128)(2,1)}, u32[]{:S(2)}, u32[]{:S(2)}) collective-permute-start(bf16[80,1024]{1,0:T(8,128)(2,1)} %collective-permute-done.44.refs_2_), channel_id=1, source_target_pairs={{0,2},{2,0},{4,6},{6,4},{1,3},{3,1},{5,7},{7,5},{8,10},{10,8},{12,... | collective-permute-start | bytes 491528 | tf_op jit(solution)/shard_map/ppermute | solution.py:656
  149.0 18.6 %collective-permute-start.49 = (bf16[80,1024]{1,0:T(8,128)(2,1)}, bf16[80,1024]{1,0:T(8,128)(2,1)}, u32[]{:S(2)}, u32[]{:S(2)}) collective-permute-start(bf16[80,1024]{1,0:T(8,128)(2,1)} %collective-permute-done.45.refs_3_), channel_id=1, source_target_pairs={{0,2},{2,0},{4,6},{6,4},{1,3},{3,1},{5,7},{7,5},{8,10},{10,8},{12,... | collective-permute-start | bytes 491528 | tf_op jit(solution)/shard_map/ppermute | solution.py:656
  178.8 128.0 %reduce-scatter.6.cloned.1.call-start = ((), (), s32[]{:S(2)}) async-start(), calls=%async_computation.8 | async-start | bytes 1310720 | tf_op jit(solution)/shard_map/reduce_scatter | solution.py:909
  183.1 9.9 %collective-permute-start.52 = (bf16[160,1024]{1,0:T(8,128)(2,1)S(1)}, bf16[160,1024]{1,0:T(8,128)(2,1)S(1)}, u32[]{:S(2)}, u32[]{:S(2)}) collective-permute-start(bf16[160,1024]{1,0:T(8,128)(2,1)S(1)} %get-tuple-element.240), channel_id=1, source_target_pairs={{0,5},{1,4},{2,7},{3,6},{4,1},{5,0},{6,3},{7,2},{8,13},{9,12},{10,... | collective-permute-start | bytes 983048 | tf_op jit(solution)/shard_map/ppermute | solution.py:668
  185.2 14.9 %collective-permute-start.53 = (bf16[160,1024]{1,0:T(8,128)(2,1)S(1)}, bf16[160,1024]{1,0:T(8,128)(2,1)S(1)}, u32[]{:S(2)}, u32[]{:S(2)}) collective-permute-start(bf16[160,1024]{1,0:T(8,128)(2,1)S(1)} %get-tuple-element.241), channel_id=1, source_target_pairs={{0,4},{2,6},{4,0},{6,2},{1,5},{3,7},{5,1},{7,3},{8,12},{10,14},{12... | collective-permute-start | bytes 983048 | tf_op jit(solution)/shard_map/ppermute | solution.py:659
  185.5 15.3 %collective-permute-start.54 = (bf16[160,1024]{1,0:T(8,128)(2,1)S(1)}, bf16[160,1024]{1,0:T(8,128)(2,1)S(1)}, u32[]{:S(2)}, u32[]{:S(2)}) collective-permute-start(bf16[160,1024]{1,0:T(8,128)(2,1)S(1)} %get-tuple-element.242), channel_id=1, source_target_pairs={{0,1},{1,0},{2,3},{3,2},{4,5},{5,4},{6,7},{7,6},{8,9},{9,8},{10,11... | collective-permute-start | bytes 983048 | tf_op jit(solution)/shard_map/ppermute | solution.py:662
  205.5 12.1 %collective-permute-start.58 = (bf16[80,1024]{1,0:T(8,128)(2,1)S(1)}, bf16[80,1024]{1,0:T(8,128)(2,1)S(1)}, u32[]{:S(2)}, u32[]{:S(2)}) collective-permute-start(bf16[80,1024]{1,0:T(8,128)(2,1)S(1)} %get-tuple-element.247.refs_0_), channel_id=1, source_target_pairs={{0,2},{2,0},{4,6},{6,4},{1,3},{3,1},{5,7},{7,5},{8,10},{10,8},{12,... | collective-permute-start | bytes 491528 | tf_op jit(solution)/shard_map/ppermute | solution.py:656
  225.0 103.4 %reduce-scatter.8.cloned.1.call-start = ((), (), s32[]{:S(2)}) async-start(), calls=%async_computation.9 | async-start | bytes 2621440 | tf_op jit(solution)/shard_map/reduce_scatter | solution.py:909
  244.1 8.7 %collective-permute-start.68 = (bf16[80,1024]{1,0:T(8,128)(2,1)S(1)}, bf16[80,1024]{1,0:T(8,128)(2,1)S(1)}, u32[]{:S(2)}, u32[]{:S(2)}) collective-permute-start(bf16[80,1024]{1,0:T(8,128)(2,1)S(1)} %get-tuple-element.270.refs_0_), channel_id=1, source_target_pairs={{0,1},{1,0},{2,3},{3,2},{4,5},{5,4},{6,7},{7,6},{8,9},{9,8},{10,11... | collective-permute-start | bytes 491528 | tf_op jit(solution)/shard_map/ppermute | solution.py:662
  244.6 10.4 %collective-permute-start.69 = (bf16[80,1024]{1,0:T(8,128)(2,1)S(1)}, bf16[80,1024]{1,0:T(8,128)(2,1)S(1)}, u32[]{:S(2)}, u32[]{:S(2)}) collective-permute-start(bf16[80,1024]{1,0:T(8,128)(2,1)S(1)} %get-tuple-element.270.refs_0_), channel_id=1, source_target_pairs={{0,2},{2,0},{4,6},{6,4},{1,3},{3,1},{5,7},{7,5},{8,10},{10,8},{12,... | collective-permute-start | bytes 491528 | tf_op jit(solution)/shard_map/ppermute | solution.py:656
  285.5 8.7 %collective-permute-start.79 = (bf16[80,1024]{1,0:T(8,128)(2,1)S(1)}, bf16[80,1024]{1,0:T(8,128)(2,1)S(1)}, u32[]{:S(2)}, u32[]{:S(2)}) collective-permute-start(bf16[80,1024]{1,0:T(8,128)(2,1)S(1)} %get-tuple-element.290.refs_0_), channel_id=1, source_target_pairs={{0,1},{1,0},{2,3},{3,2},{4,5},{5,4},{6,7},{7,6},{8,9},{9,8},{10,11... | collective-permute-start | bytes 491528 | tf_op jit(solution)/shard_map/ppermute | solution.py:662
  285.9 12.9 %collective-permute-start.80 = (bf16[80,1024]{1,0:T(8,128)(2,1)S(1)}, bf16[80,1024]{1,0:T(8,128)(2,1)S(1)}, u32[]{:S(2)}, u32[]{:S(2)}) collective-permute-start(bf16[80,1024]{1,0:T(8,128)(2,1)S(1)} %get-tuple-element.290.refs_0_), channel_id=1, source_target_pairs={{0,2},{2,0},{4,6},{6,4},{1,3},{3,1},{5,7},{7,5},{8,10},{10,8},{12,... | collective-permute-start | bytes 491528 | tf_op jit(solution)/shard_map/ppermute | solution.py:656
  289.6 9.2 %collective-permute-start.81 = (bf16[80,1024]{1,0:T(8,128)(2,1)S(1)}, bf16[80,1024]{1,0:T(8,128)(2,1)S(1)}, u32[]{:S(2)}, u32[]{:S(2)}) collective-permute-start(bf16[80,1024]{1,0:T(8,128)(2,1)S(1)} %collective-permute-done.77.refs_1_), channel_id=1, source_target_pairs={{0,2},{2,0},{4,6},{6,4},{1,3},{3,1},{5,7},{7,5},{8,10},{10,8},{12,... | collective-permute-start | bytes 491528 | tf_op jit(solution)/shard_map/ppermute | solution.py:656
  304.6 9.6 %collective-permute-start.84 = (bf16[320,1024]{1,0:T(8,128)(2,1)}, bf16[320,1024]{1,0:T(8,128)(2,1)S(1)}, u32[]{:S(2)}, u32[]{:S(2)}) collective-permute-start(bf16[320,1024]{1,0:T(8,128)(2,1)} %project.7), channel_id=1, source_target_pairs={{0,2},{2,0},{4,6},{6,4},{1,3},{3,1},{5,7},{7,5},{8,10},{10,8},{12,... | collective-permute-start | bytes 1966088 | tf_op jit(solution)/shard_map/ppermute | solution.py:656
  317.2 13.1 %collective-permute-start.96 = (bf16[256,512]{1,0:T(8,128)(2,1)}, bf16[256,512]{1,0:T(8,128)(2,1)S(1)}, u32[]{:S(2)}, u32[]{:S(2)}) collective-permute-start(bf16[256,512]{1,0:T(8,128)(2,1)} %get-tuple-element.326), channel_id=1, source_target_pairs={{0,8},{8,16},{16,24},{24,0},{1,9},{9,17},{17,25},{25,1},{2,10},{10... | collective-permute-start | bytes 786440 | tf_op jit(solution)/shard_map/ppermute | solution.py:671
  318.7 22.5 %collective-permute-start.97 = (bf16[256,512]{1,0:T(8,128)(2,1)}, bf16[256,512]{1,0:T(8,128)(2,1)}, u32[]{:S(2)}, u32[]{:S(2)}) collective-permute-start(bf16[256,512]{1,0:T(8,128)(2,1)} %get-tuple-element.327), channel_id=1, source_target_pairs={{0,16},{8,24},{16,0},{24,8},{1,17},{9,25},{17,1},{25,9},{2,18},{10... | collective-permute-start | bytes 786440 | tf_op jit(solution)/shard_map/ppermute | solution.py:671
  321.3 25.8 %collective-permute-start.98 = (bf16[256,512]{1,0:T(8,128)(2,1)}, bf16[256,512]{1,0:T(8,128)(2,1)}, u32[]{:S(2)}, u32[]{:S(2)}) collective-permute-start(bf16[256,512]{1,0:T(8,128)(2,1)} %get-tuple-element.328), channel_id=1, source_target_pairs={{0,24},{8,0},{16,8},{24,16},{1,25},{9,1},{17,9},{25,17},{2,26},{10... | collective-permute-start | bytes 786440 | tf_op jit(solution)/shard_map/ppermute | solution.py:671
  327.1 33.4 %collective-permute-start.94 = (bf16[256,1024]{1,0:T(8,128)(2,1)S(1)}, bf16[256,1024]{1,0:T(8,128)(2,1)S(1)}, u32[]{:S(2)}, u32[]{:S(2)}) collective-permute-start(bf16[256,1024]{1,0:T(8,128)(2,1)S(1)} %gate.4.refs_0_), channel_id=1, source_target_pairs={{0,4},{2,6},{4,0},{6,2},{1,5},{3,7},{5,1},{7,3},{8,12},{10,14},{12... | collective-permute-start | bytes 1572872 | tf_op jit(solution)/shard_map/ppermute | solution.py:659
  329.5 31.0 %collective-permute-start.93 = (bf16[256,1024]{1,0:T(8,128)(2,1)S(1)}, bf16[256,1024]{1,0:T(8,128)(2,1)S(1)}, u32[]{:S(2)}, u32[]{:S(2)}) collective-permute-start(bf16[256,1024]{1,0:T(8,128)(2,1)S(1)} %gate.3.refs_0_), channel_id=1, source_target_pairs={{0,4},{2,6},{4,0},{6,2},{1,5},{3,7},{5,1},{7,3},{8,12},{10,14},{12... | collective-permute-start | bytes 1572872 | tf_op jit(solution)/shard_map/ppermute | solution.py:659
  331.0 16.7 %collective-permute-start.90 = (f32[14,1024]{1,0:T(8,128)S(1)}, f32[14,1024]{1,0:T(8,128)S(1)}, u32[]{:S(2)}, u32[]{:S(2)}) collective-permute-start(f32[14,1024]{1,0:T(8,128)S(1)} %concatenate.25.refs_0_), channel_id=1, source_target_pairs={{0,8},{8,16},{16,24},{24,0},{1,9},{9,17},{17,25},{25,1},{2,10},{10... | collective-permute-start | bytes 172040 | tf_op jit(solution)/shard_map/ppermute | solution.py:671
  347.1 11.3 %collective-permute-start.88 = (f32[80,1024]{1,0:T(8,128)S(1)}, f32[80,1024]{1,0:T(8,128)S(1)}, u32[]{:S(2)}, u32[]{:S(2)}) collective-permute-start(f32[80,1024]{1,0:T(8,128)S(1)} %sum_out.1.refs_0_), channel_id=1, source_target_pairs={{0,1},{1,0},{2,3},{3,2},{4,5},{5,4},{6,7},{7,6},{8,9},{9,8},{10,11... | collective-permute-start | bytes 983048 | tf_op jit(solution)/shard_map/ppermute | solution.py:662
  347.7 12.8 %collective-permute-start.89 = (f32[80,1024]{1,0:T(8,128)}, f32[80,1024]{1,0:T(8,128)S(1)}, u32[]{:S(2)}, u32[]{:S(2)}) collective-permute-start(f32[80,1024]{1,0:T(8,128)} %copy-done.45), channel_id=1, source_target_pairs={{0,1},{1,0},{2,3},{3,2},{4,5},{5,4},{6,7},{7,6},{8,9},{9,8},{10,11... | collective-permute-start | bytes 983048 | tf_op jit(solution)/shard_map/ppermute | solution.py:662
  368.5 11.5 %collective-permute-start.106 = (bf16[256,512]{1,0:T(8,128)(2,1)}, bf16[256,512]{1,0:T(8,128)(2,1)}, u32[]{:S(2)}, u32[]{:S(2)}) collective-permute-start(bf16[256,512]{1,0:T(8,128)(2,1)} %gate.5.refs_0_), channel_id=1, source_target_pairs={{0,2},{2,0},{4,6},{6,4},{1,3},{3,1},{5,7},{7,5},{8,10},{10,8},{12,... | collective-permute-start | bytes 786440 | tf_op jit(solution)/shard_map/ppermute | solution.py:656
  373.3 11.6 %collective-permute-start.102 = (f32[7,1024]{1,0:T(8,128)S(1)}, f32[7,1024]{1,0:T(8,128)S(1)}, u32[]{:S(2)}, u32[]{:S(2)}) collective-permute-start(f32[7,1024]{1,0:T(8,128)S(1)} %pad_maximum_fusion.2), channel_id=1, source_target_pairs={{0,2},{2,0},{4,6},{6,4},{1,3},{3,1},{5,7},{7,5},{8,10},{10,8},{12,... | collective-permute-start | bytes 86024 | tf_op jit(solution)/shard_map/ppermute | solution.py:656
  376.8 24.7 %collective-permute-start.108 = (bf16[256,1024]{1,0:T(8,128)(2,1)S(1)}, bf16[256,1024]{1,0:T(8,128)(2,1)}, u32[]{:S(2)}, u32[]{:S(2)}) collective-permute-start(bf16[256,1024]{1,0:T(8,128)(2,1)S(1)} %gate.4.refs_0_), channel_id=1, source_target_pairs={{0,2},{2,0},{4,6},{6,4},{1,3},{3,1},{5,7},{7,5},{8,10},{10,8},{12,... | collective-permute-start | bytes 1572872 | tf_op jit(solution)/shard_map/ppermute | solution.py:656
  379.6 21.9 %collective-permute-start.109 = (bf16[256,1024]{1,0:T(8,128)(2,1)S(1)}, bf16[256,1024]{1,0:T(8,128)(2,1)}, u32[]{:S(2)}, u32[]{:S(2)}) collective-permute-start(bf16[256,1024]{1,0:T(8,128)(2,1)S(1)} %collective-permute-done.94.refs_5_.refs_2_), channel_id=1, source_target_pairs={{0,2},{2,0},{4,6},{6,4},{1,3},{3,1},{5,7},{7,5},{8,10},{10,8},{12,... | collective-permute-start | bytes 1572872 | tf_op jit(solution)/shard_map/ppermute | solution.py:656
  384.9 11.0 %collective-permute-start.111 = (bf16[256,1024]{1,0:T(8,128)(2,1)S(1)}, bf16[256,1024]{1,0:T(8,128)(2,1)S(1)}, u32[]{:S(2)}, u32[]{:S(2)}) collective-permute-start(bf16[256,1024]{1,0:T(8,128)(2,1)S(1)} %collective-permute-done.93.refs_4_.refs_2_), channel_id=1, source_target_pairs={{0,2},{2,0},{4,6},{6,4},{1,3},{3,1},{5,7},{7,5},{8,10},{10,8},{12,... | collective-permute-start | bytes 1572872 | tf_op jit(solution)/shard_map/ppermute | solution.py:656
  386.3 19.2 %collective-permute-start.103 = (bf16[256,512]{1,0:T(8,128)(2,1)S(1)}, bf16[256,512]{1,0:T(8,128)(2,1)}, u32[]{:S(2)}, u32[]{:S(2)}) collective-permute-start(bf16[256,512]{1,0:T(8,128)(2,1)S(1)} %shard_sum.1.refs_0_), channel_id=1, source_target_pairs={{0,2},{2,0},{4,6},{6,4},{1,3},{3,1},{5,7},{7,5},{8,10},{10,8},{12,... | collective-permute-start | bytes 786440 | tf_op jit(solution)/shard_map/ppermute | solution.py:656
  392.1 13.4 %collective-permute-start.105 = (bf16[256,512]{1,0:T(8,128)(2,1)S(1)}, bf16[256,512]{1,0:T(8,128)(2,1)}, u32[]{:S(2)}, u32[]{:S(2)}) collective-permute-start(bf16[256,512]{1,0:T(8,128)(2,1)S(1)} %collective-permute-done.104.refs_2_), channel_id=1, source_target_pairs={{0,2},{2,0},{4,6},{6,4},{1,3},{3,1},{5,7},{7,5},{8,10},{10,8},{12,... | collective-permute-start | bytes 786440 | tf_op jit(solution)/shard_map/ppermute | solution.py:656
  (150 other events, 1128.4 us)
Sparse Core Ops, SparseCore 0:
  10.2 28.8 all-gather.6
  41.2 43.8 all-gather.8
  86.6 28.2 all-gather.10
  116.3 43.8 all-gather.4
  178.9 42.0 reduce-scatter.3
  225.1 25.5 reduce-scatter.5
  267.3 41.0 reduce-scatter.7

commit v6 on v5

--- a/solution.py
+++ b/solution.py
@@ -166,13 +166,16 @@
 
 
 def prep_upstream_kernel(tp, outer, lengths, cotangent_hbm,
-                         upstream_ref, upstream_b_ref, usable_ref, mask_ref, rows_in, sems):
+                         upstream_hbm, upstream_b_ref, usable_ref, mask_ref,
+                         rows_in, upstream_ref, sems):
     rows = rows_in.shape[0]
     c = lax.axis_index("ctx")
     t = lax.axis_index("tp")
     place = lax.rem(c, GROUP) * tp + t
     start = pl.multiple_of(t * rows, rows)
-    copies = start_copies([(cotangent_hbm.at[0, pl.ds(start, rows), :], rows_in)], sems)
+    copies = start_copies(
+        [(cotangent_hbm.at[0, pl.ds(start, rows), :], rows_in)], sems.at[pl.ds(0, 1)]
+    )
     lane = lax.broadcasted_iota(jnp.int32, usable_ref.shape, 1)
     limit = jnp.zeros(usable_ref.shape, jnp.int32)
     for o in range(outer):
@@ -188,7 +191,9 @@
     copies[0].wait()
     upstream = rows_in[...] * mask[:, 0:1]
     upstream_ref[...] = upstream
+    sent = start_copies([(upstream_ref, upstream_hbm)], sems.at[pl.ds(1, 1)])
     upstream_b_ref[...] = upstream.astype(bf16)
+    sent[0].wait()
 
 
 def prep_first_kernel(depth, inputs_hbm, vecs, stream_ref, first_ref, sems):
@@ -273,23 +278,6 @@
         copy.wait()
 
 
-def touch_kernel(source, token):
-    token[...] = jnp.zeros_like(token)
-
-
-def vector_sum_kernel(*refs):
-    *terms, out_ref, token = refs
-    total = terms[0][...]
-    for term in terms[1:]:
-        total = total + term[...]
-    out_ref[...] = total
-    token[...] = jnp.zeros_like(token)
-
-
-def copy_kernel(source, target):
-    target[...] = source[...]
-
-
 def core_sum_kernel(count, *refs):
     pairs, owns = refs[: 2 * count], refs[2 * count : 3 * count]
     peers = refs[3 * count :]
@@ -325,11 +313,15 @@
     normed_ref[...] = (normed * gain + vecs[shift_row : shift_row + 1, :]).astype(bf16)
 
 
-def sum_out_kernel(bias_row, own, xy, x, y, residual_hbm, vecs, mask, out_ref, residual, sems):
-    copies = start_copies([(residual_hbm, residual)], sems)
+def sum_out_kernel(bias_row, own, xy, x, y, residual_hbm, vecs, mask, out_hbm, token,
+                   residual, out_ref, sems):
+    copies = start_copies([(residual_hbm, residual)], sems.at[pl.ds(0, 1)])
     total = total_of(own, xy, x, y, 1) + vecs[bias_row : bias_row + 1, :]
     copies[0].wait()
     out_ref[...] = (residual[...] + total) * mask[:, 0:1]
+    token[...] = jnp.zeros_like(token)
+    for copy in start_copies([(out_ref, out_hbm)], sems.at[pl.ds(1, 1)]):
+        copy.wait()
 
 
 def mlp_kernel(hidden, keep_count, saves, c0, c1, c2, c3, w, bias, *refs):
@@ -366,7 +358,7 @@
 
 def mlp_back_kernel(hidden, chunk_count, *refs):
     chunks, (w, slope_hbm, *rest) = refs[:chunk_count], refs[chunk_count:]
-    partial_ref, grad_ref, sum_ref, x, slope, sems = rest
+    partial_ref, grad_ref, sum_hbm, x, slope, sum_ref, sems = rest
     copies = start_copies([(slope_hbm, slope)], sems)
     if chunk_count == 1:
         copies += start_copies([(chunks[0], x)], sems.at[pl.ds(1, 1)])
@@ -381,31 +373,43 @@
         part = grad[:, span] * slope[k]
         grad_ref[:, span] = part.astype(bf16)
         sum_ref[:, span] = jnp.sum(part, axis=0, keepdims=True)
+    sent = start_copies([(sum_ref, sum_hbm)], sems.at[pl.ds(2, 1)])
     partial_ref[...] = dot_nt(grad_ref[...], w[:, :hidden]).astype(bf16)
+    sent[0].wait()
 
 
 def mlp_grad_kernel(hidden, second_near, second_far, act_near, act_far, up_near, up_far,
-                    grad_near, grad_far, out_ref, token, second, act, up, grad, sems):
+                    grad_near, grad_far, passed, sums, middle, out_hbm, passed_ref, sums_hbm,
+                    middle_hbm, second, act, up, grad, out_one, out_two, sems):
     rows = up_near.shape[0]
+    sent = start_copies([(sums, sums_hbm), (middle, middle_hbm)], sems.at[pl.ds(6, 2)])
     near, far = pl.ds(0, rows), pl.ds(rows, rows)
     copies = start_copies(
         [
+            (act_near, act.at[near]),
+            (act_far, act.at[far]),
             (second_near, second.at[near]),
             (second_far, second.at[far]),
-            (act_near, act.at[near]),
-            (act_far, act.at[far]),
         ],
         sems,
     )
+    passed_ref[...] = passed[...]
     up[:rows, :] = up_near[...]
     up[rows:, :] = up_far[...]
     grad[:rows, :] = grad_near[...]
     grad[rows:, :] = grad_far[...]
-    for copy in copies:
-        copy.wait()
-    out_ref[:, hidden:] = dot_tn(up[...], act[...]).astype(bf16)
-    out_ref[:, :hidden] = dot_tn(second[...], grad[...]).astype(bf16)
-    token[...] = jnp.zeros_like(token)
+    for copy in copies[:2]:
+        copy.wait()
+    out_two[...] = dot_tn(up[...], act[...]).astype(bf16)
+    sent += start_copies(
+        [(out_two, out_hbm.at[:, pl.ds(hidden, hidden)])], sems.at[pl.ds(4, 1)]
+    )
+    for copy in copies[2:]:
+        copy.wait()
+    out_one[...] = dot_tn(second[...], grad[...]).astype(bf16)
+    sent += start_copies([(out_one, out_hbm.at[:, pl.ds(0, hidden)])], sems.at[pl.ds(5, 1)])
+    for copy in sent:
+        copy.wait()
 
 
 def norm_back(upstream, values, gain):
@@ -416,12 +420,13 @@
     return back, gain_grad, jnp.sum(upstream, axis=0, keepdims=True)
 
 
-def norm_back_two_kernel(gain_row, own, xy, x, y, values_hbm, upstream, vecs,
-                         grad_ref, grad_b_ref, sums_ref, values, sems):
-    copies = start_copies([(values_hbm, values)], sems)
+def norm_back_two_kernel(gain_row, own, xy, x, y, values_hbm, upstream_hbm, vecs,
+                         grad_ref, grad_b_ref, sums_ref, values, upstream, sems):
+    copies = start_copies([(values_hbm, values), (upstream_hbm, upstream)], sems)
+    total = total_of(own, xy, x, y)
+    for copy in copies:
+        copy.wait()
     up = upstream[...]
-    total = total_of(own, xy, x, y)
-    copies[0].wait()
     back, gain_grad, shift_grad = norm_back(
         total, values[...], vecs[gain_row : gain_row + 1, :]
     )
@@ -434,11 +439,12 @@
     sums_ref[3:4, :] = jnp.sum(up, axis=0, keepdims=True)
 
 
-def norm_back_one_kernel(gain_row, own, xy, x, y, values_hbm, upstream, vecs, mask,
-                         grad_ref, grad_b_ref, sums_ref, values, sems):
-    copies = start_copies([(values_hbm, values)], sems)
+def norm_back_one_kernel(gain_row, own, xy, x, y, values_hbm, upstream_hbm, vecs, mask,
+                         grad_ref, grad_b_ref, sums_ref, values, upstream, sems):
+    copies = start_copies([(values_hbm, values), (upstream_hbm, upstream)], sems)
     total = total_of(own, xy, x, y)
-    copies[0].wait()
+    for copy in copies:
+        copy.wait()
     back, gain_grad, shift_grad = norm_back(
         total, values[...], vecs[gain_row : gain_row + 1, :]
     )
@@ -520,20 +526,24 @@
         partial_ref[:, columns] = dot_nt(packed[...], w[:, : 3 * feats]).astype(bf16)
 
 
-def attn_grad_kernel(feats, first_near, first_far, att_near, att_far, up_near, up_far,
-                     gq_near, gq_far, gk, gv, *refs):
-    *outs, sums_ref, token, first, att, up, packed, sems = refs
+def attn_grad_kernel(feats, count, first_near, first_far, att_near, att_far, up_near, up_far,
+                     gq_near, gq_far, gk, gv, passed, sums, stream, *refs):
+    outs, rest = refs[:count], refs[count:]
+    heads_hbm, passed_ref, sums_hbm, stream_hbm, *rest = rest
+    first, att, up, packed, sums_ref, *staged, sems = rest
     rows = up_near.shape[0]
+    sent = start_copies([(sums, sums_hbm), (stream, stream_hbm)], sems.at[pl.ds(6, 2)])
     near, far = pl.ds(0, rows), pl.ds(rows, rows)
     copies = start_copies(
         [
+            (att_near, att.at[near]),
+            (att_far, att.at[far]),
             (first_near, first.at[near]),
             (first_far, first.at[far]),
-            (att_near, att.at[near]),
-            (att_far, att.at[far]),
         ],
         sems,
     )
+    passed_ref[...] = passed[...]
     up[:rows, :] = up_near[...]
     up[rows:, :] = up_far[...]
     packed[:rows, :feats] = gq_near[...].astype(bf16)
@@ -544,17 +554,46 @@
         gq_far[...], axis=0, keepdims=True
     )
     sums_ref[1:2, :] = jnp.sum(gv[...], axis=0, keepdims=True)
+    sent += start_copies([(sums_ref, heads_hbm)], sems.at[pl.ds(8, 1)])
+    if count == 1:
+        out_one, out_two = staged
+        for copy in copies[:2]:
+            copy.wait()
+        out_two[...] = dot_tn(up[...], att[...]).astype(bf16)
+        sent += start_copies(
+            [(out_two, outs[0].at[:, pl.ds(3 * feats, feats)])], sems.at[pl.ds(4, 1)]
+        )
+        for copy in copies[2:]:
+            copy.wait()
+        out_one[...] = dot_tn(first[...], packed[...]).astype(bf16)
+        sent += start_copies(
+            [(out_one, outs[0].at[:, pl.ds(0, 3 * feats)])], sems.at[pl.ds(5, 1)]
+        )
+        for copy in sent:
+            copy.wait()
+        return
     for copy in copies:
         copy.wait()
     width_own = outs[0].shape[0]
     for d, out_ref in enumerate(outs):
-        place = lax.rem(lax.axis_index("fsdp") + d, len(outs)) if len(outs) > 1 else 0
-        span = pl.ds(place * width_own, width_own)
-        if len(outs) > 1:
-            span = pl.ds(pl.multiple_of(place * width_own, width_own), width_own)
+        place = lax.rem(lax.axis_index("fsdp") + d, count)
+        span = pl.ds(pl.multiple_of(place * width_own, width_own), width_own)
         out_ref[:, : 3 * feats] = dot_tn(first[:, span], packed[...]).astype(bf16)
         out_ref[:, 3 * feats :] = dot_tn(up[:, span], att[...]).astype(bf16)
+    for copy in sent:
+        copy.wait()
+
+
+def settle_kernel(passed, *refs):
+    passed_ref = refs[-1]
+    passed_ref[...] = passed[...]
+
+
+def fetch_kernel(count, *refs):
+    sources, targets, (token, sems) = refs[:count], refs[count : 2 * count], refs[2 * count :]
     token[...] = jnp.zeros_like(token)
+    for copy in start_copies(list(zip(sources, targets)), sems):
+        copy.wait()
 
 
 def shard_sum_kernel(*refs):
@@ -562,56 +601,125 @@
     out_ref[...] = sum(term[...].astype(f32) for term in terms).astype(out_ref.dtype)
 
 
-def place_mlp_kernel(layer, hidden, p0, p1, p2, p3, *refs):
-    fc1_hbm, fc2_hbm, token, fc1, fc2, sems = refs[-6:]
+def place_kernel(depth, hidden, feats, *refs):
+    pieces = refs[: 8 * depth]
+    outs, (fc1, fc2, qkv, out, sems) = refs[8 * depth : 8 * depth + 4], refs[8 * depth + 4 :]
+    qkv_hbm, out_hbm, fc1_hbm, fc2_hbm = outs
     ci = lax.rem(lax.axis_index("ctx"), GROUP)
     copies = []
-    for k, piece in enumerate((p0, p1, p2, p3)):
-        span = pl.ds(pl.multiple_of((ci ^ k) * hidden, hidden), hidden)
-        fc1[k] = piece[:, :hidden].astype(f32)
-        copies += start_copies(
-            [(fc1.at[k], fc1_hbm.at[layer, :, span])], sems.at[pl.ds(2 * k, 1)]
-        )
-        fc2[k] = piece[:, hidden:].astype(f32).T
-        copies += start_copies(
-            [(fc2.at[k], fc2_hbm.at[layer, span, :])], sems.at[pl.ds(2 * k + 1, 1)]
-        )
+
+    def send(source, target):
+        copies.extend(start_copies([(source, target)], sems.at[pl.ds(len(copies), 1)]))
+
+    for l in reversed(range(depth)):
+        for k in range(GROUP):
+            piece = pieces[8 * l + k]
+            span = pl.ds(pl.multiple_of((ci ^ k) * hidden, hidden), hidden)
+            fc1[l, k] = piece[:, :hidden].astype(f32)
+            send(fc1.at[l, k], fc1_hbm.at[l, :, span])
+            fc2[l, k] = piece[:, hidden:].T.astype(f32)
+            send(fc2.at[l, k], fc2_hbm.at[l, span, :])
+    for l in reversed(range(depth)):
+        for k in range(GROUP):
+            piece = pieces[8 * l + 4 + k]
+            span = pl.ds(pl.multiple_of((ci ^ k) * feats, feats), feats)
+            for j in range(3):
+                qkv[l, k, j] = piece[:, j * feats : (j + 1) * feats].astype(f32)
+            send(qkv.at[l, k], qkv_hbm.at[l, :, :, span])
+            out[l, k] = piece[:, 3 * feats :].T.astype(f32)
+            send(out.at[l, k], out_hbm.at[l, span, :])
+    for copy in copies:
+        copy.wait()
+
+
+def vector_pack_kernel(depth, *refs):
+    count = 5 * depth
+    out_ref, *terms, sems = refs[count:]
+    copies = start_copies(list(zip(refs[:count], terms)), sems)
+    out_ref[...] = jnp.zeros_like(out_ref)
+    for copy in copies:
+        copy.wait()
+    for l in range(depth):
+        one, two, unit_near, unit_far, head = terms[5 * l : 5 * l + 5]
+        out_ref[6 * l : 6 * l + 1, :] = one[0:1, :]
+        out_ref[6 * l + 1 : 6 * l + 2, :] = two[0:1, :]
+        out_ref[6 * l + 2 : 6 * l + 3, :] = one[1:2, :]
+        out_ref[6 * l + 3 : 6 * l + 6, :] = two[1:4, :]
+        units = unit_near.shape[1]
+        feats = head.shape[1]
+        row = 6 * depth
+        out_ref[row : row + 1, l * units : (l + 1) * units] = unit_near[...] + unit_far[...]
+        for j in range(2):
+            first = (2 * l + j) * feats
+            out_ref[row + 1 : row + 2, first : first + feats] = head[j : j + 1, :]
+
+
+def vector_own_kernel(depth, width_own, own, *refs):
+    *others, out_ref, token = refs
+    total = own[...]
+    for other in others:
+        total = total + other[...]
+    f = lax.axis_index("fsdp")
+    count = total.shape[1] // width_own
+    mine = jnp.zeros((6 * depth, width_own), f32)
+    for a in range(count):
+        piece = total[: 6 * depth, a * width_own : (a + 1) * width_own]
+        mine = jnp.where(f == a, piece, mine)
+        for r in range(2):
+            row = 6 * depth + r
+            out_ref[16 + count * r + a : 17 + count * r + a, :] = total[
+                row : row + 1, a * width_own : (a + 1) * width_own
+            ]
+    out_ref[: 6 * depth, :] = mine
     token[...] = jnp.zeros_like(token)
-    for copy in copies:
-        copy.wait()
-
-
-def place_attn_kernel(layer, feats, p0, p1, p2, p3, *refs):
-    qkv_hbm, out_hbm, token, qkv, out, sems = refs[-6:]
+
+
+def vector_plane_kernel(depth, own, xy, x, y, out_ref):
+    last = 6 * depth
+    out_ref[:last, :] = own[:last, :] + xy[:last, :] + x[:last, :] + y[:last, :]
+    out_ref[16:24, :] = own[16:24, :]
+    out_ref[24:32, :] = x[16:24, :]
+
+
+def vector_place_kernel(depth, head_dim, own, far, gains_ref, shifts_ref, unit_ref, heads_ref):
+    total = own[: 6 * depth, :] + far[: 6 * depth, :]
+    for l in range(depth):
+        gains_ref[l] = total[6 * l : 6 * l + 2, :]
+        shifts_ref[l] = total[6 * l + 2 : 6 * l + 6, :]
+    pieces = (own[16:24, :], far[16:24, :], own[24:32, :], far[24:32, :])
     ci = lax.rem(lax.axis_index("ctx"), GROUP)
-    copies = []
-    for k, piece in enumerate((p0, p1, p2, p3)):
-        span = pl.ds(pl.multiple_of((ci ^ k) * feats, feats), feats)
-        for j in range(3):
-            qkv[k, j] = piece[:, j * feats : (j + 1) * feats].astype(f32)
-        copies += start_copies(
-            [(qkv.at[k], qkv_hbm.at[layer, :, :, span])], sems.at[pl.ds(2 * k, 1)]
-        )
-        out[k] = piece[:, 3 * feats :].astype(f32).T
-        copies += start_copies(
-            [(out.at[k], out_hbm.at[layer, span, :])], sems.at[pl.ds(2 * k + 1, 1)]
-        )
-    token[...] = jnp.zeros_like(token)
-    for copy in copies:
-        copy.wait()
-
-
-def place_call(body, pieces, before, outs, scratch, name):
-    extra = () if before is None else (Far(before[0]), Far(before[1]))
-    return kernel_call(
-        body,
-        [saved(s, f32) for s in outs] + [TOKEN],
-        *pieces,
-        *extra,
-        name=name,
-        scratch=[pltpu.VMEM(s, f32) for s in scratch] + [DMA((8,))],
-        aliases={} if before is None else {4: 0, 5: 1},
-    )
+    f = lax.axis_index("fsdp")
+
+    def of_place(c):
+        k = ci ^ c
+        found = pieces[0]
+        for j in range(1, GROUP):
+            found = jnp.where(k == j, pieces[j], found)
+        return found
+
+    width_own = own.shape[1]
+    units = of_place(f)
+    parts = unit_ref.shape[2] // width_own
+    for l in range(depth):
+        for j in range(parts):
+            row = l * parts + j
+            unit_ref[l, :, j * width_own : (j + 1) * width_own] = units[row : row + 1, :]
+    head_own = heads_ref.shape[3]
+    heads = heads_ref.shape[2] // GROUP
+    for c in range(GROUP):
+        found = of_place(c)
+        for l in range(depth):
+            for j in range(2):
+                for h in range(heads):
+                    first = ((2 * l + j) * heads + h) * head_dim
+                    row, lane = 4 + first // width_own, first % width_own
+                    value = found[row : row + 1, lane : lane + head_own]
+                    for a in range(1, head_dim // head_own):
+                        start = lane + a * head_own
+                        value = jnp.where(
+                            f == a, found[row : row + 1, start : start + head_own], value
+                        )
+                    heads_ref[l, j, c * heads + h : c * heads + h + 1, :] = value
 
 
 def place_rows_kernel(own, other, out_hbm, sems):
@@ -676,13 +784,10 @@
         near = (own, swap_xy(own), swap_x(own), swap_y(own))
         return near, tuple(swap_core(chunk) for chunk in near)
 
-    def gate(value, after):
+    def settle(value, *after):
         return kernel_call(
-            copy_kernel, [(value.shape, value.dtype)], value, name="gate", after=after
+            settle_kernel, [(value.shape, value.dtype)], value, name="settle", after=after
         )[0]
-
-    def touch(value):
-        return kernel_call(touch_kernel, [TOKEN], value, name="touch")[0]
 
     def reduce_rows(*pairs, after=()):
         count = len(pairs)
@@ -777,12 +882,12 @@
     row_bf16 = ((rows, width), bf16)
     upstream, upstream_b, usable, mask = kernel_call(
         functools.partial(prep_upstream_kernel, tp, outer),
-        [row_f32, row_bf16, ((1, key_rows), f32), ((rows, 128), f32)],
+        [saved((rows, width), f32), row_bf16, ((1, key_rows), f32), ((rows, 128), f32)],
         Scalars(lengths),
         Far(cotangent),
         name="prep_upstream",
         after=(pack_token,),
-        scratch=[pltpu.VMEM((rows, width), f32), DMA((1,))],
+        scratch=[pltpu.VMEM((rows, width), f32), pltpu.VMEM((rows, width), f32), DMA((2,))],
     )
     near, far = gather_rows(upstream_b)
     half_x = pltpu.VMEM((half, width), bf16)
@@ -922,16 +1027,59 @@
         for side in (1, 0):
             back[side] = kernel_call(
                 functools.partial(mlp_back_kernel, hidden, len(upstream_chunks[side])),
-                [partial_out, ((half, hidden), bf16), ((1, hidden), f32), ((half, width), bf16)],
+                [
+                    partial_out,
+                    ((half, hidden), bf16),
+                    saved((1, hidden), f32),
+                    ((half, width), bf16),
+                ],
                 *upstream_chunks[side],
                 mlp_w[l],
                 mlp[side][3],
                 name="mlp_back",
-                scratch=[pltpu.VMEM((2, half, hidden // 2), f32), DMA((2,))],
+                scratch=[
+                    pltpu.VMEM((2, half, hidden // 2), f32),
+                    pltpu.VMEM((1, hidden), f32),
+                    DMA((3,)),
+                ],
             )
-        mlp_grad, grad_token = kernel_call(
+        pairs_now = [(back[0][0], back[1][0])]
+        if l + 1 == depth:
+            pairs_now.append((mlp[0][0], mlp[1][0]))
+        sums, *output_sums = reduce_rows(*pairs_now)
+        if l + 1 == depth:
+            outputs_own, output_token = kernel_call(
+                functools.partial(sum_out_kernel, shift_row(l, 3)),
+                [saved((rows, width), f32), TOKEN],
+                *output_sums[0],
+                Far(mlp[1][4]),
+                vecs,
+                mask,
+                name="sum_out",
+                scratch=[pltpu.VMEM((rows, width), f32)] * 2 + [DMA((2,))],
+            )
+            after = (output_token,)
+        else:
+            after = ()
+        unit_sums[l] = (back[0][2], back[1][2])
+        grad_middle, middle_b, sums_two = kernel_call(
+            functools.partial(norm_back_two_kernel, gain_row(l, 1)),
+            [row_f32, row_bf16, ((4, width), f32)],
+            *sums,
+            Far(mlp[1][4]),
+            Far(upstream),
+            vecs,
+            name="norm_back_two",
+            scratch=[pltpu.VMEM((rows, width), f32)] * 2 + [DMA((2,))],
+        )
+        mlp_grad, middle_b, sums_two, grad_middle = kernel_call(
             functools.partial(mlp_grad_kernel, hidden),
-            [((width, 2 * hidden), bf16), TOKEN],
+            [
+                saved((width, 2 * hidden), bf16),
+                row_bf16,
+                saved((4, width), f32),
+                saved((rows, width), f32),
+            ],
             mlp[0][1],
             mlp[1][1],
             mlp[0][2],
@@ -940,35 +1088,25 @@
             back[1][3],
             back[0][1],
             back[1][1],
+            middle_b,
+            sums_two,
+            grad_middle,
             name="mlp_grad",
-            after=() if l + 1 == depth else (touch(mlp_parts[l + 1]),),
+            after=after,
             scratch=[
                 pltpu.VMEM((all_rows, width), bf16),
                 pltpu.VMEM((all_rows, hidden), bf16),
                 pltpu.VMEM((all_rows, width), bf16),
                 pltpu.VMEM((all_rows, hidden), bf16),
-                DMA((4,)),
+                pltpu.VMEM((width, hidden), bf16),
+                pltpu.VMEM((width, hidden), bf16),
+                DMA((8,)),
             ],
             limit=16,
         )
-        pairs_now = [(back[0][0], back[1][0])]
-        if l + 1 == depth:
-            pairs_now.append((mlp[0][0], mlp[1][0]))
-        sums, *output_sums = reduce_rows(*pairs_now, after=(grad_token,))
-        if l + 1 == depth:
-            output_term = output_sums[0]
         mlp_parts[l] = scatter_grads(mlp_grad)
-        unit_sums[l] = back[0][2] + back[1][2]
-        grad_middle, middle_b, sums_two = kernel_call(
-            functools.partial(norm_back_two_kernel, gain_row(l, 1)),
-            [row_f32, row_bf16, ((4, width), f32)],
-            *sums,
-            Far(mlp[1][4]),
-            upstream,
-            vecs,
-            name="norm_back_two",
-            scratch=[pltpu.VMEM((rows, width), f32), DMA((1,))],
-        )
+        if l + 1 < depth:
+            middle_b = settle(middle_b, Far(mlp_parts[l + 1]))
         middle_chunks = gather_rows(middle_b)
         grad_q = [None, None]
         middle_x = [None, None]
@@ -1032,40 +1170,9 @@
                 scratch=[pltpu.VMEM((half, 3 * feats), bf16)],
             )[0]
 
-        def weight_grad(after=()):
-            count = 1 if l > 0 else fsdp
-            *parts, head_sum, token = kernel_call(
-                functools.partial(attn_grad_kernel, feats),
-                [((width // count, 4 * feats), bf16)] * count + [((2, feats), f32), TOKEN],
-                Far(attn[0][3]),
-                Far(attn[1][3]),
-                Far(attn[0][1]),
-                Far(attn[1][1]),
-                *middle_x,
-                *grad_q,
-                grad_k,
-                grad_v,
-                name="attn_grad",
-                after=after,
-                scratch=[
-                    pltpu.VMEM((all_rows, width), bf16),
-                    pltpu.VMEM((all_rows, feats), bf16),
-                    pltpu.VMEM((all_rows, width), bf16),
-                    pltpu.VMEM((all_rows, 3 * feats), bf16),
-                    DMA((4,)),
-                ],
-            )
-
-            return parts, head_sum, token
-
         far_part = project(1, ())
         near_part = project(0, ())
-        attn_grads, head_sums[l], grad_token = weight_grad(
-            () if l + 1 == depth else (touch(attn_parts[l + 1]),)
-        )
-        (sums,) = reduce_rows((near_part, far_part), after=(grad_token,))
-        if l > 0:
-            attn_parts[l] = scatter_grads(attn_grads[0])
+        (sums,) = reduce_rows((near_part, far_part))
         body = functools.partial(norm_back_one_kernel, gain_row(l, 0))
         if l > 0:
             masked = ()
@@ -1077,154 +1184,156 @@
             [row_f32, row_bf16, ((2, width), f32)],
             *sums,
             Far(attn[1][5]),
-            grad_middle,
+            Far(grad_middle),
             vecs,
             *masked,
             name="norm_back_one",
-            scratch=[pltpu.VMEM((rows, width), f32), DMA((1,))],
+            scratch=[pltpu.VMEM((rows, width), f32)] * 2 + [DMA((2,))],
+        )
+        after = ()
+        if l == 0:
+            early = [(k, kind) for k in range(depth) for kind in (0, 1) if (k, kind) != (0, 1)]
+            sources = [(mlp_parts, attn_parts)[kind][k] for k, kind in early]
+            *fetched, token = kernel_call(
+                functools.partial(fetch_kernel, len(early)),
+                [(v.shape, v.dtype) for v in sources] + [TOKEN],
+                *[Far(v) for v in sources],
+                name="fetch",
+                after=(sums_one,),
+                scratch=[DMA((len(early),))],
+            )
+            after = (token,)
+        count = 1 if l > 0 else fsdp
+        shapes = [((width, 3 * feats), bf16), ((width, feats), bf16)]
+        *attn_grads, head_sums[l], upstream_b, sums_one, upstream = kernel_call(
+            functools.partial(attn_grad_kernel, feats, count),
+            [saved((width, 4 * feats), bf16) if l > 0 else ((width_own, 4 * feats), bf16)] * count
+            + [
+                saved((2, feats), f32),
+                row_bf16,
+                saved((2, width), f32),
+                saved((rows, width), f32),
+            ],
+            Far(attn[0][3]),
+            Far(attn[1][3]),
+            Far(attn[0][1]),
+            Far(attn[1][1]),
+            *middle_x,
+            *grad_q,
+            grad_k,
+            grad_v,
+            upstream_b,
+            sums_one,
+            upstream,
+            name="attn_grad",
+            after=after,
+            scratch=[
+                pltpu.VMEM((all_rows, width), bf16),
+                pltpu.VMEM((all_rows, feats), bf16),
+                pltpu.VMEM((all_rows, width), bf16),
+                pltpu.VMEM((all_rows, 3 * feats), bf16),
+                pltpu.VMEM((2, feats), f32),
+            ]
+            + [pltpu.VMEM(*shape) for shape in shapes if count == 1]
+            + [DMA((9,))],
         )
         if l > 0:
+            attn_parts[l] = scatter_grads(attn_grads[0])
             upstream_chunks = gather_rows(upstream_b)
         row_sums[l] = (sums_one, sums_two)
 
-    vec_part = jnp.concatenate(
-        [
-            piece
-            for l in range(depth)
-            for piece in (
-                row_sums[l][0][0:1],
-                row_sums[l][1][0:1],
-                row_sums[l][0][1:2],
-                row_sums[l][1][1:4],
-            )
-        ],
-        axis=0,
-    )
-    unit_part = jnp.concatenate(unit_sums, axis=0)
-    head_part = jnp.concatenate(head_sums, axis=0)
-    unit_lines = unit_part.reshape(-1, width)
-    head_lines = head_part.reshape(1, -1)
-    head_lines = jnp.pad(head_lines, ((0, 0), (0, width - head_lines.shape[1])))
-    packed = jnp.concatenate([vec_part, unit_lines, head_lines], axis=0)
+    parts = dict(zip(early, fetched))
+    vector_rows = 6 * depth + 2
+    terms = [v for l in range(depth) for v in (*row_sums[l], *unit_sums[l], head_sums[l])]
+    packed = kernel_call(
+        functools.partial(vector_pack_kernel, depth),
+        [((vector_rows, width), f32)],
+        *[Far(v) for v in terms],
+        name="vector_pack",
+        scratch=[pltpu.VMEM(v.shape, f32) for v in terms] + [DMA((len(terms),))],
+    )[0]
     if outer > 1:
         packed = lax.psum(packed, "ctx", axis_index_groups=outer_groups)
-    early = [(l, kind) for l in range(depth) for kind in (0, 1) if (l, kind) != (0, 1)]
-    parts = {key: gate((mlp_parts, attn_parts)[key[1]][key[0]], (sums_one,)) for key in early}
-    outputs_own = kernel_call(
-        functools.partial(sum_out_kernel, shift_row(depth - 1, 3)),
-        [row_f32],
-        *output_term,
-        Far(saved_all[depth - 1][2][1][4]),
-        vecs,
-        mask,
-        name="sum_out",
-        after=(sums_one,),
-        scratch=[pltpu.VMEM((rows, width), f32), DMA((1,))],
-    )[0]
     last_terms = (attn_grads[0], *[shift_z(attn_grads[d], d) for d in range(1, fsdp)])
     crossed = {key: swap_x(parts[key]) for key in early}
     others = (swap_y(upstream), swap_y(outputs_own))
-    packed, hub_token = kernel_call(
-        vector_sum_kernel,
-        [(packed.shape, f32), TOKEN],
+    mine, hub_token = kernel_call(
+        functools.partial(vector_own_kernel, depth, width_own),
+        [((24, width_own), f32), TOKEN],
         packed,
         *[shift_z(packed, d) for d in range(1, fsdp)],
-        name="vector_sum",
+        name="vector_own",
         after=(*crossed.values(), *others, *last_terms[1:]),
+    )
+    part = kernel_call(
+        shard_sum_kernel,
+        [((width_own, 4 * feats), bf16)],
+        *last_terms,
+        name="shard_sum",
+        after=(hub_token,),
+    )[0]
+    if outer > 1:
+        part = lax.psum(part, "ctx", axis_index_groups=outer_groups)
+    parts[0, 1], crossed[0, 1] = part, swap_x(part)
+    pieces = {
+        key: (parts[key], swap_core(parts[key]), crossed[key], swap_core(crossed[key]))
+        for key in parts
+    }
+    mine = kernel_call(
+        functools.partial(vector_plane_kernel, depth),
+        [((32, width_own), f32)],
+        mine,
+        swap_xy(mine),
+        swap_x(mine),
+        swap_y(mine),
+        name="vector_plane",
+        after=(crossed[0, 1],),
+    )[0]
+    grad_gains, grad_shifts, grad_fc1_bias, grad_qv_bias = kernel_call(
+        functools.partial(vector_place_kernel, depth, head_dim),
+        [
+            (norm_gains.shape, f32),
+            (shifts.shape, f32),
+            (fc1_bias.shape, f32),
+            (qv_bias.shape, f32),
+        ],
+        mine,
+        swap_core(mine),
+        name="vector_place",
     )
     grad_inputs, outputs = (
         kernel_call(
             place_rows_kernel,
             [saved(inputs.shape, f32)],
-            own,
+            Far(own),
             other,
             name="place_rows",
             scratch=[DMA((2,))],
         )[0]
         for own, other in zip((upstream, outputs_own), others)
     )
-    vec_sum = lax.dynamic_slice_in_dim(packed[:vec_rows], f * width_own, width_own, axis=1)
-    vec_sum = vec_sum.reshape(-1, width)
-    vec_lines = vec_sum.shape[0]
-    rest = packed[vec_rows:]
-    mine = jnp.concatenate([vec_sum, rest], axis=0)
-    from_x = swap_x(mine)
-    vec_sum = vec_sum + swap_xy(vec_sum) + from_x[:vec_lines] + swap_y(vec_sum)
-    mine = jnp.concatenate([vec_sum, rest, from_x[vec_lines:]], axis=0)
-    from_core = swap_core(mine)
-    vec_sum = (vec_sum + from_core[:vec_lines]).reshape(depth, 6, width_own)
-    count = rest.shape[0]
-    rest_four = jnp.stack(
-        [
-            rest,
-            from_core[vec_lines : vec_lines + count],
-            mine[vec_lines + count :],
-            from_core[vec_lines + count :],
-        ]
-    )
-    unit_count = unit_lines.shape[0]
-
-    def of_place(c):
-        return lax.dynamic_index_in_dim(rest_four, ci ^ c, 0, keepdims=False)
-
-    grad_fc1_bias = of_place(f)[:unit_count].reshape(depth, 1, hidden)
-    grad_qv_bias = jnp.stack(
-        [
-            lax.dynamic_slice_in_dim(
-                of_place(c)[unit_count, : head_part.size].reshape(depth, 2, heads, head_dim),
-                f * head_own,
-                head_own,
-                axis=3,
-            )
-            for c in range(GROUP)
+    placed = kernel_call(
+        functools.partial(place_kernel, depth, hidden, feats),
+        [saved(v.shape, f32) for v in (w_qkv, w_out, w_fc1, w_fc2)],
+        *[piece for l in range(depth) for kind in (0, 1) for piece in pieces[l, kind]],
+        name="place",
+        limit=24,
+        scratch=[
+            pltpu.VMEM((depth, GROUP, width_own, hidden), f32),
+            pltpu.VMEM((depth, GROUP, hidden, width_own), f32),
+            pltpu.VMEM((depth, GROUP, 3, width_own, feats), f32),
+            pltpu.VMEM((depth, GROUP, feats, width_own), f32),
+            DMA((16 * depth,)),
         ],
-        axis=2,
-    ).reshape(qv_bias.shape)
-    placed = [None, None]
-    for l, kind in early + [(0, 1)]:
-        if (l, kind) in parts:
-            part, other = parts[l, kind], crossed[l, kind]
-        else:
-            part = kernel_call(
-                shard_sum_kernel,
-                [((width_own, 4 * feats), bf16)],
-                *last_terms,
-                name="shard_sum",
-                after=(hub_token,),
-            )[0]
-            if outer > 1:
-                part = lax.psum(part, "ctx", axis_index_groups=outer_groups)
-            other = swap_x(part)
-        pieces = (part, swap_core(part), other, swap_core(other))
-        if kind == 0:
-            placed[0] = place_call(
-                functools.partial(place_mlp_kernel, l, hidden),
-                pieces,
-                placed[0],
-                [w_fc1.shape, w_fc2.shape],
-                [(GROUP, width_own, hidden), (GROUP, hidden, width_own)],
-                "place_mlp",
-            )
-        else:
-            placed[1] = place_call(
-                functools.partial(place_attn_kernel, l, feats),
-                pieces,
-                placed[1],
-                [w_qkv.shape, w_out.shape],
-                [(GROUP, 3, width_own, feats), (GROUP, feats, width_own)],
-                "place_attn",
-            )
+    )
     return (
         outputs,
         grad_inputs,
-        vec_sum[:, :2],
-        vec_sum[:, 2:],
+        grad_gains,
+        grad_shifts,
         grad_qv_bias,
         grad_fc1_bias,
-        placed[1][0],
-        placed[1][1],
-        placed[0][0],
-        placed[0][1],
+        *placed,
     )
 
 

time: 422 us -> 417 us (0.988)
  local copies, waits for them, and re-layouts: 42.6 us -> 7.99 us
  Pallas kernels: 108 us -> 124 us
  starting transfers between devices: 114 us -> 121 us
  waiting for transfers between devices: 134 us -> 141 us
    unnamed x165 -> x46, local copies, waits for them, and re-layouts: 37.4 us -> 7.28 us
    pallas_call x63 -> x60, Pallas kernels: 108 us -> 124 us  [kernel_call(): pl.pallas_call(run, out_shape=out_shape, in_specs=specs, out_specs=out_sp...]
    ppermute x9, waiting for transfers between devices: 11.5 us -> 26.1 us  [shift_z(): lax.ppermute(value, 'fsdp', [(i, (i + d) % fsdp) for i in range(fsdp)])]
    ppermute x20, waiting for transfers between devices: 45.6 us -> 32.2 us  [swap_x(): return lax.ppermute(value, 'ctx', [(i, i ^ 2) for i in range(ctx)])]
    ppermute x16, starting transfers between devices: 30.7 us -> 17.7 us  [swap_xy(): return lax.ppermute(value, ('ctx', 'tp'), pairs)]
    ppermute x49, starting transfers between devices: 49.8 us -> 62.8 us  [swap_core(): return lax.ppermute(value, 'ctx', [(i, i ^ 1) for i in range(ctx)])]
    ppermute x18, waiting for transfers between devices: 8.24 us -> 18.7 us  [swap_y(): return lax.ppermute(value, 'tp', [(i, i ^ 1) for i in range(tp)])]
    ppermute x20, starting transfers between devices: 7.97 us -> 15.7 us  [swap_x(): return lax.ppermute(value, 'ctx', [(i, i ^ 2) for i in range(ctx)])]
  transfers between devices with their start and end apart: 119 -> 119, of which waited for: 50 -> 50; matrix products, arithmetic and copies ran while one was open for 1% -> 1% of each run, Pallas kernels for 23% -> 25%
where the time goes in v6:
time: 417 us; the launch traced here: 411 us
  waiting for transfers between devices  141 us (34%)
  Pallas kernels  124 us (30%)
  starting transfers between devices  121 us (29%)
  between operations  15.6 us (4%)
  local copies, waits for them, and re-layouts  7.99 us (2%)
    pallas_call x60, Pallas kernels, kernel_call(): pl.pallas_call(run, out_shape=out_shape, in_specs=specs, out_specs=out_sp...  124 us
    ppermute x49, starting transfers between devices, swap_core(): return lax.ppermute(value, 'ctx', [(i, i ^ 1) for i in range(ctx)])  62.8 us
    ppermute x16, waiting for transfers between devices, swap_xy(): return lax.ppermute(value, ('ctx', 'tp'), pairs)  35.9 us
    ppermute x20, waiting for transfers between devices, swap_x(): return lax.ppermute(value, 'ctx', [(i, i ^ 2) for i in range(ctx)])  32.2 us
    ppermute x9, waiting for transfers between devices, shift_z(): lax.ppermute(value, 'fsdp', [(i, (i + d) % fsdp) for i in range(fsdp)])  26.1 us
    ppermute x18, waiting for transfers between devices, swap_y(): return lax.ppermute(value, 'tp', [(i, i ^ 1) for i in range(tp)])  18.7 us
    ppermute x16, starting transfers between devices, swap_xy(): return lax.ppermute(value, ('ctx', 'tp'), pairs)  17.7 us
    all_gather x2, waiting for transfers between devices, per_device(): mlp_w.append(lax.all_gather(own, 'fsdp', axis=0, tiled=True))  16.7 us
  transfers between devices with their start and end apart: 119, of which 50 were waited for; matrix products, arithmetic and copies ran while one was open for 1% of the time, Pallas kernels for 25%

profile of v6, /device:TPU:9, one launch (start us, length us, event | category | flops | bytes accessed | tf_op | source)
XLA Modules:
  0.0 410.7 jit_solution(3528863835573964146)
XLA Ops:
  46.0 3.4 attn.5
  52.4 2.6 attn.4
  57.8 3.7 collective-permute-done.18.refs_1_
  61.5 3.6 collective-permute-done.19.refs_2_
  73.6 2.6 collective-permute-start.26
  79.3 5.8 %all-gather.9.cloned.1.call-done.refs_4_ = bf16[1024,1024]{1,0:T(8,128)(2,1)} async-done(((bf16[256,1024]{1,0:T(8,128)(2,1)}), bf16[1024,1024]{1,0:T(8,128)(2,1)}) %all-gather.9.cloned.1.call-update) | async-done | bytes 2097168 | tf_op jit(solution)/shard_map/all_gather | solution.py:841
  94.1 3.6 collective-permute-done.29.refs_1_
  97.6 3.6 collective-permute-done.30.refs_2_
  120.4 2.6 attn.7
  123.3 2.6 attn.6
  128.8 3.7 collective-permute-done.40.refs_1_
  132.5 3.6 collective-permute-done.41.refs_2_
  149.4 10.9 %all-gather.5.cloned.1.call-done.refs_4_.refs_1_ = bf16[1024,1024]{1,0:T(8,128)(2,1)} async-done(((bf16[256,1024]{1,0:T(8,128)(2,1)}), bf16[1024,1024]{1,0:T(8,128)(2,1)}) %all-gather.5.cloned.1.call-update) | async-done | bytes 2097168 | tf_op jit(solution)/shard_map/all_gather | solution.py:841
  161.9 2.6 mlp.7
  164.5 3.3 mlp_back.5
  170.1 2.9 mlp_back.4
  176.0 7.1 %collective-permute-done.52.refs_1_ = bf16[160,1024]{1,0:T(8,128)(2,1)S(1)} collective-permute-done((bf16[160,1024]{1,0:T(8,128)(2,1)S(1)}, bf16[160,1024]{1,0:T(8,128)(2,1)S(1)}, u32[]{:S(2)}, u32[]{:S(2)}) %collective-permute-start.52) | collective-permute-done | bytes 327712 | tf_op jit(solution)/shard_map/ppermute | solution.py:776
  183.2 7.0 %collective-permute-done.53.refs_2_ = bf16[160,1024]{1,0:T(8,128)(2,1)S(1)} collective-permute-done((bf16[160,1024]{1,0:T(8,128)(2,1)S(1)}, bf16[160,1024]{1,0:T(8,128)(2,1)S(1)}, u32[]{:S(2)}, u32[]{:S(2)}) %collective-permute-start.53) | collective-permute-done | bytes 327712 | tf_op jit(solution)/shard_map/ppermute | solution.py:767
  194.2 3.8 mlp_grad.2
  204.9 2.3 collective-permute-start.61
  209.5 3.6 attn_back.4
  213.2 3.6 attn_back.5
  222.4 3.9 collective-permute-done.64.refs_1_
  226.3 3.7 collective-permute-done.65.refs_2_
  231.8 4.0 attn_grad.2
  242.7 2.3 collective-permute-start.72
  248.4 2.4 mlp_back.7
  251.3 2.5 mlp_back.6
  256.7 3.9 collective-permute-done.75.refs_1_
  260.6 3.6 collective-permute-done.76.refs_2_
  266.1 4.3 %mlp_grad.3 = (bf16[1024,1024]{1,0:T(8,128)(2,1)}, bf16[80,1024]{1,0:T(8,128)(2,1)S(1)}, f32[4,1024]{1,0:T(4,128)}, f32[80,1024]{1,0:T(8,128)}) custom-call(bf16[320,1024]{1,0:T(8,128)(2,1)} %get-tuple-element.255.refs_0_, bf16[320,1024]{1,0:T(8,128)(2,1)} %get-tuple-element.256.refs_1_, bf16[320,512]{1,0:T(8,128)(2,1)} %get-tuple-element.257.refs_2_, ...), custom_call_target="tpu_custom_call" | custom-call | tf_op jit(solution)/shard_map/mlp_grad/pallas_call | solution.py:79
  281.9 3.6 attn_back.6
  285.6 3.6 attn_back.7
  294.8 3.6 collective-permute-done.86.refs_1_
  298.4 3.9 collective-permute-done.87.refs_2_
  302.3 3.7 collective-permute-done.88.refs_3_
  307.6 6.9 %reduce-scatter.6.cloned.1.call-done.refs_0_ = bf16[256,1024]{1,0:T(8,128)(2,1)} async-done(((bf16[1024,1024]{1,0:T(8,128)(2,1)}), bf16[256,1024]{1,0:T(8,128)(2,1)}) %reduce-scatter.6.cloned.1.call-update) | async-done | bytes 524304 | tf_op jit(solution)/shard_map/reduce_scatter | solution.py:1014
  315.8 3.8 attn_grad.3
  319.7 3.1 collective-permute-start.96
  326.7 15.3 %collective-permute-done.92.refs_3_ = f32[14,1024]{1,0:T(8,128)S(1)} collective-permute-done((f32[14,1024]{1,0:T(8,128)S(1)}, f32[14,1024]{1,0:T(8,128)S(1)}, u32[]{:S(2)}, u32[]{:S(2)}) %collective-permute-start.92) | collective-permute-done | bytes 57376 | tf_op jit(solution)/shard_map/ppermute | solution.py:779
  342.0 4.0 collective-permute-done.91.refs_2_
  346.0 3.4 collective-permute-done.90.refs_1_
  352.5 3.4 collective-permute-done.98.refs_11_.refs_3_
  355.9 6.2 %collective-permute-start.110 = (bf16[256,512]{1,0:T(8,128)(2,1)S(1)}, bf16[256,512]{1,0:T(8,128)(2,1)S(1)}, u32[]{:S(2)}, u32[]{:S(2)}) collective-permute-start(bf16[256,512]{1,0:T(8,128)(2,1)S(1)} %get-tuple-element.353.refs_12_), channel_id=1, source_target_pairs={{0,2},{2,0},{4,6},{6,4},{1,3},{3,1},{5,7},{7,5},{8,10},{10,8},{12,... | collective-permute-start | bytes 786440 | tf_op jit(solution)/shard_map/ppermute | solution.py:764
  367.3 3.1 collective-permute-done.100.refs_2_
  375.6 11.0 %place_rows.2 = f32[1,160,1024]{2,1,0:T(8,128)} custom-call(f32[80,1024]{1,0:T(8,128)} %get-tuple-element.250.refs_0_, f32[80,1024]{1,0:T(8,128)S(1)} %collective-permute-done.55.refs_1_.refs_8_), custom_call_target="tpu_custom_call" | custom-call | tf_op jit(solution)/shard_map/place_rows/pallas_call | solution.py:79
  386.6 11.1 %place_rows.3 = f32[1,160,1024]{2,1,0:T(8,128)} custom-call(f32[80,1024]{1,0:T(8,128)} %get-tuple-element.340.refs_0_, f32[80,1024]{1,0:T(8,128)S(1)} %collective-permute-done.89.refs_1_.refs_7_), custom_call_target="tpu_custom_call" | custom-call | tf_op jit(solution)/shard_map/place_rows/pallas_call | solution.py:79
  398.7 4.9 %place.1 = (f32[2,3,256,512]{3,2,1,0:T(8,128)}, f32[2,512,256]{2,1,0:T(8,128)}, f32[2,256,2048]{2,1,0:T(8,128)}, f32[2,2048,256]{2,1,0:T(8,128)}) custom-call(bf16[256,1024]{1,0:T(8,128)(2,1)S(1)} %get-tuple-element.351.refs_0_, bf16[256,1024]{1,0:T(8,128)(2,1)S(1)} %collective-permute-done.104.refs_1_, ...), custom_call_target="tpu_custom_call" | custom-call | tf_op jit(solution)/shard_map/place/pallas_call | solution.py:79
  (329 shorter events, 181.1 us)
Async XLA Ops:
  7.2 34.2 %all-gather.7.cloned.1.call-start = ((), (), s32[]{:S(2)}) async-start(), calls=%async_computation.4 | async-start | bytes 1310720 | tf_op jit(solution)/shard_map/all_gather | solution.py:839
  9.0 76.0 %all-gather.9.cloned.1.call-start = ((), (), s32[]{:S(2)}) async-start(), calls=%async_computation.5 | async-start | bytes 2621440 | tf_op jit(solution)/shard_map/all_gather | solution.py:841
  11.2 104.5 %all-gather.11.cloned.1.call-start = ((), (), s32[]{:S(2)}) async-start(), calls=%async_computation.6 | async-start | bytes 1310720 | tf_op jit(solution)/shard_map/all_gather | solution.py:839
  11.4 10.9 %collective-permute-start.9 = (bf16[17,256]{1,0:T(8,128)(2,1)S(1)}, bf16[17,256]{1,0:T(8,128)(2,1)S(1)}, u32[]{:S(2)}, u32[]{:S(2)}) collective-permute-start(bf16[17,256]{1,0:T(8,128)(2,1)S(1)} %fusion.1), channel_id=1, source_target_pairs={{0,8},{8,16},{16,24},{24,0},{1,9},{9,17},{17,25},{25,1},{2,10},{10... | collective-permute-start | bytes 26120 | tf_op jit(solution)/shard_map/ppermute | solution.py:779
  12.8 10.8 %collective-permute-start.8 = (bf16[17,256]{1,0:T(8,128)(2,1)S(1)}, bf16[17,256]{1,0:T(8,128)(2,1)S(1)}, u32[]{:S(2)}, u32[]{:S(2)}) collective-permute-start(bf16[17,256]{1,0:T(8,128)(2,1)S(1)} %fusion.1), channel_id=1, source_target_pairs={{0,16},{8,24},{16,0},{24,8},{1,17},{9,25},{17,1},{25,9},{2,18},{10... | collective-permute-start | bytes 26120 | tf_op jit(solution)/shard_map/ppermute | solution.py:779
  13.9 10.0 %collective-permute-start.7 = (bf16[17,256]{1,0:T(8,128)(2,1)S(1)}, bf16[17,256]{1,0:T(8,128)(2,1)S(1)}, u32[]{:S(2)}, u32[]{:S(2)}) collective-permute-start(bf16[17,256]{1,0:T(8,128)(2,1)S(1)} %fusion.1), channel_id=1, source_target_pairs={{0,24},{8,0},{16,8},{24,16},{1,25},{9,1},{17,9},{25,17},{2,26},{10... | collective-permute-start | bytes 26120 | tf_op jit(solution)/shard_map/ppermute | solution.py:779
  17.6 9.8 %collective-permute-start.3 = (bf16[80,1024]{1,0:T(8,128)(2,1)S(1)}, bf16[80,1024]{1,0:T(8,128)(2,1)S(1)}, u32[]{:S(2)}, u32[]{:S(2)}) collective-permute-start(bf16[80,1024]{1,0:T(8,128)(2,1)S(1)} %get-tuple-element.191.refs_0_), channel_id=1, source_target_pairs={{0,2},{2,0},{4,6},{6,4},{1,3},{3,1},{5,7},{7,5},{8,10},{10,8},{12,... | collective-permute-start | bytes 491528 | tf_op jit(solution)/shard_map/ppermute | solution.py:764
  19.1 9.5 %collective-permute-start.2 = (bf16[80,1024]{1,0:T(8,128)(2,1)S(1)}, bf16[80,1024]{1,0:T(8,128)(2,1)S(1)}, u32[]{:S(2)}, u32[]{:S(2)}) collective-permute-start(bf16[80,1024]{1,0:T(8,128)(2,1)S(1)} %get-tuple-element.191.refs_0_), channel_id=1, source_target_pairs={{0,1},{1,0},{2,3},{3,2},{4,5},{5,4},{6,7},{7,6},{8,9},{9,8},{10,11... | collective-permute-start | bytes 491528 | tf_op jit(solution)/shard_map/ppermute | solution.py:770
  22.2 138.1 %all-gather.5.cloned.1.call-start = ((), (), s32[]{:S(2)}) async-start(), calls=%async_computation.3 | async-start | bytes 2621440 | tf_op jit(solution)/shard_map/all_gather | solution.py:841
  26.1 9.2 %collective-permute-start.12 = (bf16[80,1024]{1,0:T(8,128)(2,1)S(1)}, bf16[80,1024]{1,0:T(8,128)(2,1)}, u32[]{:S(2)}, u32[]{:S(2)}) collective-permute-start(bf16[80,1024]{1,0:T(8,128)(2,1)S(1)} %get-tuple-element.195.refs_0_), channel_id=1, source_target_pairs={{0,1},{1,0},{2,3},{3,2},{4,5},{5,4},{6,7},{7,6},{8,9},{9,8},{10,11... | collective-permute-start | bytes 491528 | tf_op jit(solution)/shard_map/ppermute | solution.py:770
  27.4 8.9 %collective-permute-start.11 = (bf16[80,1024]{1,0:T(8,128)(2,1)S(1)}, bf16[80,1024]{1,0:T(8,128)(2,1)}, u32[]{:S(2)}, u32[]{:S(2)}) collective-permute-start(bf16[80,1024]{1,0:T(8,128)(2,1)S(1)} %get-tuple-element.195.refs_0_), channel_id=1, source_target_pairs={{0,4},{2,6},{4,0},{6,2},{1,5},{3,7},{5,1},{7,3},{8,12},{10,14},{12... | collective-permute-start | bytes 491528 | tf_op jit(solution)/shard_map/ppermute | solution.py:767
  28.6 9.9 %collective-permute-start.10 = (bf16[80,1024]{1,0:T(8,128)(2,1)S(1)}, bf16[80,1024]{1,0:T(8,128)(2,1)}, u32[]{:S(2)}, u32[]{:S(2)}) collective-permute-start(bf16[80,1024]{1,0:T(8,128)(2,1)S(1)} %get-tuple-element.195.refs_0_), channel_id=1, source_target_pairs={{0,5},{1,4},{2,7},{3,6},{4,1},{5,0},{6,3},{7,2},{8,13},{9,12},{10,... | collective-permute-start | bytes 491528 | tf_op jit(solution)/shard_map/ppermute | solution.py:776
  28.8 10.8 %collective-permute-start.6 = (bf16[80,1024]{1,0:T(8,128)(2,1)S(1)}, bf16[80,1024]{1,0:T(8,128)(2,1)S(1)}, u32[]{:S(2)}, u32[]{:S(2)}) collective-permute-start(bf16[80,1024]{1,0:T(8,128)(2,1)S(1)} %collective-permute-done.2.refs_3_), channel_id=1, source_target_pairs={{0,2},{2,0},{4,6},{6,4},{1,3},{3,1},{5,7},{7,5},{8,10},{10,8},{12,... | collective-permute-start | bytes 491528 | tf_op jit(solution)/shard_map/ppermute | solution.py:764
  35.2 9.1 %collective-permute-start.13 = (bf16[80,1024]{1,0:T(8,128)(2,1)S(1)}, bf16[80,1024]{1,0:T(8,128)(2,1)}, u32[]{:S(2)}, u32[]{:S(2)}) collective-permute-start(bf16[80,1024]{1,0:T(8,128)(2,1)S(1)} %get-tuple-element.195.refs_0_), channel_id=1, source_target_pairs={{0,2},{2,0},{4,6},{6,4},{1,3},{3,1},{5,7},{7,5},{8,10},{10,8},{12,... | collective-permute-start | bytes 491528 | tf_op jit(solution)/shard_map/ppermute | solution.py:764
  52.1 218.3 %reduce-scatter.4.cloned.1.call-start = ((), (), s32[]{:S(2)}) async-start(), calls=%async_computation.7 | async-start | bytes 2621440 | tf_op jit(solution)/shard_map/reduce_scatter | solution.py:1014
  69.6 9.4 %collective-permute-start.24 = (bf16[80,1024]{1,0:T(8,128)(2,1)S(1)}, bf16[80,1024]{1,0:T(8,128)(2,1)S(1)}, u32[]{:S(2)}, u32[]{:S(2)}) collective-permute-start(bf16[80,1024]{1,0:T(8,128)(2,1)S(1)} %get-tuple-element.211.refs_0_), channel_id=1, source_target_pairs={{0,2},{2,0},{4,6},{6,4},{1,3},{3,1},{5,7},{7,5},{8,10},{10,8},{12,... | collective-permute-start | bytes 491528 | tf_op jit(solution)/shard_map/ppermute | solution.py:764
  106.6 12.1 %collective-permute-start.35 = (bf16[80,1024]{1,0:T(8,128)(2,1)}, bf16[80,1024]{1,0:T(8,128)(2,1)}, u32[]{:S(2)}, u32[]{:S(2)}) collective-permute-start(bf16[80,1024]{1,0:T(8,128)(2,1)} %get-tuple-element.221.refs_0_), channel_id=1, source_target_pairs={{0,2},{2,0},{4,6},{6,4},{1,3},{3,1},{5,7},{7,5},{8,10},{10,8},{12,... | collective-permute-start | bytes 491528 | tf_op jit(solution)/shard_map/ppermute | solution.py:764
  109.5 9.2 %collective-permute-start.38 = (bf16[80,1024]{1,0:T(8,128)(2,1)}, bf16[80,1024]{1,0:T(8,128)(2,1)}, u32[]{:S(2)}, u32[]{:S(2)}) collective-permute-start(bf16[80,1024]{1,0:T(8,128)(2,1)} %collective-permute-done.34.refs_3_), channel_id=1, source_target_pairs={{0,2},{2,0},{4,6},{6,4},{1,3},{3,1},{5,7},{7,5},{8,10},{10,8},{12,... | collective-permute-start | bytes 491528 | tf_op jit(solution)/shard_map/ppermute | solution.py:764
  140.7 19.6 %collective-permute-start.46 = (bf16[80,1024]{1,0:T(8,128)(2,1)S(1)}, bf16[80,1024]{1,0:T(8,128)(2,1)S(1)}, u32[]{:S(2)}, u32[]{:S(2)}) collective-permute-start(bf16[80,1024]{1,0:T(8,128)(2,1)S(1)} %get-tuple-element.235.refs_0_), channel_id=1, source_target_pairs={{0,2},{2,0},{4,6},{6,4},{1,3},{3,1},{5,7},{7,5},{8,10},{10,8},{12,... | collective-permute-start | bytes 491528 | tf_op jit(solution)/shard_map/ppermute | solution.py:764
  143.5 16.8 %collective-permute-start.49 = (bf16[80,1024]{1,0:T(8,128)(2,1)S(1)}, bf16[80,1024]{1,0:T(8,128)(2,1)S(1)}, u32[]{:S(2)}, u32[]{:S(2)}) collective-permute-start(bf16[80,1024]{1,0:T(8,128)(2,1)S(1)} %collective-permute-done.45.refs_3_), channel_id=1, source_target_pairs={{0,2},{2,0},{4,6},{6,4},{1,3},{3,1},{5,7},{7,5},{8,10},{10,8},{12,... | collective-permute-start | bytes 491528 | tf_op jit(solution)/shard_map/ppermute | solution.py:764
  144.7 15.6 %collective-permute-start.48 = (bf16[80,1024]{1,0:T(8,128)(2,1)S(1)}, bf16[80,1024]{1,0:T(8,128)(2,1)}, u32[]{:S(2)}, u32[]{:S(2)}) collective-permute-start(bf16[80,1024]{1,0:T(8,128)(2,1)S(1)} %collective-permute-done.44.refs_2_), channel_id=1, source_target_pairs={{0,2},{2,0},{4,6},{6,4},{1,3},{3,1},{5,7},{7,5},{8,10},{10,8},{12,... | collective-permute-start | bytes 491528 | tf_op jit(solution)/shard_map/ppermute | solution.py:764
  147.7 12.5 %collective-permute-start.47 = (bf16[80,1024]{1,0:T(8,128)(2,1)S(1)}, bf16[80,1024]{1,0:T(8,128)(2,1)}, u32[]{:S(2)}, u32[]{:S(2)}) collective-permute-start(bf16[80,1024]{1,0:T(8,128)(2,1)S(1)} %collective-permute-done.43.refs_1_), channel_id=1, source_target_pairs={{0,2},{2,0},{4,6},{6,4},{1,3},{3,1},{5,7},{7,5},{8,10},{10,8},{12,... | collective-permute-start | bytes 491528 | tf_op jit(solution)/shard_map/ppermute | solution.py:764
  173.3 9.9 %collective-permute-start.52 = (bf16[160,1024]{1,0:T(8,128)(2,1)S(1)}, bf16[160,1024]{1,0:T(8,128)(2,1)S(1)}, u32[]{:S(2)}, u32[]{:S(2)}) collective-permute-start(bf16[160,1024]{1,0:T(8,128)(2,1)S(1)} %get-tuple-element.245), channel_id=1, source_target_pairs={{0,5},{1,4},{2,7},{3,6},{4,1},{5,0},{6,3},{7,2},{8,13},{9,12},{10,... | collective-permute-start | bytes 983048 | tf_op jit(solution)/shard_map/ppermute | solution.py:776
  175.5 14.7 %collective-permute-start.53 = (bf16[160,1024]{1,0:T(8,128)(2,1)S(1)}, bf16[160,1024]{1,0:T(8,128)(2,1)S(1)}, u32[]{:S(2)}, u32[]{:S(2)}) collective-permute-start(bf16[160,1024]{1,0:T(8,128)(2,1)S(1)} %get-tuple-element.246), channel_id=1, source_target_pairs={{0,4},{2,6},{4,0},{6,2},{1,5},{3,7},{5,1},{7,3},{8,12},{10,14},{12... | collective-permute-start | bytes 983048 | tf_op jit(solution)/shard_map/ppermute | solution.py:767
  175.7 15.2 %collective-permute-start.54 = (bf16[160,1024]{1,0:T(8,128)(2,1)S(1)}, bf16[160,1024]{1,0:T(8,128)(2,1)S(1)}, u32[]{:S(2)}, u32[]{:S(2)}) collective-permute-start(bf16[160,1024]{1,0:T(8,128)(2,1)S(1)} %get-tuple-element.247), channel_id=1, source_target_pairs={{0,1},{1,0},{2,3},{3,2},{4,5},{5,4},{6,7},{7,6},{8,9},{9,8},{10,11... | collective-permute-start | bytes 983048 | tf_op jit(solution)/shard_map/ppermute | solution.py:770
  198.1 109.5 %reduce-scatter.8.cloned.1.call-start = ((), (), s32[]{:S(2)}) async-start(), calls=%async_computation.9 | async-start | bytes 1310720 | tf_op jit(solution)/shard_map/reduce_scatter | solution.py:1014
  200.8 12.3 %collective-permute-start.59 = (bf16[80,1024]{1,0:T(8,128)(2,1)S(1)}, bf16[80,1024]{1,0:T(8,128)(2,1)S(1)}, u32[]{:S(2)}, u32[]{:S(2)}) collective-permute-start(bf16[80,1024]{1,0:T(8,128)(2,1)S(1)} %get-tuple-element.277.refs_0_), channel_id=1, source_target_pairs={{0,2},{2,0},{4,6},{6,4},{1,3},{3,1},{5,7},{7,5},{8,10},{10,8},{12,... | collective-permute-start | bytes 491528 | tf_op jit(solution)/shard_map/ppermute | solution.py:764
  203.4 9.7 %collective-permute-start.62 = (bf16[80,1024]{1,0:T(8,128)(2,1)S(1)}, bf16[80,1024]{1,0:T(8,128)(2,1)S(1)}, u32[]{:S(2)}, u32[]{:S(2)}) collective-permute-start(bf16[80,1024]{1,0:T(8,128)(2,1)S(1)} %collective-permute-done.58.refs_3_), channel_id=1, source_target_pairs={{0,2},{2,0},{4,6},{6,4},{1,3},{3,1},{5,7},{7,5},{8,10},{10,8},{12,... | collective-permute-start | bytes 491528 | tf_op jit(solution)/shard_map/ppermute | solution.py:764
  235.8 78.7 %reduce-scatter.6.cloned.1.call-start = ((), (), s32[]{:S(2)}) async-start(), calls=%async_computation.8 | async-start | bytes 2621440 | tf_op jit(solution)/shard_map/reduce_scatter | solution.py:1014
  273.2 12.3 %collective-permute-start.81 = (bf16[80,1024]{1,0:T(8,128)(2,1)S(1)}, bf16[80,1024]{1,0:T(8,128)(2,1)S(1)}, u32[]{:S(2)}, u32[]{:S(2)}) collective-permute-start(bf16[80,1024]{1,0:T(8,128)(2,1)S(1)} %settle.1.refs_0_), channel_id=1, source_target_pairs={{0,2},{2,0},{4,6},{6,4},{1,3},{3,1},{5,7},{7,5},{8,10},{10,8},{12,... | collective-permute-start | bytes 491528 | tf_op jit(solution)/shard_map/ppermute | solution.py:764
  275.9 9.6 %collective-permute-start.84 = (bf16[80,1024]{1,0:T(8,128)(2,1)S(1)}, bf16[80,1024]{1,0:T(8,128)(2,1)S(1)}, u32[]{:S(2)}, u32[]{:S(2)}) collective-permute-start(bf16[80,1024]{1,0:T(8,128)(2,1)S(1)} %collective-permute-done.80.refs_3_), channel_id=1, source_target_pairs={{0,2},{2,0},{4,6},{6,4},{1,3},{3,1},{5,7},{7,5},{8,10},{10,8},{12,... | collective-permute-start | bytes 491528 | tf_op jit(solution)/shard_map/ppermute | solution.py:764
  289.8 36.8 %collective-permute-start.55 = (f32[80,1024]{1,0:T(8,128)}, f32[80,1024]{1,0:T(8,128)S(1)}, u32[]{:S(2)}, u32[]{:S(2)}) collective-permute-start(f32[80,1024]{1,0:T(8,128)} %get-tuple-element.250.refs_0_), channel_id=1, source_target_pairs={{0,1},{1,0},{2,3},{3,2},{4,5},{5,4},{6,7},{7,6},{8,9},{9,8},{10,11... | collective-permute-start | bytes 983048 | tf_op jit(solution)/shard_map/ppermute | solution.py:770
  294.5 11.6 %collective-permute-start.88 = (bf16[80,1024]{1,0:T(8,128)(2,1)S(1)}, bf16[80,1024]{1,0:T(8,128)(2,1)S(1)}, u32[]{:S(2)}, u32[]{:S(2)}) collective-permute-start(bf16[80,1024]{1,0:T(8,128)(2,1)S(1)} %get-tuple-element.332), channel_id=1, source_target_pairs={{0,1},{1,0},{2,3},{3,2},{4,5},{5,4},{6,7},{7,6},{8,9},{9,8},{10,11... | collective-permute-start | bytes 491528 | tf_op jit(solution)/shard_map/ppermute | solution.py:770
  319.7 31.0 %collective-permute-start.96 = (bf16[256,512]{1,0:T(8,128)(2,1)S(1)}, bf16[256,512]{1,0:T(8,128)(2,1)S(1)}, u32[]{:S(2)}, u32[]{:S(2)}) collective-permute-start(bf16[256,512]{1,0:T(8,128)(2,1)S(1)} %get-tuple-element.354), channel_id=1, source_target_pairs={{0,8},{8,16},{16,24},{24,0},{1,9},{9,17},{17,25},{25,1},{2,10},{10... | collective-permute-start | bytes 786440 | tf_op jit(solution)/shard_map/ppermute | solution.py:779
  322.7 28.6 %collective-permute-start.97 = (bf16[256,512]{1,0:T(8,128)(2,1)S(1)}, bf16[256,512]{1,0:T(8,128)(2,1)S(1)}, u32[]{:S(2)}, u32[]{:S(2)}) collective-permute-start(bf16[256,512]{1,0:T(8,128)(2,1)S(1)} %get-tuple-element.355), channel_id=1, source_target_pairs={{0,16},{8,24},{16,0},{24,8},{1,17},{9,25},{17,1},{25,9},{2,18},{10... | collective-permute-start | bytes 786440 | tf_op jit(solution)/shard_map/ppermute | solution.py:779
  324.3 37.9 %collective-permute-start.93 = (bf16[256,1024]{1,0:T(8,128)(2,1)S(1)}, bf16[256,1024]{1,0:T(8,128)(2,1)S(1)}, u32[]{:S(2)}, u32[]{:S(2)}) collective-permute-start(bf16[256,1024]{1,0:T(8,128)(2,1)S(1)} %get-tuple-element.351.refs_0_), channel_id=1, source_target_pairs={{0,4},{2,6},{4,0},{6,2},{1,5},{3,7},{5,1},{7,3},{8,12},{10,14},{12... | collective-permute-start | bytes 1572872 | tf_op jit(solution)/shard_map/ppermute | solution.py:767
  325.5 36.7 %collective-permute-start.94 = (bf16[256,1024]{1,0:T(8,128)(2,1)S(1)}, bf16[256,1024]{1,0:T(8,128)(2,1)S(1)}, u32[]{:S(2)}, u32[]{:S(2)}) collective-permute-start(bf16[256,1024]{1,0:T(8,128)(2,1)S(1)} %get-tuple-element.352.refs_8_), channel_id=1, source_target_pairs={{0,4},{2,6},{4,0},{6,2},{1,5},{3,7},{5,1},{7,3},{8,12},{10,14},{12... | collective-permute-start | bytes 1572872 | tf_op jit(solution)/shard_map/ppermute | solution.py:767
  326.7 15.4 %collective-permute-start.92 = (f32[14,1024]{1,0:T(8,128)S(1)}, f32[14,1024]{1,0:T(8,128)S(1)}, u32[]{:S(2)}, u32[]{:S(2)}) collective-permute-start(f32[14,1024]{1,0:T(8,128)S(1)} %vector_pack.1.refs_0_), channel_id=1, source_target_pairs={{0,24},{8,0},{16,8},{24,16},{1,25},{9,1},{17,9},{25,17},{2,26},{10... | collective-permute-start | bytes 172040 | tf_op jit(solution)/shard_map/ppermute | solution.py:779
  349.4 12.7 %collective-permute-start.89 = (f32[80,1024]{1,0:T(8,128)}, f32[80,1024]{1,0:T(8,128)S(1)}, u32[]{:S(2)}, u32[]{:S(2)}) collective-permute-start(f32[80,1024]{1,0:T(8,128)} %get-tuple-element.340.refs_0_), channel_id=1, source_target_pairs={{0,1},{1,0},{2,3},{3,2},{4,5},{5,4},{6,7},{7,6},{8,9},{9,8},{10,11... | collective-permute-start | bytes 983048 | tf_op jit(solution)/shard_map/ppermute | solution.py:770
  351.3 10.7 %collective-permute-start.95 = (bf16[256,512]{1,0:T(8,128)(2,1)S(1)}, bf16[256,512]{1,0:T(8,128)(2,1)S(1)}, u32[]{:S(2)}, u32[]{:S(2)}) collective-permute-start(bf16[256,512]{1,0:T(8,128)(2,1)S(1)} %get-tuple-element.353.refs_12_), channel_id=1, source_target_pairs={{0,4},{2,6},{4,0},{6,2},{1,5},{3,7},{5,1},{7,3},{8,12},{10,14},{12... | collective-permute-start | bytes 786440 | tf_op jit(solution)/shard_map/ppermute | solution.py:767
  362.1 11.4 %collective-permute-start.104 = (bf16[256,1024]{1,0:T(8,128)(2,1)S(1)}, bf16[256,1024]{1,0:T(8,128)(2,1)S(1)}, u32[]{:S(2)}, u32[]{:S(2)}) collective-permute-start(bf16[256,1024]{1,0:T(8,128)(2,1)S(1)} %get-tuple-element.351.refs_0_), channel_id=1, source_target_pairs={{0,2},{2,0},{4,6},{6,4},{1,3},{3,1},{5,7},{7,5},{8,10},{10,8},{12,... | collective-permute-start | bytes 1572872 | tf_op jit(solution)/shard_map/ppermute | solution.py:764
  362.3 10.5 %collective-permute-start.102 = (bf16[256,512]{1,0:T(8,128)(2,1)S(1)}, bf16[256,512]{1,0:T(8,128)(2,1)S(1)}, u32[]{:S(2)}, u32[]{:S(2)}) collective-permute-start(bf16[256,512]{1,0:T(8,128)(2,1)S(1)} %shard_sum.1.refs_4_), channel_id=1, source_target_pairs={{0,4},{2,6},{4,0},{6,2},{1,5},{3,7},{5,1},{7,3},{8,12},{10,14},{12... | collective-permute-start | bytes 786440 | tf_op jit(solution)/shard_map/ppermute | solution.py:767
  363.6 9.3 %collective-permute-start.111 = (bf16[256,512]{1,0:T(8,128)(2,1)S(1)}, bf16[256,512]{1,0:T(8,128)(2,1)S(1)}, u32[]{:S(2)}, u32[]{:S(2)}) collective-permute-start(bf16[256,512]{1,0:T(8,128)(2,1)S(1)} %collective-permute-done.95.refs_6_.refs_14_), channel_id=1, source_target_pairs={{0,2},{2,0},{4,6},{6,4},{1,3},{3,1},{5,7},{7,5},{8,10},{10,8},{12,... | collective-permute-start | bytes 786440 | tf_op jit(solution)/shard_map/ppermute | solution.py:764
  370.4 28.3 %collective-permute-start.108 = (bf16[256,1024]{1,0:T(8,128)(2,1)S(1)}, bf16[256,1024]{1,0:T(8,128)(2,1)S(1)}, u32[]{:S(2)}, u32[]{:S(2)}) collective-permute-start(bf16[256,1024]{1,0:T(8,128)(2,1)S(1)} %get-tuple-element.352.refs_8_), channel_id=1, source_target_pairs={{0,2},{2,0},{4,6},{6,4},{1,3},{3,1},{5,7},{7,5},{8,10},{10,8},{12,... | collective-permute-start | bytes 1572872 | tf_op jit(solution)/shard_map/ppermute | solution.py:764
  371.9 26.7 %collective-permute-start.105 = (bf16[256,1024]{1,0:T(8,128)(2,1)S(1)}, bf16[256,1024]{1,0:T(8,128)(2,1)S(1)}, u32[]{:S(2)}, u32[]{:S(2)}) collective-permute-start(bf16[256,1024]{1,0:T(8,128)(2,1)S(1)} %collective-permute-done.93.refs_4_.refs_2_), channel_id=1, source_target_pairs={{0,2},{2,0},{4,6},{6,4},{1,3},{3,1},{5,7},{7,5},{8,10},{10,8},{12,... | collective-permute-start | bytes 1572872 | tf_op jit(solution)/shard_map/ppermute | solution.py:764
  372.9 25.8 %collective-permute-start.109 = (bf16[256,1024]{1,0:T(8,128)(2,1)S(1)}, bf16[256,1024]{1,0:T(8,128)(2,1)S(1)}, u32[]{:S(2)}, u32[]{:S(2)}) collective-permute-start(bf16[256,1024]{1,0:T(8,128)(2,1)S(1)} %collective-permute-done.94.refs_5_.refs_10_), channel_id=1, source_target_pairs={{0,2},{2,0},{4,6},{6,4},{1,3},{3,1},{5,7},{7,5},{8,10},{10,8},{12,... | collective-permute-start | bytes 1572872 | tf_op jit(solution)/shard_map/ppermute | solution.py:764
  373.5 25.2 %collective-permute-start.106 = (bf16[256,512]{1,0:T(8,128)(2,1)S(1)}, bf16[256,512]{1,0:T(8,128)(2,1)S(1)}, u32[]{:S(2)}, u32[]{:S(2)}) collective-permute-start(bf16[256,512]{1,0:T(8,128)(2,1)S(1)} %shard_sum.1.refs_4_), channel_id=1, source_target_pairs={{0,2},{2,0},{4,6},{6,4},{1,3},{3,1},{5,7},{7,5},{8,10},{10,8},{12,... | collective-permute-start | bytes 786440 | tf_op jit(solution)/shard_map/ppermute | solution.py:764
  375.2 23.4 %collective-permute-start.107 = (bf16[256,512]{1,0:T(8,128)(2,1)S(1)}, bf16[256,512]{1,0:T(8,128)(2,1)S(1)}, u32[]{:S(2)}, u32[]{:S(2)}) collective-permute-start(bf16[256,512]{1,0:T(8,128)(2,1)S(1)} %collective-permute-done.102.refs_4_.refs_6_), channel_id=1, source_target_pairs={{0,2},{2,0},{4,6},{6,4},{1,3},{3,1},{5,7},{7,5},{8,10},{10,8},{12,... | collective-permute-start | bytes 786440 | tf_op jit(solution)/shard_map/ppermute | solution.py:764
  (91 other events, 692.5 us)
Sparse Core Ops, SparseCore 0:
  10.2 28.8 all-gather.6
  41.2 43.8 all-gather.8
  86.6 28.3 all-gather.10
  116.4 43.8 all-gather.4
  198.2 41.5 reduce-scatter.3
  242.6 26.8 reduce-scatter.7
  272.3 42.1 reduce-scatter.5

commit v7 on v6

--- a/solution.py
+++ b/solution.py
@@ -527,7 +527,7 @@
 
 
 def attn_grad_kernel(feats, count, first_near, first_far, att_near, att_far, up_near, up_far,
-                     gq_near, gq_far, gk, gv, passed, sums, stream, *refs):
+                     gq_near, gq_far, gk, gv, passed, sums, stream, lines, *refs):
     outs, rest = refs[:count], refs[count:]
     heads_hbm, passed_ref, sums_hbm, stream_hbm, *rest = rest
     first, att, up, packed, sums_ref, *staged, sems = rest
@@ -572,14 +572,18 @@
         for copy in sent:
             copy.wait()
         return
+    (stage,) = staged
     for copy in copies:
         copy.wait()
-    width_own = outs[0].shape[0]
-    for d, out_ref in enumerate(outs):
+    below = lines.shape[1]
+    width_own = outs[0].shape[0] - below
+    for d in reversed(range(count)):
         place = lax.rem(lax.axis_index("fsdp") + d, count)
         span = pl.ds(pl.multiple_of(place * width_own, width_own), width_own)
-        out_ref[:, : 3 * feats] = dot_tn(first[:, span], packed[...]).astype(bf16)
-        out_ref[:, 3 * feats :] = dot_tn(up[:, span], att[...]).astype(bf16)
+        stage[d, :width_own, : 3 * feats] = dot_tn(first[:, span], packed[...]).astype(bf16)
+        stage[d, :width_own, 3 * feats :] = dot_tn(up[:, span], att[...]).astype(bf16)
+        stage[d, width_own:, :] = lines[d]
+        sent += start_copies([(stage.at[d], outs[d])], sems.at[pl.ds(9 + d, 1)])
     for copy in sent:
         copy.wait()
 
@@ -590,38 +594,60 @@
 
 
 def fetch_kernel(count, *refs):
-    sources, targets, (token, sems) = refs[:count], refs[count : 2 * count], refs[2 * count :]
-    token[...] = jnp.zeros_like(token)
-    for copy in start_copies(list(zip(sources, targets)), sems):
-        copy.wait()
-
-
-def shard_sum_kernel(*refs):
-    *terms, out_ref = refs
-    out_ref[...] = sum(term[...].astype(f32) for term in terms).astype(out_ref.dtype)
+    sources, (target, sems) = refs[:count], refs[count:]
+    columns = target.shape[1]
+    moves = []
+    row = 0
+    for source in sources:
+        rows = source.shape[0]
+        for first in range(0, source.shape[1], columns):
+            moves.append(
+                (source.at[:, pl.ds(first, columns)], target.at[pl.ds(row, rows), :])
+            )
+            row += rows
+    for copy in start_copies(moves, sems):
+        copy.wait()
+
+
+def shard_sum_kernel(depth, own_hbm, *refs):
+    *others, part_ref, mine_ref, own, sems = refs
+    (copy,) = start_copies([(own_hbm, own)], sems)
+    copy.wait()
+    rows, width = part_ref.shape[0], mine_ref.shape[1]
+    terms = [ref[...].astype(f32) for ref in (own, *others)]
+    total = terms[0]
+    for term in terms[1:]:
+        total = total + term
+    part_ref[...] = total[:rows, :].astype(bf16)
+    lines = total[rows:, :width] + total[rows:, width:]
+    mine_ref[: 6 * depth, :] = lines[: 6 * depth, :]
+    for k in range(mine_ref.shape[0] - 16):
+        mine_ref[16 + k : 17 + k, :] = lines[6 * depth + k : 6 * depth + k + 1, :]
 
 
 def place_kernel(depth, hidden, feats, *refs):
-    pieces = refs[: 8 * depth]
-    outs, (fc1, fc2, qkv, out, sems) = refs[8 * depth : 8 * depth + 4], refs[8 * depth + 4 :]
-    qkv_hbm, out_hbm, fc1_hbm, fc2_hbm = outs
+    slices = [(refs[k], refs[GROUP + k]) for k in range(GROUP)]
+    qkv_hbm, out_hbm, fc1_hbm, fc2_hbm, fc1, fc2, qkv, out, sems = refs[2 * GROUP :]
     ci = lax.rem(lax.axis_index("ctx"), GROUP)
+    rows = fc1.shape[2]
     copies = []
 
     def send(source, target):
         copies.extend(start_copies([(source, target)], sems.at[pl.ds(len(copies), 1)]))
 
-    for l in reversed(range(depth)):
+    for l in range(depth):
         for k in range(GROUP):
-            piece = pieces[8 * l + k]
+            _, stacked = slices[k]
+            first = 0 if l == 0 else (3 * l - 1) * rows
             span = pl.ds(pl.multiple_of((ci ^ k) * hidden, hidden), hidden)
-            fc1[l, k] = piece[:, :hidden].astype(f32)
+            fc1[l, k] = stacked[first : first + rows, :].astype(f32)
             send(fc1.at[l, k], fc1_hbm.at[l, :, span])
-            fc2[l, k] = piece[:, hidden:].T.astype(f32)
+            fc2[l, k] = stacked[first + rows : first + 2 * rows, :].T.astype(f32)
             send(fc2.at[l, k], fc2_hbm.at[l, span, :])
     for l in reversed(range(depth)):
         for k in range(GROUP):
-            piece = pieces[8 * l + 4 + k]
+            alone, stacked = slices[k]
+            piece = alone if l == 0 else stacked.at[pl.ds((3 * l + 1) * rows, rows), :]
             span = pl.ds(pl.multiple_of((ci ^ k) * feats, feats), feats)
             for j in range(3):
                 qkv[l, k, j] = piece[:, j * feats : (j + 1) * feats].astype(f32)
@@ -632,46 +658,58 @@
         copy.wait()
 
 
-def vector_pack_kernel(depth, *refs):
-    count = 5 * depth
-    out_ref, *terms, sems = refs[count:]
-    copies = start_copies(list(zip(refs[:count], terms)), sems)
+def vector_pack_kernel(depth, one_now, gq_near, gq_far, gv, *refs):
+    count = 5 * depth - 2
+    out_ref, *found, sems = refs[count:]
+    copies = start_copies(list(zip(refs[:count], found)), sems)
     out_ref[...] = jnp.zeros_like(out_ref)
+    feats = gv.shape[1]
+    head_now = [
+        jnp.sum(gq_near[...], axis=0, keepdims=True) + jnp.sum(gq_far[...], axis=0, keepdims=True),
+        jnp.sum(gv[...], axis=0, keepdims=True),
+    ]
     for copy in copies:
         copy.wait()
     for l in range(depth):
-        one, two, unit_near, unit_far, head = terms[5 * l : 5 * l + 5]
+        if l == 0:
+            one, (two, unit_near, unit_far) = one_now, found[:3]
+            heads = head_now
+        else:
+            one, two, unit_near, unit_far, head = found[5 * l - 2 : 5 * l + 3]
+            heads = [head[0:1, :], head[1:2, :]]
         out_ref[6 * l : 6 * l + 1, :] = one[0:1, :]
         out_ref[6 * l + 1 : 6 * l + 2, :] = two[0:1, :]
         out_ref[6 * l + 2 : 6 * l + 3, :] = one[1:2, :]
         out_ref[6 * l + 3 : 6 * l + 6, :] = two[1:4, :]
         units = unit_near.shape[1]
-        feats = head.shape[1]
         row = 6 * depth
         out_ref[row : row + 1, l * units : (l + 1) * units] = unit_near[...] + unit_far[...]
         for j in range(2):
-            first = (2 * l + j) * feats
-            out_ref[row + 1 : row + 2, first : first + feats] = head[j : j + 1, :]
-
-
-def vector_own_kernel(depth, width_own, own, *refs):
-    *others, out_ref, token = refs
-    total = own[...]
-    for other in others:
-        total = total + other[...]
+            start = (2 * l + j) * feats
+            out_ref[row + 1 : row + 2, start : start + feats] = heads[j]
+
+
+def vector_lines_kernel(depth, width_own, packed, lines_ref):
+    count = lines_ref.shape[0]
     f = lax.axis_index("fsdp")
-    count = total.shape[1] // width_own
-    mine = jnp.zeros((6 * depth, width_own), f32)
-    for a in range(count):
-        piece = total[: 6 * depth, a * width_own : (a + 1) * width_own]
-        mine = jnp.where(f == a, piece, mine)
-        for r in range(2):
-            row = 6 * depth + r
-            out_ref[16 + count * r + a : 17 + count * r + a, :] = total[
-                row : row + 1, a * width_own : (a + 1) * width_own
-            ]
-    out_ref[: 6 * depth, :] = mine
-    token[...] = jnp.zeros_like(token)
+    total = packed[...]
+    high = total.astype(bf16).astype(f32)
+    low = total - high
+    lines_ref[...] = jnp.zeros_like(lines_ref)
+    last = 6 * depth
+    for k, value in enumerate((high, low)):
+        lanes = slice(k * width_own, (k + 1) * width_own)
+        columns = [value[:, a * width_own : (a + 1) * width_own] for a in range(count)]
+        for d in range(count):
+            mine = columns[0]
+            for a in range(1, count):
+                mine = jnp.where(lax.rem(f + d, count) == a, columns[a], mine)
+            rows = [mine[:last, :]]
+            for r in range(2):
+                for a in range(count):
+                    rows.append(columns[a][last + r : last + r + 1, :])
+            rows.append(jnp.zeros((lines_ref.shape[1] - last - 2 * count, width_own), f32))
+            lines_ref[d, :, lanes] = jnp.concatenate(rows, axis=0).astype(bf16)
 
 
 def vector_plane_kernel(depth, own, xy, x, y, out_ref):
@@ -1190,24 +1228,36 @@
             name="norm_back_one",
             scratch=[pltpu.VMEM((rows, width), f32)] * 2 + [DMA((2,))],
         )
-        after = ()
+        lines = ()
         if l == 0:
-            early = [(k, kind) for k in range(depth) for kind in (0, 1) if (k, kind) != (0, 1)]
-            sources = [(mlp_parts, attn_parts)[kind][k] for k, kind in early]
-            *fetched, token = kernel_call(
-                functools.partial(fetch_kernel, len(early)),
-                [(v.shape, v.dtype) for v in sources] + [TOKEN],
-                *[Far(v) for v in sources],
-                name="fetch",
-                after=(sums_one,),
-                scratch=[DMA((len(early),))],
+            terms = [sums_two, *unit_sums[0]]
+            for k in range(1, depth):
+                terms += [*row_sums[k], *unit_sums[k], head_sums[k]]
+            packed = kernel_call(
+                functools.partial(vector_pack_kernel, depth),
+                [((6 * depth + 2, width), f32)],
+                sums_one,
+                *grad_q,
+                grad_v,
+                *[Far(v) for v in terms],
+                name="vector_pack",
+                scratch=[pltpu.VMEM(v.shape, f32) for v in terms] + [DMA((len(terms),))],
+            )[0]
+            if outer > 1:
+                packed = lax.psum(packed, "ctx", axis_index_groups=outer_groups)
+            lines = kernel_call(
+                functools.partial(vector_lines_kernel, depth, width_own),
+                [((fsdp, 32, 2 * width_own), bf16)],
+                packed,
+                name="vector_lines",
             )
-            after = (token,)
         count = 1 if l > 0 else fsdp
         shapes = [((width, 3 * feats), bf16), ((width, feats), bf16)]
+        if l == 0:
+            shapes = [((fsdp, width_own + 32, 4 * feats), bf16)]
         *attn_grads, head_sums[l], upstream_b, sums_one, upstream = kernel_call(
             functools.partial(attn_grad_kernel, feats, count),
-            [saved((width, 4 * feats), bf16) if l > 0 else ((width_own, 4 * feats), bf16)] * count
+            [saved((width if l > 0 else width_own + 32, 4 * feats), bf16)] * count
             + [
                 saved((2, feats), f32),
                 row_bf16,
@@ -1225,8 +1275,8 @@
             upstream_b,
             sums_one,
             upstream,
+            *(lines or (sums_one,)),
             name="attn_grad",
-            after=after,
             scratch=[
                 pltpu.VMEM((all_rows, width), bf16),
                 pltpu.VMEM((all_rows, feats), bf16),
@@ -1234,51 +1284,46 @@
                 pltpu.VMEM((all_rows, 3 * feats), bf16),
                 pltpu.VMEM((2, feats), f32),
             ]
-            + [pltpu.VMEM(*shape) for shape in shapes if count == 1]
-            + [DMA((9,))],
+            + [pltpu.VMEM(*shape) for shape in shapes]
+            + [DMA((9 + count,))],
         )
         if l > 0:
             attn_parts[l] = scatter_grads(attn_grads[0])
             upstream_chunks = gather_rows(upstream_b)
         row_sums[l] = (sums_one, sums_two)
 
-    parts = dict(zip(early, fetched))
-    vector_rows = 6 * depth + 2
-    terms = [v for l in range(depth) for v in (*row_sums[l], *unit_sums[l], head_sums[l])]
-    packed = kernel_call(
-        functools.partial(vector_pack_kernel, depth),
-        [((vector_rows, width), f32)],
-        *[Far(v) for v in terms],
-        name="vector_pack",
-        scratch=[pltpu.VMEM(v.shape, f32) for v in terms] + [DMA((len(terms),))],
-    )[0]
-    if outer > 1:
-        packed = lax.psum(packed, "ctx", axis_index_groups=outer_groups)
-    last_terms = (attn_grads[0], *[shift_z(attn_grads[d], d) for d in range(1, fsdp)])
-    crossed = {key: swap_x(parts[key]) for key in early}
+    sources = [mlp_parts[0]]
+    for l in range(1, depth):
+        sources += [mlp_parts[l], attn_parts[l]]
+    blocks = 3 * depth - 1
+    (stacked,) = kernel_call(
+        functools.partial(fetch_kernel, len(sources)),
+        [((blocks * width_own, hidden), bf16)],
+        *[Far(v) for v in sources],
+        name="fetch",
+        after=(upstream_b,),
+        scratch=[DMA((blocks,))],
+    )
+    own_term, *other_terms = attn_grads
+    other_terms = [shift_z(term, d + 1) for d, term in enumerate(other_terms)]
+    crossed = swap_x(stacked)
     others = (swap_y(upstream), swap_y(outputs_own))
-    mine, hub_token = kernel_call(
-        functools.partial(vector_own_kernel, depth, width_own),
-        [((24, width_own), f32), TOKEN],
-        packed,
-        *[shift_z(packed, d) for d in range(1, fsdp)],
-        name="vector_own",
-        after=(*crossed.values(), *others, *last_terms[1:]),
-    )
-    part = kernel_call(
-        shard_sum_kernel,
-        [((width_own, 4 * feats), bf16)],
-        *last_terms,
+    part, mine = kernel_call(
+        functools.partial(shard_sum_kernel, depth),
+        [((width_own, 4 * feats), bf16), ((24, width_own), f32)],
+        Far(own_term),
+        *other_terms,
         name="shard_sum",
-        after=(hub_token,),
-    )[0]
+        after=(crossed, *others),
+        scratch=[pltpu.VMEM(own_term.shape, bf16), DMA((1,))],
+    )
     if outer > 1:
         part = lax.psum(part, "ctx", axis_index_groups=outer_groups)
-    parts[0, 1], crossed[0, 1] = part, swap_x(part)
-    pieces = {
-        key: (parts[key], swap_core(parts[key]), crossed[key], swap_core(crossed[key]))
-        for key in parts
-    }
+    part_crossed = swap_x(part)
+    pieces = [
+        *(part, swap_core(part), part_crossed, swap_core(part_crossed)),
+        *(stacked, swap_core(stacked), crossed, swap_core(crossed)),
+    ]
     mine = kernel_call(
         functools.partial(vector_plane_kernel, depth),
         [((32, width_own), f32)],
@@ -1287,7 +1332,7 @@
         swap_x(mine),
         swap_y(mine),
         name="vector_plane",
-        after=(crossed[0, 1],),
+        after=(part_crossed,),
     )[0]
     grad_gains, grad_shifts, grad_fc1_bias, grad_qv_bias = kernel_call(
         functools.partial(vector_place_kernel, depth, head_dim),
@@ -1305,7 +1350,7 @@
         kernel_call(
             place_rows_kernel,
             [saved(inputs.shape, f32)],
-            Far(own),
+            own,
             other,
             name="place_rows",
             scratch=[DMA((2,))],
@@ -1315,7 +1360,7 @@
     placed = kernel_call(
         functools.partial(place_kernel, depth, hidden, feats),
         [saved(v.shape, f32) for v in (w_qkv, w_out, w_fc1, w_fc2)],
-        *[piece for l in range(depth) for kind in (0, 1) for piece in pieces[l, kind]],
+        *pieces,
         name="place",
         limit=24,
         scratch=[

time: 417 us -> 422 us (1.012)
  waiting for transfers between devices: 141 us -> 168 us
  Pallas kernels: 124 us -> 103 us
    ppermute x20 -> x18, waiting for transfers between devices: 32.2 us -> 62.9 us  [swap_x(): return lax.ppermute(value, 'ctx', [(i, i ^ 2) for i in range(ctx)])]
    pallas_call x60, Pallas kernels: 124 us -> 103 us  [kernel_call(): pl.pallas_call(run, out_shape=out_shape, in_specs=specs, out_specs=out_sp...]
    ppermute x9 -> x6, waiting for transfers between devices: 26.1 us -> 18.6 us  [shift_z(): lax.ppermute(value, 'fsdp', [(i, (i + d) % fsdp) for i in range(fsdp)])]
    ppermute x9 -> x6, starting transfers between devices: 9.18 us -> 11.3 us  [shift_z(): lax.ppermute(value, 'fsdp', [(i, (i + d) % fsdp) for i in range(fsdp)])]
    ppermute x49 -> x45, starting transfers between devices: 62.8 us -> 61.3 us  [swap_core(): return lax.ppermute(value, 'ctx', [(i, i ^ 1) for i in range(ctx)])]
    ppermute x20 -> x18, starting transfers between devices: 15.7 us -> 15.3 us  [swap_x(): return lax.ppermute(value, 'ctx', [(i, i ^ 2) for i in range(ctx)])]
  transfers between devices with their start and end apart: 119 -> 110, of which waited for: 50 -> 52; matrix products, arithmetic and copies ran while one was open for 1% -> 0% of each run, Pallas kernels for 25% -> 20%
where the time goes in v7:
time: 422 us; the launch traced here: 416 us
  waiting for transfers between devices  168 us (40%)
  starting transfers between devices  123 us (29%)
  Pallas kernels  103 us (24%)
  between operations  15.5 us (4%)
  local copies, waits for them, and re-layouts  7.12 us (2%)
    pallas_call x60, Pallas kernels, kernel_call(): pl.pallas_call(run, out_shape=out_shape, in_specs=specs, out_specs=out_sp...  103 us
    ppermute x18, waiting for transfers between devices, swap_x(): return lax.ppermute(value, 'ctx', [(i, i ^ 2) for i in range(ctx)])  62.9 us
    ppermute x45, starting transfers between devices, swap_core(): return lax.ppermute(value, 'ctx', [(i, i ^ 1) for i in range(ctx)])  61.3 us
    ppermute x16, waiting for transfers between devices, swap_xy(): return lax.ppermute(value, ('ctx', 'tp'), pairs)  38.8 us
    ppermute x16, starting transfers between devices, swap_xy(): return lax.ppermute(value, ('ctx', 'tp'), pairs)  19.2 us
    ppermute x18, waiting for transfers between devices, swap_y(): return lax.ppermute(value, 'tp', [(i, i ^ 1) for i in range(tp)])  18.9 us
    ppermute x6, waiting for transfers between devices, shift_z(): lax.ppermute(value, 'fsdp', [(i, (i + d) % fsdp) for i in range(fsdp)])  18.6 us
    all_gather x2, waiting for transfers between devices, per_device(): mlp_w.append(lax.all_gather(own, 'fsdp', axis=0, tiled=True))  17.9 us
  transfers between devices with their start and end apart: 110, of which 52 were waited for; matrix products, arithmetic and copies ran while one was open for 0% of the time, Pallas kernels for 20%

profile of v7, /device:TPU:9, one launch (start us, length us, event | category | flops | bytes accessed | tf_op | source)
XLA Modules:
  0.0 416.4 jit_solution(13427918506907632422)
XLA Ops:
  45.9 3.4 attn.5
  51.7 2.6 attn.4
  57.2 3.5 collective-permute-done.18.refs_1_
  60.8 3.8 collective-permute-done.19.refs_2_
  73.0 2.5 collective-permute-start.26
  78.7 6.3 %all-gather.9.cloned.1.call-done.refs_4_ = bf16[1024,1024]{1,0:T(8,128)(2,1)} async-done(((bf16[256,1024]{1,0:T(8,128)(2,1)}), bf16[1024,1024]{1,0:T(8,128)(2,1)}) %all-gather.9.cloned.1.call-update) | async-done | bytes 2097168 | tf_op jit(solution)/shard_map/all_gather | solution.py:879
  94.1 3.6 collective-permute-done.29.refs_1_
  97.7 3.5 collective-permute-done.30.refs_2_
  110.0 2.3 collective-permute-start.37
  118.9 2.6 attn.7
  122.4 2.6 attn.6
  127.9 4.2 %collective-permute-done.40.refs_1_ = bf16[80,1024]{1,0:T(8,128)(2,1)S(1)} collective-permute-done((bf16[80,1024]{1,0:T(8,128)(2,1)S(1)}, bf16[80,1024]{1,0:T(8,128)(2,1)S(1)}, u32[]{:S(2)}, u32[]{:S(2)}) %collective-permute-start.40) | collective-permute-done | bytes 163872 | tf_op jit(solution)/shard_map/ppermute | solution.py:814
  132.1 3.4 collective-permute-done.41.refs_2_
  143.8 2.3 collective-permute-start.48
  148.5 11.6 %all-gather.5.cloned.1.call-done.refs_4_.refs_1_ = bf16[1024,1024]{1,0:T(8,128)(2,1)} async-done(((bf16[256,1024]{1,0:T(8,128)(2,1)}), bf16[1024,1024]{1,0:T(8,128)(2,1)}) %all-gather.5.cloned.1.call-update) | async-done | bytes 2097168 | tf_op jit(solution)/shard_map/all_gather | solution.py:879
  161.7 2.7 mlp.7
  164.4 3.3 mlp_back.5
  170.0 2.9 mlp_back.4
  175.9 7.1 %collective-permute-done.52.refs_1_ = bf16[160,1024]{1,0:T(8,128)(2,1)S(1)} collective-permute-done((bf16[160,1024]{1,0:T(8,128)(2,1)S(1)}, bf16[160,1024]{1,0:T(8,128)(2,1)S(1)}, u32[]{:S(2)}, u32[]{:S(2)}) %collective-permute-start.52) | collective-permute-done | bytes 327712 | tf_op jit(solution)/shard_map/ppermute | solution.py:814
  183.1 7.1 %collective-permute-done.53.refs_2_ = bf16[160,1024]{1,0:T(8,128)(2,1)S(1)} collective-permute-done((bf16[160,1024]{1,0:T(8,128)(2,1)S(1)}, bf16[160,1024]{1,0:T(8,128)(2,1)S(1)}, u32[]{:S(2)}, u32[]{:S(2)}) %collective-permute-start.53) | collective-permute-done | bytes 327712 | tf_op jit(solution)/shard_map/ppermute | solution.py:805
  194.1 3.8 mlp_grad.2
  204.9 2.3 collective-permute-start.61
  209.4 3.6 attn_back.4
  213.1 3.6 attn_back.5
  222.3 3.9 collective-permute-done.64.refs_1_
  226.2 3.7 collective-permute-done.65.refs_2_
  231.7 4.0 attn_grad.2
  242.6 2.3 collective-permute-start.72
  248.3 2.5 mlp_back.7
  251.2 2.5 mlp_back.6
  256.6 3.9 collective-permute-done.75.refs_1_
  260.5 3.7 collective-permute-done.76.refs_2_
  266.1 4.3 %mlp_grad.3 = (bf16[1024,1024]{1,0:T(8,128)(2,1)}, bf16[80,1024]{1,0:T(8,128)(2,1)S(1)}, f32[4,1024]{1,0:T(4,128)}, f32[80,1024]{1,0:T(8,128)}) custom-call(bf16[320,1024]{1,0:T(8,128)(2,1)} %get-tuple-element.250.refs_0_, bf16[320,1024]{1,0:T(8,128)(2,1)} %get-tuple-element.251.refs_1_, bf16[320,512]{1,0:T(8,128)(2,1)} %get-tuple-element.252.refs_2_, ...), custom_call_target="tpu_custom_call" | custom-call | tf_op jit(solution)/shard_map/mlp_grad/pallas_call | solution.py:79
  277.1 2.3 collective-permute-start.83
  281.8 3.6 attn_back.6
  285.5 3.6 attn_back.7
  294.7 3.9 collective-permute-done.86.refs_1_
  298.6 3.7 collective-permute-done.87.refs_2_
  305.0 3.9 attn_grad.3
  309.1 5.4 %reduce-scatter.6.cloned.1.call-done.refs_0_ = bf16[256,1024]{1,0:T(8,128)(2,1)} async-done(((bf16[1024,1024]{1,0:T(8,128)(2,1)}), bf16[256,1024]{1,0:T(8,128)(2,1)}) %reduce-scatter.6.cloned.1.call-update) | async-done | bytes 524304 | tf_op jit(solution)/shard_map/reduce_scatter | solution.py:1052
  318.1 27.2 %collective-permute-done.93.refs_4_.refs_6_ = bf16[1280,512]{1,0:T(8,128)(2,1)S(1)} collective-permute-done((bf16[1280,512]{1,0:T(8,128)(2,1)S(1)}, bf16[1280,512]{1,0:T(8,128)(2,1)S(1)}, u32[]{:S(2)}, u32[]{:S(2)}) %collective-permute-start.93) | collective-permute-done | bytes 1310752 | tf_op jit(solution)/shard_map/ppermute | solution.py:805
  348.3 3.0 collective-permute-start.90
  351.5 4.9 %collective-permute-done.55.refs_1_.refs_6_ = f32[80,1024]{1,0:T(8,128)S(1)} collective-permute-done((f32[80,1024]{1,0:T(8,128)S(1)}, f32[80,1024]{1,0:T(8,128)S(1)}, u32[]{:S(2)}, u32[]{:S(2)}) %collective-permute-start.55) | collective-permute-done | bytes 327712 | tf_op jit(solution)/shard_map/ppermute | solution.py:808
  356.4 2.9 collective-permute-start.91
  360.9 16.7 %collective-permute-done.91.refs_2_ = bf16[288,512]{1,0:T(8,128)(2,1)S(1)} collective-permute-done((bf16[288,512]{1,0:T(8,128)(2,1)S(1)}, bf16[288,512]{1,0:T(8,128)(2,1)S(1)}, u32[]{:S(2)}, u32[]{:S(2)}) %collective-permute-start.91) | collective-permute-done | bytes 294944 | tf_op jit(solution)/shard_map/ppermute | solution.py:817
  382.6 5.4 %collective-permute-done.97.refs_4_.refs_2_ = bf16[256,512]{1,0:T(8,128)(2,1)S(1)} collective-permute-done((bf16[256,512]{1,0:T(8,128)(2,1)S(1)}, bf16[256,512]{1,0:T(8,128)(2,1)S(1)}, u32[]{:S(2)}, u32[]{:S(2)}) %collective-permute-start.97) | collective-permute-done | bytes 262176 | tf_op jit(solution)/shard_map/ppermute | solution.py:805
  398.3 3.5 collective-permute-start.98
  404.4 4.9 %place.1 = (f32[2,3,256,512]{3,2,1,0:T(8,128)}, f32[2,512,256]{2,1,0:T(8,128)}, f32[2,256,2048]{2,1,0:T(8,128)}, f32[2,2048,256]{2,1,0:T(8,128)}) custom-call(bf16[256,512]{1,0:T(8,128)(2,1)S(1)} %get-tuple-element.349.refs_0_, bf16[256,512]{1,0:T(8,128)(2,1)S(1)} %collective-permute-done.99.refs_1_, ...), custom_call_target="tpu_custom_call" | custom-call | tf_op jit(solution)/shard_map/place/pallas_call | solution.py:79
  (311 shorter events, 180.5 us)
Async XLA Ops:
  7.2 34.2 %all-gather.7.cloned.1.call-start = ((), (), s32[]{:S(2)}) async-start(), calls=%async_computation.4 | async-start | bytes 1310720 | tf_op jit(solution)/shard_map/all_gather | solution.py:877
  9.0 76.0 %all-gather.9.cloned.1.call-start = ((), (), s32[]{:S(2)}) async-start(), calls=%async_computation.5 | async-start | bytes 2621440 | tf_op jit(solution)/shard_map/all_gather | solution.py:879
  11.2 103.7 %all-gather.11.cloned.1.call-start = ((), (), s32[]{:S(2)}) async-start(), calls=%async_computation.6 | async-start | bytes 1310720 | tf_op jit(solution)/shard_map/all_gather | solution.py:877
  11.4 10.9 %collective-permute-start.9 = (bf16[17,256]{1,0:T(8,128)(2,1)S(1)}, bf16[17,256]{1,0:T(8,128)(2,1)S(1)}, u32[]{:S(2)}, u32[]{:S(2)}) collective-permute-start(bf16[17,256]{1,0:T(8,128)(2,1)S(1)} %fusion.1), channel_id=1, source_target_pairs={{0,8},{8,16},{16,24},{24,0},{1,9},{9,17},{17,25},{25,1},{2,10},{10... | collective-permute-start | bytes 26120 | tf_op jit(solution)/shard_map/ppermute | solution.py:817
  12.8 10.8 %collective-permute-start.8 = (bf16[17,256]{1,0:T(8,128)(2,1)S(1)}, bf16[17,256]{1,0:T(8,128)(2,1)S(1)}, u32[]{:S(2)}, u32[]{:S(2)}) collective-permute-start(bf16[17,256]{1,0:T(8,128)(2,1)S(1)} %fusion.1), channel_id=1, source_target_pairs={{0,16},{8,24},{16,0},{24,8},{1,17},{9,25},{17,1},{25,9},{2,18},{10... | collective-permute-start | bytes 26120 | tf_op jit(solution)/shard_map/ppermute | solution.py:817
  13.9 10.0 %collective-permute-start.7 = (bf16[17,256]{1,0:T(8,128)(2,1)S(1)}, bf16[17,256]{1,0:T(8,128)(2,1)S(1)}, u32[]{:S(2)}, u32[]{:S(2)}) collective-permute-start(bf16[17,256]{1,0:T(8,128)(2,1)S(1)} %fusion.1), channel_id=1, source_target_pairs={{0,24},{8,0},{16,8},{24,16},{1,25},{9,1},{17,9},{25,17},{2,26},{10... | collective-permute-start | bytes 26120 | tf_op jit(solution)/shard_map/ppermute | solution.py:817
  17.6 9.2 %collective-permute-start.3 = (bf16[80,1024]{1,0:T(8,128)(2,1)S(1)}, bf16[80,1024]{1,0:T(8,128)(2,1)S(1)}, u32[]{:S(2)}, u32[]{:S(2)}) collective-permute-start(bf16[80,1024]{1,0:T(8,128)(2,1)S(1)} %get-tuple-element.186.refs_0_), channel_id=1, source_target_pairs={{0,2},{2,0},{4,6},{6,4},{1,3},{3,1},{5,7},{7,5},{8,10},{10,8},{12,... | collective-permute-start | bytes 491528 | tf_op jit(solution)/shard_map/ppermute | solution.py:802
  19.1 8.9 %collective-permute-start.2 = (bf16[80,1024]{1,0:T(8,128)(2,1)S(1)}, bf16[80,1024]{1,0:T(8,128)(2,1)S(1)}, u32[]{:S(2)}, u32[]{:S(2)}) collective-permute-start(bf16[80,1024]{1,0:T(8,128)(2,1)S(1)} %get-tuple-element.186.refs_0_), channel_id=1, source_target_pairs={{0,1},{1,0},{2,3},{3,2},{4,5},{5,4},{6,7},{7,6},{8,9},{9,8},{10,11... | collective-permute-start | bytes 491528 | tf_op jit(solution)/shard_map/ppermute | solution.py:808
  22.2 137.9 %all-gather.5.cloned.1.call-start = ((), (), s32[]{:S(2)}) async-start(), calls=%async_computation.3 | async-start | bytes 2621440 | tf_op jit(solution)/shard_map/all_gather | solution.py:879
  25.5 9.0 %collective-permute-start.12 = (bf16[80,1024]{1,0:T(8,128)(2,1)S(1)}, bf16[80,1024]{1,0:T(8,128)(2,1)S(1)}, u32[]{:S(2)}, u32[]{:S(2)}) collective-permute-start(bf16[80,1024]{1,0:T(8,128)(2,1)S(1)} %get-tuple-element.190.refs_0_), channel_id=1, source_target_pairs={{0,1},{1,0},{2,3},{3,2},{4,5},{5,4},{6,7},{7,6},{8,9},{9,8},{10,11... | collective-permute-start | bytes 491528 | tf_op jit(solution)/shard_map/ppermute | solution.py:808
  26.8 8.8 %collective-permute-start.11 = (bf16[80,1024]{1,0:T(8,128)(2,1)S(1)}, bf16[80,1024]{1,0:T(8,128)(2,1)S(1)}, u32[]{:S(2)}, u32[]{:S(2)}) collective-permute-start(bf16[80,1024]{1,0:T(8,128)(2,1)S(1)} %get-tuple-element.190.refs_0_), channel_id=1, source_target_pairs={{0,4},{2,6},{4,0},{6,2},{1,5},{3,7},{5,1},{7,3},{8,12},{10,14},{12... | collective-permute-start | bytes 491528 | tf_op jit(solution)/shard_map/ppermute | solution.py:805
  28.0 10.5 %collective-permute-start.10 = (bf16[80,1024]{1,0:T(8,128)(2,1)S(1)}, bf16[80,1024]{1,0:T(8,128)(2,1)}, u32[]{:S(2)}, u32[]{:S(2)}) collective-permute-start(bf16[80,1024]{1,0:T(8,128)(2,1)S(1)} %get-tuple-element.190.refs_0_), channel_id=1, source_target_pairs={{0,5},{1,4},{2,7},{3,6},{4,1},{5,0},{6,3},{7,2},{8,13},{9,12},{10,... | collective-permute-start | bytes 491528 | tf_op jit(solution)/shard_map/ppermute | solution.py:814
  28.2 11.4 %collective-permute-start.6 = (bf16[80,1024]{1,0:T(8,128)(2,1)S(1)}, bf16[80,1024]{1,0:T(8,128)(2,1)S(1)}, u32[]{:S(2)}, u32[]{:S(2)}) collective-permute-start(bf16[80,1024]{1,0:T(8,128)(2,1)S(1)} %collective-permute-done.2.refs_3_), channel_id=1, source_target_pairs={{0,2},{2,0},{4,6},{6,4},{1,3},{3,1},{5,7},{7,5},{8,10},{10,8},{12,... | collective-permute-start | bytes 491528 | tf_op jit(solution)/shard_map/ppermute | solution.py:802
  31.3 8.3 %collective-permute-start.5 = (bf16[80,1024]{1,0:T(8,128)(2,1)S(1)}, bf16[80,1024]{1,0:T(8,128)(2,1)S(1)}, u32[]{:S(2)}, u32[]{:S(2)}) collective-permute-start(bf16[80,1024]{1,0:T(8,128)(2,1)S(1)} %collective-permute-done.1.refs_2_), channel_id=1, source_target_pairs={{0,2},{2,0},{4,6},{6,4},{1,3},{3,1},{5,7},{7,5},{8,10},{10,8},{12,... | collective-permute-start | bytes 491528 | tf_op jit(solution)/shard_map/ppermute | solution.py:802
  34.5 9.7 %collective-permute-start.13 = (bf16[80,1024]{1,0:T(8,128)(2,1)S(1)}, bf16[80,1024]{1,0:T(8,128)(2,1)}, u32[]{:S(2)}, u32[]{:S(2)}) collective-permute-start(bf16[80,1024]{1,0:T(8,128)(2,1)S(1)} %get-tuple-element.190.refs_0_), channel_id=1, source_target_pairs={{0,2},{2,0},{4,6},{6,4},{1,3},{3,1},{5,7},{7,5},{8,10},{10,8},{12,... | collective-permute-start | bytes 491528 | tf_op jit(solution)/shard_map/ppermute | solution.py:802
  51.5 218.9 %reduce-scatter.4.cloned.1.call-start = ((), (), s32[]{:S(2)}) async-start(), calls=%async_computation.7 | async-start | bytes 2621440 | tf_op jit(solution)/shard_map/reduce_scatter | solution.py:1052
  69.0 8.7 %collective-permute-start.24 = (bf16[80,1024]{1,0:T(8,128)(2,1)S(1)}, bf16[80,1024]{1,0:T(8,128)(2,1)S(1)}, u32[]{:S(2)}, u32[]{:S(2)}) collective-permute-start(bf16[80,1024]{1,0:T(8,128)(2,1)S(1)} %get-tuple-element.206.refs_0_), channel_id=1, source_target_pairs={{0,2},{2,0},{4,6},{6,4},{1,3},{3,1},{5,7},{7,5},{8,10},{10,8},{12,... | collective-permute-start | bytes 491528 | tf_op jit(solution)/shard_map/ppermute | solution.py:802
  93.8 8.2 %collective-permute-start.31 = (bf16[80,1024]{1,0:T(8,128)(2,1)S(1)}, bf16[80,1024]{1,0:T(8,128)(2,1)S(1)}, u32[]{:S(2)}, u32[]{:S(2)}) collective-permute-start(bf16[80,1024]{1,0:T(8,128)(2,1)S(1)} %get-tuple-element.214), channel_id=1, source_target_pairs={{0,1},{1,0},{2,3},{3,2},{4,5},{5,4},{6,7},{7,6},{8,9},{9,8},{10,11... | collective-permute-start | bytes 491528 | tf_op jit(solution)/shard_map/ppermute | solution.py:808
  105.9 10.6 %collective-permute-start.35 = (bf16[80,1024]{1,0:T(8,128)(2,1)S(1)}, bf16[80,1024]{1,0:T(8,128)(2,1)S(1)}, u32[]{:S(2)}, u32[]{:S(2)}) collective-permute-start(bf16[80,1024]{1,0:T(8,128)(2,1)S(1)} %get-tuple-element.216.refs_0_), channel_id=1, source_target_pairs={{0,2},{2,0},{4,6},{6,4},{1,3},{3,1},{5,7},{7,5},{8,10},{10,8},{12,... | collective-permute-start | bytes 491528 | tf_op jit(solution)/shard_map/ppermute | solution.py:802
  127.6 8.3 %collective-permute-start.42 = (bf16[80,1024]{1,0:T(8,128)(2,1)S(1)}, bf16[80,1024]{1,0:T(8,128)(2,1)S(1)}, u32[]{:S(2)}, u32[]{:S(2)}) collective-permute-start(bf16[80,1024]{1,0:T(8,128)(2,1)S(1)} %get-tuple-element.228), channel_id=1, source_target_pairs={{0,1},{1,0},{2,3},{3,2},{4,5},{5,4},{6,7},{7,6},{8,9},{9,8},{10,11... | collective-permute-start | bytes 491528 | tf_op jit(solution)/shard_map/ppermute | solution.py:808
  139.8 20.3 %collective-permute-start.46 = (bf16[80,1024]{1,0:T(8,128)(2,1)S(1)}, bf16[80,1024]{1,0:T(8,128)(2,1)S(1)}, u32[]{:S(2)}, u32[]{:S(2)}) collective-permute-start(bf16[80,1024]{1,0:T(8,128)(2,1)S(1)} %get-tuple-element.230.refs_0_), channel_id=1, source_target_pairs={{0,2},{2,0},{4,6},{6,4},{1,3},{3,1},{5,7},{7,5},{8,10},{10,8},{12,... | collective-permute-start | bytes 491528 | tf_op jit(solution)/shard_map/ppermute | solution.py:802
  142.6 17.5 %collective-permute-start.49 = (bf16[80,1024]{1,0:T(8,128)(2,1)S(1)}, bf16[80,1024]{1,0:T(8,128)(2,1)}, u32[]{:S(2)}, u32[]{:S(2)}) collective-permute-start(bf16[80,1024]{1,0:T(8,128)(2,1)S(1)} %collective-permute-done.45.refs_3_), channel_id=1, source_target_pairs={{0,2},{2,0},{4,6},{6,4},{1,3},{3,1},{5,7},{7,5},{8,10},{10,8},{12,... | collective-permute-start | bytes 491528 | tf_op jit(solution)/shard_map/ppermute | solution.py:802
  143.8 16.3 %collective-permute-start.48 = (bf16[80,1024]{1,0:T(8,128)(2,1)S(1)}, bf16[80,1024]{1,0:T(8,128)(2,1)}, u32[]{:S(2)}, u32[]{:S(2)}) collective-permute-start(bf16[80,1024]{1,0:T(8,128)(2,1)S(1)} %collective-permute-done.44.refs_2_), channel_id=1, source_target_pairs={{0,2},{2,0},{4,6},{6,4},{1,3},{3,1},{5,7},{7,5},{8,10},{10,8},{12,... | collective-permute-start | bytes 491528 | tf_op jit(solution)/shard_map/ppermute | solution.py:802
  146.9 13.2 %collective-permute-start.47 = (bf16[80,1024]{1,0:T(8,128)(2,1)S(1)}, bf16[80,1024]{1,0:T(8,128)(2,1)}, u32[]{:S(2)}, u32[]{:S(2)}) collective-permute-start(bf16[80,1024]{1,0:T(8,128)(2,1)S(1)} %collective-permute-done.43.refs_1_), channel_id=1, source_target_pairs={{0,2},{2,0},{4,6},{6,4},{1,3},{3,1},{5,7},{7,5},{8,10},{10,8},{12,... | collective-permute-start | bytes 491528 | tf_op jit(solution)/shard_map/ppermute | solution.py:802
  173.2 9.9 %collective-permute-start.52 = (bf16[160,1024]{1,0:T(8,128)(2,1)S(1)}, bf16[160,1024]{1,0:T(8,128)(2,1)S(1)}, u32[]{:S(2)}, u32[]{:S(2)}) collective-permute-start(bf16[160,1024]{1,0:T(8,128)(2,1)S(1)} %get-tuple-element.240), channel_id=1, source_target_pairs={{0,5},{1,4},{2,7},{3,6},{4,1},{5,0},{6,3},{7,2},{8,13},{9,12},{10,... | collective-permute-start | bytes 983048 | tf_op jit(solution)/shard_map/ppermute | solution.py:814
  175.4 14.7 %collective-permute-start.53 = (bf16[160,1024]{1,0:T(8,128)(2,1)S(1)}, bf16[160,1024]{1,0:T(8,128)(2,1)S(1)}, u32[]{:S(2)}, u32[]{:S(2)}) collective-permute-start(bf16[160,1024]{1,0:T(8,128)(2,1)S(1)} %get-tuple-element.241), channel_id=1, source_target_pairs={{0,4},{2,6},{4,0},{6,2},{1,5},{3,7},{5,1},{7,3},{8,12},{10,14},{12... | collective-permute-start | bytes 983048 | tf_op jit(solution)/shard_map/ppermute | solution.py:805
  175.7 15.2 %collective-permute-start.54 = (bf16[160,1024]{1,0:T(8,128)(2,1)S(1)}, bf16[160,1024]{1,0:T(8,128)(2,1)S(1)}, u32[]{:S(2)}, u32[]{:S(2)}) collective-permute-start(bf16[160,1024]{1,0:T(8,128)(2,1)S(1)} %get-tuple-element.242), channel_id=1, source_target_pairs={{0,1},{1,0},{2,3},{3,2},{4,5},{5,4},{6,7},{7,6},{8,9},{9,8},{10,11... | collective-permute-start | bytes 983048 | tf_op jit(solution)/shard_map/ppermute | solution.py:808
  198.0 111.1 %reduce-scatter.8.cloned.1.call-start = ((), (), s32[]{:S(2)}) async-start(), calls=%async_computation.9 | async-start | bytes 1310720 | tf_op jit(solution)/shard_map/reduce_scatter | solution.py:1052
  200.7 12.3 %collective-permute-start.59 = (bf16[80,1024]{1,0:T(8,128)(2,1)S(1)}, bf16[80,1024]{1,0:T(8,128)(2,1)S(1)}, u32[]{:S(2)}, u32[]{:S(2)}) collective-permute-start(bf16[80,1024]{1,0:T(8,128)(2,1)S(1)} %get-tuple-element.272.refs_0_), channel_id=1, source_target_pairs={{0,2},{2,0},{4,6},{6,4},{1,3},{3,1},{5,7},{7,5},{8,10},{10,8},{12,... | collective-permute-start | bytes 491528 | tf_op jit(solution)/shard_map/ppermute | solution.py:802
  203.3 9.8 %collective-permute-start.62 = (bf16[80,1024]{1,0:T(8,128)(2,1)S(1)}, bf16[80,1024]{1,0:T(8,128)(2,1)S(1)}, u32[]{:S(2)}, u32[]{:S(2)}) collective-permute-start(bf16[80,1024]{1,0:T(8,128)(2,1)S(1)} %collective-permute-done.58.refs_3_), channel_id=1, source_target_pairs={{0,2},{2,0},{4,6},{6,4},{1,3},{3,1},{5,7},{7,5},{8,10},{10,8},{12,... | collective-permute-start | bytes 491528 | tf_op jit(solution)/shard_map/ppermute | solution.py:802
  222.0 8.3 %collective-permute-start.66 = (bf16[80,1024]{1,0:T(8,128)(2,1)S(1)}, bf16[80,1024]{1,0:T(8,128)(2,1)S(1)}, u32[]{:S(2)}, u32[]{:S(2)}) collective-permute-start(bf16[80,1024]{1,0:T(8,128)(2,1)S(1)} %get-tuple-element.288), channel_id=1, source_target_pairs={{0,1},{1,0},{2,3},{3,2},{4,5},{5,4},{6,7},{7,6},{8,9},{9,8},{10,11... | collective-permute-start | bytes 491528 | tf_op jit(solution)/shard_map/ppermute | solution.py:808
  235.7 78.8 %reduce-scatter.6.cloned.1.call-start = ((), (), s32[]{:S(2)}) async-start(), calls=%async_computation.8 | async-start | bytes 2621440 | tf_op jit(solution)/shard_map/reduce_scatter | solution.py:1052
  238.6 8.7 %collective-permute-start.70 = (bf16[80,1024]{1,0:T(8,128)(2,1)S(1)}, bf16[80,1024]{1,0:T(8,128)(2,1)S(1)}, u32[]{:S(2)}, u32[]{:S(2)}) collective-permute-start(bf16[80,1024]{1,0:T(8,128)(2,1)S(1)} %get-tuple-element.293.refs_0_), channel_id=1, source_target_pairs={{0,2},{2,0},{4,6},{6,4},{1,3},{3,1},{5,7},{7,5},{8,10},{10,8},{12,... | collective-permute-start | bytes 491528 | tf_op jit(solution)/shard_map/ppermute | solution.py:802
  256.4 8.3 %collective-permute-start.77 = (bf16[80,1024]{1,0:T(8,128)(2,1)S(1)}, bf16[80,1024]{1,0:T(8,128)(2,1)S(1)}, u32[]{:S(2)}, u32[]{:S(2)}) collective-permute-start(bf16[80,1024]{1,0:T(8,128)(2,1)S(1)} %get-tuple-element.305), channel_id=1, source_target_pairs={{0,1},{1,0},{2,3},{3,2},{4,5},{5,4},{6,7},{7,6},{8,9},{9,8},{10,11... | collective-permute-start | bytes 491528 | tf_op jit(solution)/shard_map/ppermute | solution.py:808
  273.2 12.3 %collective-permute-start.81 = (bf16[80,1024]{1,0:T(8,128)(2,1)S(1)}, bf16[80,1024]{1,0:T(8,128)(2,1)S(1)}, u32[]{:S(2)}, u32[]{:S(2)}) collective-permute-start(bf16[80,1024]{1,0:T(8,128)(2,1)S(1)} %settle.1.refs_0_), channel_id=1, source_target_pairs={{0,2},{2,0},{4,6},{6,4},{1,3},{3,1},{5,7},{7,5},{8,10},{10,8},{12,... | collective-permute-start | bytes 491528 | tf_op jit(solution)/shard_map/ppermute | solution.py:802
  275.9 9.6 %collective-permute-start.84 = (bf16[80,1024]{1,0:T(8,128)(2,1)S(1)}, bf16[80,1024]{1,0:T(8,128)(2,1)S(1)}, u32[]{:S(2)}, u32[]{:S(2)}) collective-permute-start(bf16[80,1024]{1,0:T(8,128)(2,1)S(1)} %collective-permute-done.80.refs_3_), channel_id=1, source_target_pairs={{0,2},{2,0},{4,6},{6,4},{1,3},{3,1},{5,7},{7,5},{8,10},{10,8},{12,... | collective-permute-start | bytes 491528 | tf_op jit(solution)/shard_map/ppermute | solution.py:802
  277.1 8.3 %collective-permute-start.83 = (bf16[80,1024]{1,0:T(8,128)(2,1)S(1)}, bf16[80,1024]{1,0:T(8,128)(2,1)S(1)}, u32[]{:S(2)}, u32[]{:S(2)}) collective-permute-start(bf16[80,1024]{1,0:T(8,128)(2,1)S(1)} %collective-permute-done.79.refs_2_), channel_id=1, source_target_pairs={{0,2},{2,0},{4,6},{6,4},{1,3},{3,1},{5,7},{7,5},{8,10},{10,8},{12,... | collective-permute-start | bytes 491528 | tf_op jit(solution)/shard_map/ppermute | solution.py:802
  294.4 8.3 %collective-permute-start.88 = (bf16[80,1024]{1,0:T(8,128)(2,1)S(1)}, bf16[80,1024]{1,0:T(8,128)(2,1)S(1)}, u32[]{:S(2)}, u32[]{:S(2)}) collective-permute-start(bf16[80,1024]{1,0:T(8,128)(2,1)S(1)} %get-tuple-element.327), channel_id=1, source_target_pairs={{0,1},{1,0},{2,3},{3,2},{4,5},{5,4},{6,7},{7,6},{8,9},{9,8},{10,11... | collective-permute-start | bytes 491528 | tf_op jit(solution)/shard_map/ppermute | solution.py:808
  315.8 29.6 %collective-permute-start.93 = (bf16[1280,512]{1,0:T(8,128)(2,1)S(1)}, bf16[1280,512]{1,0:T(8,128)(2,1)S(1)}, u32[]{:S(2)}, u32[]{:S(2)}) collective-permute-start(bf16[1280,512]{1,0:T(8,128)(2,1)S(1)} %fetch.1.refs_4_), channel_id=1, source_target_pairs={{0,4},{2,6},{4,0},{6,2},{1,5},{3,7},{5,1},{7,3},{8,12},{10,14},{12... | collective-permute-start | bytes 3932168 | tf_op jit(solution)/shard_map/ppermute | solution.py:805
  317.1 87.4 %collective-permute-start.101 = (bf16[1280,512]{1,0:T(8,128)(2,1)S(1)}, bf16[1280,512]{1,0:T(8,128)(2,1)S(1)}, u32[]{:S(2)}, u32[]{:S(2)}) collective-permute-start(bf16[1280,512]{1,0:T(8,128)(2,1)S(1)} %fetch.1.refs_4_), channel_id=1, source_target_pairs={{0,2},{2,0},{4,6},{6,4},{1,3},{3,1},{5,7},{7,5},{8,10},{10,8},{12,... | collective-permute-start | bytes 3932168 | tf_op jit(solution)/shard_map/ppermute | solution.py:802
  345.4 59.1 %collective-permute-start.102 = (bf16[1280,512]{1,0:T(8,128)(2,1)S(1)}, bf16[1280,512]{1,0:T(8,128)(2,1)S(1)}, u32[]{:S(2)}, u32[]{:S(2)}) collective-permute-start(bf16[1280,512]{1,0:T(8,128)(2,1)S(1)} %collective-permute-done.93.refs_4_.refs_6_), channel_id=1, source_target_pairs={{0,2},{2,0},{4,6},{6,4},{1,3},{3,1},{5,7},{7,5},{8,10},{10,8},{12,... | collective-permute-start | bytes 3932168 | tf_op jit(solution)/shard_map/ppermute | solution.py:802
  347.1 9.3 %collective-permute-start.55 = (f32[80,1024]{1,0:T(8,128)S(1)}, f32[80,1024]{1,0:T(8,128)S(1)}, u32[]{:S(2)}, u32[]{:S(2)}) collective-permute-start(f32[80,1024]{1,0:T(8,128)S(1)} %copy-done.11), channel_id=1, source_target_pairs={{0,1},{1,0},{2,3},{3,2},{4,5},{5,4},{6,7},{7,6},{8,9},{9,8},{10,11... | collective-permute-start | bytes 983048 | tf_op jit(solution)/shard_map/ppermute | solution.py:808
  348.3 11.0 %collective-permute-start.90 = (bf16[288,512]{1,0:T(8,128)(2,1)S(1)}, bf16[288,512]{1,0:T(8,128)(2,1)S(1)}, u32[]{:S(2)}, u32[]{:S(2)}) collective-permute-start(bf16[288,512]{1,0:T(8,128)(2,1)S(1)} %copy-done.19), channel_id=1, source_target_pairs={{0,8},{8,16},{16,24},{24,0},{1,9},{9,17},{17,25},{25,1},{2,10},{10... | collective-permute-start | bytes 884744 | tf_op jit(solution)/shard_map/ppermute | solution.py:817
  351.2 28.2 %collective-permute-start.89 = (f32[80,1024]{1,0:T(8,128)S(1)}, f32[80,1024]{1,0:T(8,128)S(1)}, u32[]{:S(2)}, u32[]{:S(2)}) collective-permute-start(f32[80,1024]{1,0:T(8,128)S(1)} %copy-done.12), channel_id=1, source_target_pairs={{0,1},{1,0},{2,3},{3,2},{4,5},{5,4},{6,7},{7,6},{8,9},{9,8},{10,11... | collective-permute-start | bytes 983048 | tf_op jit(solution)/shard_map/ppermute | solution.py:808
  356.4 21.2 %collective-permute-start.91 = (bf16[288,512]{1,0:T(8,128)(2,1)S(1)}, bf16[288,512]{1,0:T(8,128)(2,1)S(1)}, u32[]{:S(2)}, u32[]{:S(2)}) collective-permute-start(bf16[288,512]{1,0:T(8,128)(2,1)S(1)} %copy-done.18), channel_id=1, source_target_pairs={{0,16},{8,24},{16,0},{24,8},{1,17},{9,25},{17,1},{25,9},{2,18},{10... | collective-permute-start | bytes 884744 | tf_op jit(solution)/shard_map/ppermute | solution.py:817
  359.3 20.1 %collective-permute-start.92 = (bf16[288,512]{1,0:T(8,128)(2,1)S(1)}, bf16[288,512]{1,0:T(8,128)(2,1)S(1)}, u32[]{:S(2)}, u32[]{:S(2)}) collective-permute-start(bf16[288,512]{1,0:T(8,128)(2,1)S(1)} %copy-done.17), channel_id=1, source_target_pairs={{0,24},{8,0},{16,8},{24,16},{1,25},{9,1},{17,9},{25,17},{2,26},{10... | collective-permute-start | bytes 884744 | tf_op jit(solution)/shard_map/ppermute | solution.py:817
  381.8 22.6 %collective-permute-start.99 = (bf16[256,512]{1,0:T(8,128)(2,1)S(1)}, bf16[256,512]{1,0:T(8,128)(2,1)S(1)}, u32[]{:S(2)}, u32[]{:S(2)}) collective-permute-start(bf16[256,512]{1,0:T(8,128)(2,1)S(1)} %get-tuple-element.349.refs_0_), channel_id=1, source_target_pairs={{0,2},{2,0},{4,6},{6,4},{1,3},{3,1},{5,7},{7,5},{8,10},{10,8},{12,... | collective-permute-start | bytes 786440 | tf_op jit(solution)/shard_map/ppermute | solution.py:802
  388.0 16.4 %collective-permute-start.100 = (bf16[256,512]{1,0:T(8,128)(2,1)S(1)}, bf16[256,512]{1,0:T(8,128)(2,1)S(1)}, u32[]{:S(2)}, u32[]{:S(2)}) collective-permute-start(bf16[256,512]{1,0:T(8,128)(2,1)S(1)} %collective-permute-done.97.refs_4_.refs_2_), channel_id=1, source_target_pairs={{0,2},{2,0},{4,6},{6,4},{1,3},{3,1},{5,7},{7,5},{8,10},{10,8},{12,... | collective-permute-start | bytes 786440 | tf_op jit(solution)/shard_map/ppermute | solution.py:802
  (82 other events, 620.9 us)
Sparse Core Ops, SparseCore 0:
  10.2 28.8 all-gather.6
  41.2 43.7 all-gather.8
  86.6 28.1 all-gather.10
  116.2 43.8 all-gather.4
  198.1 41.6 reduce-scatter.3
  242.6 26.8 reduce-scatter.7
  272.3 42.1 reduce-scatter.5

commit v8 on v7

--- a/solution.py
+++ b/solution.py
@@ -609,10 +609,18 @@
         copy.wait()
 
 
-def shard_sum_kernel(depth, own_hbm, *refs):
-    *others, part_ref, mine_ref, own, sems = refs
-    (copy,) = start_copies([(own_hbm, own)], sems)
-    copy.wait()
+def shard_sum_kernel(depth, own_hbm, stacked, crossed, *refs):
+    *others, part_ref, mine_ref, pair_ref, own, sems = refs
+    count = stacked.shape[0]
+    first, *copies = start_copies(
+        [
+            (own_hbm, own),
+            (stacked, pair_ref.at[pl.ds(0, count), :]),
+            (crossed, pair_ref.at[pl.ds(count, count), :]),
+        ],
+        sems,
+    )
+    first.wait()
     rows, width = part_ref.shape[0], mine_ref.shape[1]
     terms = [ref[...].astype(f32) for ref in (own, *others)]
     total = terms[0]
@@ -623,11 +631,17 @@
     mine_ref[: 6 * depth, :] = lines[: 6 * depth, :]
     for k in range(mine_ref.shape[0] - 16):
         mine_ref[16 + k : 17 + k, :] = lines[6 * depth + k : 6 * depth + k + 1, :]
+    for copy in copies:
+        copy.wait()
 
 
 def place_kernel(depth, hidden, feats, *refs):
-    slices = [(refs[k], refs[GROUP + k]) for k in range(GROUP)]
-    qkv_hbm, out_hbm, fc1_hbm, fc2_hbm, fc1, fc2, qkv, out, sems = refs[2 * GROUP :]
+    alone_refs, pairs, rest = refs[:GROUP], refs[GROUP : GROUP + 2], refs[GROUP + 2 :]
+    count = pairs[0].shape[0] // 2
+    slices = [
+        (alone_refs[k], pairs[k % 2].at[pl.ds(k // 2 * count, count), :]) for k in range(GROUP)
+    ]
+    qkv_hbm, out_hbm, fc1_hbm, fc2_hbm, fc1, fc2, qkv, out, sems = rest
     ci = lax.rem(lax.axis_index("ctx"), GROUP)
     rows = fc1.shape[2]
     copies = []
@@ -1308,21 +1322,27 @@
     other_terms = [shift_z(term, d + 1) for d, term in enumerate(other_terms)]
     crossed = swap_x(stacked)
     others = (swap_y(upstream), swap_y(outputs_own))
-    part, mine = kernel_call(
+    part, mine, pair = kernel_call(
         functools.partial(shard_sum_kernel, depth),
-        [((width_own, 4 * feats), bf16), ((24, width_own), f32)],
+        [
+            ((width_own, 4 * feats), bf16),
+            ((24, width_own), f32),
+            ((2 * blocks * width_own, hidden), bf16),
+        ],
         Far(own_term),
+        stacked,
+        crossed,
         *other_terms,
         name="shard_sum",
-        after=(crossed, *others),
-        scratch=[pltpu.VMEM(own_term.shape, bf16), DMA((1,))],
+        after=others,
+        scratch=[pltpu.VMEM(own_term.shape, bf16), DMA((3,))],
     )
     if outer > 1:
         part = lax.psum(part, "ctx", axis_index_groups=outer_groups)
     part_crossed = swap_x(part)
     pieces = [
         *(part, swap_core(part), part_crossed, swap_core(part_crossed)),
-        *(stacked, swap_core(stacked), crossed, swap_core(crossed)),
+        *(pair, swap_core(pair)),
     ]
     mine = kernel_call(
         functools.partial(vector_plane_kernel, depth),

time: 422 us -> 389 us (0.922)
  waiting for transfers between devices: 168 us -> 141 us
  starting transfers between devices: 123 us -> 116 us
    ppermute x18, waiting for transfers between devices: 62.9 us -> 36.1 us  [swap_x(): return lax.ppermute(value, 'ctx', [(i, i ^ 2) for i in range(ctx)])]
    ppermute x45 -> x44, starting transfers between devices: 61.3 us -> 58.3 us  [swap_core(): return lax.ppermute(value, 'ctx', [(i, i ^ 1) for i in range(ctx)])]
  transfers between devices with their start and end apart: 110 -> 109, of which waited for: 52 -> 50; matrix products, arithmetic and copies ran while one was open for 0% -> 0% of each run, Pallas kernels for 20% -> 21%
where the time goes in v8:
time: 389 us; the launch traced here: 383 us
  waiting for transfers between devices  141 us (36%)
  starting transfers between devices  116 us (30%)
  Pallas kernels  103 us (26%)
  between operations  15.5 us (4%)
  local copies, waits for them, and re-layouts  7.12 us (2%)
    pallas_call x60, Pallas kernels, kernel_call(): pl.pallas_call(run, out_shape=out_shape, in_specs=specs, out_specs=out_sp...  103 us
    ppermute x44, starting transfers between devices, swap_core(): return lax.ppermute(value, 'ctx', [(i, i ^ 1) for i in range(ctx)])  58.3 us
    ppermute x16, waiting for transfers between devices, swap_xy(): return lax.ppermute(value, ('ctx', 'tp'), pairs)  39.5 us
    ppermute x18, waiting for transfers between devices, swap_x(): return lax.ppermute(value, 'ctx', [(i, i ^ 2) for i in range(ctx)])  36.1 us
    ppermute x6, waiting for transfers between devices, shift_z(): lax.ppermute(value, 'fsdp', [(i, (i + d) % fsdp) for i in range(fsdp)])  20.2 us
    ppermute x16, starting transfers between devices, swap_xy(): return lax.ppermute(value, ('ctx', 'tp'), pairs)  18.3 us
    all_gather x2, waiting for transfers between devices, per_device(): mlp_w.append(lax.all_gather(own, 'fsdp', axis=0, tiled=True))  17.9 us
    ppermute x18, waiting for transfers between devices, swap_y(): return lax.ppermute(value, 'tp', [(i, i ^ 1) for i in range(tp)])  15.7 us
  transfers between devices with their start and end apart: 109, of which 50 were waited for; matrix products, arithmetic and copies ran while one was open for 0% of the time, Pallas kernels for 21%

profile of v8, /device:TPU:9, one launch (start us, length us, event | category | flops | bytes accessed | tf_op | source)
XLA Modules:
  0.0 382.6 jit_solution(475160019945526021)
XLA Ops:
  15.2 2.3 prep_upstream.1
  45.9 3.4 attn.5
  51.7 2.6 attn.4
  57.2 3.6 collective-permute-done.18.refs_1_
  60.8 3.7 collective-permute-done.19.refs_2_
  73.0 2.5 collective-permute-start.26
  78.7 6.3 %all-gather.9.cloned.1.call-done.refs_4_ = bf16[1024,1024]{1,0:T(8,128)(2,1)} async-done(((bf16[256,1024]{1,0:T(8,128)(2,1)}), bf16[1024,1024]{1,0:T(8,128)(2,1)}) %all-gather.9.cloned.1.call-update) | async-done | bytes 2097168 | tf_op jit(solution)/shard_map/all_gather | solution.py:893
  94.1 3.6 collective-permute-done.29.refs_1_
  97.7 3.6 collective-permute-done.30.refs_2_
  118.9 2.6 attn.7
  122.5 2.6 attn.6
  128.0 4.2 %collective-permute-done.40.refs_1_ = bf16[80,1024]{1,0:T(8,128)(2,1)S(1)} collective-permute-done((bf16[80,1024]{1,0:T(8,128)(2,1)S(1)}, bf16[80,1024]{1,0:T(8,128)(2,1)S(1)}, u32[]{:S(2)}, u32[]{:S(2)}) %collective-permute-start.40) | collective-permute-done | bytes 163872 | tf_op jit(solution)/shard_map/ppermute | solution.py:828
  132.1 3.4 collective-permute-done.41.refs_2_
  143.9 2.3 collective-permute-start.48
  148.5 11.6 %all-gather.5.cloned.1.call-done.refs_4_.refs_1_ = bf16[1024,1024]{1,0:T(8,128)(2,1)} async-done(((bf16[256,1024]{1,0:T(8,128)(2,1)}), bf16[1024,1024]{1,0:T(8,128)(2,1)}) %all-gather.5.cloned.1.call-update) | async-done | bytes 2097168 | tf_op jit(solution)/shard_map/all_gather | solution.py:893
  161.7 2.7 mlp.7
  164.5 3.3 mlp_back.5
  170.0 2.9 mlp_back.4
  176.0 7.1 %collective-permute-done.52.refs_1_ = bf16[160,1024]{1,0:T(8,128)(2,1)S(1)} collective-permute-done((bf16[160,1024]{1,0:T(8,128)(2,1)S(1)}, bf16[160,1024]{1,0:T(8,128)(2,1)S(1)}, u32[]{:S(2)}, u32[]{:S(2)}) %collective-permute-start.52) | collective-permute-done | bytes 327712 | tf_op jit(solution)/shard_map/ppermute | solution.py:828
  183.1 7.0 %collective-permute-done.53.refs_2_ = bf16[160,1024]{1,0:T(8,128)(2,1)S(1)} collective-permute-done((bf16[160,1024]{1,0:T(8,128)(2,1)S(1)}, bf16[160,1024]{1,0:T(8,128)(2,1)S(1)}, u32[]{:S(2)}, u32[]{:S(2)}) %collective-permute-start.53) | collective-permute-done | bytes 327712 | tf_op jit(solution)/shard_map/ppermute | solution.py:819
  194.2 3.8 mlp_grad.2
  204.9 2.3 collective-permute-start.61
  209.4 3.6 attn_back.4
  213.1 3.6 attn_back.5
  222.3 3.9 %collective-permute-done.64.refs_1_ = bf16[80,1024]{1,0:T(8,128)(2,1)S(1)} collective-permute-done((bf16[80,1024]{1,0:T(8,128)(2,1)S(1)}, bf16[80,1024]{1,0:T(8,128)(2,1)S(1)}, u32[]{:S(2)}, u32[]{:S(2)}) %collective-permute-start.64) | collective-permute-done | bytes 163872 | tf_op jit(solution)/shard_map/ppermute | solution.py:828
  226.2 3.7 collective-permute-done.65.refs_2_
  231.7 4.0 %attn_grad.2 = (bf16[1024,512]{1,0:T(8,128)(2,1)}, f32[2,128]{1,0:T(2,128)}, bf16[80,1024]{1,0:T(8,128)(2,1)S(1)}, f32[2,1024]{1,0:T(2,128)}, f32[80,1024]{1,0:T(8,128)}) custom-call(bf16[320,1024]{1,0:T(8,128)(2,1)} %get-tuple-element.255.refs_0_, bf16[320,1024]{1,0:T(8,128)(2,1)} %get-tuple-element.256.refs_1_, ...), custom_call_target="tpu_custom_call" | custom-call | tf_op jit(solution)/shard_map/attn_grad/pallas_call | solution.py:79
  242.7 2.3 collective-permute-start.72
  248.3 2.5 mlp_back.7
  251.3 2.5 mlp_back.6
  256.7 3.9 %collective-permute-done.75.refs_1_ = bf16[80,1024]{1,0:T(8,128)(2,1)S(1)} collective-permute-done((bf16[80,1024]{1,0:T(8,128)(2,1)S(1)}, bf16[80,1024]{1,0:T(8,128)(2,1)S(1)}, u32[]{:S(2)}, u32[]{:S(2)}) %collective-permute-start.75) | collective-permute-done | bytes 163872 | tf_op jit(solution)/shard_map/ppermute | solution.py:828
  260.6 3.7 collective-permute-done.76.refs_2_
  266.1 4.3 %mlp_grad.3 = (bf16[1024,1024]{1,0:T(8,128)(2,1)}, bf16[80,1024]{1,0:T(8,128)(2,1)S(1)}, f32[4,1024]{1,0:T(4,128)}, f32[80,1024]{1,0:T(8,128)}) custom-call(bf16[320,1024]{1,0:T(8,128)(2,1)} %get-tuple-element.251.refs_0_, bf16[320,1024]{1,0:T(8,128)(2,1)} %get-tuple-element.252.refs_1_, bf16[320,512]{1,0:T(8,128)(2,1)} %get-tuple-element.253.refs_2_, ...), custom_call_target="tpu_custom_call" | custom-call | tf_op jit(solution)/shard_map/mlp_grad/pallas_call | solution.py:79
  277.2 2.3 collective-permute-start.83
  281.9 3.6 attn_back.6
  285.5 3.6 attn_back.7
  294.7 3.9 %collective-permute-done.86.refs_1_ = bf16[80,1024]{1,0:T(8,128)(2,1)S(1)} collective-permute-done((bf16[80,1024]{1,0:T(8,128)(2,1)S(1)}, bf16[80,1024]{1,0:T(8,128)(2,1)S(1)}, u32[]{:S(2)}, u32[]{:S(2)}) %collective-permute-start.86) | collective-permute-done | bytes 163872 | tf_op jit(solution)/shard_map/ppermute | solution.py:828
  298.6 3.7 collective-permute-done.87.refs_2_
  305.1 3.9 %attn_grad.3 = (bf16[288,512]{1,0:T(8,128)(2,1)}, bf16[288,512]{1,0:T(8,128)(2,1)}, bf16[288,512]{1,0:T(8,128)(2,1)}, bf16[288,512]{1,0:T(8,128)(2,1)}, f32[2,12...) custom-call(bf16[320,1024]{1,0:T(8,128)(2,1)} %get-tuple-element.247.refs_0_, ...), custom_call_target="tpu_custom_call" | custom-call | tf_op jit(solution)/shard_map/attn_grad/pallas_call | solution.py:79
  309.1 5.6 %reduce-scatter.6.cloned.1.call-done.refs_0_ = bf16[256,1024]{1,0:T(8,128)(2,1)} async-done(((bf16[1024,1024]{1,0:T(8,128)(2,1)}), bf16[256,1024]{1,0:T(8,128)(2,1)}) %reduce-scatter.6.cloned.1.call-update) | async-done | bytes 524304 | tf_op jit(solution)/shard_map/reduce_scatter | solution.py:1066
  318.7 3.0 collective-permute-start.91
  325.3 2.5 collective-permute-start.93
  327.8 17.7 %collective-permute-done.92.refs_4_ = bf16[288,512]{1,0:T(8,128)(2,1)S(1)} collective-permute-done((bf16[288,512]{1,0:T(8,128)(2,1)S(1)}, bf16[288,512]{1,0:T(8,128)(2,1)S(1)}, u32[]{:S(2)}, u32[]{:S(2)}) %collective-permute-start.92) | collective-permute-done | bytes 294944 | tf_op jit(solution)/shard_map/ppermute | solution.py:831
  345.5 2.5 collective-permute-done.93.refs_5_
  351.3 7.2 %collective-permute-done.97.refs_4_.refs_2_ = bf16[256,512]{1,0:T(8,128)(2,1)S(1)} collective-permute-done((bf16[256,512]{1,0:T(8,128)(2,1)S(1)}, bf16[256,512]{1,0:T(8,128)(2,1)S(1)}, u32[]{:S(2)}, u32[]{:S(2)}) %collective-permute-start.97) | collective-permute-done | bytes 262176 | tf_op jit(solution)/shard_map/ppermute | solution.py:819
  363.2 2.4 collective-permute-done.94.refs_1_
  365.6 2.3 collective-permute-start.98
  370.6 4.9 %place.1 = (f32[2,3,256,512]{3,2,1,0:T(8,128)}, f32[2,512,256]{2,1,0:T(8,128)}, f32[2,256,2048]{2,1,0:T(8,128)}, f32[2,2048,256]{2,1,0:T(8,128)}) custom-call(bf16[256,512]{1,0:T(8,128)(2,1)S(1)} %get-tuple-element.350.refs_0_, bf16[256,512]{1,0:T(8,128)(2,1)S(1)} %collective-permute-done.99.refs_1_, ...), custom_call_target="tpu_custom_call" | custom-call | tf_op jit(solution)/shard_map/place/pallas_call | solution.py:79
  (309 shorter events, 172.6 us)
Async XLA Ops:
  7.2 34.2 %all-gather.7.cloned.1.call-start = ((), (), s32[]{:S(2)}) async-start(), calls=%async_computation.4 | async-start | bytes 1310720 | tf_op jit(solution)/shard_map/all_gather | solution.py:891
  9.0 76.0 %all-gather.9.cloned.1.call-start = ((), (), s32[]{:S(2)}) async-start(), calls=%async_computation.5 | async-start | bytes 2621440 | tf_op jit(solution)/shard_map/all_gather | solution.py:893
  11.2 103.7 %all-gather.11.cloned.1.call-start = ((), (), s32[]{:S(2)}) async-start(), calls=%async_computation.6 | async-start | bytes 1310720 | tf_op jit(solution)/shard_map/all_gather | solution.py:891
  11.4 10.9 %collective-permute-start.9 = (bf16[17,256]{1,0:T(8,128)(2,1)S(1)}, bf16[17,256]{1,0:T(8,128)(2,1)S(1)}, u32[]{:S(2)}, u32[]{:S(2)}) collective-permute-start(bf16[17,256]{1,0:T(8,128)(2,1)S(1)} %fusion.1), channel_id=1, source_target_pairs={{0,8},{8,16},{16,24},{24,0},{1,9},{9,17},{17,25},{25,1},{2,10},{10... | collective-permute-start | bytes 26120 | tf_op jit(solution)/shard_map/ppermute | solution.py:831
  12.8 10.9 %collective-permute-start.8 = (bf16[17,256]{1,0:T(8,128)(2,1)S(1)}, bf16[17,256]{1,0:T(8,128)(2,1)S(1)}, u32[]{:S(2)}, u32[]{:S(2)}) collective-permute-start(bf16[17,256]{1,0:T(8,128)(2,1)S(1)} %fusion.1), channel_id=1, source_target_pairs={{0,16},{8,24},{16,0},{24,8},{1,17},{9,25},{17,1},{25,9},{2,18},{10... | collective-permute-start | bytes 26120 | tf_op jit(solution)/shard_map/ppermute | solution.py:831
  13.9 10.0 %collective-permute-start.7 = (bf16[17,256]{1,0:T(8,128)(2,1)S(1)}, bf16[17,256]{1,0:T(8,128)(2,1)S(1)}, u32[]{:S(2)}, u32[]{:S(2)}) collective-permute-start(bf16[17,256]{1,0:T(8,128)(2,1)S(1)} %fusion.1), channel_id=1, source_target_pairs={{0,24},{8,0},{16,8},{24,16},{1,25},{9,1},{17,9},{25,17},{2,26},{10... | collective-permute-start | bytes 26120 | tf_op jit(solution)/shard_map/ppermute | solution.py:831
  17.6 9.2 %collective-permute-start.3 = (bf16[80,1024]{1,0:T(8,128)(2,1)S(1)}, bf16[80,1024]{1,0:T(8,128)(2,1)S(1)}, u32[]{:S(2)}, u32[]{:S(2)}) collective-permute-start(bf16[80,1024]{1,0:T(8,128)(2,1)S(1)} %get-tuple-element.187.refs_0_), channel_id=1, source_target_pairs={{0,2},{2,0},{4,6},{6,4},{1,3},{3,1},{5,7},{7,5},{8,10},{10,8},{12,... | collective-permute-start | bytes 491528 | tf_op jit(solution)/shard_map/ppermute | solution.py:816
  19.1 8.9 %collective-permute-start.2 = (bf16[80,1024]{1,0:T(8,128)(2,1)S(1)}, bf16[80,1024]{1,0:T(8,128)(2,1)S(1)}, u32[]{:S(2)}, u32[]{:S(2)}) collective-permute-start(bf16[80,1024]{1,0:T(8,128)(2,1)S(1)} %get-tuple-element.187.refs_0_), channel_id=1, source_target_pairs={{0,1},{1,0},{2,3},{3,2},{4,5},{5,4},{6,7},{7,6},{8,9},{9,8},{10,11... | collective-permute-start | bytes 491528 | tf_op jit(solution)/shard_map/ppermute | solution.py:822
  22.2 137.9 %all-gather.5.cloned.1.call-start = ((), (), s32[]{:S(2)}) async-start(), calls=%async_computation.3 | async-start | bytes 2621440 | tf_op jit(solution)/shard_map/all_gather | solution.py:893
  25.5 9.0 %collective-permute-start.12 = (bf16[80,1024]{1,0:T(8,128)(2,1)S(1)}, bf16[80,1024]{1,0:T(8,128)(2,1)S(1)}, u32[]{:S(2)}, u32[]{:S(2)}) collective-permute-start(bf16[80,1024]{1,0:T(8,128)(2,1)S(1)} %get-tuple-element.191.refs_0_), channel_id=1, source_target_pairs={{0,1},{1,0},{2,3},{3,2},{4,5},{5,4},{6,7},{7,6},{8,9},{9,8},{10,11... | collective-permute-start | bytes 491528 | tf_op jit(solution)/shard_map/ppermute | solution.py:822
  26.8 8.8 %collective-permute-start.11 = (bf16[80,1024]{1,0:T(8,128)(2,1)S(1)}, bf16[80,1024]{1,0:T(8,128)(2,1)S(1)}, u32[]{:S(2)}, u32[]{:S(2)}) collective-permute-start(bf16[80,1024]{1,0:T(8,128)(2,1)S(1)} %get-tuple-element.191.refs_0_), channel_id=1, source_target_pairs={{0,4},{2,6},{4,0},{6,2},{1,5},{3,7},{5,1},{7,3},{8,12},{10,14},{12... | collective-permute-start | bytes 491528 | tf_op jit(solution)/shard_map/ppermute | solution.py:819
  28.0 10.5 %collective-permute-start.10 = (bf16[80,1024]{1,0:T(8,128)(2,1)S(1)}, bf16[80,1024]{1,0:T(8,128)(2,1)}, u32[]{:S(2)}, u32[]{:S(2)}) collective-permute-start(bf16[80,1024]{1,0:T(8,128)(2,1)S(1)} %get-tuple-element.191.refs_0_), channel_id=1, source_target_pairs={{0,5},{1,4},{2,7},{3,6},{4,1},{5,0},{6,3},{7,2},{8,13},{9,12},{10,... | collective-permute-start | bytes 491528 | tf_op jit(solution)/shard_map/ppermute | solution.py:828
  28.2 11.4 %collective-permute-start.6 = (bf16[80,1024]{1,0:T(8,128)(2,1)S(1)}, bf16[80,1024]{1,0:T(8,128)(2,1)S(1)}, u32[]{:S(2)}, u32[]{:S(2)}) collective-permute-start(bf16[80,1024]{1,0:T(8,128)(2,1)S(1)} %collective-permute-done.2.refs_3_), channel_id=1, source_target_pairs={{0,2},{2,0},{4,6},{6,4},{1,3},{3,1},{5,7},{7,5},{8,10},{10,8},{12,... | collective-permute-start | bytes 491528 | tf_op jit(solution)/shard_map/ppermute | solution.py:816
  31.3 8.3 %collective-permute-start.5 = (bf16[80,1024]{1,0:T(8,128)(2,1)S(1)}, bf16[80,1024]{1,0:T(8,128)(2,1)S(1)}, u32[]{:S(2)}, u32[]{:S(2)}) collective-permute-start(bf16[80,1024]{1,0:T(8,128)(2,1)S(1)} %collective-permute-done.1.refs_2_), channel_id=1, source_target_pairs={{0,2},{2,0},{4,6},{6,4},{1,3},{3,1},{5,7},{7,5},{8,10},{10,8},{12,... | collective-permute-start | bytes 491528 | tf_op jit(solution)/shard_map/ppermute | solution.py:816
  34.5 9.7 %collective-permute-start.13 = (bf16[80,1024]{1,0:T(8,128)(2,1)S(1)}, bf16[80,1024]{1,0:T(8,128)(2,1)}, u32[]{:S(2)}, u32[]{:S(2)}) collective-permute-start(bf16[80,1024]{1,0:T(8,128)(2,1)S(1)} %get-tuple-element.191.refs_0_), channel_id=1, source_target_pairs={{0,2},{2,0},{4,6},{6,4},{1,3},{3,1},{5,7},{7,5},{8,10},{10,8},{12,... | collective-permute-start | bytes 491528 | tf_op jit(solution)/shard_map/ppermute | solution.py:816
  51.5 219.0 %reduce-scatter.4.cloned.1.call-start = ((), (), s32[]{:S(2)}) async-start(), calls=%async_computation.7 | async-start | bytes 2621440 | tf_op jit(solution)/shard_map/reduce_scatter | solution.py:1066
  69.0 8.7 %collective-permute-start.24 = (bf16[80,1024]{1,0:T(8,128)(2,1)S(1)}, bf16[80,1024]{1,0:T(8,128)(2,1)S(1)}, u32[]{:S(2)}, u32[]{:S(2)}) collective-permute-start(bf16[80,1024]{1,0:T(8,128)(2,1)S(1)} %get-tuple-element.207.refs_0_), channel_id=1, source_target_pairs={{0,2},{2,0},{4,6},{6,4},{1,3},{3,1},{5,7},{7,5},{8,10},{10,8},{12,... | collective-permute-start | bytes 491528 | tf_op jit(solution)/shard_map/ppermute | solution.py:816
  93.8 8.2 %collective-permute-start.31 = (bf16[80,1024]{1,0:T(8,128)(2,1)S(1)}, bf16[80,1024]{1,0:T(8,128)(2,1)S(1)}, u32[]{:S(2)}, u32[]{:S(2)}) collective-permute-start(bf16[80,1024]{1,0:T(8,128)(2,1)S(1)} %get-tuple-element.215), channel_id=1, source_target_pairs={{0,1},{1,0},{2,3},{3,2},{4,5},{5,4},{6,7},{7,6},{8,9},{9,8},{10,11... | collective-permute-start | bytes 491528 | tf_op jit(solution)/shard_map/ppermute | solution.py:822
  105.9 10.7 %collective-permute-start.35 = (bf16[80,1024]{1,0:T(8,128)(2,1)S(1)}, bf16[80,1024]{1,0:T(8,128)(2,1)S(1)}, u32[]{:S(2)}, u32[]{:S(2)}) collective-permute-start(bf16[80,1024]{1,0:T(8,128)(2,1)S(1)} %get-tuple-element.217.refs_0_), channel_id=1, source_target_pairs={{0,2},{2,0},{4,6},{6,4},{1,3},{3,1},{5,7},{7,5},{8,10},{10,8},{12,... | collective-permute-start | bytes 491528 | tf_op jit(solution)/shard_map/ppermute | solution.py:816
  127.4 8.2 %collective-permute-start.41 = (bf16[80,1024]{1,0:T(8,128)(2,1)S(1)}, bf16[80,1024]{1,0:T(8,128)(2,1)S(1)}, u32[]{:S(2)}, u32[]{:S(2)}) collective-permute-start(bf16[80,1024]{1,0:T(8,128)(2,1)S(1)} %get-tuple-element.228), channel_id=1, source_target_pairs={{0,4},{2,6},{4,0},{6,2},{1,5},{3,7},{5,1},{7,3},{8,12},{10,14},{12... | collective-permute-start | bytes 491528 | tf_op jit(solution)/shard_map/ppermute | solution.py:819
  127.7 8.3 %collective-permute-start.42 = (bf16[80,1024]{1,0:T(8,128)(2,1)S(1)}, bf16[80,1024]{1,0:T(8,128)(2,1)S(1)}, u32[]{:S(2)}, u32[]{:S(2)}) collective-permute-start(bf16[80,1024]{1,0:T(8,128)(2,1)S(1)} %get-tuple-element.229), channel_id=1, source_target_pairs={{0,1},{1,0},{2,3},{3,2},{4,5},{5,4},{6,7},{7,6},{8,9},{9,8},{10,11... | collective-permute-start | bytes 491528 | tf_op jit(solution)/shard_map/ppermute | solution.py:822
  139.9 20.3 %collective-permute-start.46 = (bf16[80,1024]{1,0:T(8,128)(2,1)S(1)}, bf16[80,1024]{1,0:T(8,128)(2,1)S(1)}, u32[]{:S(2)}, u32[]{:S(2)}) collective-permute-start(bf16[80,1024]{1,0:T(8,128)(2,1)S(1)} %get-tuple-element.231.refs_0_), channel_id=1, source_target_pairs={{0,2},{2,0},{4,6},{6,4},{1,3},{3,1},{5,7},{7,5},{8,10},{10,8},{12,... | collective-permute-start | bytes 491528 | tf_op jit(solution)/shard_map/ppermute | solution.py:816
  142.7 17.5 %collective-permute-start.49 = (bf16[80,1024]{1,0:T(8,128)(2,1)S(1)}, bf16[80,1024]{1,0:T(8,128)(2,1)}, u32[]{:S(2)}, u32[]{:S(2)}) collective-permute-start(bf16[80,1024]{1,0:T(8,128)(2,1)S(1)} %collective-permute-done.45.refs_3_), channel_id=1, source_target_pairs={{0,2},{2,0},{4,6},{6,4},{1,3},{3,1},{5,7},{7,5},{8,10},{10,8},{12,... | collective-permute-start | bytes 491528 | tf_op jit(solution)/shard_map/ppermute | solution.py:816
  143.9 16.3 %collective-permute-start.48 = (bf16[80,1024]{1,0:T(8,128)(2,1)S(1)}, bf16[80,1024]{1,0:T(8,128)(2,1)}, u32[]{:S(2)}, u32[]{:S(2)}) collective-permute-start(bf16[80,1024]{1,0:T(8,128)(2,1)S(1)} %collective-permute-done.44.refs_2_), channel_id=1, source_target_pairs={{0,2},{2,0},{4,6},{6,4},{1,3},{3,1},{5,7},{7,5},{8,10},{10,8},{12,... | collective-permute-start | bytes 491528 | tf_op jit(solution)/shard_map/ppermute | solution.py:816
  146.9 13.2 %collective-permute-start.47 = (bf16[80,1024]{1,0:T(8,128)(2,1)S(1)}, bf16[80,1024]{1,0:T(8,128)(2,1)}, u32[]{:S(2)}, u32[]{:S(2)}) collective-permute-start(bf16[80,1024]{1,0:T(8,128)(2,1)S(1)} %collective-permute-done.43.refs_1_), channel_id=1, source_target_pairs={{0,2},{2,0},{4,6},{6,4},{1,3},{3,1},{5,7},{7,5},{8,10},{10,8},{12,... | collective-permute-start | bytes 491528 | tf_op jit(solution)/shard_map/ppermute | solution.py:816
  173.3 9.9 %collective-permute-start.52 = (bf16[160,1024]{1,0:T(8,128)(2,1)S(1)}, bf16[160,1024]{1,0:T(8,128)(2,1)S(1)}, u32[]{:S(2)}, u32[]{:S(2)}) collective-permute-start(bf16[160,1024]{1,0:T(8,128)(2,1)S(1)} %get-tuple-element.241), channel_id=1, source_target_pairs={{0,5},{1,4},{2,7},{3,6},{4,1},{5,0},{6,3},{7,2},{8,13},{9,12},{10,... | collective-permute-start | bytes 983048 | tf_op jit(solution)/shard_map/ppermute | solution.py:828
  175.4 14.7 %collective-permute-start.53 = (bf16[160,1024]{1,0:T(8,128)(2,1)S(1)}, bf16[160,1024]{1,0:T(8,128)(2,1)S(1)}, u32[]{:S(2)}, u32[]{:S(2)}) collective-permute-start(bf16[160,1024]{1,0:T(8,128)(2,1)S(1)} %get-tuple-element.242), channel_id=1, source_target_pairs={{0,4},{2,6},{4,0},{6,2},{1,5},{3,7},{5,1},{7,3},{8,12},{10,14},{12... | collective-permute-start | bytes 983048 | tf_op jit(solution)/shard_map/ppermute | solution.py:819
  175.7 15.2 %collective-permute-start.54 = (bf16[160,1024]{1,0:T(8,128)(2,1)S(1)}, bf16[160,1024]{1,0:T(8,128)(2,1)S(1)}, u32[]{:S(2)}, u32[]{:S(2)}) collective-permute-start(bf16[160,1024]{1,0:T(8,128)(2,1)S(1)} %get-tuple-element.243), channel_id=1, source_target_pairs={{0,1},{1,0},{2,3},{3,2},{4,5},{5,4},{6,7},{7,6},{8,9},{9,8},{10,11... | collective-permute-start | bytes 983048 | tf_op jit(solution)/shard_map/ppermute | solution.py:822
  198.0 111.1 %reduce-scatter.8.cloned.1.call-start = ((), (), s32[]{:S(2)}) async-start(), calls=%async_computation.9 | async-start | bytes 1310720 | tf_op jit(solution)/shard_map/reduce_scatter | solution.py:1066
  200.8 12.3 %collective-permute-start.59 = (bf16[80,1024]{1,0:T(8,128)(2,1)S(1)}, bf16[80,1024]{1,0:T(8,128)(2,1)S(1)}, u32[]{:S(2)}, u32[]{:S(2)}) collective-permute-start(bf16[80,1024]{1,0:T(8,128)(2,1)S(1)} %get-tuple-element.273.refs_0_), channel_id=1, source_target_pairs={{0,2},{2,0},{4,6},{6,4},{1,3},{3,1},{5,7},{7,5},{8,10},{10,8},{12,... | collective-permute-start | bytes 491528 | tf_op jit(solution)/shard_map/ppermute | solution.py:816
  203.3 9.8 %collective-permute-start.62 = (bf16[80,1024]{1,0:T(8,128)(2,1)S(1)}, bf16[80,1024]{1,0:T(8,128)(2,1)S(1)}, u32[]{:S(2)}, u32[]{:S(2)}) collective-permute-start(bf16[80,1024]{1,0:T(8,128)(2,1)S(1)} %collective-permute-done.58.refs_3_), channel_id=1, source_target_pairs={{0,2},{2,0},{4,6},{6,4},{1,3},{3,1},{5,7},{7,5},{8,10},{10,8},{12,... | collective-permute-start | bytes 491528 | tf_op jit(solution)/shard_map/ppermute | solution.py:816
  204.9 8.2 %collective-permute-start.61 = (bf16[80,1024]{1,0:T(8,128)(2,1)S(1)}, bf16[80,1024]{1,0:T(8,128)(2,1)S(1)}, u32[]{:S(2)}, u32[]{:S(2)}) collective-permute-start(bf16[80,1024]{1,0:T(8,128)(2,1)S(1)} %collective-permute-done.57.refs_2_), channel_id=1, source_target_pairs={{0,2},{2,0},{4,6},{6,4},{1,3},{3,1},{5,7},{7,5},{8,10},{10,8},{12,... | collective-permute-start | bytes 491528 | tf_op jit(solution)/shard_map/ppermute | solution.py:816
  222.0 8.2 %collective-permute-start.66 = (bf16[80,1024]{1,0:T(8,128)(2,1)S(1)}, bf16[80,1024]{1,0:T(8,128)(2,1)S(1)}, u32[]{:S(2)}, u32[]{:S(2)}) collective-permute-start(bf16[80,1024]{1,0:T(8,128)(2,1)S(1)} %get-tuple-element.289), channel_id=1, source_target_pairs={{0,1},{1,0},{2,3},{3,2},{4,5},{5,4},{6,7},{7,6},{8,9},{9,8},{10,11... | collective-permute-start | bytes 491528 | tf_op jit(solution)/shard_map/ppermute | solution.py:822
  235.7 78.9 %reduce-scatter.6.cloned.1.call-start = ((), (), s32[]{:S(2)}) async-start(), calls=%async_computation.8 | async-start | bytes 2621440 | tf_op jit(solution)/shard_map/reduce_scatter | solution.py:1066
  238.7 8.7 %collective-permute-start.70 = (bf16[80,1024]{1,0:T(8,128)(2,1)S(1)}, bf16[80,1024]{1,0:T(8,128)(2,1)S(1)}, u32[]{:S(2)}, u32[]{:S(2)}) collective-permute-start(bf16[80,1024]{1,0:T(8,128)(2,1)S(1)} %get-tuple-element.294.refs_0_), channel_id=1, source_target_pairs={{0,2},{2,0},{4,6},{6,4},{1,3},{3,1},{5,7},{7,5},{8,10},{10,8},{12,... | collective-permute-start | bytes 491528 | tf_op jit(solution)/shard_map/ppermute | solution.py:816
  256.4 8.2 %collective-permute-start.77 = (bf16[80,1024]{1,0:T(8,128)(2,1)S(1)}, bf16[80,1024]{1,0:T(8,128)(2,1)S(1)}, u32[]{:S(2)}, u32[]{:S(2)}) collective-permute-start(bf16[80,1024]{1,0:T(8,128)(2,1)S(1)} %get-tuple-element.306), channel_id=1, source_target_pairs={{0,1},{1,0},{2,3},{3,2},{4,5},{5,4},{6,7},{7,6},{8,9},{9,8},{10,11... | collective-permute-start | bytes 491528 | tf_op jit(solution)/shard_map/ppermute | solution.py:822
  273.2 12.3 %collective-permute-start.81 = (bf16[80,1024]{1,0:T(8,128)(2,1)S(1)}, bf16[80,1024]{1,0:T(8,128)(2,1)S(1)}, u32[]{:S(2)}, u32[]{:S(2)}) collective-permute-start(bf16[80,1024]{1,0:T(8,128)(2,1)S(1)} %settle.1.refs_0_), channel_id=1, source_target_pairs={{0,2},{2,0},{4,6},{6,4},{1,3},{3,1},{5,7},{7,5},{8,10},{10,8},{12,... | collective-permute-start | bytes 491528 | tf_op jit(solution)/shard_map/ppermute | solution.py:816
  275.9 9.6 %collective-permute-start.84 = (bf16[80,1024]{1,0:T(8,128)(2,1)S(1)}, bf16[80,1024]{1,0:T(8,128)(2,1)S(1)}, u32[]{:S(2)}, u32[]{:S(2)}) collective-permute-start(bf16[80,1024]{1,0:T(8,128)(2,1)S(1)} %collective-permute-done.80.refs_3_), channel_id=1, source_target_pairs={{0,2},{2,0},{4,6},{6,4},{1,3},{3,1},{5,7},{7,5},{8,10},{10,8},{12,... | collective-permute-start | bytes 491528 | tf_op jit(solution)/shard_map/ppermute | solution.py:816
  277.2 8.3 %collective-permute-start.83 = (bf16[80,1024]{1,0:T(8,128)(2,1)S(1)}, bf16[80,1024]{1,0:T(8,128)(2,1)S(1)}, u32[]{:S(2)}, u32[]{:S(2)}) collective-permute-start(bf16[80,1024]{1,0:T(8,128)(2,1)S(1)} %collective-permute-done.79.refs_2_), channel_id=1, source_target_pairs={{0,2},{2,0},{4,6},{6,4},{1,3},{3,1},{5,7},{7,5},{8,10},{10,8},{12,... | collective-permute-start | bytes 491528 | tf_op jit(solution)/shard_map/ppermute | solution.py:816
  294.4 8.3 %collective-permute-start.88 = (bf16[80,1024]{1,0:T(8,128)(2,1)S(1)}, bf16[80,1024]{1,0:T(8,128)(2,1)S(1)}, u32[]{:S(2)}, u32[]{:S(2)}) collective-permute-start(bf16[80,1024]{1,0:T(8,128)(2,1)S(1)} %get-tuple-element.328), channel_id=1, source_target_pairs={{0,1},{1,0},{2,3},{3,2},{4,5},{5,4},{6,7},{7,6},{8,9},{9,8},{10,11... | collective-permute-start | bytes 491528 | tf_op jit(solution)/shard_map/ppermute | solution.py:822
  316.0 32.1 %collective-permute-start.90 = (bf16[1280,512]{1,0:T(8,128)(2,1)S(1)}, bf16[1280,512]{1,0:T(8,128)(2,1)S(1)}, u32[]{:S(2)}, u32[]{:S(2)}) collective-permute-start(bf16[1280,512]{1,0:T(8,128)(2,1)S(1)} %fetch.1.refs_1_), channel_id=1, source_target_pairs={{0,4},{2,6},{4,0},{6,2},{1,5},{3,7},{5,1},{7,3},{8,12},{10,14},{12... | collective-permute-start | bytes 3932168 | tf_op jit(solution)/shard_map/ppermute | solution.py:819
  318.4 29.6 %collective-permute-start.89 = (f32[80,1024]{1,0:T(8,128)S(1)}, f32[80,1024]{1,0:T(8,128)S(1)}, u32[]{:S(2)}, u32[]{:S(2)}) collective-permute-start(f32[80,1024]{1,0:T(8,128)S(1)} %copy-done.12), channel_id=1, source_target_pairs={{0,1},{1,0},{2,3},{3,2},{4,5},{5,4},{6,7},{7,6},{8,9},{9,8},{10,11... | collective-permute-start | bytes 983048 | tf_op jit(solution)/shard_map/ppermute | solution.py:822
  318.7 9.1 %collective-permute-start.91 = (bf16[288,512]{1,0:T(8,128)(2,1)S(1)}, bf16[288,512]{1,0:T(8,128)(2,1)S(1)}, u32[]{:S(2)}, u32[]{:S(2)}) collective-permute-start(bf16[288,512]{1,0:T(8,128)(2,1)S(1)} %copy-done.19), channel_id=1, source_target_pairs={{0,8},{8,16},{16,24},{24,0},{1,9},{9,17},{17,25},{25,1},{2,10},{10... | collective-permute-start | bytes 884744 | tf_op jit(solution)/shard_map/ppermute | solution.py:831
  321.7 23.8 %collective-permute-start.92 = (bf16[288,512]{1,0:T(8,128)(2,1)S(1)}, bf16[288,512]{1,0:T(8,128)(2,1)S(1)}, u32[]{:S(2)}, u32[]{:S(2)}) collective-permute-start(bf16[288,512]{1,0:T(8,128)(2,1)S(1)} %copy-done.18), channel_id=1, source_target_pairs={{0,16},{8,24},{16,0},{24,8},{1,17},{9,25},{17,1},{25,9},{2,18},{10... | collective-permute-start | bytes 884744 | tf_op jit(solution)/shard_map/ppermute | solution.py:831
  325.3 22.7 %collective-permute-start.93 = (bf16[288,512]{1,0:T(8,128)(2,1)S(1)}, bf16[288,512]{1,0:T(8,128)(2,1)S(1)}, u32[]{:S(2)}, u32[]{:S(2)}) collective-permute-start(bf16[288,512]{1,0:T(8,128)(2,1)S(1)} %copy-done.17), channel_id=1, source_target_pairs={{0,24},{8,0},{16,8},{24,16},{1,25},{9,1},{17,9},{25,17},{2,26},{10... | collective-permute-start | bytes 884744 | tf_op jit(solution)/shard_map/ppermute | solution.py:831
  349.2 21.4 %collective-permute-start.101 = (bf16[2560,512]{1,0:T(8,128)(2,1)S(1)}, bf16[2560,512]{1,0:T(8,128)(2,1)S(1)}, u32[]{:S(2)}, u32[]{:S(2)}) collective-permute-start(bf16[2560,512]{1,0:T(8,128)(2,1)S(1)} %get-tuple-element.355.refs_4_), channel_id=1, source_target_pairs={{0,2},{2,0},{4,6},{6,4},{1,3},{3,1},{5,7},{7,5},{8,10},{10,8},{12,... | collective-permute-start | bytes 7864328 | tf_op jit(solution)/shard_map/ppermute | solution.py:816
  350.9 19.7 %collective-permute-start.99 = (bf16[256,512]{1,0:T(8,128)(2,1)S(1)}, bf16[256,512]{1,0:T(8,128)(2,1)S(1)}, u32[]{:S(2)}, u32[]{:S(2)}) collective-permute-start(bf16[256,512]{1,0:T(8,128)(2,1)S(1)} %get-tuple-element.350.refs_0_), channel_id=1, source_target_pairs={{0,2},{2,0},{4,6},{6,4},{1,3},{3,1},{5,7},{7,5},{8,10},{10,8},{12,... | collective-permute-start | bytes 786440 | tf_op jit(solution)/shard_map/ppermute | solution.py:816
  358.5 12.1 %collective-permute-start.100 = (bf16[256,512]{1,0:T(8,128)(2,1)S(1)}, bf16[256,512]{1,0:T(8,128)(2,1)S(1)}, u32[]{:S(2)}, u32[]{:S(2)}) collective-permute-start(bf16[256,512]{1,0:T(8,128)(2,1)S(1)} %collective-permute-done.97.refs_4_.refs_2_), channel_id=1, source_target_pairs={{0,2},{2,0},{4,6},{6,4},{1,3},{3,1},{5,7},{7,5},{8,10},{10,8},{12,... | collective-permute-start | bytes 786440 | tf_op jit(solution)/shard_map/ppermute | solution.py:816
  (81 other events, 451.1 us)
Sparse Core Ops, SparseCore 0:
  10.2 28.8 all-gather.6
  41.2 43.8 all-gather.8
  86.6 28.1 all-gather.10
  116.3 43.8 all-gather.4
  198.1 41.7 reduce-scatter.3
  242.8 26.8 reduce-scatter.7
  272.5 42.1 reduce-scatter.5

commit v9 on v8

--- a/solution.py
+++ b/solution.py
@@ -152,6 +152,78 @@
     token[...] = jnp.zeros_like(token)
 
 
+def pack_first_kernel(feats, qkv_hbm, out_hbm, gains, shifts, units, heads_ref,
+                      packed_ref, token, qkv, out, sems):
+    width_own = qkv.shape[1]
+    weights = packed_ref.at[pl.ds(0, width_own), :]
+    pack_attn_kernel(0, feats, qkv_hbm, out_hbm, weights, token, qkv, out, sems)
+    packed_ref[width_own:, :] = jnp.zeros_like(packed_ref[width_own:, :])
+    depth = gains.shape[0]
+    ci = lax.rem(lax.axis_index("ctx"), GROUP)
+    lines = [gains[l].astype(f32) for l in range(depth)]
+    lines += [shifts[l].astype(f32) for l in range(depth)]
+    for l in range(depth):
+        for first in range(0, units.shape[2], width_own):
+            lines.append(units[l, :, first : first + width_own].astype(f32))
+    lines = jnp.concatenate(lines, axis=0)
+    count = lines.shape[0]
+    packed_ref[width_own : width_own + count, :width_own] = lines.astype(bf16)
+    heads = heads_ref.shape[2] // GROUP
+    values = []
+    for l in range(depth):
+        for j in range(2):
+            rows = heads_ref[l, j].astype(f32)
+            for h in range(heads):
+                value = rows[h : h + 1, :]
+                for c in range(1, GROUP):
+                    value = jnp.where(ci == c, rows[c * heads + h : c * heads + h + 1, :], value)
+                values.append(value)
+    values = jnp.concatenate(values, axis=1)
+    packed_ref[width_own + count : width_own + count + 1, : values.shape[1]] = values.astype(bf16)
+
+
+def unpack_first_kernel(feats, head_dim, *refs):
+    *chunks, weights_ref, vecs_ref, units_ref, heads_ref = refs
+    fsdp = len(chunks)
+    width_own = weights_ref.shape[0] // fsdp
+    f = lax.axis_index("fsdp")
+    ci = lax.rem(lax.axis_index("ctx"), GROUP)
+    for d, chunk in enumerate(chunks):
+        place = lax.rem(f + (fsdp - d), fsdp)
+        span = pl.ds(pl.multiple_of(place * width_own, width_own), width_own)
+        weights_ref[span, :] = chunk[:width_own, :]
+    below = [chunk[width_own:, :].astype(f32) for chunk in chunks]
+    shard = []
+    for a in range(fsdp):
+        found = below[0]
+        for d in range(1, fsdp):
+            found = jnp.where(lax.rem(f + (fsdp - d), fsdp) == a, below[d], found)
+        shard.append(found)
+    vec_rows = vecs_ref.shape[0]
+    for a in range(fsdp):
+        vecs_ref[:, a * width_own : (a + 1) * width_own] = shard[a][:vec_rows, :width_own]
+    mine = shard[0]
+    for a in range(1, fsdp):
+        mine = jnp.where(ci == a, shard[a], mine)
+    depth = units_ref.shape[0]
+    parts = units_ref.shape[2] // width_own
+    for l in range(depth):
+        for k in range(parts):
+            row = vec_rows + l * parts + k
+            units_ref[l, :, k * width_own : (k + 1) * width_own] = mine[row : row + 1, :width_own]
+    row = vec_rows + depth * parts
+    head_own = head_dim // fsdp
+    heads = feats // head_dim
+    for l in range(depth):
+        for j in range(2):
+            pieces = []
+            for h in range(heads):
+                first = ((2 * l + j) * heads + h) * head_own
+                for a in range(fsdp):
+                    pieces.append(shard[a][row : row + 1, first : first + head_own])
+            heads_ref[l, j : j + 1, :] = jnp.concatenate(pieces, axis=1)
+
+
 def pack_mlp_kernel(layer, hidden, fc1_hbm, fc2_hbm, packed_ref, token, fc1, fc2, sems):
     ci = lax.rem(lax.axis_index("ctx"), GROUP)
     span = pl.ds(pl.multiple_of(ci * hidden, hidden), hidden)
@@ -196,14 +268,12 @@
     sent[0].wait()
 
 
-def prep_first_kernel(depth, inputs_hbm, vecs, stream_ref, first_ref, sems):
+def prep_first_kernel(inputs_hbm, stream_ref, first_ref, sems):
     rows = stream_ref.shape[0]
     start = pl.multiple_of(lax.axis_index("tp") * rows, rows)
     copies = start_copies([(inputs_hbm.at[0, pl.ds(start, rows), :], stream_ref)], sems)
     copies[0].wait()
-    normed, _ = normalize(stream_ref[...])
-    shift = vecs[2 * depth : 2 * depth + 1, :]
-    first_ref[...] = (normed * vecs[0:1, :] + shift).astype(bf16)
+    first_ref[...] = normalize(stream_ref[...])[0].astype(bf16)
 
 
 def keep_rows_kernel(*refs):
@@ -215,11 +285,19 @@
     token[...] = jnp.zeros_like(token)
 
 
-def qkv_kernel(feats, weight_count, *refs):
+def qkv_kernel(feats, weight_count, shift_row, *refs):
     c0, c1, c2, c3, *rest = refs
     weights = rest[:weight_count]
-    bias, qkv_ref, x = rest[weight_count:]
-    assemble((c0, c1, c2, c3), x)
+    if shift_row is None:
+        bias, qkv_ref, x = rest[weight_count:]
+        assemble((c0, c1, c2, c3), x)
+    else:
+        bias, vecs, qkv_ref, x = rest[weight_count:]
+        rows = c0.shape[0]
+        gain, shift = vecs[0:1, :], vecs[shift_row : shift_row + 1, :]
+        for k, chunk in enumerate((c0, c1, c2, c3)):
+            value = chunk[...].astype(f32) * gain + shift
+            x[k * rows : (k + 1) * rows, :] = value.astype(bf16)
     qkv = sum(dot(x[:, span], w[:, : 3 * feats]) for span, w in shards(weights))
     qkv_ref[:, :feats] = (qkv[:, :feats] + bias[0:1, :]).astype(bf16)
     qkv_ref[:, feats : 2 * feats] = qkv[:, feats : 2 * feats].astype(bf16)
@@ -636,11 +714,13 @@
 
 
 def place_kernel(depth, hidden, feats, *refs):
-    alone_refs, pairs, rest = refs[:GROUP], refs[GROUP : GROUP + 2], refs[GROUP + 2 :]
-    count = pairs[0].shape[0] // 2
-    slices = [
-        (alone_refs[k], pairs[k % 2].at[pl.ds(k // 2 * count, count), :]) for k in range(GROUP)
-    ]
+    alone, pairs, rest = refs[:2], refs[2:4], refs[4:]
+
+    def half_of(pair, k):
+        count = pair[k % 2].shape[0] // 2
+        return pair[k % 2].at[pl.ds(k // 2 * count, count), :]
+
+    slices = [(half_of(alone, k), half_of(pairs, k)) for k in range(GROUP)]
     qkv_hbm, out_hbm, fc1_hbm, fc2_hbm, fc1, fc2, qkv, out, sems = rest
     ci = lax.rem(lax.axis_index("ctx"), GROUP)
     rows = fc1.shape[2]
@@ -660,8 +740,8 @@
             send(fc2.at[l, k], fc2_hbm.at[l, span, :])
     for l in reversed(range(depth)):
         for k in range(GROUP):
-            alone, stacked = slices[k]
-            piece = alone if l == 0 else stacked.at[pl.ds((3 * l + 1) * rows, rows), :]
+            last, stacked = slices[k]
+            piece = last if l == 0 else stacked.at[pl.ds((3 * l + 1) * rows, rows), :]
             span = pl.ds(pl.multiple_of((ci ^ k) * feats, feats), feats)
             for j in range(3):
                 qkv[l, k, j] = piece[:, j * feats : (j + 1) * feats].astype(f32)
@@ -726,8 +806,11 @@
             lines_ref[d, :, lanes] = jnp.concatenate(rows, axis=0).astype(bf16)
 
 
-def vector_plane_kernel(depth, own, xy, x, y, out_ref):
+def vector_plane_kernel(depth, own, xy, x, y, part, part_x, out_ref, pair_ref):
     last = 6 * depth
+    rows = part.shape[0]
+    pair_ref[:rows, :] = part[...]
+    pair_ref[rows:, :] = part_x[...]
     out_ref[:last, :] = own[:last, :] + xy[:last, :] + x[:last, :] + y[:last, :]
     out_ref[16:24, :] = own[16:24, :]
     out_ref[24:32, :] = x[16:24, :]
@@ -883,45 +966,45 @@
             ],
         )
 
-    attn_w = []
-    mlp_w = []
-    token = None
+    first_own, token = kernel_call(
+        functools.partial(pack_first_kernel, feats),
+        [((width_own + 32, 4 * feats), bf16), TOKEN],
+        Far(w_qkv),
+        Far(w_out),
+        norm_gains,
+        shifts,
+        fc1_bias,
+        qv_bias,
+        name="pack_first",
+        scratch=[
+            pltpu.VMEM((3, width_own, feats), bf16),
+            pltpu.VMEM((feats, width_own), bf16),
+            DMA((2,)),
+        ],
+    )
+    first_shards = [first_own] + [shift_z(first_own, d) for d in range(1, fsdp)]
+    attn_w = [None] * depth
+    mlp_w = [None] * depth
     for l in range(depth):
-        own, token = pack_attn(l, () if token is None else (token,))
-        attn_w.append((lax.all_gather(own, "fsdp", axis=0, tiled=True),))
+        if l > 0:
+            own, token = pack_attn(l, (token,))
+            attn_w[l] = (lax.all_gather(own, "fsdp", axis=0, tiled=True),)
         own, token = pack_mlp(l, (token,))
-        mlp_w.append(lax.all_gather(own, "fsdp", axis=0, tiled=True))
+        mlp_w[l] = lax.all_gather(own, "fsdp", axis=0, tiled=True)
         if l == 0:
             pack_token = token
-
-    qv_own = lax.dynamic_slice_in_dim(qv_bias, ci * heads, heads, axis=2)
-    vec_rows = depth * 6
-    c1_rows = depth * fc1_bias.shape[2] // width_own
-    qv_own = qv_own.reshape(1, -1)
-    small_own = jnp.concatenate(
+    first_w, vecs, fc1_all, qv_all = kernel_call(
+        functools.partial(unpack_first_kernel, feats, head_dim),
         [
-            norm_gains.reshape(-1, width_own),
-            shifts.reshape(-1, width_own),
-            fc1_bias.reshape(-1, width_own),
-            jnp.pad(qv_own, ((0, 0), (0, width_own - qv_own.shape[1]))),
+            ((width, 4 * feats), bf16),
+            ((6 * depth, width), f32),
+            ((depth, 1, hidden), f32),
+            ((depth, 2, feats), f32),
         ],
-        axis=0,
-    )
-    shifted = [small_own] + [shift_z(small_own, d) for d in range(1, fsdp)]
-
-    def shard(a):
-        picked = shifted[0]
-        for d in range(1, fsdp):
-            picked = jnp.where((f - d) % fsdp == a, shifted[d], picked)
-        return picked.astype(f32)
-
-    small = [shard(a) for a in range(fsdp)]
-    vecs = jnp.concatenate([s[:vec_rows] for s in small], axis=1)
-    fc1_all = shard(ci)[vec_rows : vec_rows + c1_rows].reshape(depth, 1, hidden)
-    qv_all = jnp.stack(
-        [s[vec_rows + c1_rows, : qv_own.shape[1]].reshape(depth, 2, heads, head_own) for s in small],
-        axis=3,
-    ).reshape(depth, 2, feats)
+        *first_shards,
+        name="unpack_first",
+    )
+    attn_w[0] = (first_w,)
 
     def gain_row(l, i):
         return 2 * l + i
@@ -953,11 +1036,11 @@
     )
     upstream_chunks = [(Far(x),) for x in upstream_rows]
     stream, first = kernel_call(
-        functools.partial(prep_first_kernel, depth),
+        prep_first_kernel,
         [row_f32, row_bf16],
         Far(inputs),
-        vecs,
         name="prep_first",
+        after=(pack_token,),
         scratch=[DMA((1,))],
     )
     first_chunks = gather_rows(first)
@@ -969,11 +1052,14 @@
         first_x = []
         for side in (0, 1):
             qkv_half, x_half = kernel_call(
-                functools.partial(qkv_kernel, feats, len(attn_w[l])),
+                functools.partial(
+                    qkv_kernel, feats, len(attn_w[l]), shift_row(0, 0) if l == 0 else None
+                ),
                 [((half, 3 * feats), bf16), ((half, width), bf16)],
                 *first_chunks[side],
                 *attn_w[l],
                 qv_all[l],
+                *((vecs,) if l == 0 else ()),
                 name="qkv",
                 after=(upstream_token,) if l == 0 and side == 0 else (),
             )
@@ -990,6 +1076,8 @@
         attn = [None, None]
         for side in (1, 0):
             kept = (first_x[side], qkv[side]) + ((stream,) if side == 1 else ())
+            if l == 0 and side == 1:
+                kept += attn_w[0]
             attn[side] = kernel_call(
                 functools.partial(
                     attn_kernel, feats, heads, len(attn_w[l]), len(key_parts), len(kept), tile
@@ -1075,6 +1163,8 @@
     attn_parts = [None] * depth
     for l in reversed(range(depth)):
         attn, pairs, mlp = saved_all[l]
+        if l == 0:
+            attn_w[0] = (attn[1][6],)
         back = [None, None]
         for side in (1, 0):
             back[side] = kernel_call(
@@ -1339,21 +1429,18 @@
     )
     if outer > 1:
         part = lax.psum(part, "ctx", axis_index_groups=outer_groups)
-    part_crossed = swap_x(part)
-    pieces = [
-        *(part, swap_core(part), part_crossed, swap_core(part_crossed)),
-        *(pair, swap_core(pair)),
-    ]
-    mine = kernel_call(
+    mine, last_pair = kernel_call(
         functools.partial(vector_plane_kernel, depth),
-        [((32, width_own), f32)],
+        [((32, width_own), f32), ((2 * width_own, 4 * feats), bf16)],
         mine,
         swap_xy(mine),
         swap_x(mine),
         swap_y(mine),
+        part,
+        swap_x(part),
         name="vector_plane",
-        after=(part_crossed,),
-    )[0]
+    )
+    pieces = [last_pair, swap_core(last_pair), pair, swap_core(pair)]
     grad_gains, grad_shifts, grad_fc1_bias, grad_qv_bias = kernel_call(
         functools.partial(vector_place_kernel, depth, head_dim),
         [

time: 389 us -> 404 us (1.039)
  waiting for transfers between devices: 141 us -> 154 us
    ppermute x6, waiting for transfers between devices: 20.2 us -> 49 us  [shift_z(): lax.ppermute(value, 'fsdp', [(i, (i + d) % fsdp) for i in range(fsdp)])]
    all_gather x4 -> x3, waiting for transfers between devices: 18.1 us -> 0.01 us  [the longest x2 0.01 us: per_device(): mlp_w[l] = lax.all_gather(own, 'fsdp', axis=0, tiled=True)]
    ppermute x18, waiting for transfers between devices: 15.7 us -> 23.8 us  [swap_y(): return lax.ppermute(value, 'tp', [(i, i ^ 1) for i in range(tp)])]
    ppermute x18, waiting for transfers between devices: 36.1 us -> 29.2 us  [swap_x(): return lax.ppermute(value, 'ctx', [(i, i ^ 2) for i in range(ctx)])]
    unnamed x46 -> x47, local copies, waits for them, and re-layouts: 6.4 us -> 11 us
    ppermute x44 -> x43, starting transfers between devices: 58.3 us -> 54.6 us  [swap_core(): return lax.ppermute(value, 'ctx', [(i, i ^ 1) for i in range(ctx)])]
    pallas_call x60 -> x61, Pallas kernels: 103 us -> 104 us  [kernel_call(): pl.pallas_call(run, out_shape=out_shape, in_specs=specs, out_specs=out_sp...]
  transfers between devices with their start and end apart: 109 -> 107, of which waited for: 50 -> 49; matrix products, arithmetic and copies ran while one was open for 0% -> 0% of each run, Pallas kernels for 21% -> 20%
where the time goes in v9:
time: 404 us; the launch traced here: 398 us
  waiting for transfers between devices  154 us (38%)
  starting transfers between devices  113 us (28%)
  Pallas kernels  104 us (26%)
  between operations  15.3 us (4%)
  local copies, waits for them, and re-layouts  11 us (3%)
    pallas_call x61, Pallas kernels, kernel_call(): pl.pallas_call(run, out_shape=out_shape, in_specs=specs, out_specs=out_sp...  104 us
    ppermute x43, starting transfers between devices, swap_core(): return lax.ppermute(value, 'ctx', [(i, i ^ 1) for i in range(ctx)])  54.6 us
    ppermute x6, waiting for transfers between devices, shift_z(): lax.ppermute(value, 'fsdp', [(i, (i + d) % fsdp) for i in range(fsdp)])  49 us
    ppermute x16, waiting for transfers between devices, swap_xy(): return lax.ppermute(value, ('ctx', 'tp'), pairs)  39.4 us
    ppermute x18, waiting for transfers between devices, swap_x(): return lax.ppermute(value, 'ctx', [(i, i ^ 2) for i in range(ctx)])  29.2 us
    ppermute x18, waiting for transfers between devices, swap_y(): return lax.ppermute(value, 'tp', [(i, i ^ 1) for i in range(tp)])  23.8 us
    ppermute x16, starting transfers between devices, swap_xy(): return lax.ppermute(value, ('ctx', 'tp'), pairs)  17.8 us
    ppermute x18, starting transfers between devices, swap_y(): return lax.ppermute(value, 'tp', [(i, i ^ 1) for i in range(tp)])  14.3 us
  transfers between devices with their start and end apart: 107, of which 49 were waited for; matrix products, arithmetic and copies ran while one was open for 0% of the time, Pallas kernels for 20%

profile of v9, /device:TPU:9, one launch (start us, length us, event | category | flops | bytes accessed | tf_op | source)
XLA Modules:
  0.0 397.5 jit_solution(14043573734021631811)
XLA Ops:
  18.9 2.3 collective-permute-start.11
  21.2 2.2 collective-permute-start.10
  23.4 2.3 prep_upstream.1
  26.8 4.0 collective-permute-done.2.refs_3_
  31.1 3.3 collective-permute-start.3
  36.4 14.5 %collective-permute-done.11.refs_2_ = bf16[288,512]{1,0:T(8,128)(2,1)S(1)} collective-permute-done((bf16[288,512]{1,0:T(8,128)(2,1)S(1)}, bf16[288,512]{1,0:T(8,128)(2,1)S(1)}, u32[]{:S(2)}, u32[]{:S(2)}) %collective-permute-start.11) | collective-permute-done | bytes 294944 | tf_op jit(solution)/shard_map/ppermute | solution.py:914
  50.8 5.8 %collective-permute-start.6 = (bf16[80,1024]{1,0:T(8,128)(2,1)S(1)}, bf16[80,1024]{1,0:T(8,128)(2,1)S(1)}, u32[]{:S(2)}, u32[]{:S(2)}) collective-permute-start(bf16[80,1024]{1,0:T(8,128)(2,1)S(1)} %collective-permute-done.2.refs_3_), channel_id=1, source_target_pairs={{0,2},{2,0},{4,6},{6,4},{1,3},{3,1},{5,7},{7,5},{8,10},{10,8},{12,... | collective-permute-start | bytes 491528 | tf_op jit(solution)/shard_map/ppermute | solution.py:899
  56.7 14.3 %collective-permute-done.10.refs_1_ = bf16[288,512]{1,0:T(8,128)(2,1)S(1)} collective-permute-done((bf16[288,512]{1,0:T(8,128)(2,1)S(1)}, bf16[288,512]{1,0:T(8,128)(2,1)S(1)}, u32[]{:S(2)}, u32[]{:S(2)}) %collective-permute-start.10) | collective-permute-done | bytes 294944 | tf_op jit(solution)/shard_map/ppermute | solution.py:914
  71.0 4.2 %collective-permute-start.5 = (bf16[80,1024]{1,0:T(8,128)(2,1)S(1)}, bf16[80,1024]{1,0:T(8,128)(2,1)S(1)}, u32[]{:S(2)}, u32[]{:S(2)}) collective-permute-start(bf16[80,1024]{1,0:T(8,128)(2,1)S(1)} %collective-permute-done.1.refs_2_), channel_id=1, source_target_pairs={{0,2},{2,0},{4,6},{6,4},{1,3},{3,1},{5,7},{7,5},{8,10},{10,8},{12,... | collective-permute-start | bytes 491528 | tf_op jit(solution)/shard_map/ppermute | solution.py:899
  80.0 3.5 attn.5
  86.0 2.6 attn.4
  91.5 3.8 collective-permute-done.18.refs_1_
  95.3 2.8 collective-permute-done.19.refs_2_
  124.1 3.8 collective-permute-done.29.refs_1_
  127.9 3.0 collective-permute-done.30.refs_2_
  150.3 2.6 attn.7
  153.0 2.6 attn.6
  158.5 3.6 collective-permute-done.40.refs_1_
  162.1 2.9 collective-permute-done.41.refs_2_
  182.9 2.8 mlp.7
  185.7 3.3 mlp_back.5
  189.6 2.4 mlp.6
  192.0 2.9 mlp_back.4
  197.9 7.2 %collective-permute-done.52.refs_1_ = bf16[160,1024]{1,0:T(8,128)(2,1)S(1)} collective-permute-done((bf16[160,1024]{1,0:T(8,128)(2,1)S(1)}, bf16[160,1024]{1,0:T(8,128)(2,1)S(1)}, u32[]{:S(2)}, u32[]{:S(2)}) %collective-permute-start.52) | collective-permute-done | bytes 327712 | tf_op jit(solution)/shard_map/ppermute | solution.py:911
  205.1 6.4 %collective-permute-done.53.refs_2_ = bf16[160,1024]{1,0:T(8,128)(2,1)S(1)} collective-permute-done((bf16[160,1024]{1,0:T(8,128)(2,1)S(1)}, bf16[160,1024]{1,0:T(8,128)(2,1)S(1)}, u32[]{:S(2)}, u32[]{:S(2)}) %collective-permute-start.53) | collective-permute-done | bytes 327712 | tf_op jit(solution)/shard_map/ppermute | solution.py:902
  216.1 3.8 mlp_grad.2
  231.4 3.6 attn_back.4
  235.1 3.6 attn_back.5
  244.2 4.0 collective-permute-done.64.refs_1_
  248.2 3.0 collective-permute-done.65.refs_2_
  253.7 3.9 attn_grad.2
  270.2 2.5 mlp_back.7
  273.2 2.5 mlp_back.6
  278.5 3.9 collective-permute-done.75.refs_1_
  282.5 3.0 collective-permute-done.76.refs_2_
  288.0 4.3 %mlp_grad.3 = (bf16[1024,1024]{1,0:T(8,128)(2,1)}, bf16[80,1024]{1,0:T(8,128)(2,1)S(1)}, f32[4,1024]{1,0:T(4,128)}, f32[80,1024]{1,0:T(8,128)}) custom-call(bf16[320,1024]{1,0:T(8,128)(2,1)} %get-tuple-element.262.refs_0_, bf16[320,1024]{1,0:T(8,128)(2,1)} %get-tuple-element.263.refs_1_, bf16[320,512]{1,0:T(8,128)(2,1)} %get-tuple-element.264.refs_2_, ...), custom_call_target="tpu_custom_call" | custom-call | tf_op jit(solution)/shard_map/mlp_grad/pallas_call | solution.py:79
  303.7 3.6 attn_back.6
  307.4 3.6 attn_back.7
  316.6 4.0 collective-permute-done.86.refs_1_
  320.5 3.0 collective-permute-done.87.refs_2_
  327.0 3.9 attn_grad.3
  331.0 5.1 %reduce-scatter.6.cloned.1.call-done.refs_0_ = bf16[256,1024]{1,0:T(8,128)(2,1)} async-done(((bf16[1024,1024]{1,0:T(8,128)(2,1)}), bf16[256,1024]{1,0:T(8,128)(2,1)}) %reduce-scatter.6.cloned.1.call-update) | async-done | bytes 524304 | tf_op jit(solution)/shard_map/reduce_scatter | solution.py:1154
  340.1 3.0 collective-permute-start.91
  346.7 2.5 collective-permute-start.93
  349.2 17.7 %collective-permute-done.92.refs_4_ = bf16[288,512]{1,0:T(8,128)(2,1)S(1)} collective-permute-done((bf16[288,512]{1,0:T(8,128)(2,1)S(1)}, bf16[288,512]{1,0:T(8,128)(2,1)S(1)}, u32[]{:S(2)}, u32[]{:S(2)}) %collective-permute-start.92) | collective-permute-done | bytes 294944 | tf_op jit(solution)/shard_map/ppermute | solution.py:914
  366.9 2.5 collective-permute-done.93.refs_5_
  375.3 5.2 %collective-permute-done.95.refs_2_ = f32[24,256]{1,0:T(8,128)S(1)} collective-permute-done((f32[24,256]{1,0:T(8,128)S(1)}, f32[24,256]{1,0:T(8,128)S(1)}, u32[]{:S(2)}, u32[]{:S(2)}) %collective-permute-start.95) | collective-permute-done | bytes 24608 | tf_op jit(solution)/shard_map/ppermute | solution.py:902
  385.6 4.9 %place.1 = (f32[2,3,256,512]{3,2,1,0:T(8,128)}, f32[2,512,256]{2,1,0:T(8,128)}, f32[2,256,2048]{2,1,0:T(8,128)}, f32[2,2048,256]{2,1,0:T(8,128)}) custom-call(bf16[512,512]{1,0:T(8,128)(2,1)S(1)} %get-tuple-element.368.refs_0_, bf16[512,512]{1,0:T(8,128)(2,1)S(1)} %collective-permute-done.99.refs_1_, bf16[2560,512]{1,0:T(8,128)(2,1)S(1)} %get-tuple-element.369.refs_2_, ...), custom_call_target="tpu_custom_call" | custom-call | tf_op jit(solution)/shard_map/place/pallas_call | solution.py:79
  (282 shorter events, 176.4 us)
Async XLA Ops:
  7.2 106.5 %all-gather.6.cloned.1.call-start = ((), (), s32[]{:S(2)}) async-start(), calls=%async_computation.4 | async-start | bytes 2621440 | tf_op jit(solution)/shard_map/all_gather | solution.py:993
  13.1 132.5 %all-gather.8.cloned.1.call-start = ((), (), s32[]{:S(2)}) async-start(), calls=%async_computation.5 | async-start | bytes 1310720 | tf_op jit(solution)/shard_map/all_gather | solution.py:991
  14.9 165.0 %all-gather.4.cloned.1.call-start = ((), (), s32[]{:S(2)}) async-start(), calls=%async_computation.3 | async-start | bytes 2621440 | tf_op jit(solution)/shard_map/all_gather | solution.py:993
  16.2 10.1 %collective-permute-start.9 = (bf16[80,1024]{1,0:T(8,128)(2,1)S(1)}, bf16[80,1024]{1,0:T(8,128)(2,1)S(1)}, u32[]{:S(2)}, u32[]{:S(2)}) collective-permute-start(bf16[80,1024]{1,0:T(8,128)(2,1)S(1)} %get-tuple-element.198.refs_0_), channel_id=1, source_target_pairs={{0,1},{1,0},{2,3},{3,2},{4,5},{5,4},{6,7},{7,6},{8,9},{9,8},{10,11... | collective-permute-start | bytes 491528 | tf_op jit(solution)/shard_map/ppermute | solution.py:905
  17.5 9.1 %collective-permute-start.8 = (bf16[80,1024]{1,0:T(8,128)(2,1)S(1)}, bf16[80,1024]{1,0:T(8,128)(2,1)S(1)}, u32[]{:S(2)}, u32[]{:S(2)}) collective-permute-start(bf16[80,1024]{1,0:T(8,128)(2,1)S(1)} %get-tuple-element.198.refs_0_), channel_id=1, source_target_pairs={{0,4},{2,6},{4,0},{6,2},{1,5},{3,7},{5,1},{7,3},{8,12},{10,14},{12... | collective-permute-start | bytes 491528 | tf_op jit(solution)/shard_map/ppermute | solution.py:902
  18.7 15.7 %collective-permute-start.12 = (bf16[288,512]{1,0:T(8,128)(2,1)S(1)}, bf16[288,512]{1,0:T(8,128)(2,1)S(1)}, u32[]{:S(2)}, u32[]{:S(2)}) collective-permute-start(bf16[288,512]{1,0:T(8,128)(2,1)S(1)} %get-tuple-element.199.refs_0_), channel_id=1, source_target_pairs={{0,24},{8,0},{16,8},{24,16},{1,25},{9,1},{17,9},{25,17},{2,26},{10... | collective-permute-start | bytes 884744 | tf_op jit(solution)/shard_map/ppermute | solution.py:914
  18.9 32.0 %collective-permute-start.11 = (bf16[288,512]{1,0:T(8,128)(2,1)S(1)}, bf16[288,512]{1,0:T(8,128)(2,1)S(1)}, u32[]{:S(2)}, u32[]{:S(2)}) collective-permute-start(bf16[288,512]{1,0:T(8,128)(2,1)S(1)} %get-tuple-element.199.refs_0_), channel_id=1, source_target_pairs={{0,16},{8,24},{16,0},{24,8},{1,17},{9,25},{17,1},{25,9},{2,18},{10... | collective-permute-start | bytes 884744 | tf_op jit(solution)/shard_map/ppermute | solution.py:914
  21.2 49.8 %collective-permute-start.10 = (bf16[288,512]{1,0:T(8,128)(2,1)S(1)}, bf16[288,512]{1,0:T(8,128)(2,1)S(1)}, u32[]{:S(2)}, u32[]{:S(2)}) collective-permute-start(bf16[288,512]{1,0:T(8,128)(2,1)S(1)} %get-tuple-element.199.refs_0_), channel_id=1, source_target_pairs={{0,8},{8,16},{16,24},{24,0},{1,9},{9,17},{17,25},{25,1},{2,10},{10... | collective-permute-start | bytes 884744 | tf_op jit(solution)/shard_map/ppermute | solution.py:914
  30.8 44.6 %collective-permute-start.7 = (bf16[80,1024]{1,0:T(8,128)(2,1)S(1)}, bf16[80,1024]{1,0:T(8,128)(2,1)S(1)}, u32[]{:S(2)}, u32[]{:S(2)}) collective-permute-start(bf16[80,1024]{1,0:T(8,128)(2,1)S(1)} %get-tuple-element.198.refs_0_), channel_id=1, source_target_pairs={{0,5},{1,4},{2,7},{3,6},{4,1},{5,0},{6,3},{7,2},{8,13},{9,12},{10,... | collective-permute-start | bytes 491528 | tf_op jit(solution)/shard_map/ppermute | solution.py:911
  31.1 44.3 %collective-permute-start.3 = (bf16[80,1024]{1,0:T(8,128)(2,1)S(1)}, bf16[80,1024]{1,0:T(8,128)(2,1)S(1)}, u32[]{:S(2)}, u32[]{:S(2)}) collective-permute-start(bf16[80,1024]{1,0:T(8,128)(2,1)S(1)} %get-tuple-element.194.refs_0_), channel_id=1, source_target_pairs={{0,2},{2,0},{4,6},{6,4},{1,3},{3,1},{5,7},{7,5},{8,10},{10,8},{12,... | collective-permute-start | bytes 491528 | tf_op jit(solution)/shard_map/ppermute | solution.py:899
  34.4 41.5 %collective-permute-start = (bf16[80,1024]{1,0:T(8,128)(2,1)S(1)}, bf16[80,1024]{1,0:T(8,128)(2,1)S(1)}, u32[]{:S(2)}, u32[]{:S(2)}) collective-permute-start(bf16[80,1024]{1,0:T(8,128)(2,1)S(1)} %get-tuple-element.194.refs_0_), channel_id=1, source_target_pairs={{0,5},{1,4},{2,7},{3,6},{4,1},{5,0},{6,3},{7,2},{8,13},{9,12},{10,... | collective-permute-start | bytes 491528 | tf_op jit(solution)/shard_map/ppermute | solution.py:911
  50.8 25.2 %collective-permute-start.6 = (bf16[80,1024]{1,0:T(8,128)(2,1)S(1)}, bf16[80,1024]{1,0:T(8,128)(2,1)S(1)}, u32[]{:S(2)}, u32[]{:S(2)}) collective-permute-start(bf16[80,1024]{1,0:T(8,128)(2,1)S(1)} %collective-permute-done.2.refs_3_), channel_id=1, source_target_pairs={{0,2},{2,0},{4,6},{6,4},{1,3},{3,1},{5,7},{7,5},{8,10},{10,8},{12,... | collective-permute-start | bytes 491528 | tf_op jit(solution)/shard_map/ppermute | solution.py:899
  85.8 206.5 %reduce-scatter.4.cloned.1.call-start = ((), (), s32[]{:S(2)}) async-start(), calls=%async_computation.6 | async-start | bytes 2621440 | tf_op jit(solution)/shard_map/reduce_scatter | solution.py:1154
  89.4 8.8 %collective-permute-start.19 = (bf16[80,1024]{1,0:T(8,128)(2,1)S(1)}, bf16[80,1024]{1,0:T(8,128)(2,1)S(1)}, u32[]{:S(2)}, u32[]{:S(2)}) collective-permute-start(bf16[80,1024]{1,0:T(8,128)(2,1)S(1)} %get-tuple-element.214), channel_id=1, source_target_pairs={{0,4},{2,6},{4,0},{6,2},{1,5},{3,7},{5,1},{7,3},{8,12},{10,14},{12... | collective-permute-start | bytes 491528 | tf_op jit(solution)/shard_map/ppermute | solution.py:902
  90.6 8.8 %collective-permute-start.20 = (bf16[80,1024]{1,0:T(8,128)(2,1)S(1)}, bf16[80,1024]{1,0:T(8,128)(2,1)S(1)}, u32[]{:S(2)}, u32[]{:S(2)}) collective-permute-start(bf16[80,1024]{1,0:T(8,128)(2,1)S(1)} %get-tuple-element.215), channel_id=1, source_target_pairs={{0,1},{1,0},{2,3},{3,2},{4,5},{5,4},{6,7},{7,6},{8,9},{9,8},{10,11... | collective-permute-start | bytes 491528 | tf_op jit(solution)/shard_map/ppermute | solution.py:905
  101.6 8.8 %collective-permute-start.21 = (bf16[80,1024]{1,0:T(8,128)(2,1)S(1)}, bf16[80,1024]{1,0:T(8,128)(2,1)S(1)}, u32[]{:S(2)}, u32[]{:S(2)}) collective-permute-start(bf16[80,1024]{1,0:T(8,128)(2,1)S(1)} %get-tuple-element.217.refs_0_), channel_id=1, source_target_pairs={{0,5},{1,4},{2,7},{3,6},{4,1},{5,0},{6,3},{7,2},{8,13},{9,12},{10,... | collective-permute-start | bytes 491528 | tf_op jit(solution)/shard_map/ppermute | solution.py:911
  122.0 8.8 %collective-permute-start.30 = (bf16[80,1024]{1,0:T(8,128)(2,1)S(1)}, bf16[80,1024]{1,0:T(8,128)(2,1)S(1)}, u32[]{:S(2)}, u32[]{:S(2)}) collective-permute-start(bf16[80,1024]{1,0:T(8,128)(2,1)S(1)} %get-tuple-element.225), channel_id=1, source_target_pairs={{0,4},{2,6},{4,0},{6,2},{1,5},{3,7},{5,1},{7,3},{8,12},{10,14},{12... | collective-permute-start | bytes 491528 | tf_op jit(solution)/shard_map/ppermute | solution.py:902
  123.2 8.8 %collective-permute-start.31 = (bf16[80,1024]{1,0:T(8,128)(2,1)S(1)}, bf16[80,1024]{1,0:T(8,128)(2,1)S(1)}, u32[]{:S(2)}, u32[]{:S(2)}) collective-permute-start(bf16[80,1024]{1,0:T(8,128)(2,1)S(1)} %get-tuple-element.226), channel_id=1, source_target_pairs={{0,1},{1,0},{2,3},{3,2},{4,5},{5,4},{6,7},{7,6},{8,9},{9,8},{10,11... | collective-permute-start | bytes 491528 | tf_op jit(solution)/shard_map/ppermute | solution.py:905
  134.9 9.2 %collective-permute-start.32 = (bf16[80,1024]{1,0:T(8,128)(2,1)}, bf16[80,1024]{1,0:T(8,128)(2,1)}, u32[]{:S(2)}, u32[]{:S(2)}) collective-permute-start(bf16[80,1024]{1,0:T(8,128)(2,1)} %get-tuple-element.228.refs_0_), channel_id=1, source_target_pairs={{0,5},{1,4},{2,7},{3,6},{4,1},{5,0},{6,3},{7,2},{8,13},{9,12},{10,... | collective-permute-start | bytes 491528 | tf_op jit(solution)/shard_map/ppermute | solution.py:911
  136.7 12.0 %collective-permute-start.35 = (bf16[80,1024]{1,0:T(8,128)(2,1)}, bf16[80,1024]{1,0:T(8,128)(2,1)}, u32[]{:S(2)}, u32[]{:S(2)}) collective-permute-start(bf16[80,1024]{1,0:T(8,128)(2,1)} %get-tuple-element.228.refs_0_), channel_id=1, source_target_pairs={{0,2},{2,0},{4,6},{6,4},{1,3},{3,1},{5,7},{7,5},{8,10},{10,8},{12,... | collective-permute-start | bytes 491528 | tf_op jit(solution)/shard_map/ppermute | solution.py:899
  139.7 8.9 %collective-permute-start.38 = (bf16[80,1024]{1,0:T(8,128)(2,1)}, bf16[80,1024]{1,0:T(8,128)(2,1)}, u32[]{:S(2)}, u32[]{:S(2)}) collective-permute-start(bf16[80,1024]{1,0:T(8,128)(2,1)} %collective-permute-done.34.refs_3_), channel_id=1, source_target_pairs={{0,2},{2,0},{4,6},{6,4},{1,3},{3,1},{5,7},{7,5},{8,10},{10,8},{12,... | collective-permute-start | bytes 491528 | tf_op jit(solution)/shard_map/ppermute | solution.py:899
  169.2 9.1 %collective-permute-start.43 = (bf16[80,1024]{1,0:T(8,128)(2,1)}, bf16[80,1024]{1,0:T(8,128)(2,1)}, u32[]{:S(2)}, u32[]{:S(2)}) collective-permute-start(bf16[80,1024]{1,0:T(8,128)(2,1)} %get-tuple-element.242.refs_0_), channel_id=1, source_target_pairs={{0,5},{1,4},{2,7},{3,6},{4,1},{5,0},{6,3},{7,2},{8,13},{9,12},{10,... | collective-permute-start | bytes 491528 | tf_op jit(solution)/shard_map/ppermute | solution.py:911
  171.0 9.0 %collective-permute-start.46 = (bf16[80,1024]{1,0:T(8,128)(2,1)}, bf16[80,1024]{1,0:T(8,128)(2,1)}, u32[]{:S(2)}, u32[]{:S(2)}) collective-permute-start(bf16[80,1024]{1,0:T(8,128)(2,1)} %get-tuple-element.242.refs_0_), channel_id=1, source_target_pairs={{0,2},{2,0},{4,6},{6,4},{1,3},{3,1},{5,7},{7,5},{8,10},{10,8},{12,... | collective-permute-start | bytes 491528 | tf_op jit(solution)/shard_map/ppermute | solution.py:899
  195.2 9.9 %collective-permute-start.52 = (bf16[160,1024]{1,0:T(8,128)(2,1)S(1)}, bf16[160,1024]{1,0:T(8,128)(2,1)S(1)}, u32[]{:S(2)}, u32[]{:S(2)}) collective-permute-start(bf16[160,1024]{1,0:T(8,128)(2,1)S(1)} %get-tuple-element.252), channel_id=1, source_target_pairs={{0,5},{1,4},{2,7},{3,6},{4,1},{5,0},{6,3},{7,2},{8,13},{9,12},{10,... | collective-permute-start | bytes 983048 | tf_op jit(solution)/shard_map/ppermute | solution.py:911
  195.8 15.7 %collective-permute-start.53 = (bf16[160,1024]{1,0:T(8,128)(2,1)S(1)}, bf16[160,1024]{1,0:T(8,128)(2,1)S(1)}, u32[]{:S(2)}, u32[]{:S(2)}) collective-permute-start(bf16[160,1024]{1,0:T(8,128)(2,1)S(1)} %get-tuple-element.253), channel_id=1, source_target_pairs={{0,4},{2,6},{4,0},{6,2},{1,5},{3,7},{5,1},{7,3},{8,12},{10,14},{12... | collective-permute-start | bytes 983048 | tf_op jit(solution)/shard_map/ppermute | solution.py:902
  197.0 15.8 %collective-permute-start.54 = (bf16[160,1024]{1,0:T(8,128)(2,1)S(1)}, bf16[160,1024]{1,0:T(8,128)(2,1)S(1)}, u32[]{:S(2)}, u32[]{:S(2)}) collective-permute-start(bf16[160,1024]{1,0:T(8,128)(2,1)S(1)} %get-tuple-element.254), channel_id=1, source_target_pairs={{0,1},{1,0},{2,3},{3,2},{4,5},{5,4},{6,7},{7,6},{8,9},{9,8},{10,11... | collective-permute-start | bytes 983048 | tf_op jit(solution)/shard_map/ppermute | solution.py:905
  219.9 111.0 %reduce-scatter.8.cloned.1.call-start = ((), (), s32[]{:S(2)}) async-start(), calls=%async_computation.8 | async-start | bytes 1310720 | tf_op jit(solution)/shard_map/reduce_scatter | solution.py:1154
  220.9 8.8 %collective-permute-start.56 = (bf16[80,1024]{1,0:T(8,128)(2,1)S(1)}, bf16[80,1024]{1,0:T(8,128)(2,1)S(1)}, u32[]{:S(2)}, u32[]{:S(2)}) collective-permute-start(bf16[80,1024]{1,0:T(8,128)(2,1)S(1)} %get-tuple-element.284.refs_0_), channel_id=1, source_target_pairs={{0,5},{1,4},{2,7},{3,6},{4,1},{5,0},{6,3},{7,2},{8,13},{9,12},{10,... | collective-permute-start | bytes 491528 | tf_op jit(solution)/shard_map/ppermute | solution.py:911
  222.7 12.3 %collective-permute-start.59 = (bf16[80,1024]{1,0:T(8,128)(2,1)S(1)}, bf16[80,1024]{1,0:T(8,128)(2,1)S(1)}, u32[]{:S(2)}, u32[]{:S(2)}) collective-permute-start(bf16[80,1024]{1,0:T(8,128)(2,1)S(1)} %get-tuple-element.284.refs_0_), channel_id=1, source_target_pairs={{0,2},{2,0},{4,6},{6,4},{1,3},{3,1},{5,7},{7,5},{8,10},{10,8},{12,... | collective-permute-start | bytes 491528 | tf_op jit(solution)/shard_map/ppermute | solution.py:899
  225.3 9.7 %collective-permute-start.62 = (bf16[80,1024]{1,0:T(8,128)(2,1)S(1)}, bf16[80,1024]{1,0:T(8,128)(2,1)S(1)}, u32[]{:S(2)}, u32[]{:S(2)}) collective-permute-start(bf16[80,1024]{1,0:T(8,128)(2,1)S(1)} %collective-permute-done.58.refs_3_), channel_id=1, source_target_pairs={{0,2},{2,0},{4,6},{6,4},{1,3},{3,1},{5,7},{7,5},{8,10},{10,8},{12,... | collective-permute-start | bytes 491528 | tf_op jit(solution)/shard_map/ppermute | solution.py:899
  242.1 9.1 %collective-permute-start.65 = (bf16[80,1024]{1,0:T(8,128)(2,1)S(1)}, bf16[80,1024]{1,0:T(8,128)(2,1)S(1)}, u32[]{:S(2)}, u32[]{:S(2)}) collective-permute-start(bf16[80,1024]{1,0:T(8,128)(2,1)S(1)} %get-tuple-element.299), channel_id=1, source_target_pairs={{0,4},{2,6},{4,0},{6,2},{1,5},{3,7},{5,1},{7,3},{8,12},{10,14},{12... | collective-permute-start | bytes 491528 | tf_op jit(solution)/shard_map/ppermute | solution.py:902
  243.3 8.9 %collective-permute-start.66 = (bf16[80,1024]{1,0:T(8,128)(2,1)S(1)}, bf16[80,1024]{1,0:T(8,128)(2,1)S(1)}, u32[]{:S(2)}, u32[]{:S(2)}) collective-permute-start(bf16[80,1024]{1,0:T(8,128)(2,1)S(1)} %get-tuple-element.300), channel_id=1, source_target_pairs={{0,1},{1,0},{2,3},{3,2},{4,5},{5,4},{6,7},{7,6},{8,9},{9,8},{10,11... | collective-permute-start | bytes 491528 | tf_op jit(solution)/shard_map/ppermute | solution.py:905
  257.6 78.4 %reduce-scatter.6.cloned.1.call-start = ((), (), s32[]{:S(2)}) async-start(), calls=%async_computation.7 | async-start | bytes 2621440 | tf_op jit(solution)/shard_map/reduce_scatter | solution.py:1154
  258.7 9.0 %collective-permute-start.67 = (bf16[80,1024]{1,0:T(8,128)(2,1)S(1)}, bf16[80,1024]{1,0:T(8,128)(2,1)S(1)}, u32[]{:S(2)}, u32[]{:S(2)}) collective-permute-start(bf16[80,1024]{1,0:T(8,128)(2,1)S(1)} %get-tuple-element.305.refs_0_), channel_id=1, source_target_pairs={{0,5},{1,4},{2,7},{3,6},{4,1},{5,0},{6,3},{7,2},{8,13},{9,12},{10,... | collective-permute-start | bytes 491528 | tf_op jit(solution)/shard_map/ppermute | solution.py:911
  276.5 9.0 %collective-permute-start.76 = (bf16[80,1024]{1,0:T(8,128)(2,1)S(1)}, bf16[80,1024]{1,0:T(8,128)(2,1)S(1)}, u32[]{:S(2)}, u32[]{:S(2)}) collective-permute-start(bf16[80,1024]{1,0:T(8,128)(2,1)S(1)} %get-tuple-element.316), channel_id=1, source_target_pairs={{0,4},{2,6},{4,0},{6,2},{1,5},{3,7},{5,1},{7,3},{8,12},{10,14},{12... | collective-permute-start | bytes 491528 | tf_op jit(solution)/shard_map/ppermute | solution.py:902
  277.6 8.9 %collective-permute-start.77 = (bf16[80,1024]{1,0:T(8,128)(2,1)S(1)}, bf16[80,1024]{1,0:T(8,128)(2,1)S(1)}, u32[]{:S(2)}, u32[]{:S(2)}) collective-permute-start(bf16[80,1024]{1,0:T(8,128)(2,1)S(1)} %get-tuple-element.317), channel_id=1, source_target_pairs={{0,1},{1,0},{2,3},{3,2},{4,5},{5,4},{6,7},{7,6},{8,9},{9,8},{10,11... | collective-permute-start | bytes 491528 | tf_op jit(solution)/shard_map/ppermute | solution.py:905
  293.3 8.9 %collective-permute-start.78 = (bf16[80,1024]{1,0:T(8,128)(2,1)S(1)}, bf16[80,1024]{1,0:T(8,128)(2,1)S(1)}, u32[]{:S(2)}, u32[]{:S(2)}) collective-permute-start(bf16[80,1024]{1,0:T(8,128)(2,1)S(1)} %settle.1.refs_0_), channel_id=1, source_target_pairs={{0,5},{1,4},{2,7},{3,6},{4,1},{5,0},{6,3},{7,2},{8,13},{9,12},{10,... | collective-permute-start | bytes 491528 | tf_op jit(solution)/shard_map/ppermute | solution.py:911
  295.1 12.3 %collective-permute-start.81 = (bf16[80,1024]{1,0:T(8,128)(2,1)S(1)}, bf16[80,1024]{1,0:T(8,128)(2,1)S(1)}, u32[]{:S(2)}, u32[]{:S(2)}) collective-permute-start(bf16[80,1024]{1,0:T(8,128)(2,1)S(1)} %settle.1.refs_0_), channel_id=1, source_target_pairs={{0,2},{2,0},{4,6},{6,4},{1,3},{3,1},{5,7},{7,5},{8,10},{10,8},{12,... | collective-permute-start | bytes 491528 | tf_op jit(solution)/shard_map/ppermute | solution.py:899
  297.8 9.5 %collective-permute-start.84 = (bf16[80,1024]{1,0:T(8,128)(2,1)S(1)}, bf16[80,1024]{1,0:T(8,128)(2,1)S(1)}, u32[]{:S(2)}, u32[]{:S(2)}) collective-permute-start(bf16[80,1024]{1,0:T(8,128)(2,1)S(1)} %collective-permute-done.80.refs_3_), channel_id=1, source_target_pairs={{0,2},{2,0},{4,6},{6,4},{1,3},{3,1},{5,7},{7,5},{8,10},{10,8},{12,... | collective-permute-start | bytes 491528 | tf_op jit(solution)/shard_map/ppermute | solution.py:899
  314.6 8.9 %collective-permute-start.87 = (bf16[80,1024]{1,0:T(8,128)(2,1)S(1)}, bf16[80,1024]{1,0:T(8,128)(2,1)S(1)}, u32[]{:S(2)}, u32[]{:S(2)}) collective-permute-start(bf16[80,1024]{1,0:T(8,128)(2,1)S(1)} %get-tuple-element.339), channel_id=1, source_target_pairs={{0,4},{2,6},{4,0},{6,2},{1,5},{3,7},{5,1},{7,3},{8,12},{10,14},{12... | collective-permute-start | bytes 491528 | tf_op jit(solution)/shard_map/ppermute | solution.py:902
  315.7 8.9 %collective-permute-start.88 = (bf16[80,1024]{1,0:T(8,128)(2,1)S(1)}, bf16[80,1024]{1,0:T(8,128)(2,1)S(1)}, u32[]{:S(2)}, u32[]{:S(2)}) collective-permute-start(bf16[80,1024]{1,0:T(8,128)(2,1)S(1)} %get-tuple-element.340), channel_id=1, source_target_pairs={{0,1},{1,0},{2,3},{3,2},{4,5},{5,4},{6,7},{7,6},{8,9},{9,8},{10,11... | collective-permute-start | bytes 491528 | tf_op jit(solution)/shard_map/ppermute | solution.py:905
  337.4 32.0 %collective-permute-start.90 = (bf16[1280,512]{1,0:T(8,128)(2,1)S(1)}, bf16[1280,512]{1,0:T(8,128)(2,1)S(1)}, u32[]{:S(2)}, u32[]{:S(2)}) collective-permute-start(bf16[1280,512]{1,0:T(8,128)(2,1)S(1)} %fetch.1.refs_1_), channel_id=1, source_target_pairs={{0,4},{2,6},{4,0},{6,2},{1,5},{3,7},{5,1},{7,3},{8,12},{10,14},{12... | collective-permute-start | bytes 3932168 | tf_op jit(solution)/shard_map/ppermute | solution.py:902
  339.8 29.6 %collective-permute-start.89 = (f32[80,1024]{1,0:T(8,128)S(1)}, f32[80,1024]{1,0:T(8,128)S(1)}, u32[]{:S(2)}, u32[]{:S(2)}) collective-permute-start(f32[80,1024]{1,0:T(8,128)S(1)} %copy-done.8), channel_id=1, source_target_pairs={{0,1},{1,0},{2,3},{3,2},{4,5},{5,4},{6,7},{7,6},{8,9},{9,8},{10,11... | collective-permute-start | bytes 983048 | tf_op jit(solution)/shard_map/ppermute | solution.py:905
  340.1 9.1 %collective-permute-start.91 = (bf16[288,512]{1,0:T(8,128)(2,1)S(1)}, bf16[288,512]{1,0:T(8,128)(2,1)S(1)}, u32[]{:S(2)}, u32[]{:S(2)}) collective-permute-start(bf16[288,512]{1,0:T(8,128)(2,1)S(1)} %copy-done.22), channel_id=1, source_target_pairs={{0,8},{8,16},{16,24},{24,0},{1,9},{9,17},{17,25},{25,1},{2,10},{10... | collective-permute-start | bytes 884744 | tf_op jit(solution)/shard_map/ppermute | solution.py:914
  343.1 23.8 %collective-permute-start.92 = (bf16[288,512]{1,0:T(8,128)(2,1)S(1)}, bf16[288,512]{1,0:T(8,128)(2,1)S(1)}, u32[]{:S(2)}, u32[]{:S(2)}) collective-permute-start(bf16[288,512]{1,0:T(8,128)(2,1)S(1)} %copy-done.21), channel_id=1, source_target_pairs={{0,16},{8,24},{16,0},{24,8},{1,17},{9,25},{17,1},{25,9},{2,18},{10... | collective-permute-start | bytes 884744 | tf_op jit(solution)/shard_map/ppermute | solution.py:914
  346.7 22.7 %collective-permute-start.93 = (bf16[288,512]{1,0:T(8,128)(2,1)S(1)}, bf16[288,512]{1,0:T(8,128)(2,1)S(1)}, u32[]{:S(2)}, u32[]{:S(2)}) collective-permute-start(bf16[288,512]{1,0:T(8,128)(2,1)S(1)} %copy-done.20), channel_id=1, source_target_pairs={{0,24},{8,0},{16,8},{24,16},{1,25},{9,1},{17,9},{25,17},{2,26},{10... | collective-permute-start | bytes 884744 | tf_op jit(solution)/shard_map/ppermute | solution.py:914
  370.6 15.0 %collective-permute-start.100 = (bf16[2560,512]{1,0:T(8,128)(2,1)S(1)}, bf16[2560,512]{1,0:T(8,128)(2,1)S(1)}, u32[]{:S(2)}, u32[]{:S(2)}) collective-permute-start(bf16[2560,512]{1,0:T(8,128)(2,1)S(1)} %get-tuple-element.369.refs_2_), channel_id=1, source_target_pairs={{0,2},{2,0},{4,6},{6,4},{1,3},{3,1},{5,7},{7,5},{8,10},{10,8},{12,... | collective-permute-start | bytes 7864328 | tf_op jit(solution)/shard_map/ppermute | solution.py:899
  372.0 9.6 %collective-permute-start.97 = (bf16[256,512]{1,0:T(8,128)(2,1)S(1)}, bf16[256,512]{1,0:T(8,128)(2,1)S(1)}, u32[]{:S(2)}, u32[]{:S(2)}) collective-permute-start(bf16[256,512]{1,0:T(8,128)(2,1)S(1)} %get-tuple-element.362.refs_4_), channel_id=1, source_target_pairs={{0,4},{2,6},{4,0},{6,2},{1,5},{3,7},{5,1},{7,3},{8,12},{10,14},{12... | collective-permute-start | bytes 786440 | tf_op jit(solution)/shard_map/ppermute | solution.py:902
  (82 other events, 439.0 us)
Sparse Core Ops, SparseCore 0:
  13.2 67.5 all-gather.5
  82.3 27.7 all-gather.7
  112.3 43.8 all-gather.3
  220.1 41.3 reduce-scatter.3
  264.3 26.8 reduce-scatter.7
  293.9 42.1 reduce-scatter.5

commit v10 on v8

--- a/solution.py
+++ b/solution.py
@@ -357,23 +357,17 @@
 
 
 def mlp_back_kernel(hidden, chunk_count, *refs):
-    chunks, (w, slope_hbm, *rest) = refs[:chunk_count], refs[chunk_count:]
-    partial_ref, grad_ref, sum_hbm, x, slope, sum_ref, sems = rest
-    copies = start_copies([(slope_hbm, slope)], sems)
-    if chunk_count == 1:
-        copies += start_copies([(chunks[0], x)], sems.at[pl.ds(1, 1)])
-        copies[1].wait()
-    else:
-        assemble(chunks, x)
+    chunks, (w, slope, *rest) = refs[:chunk_count], refs[chunk_count:]
+    partial_ref, grad_ref, sum_hbm, x, sum_ref, sems = rest
+    assemble(chunks, x)
     grad = dot(x[...], w[:, hidden:])
-    copies[0].wait()
     block = hidden // 2
     for k in range(2):
         span = slice(k * block, (k + 1) * block)
         part = grad[:, span] * slope[k]
         grad_ref[:, span] = part.astype(bf16)
         sum_ref[:, span] = jnp.sum(part, axis=0, keepdims=True)
-    sent = start_copies([(sum_ref, sum_hbm)], sems.at[pl.ds(2, 1)])
+    sent = start_copies([(sum_ref, sum_hbm)], sems)
     partial_ref[...] = dot_nt(grad_ref[...], w[:, :hidden]).astype(bf16)
     sent[0].wait()
 
@@ -460,39 +454,33 @@
 def attn_back_kernel(feats, heads, weight_count, part_count, tile, carried, *refs):
     c0, c1, c2, c3, *rest = refs
     weights, rest = rest[:weight_count], rest[weight_count:]
-    usable, q_hbm, attended_hbm, norm_hbm, *rest = rest
+    usable, qkv, attended, norms, *rest = rest
     parts, rest = rest[:part_count], rest[part_count:]
     if carried:
         keys_before, values_before, *rest = rest
-    x, grad_q, grad_k, grad_v, pairs, q_ref, attended, norms, grad_att, sems = rest
+    x, grad_q, grad_k, grad_v, pairs, grad_att = rest
     head_dim = feats // heads
     scale = 1.0 / math.sqrt(head_dim)
-    moves = [(q_hbm.at[:, pl.ds(0, feats)], q_ref), (attended_hbm, attended), (norm_hbm, norms)]
     first = 0
     for part in parts:
         rows, width = part.shape
-        moves.append(
-            (part.at[:, pl.ds(width - 2 * feats, 2 * feats)], pairs.at[pl.ds(first, rows)])
-        )
+        pairs[first : first + rows, :] = part[:, width - 2 * feats :]
         first += rows
-    copies = start_copies(moves, sems)
     assemble((c0, c1, c2, c3), x)
     grad_att[...] = sum(
         dot(x[:, span], w[:, 3 * feats :]) for span, w in shards(weights)
     ).astype(bf16)
     keep = usable[...] > 0.5
-    rows = q_ref.shape[0]
+    rows = qkv.shape[0]
     if carried:
         sum_k, sum_v = keys_before[...], values_before[...]
     else:
         sum_k = jnp.zeros(grad_k.shape, f32)
         sum_v = jnp.zeros(grad_v.shape, f32)
-    for copy in copies:
-        copy.wait()
     keys, values = pairs[:, :feats], pairs[:, feats:]
     for first in range(0, rows, tile):
         span = slice(first, first + tile)
-        q = q_ref[span, :]
+        q = qkv[span, :feats]
         ga = grad_att[span, :]
         products = ga.astype(f32) * attended[span, :].astype(f32)
         gq = None
@@ -636,11 +624,13 @@
 
 
 def place_kernel(depth, hidden, feats, *refs):
-    alone_refs, pairs, rest = refs[:GROUP], refs[GROUP : GROUP + 2], refs[GROUP + 2 :]
-    count = pairs[0].shape[0] // 2
-    slices = [
-        (alone_refs[k], pairs[k % 2].at[pl.ds(k // 2 * count, count), :]) for k in range(GROUP)
-    ]
+    alone, pairs, rest = refs[:2], refs[2:4], refs[4:]
+
+    def half_of(pair, k):
+        count = pair[k % 2].shape[0] // 2
+        return pair[k % 2].at[pl.ds(k // 2 * count, count), :]
+
+    slices = [(half_of(alone, k), half_of(pairs, k)) for k in range(GROUP)]
     qkv_hbm, out_hbm, fc1_hbm, fc2_hbm, fc1, fc2, qkv, out, sems = rest
     ci = lax.rem(lax.axis_index("ctx"), GROUP)
     rows = fc1.shape[2]
@@ -660,8 +650,8 @@
             send(fc2.at[l, k], fc2_hbm.at[l, span, :])
     for l in reversed(range(depth)):
         for k in range(GROUP):
-            alone, stacked = slices[k]
-            piece = alone if l == 0 else stacked.at[pl.ds((3 * l + 1) * rows, rows), :]
+            last, stacked = slices[k]
+            piece = last if l == 0 else stacked.at[pl.ds((3 * l + 1) * rows, rows), :]
             span = pl.ds(pl.multiple_of((ci ^ k) * feats, feats), feats)
             for j in range(3):
                 qkv[l, k, j] = piece[:, j * feats : (j + 1) * feats].astype(f32)
@@ -726,8 +716,11 @@
             lines_ref[d, :, lanes] = jnp.concatenate(rows, axis=0).astype(bf16)
 
 
-def vector_plane_kernel(depth, own, xy, x, y, out_ref):
+def vector_plane_kernel(depth, own, xy, x, y, part, part_x, out_ref, pair_ref):
     last = 6 * depth
+    rows = part.shape[0]
+    pair_ref[:rows, :] = part[...]
+    pair_ref[rows:, :] = part_x[...]
     out_ref[:last, :] = own[:last, :] + xy[:last, :] + x[:last, :] + y[:last, :]
     out_ref[16:24, :] = own[16:24, :]
     out_ref[24:32, :] = x[16:24, :]
@@ -951,7 +944,7 @@
         name="keep_rows",
         scratch=[half_x, half_x, DMA((2,))],
     )
-    upstream_chunks = [(Far(x),) for x in upstream_rows]
+    upstream_chunks = [(x,) for x in upstream_rows]
     stream, first = kernel_call(
         functools.partial(prep_first_kernel, depth),
         [row_f32, row_bf16],
@@ -1044,8 +1037,6 @@
                 scratch=[pltpu.VMEM(*shape) for shape in shapes if saves]
                 + [DMA((4 + len(kept),))],
             )
-            if saves:
-                mlp[side] = [mlp[side][0], *[Far(v) for v in mlp[side][1:4]], *mlp[side][4:]]
         saved_all.append((attn, pairs if outer > 1 else None, mlp))
         if l + 1 < depth:
             (sums,) = reduce_rows((mlp[0][0], mlp[1][0]))
@@ -1089,11 +1080,7 @@
                 mlp_w[l],
                 mlp[side][3],
                 name="mlp_back",
-                scratch=[
-                    pltpu.VMEM((2, half, hidden // 2), f32),
-                    pltpu.VMEM((1, hidden), f32),
-                    DMA((3,)),
-                ],
+                scratch=[pltpu.VMEM((1, hidden), f32), DMA((1,))],
             )
         pairs_now = [(back[0][0], back[1][0])]
         if l + 1 == depth:
@@ -1184,19 +1171,15 @@
                 *middle_chunks[side],
                 *attn_w[l],
                 usable,
-                Far(attn[side][4]),
-                Far(attn[side][1]),
-                Far(attn[side][2]),
-                *[Far(part) for part in key_parts],
+                attn[side][4],
+                attn[side][1],
+                attn[side][2],
+                *key_parts,
                 *carried,
                 name="attn_back",
                 scratch=[
                     pltpu.VMEM((key_rows, 2 * feats), bf16),
                     pltpu.VMEM((half, feats), bf16),
-                    pltpu.VMEM((half, feats), bf16),
-                    pltpu.VMEM((half, feats), f32),
-                    pltpu.VMEM((half, feats), bf16),
-                    DMA((3 + len(key_parts),)),
                 ],
                 limit=attn_limit,
             )
@@ -1339,21 +1322,18 @@
     )
     if outer > 1:
         part = lax.psum(part, "ctx", axis_index_groups=outer_groups)
-    part_crossed = swap_x(part)
-    pieces = [
-        *(part, swap_core(part), part_crossed, swap_core(part_crossed)),
-        *(pair, swap_core(pair)),
-    ]
-    mine = kernel_call(
+    mine, last_pair = kernel_call(
         functools.partial(vector_plane_kernel, depth),
-        [((32, width_own), f32)],
+        [((32, width_own), f32), ((2 * width_own, 4 * feats), bf16)],
         mine,
         swap_xy(mine),
         swap_x(mine),
         swap_y(mine),
+        part,
+        swap_x(part),
         name="vector_plane",
-        after=(part_crossed,),
-    )[0]
+    )
+    pieces = [last_pair, swap_core(last_pair), pair, swap_core(pair)]
     grad_gains, grad_shifts, grad_fc1_bias, grad_qv_bias = kernel_call(
         functools.partial(vector_place_kernel, depth, head_dim),
         [

time: 389 us -> 381 us (0.979)
  Pallas kernels: 103 us -> 92.7 us
    pallas_call x60, Pallas kernels: 103 us -> 92.7 us  [kernel_call(): pl.pallas_call(run, out_shape=out_shape, in_specs=specs, out_specs=out_sp...]
    reduce_scatter x3, waiting for transfers between devices: 5.62 us -> 11.4 us  [scatter_grads(): part = lax.psum_scatter(grad, 'fsdp', scatter_dimension=0, tiled=True)]
    ppermute x44 -> x43, starting transfers between devices: 58.3 us -> 56 us  [swap_core(): return lax.ppermute(value, 'ctx', [(i, i ^ 1) for i in range(ctx)])]
    unnamed x46 -> x90, local copies, waits for them, and re-layouts: 6.4 us -> 8.24 us
  transfers between devices with their start and end apart: 109 -> 108, of which waited for: 50 -> 51; matrix products, arithmetic and copies ran while one was open for 0% -> 0% of each run, Pallas kernels for 21% -> 19%
where the time goes in v10:
time: 381 us; the launch traced here: 374 us
  waiting for transfers between devices  143 us (38%)
  starting transfers between devices  114 us (30%)
  Pallas kernels  92.7 us (24%)
  between operations  15.7 us (4%)
  local copies, waits for them, and re-layouts  8.96 us (2%)
    pallas_call x60, Pallas kernels, kernel_call(): pl.pallas_call(run, out_shape=out_shape, in_specs=specs, out_specs=out_sp...  92.7 us
    ppermute x43, starting transfers between devices, swap_core(): return lax.ppermute(value, 'ctx', [(i, i ^ 1) for i in range(ctx)])  56 us
    ppermute x16, waiting for transfers between devices, swap_xy(): return lax.ppermute(value, ('ctx', 'tp'), pairs)  37.9 us
    ppermute x18, waiting for transfers between devices, swap_x(): return lax.ppermute(value, 'ctx', [(i, i ^ 2) for i in range(ctx)])  34 us
    ppermute x6, waiting for transfers between devices, shift_z(): lax.ppermute(value, 'fsdp', [(i, (i + d) % fsdp) for i in range(fsdp)])  20.2 us
    all_gather x2, waiting for transfers between devices, per_device(): mlp_w.append(lax.all_gather(own, 'fsdp', axis=0, tiled=True))  18.3 us
    ppermute x16, starting transfers between devices, swap_xy(): return lax.ppermute(value, ('ctx', 'tp'), pairs)  17.4 us
    ppermute x18, waiting for transfers between devices, swap_y(): return lax.ppermute(value, 'tp', [(i, i ^ 1) for i in range(tp)])  15.3 us
  transfers between devices with their start and end apart: 108, of which 51 were waited for; matrix products, arithmetic and copies ran while one was open for 0% of the time, Pallas kernels for 19%

profile of v10, /device:TPU:9, one launch (start us, length us, event | category | flops | bytes accessed | tf_op | source)
XLA Modules:
  0.0 374.1 jit_solution(9596544001613740581)
XLA Ops:
  15.2 2.3 prep_upstream.1
  45.4 3.5 attn.5
  51.3 2.6 attn.4
  54.0 2.2 collective-permute-start.18
  56.8 3.6 collective-permute-done.18.refs_1_
  60.3 3.7 collective-permute-done.19.refs_2_
  72.6 2.4 collective-permute-start.26
  78.3 6.8 %all-gather.9.cloned.1.call-done.refs_4_ = bf16[1024,1024]{1,0:T(8,128)(2,1)} async-done(((bf16[256,1024]{1,0:T(8,128)(2,1)}), bf16[1024,1024]{1,0:T(8,128)(2,1)}) %all-gather.9.cloned.1.call-update) | async-done | bytes 2097168 | tf_op jit(solution)/shard_map/all_gather | solution.py:886
  94.1 3.6 collective-permute-done.29.refs_1_
  97.6 3.6 collective-permute-done.30.refs_2_
  110.0 2.3 collective-permute-start.37
  118.9 2.6 attn.7
  122.4 2.6 attn.6
  125.2 2.2 collective-permute-start.40
  127.9 4.2 %collective-permute-done.40.refs_1_ = bf16[80,1024]{1,0:T(8,128)(2,1)S(1)} collective-permute-done((bf16[80,1024]{1,0:T(8,128)(2,1)S(1)}, bf16[80,1024]{1,0:T(8,128)(2,1)S(1)}, u32[]{:S(2)}, u32[]{:S(2)}) %collective-permute-start.40) | collective-permute-done | bytes 163872 | tf_op jit(solution)/shard_map/ppermute | solution.py:821
  132.1 3.4 collective-permute-done.41.refs_2_
  143.9 2.4 collective-permute-start.48
  148.7 11.5 %all-gather.5.cloned.1.call-done.refs_4_.refs_1_ = bf16[1024,1024]{1,0:T(8,128)(2,1)} async-done(((bf16[256,1024]{1,0:T(8,128)(2,1)}), bf16[1024,1024]{1,0:T(8,128)(2,1)}) %all-gather.5.cloned.1.call-update) | async-done | bytes 2097168 | tf_op jit(solution)/shard_map/all_gather | solution.py:886
  161.8 2.8 mlp.7
  167.4 2.2 mlp.6
  171.3 2.2 collective-permute-start.52
  174.0 7.2 %collective-permute-done.52.refs_1_ = bf16[160,1024]{1,0:T(8,128)(2,1)S(1)} collective-permute-done((bf16[160,1024]{1,0:T(8,128)(2,1)S(1)}, bf16[160,1024]{1,0:T(8,128)(2,1)S(1)}, u32[]{:S(2)}, u32[]{:S(2)}) %collective-permute-start.52) | collective-permute-done | bytes 327712 | tf_op jit(solution)/shard_map/ppermute | solution.py:821
  181.2 7.0 %collective-permute-done.53.refs_2_ = bf16[160,1024]{1,0:T(8,128)(2,1)S(1)} collective-permute-done((bf16[160,1024]{1,0:T(8,128)(2,1)S(1)}, bf16[160,1024]{1,0:T(8,128)(2,1)S(1)}, u32[]{:S(2)}, u32[]{:S(2)}) %collective-permute-start.53) | collective-permute-done | bytes 327712 | tf_op jit(solution)/shard_map/ppermute | solution.py:812
  192.2 3.8 %mlp_grad.2 = (bf16[1024,1024]{1,0:T(8,128)(2,1)}, bf16[80,1024]{1,0:T(8,128)(2,1)S(1)}, f32[4,1024]{1,0:T(4,128)}, f32[80,1024]{1,0:T(8,128)}) custom-call(bf16[320,1024]{1,0:T(8,128)(2,1)S(1)} %get-tuple-element.261.refs_0_, bf16[320,1024]{1,0:T(8,128)(2,1)S(1)} %get-tuple-element.262.refs_1_, bf16[320,512]{1,0:T(8,128)(2,1)S(1)} %get-tuple-element.263.refs_2_, ...), custom_call_target="tpu_custom_call" | custom-call | tf_op jit(solution)/shard_map/mlp_grad/pallas_call | solution.py:79
  203.0 2.3 collective-permute-start.61
  207.6 2.5 attn_back.4
  210.1 2.5 attn_back.5
  218.2 3.9 %collective-permute-done.64.refs_1_ = bf16[80,1024]{1,0:T(8,128)(2,1)S(1)} collective-permute-done((bf16[80,1024]{1,0:T(8,128)(2,1)S(1)}, bf16[80,1024]{1,0:T(8,128)(2,1)S(1)}, u32[]{:S(2)}, u32[]{:S(2)}) %collective-permute-start.64) | collective-permute-done | bytes 163872 | tf_op jit(solution)/shard_map/ppermute | solution.py:821
  222.1 3.7 collective-permute-done.65.refs_2_
  227.6 4.0 %attn_grad.2 = (bf16[1024,512]{1,0:T(8,128)(2,1)}, f32[2,128]{1,0:T(2,128)}, bf16[80,1024]{1,0:T(8,128)(2,1)S(1)}, f32[2,1024]{1,0:T(2,128)}, f32[80,1024]{1,0:T(8,128)}) custom-call(bf16[320,1024]{1,0:T(8,128)(2,1)} %get-tuple-element.257.refs_0_, bf16[320,1024]{1,0:T(8,128)(2,1)} %get-tuple-element.258.refs_1_, ...), custom_call_target="tpu_custom_call" | custom-call | tf_op jit(solution)/shard_map/attn_grad/pallas_call | solution.py:79
  238.4 2.3 collective-permute-start.72
  251.5 3.7 collective-permute-done.75.refs_1_
  255.2 3.7 collective-permute-done.76.refs_2_
  261.0 4.0 %mlp_grad.3 = (bf16[1024,1024]{1,0:T(8,128)(2,1)}, bf16[80,1024]{1,0:T(8,128)(2,1)S(1)}, f32[4,1024]{1,0:T(4,128)}, f32[80,1024]{1,0:T(8,128)}) custom-call(bf16[320,1024]{1,0:T(8,128)(2,1)S(1)} %copy-done.16, bf16[320,1024]{1,0:T(8,128)(2,1)S(1)} %copy-done.15, bf16[320,512]{1,0:T(8,128)(2,1)S(1)} %copy-done.22, bf16[320,512]{1,0:T(8,128)(2,1)S(1)} %copy-done.21, ...), custom_call_target="tpu_custom_call" | custom-call | tf_op jit(solution)/shard_map/mlp_grad/pallas_call | solution.py:79
  271.9 2.3 collective-permute-start.83
  276.5 2.5 attn_back.6
  279.0 2.5 attn_back.7
  284.4 2.2 collective-permute-start.86
  287.1 3.9 %collective-permute-done.86.refs_1_ = bf16[80,1024]{1,0:T(8,128)(2,1)S(1)} collective-permute-done((bf16[80,1024]{1,0:T(8,128)(2,1)S(1)}, bf16[80,1024]{1,0:T(8,128)(2,1)S(1)}, u32[]{:S(2)}, u32[]{:S(2)}) %collective-permute-start.86) | collective-permute-done | bytes 163872 | tf_op jit(solution)/shard_map/ppermute | solution.py:821
  291.0 3.7 collective-permute-done.87.refs_2_
  297.5 3.7 attn_grad.3
  301.3 11.4 %reduce-scatter.6.cloned.1.call-done.refs_0_ = bf16[256,1024]{1,0:T(8,128)(2,1)} async-done(((bf16[1024,1024]{1,0:T(8,128)(2,1)}), bf16[256,1024]{1,0:T(8,128)(2,1)}) %reduce-scatter.6.cloned.1.call-update) | async-done | bytes 524304 | tf_op jit(solution)/shard_map/reduce_scatter | solution.py:1057
  316.7 3.0 collective-permute-start.91
  323.3 2.4 collective-permute-start.93
  325.8 17.7 %collective-permute-done.92.refs_4_ = bf16[288,512]{1,0:T(8,128)(2,1)S(1)} collective-permute-done((bf16[288,512]{1,0:T(8,128)(2,1)S(1)}, bf16[288,512]{1,0:T(8,128)(2,1)S(1)}, u32[]{:S(2)}, u32[]{:S(2)}) %collective-permute-start.92) | collective-permute-done | bytes 294944 | tf_op jit(solution)/shard_map/ppermute | solution.py:824
  343.5 2.5 collective-permute-done.93.refs_5_
  351.9 5.1 %collective-permute-done.95.refs_2_ = f32[24,256]{1,0:T(8,128)S(1)} collective-permute-done((f32[24,256]{1,0:T(8,128)S(1)}, f32[24,256]{1,0:T(8,128)S(1)}, u32[]{:S(2)}, u32[]{:S(2)}) %collective-permute-start.95) | collective-permute-done | bytes 24608 | tf_op jit(solution)/shard_map/ppermute | solution.py:812
  362.2 4.9 %place.1 = (f32[2,3,256,512]{3,2,1,0:T(8,128)}, f32[2,512,256]{2,1,0:T(8,128)}, f32[2,256,2048]{2,1,0:T(8,128)}, f32[2,2048,256]{2,1,0:T(8,128)}) custom-call(bf16[512,512]{1,0:T(8,128)(2,1)S(1)} %get-tuple-element.358.refs_0_, bf16[512,512]{1,0:T(8,128)(2,1)S(1)} %collective-permute-done.99.refs_1_, bf16[2560,512]{1,0:T(8,128)(2,1)S(1)} %get-tuple-element.359.refs_2_, ...), custom_call_target="tpu_custom_call" | custom-call | tf_op jit(solution)/shard_map/place/pallas_call | solution.py:79
  (351 shorter events, 167.6 us)
Async XLA Ops:
  7.2 34.1 %all-gather.7.cloned.1.call-start = ((), (), s32[]{:S(2)}) async-start(), calls=%async_computation.4 | async-start | bytes 1310720 | tf_op jit(solution)/shard_map/all_gather | solution.py:884
  9.0 76.0 %all-gather.9.cloned.1.call-start = ((), (), s32[]{:S(2)}) async-start(), calls=%async_computation.5 | async-start | bytes 2621440 | tf_op jit(solution)/shard_map/all_gather | solution.py:886
  11.2 103.8 %all-gather.11.cloned.1.call-start = ((), (), s32[]{:S(2)}) async-start(), calls=%async_computation.6 | async-start | bytes 1310720 | tf_op jit(solution)/shard_map/all_gather | solution.py:884
  11.4 10.9 %collective-permute-start.9 = (bf16[17,256]{1,0:T(8,128)(2,1)S(1)}, bf16[17,256]{1,0:T(8,128)(2,1)S(1)}, u32[]{:S(2)}, u32[]{:S(2)}) collective-permute-start(bf16[17,256]{1,0:T(8,128)(2,1)S(1)} %fusion.1), channel_id=1, source_target_pairs={{0,8},{8,16},{16,24},{24,0},{1,9},{9,17},{17,25},{25,1},{2,10},{10... | collective-permute-start | bytes 26120 | tf_op jit(solution)/shard_map/ppermute | solution.py:824
  12.8 10.8 %collective-permute-start.8 = (bf16[17,256]{1,0:T(8,128)(2,1)S(1)}, bf16[17,256]{1,0:T(8,128)(2,1)S(1)}, u32[]{:S(2)}, u32[]{:S(2)}) collective-permute-start(bf16[17,256]{1,0:T(8,128)(2,1)S(1)} %fusion.1), channel_id=1, source_target_pairs={{0,16},{8,24},{16,0},{24,8},{1,17},{9,25},{17,1},{25,9},{2,18},{10... | collective-permute-start | bytes 26120 | tf_op jit(solution)/shard_map/ppermute | solution.py:824
  13.9 9.9 %collective-permute-start.7 = (bf16[17,256]{1,0:T(8,128)(2,1)S(1)}, bf16[17,256]{1,0:T(8,128)(2,1)S(1)}, u32[]{:S(2)}, u32[]{:S(2)}) collective-permute-start(bf16[17,256]{1,0:T(8,128)(2,1)S(1)} %fusion.1), channel_id=1, source_target_pairs={{0,24},{8,0},{16,8},{24,16},{1,25},{9,1},{17,9},{25,17},{2,26},{10... | collective-permute-start | bytes 26120 | tf_op jit(solution)/shard_map/ppermute | solution.py:824
  17.5 9.2 %collective-permute-start.3 = (bf16[80,1024]{1,0:T(8,128)(2,1)S(1)}, bf16[80,1024]{1,0:T(8,128)(2,1)S(1)}, u32[]{:S(2)}, u32[]{:S(2)}) collective-permute-start(bf16[80,1024]{1,0:T(8,128)(2,1)S(1)} %get-tuple-element.189.refs_0_), channel_id=1, source_target_pairs={{0,2},{2,0},{4,6},{6,4},{1,3},{3,1},{5,7},{7,5},{8,10},{10,8},{12,... | collective-permute-start | bytes 491528 | tf_op jit(solution)/shard_map/ppermute | solution.py:809
  19.1 8.9 %collective-permute-start.2 = (bf16[80,1024]{1,0:T(8,128)(2,1)S(1)}, bf16[80,1024]{1,0:T(8,128)(2,1)S(1)}, u32[]{:S(2)}, u32[]{:S(2)}) collective-permute-start(bf16[80,1024]{1,0:T(8,128)(2,1)S(1)} %get-tuple-element.189.refs_0_), channel_id=1, source_target_pairs={{0,1},{1,0},{2,3},{3,2},{4,5},{5,4},{6,7},{7,6},{8,9},{9,8},{10,11... | collective-permute-start | bytes 491528 | tf_op jit(solution)/shard_map/ppermute | solution.py:815
  22.2 138.0 %all-gather.5.cloned.1.call-start = ((), (), s32[]{:S(2)}) async-start(), calls=%async_computation.3 | async-start | bytes 2621440 | tf_op jit(solution)/shard_map/all_gather | solution.py:886
  25.5 9.0 %collective-permute-start.12 = (bf16[80,1024]{1,0:T(8,128)(2,1)S(1)}, bf16[80,1024]{1,0:T(8,128)(2,1)S(1)}, u32[]{:S(2)}, u32[]{:S(2)}) collective-permute-start(bf16[80,1024]{1,0:T(8,128)(2,1)S(1)} %get-tuple-element.193.refs_0_), channel_id=1, source_target_pairs={{0,1},{1,0},{2,3},{3,2},{4,5},{5,4},{6,7},{7,6},{8,9},{9,8},{10,11... | collective-permute-start | bytes 491528 | tf_op jit(solution)/shard_map/ppermute | solution.py:815
  26.8 8.8 %collective-permute-start.11 = (bf16[80,1024]{1,0:T(8,128)(2,1)S(1)}, bf16[80,1024]{1,0:T(8,128)(2,1)S(1)}, u32[]{:S(2)}, u32[]{:S(2)}) collective-permute-start(bf16[80,1024]{1,0:T(8,128)(2,1)S(1)} %get-tuple-element.193.refs_0_), channel_id=1, source_target_pairs={{0,4},{2,6},{4,0},{6,2},{1,5},{3,7},{5,1},{7,3},{8,12},{10,14},{12... | collective-permute-start | bytes 491528 | tf_op jit(solution)/shard_map/ppermute | solution.py:812
  28.0 10.3 %collective-permute-start.10 = (bf16[80,1024]{1,0:T(8,128)(2,1)S(1)}, bf16[80,1024]{1,0:T(8,128)(2,1)S(1)}, u32[]{:S(2)}, u32[]{:S(2)}) collective-permute-start(bf16[80,1024]{1,0:T(8,128)(2,1)S(1)} %get-tuple-element.193.refs_0_), channel_id=1, source_target_pairs={{0,5},{1,4},{2,7},{3,6},{4,1},{5,0},{6,3},{7,2},{8,13},{9,12},{10,... | collective-permute-start | bytes 491528 | tf_op jit(solution)/shard_map/ppermute | solution.py:821
  28.2 11.3 %collective-permute-start.6 = (bf16[80,1024]{1,0:T(8,128)(2,1)S(1)}, bf16[80,1024]{1,0:T(8,128)(2,1)S(1)}, u32[]{:S(2)}, u32[]{:S(2)}) collective-permute-start(bf16[80,1024]{1,0:T(8,128)(2,1)S(1)} %collective-permute-done.2.refs_3_), channel_id=1, source_target_pairs={{0,2},{2,0},{4,6},{6,4},{1,3},{3,1},{5,7},{7,5},{8,10},{10,8},{12,... | collective-permute-start | bytes 491528 | tf_op jit(solution)/shard_map/ppermute | solution.py:809
  31.3 8.2 %collective-permute-start.5 = (bf16[80,1024]{1,0:T(8,128)(2,1)S(1)}, bf16[80,1024]{1,0:T(8,128)(2,1)S(1)}, u32[]{:S(2)}, u32[]{:S(2)}) collective-permute-start(bf16[80,1024]{1,0:T(8,128)(2,1)S(1)} %collective-permute-done.1.refs_2_), channel_id=1, source_target_pairs={{0,2},{2,0},{4,6},{6,4},{1,3},{3,1},{5,7},{7,5},{8,10},{10,8},{12,... | collective-permute-start | bytes 491528 | tf_op jit(solution)/shard_map/ppermute | solution.py:809
  34.4 8.6 %collective-permute-start.13 = (bf16[80,1024]{1,0:T(8,128)(2,1)S(1)}, bf16[80,1024]{1,0:T(8,128)(2,1)}, u32[]{:S(2)}, u32[]{:S(2)}) collective-permute-start(bf16[80,1024]{1,0:T(8,128)(2,1)S(1)} %get-tuple-element.193.refs_0_), channel_id=1, source_target_pairs={{0,2},{2,0},{4,6},{6,4},{1,3},{3,1},{5,7},{7,5},{8,10},{10,8},{12,... | collective-permute-start | bytes 491528 | tf_op jit(solution)/shard_map/ppermute | solution.py:809
  51.0 214.1 %reduce-scatter.4.cloned.1.call-start = ((), (), s32[]{:S(2)}) async-start(), calls=%async_computation.7 | async-start | bytes 2621440 | tf_op jit(solution)/shard_map/reduce_scatter | solution.py:1057
  56.5 8.1 %collective-permute-start.20 = (bf16[80,1024]{1,0:T(8,128)(2,1)S(1)}, bf16[80,1024]{1,0:T(8,128)(2,1)S(1)}, u32[]{:S(2)}, u32[]{:S(2)}) collective-permute-start(bf16[80,1024]{1,0:T(8,128)(2,1)S(1)} %get-tuple-element.207), channel_id=1, source_target_pairs={{0,1},{1,0},{2,3},{3,2},{4,5},{5,4},{6,7},{7,6},{8,9},{9,8},{10,11... | collective-permute-start | bytes 491528 | tf_op jit(solution)/shard_map/ppermute | solution.py:815
  68.6 8.7 %collective-permute-start.24 = (bf16[80,1024]{1,0:T(8,128)(2,1)S(1)}, bf16[80,1024]{1,0:T(8,128)(2,1)S(1)}, u32[]{:S(2)}, u32[]{:S(2)}) collective-permute-start(bf16[80,1024]{1,0:T(8,128)(2,1)S(1)} %get-tuple-element.209.refs_0_), channel_id=1, source_target_pairs={{0,2},{2,0},{4,6},{6,4},{1,3},{3,1},{5,7},{7,5},{8,10},{10,8},{12,... | collective-permute-start | bytes 491528 | tf_op jit(solution)/shard_map/ppermute | solution.py:809
  93.8 8.2 %collective-permute-start.31 = (bf16[80,1024]{1,0:T(8,128)(2,1)S(1)}, bf16[80,1024]{1,0:T(8,128)(2,1)S(1)}, u32[]{:S(2)}, u32[]{:S(2)}) collective-permute-start(bf16[80,1024]{1,0:T(8,128)(2,1)S(1)} %get-tuple-element.217), channel_id=1, source_target_pairs={{0,1},{1,0},{2,3},{3,2},{4,5},{5,4},{6,7},{7,6},{8,9},{9,8},{10,11... | collective-permute-start | bytes 491528 | tf_op jit(solution)/shard_map/ppermute | solution.py:815
  105.9 10.7 %collective-permute-start.35 = (bf16[80,1024]{1,0:T(8,128)(2,1)S(1)}, bf16[80,1024]{1,0:T(8,128)(2,1)S(1)}, u32[]{:S(2)}, u32[]{:S(2)}) collective-permute-start(bf16[80,1024]{1,0:T(8,128)(2,1)S(1)} %get-tuple-element.219.refs_0_), channel_id=1, source_target_pairs={{0,2},{2,0},{4,6},{6,4},{1,3},{3,1},{5,7},{7,5},{8,10},{10,8},{12,... | collective-permute-start | bytes 491528 | tf_op jit(solution)/shard_map/ppermute | solution.py:809
  127.4 8.2 %collective-permute-start.41 = (bf16[80,1024]{1,0:T(8,128)(2,1)S(1)}, bf16[80,1024]{1,0:T(8,128)(2,1)S(1)}, u32[]{:S(2)}, u32[]{:S(2)}) collective-permute-start(bf16[80,1024]{1,0:T(8,128)(2,1)S(1)} %get-tuple-element.230), channel_id=1, source_target_pairs={{0,4},{2,6},{4,0},{6,2},{1,5},{3,7},{5,1},{7,3},{8,12},{10,14},{12... | collective-permute-start | bytes 491528 | tf_op jit(solution)/shard_map/ppermute | solution.py:812
  127.6 8.3 %collective-permute-start.42 = (bf16[80,1024]{1,0:T(8,128)(2,1)S(1)}, bf16[80,1024]{1,0:T(8,128)(2,1)S(1)}, u32[]{:S(2)}, u32[]{:S(2)}) collective-permute-start(bf16[80,1024]{1,0:T(8,128)(2,1)S(1)} %get-tuple-element.231), channel_id=1, source_target_pairs={{0,1},{1,0},{2,3},{3,2},{4,5},{5,4},{6,7},{7,6},{8,9},{9,8},{10,11... | collective-permute-start | bytes 491528 | tf_op jit(solution)/shard_map/ppermute | solution.py:815
  139.9 20.3 %collective-permute-start.46 = (bf16[80,1024]{1,0:T(8,128)(2,1)S(1)}, bf16[80,1024]{1,0:T(8,128)(2,1)}, u32[]{:S(2)}, u32[]{:S(2)}) collective-permute-start(bf16[80,1024]{1,0:T(8,128)(2,1)S(1)} %get-tuple-element.233.refs_0_), channel_id=1, source_target_pairs={{0,2},{2,0},{4,6},{6,4},{1,3},{3,1},{5,7},{7,5},{8,10},{10,8},{12,... | collective-permute-start | bytes 491528 | tf_op jit(solution)/shard_map/ppermute | solution.py:809
  142.7 17.5 %collective-permute-start.49 = (bf16[80,1024]{1,0:T(8,128)(2,1)S(1)}, bf16[80,1024]{1,0:T(8,128)(2,1)}, u32[]{:S(2)}, u32[]{:S(2)}) collective-permute-start(bf16[80,1024]{1,0:T(8,128)(2,1)S(1)} %collective-permute-done.45.refs_3_), channel_id=1, source_target_pairs={{0,2},{2,0},{4,6},{6,4},{1,3},{3,1},{5,7},{7,5},{8,10},{10,8},{12,... | collective-permute-start | bytes 491528 | tf_op jit(solution)/shard_map/ppermute | solution.py:809
  143.9 16.3 %collective-permute-start.48 = (bf16[80,1024]{1,0:T(8,128)(2,1)}, bf16[80,1024]{1,0:T(8,128)(2,1)}, u32[]{:S(2)}, u32[]{:S(2)}) collective-permute-start(bf16[80,1024]{1,0:T(8,128)(2,1)} %collective-permute-done.44.refs_2_), channel_id=1, source_target_pairs={{0,2},{2,0},{4,6},{6,4},{1,3},{3,1},{5,7},{7,5},{8,10},{10,8},{12,... | collective-permute-start | bytes 491528 | tf_op jit(solution)/shard_map/ppermute | solution.py:809
  147.0 13.2 %collective-permute-start.47 = (bf16[80,1024]{1,0:T(8,128)(2,1)}, bf16[80,1024]{1,0:T(8,128)(2,1)}, u32[]{:S(2)}, u32[]{:S(2)}) collective-permute-start(bf16[80,1024]{1,0:T(8,128)(2,1)} %collective-permute-done.43.refs_1_), channel_id=1, source_target_pairs={{0,2},{2,0},{4,6},{6,4},{1,3},{3,1},{5,7},{7,5},{8,10},{10,8},{12,... | collective-permute-start | bytes 491528 | tf_op jit(solution)/shard_map/ppermute | solution.py:809
  171.3 9.9 %collective-permute-start.52 = (bf16[160,1024]{1,0:T(8,128)(2,1)S(1)}, bf16[160,1024]{1,0:T(8,128)(2,1)S(1)}, u32[]{:S(2)}, u32[]{:S(2)}) collective-permute-start(bf16[160,1024]{1,0:T(8,128)(2,1)S(1)} %get-tuple-element.243), channel_id=1, source_target_pairs={{0,5},{1,4},{2,7},{3,6},{4,1},{5,0},{6,3},{7,2},{8,13},{9,12},{10,... | collective-permute-start | bytes 983048 | tf_op jit(solution)/shard_map/ppermute | solution.py:821
  173.5 14.7 %collective-permute-start.53 = (bf16[160,1024]{1,0:T(8,128)(2,1)S(1)}, bf16[160,1024]{1,0:T(8,128)(2,1)S(1)}, u32[]{:S(2)}, u32[]{:S(2)}) collective-permute-start(bf16[160,1024]{1,0:T(8,128)(2,1)S(1)} %get-tuple-element.244), channel_id=1, source_target_pairs={{0,4},{2,6},{4,0},{6,2},{1,5},{3,7},{5,1},{7,3},{8,12},{10,14},{12... | collective-permute-start | bytes 983048 | tf_op jit(solution)/shard_map/ppermute | solution.py:812
  173.8 15.2 %collective-permute-start.54 = (bf16[160,1024]{1,0:T(8,128)(2,1)S(1)}, bf16[160,1024]{1,0:T(8,128)(2,1)S(1)}, u32[]{:S(2)}, u32[]{:S(2)}) collective-permute-start(bf16[160,1024]{1,0:T(8,128)(2,1)S(1)} %get-tuple-element.245), channel_id=1, source_target_pairs={{0,1},{1,0},{2,3},{3,2},{4,5},{5,4},{6,7},{7,6},{8,9},{9,8},{10,11... | collective-permute-start | bytes 983048 | tf_op jit(solution)/shard_map/ppermute | solution.py:815
  196.1 105.1 %reduce-scatter.8.cloned.1.call-start = ((), (), s32[]{:S(2)}) async-start(), calls=%async_computation.9 | async-start | bytes 1310720 | tf_op jit(solution)/shard_map/reduce_scatter | solution.py:1057
  198.9 11.1 %collective-permute-start.59 = (bf16[80,1024]{1,0:T(8,128)(2,1)S(1)}, bf16[80,1024]{1,0:T(8,128)(2,1)S(1)}, u32[]{:S(2)}, u32[]{:S(2)}) collective-permute-start(bf16[80,1024]{1,0:T(8,128)(2,1)S(1)} %get-tuple-element.275.refs_0_), channel_id=1, source_target_pairs={{0,2},{2,0},{4,6},{6,4},{1,3},{3,1},{5,7},{7,5},{8,10},{10,8},{12,... | collective-permute-start | bytes 491528 | tf_op jit(solution)/shard_map/ppermute | solution.py:809
  201.5 8.6 %collective-permute-start.62 = (bf16[80,1024]{1,0:T(8,128)(2,1)S(1)}, bf16[80,1024]{1,0:T(8,128)(2,1)S(1)}, u32[]{:S(2)}, u32[]{:S(2)}) collective-permute-start(bf16[80,1024]{1,0:T(8,128)(2,1)S(1)} %collective-permute-done.58.refs_3_), channel_id=1, source_target_pairs={{0,2},{2,0},{4,6},{6,4},{1,3},{3,1},{5,7},{7,5},{8,10},{10,8},{12,... | collective-permute-start | bytes 491528 | tf_op jit(solution)/shard_map/ppermute | solution.py:809
  217.6 8.1 %collective-permute-start.65 = (bf16[80,1024]{1,0:T(8,128)(2,1)S(1)}, bf16[80,1024]{1,0:T(8,128)(2,1)S(1)}, u32[]{:S(2)}, u32[]{:S(2)}) collective-permute-start(bf16[80,1024]{1,0:T(8,128)(2,1)S(1)} %get-tuple-element.290), channel_id=1, source_target_pairs={{0,4},{2,6},{4,0},{6,2},{1,5},{3,7},{5,1},{7,3},{8,12},{10,14},{12... | collective-permute-start | bytes 491528 | tf_op jit(solution)/shard_map/ppermute | solution.py:812
  217.9 8.2 %collective-permute-start.66 = (bf16[80,1024]{1,0:T(8,128)(2,1)S(1)}, bf16[80,1024]{1,0:T(8,128)(2,1)S(1)}, u32[]{:S(2)}, u32[]{:S(2)}) collective-permute-start(bf16[80,1024]{1,0:T(8,128)(2,1)S(1)} %get-tuple-element.291), channel_id=1, source_target_pairs={{0,1},{1,0},{2,3},{3,2},{4,5},{5,4},{6,7},{7,6},{8,9},{9,8},{10,11... | collective-permute-start | bytes 491528 | tf_op jit(solution)/shard_map/ppermute | solution.py:815
  231.6 81.0 %reduce-scatter.6.cloned.1.call-start = ((), (), s32[]{:S(2)}) async-start(), calls=%async_computation.8 | async-start | bytes 2621440 | tf_op jit(solution)/shard_map/reduce_scatter | solution.py:1057
  234.4 8.7 %collective-permute-start.70 = (bf16[80,1024]{1,0:T(8,128)(2,1)S(1)}, bf16[80,1024]{1,0:T(8,128)(2,1)S(1)}, u32[]{:S(2)}, u32[]{:S(2)}) collective-permute-start(bf16[80,1024]{1,0:T(8,128)(2,1)S(1)} %get-tuple-element.296.refs_0_), channel_id=1, source_target_pairs={{0,2},{2,0},{4,6},{6,4},{1,3},{3,1},{5,7},{7,5},{8,10},{10,8},{12,... | collective-permute-start | bytes 491528 | tf_op jit(solution)/shard_map/ppermute | solution.py:809
  251.2 8.2 %collective-permute-start.77 = (bf16[80,1024]{1,0:T(8,128)(2,1)S(1)}, bf16[80,1024]{1,0:T(8,128)(2,1)S(1)}, u32[]{:S(2)}, u32[]{:S(2)}) collective-permute-start(bf16[80,1024]{1,0:T(8,128)(2,1)S(1)} %get-tuple-element.308), channel_id=1, source_target_pairs={{0,1},{1,0},{2,3},{3,2},{4,5},{5,4},{6,7},{7,6},{8,9},{9,8},{10,11... | collective-permute-start | bytes 491528 | tf_op jit(solution)/shard_map/ppermute | solution.py:815
  267.8 11.1 %collective-permute-start.81 = (bf16[80,1024]{1,0:T(8,128)(2,1)S(1)}, bf16[80,1024]{1,0:T(8,128)(2,1)S(1)}, u32[]{:S(2)}, u32[]{:S(2)}) collective-permute-start(bf16[80,1024]{1,0:T(8,128)(2,1)S(1)} %settle.1.refs_0_), channel_id=1, source_target_pairs={{0,2},{2,0},{4,6},{6,4},{1,3},{3,1},{5,7},{7,5},{8,10},{10,8},{12,... | collective-permute-start | bytes 491528 | tf_op jit(solution)/shard_map/ppermute | solution.py:809
  270.5 8.5 %collective-permute-start.84 = (bf16[80,1024]{1,0:T(8,128)(2,1)S(1)}, bf16[80,1024]{1,0:T(8,128)(2,1)S(1)}, u32[]{:S(2)}, u32[]{:S(2)}) collective-permute-start(bf16[80,1024]{1,0:T(8,128)(2,1)S(1)} %collective-permute-done.80.refs_3_), channel_id=1, source_target_pairs={{0,2},{2,0},{4,6},{6,4},{1,3},{3,1},{5,7},{7,5},{8,10},{10,8},{12,... | collective-permute-start | bytes 491528 | tf_op jit(solution)/shard_map/ppermute | solution.py:809
  286.6 8.1 %collective-permute-start.87 = (bf16[80,1024]{1,0:T(8,128)(2,1)S(1)}, bf16[80,1024]{1,0:T(8,128)(2,1)S(1)}, u32[]{:S(2)}, u32[]{:S(2)}) collective-permute-start(bf16[80,1024]{1,0:T(8,128)(2,1)S(1)} %get-tuple-element.329), channel_id=1, source_target_pairs={{0,4},{2,6},{4,0},{6,2},{1,5},{3,7},{5,1},{7,3},{8,12},{10,14},{12... | collective-permute-start | bytes 491528 | tf_op jit(solution)/shard_map/ppermute | solution.py:812
  286.9 8.2 %collective-permute-start.88 = (bf16[80,1024]{1,0:T(8,128)(2,1)S(1)}, bf16[80,1024]{1,0:T(8,128)(2,1)S(1)}, u32[]{:S(2)}, u32[]{:S(2)}) collective-permute-start(bf16[80,1024]{1,0:T(8,128)(2,1)S(1)} %get-tuple-element.330), channel_id=1, source_target_pairs={{0,1},{1,0},{2,3},{3,2},{4,5},{5,4},{6,7},{7,6},{8,9},{9,8},{10,11... | collective-permute-start | bytes 491528 | tf_op jit(solution)/shard_map/ppermute | solution.py:815
  314.0 32.0 %collective-permute-start.90 = (bf16[1280,512]{1,0:T(8,128)(2,1)S(1)}, bf16[1280,512]{1,0:T(8,128)(2,1)S(1)}, u32[]{:S(2)}, u32[]{:S(2)}) collective-permute-start(bf16[1280,512]{1,0:T(8,128)(2,1)S(1)} %fetch.1.refs_1_), channel_id=1, source_target_pairs={{0,4},{2,6},{4,0},{6,2},{1,5},{3,7},{5,1},{7,3},{8,12},{10,14},{12... | collective-permute-start | bytes 3932168 | tf_op jit(solution)/shard_map/ppermute | solution.py:812
  316.4 29.6 %collective-permute-start.89 = (f32[80,1024]{1,0:T(8,128)S(1)}, f32[80,1024]{1,0:T(8,128)S(1)}, u32[]{:S(2)}, u32[]{:S(2)}) collective-permute-start(f32[80,1024]{1,0:T(8,128)S(1)} %copy-done.24), channel_id=1, source_target_pairs={{0,1},{1,0},{2,3},{3,2},{4,5},{5,4},{6,7},{7,6},{8,9},{9,8},{10,11... | collective-permute-start | bytes 983048 | tf_op jit(solution)/shard_map/ppermute | solution.py:815
  316.7 9.1 %collective-permute-start.91 = (bf16[288,512]{1,0:T(8,128)(2,1)S(1)}, bf16[288,512]{1,0:T(8,128)(2,1)S(1)}, u32[]{:S(2)}, u32[]{:S(2)}) collective-permute-start(bf16[288,512]{1,0:T(8,128)(2,1)S(1)} %copy-done.41), channel_id=1, source_target_pairs={{0,8},{8,16},{16,24},{24,0},{1,9},{9,17},{17,25},{25,1},{2,10},{10... | collective-permute-start | bytes 884744 | tf_op jit(solution)/shard_map/ppermute | solution.py:824
  319.7 23.8 %collective-permute-start.92 = (bf16[288,512]{1,0:T(8,128)(2,1)S(1)}, bf16[288,512]{1,0:T(8,128)(2,1)S(1)}, u32[]{:S(2)}, u32[]{:S(2)}) collective-permute-start(bf16[288,512]{1,0:T(8,128)(2,1)S(1)} %copy-done.40), channel_id=1, source_target_pairs={{0,16},{8,24},{16,0},{24,8},{1,17},{9,25},{17,1},{25,9},{2,18},{10... | collective-permute-start | bytes 884744 | tf_op jit(solution)/shard_map/ppermute | solution.py:824
  323.3 22.7 %collective-permute-start.93 = (bf16[288,512]{1,0:T(8,128)(2,1)S(1)}, bf16[288,512]{1,0:T(8,128)(2,1)S(1)}, u32[]{:S(2)}, u32[]{:S(2)}) collective-permute-start(bf16[288,512]{1,0:T(8,128)(2,1)S(1)} %copy-done.39), channel_id=1, source_target_pairs={{0,24},{8,0},{16,8},{24,16},{1,25},{9,1},{17,9},{25,17},{2,26},{10... | collective-permute-start | bytes 884744 | tf_op jit(solution)/shard_map/ppermute | solution.py:824
  347.1 15.0 %collective-permute-start.100 = (bf16[2560,512]{1,0:T(8,128)(2,1)S(1)}, bf16[2560,512]{1,0:T(8,128)(2,1)S(1)}, u32[]{:S(2)}, u32[]{:S(2)}) collective-permute-start(bf16[2560,512]{1,0:T(8,128)(2,1)S(1)} %get-tuple-element.359.refs_2_), channel_id=1, source_target_pairs={{0,2},{2,0},{4,6},{6,4},{1,3},{3,1},{5,7},{7,5},{8,10},{10,8},{12,... | collective-permute-start | bytes 7864328 | tf_op jit(solution)/shard_map/ppermute | solution.py:809
  348.6 9.6 %collective-permute-start.97 = (bf16[256,512]{1,0:T(8,128)(2,1)S(1)}, bf16[256,512]{1,0:T(8,128)(2,1)S(1)}, u32[]{:S(2)}, u32[]{:S(2)}) collective-permute-start(bf16[256,512]{1,0:T(8,128)(2,1)S(1)} %get-tuple-element.352.refs_4_), channel_id=1, source_target_pairs={{0,4},{2,6},{4,0},{6,2},{1,5},{3,7},{5,1},{7,3},{8,12},{10,14},{12... | collective-permute-start | bytes 786440 | tf_op jit(solution)/shard_map/ppermute | solution.py:812
  (102 other events, 883.4 us)
Sparse Core Ops, SparseCore 0:
  10.2 28.8 all-gather.6
  41.2 43.8 all-gather.8
  86.6 28.2 all-gather.10
  116.3 43.8 all-gather.4
  196.3 41.6 reduce-scatter.3
  240.7 26.8 reduce-scatter.7
  270.5 42.1 reduce-scatter.5

commit v11 on v10

--- a/solution.py
+++ b/solution.py
@@ -324,10 +324,16 @@
         copy.wait()
 
 
-def mlp_kernel(hidden, keep_count, saves, c0, c1, c2, c3, w, bias, *refs):
+def mlp_kernel(hidden, keep_count, saves, loads, c0, c1, c2, c3, w, bias, *refs):
     kept, rest = refs[:keep_count], refs[keep_count:]
     partial_ref, x_out, act_out, slope_out, *rest = rest
     kept_hbm, rest = rest[:keep_count], rest[keep_count:]
+    loaded = []
+    if loads:
+        *rest, w_ref, w_sems = rest
+        spans = (pl.ds(0, hidden), pl.ds(hidden, hidden))
+        loaded = start_copies([(w.at[:, c], w_ref.at[:, c]) for c in spans], w_sems)
+        w = w_ref
     if saves:
         x, act_ref, slope_ref, sems = rest
     else:
@@ -338,6 +344,8 @@
     if saves:
         copies += start_copies([(x, x_out)], sems.at[pl.ds(keep_count, 1)])
     block = hidden // 2
+    if loads:
+        loaded[0].wait()
     for k in range(2):
         span = slice(k * block, (k + 1) * block)
         pre = dot(x[...], w[:, span]) + bias[:, span]
@@ -351,6 +359,8 @@
             )
     if saves:
         copies += start_copies([(act_ref, act_out)], sems.at[pl.ds(3 + keep_count, 1)])
+    if loads:
+        loaded[1].wait()
     partial_ref[...] = dot_nt(act_ref[...], w[:, hidden:]).astype(bf16)
     for copy in copies:
         copy.wait()
@@ -373,35 +383,16 @@
 
 
 def mlp_grad_kernel(hidden, second_near, second_far, act_near, act_far, up_near, up_far,
-                    grad_near, grad_far, passed, sums, middle, out_hbm, passed_ref, sums_hbm,
-                    middle_hbm, second, act, up, grad, out_one, out_two, sems):
-    rows = up_near.shape[0]
-    sent = start_copies([(sums, sums_hbm), (middle, middle_hbm)], sems.at[pl.ds(6, 2)])
-    near, far = pl.ds(0, rows), pl.ds(rows, rows)
-    copies = start_copies(
-        [
-            (act_near, act.at[near]),
-            (act_far, act.at[far]),
-            (second_near, second.at[near]),
-            (second_far, second.at[far]),
-        ],
-        sems,
-    )
-    passed_ref[...] = passed[...]
-    up[:rows, :] = up_near[...]
-    up[rows:, :] = up_far[...]
-    grad[:rows, :] = grad_near[...]
-    grad[rows:, :] = grad_far[...]
-    for copy in copies[:2]:
-        copy.wait()
-    out_two[...] = dot_tn(up[...], act[...]).astype(bf16)
-    sent += start_copies(
-        [(out_two, out_hbm.at[:, pl.ds(hidden, hidden)])], sems.at[pl.ds(4, 1)]
-    )
-    for copy in copies[2:]:
-        copy.wait()
-    out_one[...] = dot_tn(second[...], grad[...]).astype(bf16)
-    sent += start_copies([(out_one, out_hbm.at[:, pl.ds(0, hidden)])], sems.at[pl.ds(5, 1)])
+                    grad_near, grad_far, out_hbm, token, out_one, out_two, sems):
+    token[...] = jnp.zeros_like(token)
+    total = dot_tn(up_near[...], act_near[...]) + dot_tn(up_far[...], act_far[...])
+    out_two[...] = total.astype(bf16)
+    sent = start_copies(
+        [(out_two, out_hbm.at[:, pl.ds(hidden, hidden)])], sems.at[pl.ds(0, 1)]
+    )
+    total = dot_tn(second_near[...], grad_near[...]) + dot_tn(second_far[...], grad_far[...])
+    out_one[...] = total.astype(bf16)
+    sent += start_copies([(out_one, out_hbm.at[:, pl.ds(0, hidden)])], sems.at[pl.ds(1, 1)])
     for copy in sent:
         copy.wait()
 
@@ -514,26 +505,16 @@
         partial_ref[:, columns] = dot_nt(packed[...], w[:, : 3 * feats]).astype(bf16)
 
 
-def attn_grad_kernel(feats, count, first_near, first_far, att_near, att_far, up_near, up_far,
-                     gq_near, gq_far, gk, gv, passed, sums, stream, lines, *refs):
-    outs, rest = refs[:count], refs[count:]
-    heads_hbm, passed_ref, sums_hbm, stream_hbm, *rest = rest
-    first, att, up, packed, sums_ref, *staged, sems = rest
+def attn_grad_kernel(feats, count, keep_count, first_near, first_far, att_near, att_far,
+                     up_near, up_far, gq_near, gq_far, gk, gv, passed, lines, *refs):
+    kept, refs = refs[:keep_count], refs[keep_count:]
+    outs, refs = refs[:count], refs[count:]
+    heads_hbm, passed_ref, *refs = refs
+    kept_hbm, (packed, sums_ref, *staged, sems) = refs[:keep_count], refs[keep_count:]
     rows = up_near.shape[0]
-    sent = start_copies([(sums, sums_hbm), (stream, stream_hbm)], sems.at[pl.ds(6, 2)])
-    near, far = pl.ds(0, rows), pl.ds(rows, rows)
-    copies = start_copies(
-        [
-            (att_near, att.at[near]),
-            (att_far, att.at[far]),
-            (first_near, first.at[near]),
-            (first_far, first.at[far]),
-        ],
-        sems,
-    )
+    used = count + 2
+    sent = start_copies(list(zip(kept, kept_hbm)), sems.at[pl.ds(used, keep_count)])
     passed_ref[...] = passed[...]
-    up[:rows, :] = up_near[...]
-    up[rows:, :] = up_far[...]
     packed[:rows, :feats] = gq_near[...].astype(bf16)
     packed[rows:, :feats] = gq_far[...].astype(bf16)
     packed[:, feats : 2 * feats] = gk[...].astype(bf16)
@@ -542,43 +523,49 @@
         gq_far[...], axis=0, keepdims=True
     )
     sums_ref[1:2, :] = jnp.sum(gv[...], axis=0, keepdims=True)
-    sent += start_copies([(sums_ref, heads_hbm)], sems.at[pl.ds(8, 1)])
+    sent += start_copies([(sums_ref, heads_hbm)], sems.at[pl.ds(0, 1)])
+
+    def out_part(span):
+        return dot_tn(up_near[:, span], att_near[...]) + dot_tn(up_far[:, span], att_far[...])
+
+    def qkv_part(span):
+        return dot_tn(first_near[:, span], packed[:rows, :]) + dot_tn(
+            first_far[:, span], packed[rows:, :]
+        )
+
     if count == 1:
         out_one, out_two = staged
-        for copy in copies[:2]:
-            copy.wait()
-        out_two[...] = dot_tn(up[...], att[...]).astype(bf16)
+        whole = slice(None)
+        out_two[...] = out_part(whole).astype(bf16)
         sent += start_copies(
-            [(out_two, outs[0].at[:, pl.ds(3 * feats, feats)])], sems.at[pl.ds(4, 1)]
+            [(out_two, outs[0].at[:, pl.ds(3 * feats, feats)])], sems.at[pl.ds(1, 1)]
         )
-        for copy in copies[2:]:
-            copy.wait()
-        out_one[...] = dot_tn(first[...], packed[...]).astype(bf16)
+        out_one[...] = qkv_part(whole).astype(bf16)
         sent += start_copies(
-            [(out_one, outs[0].at[:, pl.ds(0, 3 * feats)])], sems.at[pl.ds(5, 1)]
+            [(out_one, outs[0].at[:, pl.ds(0, 3 * feats)])], sems.at[pl.ds(2, 1)]
         )
-        for copy in sent:
-            copy.wait()
-        return
-    (stage,) = staged
+    else:
+        (stage,) = staged
+        below = lines.shape[1]
+        width_own = outs[0].shape[0] - below
+        for d in reversed(range(count)):
+            place = lax.rem(lax.axis_index("fsdp") + d, count)
+            span = pl.ds(pl.multiple_of(place * width_own, width_own), width_own)
+            stage[d, :width_own, : 3 * feats] = qkv_part(span).astype(bf16)
+            stage[d, :width_own, 3 * feats :] = out_part(span).astype(bf16)
+            stage[d, width_own:, :] = lines[d]
+            sent += start_copies([(stage.at[d], outs[d])], sems.at[pl.ds(1 + d, 1)])
+    for copy in sent:
+        copy.wait()
+
+
+def settle_kernel(keep_count, after_count, passed, *refs):
+    kept, refs = refs[:keep_count], refs[keep_count + after_count :]
+    passed_ref, *kept_hbm, sems = refs
+    copies = start_copies(list(zip(kept, kept_hbm)), sems)
+    passed_ref[...] = passed[...]
     for copy in copies:
         copy.wait()
-    below = lines.shape[1]
-    width_own = outs[0].shape[0] - below
-    for d in reversed(range(count)):
-        place = lax.rem(lax.axis_index("fsdp") + d, count)
-        span = pl.ds(pl.multiple_of(place * width_own, width_own), width_own)
-        stage[d, :width_own, : 3 * feats] = dot_tn(first[:, span], packed[...]).astype(bf16)
-        stage[d, :width_own, 3 * feats :] = dot_tn(up[:, span], att[...]).astype(bf16)
-        stage[d, width_own:, :] = lines[d]
-        sent += start_copies([(stage.at[d], outs[d])], sems.at[pl.ds(9 + d, 1)])
-    for copy in sent:
-        copy.wait()
-
-
-def settle_kernel(passed, *refs):
-    passed_ref = refs[-1]
-    passed_ref[...] = passed[...]
 
 
 def fetch_kernel(count, *refs):
@@ -829,10 +816,16 @@
         near = (own, swap_xy(own), swap_x(own), swap_y(own))
         return near, tuple(swap_core(chunk) for chunk in near)
 
-    def settle(value, *after):
+    def settle(value, there, *kept):
         return kernel_call(
-            settle_kernel, [(value.shape, value.dtype)], value, name="settle", after=after
-        )[0]
+            functools.partial(settle_kernel, len(kept), 1),
+            [(value.shape, value.dtype)] + [saved(k.shape, k.dtype) for k in kept],
+            value,
+            *kept,
+            Far(there),
+            name="settle",
+            scratch=[DMA((max(1, len(kept)),))],
+        )
 
     def reduce_rows(*pairs, after=()):
         count = len(pairs)
@@ -1019,23 +1012,25 @@
         for side in (1, 0):
             kept = (middle,) if side == 1 else ()
             saves = l + 1 < depth
+            loads = not saves and side == 1
             shapes = [
                 ((half, width), bf16),
                 ((half, hidden), bf16),
                 ((2, half, hidden // 2), f32),
             ]
             mlp[side] = kernel_call(
-                functools.partial(mlp_kernel, hidden, len(kept), saves),
+                functools.partial(mlp_kernel, hidden, len(kept), saves, loads),
                 [partial_out]
                 + [saved(*shape) if saves else shape for shape in shapes]
                 + [saved(k.shape, k.dtype) for k in kept],
                 *second_chunks[side],
-                mlp_w[l],
+                Far(mlp_w[l]) if loads else mlp_w[l],
                 fc1_all[l],
                 *kept,
                 name="mlp",
                 scratch=[pltpu.VMEM(*shape) for shape in shapes if saves]
-                + [DMA((4 + len(kept),))],
+                + [DMA((4 + len(kept),))]
+                + ([pltpu.VMEM((width, 2 * hidden), bf16), DMA((2,))] if loads else []),
             )
         saved_all.append((attn, pairs if outer > 1 else None, mlp))
         if l + 1 < depth:
@@ -1082,10 +1077,29 @@
                 name="mlp_back",
                 scratch=[pltpu.VMEM((1, hidden), f32), DMA((1,))],
             )
+        mlp_grad, token = kernel_call(
+            functools.partial(mlp_grad_kernel, hidden),
+            [saved((width, 2 * hidden), bf16), TOKEN],
+            mlp[0][1],
+            mlp[1][1],
+            mlp[0][2],
+            mlp[1][2],
+            back[0][3],
+            back[1][3],
+            back[0][1],
+            back[1][1],
+            name="mlp_grad",
+            scratch=[
+                pltpu.VMEM((width, hidden), bf16),
+                pltpu.VMEM((width, hidden), bf16),
+                DMA((2,)),
+            ],
+        )
+        mlp_parts[l] = scatter_grads(mlp_grad)
         pairs_now = [(back[0][0], back[1][0])]
         if l + 1 == depth:
             pairs_now.append((mlp[0][0], mlp[1][0]))
-        sums, *output_sums = reduce_rows(*pairs_now)
+        sums, *output_sums = reduce_rows(*pairs_now, after=(token,))
         if l + 1 == depth:
             outputs_own, output_token = kernel_call(
                 functools.partial(sum_out_kernel, shift_row(l, 3)),
@@ -1109,43 +1123,13 @@
             Far(upstream),
             vecs,
             name="norm_back_two",
+            after=after,
             scratch=[pltpu.VMEM((rows, width), f32)] * 2 + [DMA((2,))],
         )
-        mlp_grad, middle_b, sums_two, grad_middle = kernel_call(
-            functools.partial(mlp_grad_kernel, hidden),
-            [
-                saved((width, 2 * hidden), bf16),
-                row_bf16,
-                saved((4, width), f32),
-                saved((rows, width), f32),
-            ],
-            mlp[0][1],
-            mlp[1][1],
-            mlp[0][2],
-            mlp[1][2],
-            back[0][3],
-            back[1][3],
-            back[0][1],
-            back[1][1],
-            middle_b,
-            sums_two,
-            grad_middle,
-            name="mlp_grad",
-            after=after,
-            scratch=[
-                pltpu.VMEM((all_rows, width), bf16),
-                pltpu.VMEM((all_rows, hidden), bf16),
-                pltpu.VMEM((all_rows, width), bf16),
-                pltpu.VMEM((all_rows, hidden), bf16),
-                pltpu.VMEM((width, hidden), bf16),
-                pltpu.VMEM((width, hidden), bf16),
-                DMA((8,)),
-            ],
-            limit=16,
-        )
-        mlp_parts[l] = scatter_grads(mlp_grad)
         if l + 1 < depth:
-            middle_b = settle(middle_b, Far(mlp_parts[l + 1]))
+            middle_b, sums_two, grad_middle = settle(
+                middle_b, attn_parts[l + 1], sums_two, grad_middle
+            )
         middle_chunks = gather_rows(middle_b)
         grad_q = [None, None]
         middle_x = [None, None]
@@ -1219,7 +1203,7 @@
             [row_f32, row_bf16, ((2, width), f32)],
             *sums,
             Far(attn[1][5]),
-            Far(grad_middle),
+            Far(grad_middle) if l + 1 < depth else grad_middle,
             vecs,
             *masked,
             name="norm_back_one",
@@ -1252,40 +1236,39 @@
         shapes = [((width, 3 * feats), bf16), ((width, feats), bf16)]
         if l == 0:
             shapes = [((fsdp, width_own + 32, 4 * feats), bf16)]
-        *attn_grads, head_sums[l], upstream_b, sums_one, upstream = kernel_call(
-            functools.partial(attn_grad_kernel, feats, count),
-            [saved((width if l > 0 else width_own + 32, 4 * feats), bf16)] * count
-            + [
-                saved((2, feats), f32),
-                row_bf16,
-                saved((2, width), f32),
-                saved((rows, width), f32),
-            ],
-            Far(attn[0][3]),
-            Far(attn[1][3]),
-            Far(attn[0][1]),
-            Far(attn[1][1]),
-            *middle_x,
-            *grad_q,
-            grad_k,
-            grad_v,
-            upstream_b,
-            sums_one,
-            upstream,
-            *(lines or (sums_one,)),
-            name="attn_grad",
-            scratch=[
-                pltpu.VMEM((all_rows, width), bf16),
-                pltpu.VMEM((all_rows, feats), bf16),
-                pltpu.VMEM((all_rows, width), bf16),
-                pltpu.VMEM((all_rows, 3 * feats), bf16),
-                pltpu.VMEM((2, feats), f32),
-            ]
-            + [pltpu.VMEM(*shape) for shape in shapes]
-            + [DMA((9 + count,))],
-        )
+        kept = [sums_one, upstream] + ([sums_two] if l + 1 == depth else [])
+        *attn_grads, head_sums[l], upstream_b, sums_one, upstream, sums_kept = [
+            *kernel_call(
+                functools.partial(attn_grad_kernel, feats, count, len(kept)),
+                [saved((width if l > 0 else width_own + 32, 4 * feats), bf16)] * count
+                + [saved((2, feats), f32), row_bf16]
+                + [saved(k.shape, k.dtype) for k in kept],
+                attn[0][3],
+                attn[1][3],
+                attn[0][1],
+                attn[1][1],
+                *middle_x,
+                *grad_q,
+                grad_k,
+                grad_v,
+                upstream_b,
+                *(lines or (sums_one,)),
+                *kept,
+                name="attn_grad",
+                scratch=[
+                    pltpu.VMEM((all_rows, 3 * feats), bf16),
+                    pltpu.VMEM((2, feats), f32),
+                ]
+                + [pltpu.VMEM(*shape) for shape in shapes]
+                + [DMA((count + 2 + len(kept),))],
+            ),
+            sums_two,
+        ][: count + 5]
+        if l + 1 == depth:
+            sums_two = sums_kept
         if l > 0:
             attn_parts[l] = scatter_grads(attn_grads[0])
+            (upstream_b,) = settle(upstream_b, mlp_parts[l])
             upstream_chunks = gather_rows(upstream_b)
         row_sums[l] = (sums_one, sums_two)
 

time: 381 us -> 377 us (0.990)
  waiting for transfers between devices: 143 us -> 136 us
  local copies, waits for them, and re-layouts: 8.96 us -> 14.7 us
    reduce_scatter x3, waiting for transfers between devices: 11.4 us -> 0.66 us  [scatter_grads(): part = lax.psum_scatter(grad, 'fsdp', scatter_dimension=0, tiled=True)]
    unnamed x90 -> x114, local copies, waits for them, and re-layouts: 8.24 us -> 14 us
    pallas_call x60 -> x61, Pallas kernels: 92.7 us -> 91.2 us  [kernel_call(): pl.pallas_call(run, out_shape=out_shape, in_specs=specs, out_specs=out_sp...]
  transfers between devices with their start and end apart: 108 -> 108, of which waited for: 51 -> 51; matrix products, arithmetic and copies ran while one was open for 0% -> 0% of each run, Pallas kernels for 19% -> 20%
where the time goes in v11:
time: 377 us; the launch traced here: 370 us
  waiting for transfers between devices  136 us (36%)
  starting transfers between devices  112 us (30%)
  Pallas kernels  91.2 us (24%)
  between operations  15.8 us (4%)
  local copies, waits for them, and re-layouts  14.7 us (4%)
    pallas_call x61, Pallas kernels, kernel_call(): pl.pallas_call(run, out_shape=out_shape, in_specs=specs, out_specs=out_sp...  91.2 us
    ppermute x43, starting transfers between devices, swap_core(): return lax.ppermute(value, 'ctx', [(i, i ^ 1) for i in range(ctx)])  55.7 us
    ppermute x16, waiting for transfers between devices, swap_xy(): return lax.ppermute(value, ('ctx', 'tp'), pairs)  38.1 us
    ppermute x18, waiting for transfers between devices, swap_x(): return lax.ppermute(value, 'ctx', [(i, i ^ 2) for i in range(ctx)])  34.2 us
    ppermute x6, waiting for transfers between devices, shift_z(): lax.ppermute(value, 'fsdp', [(i, (i + d) % fsdp) for i in range(fsdp)])  19.8 us
    all_gather x2, waiting for transfers between devices, per_device(): mlp_w.append(lax.all_gather(own, 'fsdp', axis=0, tiled=True))  18.3 us
    ppermute x16, starting transfers between devices, swap_xy(): return lax.ppermute(value, ('ctx', 'tp'), pairs)  17.3 us
    ppermute x18, waiting for transfers between devices, swap_y(): return lax.ppermute(value, 'tp', [(i, i ^ 1) for i in range(tp)])  15.9 us
  transfers between devices with their start and end apart: 108, of which 51 were waited for; matrix products, arithmetic and copies ran while one was open for 0% of the time, Pallas kernels for 20%

profile of v11, /device:TPU:9, one launch (start us, length us, event | category | flops | bytes accessed | tf_op | source)
XLA Modules:
  0.0 369.8 jit_solution(3731439078124184399)
XLA Ops:
  15.2 2.3 prep_upstream.1
  45.4 3.5 attn.5
  51.3 2.6 attn.4
  54.0 2.2 collective-permute-start.18
  56.8 3.6 collective-permute-done.18.refs_1_
  60.3 3.7 %collective-permute-done.19.refs_2_ = bf16[80,1024]{1,0:T(8,128)(2,1)S(1)} collective-permute-done((bf16[80,1024]{1,0:T(8,128)(2,1)S(1)}, bf16[80,1024]{1,0:T(8,128)(2,1)S(1)}, u32[]{:S(2)}, u32[]{:S(2)}) %collective-permute-start.19) | collective-permute-done | bytes 163872 | tf_op jit(solution)/shard_map/ppermute | solution.py:799
  72.6 2.4 collective-permute-start.26
  78.3 6.7 %all-gather.9.cloned.1.call-done.refs_4_ = bf16[1024,1024]{1,0:T(8,128)(2,1)} async-done(((bf16[256,1024]{1,0:T(8,128)(2,1)}), bf16[1024,1024]{1,0:T(8,128)(2,1)}) %all-gather.9.cloned.1.call-update) | async-done | bytes 2097168 | tf_op jit(solution)/shard_map/all_gather | solution.py:879
  91.3 2.2 collective-permute-start.29
  94.0 3.6 collective-permute-done.29.refs_1_
  97.6 3.5 collective-permute-done.30.refs_2_
  110.0 2.3 collective-permute-start.37
  118.8 2.6 attn.7
  122.4 2.6 attn.6
  125.1 2.2 collective-permute-start.40
  127.8 4.2 %collective-permute-done.40.refs_1_ = bf16[80,1024]{1,0:T(8,128)(2,1)S(1)} collective-permute-done((bf16[80,1024]{1,0:T(8,128)(2,1)S(1)}, bf16[80,1024]{1,0:T(8,128)(2,1)S(1)}, u32[]{:S(2)}, u32[]{:S(2)}) %collective-permute-start.40) | collective-permute-done | bytes 163872 | tf_op jit(solution)/shard_map/ppermute | solution.py:808
  132.0 3.4 collective-permute-done.41.refs_2_
  143.8 2.4 collective-permute-start.48
  148.5 11.6 %all-gather.5.cloned.1.call-done.refs_4_.refs_1_ = bf16[1024,1024]{1,0:T(8,128)(2,1)} async-done(((bf16[256,1024]{1,0:T(8,128)(2,1)}), bf16[1024,1024]{1,0:T(8,128)(2,1)}) %all-gather.5.cloned.1.call-update) | async-done | bytes 2097168 | tf_op jit(solution)/shard_map/all_gather | solution.py:879
  161.7 2.2 mlp.6
  167.6 4.0 %mlp.7 = (bf16[320,1024]{1,0:T(8,128)(2,1)S(1)}, bf16[320,1024]{1,0:T(8,128)(2,1)S(1)}, bf16[320,512]{1,0:T(8,128)(2,1)S(1)}, f32[2,320,256]{2,1,0:T(8,128)S(1)}, f32[80,1024]{1,0:T(8,128)}) custom-call(bf16[80,1024]{1,0:T(8,128)(2,1)} %collective-permute-done.46.refs_0_, bf16[80,1024]{1,0:T(8,128)(2,1)} %collective-permute-done.47.refs_1_, ...), custom_call_target="tpu_custom_call" | custom-call | tf_op jit(solution)/shard_map/mlp/pallas_call | solution.py:79
  173.8 3.4 mlp_grad.2
  185.3 7.2 %collective-permute-done.52.refs_1_ = bf16[160,1024]{1,0:T(8,128)(2,1)S(1)} collective-permute-done((bf16[160,1024]{1,0:T(8,128)(2,1)S(1)}, bf16[160,1024]{1,0:T(8,128)(2,1)S(1)}, u32[]{:S(2)}, u32[]{:S(2)}) %collective-permute-start.52) | collective-permute-done | bytes 327712 | tf_op jit(solution)/shard_map/ppermute | solution.py:808
  192.5 7.1 %collective-permute-done.53.refs_2_ = bf16[160,1024]{1,0:T(8,128)(2,1)S(1)} collective-permute-done((bf16[160,1024]{1,0:T(8,128)(2,1)S(1)}, bf16[160,1024]{1,0:T(8,128)(2,1)S(1)}, u32[]{:S(2)}, u32[]{:S(2)}) %collective-permute-start.53) | collective-permute-done | bytes 327712 | tf_op jit(solution)/shard_map/ppermute | solution.py:799
  210.4 2.3 collective-permute-start.61
  215.1 2.5 attn_back.4
  217.6 2.5 attn_back.5
  223.0 2.2 collective-permute-start.64
  225.7 3.9 %collective-permute-done.64.refs_1_ = bf16[80,1024]{1,0:T(8,128)(2,1)S(1)} collective-permute-done((bf16[80,1024]{1,0:T(8,128)(2,1)S(1)}, bf16[80,1024]{1,0:T(8,128)(2,1)S(1)}, u32[]{:S(2)}, u32[]{:S(2)}) %collective-permute-start.64) | collective-permute-done | bytes 163872 | tf_op jit(solution)/shard_map/ppermute | solution.py:808
  229.6 3.6 collective-permute-done.65.refs_2_
  234.9 2.6 attn_grad.2
  244.7 2.3 collective-permute-start.72
  254.0 3.4 mlp_grad.3
  260.7 2.2 collective-permute-start.75
  263.4 3.9 %collective-permute-done.75.refs_1_ = bf16[80,1024]{1,0:T(8,128)(2,1)S(1)} collective-permute-done((bf16[80,1024]{1,0:T(8,128)(2,1)S(1)}, bf16[80,1024]{1,0:T(8,128)(2,1)S(1)}, u32[]{:S(2)}, u32[]{:S(2)}) %collective-permute-start.75) | collective-permute-done | bytes 163872 | tf_op jit(solution)/shard_map/ppermute | solution.py:808
  267.3 3.6 collective-permute-done.76.refs_2_
  280.4 2.3 collective-permute-start.83
  285.0 2.5 attn_back.6
  287.5 2.5 attn_back.7
  292.9 2.2 collective-permute-start.86
  295.6 3.9 %collective-permute-done.86.refs_1_ = bf16[80,1024]{1,0:T(8,128)(2,1)S(1)} collective-permute-done((bf16[80,1024]{1,0:T(8,128)(2,1)S(1)}, bf16[80,1024]{1,0:T(8,128)(2,1)S(1)}, u32[]{:S(2)}, u32[]{:S(2)}) %collective-permute-start.86) | collective-permute-done | bytes 163872 | tf_op jit(solution)/shard_map/ppermute | solution.py:808
  299.5 3.7 collective-permute-done.87.refs_2_
  306.0 2.7 attn_grad.3
  316.9 3.2 collective-permute-done.55.refs_1_.refs_7_
  321.9 16.9 %collective-permute-done.92.refs_4_ = bf16[288,512]{1,0:T(8,128)(2,1)S(1)} collective-permute-done((bf16[288,512]{1,0:T(8,128)(2,1)S(1)}, bf16[288,512]{1,0:T(8,128)(2,1)S(1)}, u32[]{:S(2)}, u32[]{:S(2)}) %collective-permute-start.92) | collective-permute-done | bytes 294944 | tf_op jit(solution)/shard_map/ppermute | solution.py:811
  338.8 2.9 collective-permute-done.93.refs_5_
  347.2 5.5 %collective-permute-done.95.refs_2_ = f32[24,256]{1,0:T(8,128)S(1)} collective-permute-done((f32[24,256]{1,0:T(8,128)S(1)}, f32[24,256]{1,0:T(8,128)S(1)}, u32[]{:S(2)}, u32[]{:S(2)}) %collective-permute-start.95) | collective-permute-done | bytes 24608 | tf_op jit(solution)/shard_map/ppermute | solution.py:799
  357.9 4.9 %place.1 = (f32[2,3,256,512]{3,2,1,0:T(8,128)}, f32[2,512,256]{2,1,0:T(8,128)}, f32[2,256,2048]{2,1,0:T(8,128)}, f32[2,2048,256]{2,1,0:T(8,128)}) custom-call(bf16[512,512]{1,0:T(8,128)(2,1)S(1)} %get-tuple-element.358.refs_0_, bf16[512,512]{1,0:T(8,128)(2,1)S(1)} %collective-permute-done.99.refs_1_, bf16[2560,512]{1,0:T(8,128)(2,1)S(1)} %get-tuple-element.359.refs_2_, ...), custom_call_target="tpu_custom_call" | custom-call | tf_op jit(solution)/shard_map/place/pallas_call | solution.py:79
  (376 shorter events, 174.6 us)
Async XLA Ops:
  7.2 34.1 %all-gather.7.cloned.1.call-start = ((), (), s32[]{:S(2)}) async-start(), calls=%async_computation.4 | async-start | bytes 1310720 | tf_op jit(solution)/shard_map/all_gather | solution.py:877
  9.0 76.0 %all-gather.9.cloned.1.call-start = ((), (), s32[]{:S(2)}) async-start(), calls=%async_computation.5 | async-start | bytes 2621440 | tf_op jit(solution)/shard_map/all_gather | solution.py:879
  11.2 103.7 %all-gather.11.cloned.1.call-start = ((), (), s32[]{:S(2)}) async-start(), calls=%async_computation.6 | async-start | bytes 1310720 | tf_op jit(solution)/shard_map/all_gather | solution.py:877
  11.4 10.9 %collective-permute-start.9 = (bf16[17,256]{1,0:T(8,128)(2,1)S(1)}, bf16[17,256]{1,0:T(8,128)(2,1)S(1)}, u32[]{:S(2)}, u32[]{:S(2)}) collective-permute-start(bf16[17,256]{1,0:T(8,128)(2,1)S(1)} %fusion.1), channel_id=1, source_target_pairs={{0,8},{8,16},{16,24},{24,0},{1,9},{9,17},{17,25},{25,1},{2,10},{10... | collective-permute-start | bytes 26120 | tf_op jit(solution)/shard_map/ppermute | solution.py:811
  12.8 10.9 %collective-permute-start.8 = (bf16[17,256]{1,0:T(8,128)(2,1)S(1)}, bf16[17,256]{1,0:T(8,128)(2,1)S(1)}, u32[]{:S(2)}, u32[]{:S(2)}) collective-permute-start(bf16[17,256]{1,0:T(8,128)(2,1)S(1)} %fusion.1), channel_id=1, source_target_pairs={{0,16},{8,24},{16,0},{24,8},{1,17},{9,25},{17,1},{25,9},{2,18},{10... | collective-permute-start | bytes 26120 | tf_op jit(solution)/shard_map/ppermute | solution.py:811
  13.9 10.0 %collective-permute-start.7 = (bf16[17,256]{1,0:T(8,128)(2,1)S(1)}, bf16[17,256]{1,0:T(8,128)(2,1)S(1)}, u32[]{:S(2)}, u32[]{:S(2)}) collective-permute-start(bf16[17,256]{1,0:T(8,128)(2,1)S(1)} %fusion.1), channel_id=1, source_target_pairs={{0,24},{8,0},{16,8},{24,16},{1,25},{9,1},{17,9},{25,17},{2,26},{10... | collective-permute-start | bytes 26120 | tf_op jit(solution)/shard_map/ppermute | solution.py:811
  17.6 9.2 %collective-permute-start.3 = (bf16[80,1024]{1,0:T(8,128)(2,1)S(1)}, bf16[80,1024]{1,0:T(8,128)(2,1)S(1)}, u32[]{:S(2)}, u32[]{:S(2)}) collective-permute-start(bf16[80,1024]{1,0:T(8,128)(2,1)S(1)} %get-tuple-element.189.refs_0_), channel_id=1, source_target_pairs={{0,2},{2,0},{4,6},{6,4},{1,3},{3,1},{5,7},{7,5},{8,10},{10,8},{12,... | collective-permute-start | bytes 491528 | tf_op jit(solution)/shard_map/ppermute | solution.py:796
  19.2 8.9 %collective-permute-start.2 = (bf16[80,1024]{1,0:T(8,128)(2,1)S(1)}, bf16[80,1024]{1,0:T(8,128)(2,1)S(1)}, u32[]{:S(2)}, u32[]{:S(2)}) collective-permute-start(bf16[80,1024]{1,0:T(8,128)(2,1)S(1)} %get-tuple-element.189.refs_0_), channel_id=1, source_target_pairs={{0,1},{1,0},{2,3},{3,2},{4,5},{5,4},{6,7},{7,6},{8,9},{9,8},{10,11... | collective-permute-start | bytes 491528 | tf_op jit(solution)/shard_map/ppermute | solution.py:802
  22.2 137.9 %all-gather.5.cloned.1.call-start = ((), (), s32[]{:S(2)}) async-start(), calls=%async_computation.3 | async-start | bytes 2621440 | tf_op jit(solution)/shard_map/all_gather | solution.py:879
  25.5 9.0 %collective-permute-start.12 = (bf16[80,1024]{1,0:T(8,128)(2,1)S(1)}, bf16[80,1024]{1,0:T(8,128)(2,1)S(1)}, u32[]{:S(2)}, u32[]{:S(2)}) collective-permute-start(bf16[80,1024]{1,0:T(8,128)(2,1)S(1)} %get-tuple-element.193.refs_0_), channel_id=1, source_target_pairs={{0,1},{1,0},{2,3},{3,2},{4,5},{5,4},{6,7},{7,6},{8,9},{9,8},{10,11... | collective-permute-start | bytes 491528 | tf_op jit(solution)/shard_map/ppermute | solution.py:802
  26.8 8.8 %collective-permute-start.11 = (bf16[80,1024]{1,0:T(8,128)(2,1)S(1)}, bf16[80,1024]{1,0:T(8,128)(2,1)S(1)}, u32[]{:S(2)}, u32[]{:S(2)}) collective-permute-start(bf16[80,1024]{1,0:T(8,128)(2,1)S(1)} %get-tuple-element.193.refs_0_), channel_id=1, source_target_pairs={{0,4},{2,6},{4,0},{6,2},{1,5},{3,7},{5,1},{7,3},{8,12},{10,14},{12... | collective-permute-start | bytes 491528 | tf_op jit(solution)/shard_map/ppermute | solution.py:799
  28.0 10.4 %collective-permute-start.10 = (bf16[80,1024]{1,0:T(8,128)(2,1)S(1)}, bf16[80,1024]{1,0:T(8,128)(2,1)S(1)}, u32[]{:S(2)}, u32[]{:S(2)}) collective-permute-start(bf16[80,1024]{1,0:T(8,128)(2,1)S(1)} %get-tuple-element.193.refs_0_), channel_id=1, source_target_pairs={{0,5},{1,4},{2,7},{3,6},{4,1},{5,0},{6,3},{7,2},{8,13},{9,12},{10,... | collective-permute-start | bytes 491528 | tf_op jit(solution)/shard_map/ppermute | solution.py:808
  28.2 11.3 %collective-permute-start.6 = (bf16[80,1024]{1,0:T(8,128)(2,1)S(1)}, bf16[80,1024]{1,0:T(8,128)(2,1)S(1)}, u32[]{:S(2)}, u32[]{:S(2)}) collective-permute-start(bf16[80,1024]{1,0:T(8,128)(2,1)S(1)} %collective-permute-done.2.refs_3_), channel_id=1, source_target_pairs={{0,2},{2,0},{4,6},{6,4},{1,3},{3,1},{5,7},{7,5},{8,10},{10,8},{12,... | collective-permute-start | bytes 491528 | tf_op jit(solution)/shard_map/ppermute | solution.py:796
  31.4 8.2 %collective-permute-start.5 = (bf16[80,1024]{1,0:T(8,128)(2,1)S(1)}, bf16[80,1024]{1,0:T(8,128)(2,1)S(1)}, u32[]{:S(2)}, u32[]{:S(2)}) collective-permute-start(bf16[80,1024]{1,0:T(8,128)(2,1)S(1)} %collective-permute-done.1.refs_2_), channel_id=1, source_target_pairs={{0,2},{2,0},{4,6},{6,4},{1,3},{3,1},{5,7},{7,5},{8,10},{10,8},{12,... | collective-permute-start | bytes 491528 | tf_op jit(solution)/shard_map/ppermute | solution.py:796
  34.5 8.6 %collective-permute-start.13 = (bf16[80,1024]{1,0:T(8,128)(2,1)S(1)}, bf16[80,1024]{1,0:T(8,128)(2,1)}, u32[]{:S(2)}, u32[]{:S(2)}) collective-permute-start(bf16[80,1024]{1,0:T(8,128)(2,1)S(1)} %get-tuple-element.193.refs_0_), channel_id=1, source_target_pairs={{0,2},{2,0},{4,6},{6,4},{1,3},{3,1},{5,7},{7,5},{8,10},{10,8},{12,... | collective-permute-start | bytes 491528 | tf_op jit(solution)/shard_map/ppermute | solution.py:796
  51.1 186.8 %reduce-scatter.4.cloned.1.call-start = ((), (), s32[]{:S(2)}) async-start(), calls=%async_computation.7 | async-start | bytes 2621440 | tf_op jit(solution)/shard_map/reduce_scatter | solution.py:1052
  56.5 8.1 %collective-permute-start.20 = (bf16[80,1024]{1,0:T(8,128)(2,1)S(1)}, bf16[80,1024]{1,0:T(8,128)(2,1)S(1)}, u32[]{:S(2)}, u32[]{:S(2)}) collective-permute-start(bf16[80,1024]{1,0:T(8,128)(2,1)S(1)} %get-tuple-element.207), channel_id=1, source_target_pairs={{0,1},{1,0},{2,3},{3,2},{4,5},{5,4},{6,7},{7,6},{8,9},{9,8},{10,11... | collective-permute-start | bytes 491528 | tf_op jit(solution)/shard_map/ppermute | solution.py:802
  68.6 8.7 %collective-permute-start.24 = (bf16[80,1024]{1,0:T(8,128)(2,1)S(1)}, bf16[80,1024]{1,0:T(8,128)(2,1)S(1)}, u32[]{:S(2)}, u32[]{:S(2)}) collective-permute-start(bf16[80,1024]{1,0:T(8,128)(2,1)S(1)} %get-tuple-element.209.refs_0_), channel_id=1, source_target_pairs={{0,2},{2,0},{4,6},{6,4},{1,3},{3,1},{5,7},{7,5},{8,10},{10,8},{12,... | collective-permute-start | bytes 491528 | tf_op jit(solution)/shard_map/ppermute | solution.py:796
  93.8 8.2 %collective-permute-start.31 = (bf16[80,1024]{1,0:T(8,128)(2,1)S(1)}, bf16[80,1024]{1,0:T(8,128)(2,1)S(1)}, u32[]{:S(2)}, u32[]{:S(2)}) collective-permute-start(bf16[80,1024]{1,0:T(8,128)(2,1)S(1)} %get-tuple-element.217), channel_id=1, source_target_pairs={{0,1},{1,0},{2,3},{3,2},{4,5},{5,4},{6,7},{7,6},{8,9},{9,8},{10,11... | collective-permute-start | bytes 491528 | tf_op jit(solution)/shard_map/ppermute | solution.py:802
  105.9 10.7 %collective-permute-start.35 = (bf16[80,1024]{1,0:T(8,128)(2,1)S(1)}, bf16[80,1024]{1,0:T(8,128)(2,1)S(1)}, u32[]{:S(2)}, u32[]{:S(2)}) collective-permute-start(bf16[80,1024]{1,0:T(8,128)(2,1)S(1)} %get-tuple-element.219.refs_0_), channel_id=1, source_target_pairs={{0,2},{2,0},{4,6},{6,4},{1,3},{3,1},{5,7},{7,5},{8,10},{10,8},{12,... | collective-permute-start | bytes 491528 | tf_op jit(solution)/shard_map/ppermute | solution.py:796
  127.3 8.2 %collective-permute-start.41 = (bf16[80,1024]{1,0:T(8,128)(2,1)S(1)}, bf16[80,1024]{1,0:T(8,128)(2,1)S(1)}, u32[]{:S(2)}, u32[]{:S(2)}) collective-permute-start(bf16[80,1024]{1,0:T(8,128)(2,1)S(1)} %get-tuple-element.230), channel_id=1, source_target_pairs={{0,4},{2,6},{4,0},{6,2},{1,5},{3,7},{5,1},{7,3},{8,12},{10,14},{12... | collective-permute-start | bytes 491528 | tf_op jit(solution)/shard_map/ppermute | solution.py:799
  127.6 8.3 %collective-permute-start.42 = (bf16[80,1024]{1,0:T(8,128)(2,1)S(1)}, bf16[80,1024]{1,0:T(8,128)(2,1)S(1)}, u32[]{:S(2)}, u32[]{:S(2)}) collective-permute-start(bf16[80,1024]{1,0:T(8,128)(2,1)S(1)} %get-tuple-element.231), channel_id=1, source_target_pairs={{0,1},{1,0},{2,3},{3,2},{4,5},{5,4},{6,7},{7,6},{8,9},{9,8},{10,11... | collective-permute-start | bytes 491528 | tf_op jit(solution)/shard_map/ppermute | solution.py:802
  139.8 27.8 %collective-permute-start.46 = (bf16[80,1024]{1,0:T(8,128)(2,1)S(1)}, bf16[80,1024]{1,0:T(8,128)(2,1)}, u32[]{:S(2)}, u32[]{:S(2)}) collective-permute-start(bf16[80,1024]{1,0:T(8,128)(2,1)S(1)} %get-tuple-element.233.refs_0_), channel_id=1, source_target_pairs={{0,2},{2,0},{4,6},{6,4},{1,3},{3,1},{5,7},{7,5},{8,10},{10,8},{12,... | collective-permute-start | bytes 491528 | tf_op jit(solution)/shard_map/ppermute | solution.py:796
  142.6 25.0 %collective-permute-start.49 = (bf16[80,1024]{1,0:T(8,128)(2,1)S(1)}, bf16[80,1024]{1,0:T(8,128)(2,1)}, u32[]{:S(2)}, u32[]{:S(2)}) collective-permute-start(bf16[80,1024]{1,0:T(8,128)(2,1)S(1)} %collective-permute-done.45.refs_3_), channel_id=1, source_target_pairs={{0,2},{2,0},{4,6},{6,4},{1,3},{3,1},{5,7},{7,5},{8,10},{10,8},{12,... | collective-permute-start | bytes 491528 | tf_op jit(solution)/shard_map/ppermute | solution.py:796
  143.8 23.8 %collective-permute-start.48 = (bf16[80,1024]{1,0:T(8,128)(2,1)}, bf16[80,1024]{1,0:T(8,128)(2,1)}, u32[]{:S(2)}, u32[]{:S(2)}) collective-permute-start(bf16[80,1024]{1,0:T(8,128)(2,1)} %collective-permute-done.44.refs_2_), channel_id=1, source_target_pairs={{0,2},{2,0},{4,6},{6,4},{1,3},{3,1},{5,7},{7,5},{8,10},{10,8},{12,... | collective-permute-start | bytes 491528 | tf_op jit(solution)/shard_map/ppermute | solution.py:796
  146.9 20.7 %collective-permute-start.47 = (bf16[80,1024]{1,0:T(8,128)(2,1)}, bf16[80,1024]{1,0:T(8,128)(2,1)}, u32[]{:S(2)}, u32[]{:S(2)}) collective-permute-start(bf16[80,1024]{1,0:T(8,128)(2,1)} %collective-permute-done.43.refs_1_), channel_id=1, source_target_pairs={{0,2},{2,0},{4,6},{6,4},{1,3},{3,1},{5,7},{7,5},{8,10},{10,8},{12,... | collective-permute-start | bytes 491528 | tf_op jit(solution)/shard_map/ppermute | solution.py:796
  177.2 95.6 %reduce-scatter.6.cloned.1.call-start = ((), (), s32[]{:S(2)}) async-start(), calls=%async_computation.8 | async-start | bytes 1310720 | tf_op jit(solution)/shard_map/reduce_scatter | solution.py:1052
  182.6 9.9 %collective-permute-start.52 = (bf16[160,1024]{1,0:T(8,128)(2,1)S(1)}, bf16[160,1024]{1,0:T(8,128)(2,1)S(1)}, u32[]{:S(2)}, u32[]{:S(2)}) collective-permute-start(bf16[160,1024]{1,0:T(8,128)(2,1)S(1)} %get-tuple-element.252), channel_id=1, source_target_pairs={{0,5},{1,4},{2,7},{3,6},{4,1},{5,0},{6,3},{7,2},{8,13},{9,12},{10,... | collective-permute-start | bytes 983048 | tf_op jit(solution)/shard_map/ppermute | solution.py:808
  184.7 14.9 %collective-permute-start.53 = (bf16[160,1024]{1,0:T(8,128)(2,1)S(1)}, bf16[160,1024]{1,0:T(8,128)(2,1)S(1)}, u32[]{:S(2)}, u32[]{:S(2)}) collective-permute-start(bf16[160,1024]{1,0:T(8,128)(2,1)S(1)} %get-tuple-element.253), channel_id=1, source_target_pairs={{0,4},{2,6},{4,0},{6,2},{1,5},{3,7},{5,1},{7,3},{8,12},{10,14},{12... | collective-permute-start | bytes 983048 | tf_op jit(solution)/shard_map/ppermute | solution.py:799
  185.0 15.3 %collective-permute-start.54 = (bf16[160,1024]{1,0:T(8,128)(2,1)S(1)}, bf16[160,1024]{1,0:T(8,128)(2,1)S(1)}, u32[]{:S(2)}, u32[]{:S(2)}) collective-permute-start(bf16[160,1024]{1,0:T(8,128)(2,1)S(1)} %get-tuple-element.254), channel_id=1, source_target_pairs={{0,1},{1,0},{2,3},{3,2},{4,5},{5,4},{6,7},{7,6},{8,9},{9,8},{10,11... | collective-permute-start | bytes 983048 | tf_op jit(solution)/shard_map/ppermute | solution.py:802
  206.4 11.2 %collective-permute-start.59 = (bf16[80,1024]{1,0:T(8,128)(2,1)S(1)}, bf16[80,1024]{1,0:T(8,128)(2,1)S(1)}, u32[]{:S(2)}, u32[]{:S(2)}) collective-permute-start(bf16[80,1024]{1,0:T(8,128)(2,1)S(1)} %get-tuple-element.269.refs_0_), channel_id=1, source_target_pairs={{0,2},{2,0},{4,6},{6,4},{1,3},{3,1},{5,7},{7,5},{8,10},{10,8},{12,... | collective-permute-start | bytes 491528 | tf_op jit(solution)/shard_map/ppermute | solution.py:796
  209.2 8.4 %collective-permute-start.62 = (bf16[80,1024]{1,0:T(8,128)(2,1)S(1)}, bf16[80,1024]{1,0:T(8,128)(2,1)S(1)}, u32[]{:S(2)}, u32[]{:S(2)}) collective-permute-start(bf16[80,1024]{1,0:T(8,128)(2,1)S(1)} %collective-permute-done.58.refs_3_), channel_id=1, source_target_pairs={{0,2},{2,0},{4,6},{6,4},{1,3},{3,1},{5,7},{7,5},{8,10},{10,8},{12,... | collective-permute-start | bytes 491528 | tf_op jit(solution)/shard_map/ppermute | solution.py:796
  225.4 8.2 %collective-permute-start.66 = (bf16[80,1024]{1,0:T(8,128)(2,1)S(1)}, bf16[80,1024]{1,0:T(8,128)(2,1)S(1)}, u32[]{:S(2)}, u32[]{:S(2)}) collective-permute-start(bf16[80,1024]{1,0:T(8,128)(2,1)S(1)} %get-tuple-element.285), channel_id=1, source_target_pairs={{0,1},{1,0},{2,3},{3,2},{4,5},{5,4},{6,7},{7,6},{8,9},{9,8},{10,11... | collective-permute-start | bytes 491528 | tf_op jit(solution)/shard_map/ppermute | solution.py:802
  237.6 71.8 %reduce-scatter.8.cloned.1.call-start = ((), (), s32[]{:S(2)}) async-start(), calls=%async_computation.9 | async-start | bytes 2621440 | tf_op jit(solution)/shard_map/reduce_scatter | solution.py:1052
  240.6 12.0 %collective-permute-start.70 = (bf16[80,1024]{1,0:T(8,128)(2,1)S(1)}, bf16[80,1024]{1,0:T(8,128)(2,1)S(1)}, u32[]{:S(2)}, u32[]{:S(2)}) collective-permute-start(bf16[80,1024]{1,0:T(8,128)(2,1)S(1)} %settle.2.refs_0_), channel_id=1, source_target_pairs={{0,2},{2,0},{4,6},{6,4},{1,3},{3,1},{5,7},{7,5},{8,10},{10,8},{12,... | collective-permute-start | bytes 491528 | tf_op jit(solution)/shard_map/ppermute | solution.py:796
  243.1 9.4 %collective-permute-start.73 = (bf16[80,1024]{1,0:T(8,128)(2,1)S(1)}, bf16[80,1024]{1,0:T(8,128)(2,1)S(1)}, u32[]{:S(2)}, u32[]{:S(2)}) collective-permute-start(bf16[80,1024]{1,0:T(8,128)(2,1)S(1)} %collective-permute-done.69.refs_3_), channel_id=1, source_target_pairs={{0,2},{2,0},{4,6},{6,4},{1,3},{3,1},{5,7},{7,5},{8,10},{10,8},{12,... | collective-permute-start | bytes 491528 | tf_op jit(solution)/shard_map/ppermute | solution.py:796
  263.2 8.2 %collective-permute-start.77 = (bf16[80,1024]{1,0:T(8,128)(2,1)S(1)}, bf16[80,1024]{1,0:T(8,128)(2,1)S(1)}, u32[]{:S(2)}, u32[]{:S(2)}) collective-permute-start(bf16[80,1024]{1,0:T(8,128)(2,1)S(1)} %get-tuple-element.309), channel_id=1, source_target_pairs={{0,1},{1,0},{2,3},{3,2},{4,5},{5,4},{6,7},{7,6},{8,9},{9,8},{10,11... | collective-permute-start | bytes 491528 | tf_op jit(solution)/shard_map/ppermute | solution.py:802
  276.3 11.1 %collective-permute-start.81 = (bf16[80,1024]{1,0:T(8,128)(2,1)S(1)}, bf16[80,1024]{1,0:T(8,128)(2,1)S(1)}, u32[]{:S(2)}, u32[]{:S(2)}) collective-permute-start(bf16[80,1024]{1,0:T(8,128)(2,1)S(1)} %get-tuple-element.315.refs_0_), channel_id=1, source_target_pairs={{0,2},{2,0},{4,6},{6,4},{1,3},{3,1},{5,7},{7,5},{8,10},{10,8},{12,... | collective-permute-start | bytes 491528 | tf_op jit(solution)/shard_map/ppermute | solution.py:796
  279.0 8.5 %collective-permute-start.84 = (bf16[80,1024]{1,0:T(8,128)(2,1)S(1)}, bf16[80,1024]{1,0:T(8,128)(2,1)S(1)}, u32[]{:S(2)}, u32[]{:S(2)}) collective-permute-start(bf16[80,1024]{1,0:T(8,128)(2,1)S(1)} %collective-permute-done.80.refs_3_), channel_id=1, source_target_pairs={{0,2},{2,0},{4,6},{6,4},{1,3},{3,1},{5,7},{7,5},{8,10},{10,8},{12,... | collective-permute-start | bytes 491528 | tf_op jit(solution)/shard_map/ppermute | solution.py:796
  295.3 8.3 %collective-permute-start.88 = (bf16[80,1024]{1,0:T(8,128)(2,1)S(1)}, bf16[80,1024]{1,0:T(8,128)(2,1)S(1)}, u32[]{:S(2)}, u32[]{:S(2)}) collective-permute-start(bf16[80,1024]{1,0:T(8,128)(2,1)S(1)} %get-tuple-element.331), channel_id=1, source_target_pairs={{0,1},{1,0},{2,3},{3,2},{4,5},{5,4},{6,7},{7,6},{8,9},{9,8},{10,11... | collective-permute-start | bytes 491528 | tf_op jit(solution)/shard_map/ppermute | solution.py:802
  310.7 31.0 %collective-permute-start.90 = (bf16[1280,512]{1,0:T(8,128)(2,1)S(1)}, bf16[1280,512]{1,0:T(8,128)(2,1)S(1)}, u32[]{:S(2)}, u32[]{:S(2)}) collective-permute-start(bf16[1280,512]{1,0:T(8,128)(2,1)S(1)} %fetch.1.refs_1_), channel_id=1, source_target_pairs={{0,4},{2,6},{4,0},{6,2},{1,5},{3,7},{5,1},{7,3},{8,12},{10,14},{12... | collective-permute-start | bytes 3932168 | tf_op jit(solution)/shard_map/ppermute | solution.py:799
  311.9 8.2 %collective-permute-start.55 = (f32[80,1024]{1,0:T(8,128)S(1)}, f32[80,1024]{1,0:T(8,128)S(1)}, u32[]{:S(2)}, u32[]{:S(2)}) collective-permute-start(f32[80,1024]{1,0:T(8,128)S(1)} %copy-done.29), channel_id=1, source_target_pairs={{0,1},{1,0},{2,3},{3,2},{4,5},{5,4},{6,7},{7,6},{8,9},{9,8},{10,11... | collective-permute-start | bytes 983048 | tf_op jit(solution)/shard_map/ppermute | solution.py:802
  312.6 29.1 %collective-permute-start.89 = (f32[80,1024]{1,0:T(8,128)S(1)}, f32[80,1024]{1,0:T(8,128)S(1)}, u32[]{:S(2)}, u32[]{:S(2)}) collective-permute-start(f32[80,1024]{1,0:T(8,128)S(1)} %copy-done.30), channel_id=1, source_target_pairs={{0,1},{1,0},{2,3},{3,2},{4,5},{5,4},{6,7},{7,6},{8,9},{9,8},{10,11... | collective-permute-start | bytes 983048 | tf_op jit(solution)/shard_map/ppermute | solution.py:802
  313.4 8.5 %collective-permute-start.91 = (bf16[288,512]{1,0:T(8,128)(2,1)S(1)}, bf16[288,512]{1,0:T(8,128)(2,1)S(1)}, u32[]{:S(2)}, u32[]{:S(2)}) collective-permute-start(bf16[288,512]{1,0:T(8,128)(2,1)S(1)} %copy-done.53), channel_id=1, source_target_pairs={{0,8},{8,16},{16,24},{24,0},{1,9},{9,17},{17,25},{25,1},{2,10},{10... | collective-permute-start | bytes 884744 | tf_op jit(solution)/shard_map/ppermute | solution.py:811
  314.9 24.0 %collective-permute-start.92 = (bf16[288,512]{1,0:T(8,128)(2,1)S(1)}, bf16[288,512]{1,0:T(8,128)(2,1)S(1)}, u32[]{:S(2)}, u32[]{:S(2)}) collective-permute-start(bf16[288,512]{1,0:T(8,128)(2,1)S(1)} %copy-done.52), channel_id=1, source_target_pairs={{0,16},{8,24},{16,0},{24,8},{1,17},{9,25},{17,1},{25,9},{2,18},{10... | collective-permute-start | bytes 884744 | tf_op jit(solution)/shard_map/ppermute | solution.py:811
  320.2 21.5 %collective-permute-start.93 = (bf16[288,512]{1,0:T(8,128)(2,1)S(1)}, bf16[288,512]{1,0:T(8,128)(2,1)S(1)}, u32[]{:S(2)}, u32[]{:S(2)}) collective-permute-start(bf16[288,512]{1,0:T(8,128)(2,1)S(1)} %copy-done.51), channel_id=1, source_target_pairs={{0,24},{8,0},{16,8},{24,16},{1,25},{9,1},{17,9},{25,17},{2,26},{10... | collective-permute-start | bytes 884744 | tf_op jit(solution)/shard_map/ppermute | solution.py:811
  342.8 15.0 %collective-permute-start.100 = (bf16[2560,512]{1,0:T(8,128)(2,1)S(1)}, bf16[2560,512]{1,0:T(8,128)(2,1)S(1)}, u32[]{:S(2)}, u32[]{:S(2)}) collective-permute-start(bf16[2560,512]{1,0:T(8,128)(2,1)S(1)} %get-tuple-element.359.refs_2_), channel_id=1, source_target_pairs={{0,2},{2,0},{4,6},{6,4},{1,3},{3,1},{5,7},{7,5},{8,10},{10,8},{12,... | collective-permute-start | bytes 7864328 | tf_op jit(solution)/shard_map/ppermute | solution.py:796
  344.3 9.6 %collective-permute-start.97 = (bf16[256,512]{1,0:T(8,128)(2,1)S(1)}, bf16[256,512]{1,0:T(8,128)(2,1)S(1)}, u32[]{:S(2)}, u32[]{:S(2)}) collective-permute-start(bf16[256,512]{1,0:T(8,128)(2,1)S(1)} %get-tuple-element.352.refs_4_), channel_id=1, source_target_pairs={{0,4},{2,6},{4,0},{6,2},{1,5},{3,7},{5,1},{7,3},{8,12},{10,14},{12... | collective-permute-start | bytes 786440 | tf_op jit(solution)/shard_map/ppermute | solution.py:799
  (114 other events, 1013.0 us)
Sparse Core Ops, SparseCore 0:
  10.2 28.8 all-gather.6
  41.2 43.8 all-gather.8
  86.6 28.1 all-gather.10
  116.2 43.8 all-gather.4
  177.4 42.0 reduce-scatter.3
  237.7 25.2 reduce-scatter.5
  265.9 43.4 reduce-scatter.7

commit v12 on v11

--- a/solution.py
+++ b/solution.py
@@ -324,15 +324,19 @@
         copy.wait()
 
 
-def mlp_kernel(hidden, keep_count, saves, loads, c0, c1, c2, c3, w, bias, *refs):
+def mlp_kernel(hidden, keep_count, saves, load_count, c0, c1, c2, c3, w, bias, *refs):
     kept, rest = refs[:keep_count], refs[keep_count:]
+    sources, rest = rest[: max(0, load_count - 1)], rest[max(0, load_count - 1) :]
     partial_ref, x_out, act_out, slope_out, *rest = rest
     kept_hbm, rest = rest[:keep_count], rest[keep_count:]
     loaded = []
-    if loads:
-        *rest, w_ref, w_sems = rest
+    if load_count:
+        w_ref, *targets = rest[:load_count]
+        *rest, load_sems = rest[load_count:]
         spans = (pl.ds(0, hidden), pl.ds(hidden, hidden))
-        loaded = start_copies([(w.at[:, c], w_ref.at[:, c]) for c in spans], w_sems)
+        loaded = start_copies(
+            [(w.at[:, c], w_ref.at[:, c]) for c in spans] + list(zip(sources, targets)), load_sems
+        )
         w = w_ref
     if saves:
         x, act_ref, slope_ref, sems = rest
@@ -344,7 +348,7 @@
     if saves:
         copies += start_copies([(x, x_out)], sems.at[pl.ds(keep_count, 1)])
     block = hidden // 2
-    if loads:
+    if load_count:
         loaded[0].wait()
     for k in range(2):
         span = slice(k * block, (k + 1) * block)
@@ -359,10 +363,10 @@
             )
     if saves:
         copies += start_copies([(act_ref, act_out)], sems.at[pl.ds(3 + keep_count, 1)])
-    if loads:
+    if load_count:
         loaded[1].wait()
     partial_ref[...] = dot_nt(act_ref[...], w[:, hidden:]).astype(bf16)
-    for copy in copies:
+    for copy in copies + loaded[2:]:
         copy.wait()
 
 
@@ -382,12 +386,16 @@
     sent[0].wait()
 
 
-def mlp_grad_kernel(hidden, second_near, second_far, act_near, act_far, up_near, up_far,
-                    grad_near, grad_far, out_hbm, token, out_one, out_two, sems):
-    token[...] = jnp.zeros_like(token)
+def mlp_grad_kernel(hidden, keep_count, second_near, second_far, act_near, act_far,
+                    up_near, up_far, grad_near, grad_far, passed, *refs):
+    kept, refs = refs[:keep_count], refs[keep_count:]
+    out_hbm, passed_ref, *refs = refs
+    kept_hbm, (out_one, out_two, sems) = refs[:keep_count], refs[keep_count:]
+    sent = start_copies(list(zip(kept, kept_hbm)), sems.at[pl.ds(2, keep_count)]) if kept else []
+    passed_ref[...] = passed[...]
     total = dot_tn(up_near[...], act_near[...]) + dot_tn(up_far[...], act_far[...])
     out_two[...] = total.astype(bf16)
-    sent = start_copies(
+    sent += start_copies(
         [(out_two, out_hbm.at[:, pl.ds(hidden, hidden)])], sems.at[pl.ds(0, 1)]
     )
     total = dot_tn(second_near[...], grad_near[...]) + dot_tn(second_far[...], grad_far[...])
@@ -559,9 +567,8 @@
         copy.wait()
 
 
-def settle_kernel(keep_count, after_count, passed, *refs):
-    kept, refs = refs[:keep_count], refs[keep_count + after_count :]
-    passed_ref, *kept_hbm, sems = refs
+def settle_kernel(keep_count, passed, there, through, *refs):
+    kept, (passed_ref, _, *kept_hbm, sems) = refs[:keep_count], refs[keep_count:]
     copies = start_copies(list(zip(kept, kept_hbm)), sems)
     passed_ref[...] = passed[...]
     for copy in copies:
@@ -584,24 +591,26 @@
         copy.wait()
 
 
-def shard_sum_kernel(depth, own_hbm, stacked, crossed, *refs):
-    *others, part_ref, mine_ref, pair_ref, own, sems = refs
+def shard_sum_kernel(depth, stacked, crossed, *refs):
+    below, refs = refs[: depth - 1], refs[depth - 1 :]
+    *sources, part_ref, mine_ref, pair_ref, found, sems = refs
     count = stacked.shape[0]
-    first, *copies = start_copies(
+    rows, width = part_ref.shape[0] // depth, mine_ref.shape[1]
+    loads = start_copies([(v, found.at[k]) for k, v in enumerate(sources)], sems)
+    copies = start_copies(
         [
-            (own_hbm, own),
             (stacked, pair_ref.at[pl.ds(0, count), :]),
             (crossed, pair_ref.at[pl.ds(count, count), :]),
-        ],
-        sems,
-    )
-    first.wait()
-    rows, width = part_ref.shape[0], mine_ref.shape[1]
-    terms = [ref[...].astype(f32) for ref in (own, *others)]
-    total = terms[0]
-    for term in terms[1:]:
-        total = total + term
-    part_ref[...] = total[:rows, :].astype(bf16)
+        ]
+        + [(part, part_ref.at[pl.ds((1 + k) * rows, rows), :]) for k, part in enumerate(below)],
+        sems.at[pl.ds(len(sources), 1 + depth)],
+    )
+    for load in loads:
+        load.wait()
+    total = found[0].astype(f32)
+    for k in range(1, len(sources)):
+        total = total + found[k].astype(f32)
+    part_ref[:rows, :] = total[:rows, :].astype(bf16)
     lines = total[rows:, :width] + total[rows:, width:]
     mine_ref[: 6 * depth, :] = lines[: 6 * depth, :]
     for k in range(mine_ref.shape[0] - 16):
@@ -629,7 +638,7 @@
     for l in range(depth):
         for k in range(GROUP):
             _, stacked = slices[k]
-            first = 0 if l == 0 else (3 * l - 1) * rows
+            first = 2 * l * rows
             span = pl.ds(pl.multiple_of((ci ^ k) * hidden, hidden), hidden)
             fc1[l, k] = stacked[first : first + rows, :].astype(f32)
             send(fc1.at[l, k], fc1_hbm.at[l, :, span])
@@ -637,8 +646,7 @@
             send(fc2.at[l, k], fc2_hbm.at[l, span, :])
     for l in reversed(range(depth)):
         for k in range(GROUP):
-            last, stacked = slices[k]
-            piece = last if l == 0 else stacked.at[pl.ds((3 * l + 1) * rows, rows), :]
+            piece = slices[k][0].at[pl.ds(l * rows, rows), :]
             span = pl.ds(pl.multiple_of((ci ^ k) * feats, feats), feats)
             for j in range(3):
                 qkv[l, k, j] = piece[:, j * feats : (j + 1) * feats].astype(f32)
@@ -816,15 +824,18 @@
         near = (own, swap_xy(own), swap_x(own), swap_y(own))
         return near, tuple(swap_core(chunk) for chunk in near)
 
-    def settle(value, there, *kept):
+    def settle(value, there, through, *kept):
         return kernel_call(
-            functools.partial(settle_kernel, len(kept), 1),
-            [(value.shape, value.dtype)] + [saved(k.shape, k.dtype) for k in kept],
+            functools.partial(settle_kernel, len(kept)),
+            [(value.shape, value.dtype), saved(through.shape, through.dtype)]
+            + [saved(k.shape, k.dtype) for k in kept],
             value,
+            Far(there),
+            Far(through),
             *kept,
-            Far(there),
             name="settle",
-            scratch=[DMA((max(1, len(kept)),))],
+            scratch=[DMA((len(kept),))],
+            aliases={2: 1},
         )
 
     def reduce_rows(*pairs, after=()):
@@ -937,7 +948,6 @@
         name="keep_rows",
         scratch=[half_x, half_x, DMA((2,))],
     )
-    upstream_chunks = [(x,) for x in upstream_rows]
     stream, first = kernel_call(
         functools.partial(prep_first_kernel, depth),
         [row_f32, row_bf16],
@@ -1012,26 +1022,31 @@
         for side in (1, 0):
             kept = (middle,) if side == 1 else ()
             saves = l + 1 < depth
-            loads = not saves and side == 1
+            loads = (mlp_w[l], *upstream_rows) if not saves and side == 1 else ()
             shapes = [
                 ((half, width), bf16),
                 ((half, hidden), bf16),
                 ((2, half, hidden // 2), f32),
             ]
             mlp[side] = kernel_call(
-                functools.partial(mlp_kernel, hidden, len(kept), saves, loads),
+                functools.partial(mlp_kernel, hidden, len(kept), saves, len(loads)),
                 [partial_out]
                 + [saved(*shape) if saves else shape for shape in shapes]
-                + [saved(k.shape, k.dtype) for k in kept],
+                + [saved(k.shape, k.dtype) for k in kept]
+                + [(v.shape, v.dtype) for v in loads],
                 *second_chunks[side],
                 Far(mlp_w[l]) if loads else mlp_w[l],
                 fc1_all[l],
                 *kept,
+                *[Far(v) for v in loads[1:]],
                 name="mlp",
                 scratch=[pltpu.VMEM(*shape) for shape in shapes if saves]
                 + [DMA((4 + len(kept),))]
-                + ([pltpu.VMEM((width, 2 * hidden), bf16), DMA((2,))] if loads else []),
+                + [DMA((len(loads) + 1,)) for _ in loads[:1]],
             )
+            if loads:
+                *mlp[side], mlp_w[l], near, far = mlp[side]
+                upstream_chunks = [(near,), (far,)]
         saved_all.append((attn, pairs if outer > 1 else None, mlp))
         if l + 1 < depth:
             (sums,) = reduce_rows((mlp[0][0], mlp[1][0]))
@@ -1077,29 +1092,37 @@
                 name="mlp_back",
                 scratch=[pltpu.VMEM((1, hidden), f32), DMA((1,))],
             )
-        mlp_grad, token = kernel_call(
-            functools.partial(mlp_grad_kernel, hidden),
-            [saved((width, 2 * hidden), bf16), TOKEN],
-            mlp[0][1],
-            mlp[1][1],
-            mlp[0][2],
-            mlp[1][2],
-            back[0][3],
-            back[1][3],
-            back[0][1],
-            back[1][1],
-            name="mlp_grad",
-            scratch=[
-                pltpu.VMEM((width, hidden), bf16),
-                pltpu.VMEM((width, hidden), bf16),
-                DMA((2,)),
-            ],
-        )
-        mlp_parts[l] = scatter_grads(mlp_grad)
+        def weight_grad(passed, *kept):
+            return kernel_call(
+                functools.partial(mlp_grad_kernel, hidden, len(kept)),
+                [saved((width, 2 * hidden), bf16), (passed.shape, passed.dtype)]
+                + [saved(k.shape, k.dtype) for k in kept],
+                mlp[0][1],
+                mlp[1][1],
+                mlp[0][2],
+                mlp[1][2],
+                back[0][3],
+                back[1][3],
+                back[0][1],
+                back[1][1],
+                passed,
+                *kept,
+                name="mlp_grad",
+                scratch=[
+                    pltpu.VMEM((width, hidden), bf16),
+                    pltpu.VMEM((width, hidden), bf16),
+                    DMA((2 + len(kept),)),
+                ],
+            )
+
+        token = ()
+        if l + 1 < depth:
+            mlp_grad, *token = weight_grad(upstream_b)
+            mlp_parts[l] = scatter_grads(mlp_grad)
         pairs_now = [(back[0][0], back[1][0])]
         if l + 1 == depth:
             pairs_now.append((mlp[0][0], mlp[1][0]))
-        sums, *output_sums = reduce_rows(*pairs_now, after=(token,))
+        sums, *output_sums = reduce_rows(*pairs_now, after=token)
         if l + 1 == depth:
             outputs_own, output_token = kernel_call(
                 functools.partial(sum_out_kernel, shift_row(l, 3)),
@@ -1127,9 +1150,15 @@
             scratch=[pltpu.VMEM((rows, width), f32)] * 2 + [DMA((2,))],
         )
         if l + 1 < depth:
-            middle_b, sums_two, grad_middle = settle(
-                middle_b, attn_parts[l + 1], sums_two, grad_middle
+            middle_b, through, sums_two, grad_middle = settle(
+                middle_b, mlp_parts[l + 1], attn_later, sums_two, grad_middle
             )
+            attn_parts[l + 1] = scatter_grads(through)
+        else:
+            mlp_grad, middle_b, sums_two, grad_middle = weight_grad(
+                middle_b, sums_two, grad_middle
+            )
+            mlp_parts[l] = scatter_grads(mlp_grad)
         middle_chunks = gather_rows(middle_b)
         grad_q = [None, None]
         middle_x = [None, None]
@@ -1203,7 +1232,7 @@
             [row_f32, row_bf16, ((2, width), f32)],
             *sums,
             Far(attn[1][5]),
-            Far(grad_middle) if l + 1 < depth else grad_middle,
+            Far(grad_middle),
             vecs,
             *masked,
             name="norm_back_one",
@@ -1236,46 +1265,38 @@
         shapes = [((width, 3 * feats), bf16), ((width, feats), bf16)]
         if l == 0:
             shapes = [((fsdp, width_own + 32, 4 * feats), bf16)]
-        kept = [sums_one, upstream] + ([sums_two] if l + 1 == depth else [])
-        *attn_grads, head_sums[l], upstream_b, sums_one, upstream, sums_kept = [
-            *kernel_call(
-                functools.partial(attn_grad_kernel, feats, count, len(kept)),
-                [saved((width if l > 0 else width_own + 32, 4 * feats), bf16)] * count
-                + [saved((2, feats), f32), row_bf16]
-                + [saved(k.shape, k.dtype) for k in kept],
-                attn[0][3],
-                attn[1][3],
-                attn[0][1],
-                attn[1][1],
-                *middle_x,
-                *grad_q,
-                grad_k,
-                grad_v,
-                upstream_b,
-                *(lines or (sums_one,)),
-                *kept,
-                name="attn_grad",
-                scratch=[
-                    pltpu.VMEM((all_rows, 3 * feats), bf16),
-                    pltpu.VMEM((2, feats), f32),
-                ]
-                + [pltpu.VMEM(*shape) for shape in shapes]
-                + [DMA((count + 2 + len(kept),))],
-            ),
-            sums_two,
-        ][: count + 5]
-        if l + 1 == depth:
-            sums_two = sums_kept
+        kept = [sums_one, upstream]
+        *attn_grads, head_sums[l], upstream_b, sums_one, upstream = kernel_call(
+            functools.partial(attn_grad_kernel, feats, count, len(kept)),
+            [saved((width if l > 0 else width_own + 32, 4 * feats), bf16)] * count
+            + [saved((2, feats), f32), row_bf16]
+            + [saved(k.shape, k.dtype) for k in kept],
+            attn[0][3],
+            attn[1][3],
+            attn[0][1],
+            attn[1][1],
+            *middle_x,
+            *grad_q,
+            grad_k,
+            grad_v,
+            upstream_b,
+            *(lines or (sums_one,)),
+            *kept,
+            name="attn_grad",
+            scratch=[
+                pltpu.VMEM((all_rows, 3 * feats), bf16),
+                pltpu.VMEM((2, feats), f32),
+            ]
+            + [pltpu.VMEM(*shape) for shape in shapes]
+            + [DMA((count + 2 + len(kept),))],
+        )
         if l > 0:
-            attn_parts[l] = scatter_grads(attn_grads[0])
-            (upstream_b,) = settle(upstream_b, mlp_parts[l])
+            attn_later = attn_grads[0]
             upstream_chunks = gather_rows(upstream_b)
         row_sums[l] = (sums_one, sums_two)
 
-    sources = [mlp_parts[0]]
-    for l in range(1, depth):
-        sources += [mlp_parts[l], attn_parts[l]]
-    blocks = 3 * depth - 1
+    sources = mlp_parts
+    blocks = 2 * depth
     (stacked,) = kernel_call(
         functools.partial(fetch_kernel, len(sources)),
         [((blocks * width_own, hidden), bf16)],
@@ -1291,23 +1312,25 @@
     part, mine, pair = kernel_call(
         functools.partial(shard_sum_kernel, depth),
         [
-            ((width_own, 4 * feats), bf16),
+            ((depth * width_own, 4 * feats), bf16),
             ((24, width_own), f32),
             ((2 * blocks * width_own, hidden), bf16),
         ],
-        Far(own_term),
         stacked,
         crossed,
-        *other_terms,
+        *[Far(v) for v in (*attn_parts[1:], own_term, *other_terms)],
         name="shard_sum",
         after=others,
-        scratch=[pltpu.VMEM(own_term.shape, bf16), DMA((3,))],
+        scratch=[
+            pltpu.VMEM((fsdp, *own_term.shape), bf16),
+            DMA((fsdp + 1 + depth,)),
+        ],
     )
     if outer > 1:
         part = lax.psum(part, "ctx", axis_index_groups=outer_groups)
     mine, last_pair = kernel_call(
         functools.partial(vector_plane_kernel, depth),
-        [((32, width_own), f32), ((2 * width_own, 4 * feats), bf16)],
+        [((32, width_own), f32), ((2 * depth * width_own, 4 * feats), bf16)],
         mine,
         swap_xy(mine),
         swap_x(mine),

time: 377 us -> 382 us (1.013)
  waiting for transfers between devices: 136 us -> 151 us
  local copies, waits for them, and re-layouts: 14.7 us -> 7.02 us
    ppermute x6, waiting for transfers between devices: 19.8 us -> 32.7 us  [shift_z(): lax.ppermute(value, 'fsdp', [(i, (i + d) % fsdp) for i in range(fsdp)])]
    unnamed x114 -> x92, local copies, waits for them, and re-layouts: 14 us -> 6.3 us
    ppermute x18, waiting for transfers between devices: 34.2 us -> 38.6 us  [swap_x(): return lax.ppermute(value, 'ctx', [(i, i ^ 2) for i in range(ctx)])]
    pallas_call x61 -> x60, Pallas kernels: 91.2 us -> 90.1 us  [kernel_call(): pl.pallas_call(run, out_shape=out_shape, in_specs=specs, out_specs=out_sp...]
  transfers between devices with their start and end apart: 108 -> 108, of which waited for: 51 -> 51; matrix products, arithmetic and copies ran while one was open for 0% -> 0% of each run, Pallas kernels for 20% -> 19%
where the time goes in v12:
time: 382 us; the launch traced here: 377 us
  waiting for transfers between devices  151 us (40%)
  starting transfers between devices  112 us (29%)
  Pallas kernels  90.1 us (24%)
  between operations  15.7 us (4%)
  local copies, waits for them, and re-layouts  7.02 us (2%)
    pallas_call x60, Pallas kernels, kernel_call(): pl.pallas_call(run, out_shape=out_shape, in_specs=specs, out_specs=out_sp...  90.1 us
    ppermute x43, starting transfers between devices, swap_core(): return lax.ppermute(value, 'ctx', [(i, i ^ 1) for i in range(ctx)])  54.7 us
    ppermute x18, waiting for transfers between devices, swap_x(): return lax.ppermute(value, 'ctx', [(i, i ^ 2) for i in range(ctx)])  38.6 us
    ppermute x16, waiting for transfers between devices, swap_xy(): return lax.ppermute(value, ('ctx', 'tp'), pairs)  38.4 us
    ppermute x6, waiting for transfers between devices, shift_z(): lax.ppermute(value, 'fsdp', [(i, (i + d) % fsdp) for i in range(fsdp)])  32.7 us
    all_gather x2, waiting for transfers between devices, per_device(): mlp_w.append(lax.all_gather(own, 'fsdp', axis=0, tiled=True))  18.5 us
    ppermute x16, starting transfers between devices, swap_xy(): return lax.ppermute(value, ('ctx', 'tp'), pairs)  18.3 us
    ppermute x18, waiting for transfers between devices, swap_y(): return lax.ppermute(value, 'tp', [(i, i ^ 1) for i in range(tp)])  16.3 us
  transfers between devices with their start and end apart: 108, of which 51 were waited for; matrix products, arithmetic and copies ran while one was open for 0% of the time, Pallas kernels for 19%

profile of v12, /device:TPU:9, one launch (start us, length us, event | category | flops | bytes accessed | tf_op | source)
XLA Modules:
  0.0 376.8 jit_solution(3597670768790111357)
XLA Ops:
  15.2 2.3 prep_upstream.1
  45.3 3.4 attn.5
  51.2 2.6 attn.4
  54.0 2.2 collective-permute-start.18
  56.7 3.6 collective-permute-done.18.refs_1_
  60.3 3.7 collective-permute-done.19.refs_2_
  72.5 2.4 collective-permute-start.26
  78.2 6.8 %all-gather.7.cloned.1.call-done.refs_4_ = bf16[1024,1024]{1,0:T(8,128)(2,1)} async-done(((bf16[256,1024]{1,0:T(8,128)(2,1)}), bf16[1024,1024]{1,0:T(8,128)(2,1)}) %all-gather.7.cloned.1.call-update) | async-done | bytes 2097168 | tf_op jit(solution)/shard_map/all_gather | solution.py:890
  91.4 2.2 collective-permute-start.29
  94.1 3.6 collective-permute-done.29.refs_1_
  97.7 3.6 collective-permute-done.30.refs_2_
  110.0 2.3 collective-permute-start.37
  118.9 2.6 attn.7
  122.4 2.6 attn.6
  125.2 2.2 collective-permute-start.40
  127.9 4.2 %collective-permute-done.40.refs_1_ = bf16[80,1024]{1,0:T(8,128)(2,1)S(1)} collective-permute-done((bf16[80,1024]{1,0:T(8,128)(2,1)S(1)}, bf16[80,1024]{1,0:T(8,128)(2,1)S(1)}, u32[]{:S(2)}, u32[]{:S(2)}) %collective-permute-start.40) | collective-permute-done | bytes 163872 | tf_op jit(solution)/shard_map/ppermute | solution.py:816
  132.1 3.4 collective-permute-done.41.refs_2_
  143.9 2.3 collective-permute-start.47
  148.5 11.7 %all-gather.11.cloned.1.call-done.refs_4_ = bf16[1024,1024]{1,0:T(8,128)(2,1)} async-done(((bf16[256,1024]{1,0:T(8,128)(2,1)}), bf16[1024,1024]{1,0:T(8,128)(2,1)}) %all-gather.11.cloned.1.call-update) | async-done | bytes 2097168 | tf_op jit(solution)/shard_map/all_gather | solution.py:890
  160.2 3.7 mlp.6
  169.6 2.2 collective-permute-start.52
  172.4 7.1 %collective-permute-done.52.refs_1_ = bf16[160,1024]{1,0:T(8,128)(2,1)S(1)} collective-permute-done((bf16[160,1024]{1,0:T(8,128)(2,1)S(1)}, bf16[160,1024]{1,0:T(8,128)(2,1)S(1)}, u32[]{:S(2)}, u32[]{:S(2)}) %collective-permute-start.52) | collective-permute-done | bytes 327712 | tf_op jit(solution)/shard_map/ppermute | solution.py:816
  179.4 7.0 %collective-permute-done.53.refs_2_ = bf16[160,1024]{1,0:T(8,128)(2,1)S(1)} collective-permute-done((bf16[160,1024]{1,0:T(8,128)(2,1)S(1)}, bf16[160,1024]{1,0:T(8,128)(2,1)S(1)}, u32[]{:S(2)}, u32[]{:S(2)}) %collective-permute-start.53) | collective-permute-done | bytes 327712 | tf_op jit(solution)/shard_map/ppermute | solution.py:807
  190.6 3.7 mlp_grad.2
  201.2 2.3 collective-permute-start.61
  205.7 2.5 attn_back.4
  208.3 2.5 attn_back.5
  213.7 2.2 collective-permute-start.64
  216.4 3.9 %collective-permute-done.64.refs_1_ = bf16[80,1024]{1,0:T(8,128)(2,1)S(1)} collective-permute-done((bf16[80,1024]{1,0:T(8,128)(2,1)S(1)}, bf16[80,1024]{1,0:T(8,128)(2,1)S(1)}, u32[]{:S(2)}, u32[]{:S(2)}) %collective-permute-start.64) | collective-permute-done | bytes 163872 | tf_op jit(solution)/shard_map/ppermute | solution.py:816
  220.3 3.7 collective-permute-done.65.refs_2_
  225.8 2.6 attn_grad.2
  235.2 2.3 collective-permute-start.72
  242.7 3.4 mlp_grad.3
  248.6 2.2 collective-permute-start.75
  251.3 3.9 %collective-permute-done.75.refs_1_ = bf16[80,1024]{1,0:T(8,128)(2,1)S(1)} collective-permute-done((bf16[80,1024]{1,0:T(8,128)(2,1)S(1)}, bf16[80,1024]{1,0:T(8,128)(2,1)S(1)}, u32[]{:S(2)}, u32[]{:S(2)}) %collective-permute-start.75) | collective-permute-done | bytes 163872 | tf_op jit(solution)/shard_map/ppermute | solution.py:816
  255.2 3.7 collective-permute-done.76.refs_2_
  268.4 2.3 collective-permute-start.83
  273.0 2.5 attn_back.6
  275.6 2.5 attn_back.7
  283.6 3.9 %collective-permute-done.86.refs_1_ = bf16[80,1024]{1,0:T(8,128)(2,1)S(1)} collective-permute-done((bf16[80,1024]{1,0:T(8,128)(2,1)S(1)}, bf16[80,1024]{1,0:T(8,128)(2,1)S(1)}, u32[]{:S(2)}, u32[]{:S(2)}) %collective-permute-start.86) | collective-permute-done | bytes 163872 | tf_op jit(solution)/shard_map/ppermute | solution.py:816
  287.6 3.6 collective-permute-done.87.refs_2_
  293.9 2.5 attn_grad.3
  302.0 2.6 collective-permute-start.92
  304.6 3.0 collective-permute-done.55.refs_1_.refs_8_
  309.6 7.3 %collective-permute-done.91.refs_4_ = bf16[288,512]{1,0:T(8,128)(2,1)S(1)} collective-permute-done((bf16[288,512]{1,0:T(8,128)(2,1)S(1)}, bf16[288,512]{1,0:T(8,128)(2,1)S(1)}, u32[]{:S(2)}, u32[]{:S(2)}) %collective-permute-start.91) | collective-permute-done | bytes 294944 | tf_op jit(solution)/shard_map/ppermute | solution.py:819
  316.9 23.3 %collective-permute-done.92.refs_5_ = bf16[288,512]{1,0:T(8,128)(2,1)S(1)} collective-permute-done((bf16[288,512]{1,0:T(8,128)(2,1)S(1)}, bf16[288,512]{1,0:T(8,128)(2,1)S(1)}, u32[]{:S(2)}, u32[]{:S(2)}) %collective-permute-start.92) | collective-permute-done | bytes 294944 | tf_op jit(solution)/shard_map/ppermute | solution.py:819
  349.3 9.9 %collective-permute-done.95.refs_2_ = f32[24,256]{1,0:T(8,128)S(1)} collective-permute-done((f32[24,256]{1,0:T(8,128)S(1)}, f32[24,256]{1,0:T(8,128)S(1)}, u32[]{:S(2)}, u32[]{:S(2)}) %collective-permute-start.95) | collective-permute-done | bytes 24608 | tf_op jit(solution)/shard_map/ppermute | solution.py:807
  364.8 4.9 %place.1 = (f32[2,3,256,512]{3,2,1,0:T(8,128)}, f32[2,512,256]{2,1,0:T(8,128)}, f32[2,256,2048]{2,1,0:T(8,128)}, f32[2,2048,256]{2,1,0:T(8,128)}) custom-call(bf16[1024,512]{1,0:T(8,128)(2,1)S(1)} %get-tuple-element.368.refs_0_, bf16[1024,512]{1,0:T(8,128)(2,1)S(1)} %collective-permute-done.99.refs_1_, bf16[2048,512]{1,0:T(8,128)(2,1)S(1)} %get-tuple-element.369.refs_2_, ...), custom_call_target="tpu_custom_call" | custom-call | tf_op jit(solution)/shard_map/place/pallas_call | solution.py:79
  (353 shorter events, 166.4 us)
Async XLA Ops:
  7.2 34.1 %all-gather.5.cloned.1.call-start = ((), (), s32[]{:S(2)}) async-start(), calls=%async_computation.3 | async-start | bytes 1310720 | tf_op jit(solution)/shard_map/all_gather | solution.py:888
  9.0 76.0 %all-gather.7.cloned.1.call-start = ((), (), s32[]{:S(2)}) async-start(), calls=%async_computation.4 | async-start | bytes 2621440 | tf_op jit(solution)/shard_map/all_gather | solution.py:890
  11.2 103.8 %all-gather.9.cloned.1.call-start = ((), (), s32[]{:S(2)}) async-start(), calls=%async_computation.5 | async-start | bytes 1310720 | tf_op jit(solution)/shard_map/all_gather | solution.py:888
  11.4 10.9 %collective-permute-start.2 = (bf16[17,256]{1,0:T(8,128)(2,1)S(1)}, bf16[17,256]{1,0:T(8,128)(2,1)S(1)}, u32[]{:S(2)}, u32[]{:S(2)}) collective-permute-start(bf16[17,256]{1,0:T(8,128)(2,1)S(1)} %fusion.1), channel_id=1, source_target_pairs={{0,8},{8,16},{16,24},{24,0},{1,9},{9,17},{17,25},{25,1},{2,10},{10... | collective-permute-start | bytes 26120 | tf_op jit(solution)/shard_map/ppermute | solution.py:819
  12.8 10.8 %collective-permute-start.1 = (bf16[17,256]{1,0:T(8,128)(2,1)S(1)}, bf16[17,256]{1,0:T(8,128)(2,1)S(1)}, u32[]{:S(2)}, u32[]{:S(2)}) collective-permute-start(bf16[17,256]{1,0:T(8,128)(2,1)S(1)} %fusion.1), channel_id=1, source_target_pairs={{0,16},{8,24},{16,0},{24,8},{1,17},{9,25},{17,1},{25,9},{2,18},{10... | collective-permute-start | bytes 26120 | tf_op jit(solution)/shard_map/ppermute | solution.py:819
  13.9 9.9 %collective-permute-start = (bf16[17,256]{1,0:T(8,128)(2,1)S(1)}, bf16[17,256]{1,0:T(8,128)(2,1)S(1)}, u32[]{:S(2)}, u32[]{:S(2)}) collective-permute-start(bf16[17,256]{1,0:T(8,128)(2,1)S(1)} %fusion.1), channel_id=1, source_target_pairs={{0,24},{8,0},{16,8},{24,16},{1,25},{9,1},{17,9},{25,17},{2,26},{10... | collective-permute-start | bytes 26120 | tf_op jit(solution)/shard_map/ppermute | solution.py:819
  17.5 9.2 %collective-permute-start.9 = (bf16[80,1024]{1,0:T(8,128)(2,1)S(1)}, bf16[80,1024]{1,0:T(8,128)(2,1)S(1)}, u32[]{:S(2)}, u32[]{:S(2)}) collective-permute-start(bf16[80,1024]{1,0:T(8,128)(2,1)S(1)} %get-tuple-element.196.refs_0_), channel_id=1, source_target_pairs={{0,2},{2,0},{4,6},{6,4},{1,3},{3,1},{5,7},{7,5},{8,10},{10,8},{12,... | collective-permute-start | bytes 491528 | tf_op jit(solution)/shard_map/ppermute | solution.py:804
  19.1 8.9 %collective-permute-start.8 = (bf16[80,1024]{1,0:T(8,128)(2,1)S(1)}, bf16[80,1024]{1,0:T(8,128)(2,1)S(1)}, u32[]{:S(2)}, u32[]{:S(2)}) collective-permute-start(bf16[80,1024]{1,0:T(8,128)(2,1)S(1)} %get-tuple-element.196.refs_0_), channel_id=1, source_target_pairs={{0,1},{1,0},{2,3},{3,2},{4,5},{5,4},{6,7},{7,6},{8,9},{9,8},{10,11... | collective-permute-start | bytes 491528 | tf_op jit(solution)/shard_map/ppermute | solution.py:810
  22.2 138.0 %all-gather.11.cloned.1.call-start = ((), (), s32[]{:S(2)}) async-start(), calls=%async_computation.6 | async-start | bytes 2621440 | tf_op jit(solution)/shard_map/all_gather | solution.py:890
  25.4 9.0 %collective-permute-start.5 = (bf16[80,1024]{1,0:T(8,128)(2,1)S(1)}, bf16[80,1024]{1,0:T(8,128)(2,1)S(1)}, u32[]{:S(2)}, u32[]{:S(2)}) collective-permute-start(bf16[80,1024]{1,0:T(8,128)(2,1)S(1)} %get-tuple-element.192.refs_0_), channel_id=1, source_target_pairs={{0,1},{1,0},{2,3},{3,2},{4,5},{5,4},{6,7},{7,6},{8,9},{9,8},{10,11... | collective-permute-start | bytes 491528 | tf_op jit(solution)/shard_map/ppermute | solution.py:810
  26.8 8.8 %collective-permute-start.4 = (bf16[80,1024]{1,0:T(8,128)(2,1)S(1)}, bf16[80,1024]{1,0:T(8,128)(2,1)S(1)}, u32[]{:S(2)}, u32[]{:S(2)}) collective-permute-start(bf16[80,1024]{1,0:T(8,128)(2,1)S(1)} %get-tuple-element.192.refs_0_), channel_id=1, source_target_pairs={{0,4},{2,6},{4,0},{6,2},{1,5},{3,7},{5,1},{7,3},{8,12},{10,14},{12... | collective-permute-start | bytes 491528 | tf_op jit(solution)/shard_map/ppermute | solution.py:807
  28.0 10.3 %collective-permute-start.3 = (bf16[80,1024]{1,0:T(8,128)(2,1)S(1)}, bf16[80,1024]{1,0:T(8,128)(2,1)S(1)}, u32[]{:S(2)}, u32[]{:S(2)}) collective-permute-start(bf16[80,1024]{1,0:T(8,128)(2,1)S(1)} %get-tuple-element.192.refs_0_), channel_id=1, source_target_pairs={{0,5},{1,4},{2,7},{3,6},{4,1},{5,0},{6,3},{7,2},{8,13},{9,12},{10,... | collective-permute-start | bytes 491528 | tf_op jit(solution)/shard_map/ppermute | solution.py:816
  28.2 11.3 %collective-permute-start.12 = (bf16[80,1024]{1,0:T(8,128)(2,1)S(1)}, bf16[80,1024]{1,0:T(8,128)(2,1)S(1)}, u32[]{:S(2)}, u32[]{:S(2)}) collective-permute-start(bf16[80,1024]{1,0:T(8,128)(2,1)S(1)} %collective-permute-done.8.refs_3_), channel_id=1, source_target_pairs={{0,2},{2,0},{4,6},{6,4},{1,3},{3,1},{5,7},{7,5},{8,10},{10,8},{12,... | collective-permute-start | bytes 491528 | tf_op jit(solution)/shard_map/ppermute | solution.py:804
  31.3 8.2 %collective-permute-start.11 = (bf16[80,1024]{1,0:T(8,128)(2,1)S(1)}, bf16[80,1024]{1,0:T(8,128)(2,1)S(1)}, u32[]{:S(2)}, u32[]{:S(2)}) collective-permute-start(bf16[80,1024]{1,0:T(8,128)(2,1)S(1)} %collective-permute-done.7.refs_2_), channel_id=1, source_target_pairs={{0,2},{2,0},{4,6},{6,4},{1,3},{3,1},{5,7},{7,5},{8,10},{10,8},{12,... | collective-permute-start | bytes 491528 | tf_op jit(solution)/shard_map/ppermute | solution.py:804
  34.4 8.6 %collective-permute-start.13 = (bf16[80,1024]{1,0:T(8,128)(2,1)S(1)}, bf16[80,1024]{1,0:T(8,128)(2,1)S(1)}, u32[]{:S(2)}, u32[]{:S(2)}) collective-permute-start(bf16[80,1024]{1,0:T(8,128)(2,1)S(1)} %get-tuple-element.192.refs_0_), channel_id=1, source_target_pairs={{0,2},{2,0},{4,6},{6,4},{1,3},{3,1},{5,7},{7,5},{8,10},{10,8},{12,... | collective-permute-start | bytes 491528 | tf_op jit(solution)/shard_map/ppermute | solution.py:804
  50.9 209.9 %reduce-scatter.4.cloned.1.call-start = ((), (), s32[]{:S(2)}) async-start(), calls=%async_computation.7 | async-start | bytes 2621440 | tf_op jit(solution)/shard_map/reduce_scatter | solution.py:1067
  68.5 8.7 %collective-permute-start.24 = (bf16[80,1024]{1,0:T(8,128)(2,1)S(1)}, bf16[80,1024]{1,0:T(8,128)(2,1)S(1)}, u32[]{:S(2)}, u32[]{:S(2)}) collective-permute-start(bf16[80,1024]{1,0:T(8,128)(2,1)S(1)} %get-tuple-element.211.refs_0_), channel_id=1, source_target_pairs={{0,2},{2,0},{4,6},{6,4},{1,3},{3,1},{5,7},{7,5},{8,10},{10,8},{12,... | collective-permute-start | bytes 491528 | tf_op jit(solution)/shard_map/ppermute | solution.py:804
  93.8 8.2 %collective-permute-start.31 = (bf16[80,1024]{1,0:T(8,128)(2,1)S(1)}, bf16[80,1024]{1,0:T(8,128)(2,1)S(1)}, u32[]{:S(2)}, u32[]{:S(2)}) collective-permute-start(bf16[80,1024]{1,0:T(8,128)(2,1)S(1)} %get-tuple-element.219), channel_id=1, source_target_pairs={{0,1},{1,0},{2,3},{3,2},{4,5},{5,4},{6,7},{7,6},{8,9},{9,8},{10,11... | collective-permute-start | bytes 491528 | tf_op jit(solution)/shard_map/ppermute | solution.py:810
  106.0 10.6 %collective-permute-start.35 = (bf16[80,1024]{1,0:T(8,128)(2,1)S(1)}, bf16[80,1024]{1,0:T(8,128)(2,1)S(1)}, u32[]{:S(2)}, u32[]{:S(2)}) collective-permute-start(bf16[80,1024]{1,0:T(8,128)(2,1)S(1)} %get-tuple-element.221.refs_0_), channel_id=1, source_target_pairs={{0,2},{2,0},{4,6},{6,4},{1,3},{3,1},{5,7},{7,5},{8,10},{10,8},{12,... | collective-permute-start | bytes 491528 | tf_op jit(solution)/shard_map/ppermute | solution.py:804
  127.4 8.2 %collective-permute-start.41 = (bf16[80,1024]{1,0:T(8,128)(2,1)S(1)}, bf16[80,1024]{1,0:T(8,128)(2,1)S(1)}, u32[]{:S(2)}, u32[]{:S(2)}) collective-permute-start(bf16[80,1024]{1,0:T(8,128)(2,1)S(1)} %get-tuple-element.232), channel_id=1, source_target_pairs={{0,4},{2,6},{4,0},{6,2},{1,5},{3,7},{5,1},{7,3},{8,12},{10,14},{12... | collective-permute-start | bytes 491528 | tf_op jit(solution)/shard_map/ppermute | solution.py:807
  127.7 8.3 %collective-permute-start.42 = (bf16[80,1024]{1,0:T(8,128)(2,1)S(1)}, bf16[80,1024]{1,0:T(8,128)(2,1)S(1)}, u32[]{:S(2)}, u32[]{:S(2)}) collective-permute-start(bf16[80,1024]{1,0:T(8,128)(2,1)S(1)} %get-tuple-element.233), channel_id=1, source_target_pairs={{0,1},{1,0},{2,3},{3,2},{4,5},{5,4},{6,7},{7,6},{8,9},{9,8},{10,11... | collective-permute-start | bytes 491528 | tf_op jit(solution)/shard_map/ppermute | solution.py:810
  139.9 20.3 %collective-permute-start.43 = (bf16[80,1024]{1,0:T(8,128)(2,1)S(1)}, bf16[80,1024]{1,0:T(8,128)(2,1)S(1)}, u32[]{:S(2)}, u32[]{:S(2)}) collective-permute-start(bf16[80,1024]{1,0:T(8,128)(2,1)S(1)} %get-tuple-element.235.refs_0_), channel_id=1, source_target_pairs={{0,2},{2,0},{4,6},{6,4},{1,3},{3,1},{5,7},{7,5},{8,10},{10,8},{12,... | collective-permute-start | bytes 491528 | tf_op jit(solution)/shard_map/ppermute | solution.py:804
  142.6 17.6 %collective-permute-start.49 = (bf16[80,1024]{1,0:T(8,128)(2,1)S(1)}, bf16[80,1024]{1,0:T(8,128)(2,1)S(1)}, u32[]{:S(2)}, u32[]{:S(2)}) collective-permute-start(bf16[80,1024]{1,0:T(8,128)(2,1)S(1)} %collective-permute-done.48.refs_3_), channel_id=1, source_target_pairs={{0,2},{2,0},{4,6},{6,4},{1,3},{3,1},{5,7},{7,5},{8,10},{10,8},{12,... | collective-permute-start | bytes 491528 | tf_op jit(solution)/shard_map/ppermute | solution.py:804
  143.9 16.3 %collective-permute-start.47 = (bf16[80,1024]{1,0:T(8,128)(2,1)S(1)}, bf16[80,1024]{1,0:T(8,128)(2,1)}, u32[]{:S(2)}, u32[]{:S(2)}) collective-permute-start(bf16[80,1024]{1,0:T(8,128)(2,1)S(1)} %collective-permute-done.46.refs_2_), channel_id=1, source_target_pairs={{0,2},{2,0},{4,6},{6,4},{1,3},{3,1},{5,7},{7,5},{8,10},{10,8},{12,... | collective-permute-start | bytes 491528 | tf_op jit(solution)/shard_map/ppermute | solution.py:804
  146.9 13.3 %collective-permute-start.45 = (bf16[80,1024]{1,0:T(8,128)(2,1)S(1)}, bf16[80,1024]{1,0:T(8,128)(2,1)}, u32[]{:S(2)}, u32[]{:S(2)}) collective-permute-start(bf16[80,1024]{1,0:T(8,128)(2,1)S(1)} %collective-permute-done.44.refs_1_), channel_id=1, source_target_pairs={{0,2},{2,0},{4,6},{6,4},{1,3},{3,1},{5,7},{7,5},{8,10},{10,8},{12,... | collective-permute-start | bytes 491528 | tf_op jit(solution)/shard_map/ppermute | solution.py:804
  169.6 9.8 %collective-permute-start.52 = (bf16[160,1024]{1,0:T(8,128)(2,1)S(1)}, bf16[160,1024]{1,0:T(8,128)(2,1)S(1)}, u32[]{:S(2)}, u32[]{:S(2)}) collective-permute-start(bf16[160,1024]{1,0:T(8,128)(2,1)S(1)} %get-tuple-element.251), channel_id=1, source_target_pairs={{0,5},{1,4},{2,7},{3,6},{4,1},{5,0},{6,3},{7,2},{8,13},{9,12},{10,... | collective-permute-start | bytes 983048 | tf_op jit(solution)/shard_map/ppermute | solution.py:816
  171.8 14.6 %collective-permute-start.53 = (bf16[160,1024]{1,0:T(8,128)(2,1)S(1)}, bf16[160,1024]{1,0:T(8,128)(2,1)S(1)}, u32[]{:S(2)}, u32[]{:S(2)}) collective-permute-start(bf16[160,1024]{1,0:T(8,128)(2,1)S(1)} %get-tuple-element.252), channel_id=1, source_target_pairs={{0,4},{2,6},{4,0},{6,2},{1,5},{3,7},{5,1},{7,3},{8,12},{10,14},{12... | collective-permute-start | bytes 983048 | tf_op jit(solution)/shard_map/ppermute | solution.py:807
  172.1 15.2 %collective-permute-start.54 = (bf16[160,1024]{1,0:T(8,128)(2,1)S(1)}, bf16[160,1024]{1,0:T(8,128)(2,1)S(1)}, u32[]{:S(2)}, u32[]{:S(2)}) collective-permute-start(bf16[160,1024]{1,0:T(8,128)(2,1)S(1)} %get-tuple-element.253), channel_id=1, source_target_pairs={{0,1},{1,0},{2,3},{3,2},{4,5},{5,4},{6,7},{7,6},{8,9},{9,8},{10,11... | collective-permute-start | bytes 983048 | tf_op jit(solution)/shard_map/ppermute | solution.py:810
  194.3 102.2 %reduce-scatter.6.cloned.1.call-start = ((), (), s32[]{:S(2)}) async-start(), calls=%async_computation.8 | async-start | bytes 2621440 | tf_op jit(solution)/shard_map/reduce_scatter | solution.py:1067
  197.1 11.2 %collective-permute-start.59 = (bf16[80,1024]{1,0:T(8,128)(2,1)S(1)}, bf16[80,1024]{1,0:T(8,128)(2,1)S(1)}, u32[]{:S(2)}, u32[]{:S(2)}) collective-permute-start(bf16[80,1024]{1,0:T(8,128)(2,1)S(1)} %get-tuple-element.279.refs_0_), channel_id=1, source_target_pairs={{0,2},{2,0},{4,6},{6,4},{1,3},{3,1},{5,7},{7,5},{8,10},{10,8},{12,... | collective-permute-start | bytes 491528 | tf_op jit(solution)/shard_map/ppermute | solution.py:804
  199.6 8.6 %collective-permute-start.62 = (bf16[80,1024]{1,0:T(8,128)(2,1)S(1)}, bf16[80,1024]{1,0:T(8,128)(2,1)S(1)}, u32[]{:S(2)}, u32[]{:S(2)}) collective-permute-start(bf16[80,1024]{1,0:T(8,128)(2,1)S(1)} %collective-permute-done.58.refs_3_), channel_id=1, source_target_pairs={{0,2},{2,0},{4,6},{6,4},{1,3},{3,1},{5,7},{7,5},{8,10},{10,8},{12,... | collective-permute-start | bytes 491528 | tf_op jit(solution)/shard_map/ppermute | solution.py:804
  216.1 8.3 %collective-permute-start.66 = (bf16[80,1024]{1,0:T(8,128)(2,1)S(1)}, bf16[80,1024]{1,0:T(8,128)(2,1)S(1)}, u32[]{:S(2)}, u32[]{:S(2)}) collective-permute-start(bf16[80,1024]{1,0:T(8,128)(2,1)S(1)} %get-tuple-element.295), channel_id=1, source_target_pairs={{0,1},{1,0},{2,3},{3,2},{4,5},{5,4},{6,7},{7,6},{8,9},{9,8},{10,11... | collective-permute-start | bytes 491528 | tf_op jit(solution)/shard_map/ppermute | solution.py:810
  231.2 10.0 %collective-permute-start.70 = (bf16[80,1024]{1,0:T(8,128)(2,1)S(1)}, bf16[80,1024]{1,0:T(8,128)(2,1)S(1)}, u32[]{:S(2)}, u32[]{:S(2)}) collective-permute-start(bf16[80,1024]{1,0:T(8,128)(2,1)S(1)} %get-tuple-element.300.refs_0_.refs_8_), channel_id=1, source_target_pairs={{0,2},{2,0},{4,6},{6,4},{1,3},{3,1},{5,7},{7,5},{8,10},{10,8},{12,... | collective-permute-start | bytes 491528 | tf_op jit(solution)/shard_map/ppermute | solution.py:804
  246.0 96.9 %reduce-scatter.8.cloned.1.call-start = ((), (), s32[]{:S(2)}) async-start(), calls=%async_computation.9 | async-start | bytes 1310720 | tf_op jit(solution)/shard_map/reduce_scatter | solution.py:1067
  251.0 8.3 %collective-permute-start.77 = (bf16[80,1024]{1,0:T(8,128)(2,1)S(1)}, bf16[80,1024]{1,0:T(8,128)(2,1)S(1)}, u32[]{:S(2)}, u32[]{:S(2)}) collective-permute-start(bf16[80,1024]{1,0:T(8,128)(2,1)S(1)} %get-tuple-element.317), channel_id=1, source_target_pairs={{0,1},{1,0},{2,3},{3,2},{4,5},{5,4},{6,7},{7,6},{8,9},{9,8},{10,11... | collective-permute-start | bytes 491528 | tf_op jit(solution)/shard_map/ppermute | solution.py:810
  264.4 11.1 %collective-permute-start.81 = (bf16[80,1024]{1,0:T(8,128)(2,1)S(1)}, bf16[80,1024]{1,0:T(8,128)(2,1)S(1)}, u32[]{:S(2)}, u32[]{:S(2)}) collective-permute-start(bf16[80,1024]{1,0:T(8,128)(2,1)S(1)} %get-tuple-element.324.refs_0_), channel_id=1, source_target_pairs={{0,2},{2,0},{4,6},{6,4},{1,3},{3,1},{5,7},{7,5},{8,10},{10,8},{12,... | collective-permute-start | bytes 491528 | tf_op jit(solution)/shard_map/ppermute | solution.py:804
  267.1 8.4 %collective-permute-start.84 = (bf16[80,1024]{1,0:T(8,128)(2,1)S(1)}, bf16[80,1024]{1,0:T(8,128)(2,1)S(1)}, u32[]{:S(2)}, u32[]{:S(2)}) collective-permute-start(bf16[80,1024]{1,0:T(8,128)(2,1)S(1)} %collective-permute-done.80.refs_3_), channel_id=1, source_target_pairs={{0,2},{2,0},{4,6},{6,4},{1,3},{3,1},{5,7},{7,5},{8,10},{10,8},{12,... | collective-permute-start | bytes 491528 | tf_op jit(solution)/shard_map/ppermute | solution.py:804
  283.4 8.2 %collective-permute-start.88 = (bf16[80,1024]{1,0:T(8,128)(2,1)S(1)}, bf16[80,1024]{1,0:T(8,128)(2,1)S(1)}, u32[]{:S(2)}, u32[]{:S(2)}) collective-permute-start(bf16[80,1024]{1,0:T(8,128)(2,1)S(1)} %get-tuple-element.340), channel_id=1, source_target_pairs={{0,1},{1,0},{2,3},{3,2},{4,5},{5,4},{6,7},{7,6},{8,9},{9,8},{10,11... | collective-permute-start | bytes 491528 | tf_op jit(solution)/shard_map/ppermute | solution.py:810
  297.8 45.1 %collective-permute-start.90 = (bf16[1024,512]{1,0:T(8,128)(2,1)S(1)}, bf16[1024,512]{1,0:T(8,128)(2,1)S(1)}, u32[]{:S(2)}, u32[]{:S(2)}) collective-permute-start(bf16[1024,512]{1,0:T(8,128)(2,1)S(1)} %fetch.1.refs_0_), channel_id=1, source_target_pairs={{0,4},{2,6},{4,0},{6,2},{1,5},{3,7},{5,1},{7,3},{8,12},{10,14},{12... | collective-permute-start | bytes 3145736 | tf_op jit(solution)/shard_map/ppermute | solution.py:807
  299.1 8.5 %collective-permute-start.55 = (f32[80,1024]{1,0:T(8,128)S(1)}, f32[80,1024]{1,0:T(8,128)S(1)}, u32[]{:S(2)}, u32[]{:S(2)}) collective-permute-start(f32[80,1024]{1,0:T(8,128)S(1)} %copy-done.21), channel_id=1, source_target_pairs={{0,1},{1,0},{2,3},{3,2},{4,5},{5,4},{6,7},{7,6},{8,9},{9,8},{10,11... | collective-permute-start | bytes 983048 | tf_op jit(solution)/shard_map/ppermute | solution.py:810
  300.3 42.7 %collective-permute-start.89 = (f32[80,1024]{1,0:T(8,128)S(1)}, f32[80,1024]{1,0:T(8,128)S(1)}, u32[]{:S(2)}, u32[]{:S(2)}) collective-permute-start(f32[80,1024]{1,0:T(8,128)S(1)} %copy-done.22), channel_id=1, source_target_pairs={{0,1},{1,0},{2,3},{3,2},{4,5},{5,4},{6,7},{7,6},{8,9},{9,8},{10,11... | collective-permute-start | bytes 983048 | tf_op jit(solution)/shard_map/ppermute | solution.py:810
  300.6 16.3 %collective-permute-start.91 = (bf16[288,512]{1,0:T(8,128)(2,1)S(1)}, bf16[288,512]{1,0:T(8,128)(2,1)S(1)}, u32[]{:S(2)}, u32[]{:S(2)}) collective-permute-start(bf16[288,512]{1,0:T(8,128)(2,1)S(1)} %copy-done.42), channel_id=1, source_target_pairs={{0,8},{8,16},{16,24},{24,0},{1,9},{9,17},{17,25},{25,1},{2,10},{10... | collective-permute-start | bytes 884744 | tf_op jit(solution)/shard_map/ppermute | solution.py:819
  302.0 38.2 %collective-permute-start.92 = (bf16[288,512]{1,0:T(8,128)(2,1)S(1)}, bf16[288,512]{1,0:T(8,128)(2,1)S(1)}, u32[]{:S(2)}, u32[]{:S(2)}) collective-permute-start(bf16[288,512]{1,0:T(8,128)(2,1)S(1)} %copy-done.41), channel_id=1, source_target_pairs={{0,16},{8,24},{16,0},{24,8},{1,17},{9,25},{17,1},{25,9},{2,18},{10... | collective-permute-start | bytes 884744 | tf_op jit(solution)/shard_map/ppermute | solution.py:819
  307.6 34.7 %collective-permute-start.93 = (bf16[288,512]{1,0:T(8,128)(2,1)S(1)}, bf16[288,512]{1,0:T(8,128)(2,1)S(1)}, u32[]{:S(2)}, u32[]{:S(2)}) collective-permute-start(bf16[288,512]{1,0:T(8,128)(2,1)S(1)} %copy-done.40), channel_id=1, source_target_pairs={{0,24},{8,0},{16,8},{24,16},{1,25},{9,1},{17,9},{25,17},{2,26},{10... | collective-permute-start | bytes 884744 | tf_op jit(solution)/shard_map/ppermute | solution.py:819
  344.4 20.4 %collective-permute-start.100 = (bf16[2048,512]{1,0:T(8,128)(2,1)S(1)}, bf16[2048,512]{1,0:T(8,128)(2,1)S(1)}, u32[]{:S(2)}, u32[]{:S(2)}) collective-permute-start(bf16[2048,512]{1,0:T(8,128)(2,1)S(1)} %get-tuple-element.369.refs_2_), channel_id=1, source_target_pairs={{0,2},{2,0},{4,6},{6,4},{1,3},{3,1},{5,7},{7,5},{8,10},{10,8},{12,... | collective-permute-start | bytes 6291464 | tf_op jit(solution)/shard_map/ppermute | solution.py:804
  345.1 15.2 %collective-permute-start.97 = (bf16[512,512]{1,0:T(8,128)(2,1)S(1)}, bf16[512,512]{1,0:T(8,128)(2,1)S(1)}, u32[]{:S(2)}, u32[]{:S(2)}) collective-permute-start(bf16[512,512]{1,0:T(8,128)(2,1)S(1)} %get-tuple-element.362.refs_4_), channel_id=1, source_target_pairs={{0,4},{2,6},{4,0},{6,2},{1,5},{3,7},{5,1},{7,3},{8,12},{10,14},{12... | collective-permute-start | bytes 1572872 | tf_op jit(solution)/shard_map/ppermute | solution.py:807
  347.5 11.6 %collective-permute-start.95 = (f32[24,256]{1,0:T(8,128)S(1)}, f32[24,256]{1,0:T(8,128)S(1)}, u32[]{:S(2)}, u32[]{:S(2)}) collective-permute-start(f32[24,256]{1,0:T(8,128)S(1)} %get-tuple-element.361.refs_0_), channel_id=1, source_target_pairs={{0,4},{2,6},{4,0},{6,2},{1,5},{3,7},{5,1},{7,3},{8,12},{10,14},{12... | collective-permute-start | bytes 73736 | tf_op jit(solution)/shard_map/ppermute | solution.py:807
  347.8 12.5 %collective-permute-start.94 = (f32[24,256]{1,0:T(8,128)S(1)}, f32[24,256]{1,0:T(8,128)S(1)}, u32[]{:S(2)}, u32[]{:S(2)}) collective-permute-start(f32[24,256]{1,0:T(8,128)S(1)} %get-tuple-element.361.refs_0_), channel_id=1, source_target_pairs={{0,5},{1,4},{2,7},{3,6},{4,1},{5,0},{6,3},{7,2},{8,13},{9,12},{10,... | collective-permute-start | bytes 73736 | tf_op jit(solution)/shard_map/ppermute | solution.py:816
  (103 other events, 679.4 us)
Sparse Core Ops, SparseCore 0:
  10.2 28.8 all-gather.4
  41.2 43.8 all-gather.6
  86.6 28.2 all-gather.8
  116.3 43.8 all-gather.10
  194.4 41.5 reduce-scatter.3
  246.2 41.2 reduce-scatter.5
  290.3 46.1 reduce-scatter.7

commit v13 on v11

--- a/solution.py
+++ b/solution.py
@@ -324,15 +324,19 @@
         copy.wait()
 
 
-def mlp_kernel(hidden, keep_count, saves, loads, c0, c1, c2, c3, w, bias, *refs):
+def mlp_kernel(hidden, keep_count, saves, load_count, c0, c1, c2, c3, w, bias, *refs):
     kept, rest = refs[:keep_count], refs[keep_count:]
+    sources, rest = rest[: max(0, load_count - 1)], rest[max(0, load_count - 1) :]
     partial_ref, x_out, act_out, slope_out, *rest = rest
     kept_hbm, rest = rest[:keep_count], rest[keep_count:]
     loaded = []
-    if loads:
-        *rest, w_ref, w_sems = rest
+    if load_count:
+        w_ref, *targets = rest[:load_count]
+        *rest, load_sems = rest[load_count:]
         spans = (pl.ds(0, hidden), pl.ds(hidden, hidden))
-        loaded = start_copies([(w.at[:, c], w_ref.at[:, c]) for c in spans], w_sems)
+        loaded = start_copies(
+            [(w.at[:, c], w_ref.at[:, c]) for c in spans] + list(zip(sources, targets)), load_sems
+        )
         w = w_ref
     if saves:
         x, act_ref, slope_ref, sems = rest
@@ -344,7 +348,7 @@
     if saves:
         copies += start_copies([(x, x_out)], sems.at[pl.ds(keep_count, 1)])
     block = hidden // 2
-    if loads:
+    if load_count:
         loaded[0].wait()
     for k in range(2):
         span = slice(k * block, (k + 1) * block)
@@ -359,10 +363,10 @@
             )
     if saves:
         copies += start_copies([(act_ref, act_out)], sems.at[pl.ds(3 + keep_count, 1)])
-    if loads:
+    if load_count:
         loaded[1].wait()
     partial_ref[...] = dot_nt(act_ref[...], w[:, hidden:]).astype(bf16)
-    for copy in copies:
+    for copy in copies + loaded[2:]:
         copy.wait()
 
 
@@ -382,12 +386,15 @@
     sent[0].wait()
 
 
-def mlp_grad_kernel(hidden, second_near, second_far, act_near, act_far, up_near, up_far,
-                    grad_near, grad_far, out_hbm, token, out_one, out_two, sems):
-    token[...] = jnp.zeros_like(token)
+def mlp_grad_kernel(hidden, keep_count, second_near, second_far, act_near, act_far,
+                    up_near, up_far, grad_near, grad_far, *refs):
+    kept, refs = refs[:keep_count], refs[keep_count:]
+    out_hbm, *refs = refs
+    kept_hbm, (out_one, out_two, sems) = refs[:keep_count], refs[keep_count:]
+    sent = start_copies(list(zip(kept, kept_hbm)), sems.at[pl.ds(2, keep_count)])
     total = dot_tn(up_near[...], act_near[...]) + dot_tn(up_far[...], act_far[...])
     out_two[...] = total.astype(bf16)
-    sent = start_copies(
+    sent += start_copies(
         [(out_two, out_hbm.at[:, pl.ds(hidden, hidden)])], sems.at[pl.ds(0, 1)]
     )
     total = dot_tn(second_near[...], grad_near[...]) + dot_tn(second_far[...], grad_far[...])
@@ -937,7 +944,6 @@
         name="keep_rows",
         scratch=[half_x, half_x, DMA((2,))],
     )
-    upstream_chunks = [(x,) for x in upstream_rows]
     stream, first = kernel_call(
         functools.partial(prep_first_kernel, depth),
         [row_f32, row_bf16],
@@ -1012,26 +1018,31 @@
         for side in (1, 0):
             kept = (middle,) if side == 1 else ()
             saves = l + 1 < depth
-            loads = not saves and side == 1
+            loads = (mlp_w[l], *upstream_rows) if not saves and side == 1 else ()
             shapes = [
                 ((half, width), bf16),
                 ((half, hidden), bf16),
                 ((2, half, hidden // 2), f32),
             ]
             mlp[side] = kernel_call(
-                functools.partial(mlp_kernel, hidden, len(kept), saves, loads),
+                functools.partial(mlp_kernel, hidden, len(kept), saves, len(loads)),
                 [partial_out]
                 + [saved(*shape) if saves else shape for shape in shapes]
-                + [saved(k.shape, k.dtype) for k in kept],
+                + [saved(k.shape, k.dtype) for k in kept]
+                + [(v.shape, v.dtype) for v in loads],
                 *second_chunks[side],
                 Far(mlp_w[l]) if loads else mlp_w[l],
                 fc1_all[l],
                 *kept,
+                *[Far(v) for v in loads[1:]],
                 name="mlp",
                 scratch=[pltpu.VMEM(*shape) for shape in shapes if saves]
                 + [DMA((4 + len(kept),))]
-                + ([pltpu.VMEM((width, 2 * hidden), bf16), DMA((2,))] if loads else []),
+                + [DMA((len(loads) + 1,)) for _ in loads[:1]],
             )
+            if loads:
+                *mlp[side], mlp_w[l], near, far = mlp[side]
+                upstream_chunks = [(near,), (far,)]
         saved_all.append((attn, pairs if outer > 1 else None, mlp))
         if l + 1 < depth:
             (sums,) = reduce_rows((mlp[0][0], mlp[1][0]))
@@ -1077,9 +1088,12 @@
                 name="mlp_back",
                 scratch=[pltpu.VMEM((1, hidden), f32), DMA((1,))],
             )
-        mlp_grad, token = kernel_call(
-            functools.partial(mlp_grad_kernel, hidden),
-            [saved((width, 2 * hidden), bf16), TOKEN],
+        kept = [back[0][0], back[1][0]]
+        if l + 1 == depth:
+            kept += [mlp[0][0], mlp[1][0]]
+        mlp_grad, *kept = kernel_call(
+            functools.partial(mlp_grad_kernel, hidden, len(kept)),
+            [saved((width, 2 * hidden), bf16)] + [saved(k.shape, k.dtype) for k in kept],
             mlp[0][1],
             mlp[1][1],
             mlp[0][2],
@@ -1088,18 +1102,16 @@
             back[1][3],
             back[0][1],
             back[1][1],
+            *kept,
             name="mlp_grad",
             scratch=[
                 pltpu.VMEM((width, hidden), bf16),
                 pltpu.VMEM((width, hidden), bf16),
-                DMA((2,)),
+                DMA((2 + len(kept),)),
             ],
         )
         mlp_parts[l] = scatter_grads(mlp_grad)
-        pairs_now = [(back[0][0], back[1][0])]
-        if l + 1 == depth:
-            pairs_now.append((mlp[0][0], mlp[1][0]))
-        sums, *output_sums = reduce_rows(*pairs_now, after=(token,))
+        sums, *output_sums = reduce_rows(*zip(kept[0::2], kept[1::2]))
         if l + 1 == depth:
             outputs_own, output_token = kernel_call(
                 functools.partial(sum_out_kernel, shift_row(l, 3)),

time: 377 us -> 371 us (0.984)
  local copies, waits for them, and re-layouts: 14.7 us -> 8.84 us
    unnamed x114 -> x98, local copies, waits for them, and re-layouts: 14 us -> 8.12 us
  transfers between devices with their start and end apart: 108 -> 108, of which waited for: 51 -> 52; matrix products, arithmetic and copies ran while one was open for 0% -> 0% of each run, Pallas kernels for 20% -> 19%
where the time goes in v13:
time: 371 us; the launch traced here: 364 us
  waiting for transfers between devices  135 us (36%)
  starting transfers between devices  113 us (30%)
  Pallas kernels  91.4 us (25%)
  between operations  15.8 us (4%)
  local copies, waits for them, and re-layouts  8.84 us (2%)
    pallas_call x61, Pallas kernels, kernel_call(): pl.pallas_call(run, out_shape=out_shape, in_specs=specs, out_specs=out_sp...  91.4 us
    ppermute x43, starting transfers between devices, swap_core(): return lax.ppermute(value, 'ctx', [(i, i ^ 1) for i in range(ctx)])  55.4 us
    ppermute x16, waiting for transfers between devices, swap_xy(): return lax.ppermute(value, ('ctx', 'tp'), pairs)  38.4 us
    ppermute x18, waiting for transfers between devices, swap_x(): return lax.ppermute(value, 'ctx', [(i, i ^ 2) for i in range(ctx)])  33.8 us
    ppermute x6, waiting for transfers between devices, shift_z(): lax.ppermute(value, 'fsdp', [(i, (i + d) % fsdp) for i in range(fsdp)])  20.2 us
    all_gather x2, waiting for transfers between devices, per_device(): mlp_w.append(lax.all_gather(own, 'fsdp', axis=0, tiled=True))  17.8 us
    ppermute x16, starting transfers between devices, swap_xy(): return lax.ppermute(value, ('ctx', 'tp'), pairs)  17.4 us
    ppermute x18, waiting for transfers between devices, swap_y(): return lax.ppermute(value, 'tp', [(i, i ^ 1) for i in range(tp)])  15.3 us
  transfers between devices with their start and end apart: 108, of which 52 were waited for; matrix products, arithmetic and copies ran while one was open for 0% of the time, Pallas kernels for 19%

profile of v13, /device:TPU:9, one launch (start us, length us, event | category | flops | bytes accessed | tf_op | source)
XLA Modules:
  0.0 364.2 jit_solution(17701849754216436463)
XLA Ops:
  15.2 2.3 prep_upstream.1
  45.9 3.5 attn.5
  51.7 2.6 attn.4
  54.6 2.2 collective-permute-start.18
  57.3 3.6 collective-permute-done.18.refs_1_
  60.8 3.7 %collective-permute-done.19.refs_2_ = bf16[80,1024]{1,0:T(8,128)(2,1)S(1)} collective-permute-done((bf16[80,1024]{1,0:T(8,128)(2,1)S(1)}, bf16[80,1024]{1,0:T(8,128)(2,1)S(1)}, u32[]{:S(2)}, u32[]{:S(2)}) %collective-permute-start.19) | collective-permute-done | bytes 163872 | tf_op jit(solution)/shard_map/ppermute | solution.py:806
  73.1 2.5 collective-permute-start.26
  78.8 6.2 %all-gather.7.cloned.1.call-done.refs_4_ = bf16[1024,1024]{1,0:T(8,128)(2,1)} async-done(((bf16[256,1024]{1,0:T(8,128)(2,1)}), bf16[1024,1024]{1,0:T(8,128)(2,1)}) %all-gather.7.cloned.1.call-update) | async-done | bytes 2097168 | tf_op jit(solution)/shard_map/all_gather | solution.py:886
  94.1 3.6 collective-permute-done.29.refs_1_
  97.7 3.5 collective-permute-done.30.refs_2_
  110.0 2.3 collective-permute-start.37
  118.8 2.6 attn.7
  122.4 2.6 attn.6
  125.2 2.2 collective-permute-start.40
  127.9 4.2 %collective-permute-done.40.refs_1_ = bf16[80,1024]{1,0:T(8,128)(2,1)S(1)} collective-permute-done((bf16[80,1024]{1,0:T(8,128)(2,1)S(1)}, bf16[80,1024]{1,0:T(8,128)(2,1)S(1)}, u32[]{:S(2)}, u32[]{:S(2)}) %collective-permute-start.40) | collective-permute-done | bytes 163872 | tf_op jit(solution)/shard_map/ppermute | solution.py:815
  132.1 3.4 collective-permute-done.41.refs_2_
  143.9 2.3 collective-permute-start.48
  148.5 11.6 %all-gather.11.cloned.1.call-done.refs_4_ = bf16[1024,1024]{1,0:T(8,128)(2,1)} async-done(((bf16[256,1024]{1,0:T(8,128)(2,1)}), bf16[1024,1024]{1,0:T(8,128)(2,1)}) %all-gather.11.cloned.1.call-update) | async-done | bytes 2097168 | tf_op jit(solution)/shard_map/all_gather | solution.py:886
  160.1 3.7 %mlp.6 = (bf16[320,1024]{1,0:T(8,128)(2,1)S(1)}, bf16[320,1024]{1,0:T(8,128)(2,1)S(1)}, bf16[320,512]{1,0:T(8,128)(2,1)S(1)}, f32[2,320,256]{2,1,0:T(8,128)S(1)}...) custom-call(bf16[80,1024]{1,0:T(8,128)(2,1)S(1)} %collective-permute, ...), custom_call_target="tpu_custom_call" | custom-call | tf_op jit(solution)/shard_map/mlp/pallas_call | solution.py:79
  168.1 3.5 mlp_grad.2
  179.7 7.2 %collective-permute-done.52.refs_1_ = bf16[160,1024]{1,0:T(8,128)(2,1)S(1)} collective-permute-done((bf16[160,1024]{1,0:T(8,128)(2,1)S(1)}, bf16[160,1024]{1,0:T(8,128)(2,1)S(1)}, u32[]{:S(2)}, u32[]{:S(2)}) %collective-permute-start.52) | collective-permute-done | bytes 327712 | tf_op jit(solution)/shard_map/ppermute | solution.py:815
  186.9 7.1 %collective-permute-done.53.refs_2_ = bf16[160,1024]{1,0:T(8,128)(2,1)S(1)} collective-permute-done((bf16[160,1024]{1,0:T(8,128)(2,1)S(1)}, bf16[160,1024]{1,0:T(8,128)(2,1)S(1)}, u32[]{:S(2)}, u32[]{:S(2)}) %collective-permute-start.53) | collective-permute-done | bytes 327712 | tf_op jit(solution)/shard_map/ppermute | solution.py:806
  204.8 2.3 collective-permute-start.61
  209.5 2.5 attn_back.4
  212.1 2.5 attn_back.5
  217.4 2.2 collective-permute-start.64
  220.1 3.9 %collective-permute-done.64.refs_1_ = bf16[80,1024]{1,0:T(8,128)(2,1)S(1)} collective-permute-done((bf16[80,1024]{1,0:T(8,128)(2,1)S(1)}, bf16[80,1024]{1,0:T(8,128)(2,1)S(1)}, u32[]{:S(2)}, u32[]{:S(2)}) %collective-permute-start.64) | collective-permute-done | bytes 163872 | tf_op jit(solution)/shard_map/ppermute | solution.py:815
  224.0 3.6 collective-permute-done.65.refs_2_
  229.4 2.7 attn_grad.2
  239.2 2.3 collective-permute-start.72
  247.7 3.4 mlp_grad.3
  254.4 2.2 collective-permute-start.75
  257.1 3.9 %collective-permute-done.75.refs_1_ = bf16[80,1024]{1,0:T(8,128)(2,1)S(1)} collective-permute-done((bf16[80,1024]{1,0:T(8,128)(2,1)S(1)}, bf16[80,1024]{1,0:T(8,128)(2,1)S(1)}, u32[]{:S(2)}, u32[]{:S(2)}) %collective-permute-start.75) | collective-permute-done | bytes 163872 | tf_op jit(solution)/shard_map/ppermute | solution.py:815
  261.0 3.6 collective-permute-done.76.refs_2_
  274.1 2.3 collective-permute-start.83
  278.6 2.5 attn_back.6
  281.2 2.5 attn_back.7
  286.5 2.2 collective-permute-start.86
  289.3 3.9 %collective-permute-done.86.refs_1_ = bf16[80,1024]{1,0:T(8,128)(2,1)S(1)} collective-permute-done((bf16[80,1024]{1,0:T(8,128)(2,1)S(1)}, bf16[80,1024]{1,0:T(8,128)(2,1)S(1)}, u32[]{:S(2)}, u32[]{:S(2)}) %collective-permute-start.86) | collective-permute-done | bytes 163872 | tf_op jit(solution)/shard_map/ppermute | solution.py:815
  293.2 3.7 %collective-permute-done.87.refs_2_ = bf16[80,1024]{1,0:T(8,128)(2,1)S(1)} collective-permute-done((bf16[80,1024]{1,0:T(8,128)(2,1)S(1)}, bf16[80,1024]{1,0:T(8,128)(2,1)S(1)}, u32[]{:S(2)}, u32[]{:S(2)}) %collective-permute-start.87) | collective-permute-done | bytes 163872 | tf_op jit(solution)/shard_map/ppermute | solution.py:806
  299.7 2.7 attn_grad.3
  306.9 2.9 collective-permute-start.91
  311.3 2.3 collective-permute-done.55.refs_1_.refs_7_
  313.6 2.2 collective-permute-start.93
  315.9 17.7 %collective-permute-done.92.refs_4_ = bf16[288,512]{1,0:T(8,128)(2,1)S(1)} collective-permute-done((bf16[288,512]{1,0:T(8,128)(2,1)S(1)}, bf16[288,512]{1,0:T(8,128)(2,1)S(1)}, u32[]{:S(2)}, u32[]{:S(2)}) %collective-permute-start.92) | collective-permute-done | bytes 294944 | tf_op jit(solution)/shard_map/ppermute | solution.py:818
  333.6 2.5 collective-permute-done.93.refs_5_
  342.0 5.1 %collective-permute-done.95.refs_2_ = f32[24,256]{1,0:T(8,128)S(1)} collective-permute-done((f32[24,256]{1,0:T(8,128)S(1)}, f32[24,256]{1,0:T(8,128)S(1)}, u32[]{:S(2)}, u32[]{:S(2)}) %collective-permute-start.95) | collective-permute-done | bytes 24608 | tf_op jit(solution)/shard_map/ppermute | solution.py:806
  352.3 4.9 %place.1 = (f32[2,3,256,512]{3,2,1,0:T(8,128)}, f32[2,512,256]{2,1,0:T(8,128)}, f32[2,256,2048]{2,1,0:T(8,128)}, f32[2,2048,256]{2,1,0:T(8,128)}) custom-call(bf16[512,512]{1,0:T(8,128)(2,1)S(1)} %get-tuple-element.372.refs_0_, bf16[512,512]{1,0:T(8,128)(2,1)S(1)} %collective-permute-done.99.refs_1_, bf16[2560,512]{1,0:T(8,128)(2,1)S(1)} %get-tuple-element.373.refs_2_, ...), custom_call_target="tpu_custom_call" | custom-call | tf_op jit(solution)/shard_map/place/pallas_call | solution.py:79
  (360 shorter events, 169.6 us)
Async XLA Ops:
  7.2 34.2 %all-gather.5.cloned.1.call-start = ((), (), s32[]{:S(2)}) async-start(), calls=%async_computation.3 | async-start | bytes 1310720 | tf_op jit(solution)/shard_map/all_gather | solution.py:884
  9.0 76.0 %all-gather.7.cloned.1.call-start = ((), (), s32[]{:S(2)}) async-start(), calls=%async_computation.4 | async-start | bytes 2621440 | tf_op jit(solution)/shard_map/all_gather | solution.py:886
  11.2 103.7 %all-gather.9.cloned.1.call-start = ((), (), s32[]{:S(2)}) async-start(), calls=%async_computation.5 | async-start | bytes 1310720 | tf_op jit(solution)/shard_map/all_gather | solution.py:884
  11.4 10.9 %collective-permute-start.2 = (bf16[17,256]{1,0:T(8,128)(2,1)S(1)}, bf16[17,256]{1,0:T(8,128)(2,1)S(1)}, u32[]{:S(2)}, u32[]{:S(2)}) collective-permute-start(bf16[17,256]{1,0:T(8,128)(2,1)S(1)} %fusion.1), channel_id=1, source_target_pairs={{0,8},{8,16},{16,24},{24,0},{1,9},{9,17},{17,25},{25,1},{2,10},{10... | collective-permute-start | bytes 26120 | tf_op jit(solution)/shard_map/ppermute | solution.py:818
  12.8 10.8 %collective-permute-start.1 = (bf16[17,256]{1,0:T(8,128)(2,1)S(1)}, bf16[17,256]{1,0:T(8,128)(2,1)S(1)}, u32[]{:S(2)}, u32[]{:S(2)}) collective-permute-start(bf16[17,256]{1,0:T(8,128)(2,1)S(1)} %fusion.1), channel_id=1, source_target_pairs={{0,16},{8,24},{16,0},{24,8},{1,17},{9,25},{17,1},{25,9},{2,18},{10... | collective-permute-start | bytes 26120 | tf_op jit(solution)/shard_map/ppermute | solution.py:818
  13.9 10.0 %collective-permute-start = (bf16[17,256]{1,0:T(8,128)(2,1)S(1)}, bf16[17,256]{1,0:T(8,128)(2,1)S(1)}, u32[]{:S(2)}, u32[]{:S(2)}) collective-permute-start(bf16[17,256]{1,0:T(8,128)(2,1)S(1)} %fusion.1), channel_id=1, source_target_pairs={{0,24},{8,0},{16,8},{24,16},{1,25},{9,1},{17,9},{25,17},{2,26},{10... | collective-permute-start | bytes 26120 | tf_op jit(solution)/shard_map/ppermute | solution.py:818
  17.6 9.2 %collective-permute-start.9 = (bf16[80,1024]{1,0:T(8,128)(2,1)S(1)}, bf16[80,1024]{1,0:T(8,128)(2,1)S(1)}, u32[]{:S(2)}, u32[]{:S(2)}) collective-permute-start(bf16[80,1024]{1,0:T(8,128)(2,1)S(1)} %get-tuple-element.198.refs_0_), channel_id=1, source_target_pairs={{0,2},{2,0},{4,6},{6,4},{1,3},{3,1},{5,7},{7,5},{8,10},{10,8},{12,... | collective-permute-start | bytes 491528 | tf_op jit(solution)/shard_map/ppermute | solution.py:803
  19.1 8.9 %collective-permute-start.8 = (bf16[80,1024]{1,0:T(8,128)(2,1)S(1)}, bf16[80,1024]{1,0:T(8,128)(2,1)S(1)}, u32[]{:S(2)}, u32[]{:S(2)}) collective-permute-start(bf16[80,1024]{1,0:T(8,128)(2,1)S(1)} %get-tuple-element.198.refs_0_), channel_id=1, source_target_pairs={{0,1},{1,0},{2,3},{3,2},{4,5},{5,4},{6,7},{7,6},{8,9},{9,8},{10,11... | collective-permute-start | bytes 491528 | tf_op jit(solution)/shard_map/ppermute | solution.py:809
  22.2 137.9 %all-gather.11.cloned.1.call-start = ((), (), s32[]{:S(2)}) async-start(), calls=%async_computation.6 | async-start | bytes 2621440 | tf_op jit(solution)/shard_map/all_gather | solution.py:886
  25.5 9.0 %collective-permute-start.5 = (bf16[80,1024]{1,0:T(8,128)(2,1)S(1)}, bf16[80,1024]{1,0:T(8,128)(2,1)S(1)}, u32[]{:S(2)}, u32[]{:S(2)}) collective-permute-start(bf16[80,1024]{1,0:T(8,128)(2,1)S(1)} %get-tuple-element.194.refs_0_), channel_id=1, source_target_pairs={{0,1},{1,0},{2,3},{3,2},{4,5},{5,4},{6,7},{7,6},{8,9},{9,8},{10,11... | collective-permute-start | bytes 491528 | tf_op jit(solution)/shard_map/ppermute | solution.py:809
  26.8 8.8 %collective-permute-start.4 = (bf16[80,1024]{1,0:T(8,128)(2,1)S(1)}, bf16[80,1024]{1,0:T(8,128)(2,1)S(1)}, u32[]{:S(2)}, u32[]{:S(2)}) collective-permute-start(bf16[80,1024]{1,0:T(8,128)(2,1)S(1)} %get-tuple-element.194.refs_0_), channel_id=1, source_target_pairs={{0,4},{2,6},{4,0},{6,2},{1,5},{3,7},{5,1},{7,3},{8,12},{10,14},{12... | collective-permute-start | bytes 491528 | tf_op jit(solution)/shard_map/ppermute | solution.py:806
  28.0 10.5 %collective-permute-start.3 = (bf16[80,1024]{1,0:T(8,128)(2,1)S(1)}, bf16[80,1024]{1,0:T(8,128)(2,1)}, u32[]{:S(2)}, u32[]{:S(2)}) collective-permute-start(bf16[80,1024]{1,0:T(8,128)(2,1)S(1)} %get-tuple-element.194.refs_0_), channel_id=1, source_target_pairs={{0,5},{1,4},{2,7},{3,6},{4,1},{5,0},{6,3},{7,2},{8,13},{9,12},{10,... | collective-permute-start | bytes 491528 | tf_op jit(solution)/shard_map/ppermute | solution.py:815
  28.2 11.4 %collective-permute-start.12 = (bf16[80,1024]{1,0:T(8,128)(2,1)S(1)}, bf16[80,1024]{1,0:T(8,128)(2,1)S(1)}, u32[]{:S(2)}, u32[]{:S(2)}) collective-permute-start(bf16[80,1024]{1,0:T(8,128)(2,1)S(1)} %collective-permute-done.8.refs_3_), channel_id=1, source_target_pairs={{0,2},{2,0},{4,6},{6,4},{1,3},{3,1},{5,7},{7,5},{8,10},{10,8},{12,... | collective-permute-start | bytes 491528 | tf_op jit(solution)/shard_map/ppermute | solution.py:803
  31.3 8.3 %collective-permute-start.11 = (bf16[80,1024]{1,0:T(8,128)(2,1)S(1)}, bf16[80,1024]{1,0:T(8,128)(2,1)S(1)}, u32[]{:S(2)}, u32[]{:S(2)}) collective-permute-start(bf16[80,1024]{1,0:T(8,128)(2,1)S(1)} %collective-permute-done.7.refs_2_), channel_id=1, source_target_pairs={{0,2},{2,0},{4,6},{6,4},{1,3},{3,1},{5,7},{7,5},{8,10},{10,8},{12,... | collective-permute-start | bytes 491528 | tf_op jit(solution)/shard_map/ppermute | solution.py:803
  34.5 9.7 %collective-permute-start.13 = (bf16[80,1024]{1,0:T(8,128)(2,1)S(1)}, bf16[80,1024]{1,0:T(8,128)(2,1)}, u32[]{:S(2)}, u32[]{:S(2)}) collective-permute-start(bf16[80,1024]{1,0:T(8,128)(2,1)S(1)} %get-tuple-element.194.refs_0_), channel_id=1, source_target_pairs={{0,2},{2,0},{4,6},{6,4},{1,3},{3,1},{5,7},{7,5},{8,10},{10,8},{12,... | collective-permute-start | bytes 491528 | tf_op jit(solution)/shard_map/ppermute | solution.py:803
  51.5 180.8 %reduce-scatter.4.cloned.1.call-start = ((), (), s32[]{:S(2)}) async-start(), calls=%async_computation.7 | async-start | bytes 2621440 | tf_op jit(solution)/shard_map/reduce_scatter | solution.py:1063
  69.1 8.7 %collective-permute-start.24 = (bf16[80,1024]{1,0:T(8,128)(2,1)S(1)}, bf16[80,1024]{1,0:T(8,128)(2,1)S(1)}, u32[]{:S(2)}, u32[]{:S(2)}) collective-permute-start(bf16[80,1024]{1,0:T(8,128)(2,1)S(1)} %get-tuple-element.213.refs_0_), channel_id=1, source_target_pairs={{0,2},{2,0},{4,6},{6,4},{1,3},{3,1},{5,7},{7,5},{8,10},{10,8},{12,... | collective-permute-start | bytes 491528 | tf_op jit(solution)/shard_map/ppermute | solution.py:803
  93.8 8.2 %collective-permute-start.31 = (bf16[80,1024]{1,0:T(8,128)(2,1)S(1)}, bf16[80,1024]{1,0:T(8,128)(2,1)S(1)}, u32[]{:S(2)}, u32[]{:S(2)}) collective-permute-start(bf16[80,1024]{1,0:T(8,128)(2,1)S(1)} %get-tuple-element.221), channel_id=1, source_target_pairs={{0,1},{1,0},{2,3},{3,2},{4,5},{5,4},{6,7},{7,6},{8,9},{9,8},{10,11... | collective-permute-start | bytes 491528 | tf_op jit(solution)/shard_map/ppermute | solution.py:809
  106.0 10.6 %collective-permute-start.35 = (bf16[80,1024]{1,0:T(8,128)(2,1)S(1)}, bf16[80,1024]{1,0:T(8,128)(2,1)S(1)}, u32[]{:S(2)}, u32[]{:S(2)}) collective-permute-start(bf16[80,1024]{1,0:T(8,128)(2,1)S(1)} %get-tuple-element.223.refs_0_), channel_id=1, source_target_pairs={{0,2},{2,0},{4,6},{6,4},{1,3},{3,1},{5,7},{7,5},{8,10},{10,8},{12,... | collective-permute-start | bytes 491528 | tf_op jit(solution)/shard_map/ppermute | solution.py:803
  127.4 8.2 %collective-permute-start.41 = (bf16[80,1024]{1,0:T(8,128)(2,1)S(1)}, bf16[80,1024]{1,0:T(8,128)(2,1)S(1)}, u32[]{:S(2)}, u32[]{:S(2)}) collective-permute-start(bf16[80,1024]{1,0:T(8,128)(2,1)S(1)} %get-tuple-element.234), channel_id=1, source_target_pairs={{0,4},{2,6},{4,0},{6,2},{1,5},{3,7},{5,1},{7,3},{8,12},{10,14},{12... | collective-permute-start | bytes 491528 | tf_op jit(solution)/shard_map/ppermute | solution.py:806
  127.7 8.3 %collective-permute-start.42 = (bf16[80,1024]{1,0:T(8,128)(2,1)S(1)}, bf16[80,1024]{1,0:T(8,128)(2,1)S(1)}, u32[]{:S(2)}, u32[]{:S(2)}) collective-permute-start(bf16[80,1024]{1,0:T(8,128)(2,1)S(1)} %get-tuple-element.235), channel_id=1, source_target_pairs={{0,1},{1,0},{2,3},{3,2},{4,5},{5,4},{6,7},{7,6},{8,9},{9,8},{10,11... | collective-permute-start | bytes 491528 | tf_op jit(solution)/shard_map/ppermute | solution.py:809
  139.9 20.3 %collective-permute-start.46 = (bf16[80,1024]{1,0:T(8,128)(2,1)S(1)}, bf16[80,1024]{1,0:T(8,128)(2,1)S(1)}, u32[]{:S(2)}, u32[]{:S(2)}) collective-permute-start(bf16[80,1024]{1,0:T(8,128)(2,1)S(1)} %get-tuple-element.237.refs_0_), channel_id=1, source_target_pairs={{0,2},{2,0},{4,6},{6,4},{1,3},{3,1},{5,7},{7,5},{8,10},{10,8},{12,... | collective-permute-start | bytes 491528 | tf_op jit(solution)/shard_map/ppermute | solution.py:803
  142.6 17.5 %collective-permute-start.49 = (bf16[80,1024]{1,0:T(8,128)(2,1)S(1)}, bf16[80,1024]{1,0:T(8,128)(2,1)S(1)}, u32[]{:S(2)}, u32[]{:S(2)}) collective-permute-start(bf16[80,1024]{1,0:T(8,128)(2,1)S(1)} %collective-permute-done.45.refs_3_), channel_id=1, source_target_pairs={{0,2},{2,0},{4,6},{6,4},{1,3},{3,1},{5,7},{7,5},{8,10},{10,8},{12,... | collective-permute-start | bytes 491528 | tf_op jit(solution)/shard_map/ppermute | solution.py:803
  143.9 16.3 %collective-permute-start.48 = (bf16[80,1024]{1,0:T(8,128)(2,1)S(1)}, bf16[80,1024]{1,0:T(8,128)(2,1)}, u32[]{:S(2)}, u32[]{:S(2)}) collective-permute-start(bf16[80,1024]{1,0:T(8,128)(2,1)S(1)} %collective-permute-done.44.refs_2_), channel_id=1, source_target_pairs={{0,2},{2,0},{4,6},{6,4},{1,3},{3,1},{5,7},{7,5},{8,10},{10,8},{12,... | collective-permute-start | bytes 491528 | tf_op jit(solution)/shard_map/ppermute | solution.py:803
  146.9 13.2 %collective-permute-start.47 = (bf16[80,1024]{1,0:T(8,128)(2,1)S(1)}, bf16[80,1024]{1,0:T(8,128)(2,1)}, u32[]{:S(2)}, u32[]{:S(2)}) collective-permute-start(bf16[80,1024]{1,0:T(8,128)(2,1)S(1)} %collective-permute-done.43.refs_1_), channel_id=1, source_target_pairs={{0,2},{2,0},{4,6},{6,4},{1,3},{3,1},{5,7},{7,5},{8,10},{10,8},{12,... | collective-permute-start | bytes 491528 | tf_op jit(solution)/shard_map/ppermute | solution.py:803
  171.6 94.8 %reduce-scatter.6.cloned.1.call-start = ((), (), s32[]{:S(2)}) async-start(), calls=%async_computation.8 | async-start | bytes 1310720 | tf_op jit(solution)/shard_map/reduce_scatter | solution.py:1063
  177.0 9.9 %collective-permute-start.52 = (bf16[160,1024]{1,0:T(8,128)(2,1)S(1)}, bf16[160,1024]{1,0:T(8,128)(2,1)S(1)}, u32[]{:S(2)}, u32[]{:S(2)}) collective-permute-start(bf16[160,1024]{1,0:T(8,128)(2,1)S(1)} %get-tuple-element.265), channel_id=1, source_target_pairs={{0,5},{1,4},{2,7},{3,6},{4,1},{5,0},{6,3},{7,2},{8,13},{9,12},{10,... | collective-permute-start | bytes 983048 | tf_op jit(solution)/shard_map/ppermute | solution.py:815
  179.2 14.9 %collective-permute-start.53 = (bf16[160,1024]{1,0:T(8,128)(2,1)S(1)}, bf16[160,1024]{1,0:T(8,128)(2,1)S(1)}, u32[]{:S(2)}, u32[]{:S(2)}) collective-permute-start(bf16[160,1024]{1,0:T(8,128)(2,1)S(1)} %get-tuple-element.266), channel_id=1, source_target_pairs={{0,4},{2,6},{4,0},{6,2},{1,5},{3,7},{5,1},{7,3},{8,12},{10,14},{12... | collective-permute-start | bytes 983048 | tf_op jit(solution)/shard_map/ppermute | solution.py:806
  179.4 15.3 %collective-permute-start.54 = (bf16[160,1024]{1,0:T(8,128)(2,1)S(1)}, bf16[160,1024]{1,0:T(8,128)(2,1)S(1)}, u32[]{:S(2)}, u32[]{:S(2)}) collective-permute-start(bf16[160,1024]{1,0:T(8,128)(2,1)S(1)} %get-tuple-element.267), channel_id=1, source_target_pairs={{0,1},{1,0},{2,3},{3,2},{4,5},{5,4},{6,7},{7,6},{8,9},{9,8},{10,11... | collective-permute-start | bytes 983048 | tf_op jit(solution)/shard_map/ppermute | solution.py:809
  200.8 11.2 %collective-permute-start.59 = (bf16[80,1024]{1,0:T(8,128)(2,1)S(1)}, bf16[80,1024]{1,0:T(8,128)(2,1)S(1)}, u32[]{:S(2)}, u32[]{:S(2)}) collective-permute-start(bf16[80,1024]{1,0:T(8,128)(2,1)S(1)} %get-tuple-element.286.refs_0_), channel_id=1, source_target_pairs={{0,2},{2,0},{4,6},{6,4},{1,3},{3,1},{5,7},{7,5},{8,10},{10,8},{12,... | collective-permute-start | bytes 491528 | tf_op jit(solution)/shard_map/ppermute | solution.py:803
  203.6 8.4 %collective-permute-start.62 = (bf16[80,1024]{1,0:T(8,128)(2,1)S(1)}, bf16[80,1024]{1,0:T(8,128)(2,1)S(1)}, u32[]{:S(2)}, u32[]{:S(2)}) collective-permute-start(bf16[80,1024]{1,0:T(8,128)(2,1)S(1)} %collective-permute-done.58.refs_3_), channel_id=1, source_target_pairs={{0,2},{2,0},{4,6},{6,4},{1,3},{3,1},{5,7},{7,5},{8,10},{10,8},{12,... | collective-permute-start | bytes 491528 | tf_op jit(solution)/shard_map/ppermute | solution.py:803
  219.8 8.2 %collective-permute-start.66 = (bf16[80,1024]{1,0:T(8,128)(2,1)S(1)}, bf16[80,1024]{1,0:T(8,128)(2,1)S(1)}, u32[]{:S(2)}, u32[]{:S(2)}) collective-permute-start(bf16[80,1024]{1,0:T(8,128)(2,1)S(1)} %get-tuple-element.302), channel_id=1, source_target_pairs={{0,1},{1,0},{2,3},{3,2},{4,5},{5,4},{6,7},{7,6},{8,9},{9,8},{10,11... | collective-permute-start | bytes 491528 | tf_op jit(solution)/shard_map/ppermute | solution.py:809
  232.1 70.7 %reduce-scatter.8.cloned.1.call-start = ((), (), s32[]{:S(2)}) async-start(), calls=%async_computation.9 | async-start | bytes 2621440 | tf_op jit(solution)/shard_map/reduce_scatter | solution.py:1063
  235.1 11.1 %collective-permute-start.70 = (bf16[80,1024]{1,0:T(8,128)(2,1)S(1)}, bf16[80,1024]{1,0:T(8,128)(2,1)S(1)}, u32[]{:S(2)}, u32[]{:S(2)}) collective-permute-start(bf16[80,1024]{1,0:T(8,128)(2,1)S(1)} %settle.2.refs_0_), channel_id=1, source_target_pairs={{0,2},{2,0},{4,6},{6,4},{1,3},{3,1},{5,7},{7,5},{8,10},{10,8},{12,... | collective-permute-start | bytes 491528 | tf_op jit(solution)/shard_map/ppermute | solution.py:803
  237.6 8.6 %collective-permute-start.73 = (bf16[80,1024]{1,0:T(8,128)(2,1)S(1)}, bf16[80,1024]{1,0:T(8,128)(2,1)S(1)}, u32[]{:S(2)}, u32[]{:S(2)}) collective-permute-start(bf16[80,1024]{1,0:T(8,128)(2,1)S(1)} %collective-permute-done.69.refs_3_), channel_id=1, source_target_pairs={{0,2},{2,0},{4,6},{6,4},{1,3},{3,1},{5,7},{7,5},{8,10},{10,8},{12,... | collective-permute-start | bytes 491528 | tf_op jit(solution)/shard_map/ppermute | solution.py:803
  256.8 8.2 %collective-permute-start.77 = (bf16[80,1024]{1,0:T(8,128)(2,1)S(1)}, bf16[80,1024]{1,0:T(8,128)(2,1)S(1)}, u32[]{:S(2)}, u32[]{:S(2)}) collective-permute-start(bf16[80,1024]{1,0:T(8,128)(2,1)S(1)} %get-tuple-element.323), channel_id=1, source_target_pairs={{0,1},{1,0},{2,3},{3,2},{4,5},{5,4},{6,7},{7,6},{8,9},{9,8},{10,11... | collective-permute-start | bytes 491528 | tf_op jit(solution)/shard_map/ppermute | solution.py:809
  270.0 11.2 %collective-permute-start.81 = (bf16[80,1024]{1,0:T(8,128)(2,1)S(1)}, bf16[80,1024]{1,0:T(8,128)(2,1)S(1)}, u32[]{:S(2)}, u32[]{:S(2)}) collective-permute-start(bf16[80,1024]{1,0:T(8,128)(2,1)S(1)} %get-tuple-element.329.refs_0_), channel_id=1, source_target_pairs={{0,2},{2,0},{4,6},{6,4},{1,3},{3,1},{5,7},{7,5},{8,10},{10,8},{12,... | collective-permute-start | bytes 491528 | tf_op jit(solution)/shard_map/ppermute | solution.py:803
  272.6 8.5 %collective-permute-start.84 = (bf16[80,1024]{1,0:T(8,128)(2,1)S(1)}, bf16[80,1024]{1,0:T(8,128)(2,1)S(1)}, u32[]{:S(2)}, u32[]{:S(2)}) collective-permute-start(bf16[80,1024]{1,0:T(8,128)(2,1)S(1)} %collective-permute-done.80.refs_3_), channel_id=1, source_target_pairs={{0,2},{2,0},{4,6},{6,4},{1,3},{3,1},{5,7},{7,5},{8,10},{10,8},{12,... | collective-permute-start | bytes 491528 | tf_op jit(solution)/shard_map/ppermute | solution.py:803
  288.7 8.1 %collective-permute-start.87 = (bf16[80,1024]{1,0:T(8,128)(2,1)S(1)}, bf16[80,1024]{1,0:T(8,128)(2,1)S(1)}, u32[]{:S(2)}, u32[]{:S(2)}) collective-permute-start(bf16[80,1024]{1,0:T(8,128)(2,1)S(1)} %get-tuple-element.344), channel_id=1, source_target_pairs={{0,4},{2,6},{4,0},{6,2},{1,5},{3,7},{5,1},{7,3},{8,12},{10,14},{12... | collective-permute-start | bytes 491528 | tf_op jit(solution)/shard_map/ppermute | solution.py:806
  289.0 8.3 %collective-permute-start.88 = (bf16[80,1024]{1,0:T(8,128)(2,1)S(1)}, bf16[80,1024]{1,0:T(8,128)(2,1)S(1)}, u32[]{:S(2)}, u32[]{:S(2)}) collective-permute-start(bf16[80,1024]{1,0:T(8,128)(2,1)S(1)} %get-tuple-element.345), channel_id=1, source_target_pairs={{0,1},{1,0},{2,3},{3,2},{4,5},{5,4},{6,7},{7,6},{8,9},{9,8},{10,11... | collective-permute-start | bytes 491528 | tf_op jit(solution)/shard_map/ppermute | solution.py:809
  304.2 31.9 %collective-permute-start.90 = (bf16[1280,512]{1,0:T(8,128)(2,1)S(1)}, bf16[1280,512]{1,0:T(8,128)(2,1)S(1)}, u32[]{:S(2)}, u32[]{:S(2)}) collective-permute-start(bf16[1280,512]{1,0:T(8,128)(2,1)S(1)} %fetch.1.refs_1_), channel_id=1, source_target_pairs={{0,4},{2,6},{4,0},{6,2},{1,5},{3,7},{5,1},{7,3},{8,12},{10,14},{12... | collective-permute-start | bytes 3932168 | tf_op jit(solution)/shard_map/ppermute | solution.py:806
  305.4 8.2 %collective-permute-start.55 = (f32[80,1024]{1,0:T(8,128)S(1)}, f32[80,1024]{1,0:T(8,128)S(1)}, u32[]{:S(2)}, u32[]{:S(2)}) collective-permute-start(f32[80,1024]{1,0:T(8,128)S(1)} %copy-done.26), channel_id=1, source_target_pairs={{0,1},{1,0},{2,3},{3,2},{4,5},{5,4},{6,7},{7,6},{8,9},{9,8},{10,11... | collective-permute-start | bytes 983048 | tf_op jit(solution)/shard_map/ppermute | solution.py:809
  306.6 29.5 %collective-permute-start.89 = (f32[80,1024]{1,0:T(8,128)S(1)}, f32[80,1024]{1,0:T(8,128)S(1)}, u32[]{:S(2)}, u32[]{:S(2)}) collective-permute-start(f32[80,1024]{1,0:T(8,128)S(1)} %copy-done.27), channel_id=1, source_target_pairs={{0,1},{1,0},{2,3},{3,2},{4,5},{5,4},{6,7},{7,6},{8,9},{9,8},{10,11... | collective-permute-start | bytes 983048 | tf_op jit(solution)/shard_map/ppermute | solution.py:809
  306.9 9.0 %collective-permute-start.91 = (bf16[288,512]{1,0:T(8,128)(2,1)S(1)}, bf16[288,512]{1,0:T(8,128)(2,1)S(1)}, u32[]{:S(2)}, u32[]{:S(2)}) collective-permute-start(bf16[288,512]{1,0:T(8,128)(2,1)S(1)} %copy-done.45), channel_id=1, source_target_pairs={{0,8},{8,16},{16,24},{24,0},{1,9},{9,17},{17,25},{25,1},{2,10},{10... | collective-permute-start | bytes 884744 | tf_op jit(solution)/shard_map/ppermute | solution.py:818
  309.8 23.8 %collective-permute-start.92 = (bf16[288,512]{1,0:T(8,128)(2,1)S(1)}, bf16[288,512]{1,0:T(8,128)(2,1)S(1)}, u32[]{:S(2)}, u32[]{:S(2)}) collective-permute-start(bf16[288,512]{1,0:T(8,128)(2,1)S(1)} %copy-done.44), channel_id=1, source_target_pairs={{0,16},{8,24},{16,0},{24,8},{1,17},{9,25},{17,1},{25,9},{2,18},{10... | collective-permute-start | bytes 884744 | tf_op jit(solution)/shard_map/ppermute | solution.py:818
  313.6 22.5 %collective-permute-start.93 = (bf16[288,512]{1,0:T(8,128)(2,1)S(1)}, bf16[288,512]{1,0:T(8,128)(2,1)S(1)}, u32[]{:S(2)}, u32[]{:S(2)}) collective-permute-start(bf16[288,512]{1,0:T(8,128)(2,1)S(1)} %copy-done.43), channel_id=1, source_target_pairs={{0,24},{8,0},{16,8},{24,16},{1,25},{9,1},{17,9},{25,17},{2,26},{10... | collective-permute-start | bytes 884744 | tf_op jit(solution)/shard_map/ppermute | solution.py:818
  337.2 15.0 %collective-permute-start.100 = (bf16[2560,512]{1,0:T(8,128)(2,1)S(1)}, bf16[2560,512]{1,0:T(8,128)(2,1)S(1)}, u32[]{:S(2)}, u32[]{:S(2)}) collective-permute-start(bf16[2560,512]{1,0:T(8,128)(2,1)S(1)} %get-tuple-element.373.refs_2_), channel_id=1, source_target_pairs={{0,2},{2,0},{4,6},{6,4},{1,3},{3,1},{5,7},{7,5},{8,10},{10,8},{12,... | collective-permute-start | bytes 7864328 | tf_op jit(solution)/shard_map/ppermute | solution.py:803
  338.7 9.6 %collective-permute-start.97 = (bf16[256,512]{1,0:T(8,128)(2,1)S(1)}, bf16[256,512]{1,0:T(8,128)(2,1)S(1)}, u32[]{:S(2)}, u32[]{:S(2)}) collective-permute-start(bf16[256,512]{1,0:T(8,128)(2,1)S(1)} %get-tuple-element.366.refs_4_), channel_id=1, source_target_pairs={{0,4},{2,6},{4,0},{6,2},{1,5},{3,7},{5,1},{7,3},{8,12},{10,14},{12... | collective-permute-start | bytes 786440 | tf_op jit(solution)/shard_map/ppermute | solution.py:806
  (106 other events, 988.5 us)
Sparse Core Ops, SparseCore 0:
  10.2 28.8 all-gather.4
  41.2 43.7 all-gather.6
  86.6 28.2 all-gather.8
  116.3 43.8 all-gather.10
  171.8 42.2 reduce-scatter.3
  232.2 25.4 reduce-scatter.5
  260.6 42.1 reduce-scatter.7

commit v14 on v13

--- a/solution.py
+++ b/solution.py
@@ -42,6 +42,11 @@
         self.value = value
 
 
+class Anywhere:
+    def __init__(self, value):
+        self.value = value
+
+
 class Scalars:
     def __init__(self, value):
         self.value = value
@@ -57,6 +62,9 @@
         if isinstance(arg, Far):
             values.append(pltpu.with_memory_space_constraint(arg.value, pltpu.HBM))
             specs.append(HBM)
+        elif isinstance(arg, Anywhere):
+            values.append(arg.value)
+            specs.append(pl.BlockSpec(memory_space=pl.ANY))
         elif isinstance(arg, Scalars):
             values.append(arg.value)
             specs.append(SMEM)
@@ -332,7 +340,12 @@
     loaded = []
     if load_count:
         w_ref, *targets = rest[:load_count]
-        *rest, load_sems = rest[load_count:]
+        *rest, load_sems, chunk_sems = rest[load_count:]
+        rows = c0.shape[0]
+        chunks = start_copies(
+            [(c, x_out.at[pl.ds(k * rows, rows), :]) for k, c in enumerate((c0, c1, c2, c3))],
+            chunk_sems,
+        )
         spans = (pl.ds(0, hidden), pl.ds(hidden, hidden))
         loaded = start_copies(
             [(w.at[:, c], w_ref.at[:, c]) for c in spans] + list(zip(sources, targets)), load_sems
@@ -344,7 +357,11 @@
         x, act_ref, slope_ref = x_out, act_out, slope_out
         (sems,) = rest
     copies = start_copies(list(zip(kept, kept_hbm)), sems)
-    assemble((c0, c1, c2, c3), x)
+    if load_count:
+        for chunk in chunks:
+            chunk.wait()
+    else:
+        assemble((c0, c1, c2, c3), x)
     if saves:
         copies += start_copies([(x, x_out)], sems.at[pl.ds(keep_count, 1)])
     block = hidden // 2
@@ -412,12 +429,9 @@
     return back, gain_grad, jnp.sum(upstream, axis=0, keepdims=True)
 
 
-def norm_back_two_kernel(gain_row, own, xy, x, y, values_hbm, upstream_hbm, vecs,
-                         grad_ref, grad_b_ref, sums_ref, values, upstream, sems):
-    copies = start_copies([(values_hbm, values), (upstream_hbm, upstream)], sems)
+def norm_back_two_kernel(gain_row, own, xy, x, y, values, upstream, vecs,
+                         grad_ref, grad_b_ref, sums_ref):
     total = total_of(own, xy, x, y)
-    for copy in copies:
-        copy.wait()
     up = upstream[...]
     back, gain_grad, shift_grad = norm_back(
         total, values[...], vecs[gain_row : gain_row + 1, :]
@@ -431,12 +445,9 @@
     sums_ref[3:4, :] = jnp.sum(up, axis=0, keepdims=True)
 
 
-def norm_back_one_kernel(gain_row, own, xy, x, y, values_hbm, upstream_hbm, vecs, mask,
-                         grad_ref, grad_b_ref, sums_ref, values, upstream, sems):
-    copies = start_copies([(values_hbm, values), (upstream_hbm, upstream)], sems)
+def norm_back_one_kernel(gain_row, own, xy, x, y, values, upstream, vecs, mask,
+                         grad_ref, grad_b_ref, sums_ref):
     total = total_of(own, xy, x, y)
-    for copy in copies:
-        copy.wait()
     back, gain_grad, shift_grad = norm_back(
         total, values[...], vecs[gain_row : gain_row + 1, :]
     )
@@ -1030,7 +1041,7 @@
                 + [saved(*shape) if saves else shape for shape in shapes]
                 + [saved(k.shape, k.dtype) for k in kept]
                 + [(v.shape, v.dtype) for v in loads],
-                *second_chunks[side],
+                *[Anywhere(c) if loads else c for c in second_chunks[side]],
                 Far(mlp_w[l]) if loads else mlp_w[l],
                 fc1_all[l],
                 *kept,
@@ -1038,7 +1049,7 @@
                 name="mlp",
                 scratch=[pltpu.VMEM(*shape) for shape in shapes if saves]
                 + [DMA((4 + len(kept),))]
-                + [DMA((len(loads) + 1,)) for _ in loads[:1]],
+                + ([DMA((len(loads) + 1,)), DMA((CHIPS,))] if loads else []),
             )
             if loads:
                 *mlp[side], mlp_w[l], near, far = mlp[side]
@@ -1131,12 +1142,11 @@
             functools.partial(norm_back_two_kernel, gain_row(l, 1)),
             [row_f32, row_bf16, ((4, width), f32)],
             *sums,
-            Far(mlp[1][4]),
-            Far(upstream),
+            mlp[1][4],
+            upstream,
             vecs,
             name="norm_back_two",
             after=after,
-            scratch=[pltpu.VMEM((rows, width), f32)] * 2 + [DMA((2,))],
         )
         if l + 1 < depth:
             middle_b, sums_two, grad_middle = settle(
@@ -1214,12 +1224,11 @@
             body,
             [row_f32, row_bf16, ((2, width), f32)],
             *sums,
-            Far(attn[1][5]),
-            Far(grad_middle) if l + 1 < depth else grad_middle,
+            attn[1][5],
+            grad_middle,
             vecs,
             *masked,
             name="norm_back_one",
-            scratch=[pltpu.VMEM((rows, width), f32)] * 2 + [DMA((2,))],
         )
         lines = ()
         if l == 0:

time: 371 us -> 368 us (level)
  Pallas kernels: 91.4 us -> 86.6 us
    pallas_call x61, Pallas kernels: 91.4 us -> 86.6 us  [kernel_call(): pl.pallas_call(run, out_shape=out_shape, in_specs=specs, out_specs=out_sp...]
    unnamed x98 -> x110, local copies, waits for them, and re-layouts: 8.12 us -> 7.13 us
  transfers between devices with their start and end apart: 108 -> 108, of which waited for: 52 -> 52; matrix products, arithmetic and copies ran while one was open for 0% -> 0% of each run, Pallas kernels for 19% -> 18%
where the time goes in v14:
time: 368 us; the launch traced here: 361 us
  waiting for transfers between devices  138 us (38%)
  starting transfers between devices  114 us (31%)
  Pallas kernels  86.6 us (24%)
  between operations  15.8 us (4%)
  local copies, waits for them, and re-layouts  7.85 us (2%)
    pallas_call x61, Pallas kernels, kernel_call(): pl.pallas_call(run, out_shape=out_shape, in_specs=specs, out_specs=out_sp...  86.6 us
    ppermute x43, starting transfers between devices, swap_core(): return lax.ppermute(value, 'ctx', [(i, i ^ 1) for i in range(ctx)])  55.7 us
    ppermute x16, waiting for transfers between devices, swap_xy(): return lax.ppermute(value, ('ctx', 'tp'), pairs)  38.3 us
    ppermute x18, waiting for transfers between devices, swap_x(): return lax.ppermute(value, 'ctx', [(i, i ^ 2) for i in range(ctx)])  33.8 us
    ppermute x6, waiting for transfers between devices, shift_z(): lax.ppermute(value, 'fsdp', [(i, (i + d) % fsdp) for i in range(fsdp)])  20.2 us
    all_gather x2, waiting for transfers between devices, per_device(): mlp_w.append(lax.all_gather(own, 'fsdp', axis=0, tiled=True))  17.9 us
    ppermute x16, starting transfers between devices, swap_xy(): return lax.ppermute(value, ('ctx', 'tp'), pairs)  17.3 us
    ppermute x18, waiting for transfers between devices, swap_y(): return lax.ppermute(value, 'tp', [(i, i ^ 1) for i in range(tp)])  15 us
  transfers between devices with their start and end apart: 108, of which 52 were waited for; matrix products, arithmetic and copies ran while one was open for 0% of the time, Pallas kernels for 18%

profile of v14, /device:TPU:9, one launch (start us, length us, event | category | flops | bytes accessed | tf_op | source)
XLA Modules:
  0.0 361.5 jit_solution(17812604800366288494)
XLA Ops:
  15.2 2.3 prep_upstream.1
  45.9 3.5 attn.5
  51.7 2.6 attn.4
  54.6 2.2 collective-permute-start.18
  57.3 3.5 collective-permute-done.18.refs_1_
  60.8 3.7 %collective-permute-done.19.refs_2_ = bf16[80,1024]{1,0:T(8,128)(2,1)S(1)} collective-permute-done((bf16[80,1024]{1,0:T(8,128)(2,1)S(1)}, bf16[80,1024]{1,0:T(8,128)(2,1)S(1)}, u32[]{:S(2)}, u32[]{:S(2)}) %collective-permute-start.19) | collective-permute-done | bytes 163872 | tf_op jit(solution)/shard_map/ppermute | solution.py:817
  73.1 2.5 collective-permute-start.26
  78.8 6.3 %all-gather.7.cloned.1.call-done.refs_4_ = bf16[1024,1024]{1,0:T(8,128)(2,1)} async-done(((bf16[256,1024]{1,0:T(8,128)(2,1)}), bf16[1024,1024]{1,0:T(8,128)(2,1)}) %all-gather.7.cloned.1.call-update) | async-done | bytes 2097168 | tf_op jit(solution)/shard_map/all_gather | solution.py:897
  91.4 2.2 collective-permute-start.29
  94.1 3.6 collective-permute-done.29.refs_1_
  97.7 3.5 collective-permute-done.30.refs_2_
  110.0 2.3 collective-permute-start.37
  118.8 2.6 attn.7
  122.4 2.6 attn.6
  125.2 2.2 collective-permute-start.40
  127.9 4.2 %collective-permute-done.40.refs_1_ = bf16[80,1024]{1,0:T(8,128)(2,1)S(1)} collective-permute-done((bf16[80,1024]{1,0:T(8,128)(2,1)S(1)}, bf16[80,1024]{1,0:T(8,128)(2,1)S(1)}, u32[]{:S(2)}, u32[]{:S(2)}) %collective-permute-start.40) | collective-permute-done | bytes 163872 | tf_op jit(solution)/shard_map/ppermute | solution.py:826
  132.1 3.4 collective-permute-done.41.refs_2_
  143.8 2.3 collective-permute-start.48
  148.5 11.6 %all-gather.11.cloned.1.call-done.refs_4_ = bf16[1024,1024]{1,0:T(8,128)(2,1)} async-done(((bf16[256,1024]{1,0:T(8,128)(2,1)}), bf16[1024,1024]{1,0:T(8,128)(2,1)}) %all-gather.11.cloned.1.call-update) | async-done | bytes 2097168 | tf_op jit(solution)/shard_map/all_gather | solution.py:897
  160.1 3.6 %mlp.6 = (bf16[320,1024]{1,0:T(8,128)(2,1)S(1)}, bf16[320,1024]{1,0:T(8,128)(2,1)S(1)}, bf16[320,512]{1,0:T(8,128)(2,1)S(1)}, f32[2,320,256]{2,1,0:T(8,128)S(1)}...) custom-call(bf16[80,1024]{1,0:T(8,128)(2,1)S(1)} %collective-permute, ...), custom_call_target="tpu_custom_call" | custom-call | tf_op jit(solution)/shard_map/mlp/pallas_call | solution.py:87
  167.7 3.5 mlp_grad.2
  179.3 7.2 %collective-permute-done.52.refs_1_ = bf16[160,1024]{1,0:T(8,128)(2,1)S(1)} collective-permute-done((bf16[160,1024]{1,0:T(8,128)(2,1)S(1)}, bf16[160,1024]{1,0:T(8,128)(2,1)S(1)}, u32[]{:S(2)}, u32[]{:S(2)}) %collective-permute-start.52) | collective-permute-done | bytes 327712 | tf_op jit(solution)/shard_map/ppermute | solution.py:826
  186.5 7.1 %collective-permute-done.53.refs_2_ = bf16[160,1024]{1,0:T(8,128)(2,1)S(1)} collective-permute-done((bf16[160,1024]{1,0:T(8,128)(2,1)S(1)}, bf16[160,1024]{1,0:T(8,128)(2,1)S(1)}, u32[]{:S(2)}, u32[]{:S(2)}) %collective-permute-start.53) | collective-permute-done | bytes 327712 | tf_op jit(solution)/shard_map/ppermute | solution.py:817
  203.3 2.3 collective-permute-start.61
  208.0 2.5 attn_back.4
  210.5 2.5 attn_back.5
  218.6 3.9 %collective-permute-done.64.refs_1_ = bf16[80,1024]{1,0:T(8,128)(2,1)S(1)} collective-permute-done((bf16[80,1024]{1,0:T(8,128)(2,1)S(1)}, bf16[80,1024]{1,0:T(8,128)(2,1)S(1)}, u32[]{:S(2)}, u32[]{:S(2)}) %collective-permute-start.64) | collective-permute-done | bytes 163872 | tf_op jit(solution)/shard_map/ppermute | solution.py:826
  222.5 3.6 collective-permute-done.65.refs_2_
  226.9 2.7 attn_grad.2
  236.7 2.3 collective-permute-start.72
  245.2 3.4 mlp_grad.3
  248.8 2.3 collective-permute-done.74.refs_1_
  251.2 2.2 collective-permute-start.75
  253.9 3.9 %collective-permute-done.75.refs_1_ = bf16[80,1024]{1,0:T(8,128)(2,1)S(1)} collective-permute-done((bf16[80,1024]{1,0:T(8,128)(2,1)S(1)}, bf16[80,1024]{1,0:T(8,128)(2,1)S(1)}, u32[]{:S(2)}, u32[]{:S(2)}) %collective-permute-start.75) | collective-permute-done | bytes 163872 | tf_op jit(solution)/shard_map/ppermute | solution.py:826
  257.8 3.6 collective-permute-done.76.refs_2_
  269.9 2.3 collective-permute-start.83
  274.4 2.5 attn_back.6
  277.0 2.5 attn_back.7
  285.1 3.9 %collective-permute-done.86.refs_1_ = bf16[80,1024]{1,0:T(8,128)(2,1)S(1)} collective-permute-done((bf16[80,1024]{1,0:T(8,128)(2,1)S(1)}, bf16[80,1024]{1,0:T(8,128)(2,1)S(1)}, u32[]{:S(2)}, u32[]{:S(2)}) %collective-permute-start.86) | collective-permute-done | bytes 163872 | tf_op jit(solution)/shard_map/ppermute | solution.py:826
  289.0 3.7 %collective-permute-done.87.refs_2_ = bf16[80,1024]{1,0:T(8,128)(2,1)S(1)} collective-permute-done((bf16[80,1024]{1,0:T(8,128)(2,1)S(1)}, bf16[80,1024]{1,0:T(8,128)(2,1)S(1)}, u32[]{:S(2)}, u32[]{:S(2)}) %collective-permute-start.87) | collective-permute-done | bytes 163872 | tf_op jit(solution)/shard_map/ppermute | solution.py:817
  294.4 2.7 attn_grad.3
  297.1 2.8 reduce-scatter.8.cloned.1.call-done.refs_0_
  304.0 3.0 collective-permute-start.91
  310.7 2.4 collective-permute-start.93
  313.1 17.7 %collective-permute-done.92.refs_4_ = bf16[288,512]{1,0:T(8,128)(2,1)S(1)} collective-permute-done((bf16[288,512]{1,0:T(8,128)(2,1)S(1)}, bf16[288,512]{1,0:T(8,128)(2,1)S(1)}, u32[]{:S(2)}, u32[]{:S(2)}) %collective-permute-start.92) | collective-permute-done | bytes 294944 | tf_op jit(solution)/shard_map/ppermute | solution.py:829
  330.8 2.5 collective-permute-done.93.refs_5_
  339.2 5.1 %collective-permute-done.95.refs_2_ = f32[24,256]{1,0:T(8,128)S(1)} collective-permute-done((f32[24,256]{1,0:T(8,128)S(1)}, f32[24,256]{1,0:T(8,128)S(1)}, u32[]{:S(2)}, u32[]{:S(2)}) %collective-permute-start.95) | collective-permute-done | bytes 24608 | tf_op jit(solution)/shard_map/ppermute | solution.py:817
  349.5 4.9 %place.1 = (f32[2,3,256,512]{3,2,1,0:T(8,128)}, f32[2,512,256]{2,1,0:T(8,128)}, f32[2,256,2048]{2,1,0:T(8,128)}, f32[2,2048,256]{2,1,0:T(8,128)}) custom-call(bf16[512,512]{1,0:T(8,128)(2,1)S(1)} %get-tuple-element.372.refs_0_, bf16[512,512]{1,0:T(8,128)(2,1)S(1)} %collective-permute-done.99.refs_1_, bf16[2560,512]{1,0:T(8,128)(2,1)S(1)} %get-tuple-element.373.refs_2_, ...), custom_call_target="tpu_custom_call" | custom-call | tf_op jit(solution)/shard_map/place/pallas_call | solution.py:87
  (372 shorter events, 165.8 us)
Async XLA Ops:
  7.2 34.2 %all-gather.5.cloned.1.call-start = ((), (), s32[]{:S(2)}) async-start(), calls=%async_computation.3 | async-start | bytes 1310720 | tf_op jit(solution)/shard_map/all_gather | solution.py:895
  9.0 76.0 %all-gather.7.cloned.1.call-start = ((), (), s32[]{:S(2)}) async-start(), calls=%async_computation.4 | async-start | bytes 2621440 | tf_op jit(solution)/shard_map/all_gather | solution.py:897
  11.2 103.7 %all-gather.9.cloned.1.call-start = ((), (), s32[]{:S(2)}) async-start(), calls=%async_computation.5 | async-start | bytes 1310720 | tf_op jit(solution)/shard_map/all_gather | solution.py:895
  11.4 10.9 %collective-permute-start.2 = (bf16[17,256]{1,0:T(8,128)(2,1)S(1)}, bf16[17,256]{1,0:T(8,128)(2,1)S(1)}, u32[]{:S(2)}, u32[]{:S(2)}) collective-permute-start(bf16[17,256]{1,0:T(8,128)(2,1)S(1)} %fusion.1), channel_id=1, source_target_pairs={{0,8},{8,16},{16,24},{24,0},{1,9},{9,17},{17,25},{25,1},{2,10},{10... | collective-permute-start | bytes 26120 | tf_op jit(solution)/shard_map/ppermute | solution.py:829
  12.8 10.8 %collective-permute-start.1 = (bf16[17,256]{1,0:T(8,128)(2,1)S(1)}, bf16[17,256]{1,0:T(8,128)(2,1)S(1)}, u32[]{:S(2)}, u32[]{:S(2)}) collective-permute-start(bf16[17,256]{1,0:T(8,128)(2,1)S(1)} %fusion.1), channel_id=1, source_target_pairs={{0,16},{8,24},{16,0},{24,8},{1,17},{9,25},{17,1},{25,9},{2,18},{10... | collective-permute-start | bytes 26120 | tf_op jit(solution)/shard_map/ppermute | solution.py:829
  13.9 10.0 %collective-permute-start = (bf16[17,256]{1,0:T(8,128)(2,1)S(1)}, bf16[17,256]{1,0:T(8,128)(2,1)S(1)}, u32[]{:S(2)}, u32[]{:S(2)}) collective-permute-start(bf16[17,256]{1,0:T(8,128)(2,1)S(1)} %fusion.1), channel_id=1, source_target_pairs={{0,24},{8,0},{16,8},{24,16},{1,25},{9,1},{17,9},{25,17},{2,26},{10... | collective-permute-start | bytes 26120 | tf_op jit(solution)/shard_map/ppermute | solution.py:829
  17.6 9.2 %collective-permute-start.9 = (bf16[80,1024]{1,0:T(8,128)(2,1)S(1)}, bf16[80,1024]{1,0:T(8,128)(2,1)S(1)}, u32[]{:S(2)}, u32[]{:S(2)}) collective-permute-start(bf16[80,1024]{1,0:T(8,128)(2,1)S(1)} %get-tuple-element.198.refs_0_), channel_id=1, source_target_pairs={{0,2},{2,0},{4,6},{6,4},{1,3},{3,1},{5,7},{7,5},{8,10},{10,8},{12,... | collective-permute-start | bytes 491528 | tf_op jit(solution)/shard_map/ppermute | solution.py:814
  19.1 8.9 %collective-permute-start.8 = (bf16[80,1024]{1,0:T(8,128)(2,1)S(1)}, bf16[80,1024]{1,0:T(8,128)(2,1)S(1)}, u32[]{:S(2)}, u32[]{:S(2)}) collective-permute-start(bf16[80,1024]{1,0:T(8,128)(2,1)S(1)} %get-tuple-element.198.refs_0_), channel_id=1, source_target_pairs={{0,1},{1,0},{2,3},{3,2},{4,5},{5,4},{6,7},{7,6},{8,9},{9,8},{10,11... | collective-permute-start | bytes 491528 | tf_op jit(solution)/shard_map/ppermute | solution.py:820
  22.2 137.9 %all-gather.11.cloned.1.call-start = ((), (), s32[]{:S(2)}) async-start(), calls=%async_computation.6 | async-start | bytes 2621440 | tf_op jit(solution)/shard_map/all_gather | solution.py:897
  25.5 9.0 %collective-permute-start.5 = (bf16[80,1024]{1,0:T(8,128)(2,1)S(1)}, bf16[80,1024]{1,0:T(8,128)(2,1)S(1)}, u32[]{:S(2)}, u32[]{:S(2)}) collective-permute-start(bf16[80,1024]{1,0:T(8,128)(2,1)S(1)} %get-tuple-element.194.refs_0_), channel_id=1, source_target_pairs={{0,1},{1,0},{2,3},{3,2},{4,5},{5,4},{6,7},{7,6},{8,9},{9,8},{10,11... | collective-permute-start | bytes 491528 | tf_op jit(solution)/shard_map/ppermute | solution.py:820
  26.8 8.8 %collective-permute-start.4 = (bf16[80,1024]{1,0:T(8,128)(2,1)S(1)}, bf16[80,1024]{1,0:T(8,128)(2,1)S(1)}, u32[]{:S(2)}, u32[]{:S(2)}) collective-permute-start(bf16[80,1024]{1,0:T(8,128)(2,1)S(1)} %get-tuple-element.194.refs_0_), channel_id=1, source_target_pairs={{0,4},{2,6},{4,0},{6,2},{1,5},{3,7},{5,1},{7,3},{8,12},{10,14},{12... | collective-permute-start | bytes 491528 | tf_op jit(solution)/shard_map/ppermute | solution.py:817
  28.0 10.5 %collective-permute-start.3 = (bf16[80,1024]{1,0:T(8,128)(2,1)S(1)}, bf16[80,1024]{1,0:T(8,128)(2,1)}, u32[]{:S(2)}, u32[]{:S(2)}) collective-permute-start(bf16[80,1024]{1,0:T(8,128)(2,1)S(1)} %get-tuple-element.194.refs_0_), channel_id=1, source_target_pairs={{0,5},{1,4},{2,7},{3,6},{4,1},{5,0},{6,3},{7,2},{8,13},{9,12},{10,... | collective-permute-start | bytes 491528 | tf_op jit(solution)/shard_map/ppermute | solution.py:826
  28.2 11.4 %collective-permute-start.12 = (bf16[80,1024]{1,0:T(8,128)(2,1)S(1)}, bf16[80,1024]{1,0:T(8,128)(2,1)S(1)}, u32[]{:S(2)}, u32[]{:S(2)}) collective-permute-start(bf16[80,1024]{1,0:T(8,128)(2,1)S(1)} %collective-permute-done.8.refs_3_), channel_id=1, source_target_pairs={{0,2},{2,0},{4,6},{6,4},{1,3},{3,1},{5,7},{7,5},{8,10},{10,8},{12,... | collective-permute-start | bytes 491528 | tf_op jit(solution)/shard_map/ppermute | solution.py:814
  31.3 8.3 %collective-permute-start.11 = (bf16[80,1024]{1,0:T(8,128)(2,1)S(1)}, bf16[80,1024]{1,0:T(8,128)(2,1)S(1)}, u32[]{:S(2)}, u32[]{:S(2)}) collective-permute-start(bf16[80,1024]{1,0:T(8,128)(2,1)S(1)} %collective-permute-done.7.refs_2_), channel_id=1, source_target_pairs={{0,2},{2,0},{4,6},{6,4},{1,3},{3,1},{5,7},{7,5},{8,10},{10,8},{12,... | collective-permute-start | bytes 491528 | tf_op jit(solution)/shard_map/ppermute | solution.py:814
  34.5 9.7 %collective-permute-start.13 = (bf16[80,1024]{1,0:T(8,128)(2,1)S(1)}, bf16[80,1024]{1,0:T(8,128)(2,1)}, u32[]{:S(2)}, u32[]{:S(2)}) collective-permute-start(bf16[80,1024]{1,0:T(8,128)(2,1)S(1)} %get-tuple-element.194.refs_0_), channel_id=1, source_target_pairs={{0,2},{2,0},{4,6},{6,4},{1,3},{3,1},{5,7},{7,5},{8,10},{10,8},{12,... | collective-permute-start | bytes 491528 | tf_op jit(solution)/shard_map/ppermute | solution.py:814
  51.5 178.3 %reduce-scatter.4.cloned.1.call-start = ((), (), s32[]{:S(2)}) async-start(), calls=%async_computation.7 | async-start | bytes 2621440 | tf_op jit(solution)/shard_map/reduce_scatter | solution.py:1074
  69.1 8.7 %collective-permute-start.24 = (bf16[80,1024]{1,0:T(8,128)(2,1)S(1)}, bf16[80,1024]{1,0:T(8,128)(2,1)S(1)}, u32[]{:S(2)}, u32[]{:S(2)}) collective-permute-start(bf16[80,1024]{1,0:T(8,128)(2,1)S(1)} %get-tuple-element.213.refs_0_), channel_id=1, source_target_pairs={{0,2},{2,0},{4,6},{6,4},{1,3},{3,1},{5,7},{7,5},{8,10},{10,8},{12,... | collective-permute-start | bytes 491528 | tf_op jit(solution)/shard_map/ppermute | solution.py:814
  93.8 8.2 %collective-permute-start.31 = (bf16[80,1024]{1,0:T(8,128)(2,1)S(1)}, bf16[80,1024]{1,0:T(8,128)(2,1)S(1)}, u32[]{:S(2)}, u32[]{:S(2)}) collective-permute-start(bf16[80,1024]{1,0:T(8,128)(2,1)S(1)} %get-tuple-element.221), channel_id=1, source_target_pairs={{0,1},{1,0},{2,3},{3,2},{4,5},{5,4},{6,7},{7,6},{8,9},{9,8},{10,11... | collective-permute-start | bytes 491528 | tf_op jit(solution)/shard_map/ppermute | solution.py:820
  106.0 10.6 %collective-permute-start.35 = (bf16[80,1024]{1,0:T(8,128)(2,1)S(1)}, bf16[80,1024]{1,0:T(8,128)(2,1)S(1)}, u32[]{:S(2)}, u32[]{:S(2)}) collective-permute-start(bf16[80,1024]{1,0:T(8,128)(2,1)S(1)} %get-tuple-element.223.refs_0_), channel_id=1, source_target_pairs={{0,2},{2,0},{4,6},{6,4},{1,3},{3,1},{5,7},{7,5},{8,10},{10,8},{12,... | collective-permute-start | bytes 491528 | tf_op jit(solution)/shard_map/ppermute | solution.py:814
  127.4 8.2 %collective-permute-start.41 = (bf16[80,1024]{1,0:T(8,128)(2,1)S(1)}, bf16[80,1024]{1,0:T(8,128)(2,1)S(1)}, u32[]{:S(2)}, u32[]{:S(2)}) collective-permute-start(bf16[80,1024]{1,0:T(8,128)(2,1)S(1)} %get-tuple-element.234), channel_id=1, source_target_pairs={{0,4},{2,6},{4,0},{6,2},{1,5},{3,7},{5,1},{7,3},{8,12},{10,14},{12... | collective-permute-start | bytes 491528 | tf_op jit(solution)/shard_map/ppermute | solution.py:817
  127.6 8.3 %collective-permute-start.42 = (bf16[80,1024]{1,0:T(8,128)(2,1)S(1)}, bf16[80,1024]{1,0:T(8,128)(2,1)S(1)}, u32[]{:S(2)}, u32[]{:S(2)}) collective-permute-start(bf16[80,1024]{1,0:T(8,128)(2,1)S(1)} %get-tuple-element.235), channel_id=1, source_target_pairs={{0,1},{1,0},{2,3},{3,2},{4,5},{5,4},{6,7},{7,6},{8,9},{9,8},{10,11... | collective-permute-start | bytes 491528 | tf_op jit(solution)/shard_map/ppermute | solution.py:820
  139.8 20.3 %collective-permute-start.46 = (bf16[80,1024]{1,0:T(8,128)(2,1)S(1)}, bf16[80,1024]{1,0:T(8,128)(2,1)S(1)}, u32[]{:S(2)}, u32[]{:S(2)}) collective-permute-start(bf16[80,1024]{1,0:T(8,128)(2,1)S(1)} %get-tuple-element.237.refs_0_), channel_id=1, source_target_pairs={{0,2},{2,0},{4,6},{6,4},{1,3},{3,1},{5,7},{7,5},{8,10},{10,8},{12,... | collective-permute-start | bytes 491528 | tf_op jit(solution)/shard_map/ppermute | solution.py:814
  142.6 17.5 %collective-permute-start.49 = (bf16[80,1024]{1,0:T(8,128)(2,1)S(1)}, bf16[80,1024]{1,0:T(8,128)(2,1)S(1)}, u32[]{:S(2)}, u32[]{:S(2)}) collective-permute-start(bf16[80,1024]{1,0:T(8,128)(2,1)S(1)} %collective-permute-done.45.refs_3_), channel_id=1, source_target_pairs={{0,2},{2,0},{4,6},{6,4},{1,3},{3,1},{5,7},{7,5},{8,10},{10,8},{12,... | collective-permute-start | bytes 491528 | tf_op jit(solution)/shard_map/ppermute | solution.py:814
  143.8 16.3 %collective-permute-start.48 = (bf16[80,1024]{1,0:T(8,128)(2,1)S(1)}, bf16[80,1024]{1,0:T(8,128)(2,1)}, u32[]{:S(2)}, u32[]{:S(2)}) collective-permute-start(bf16[80,1024]{1,0:T(8,128)(2,1)S(1)} %collective-permute-done.44.refs_2_), channel_id=1, source_target_pairs={{0,2},{2,0},{4,6},{6,4},{1,3},{3,1},{5,7},{7,5},{8,10},{10,8},{12,... | collective-permute-start | bytes 491528 | tf_op jit(solution)/shard_map/ppermute | solution.py:814
  146.9 13.3 %collective-permute-start.47 = (bf16[80,1024]{1,0:T(8,128)(2,1)S(1)}, bf16[80,1024]{1,0:T(8,128)(2,1)}, u32[]{:S(2)}, u32[]{:S(2)}) collective-permute-start(bf16[80,1024]{1,0:T(8,128)(2,1)S(1)} %collective-permute-done.43.refs_1_), channel_id=1, source_target_pairs={{0,2},{2,0},{4,6},{6,4},{1,3},{3,1},{5,7},{7,5},{8,10},{10,8},{12,... | collective-permute-start | bytes 491528 | tf_op jit(solution)/shard_map/ppermute | solution.py:814
  171.2 91.1 %reduce-scatter.6.cloned.1.call-start = ((), (), s32[]{:S(2)}) async-start(), calls=%async_computation.8 | async-start | bytes 1310720 | tf_op jit(solution)/shard_map/reduce_scatter | solution.py:1074
  176.6 9.9 %collective-permute-start.52 = (bf16[160,1024]{1,0:T(8,128)(2,1)S(1)}, bf16[160,1024]{1,0:T(8,128)(2,1)S(1)}, u32[]{:S(2)}, u32[]{:S(2)}) collective-permute-start(bf16[160,1024]{1,0:T(8,128)(2,1)S(1)} %get-tuple-element.265), channel_id=1, source_target_pairs={{0,5},{1,4},{2,7},{3,6},{4,1},{5,0},{6,3},{7,2},{8,13},{9,12},{10,... | collective-permute-start | bytes 983048 | tf_op jit(solution)/shard_map/ppermute | solution.py:826
  178.7 14.9 %collective-permute-start.53 = (bf16[160,1024]{1,0:T(8,128)(2,1)S(1)}, bf16[160,1024]{1,0:T(8,128)(2,1)S(1)}, u32[]{:S(2)}, u32[]{:S(2)}) collective-permute-start(bf16[160,1024]{1,0:T(8,128)(2,1)S(1)} %get-tuple-element.266), channel_id=1, source_target_pairs={{0,4},{2,6},{4,0},{6,2},{1,5},{3,7},{5,1},{7,3},{8,12},{10,14},{12... | collective-permute-start | bytes 983048 | tf_op jit(solution)/shard_map/ppermute | solution.py:817
  179.0 15.3 %collective-permute-start.54 = (bf16[160,1024]{1,0:T(8,128)(2,1)S(1)}, bf16[160,1024]{1,0:T(8,128)(2,1)S(1)}, u32[]{:S(2)}, u32[]{:S(2)}) collective-permute-start(bf16[160,1024]{1,0:T(8,128)(2,1)S(1)} %get-tuple-element.267), channel_id=1, source_target_pairs={{0,1},{1,0},{2,3},{3,2},{4,5},{5,4},{6,7},{7,6},{8,9},{9,8},{10,11... | collective-permute-start | bytes 983048 | tf_op jit(solution)/shard_map/ppermute | solution.py:820
  199.3 11.2 %collective-permute-start.59 = (bf16[80,1024]{1,0:T(8,128)(2,1)S(1)}, bf16[80,1024]{1,0:T(8,128)(2,1)S(1)}, u32[]{:S(2)}, u32[]{:S(2)}) collective-permute-start(bf16[80,1024]{1,0:T(8,128)(2,1)S(1)} %get-tuple-element.286.refs_0_), channel_id=1, source_target_pairs={{0,2},{2,0},{4,6},{6,4},{1,3},{3,1},{5,7},{7,5},{8,10},{10,8},{12,... | collective-permute-start | bytes 491528 | tf_op jit(solution)/shard_map/ppermute | solution.py:814
  202.1 8.4 %collective-permute-start.62 = (bf16[80,1024]{1,0:T(8,128)(2,1)S(1)}, bf16[80,1024]{1,0:T(8,128)(2,1)S(1)}, u32[]{:S(2)}, u32[]{:S(2)}) collective-permute-start(bf16[80,1024]{1,0:T(8,128)(2,1)S(1)} %collective-permute-done.58.refs_3_), channel_id=1, source_target_pairs={{0,2},{2,0},{4,6},{6,4},{1,3},{3,1},{5,7},{7,5},{8,10},{10,8},{12,... | collective-permute-start | bytes 491528 | tf_op jit(solution)/shard_map/ppermute | solution.py:814
  218.3 8.2 %collective-permute-start.66 = (bf16[80,1024]{1,0:T(8,128)(2,1)S(1)}, bf16[80,1024]{1,0:T(8,128)(2,1)S(1)}, u32[]{:S(2)}, u32[]{:S(2)}) collective-permute-start(bf16[80,1024]{1,0:T(8,128)(2,1)S(1)} %get-tuple-element.302), channel_id=1, source_target_pairs={{0,1},{1,0},{2,3},{3,2},{4,5},{5,4},{6,7},{7,6},{8,9},{9,8},{10,11... | collective-permute-start | bytes 491528 | tf_op jit(solution)/shard_map/ppermute | solution.py:820
  229.6 70.4 %reduce-scatter.8.cloned.1.call-start = ((), (), s32[]{:S(2)}) async-start(), calls=%async_computation.9 | async-start | bytes 2621440 | tf_op jit(solution)/shard_map/reduce_scatter | solution.py:1074
  232.6 11.1 %collective-permute-start.70 = (bf16[80,1024]{1,0:T(8,128)(2,1)S(1)}, bf16[80,1024]{1,0:T(8,128)(2,1)S(1)}, u32[]{:S(2)}, u32[]{:S(2)}) collective-permute-start(bf16[80,1024]{1,0:T(8,128)(2,1)S(1)} %settle.2.refs_0_), channel_id=1, source_target_pairs={{0,2},{2,0},{4,6},{6,4},{1,3},{3,1},{5,7},{7,5},{8,10},{10,8},{12,... | collective-permute-start | bytes 491528 | tf_op jit(solution)/shard_map/ppermute | solution.py:814
  235.2 8.6 %collective-permute-start.73 = (bf16[80,1024]{1,0:T(8,128)(2,1)S(1)}, bf16[80,1024]{1,0:T(8,128)(2,1)S(1)}, u32[]{:S(2)}, u32[]{:S(2)}) collective-permute-start(bf16[80,1024]{1,0:T(8,128)(2,1)S(1)} %collective-permute-done.69.refs_3_), channel_id=1, source_target_pairs={{0,2},{2,0},{4,6},{6,4},{1,3},{3,1},{5,7},{7,5},{8,10},{10,8},{12,... | collective-permute-start | bytes 491528 | tf_op jit(solution)/shard_map/ppermute | solution.py:814
  253.6 8.2 %collective-permute-start.77 = (bf16[80,1024]{1,0:T(8,128)(2,1)S(1)}, bf16[80,1024]{1,0:T(8,128)(2,1)S(1)}, u32[]{:S(2)}, u32[]{:S(2)}) collective-permute-start(bf16[80,1024]{1,0:T(8,128)(2,1)S(1)} %get-tuple-element.323), channel_id=1, source_target_pairs={{0,1},{1,0},{2,3},{3,2},{4,5},{5,4},{6,7},{7,6},{8,9},{9,8},{10,11... | collective-permute-start | bytes 491528 | tf_op jit(solution)/shard_map/ppermute | solution.py:820
  265.7 11.2 %collective-permute-start.81 = (bf16[80,1024]{1,0:T(8,128)(2,1)S(1)}, bf16[80,1024]{1,0:T(8,128)(2,1)S(1)}, u32[]{:S(2)}, u32[]{:S(2)}) collective-permute-start(bf16[80,1024]{1,0:T(8,128)(2,1)S(1)} %get-tuple-element.329.refs_0_), channel_id=1, source_target_pairs={{0,2},{2,0},{4,6},{6,4},{1,3},{3,1},{5,7},{7,5},{8,10},{10,8},{12,... | collective-permute-start | bytes 491528 | tf_op jit(solution)/shard_map/ppermute | solution.py:814
  268.4 8.5 %collective-permute-start.84 = (bf16[80,1024]{1,0:T(8,128)(2,1)S(1)}, bf16[80,1024]{1,0:T(8,128)(2,1)S(1)}, u32[]{:S(2)}, u32[]{:S(2)}) collective-permute-start(bf16[80,1024]{1,0:T(8,128)(2,1)S(1)} %collective-permute-done.80.refs_3_), channel_id=1, source_target_pairs={{0,2},{2,0},{4,6},{6,4},{1,3},{3,1},{5,7},{7,5},{8,10},{10,8},{12,... | collective-permute-start | bytes 491528 | tf_op jit(solution)/shard_map/ppermute | solution.py:814
  284.5 8.1 %collective-permute-start.87 = (bf16[80,1024]{1,0:T(8,128)(2,1)S(1)}, bf16[80,1024]{1,0:T(8,128)(2,1)S(1)}, u32[]{:S(2)}, u32[]{:S(2)}) collective-permute-start(bf16[80,1024]{1,0:T(8,128)(2,1)S(1)} %get-tuple-element.344), channel_id=1, source_target_pairs={{0,4},{2,6},{4,0},{6,2},{1,5},{3,7},{5,1},{7,3},{8,12},{10,14},{12... | collective-permute-start | bytes 491528 | tf_op jit(solution)/shard_map/ppermute | solution.py:817
  284.8 8.3 %collective-permute-start.88 = (bf16[80,1024]{1,0:T(8,128)(2,1)S(1)}, bf16[80,1024]{1,0:T(8,128)(2,1)S(1)}, u32[]{:S(2)}, u32[]{:S(2)}) collective-permute-start(bf16[80,1024]{1,0:T(8,128)(2,1)S(1)} %get-tuple-element.345), channel_id=1, source_target_pairs={{0,1},{1,0},{2,3},{3,2},{4,5},{5,4},{6,7},{7,6},{8,9},{9,8},{10,11... | collective-permute-start | bytes 491528 | tf_op jit(solution)/shard_map/ppermute | solution.py:820
  301.3 32.0 %collective-permute-start.90 = (bf16[1280,512]{1,0:T(8,128)(2,1)S(1)}, bf16[1280,512]{1,0:T(8,128)(2,1)S(1)}, u32[]{:S(2)}, u32[]{:S(2)}) collective-permute-start(bf16[1280,512]{1,0:T(8,128)(2,1)S(1)} %fetch.1.refs_1_), channel_id=1, source_target_pairs={{0,4},{2,6},{4,0},{6,2},{1,5},{3,7},{5,1},{7,3},{8,12},{10,14},{12... | collective-permute-start | bytes 3932168 | tf_op jit(solution)/shard_map/ppermute | solution.py:817
  302.5 8.1 %collective-permute-start.55 = (f32[80,1024]{1,0:T(8,128)S(1)}, f32[80,1024]{1,0:T(8,128)S(1)}, u32[]{:S(2)}, u32[]{:S(2)}) collective-permute-start(f32[80,1024]{1,0:T(8,128)S(1)} %copy-done.31), channel_id=1, source_target_pairs={{0,1},{1,0},{2,3},{3,2},{4,5},{5,4},{6,7},{7,6},{8,9},{9,8},{10,11... | collective-permute-start | bytes 983048 | tf_op jit(solution)/shard_map/ppermute | solution.py:820
  303.7 29.6 %collective-permute-start.89 = (f32[80,1024]{1,0:T(8,128)S(1)}, f32[80,1024]{1,0:T(8,128)S(1)}, u32[]{:S(2)}, u32[]{:S(2)}) collective-permute-start(f32[80,1024]{1,0:T(8,128)S(1)} %copy-done.32), channel_id=1, source_target_pairs={{0,1},{1,0},{2,3},{3,2},{4,5},{5,4},{6,7},{7,6},{8,9},{9,8},{10,11... | collective-permute-start | bytes 983048 | tf_op jit(solution)/shard_map/ppermute | solution.py:820
  304.0 9.1 %collective-permute-start.91 = (bf16[288,512]{1,0:T(8,128)(2,1)S(1)}, bf16[288,512]{1,0:T(8,128)(2,1)S(1)}, u32[]{:S(2)}, u32[]{:S(2)}) collective-permute-start(bf16[288,512]{1,0:T(8,128)(2,1)S(1)} %copy-done.51), channel_id=1, source_target_pairs={{0,8},{8,16},{16,24},{24,0},{1,9},{9,17},{17,25},{25,1},{2,10},{10... | collective-permute-start | bytes 884744 | tf_op jit(solution)/shard_map/ppermute | solution.py:829
  307.0 23.8 %collective-permute-start.92 = (bf16[288,512]{1,0:T(8,128)(2,1)S(1)}, bf16[288,512]{1,0:T(8,128)(2,1)S(1)}, u32[]{:S(2)}, u32[]{:S(2)}) collective-permute-start(bf16[288,512]{1,0:T(8,128)(2,1)S(1)} %copy-done.50), channel_id=1, source_target_pairs={{0,16},{8,24},{16,0},{24,8},{1,17},{9,25},{17,1},{25,9},{2,18},{10... | collective-permute-start | bytes 884744 | tf_op jit(solution)/shard_map/ppermute | solution.py:829
  310.7 22.7 %collective-permute-start.93 = (bf16[288,512]{1,0:T(8,128)(2,1)S(1)}, bf16[288,512]{1,0:T(8,128)(2,1)S(1)}, u32[]{:S(2)}, u32[]{:S(2)}) collective-permute-start(bf16[288,512]{1,0:T(8,128)(2,1)S(1)} %copy-done.49), channel_id=1, source_target_pairs={{0,24},{8,0},{16,8},{24,16},{1,25},{9,1},{17,9},{25,17},{2,26},{10... | collective-permute-start | bytes 884744 | tf_op jit(solution)/shard_map/ppermute | solution.py:829
  334.5 15.0 %collective-permute-start.100 = (bf16[2560,512]{1,0:T(8,128)(2,1)S(1)}, bf16[2560,512]{1,0:T(8,128)(2,1)S(1)}, u32[]{:S(2)}, u32[]{:S(2)}) collective-permute-start(bf16[2560,512]{1,0:T(8,128)(2,1)S(1)} %get-tuple-element.373.refs_2_), channel_id=1, source_target_pairs={{0,2},{2,0},{4,6},{6,4},{1,3},{3,1},{5,7},{7,5},{8,10},{10,8},{12,... | collective-permute-start | bytes 7864328 | tf_op jit(solution)/shard_map/ppermute | solution.py:814
  335.9 9.6 %collective-permute-start.97 = (bf16[256,512]{1,0:T(8,128)(2,1)S(1)}, bf16[256,512]{1,0:T(8,128)(2,1)S(1)}, u32[]{:S(2)}, u32[]{:S(2)}) collective-permute-start(bf16[256,512]{1,0:T(8,128)(2,1)S(1)} %get-tuple-element.366.refs_4_), channel_id=1, source_target_pairs={{0,4},{2,6},{4,0},{6,2},{1,5},{3,7},{5,1},{7,3},{8,12},{10,14},{12... | collective-permute-start | bytes 786440 | tf_op jit(solution)/shard_map/ppermute | solution.py:817
  (112 other events, 1086.0 us)
Sparse Core Ops, SparseCore 0:
  10.2 28.8 all-gather.4
  41.2 43.8 all-gather.6
  86.6 28.1 all-gather.8
  116.3 43.8 all-gather.10
  171.3 41.9 reduce-scatter.3
  229.7 25.1 reduce-scatter.5
  257.8 42.1 reduce-scatter.7

commit v15 on v14

--- a/solution.py
+++ b/solution.py
@@ -628,41 +628,54 @@
         copy.wait()
 
 
-def place_kernel(depth, hidden, feats, *refs):
-    alone, pairs, rest = refs[:2], refs[2:4], refs[4:]
-
-    def half_of(pair, k):
-        count = pair[k % 2].shape[0] // 2
-        return pair[k % 2].at[pl.ds(k // 2 * count, count), :]
-
-    slices = [(half_of(alone, k), half_of(pairs, k)) for k in range(GROUP)]
-    qkv_hbm, out_hbm, fc1_hbm, fc2_hbm, fc1, fc2, qkv, out, sems = rest
+def place_kernel(depth, hidden, feats, here, sibling, *refs):
+    qkv_hbm, out_hbm, fc1_hbm, fc2_hbm, token, fc1, fc2, qkv, out, sems = refs
+    token[...] = jnp.zeros_like(token)
     ci = lax.rem(lax.axis_index("ctx"), GROUP)
     rows = fc1.shape[2]
+    count = here.shape[0] // 2
     copies = []
 
     def send(source, target):
         copies.extend(start_copies([(source, target)], sems.at[pl.ds(len(copies), 1)]))
 
-    for l in range(depth):
-        for k in range(GROUP):
-            _, stacked = slices[k]
+    for k in range(GROUP):
+        stacked = (here, sibling)[k % 2].at[pl.ds(k // 2 * count, count), :]
+        wide = pl.ds(pl.multiple_of((ci ^ k) * hidden, hidden), hidden)
+        narrow = pl.ds(pl.multiple_of((ci ^ k) * feats, feats), feats)
+        for l in range(depth):
             first = 0 if l == 0 else (3 * l - 1) * rows
-            span = pl.ds(pl.multiple_of((ci ^ k) * hidden, hidden), hidden)
             fc1[l, k] = stacked[first : first + rows, :].astype(f32)
-            send(fc1.at[l, k], fc1_hbm.at[l, :, span])
+            send(fc1.at[l, k], fc1_hbm.at[l, :, wide])
             fc2[l, k] = stacked[first + rows : first + 2 * rows, :].T.astype(f32)
-            send(fc2.at[l, k], fc2_hbm.at[l, span, :])
-    for l in reversed(range(depth)):
-        for k in range(GROUP):
-            last, stacked = slices[k]
-            piece = last if l == 0 else stacked.at[pl.ds((3 * l + 1) * rows, rows), :]
-            span = pl.ds(pl.multiple_of((ci ^ k) * feats, feats), feats)
-            for j in range(3):
-                qkv[l, k, j] = piece[:, j * feats : (j + 1) * feats].astype(f32)
-            send(qkv.at[l, k], qkv_hbm.at[l, :, :, span])
-            out[l, k] = piece[:, 3 * feats :].T.astype(f32)
-            send(out.at[l, k], out_hbm.at[l, span, :])
+            send(fc2.at[l, k], fc2_hbm.at[l, wide, :])
+            if l > 0:
+                piece = stacked.at[pl.ds(first + 2 * rows, rows), :]
+                for j in range(3):
+                    qkv[l - 1, k, j] = piece[:, j * feats : (j + 1) * feats].astype(f32)
+                send(qkv.at[l - 1, k], qkv_hbm.at[l, :, :, narrow])
+                out[l - 1, k] = piece[:, 3 * feats :].T.astype(f32)
+                send(out.at[l - 1, k], out_hbm.at[l, narrow, :])
+    for copy in copies:
+        copy.wait()
+
+
+def place_last_kernel(feats, here, sibling, qkv_in, out_in, qkv_hbm, out_hbm, qkv, out, sems):
+    ci = lax.rem(lax.axis_index("ctx"), GROUP)
+    rows = here.shape[0] // 2
+    copies = []
+    for k in range(GROUP):
+        piece = (here, sibling)[k % 2].at[pl.ds(k // 2 * rows, rows), :]
+        span = pl.ds(pl.multiple_of((ci ^ k) * feats, feats), feats)
+        for j in range(3):
+            qkv[k, j] = piece[:, j * feats : (j + 1) * feats].astype(f32)
+        copies += start_copies(
+            [(qkv.at[k], qkv_hbm.at[0, :, :, span])], sems.at[pl.ds(2 * k, 1)]
+        )
+        out[k] = piece[:, 3 * feats :].T.astype(f32)
+        copies += start_copies(
+            [(out.at[k], out_hbm.at[0, span, :])], sems.at[pl.ds(2 * k + 1, 1)]
+        )
     for copy in copies:
         copy.wait()
 
@@ -1326,6 +1339,21 @@
     )
     if outer > 1:
         part = lax.psum(part, "ctx", axis_index_groups=outer_groups)
+    *placed, place_token = kernel_call(
+        functools.partial(place_kernel, depth, hidden, feats),
+        [saved(v.shape, f32) for v in (w_qkv, w_out, w_fc1, w_fc2)] + [TOKEN],
+        pair,
+        swap_core(pair),
+        name="place",
+        limit=24,
+        scratch=[
+            pltpu.VMEM((depth, GROUP, width_own, hidden), f32),
+            pltpu.VMEM((depth, GROUP, hidden, width_own), f32),
+            pltpu.VMEM((depth - 1, GROUP, 3, width_own, feats), f32),
+            pltpu.VMEM((depth - 1, GROUP, feats, width_own), f32),
+            DMA((16 * depth,)),
+        ],
+    )
     mine, last_pair = kernel_call(
         functools.partial(vector_plane_kernel, depth),
         [((32, width_own), f32), ((2 * width_own, 4 * feats), bf16)],
@@ -1336,8 +1364,8 @@
         part,
         swap_x(part),
         name="vector_plane",
-    )
-    pieces = [last_pair, swap_core(last_pair), pair, swap_core(pair)]
+        after=(place_token,),
+    )
     grad_gains, grad_shifts, grad_fc1_bias, grad_qv_bias = kernel_call(
         functools.partial(vector_place_kernel, depth, head_dim),
         [
@@ -1361,19 +1389,20 @@
         )[0]
         for own, other in zip((upstream, outputs_own), others)
     )
-    placed = kernel_call(
-        functools.partial(place_kernel, depth, hidden, feats),
-        [saved(v.shape, f32) for v in (w_qkv, w_out, w_fc1, w_fc2)],
-        *pieces,
-        name="place",
-        limit=24,
+    placed[:2] = kernel_call(
+        functools.partial(place_last_kernel, feats),
+        [saved(v.shape, f32) for v in (w_qkv, w_out)],
+        last_pair,
+        swap_core(last_pair),
+        Far(placed[0]),
+        Far(placed[1]),
+        name="place_last",
         scratch=[
-            pltpu.VMEM((depth, GROUP, width_own, hidden), f32),
-            pltpu.VMEM((depth, GROUP, hidden, width_own), f32),
-            pltpu.VMEM((depth, GROUP, 3, width_own, feats), f32),
-            pltpu.VMEM((depth, GROUP, feats, width_own), f32),
-            DMA((16 * depth,)),
+            pltpu.VMEM((GROUP, 3, width_own, feats), f32),
+            pltpu.VMEM((GROUP, feats, width_own), f32),
+            DMA((2 * GROUP,)),
         ],
+        aliases={2: 0, 3: 1},
     )
     return (
         outputs,

time: 368 us -> 364 us (0.989)
  waiting for transfers between devices: 138 us -> 134 us
    ppermute x18, waiting for transfers between devices: 33.8 us -> 28.7 us  [swap_x(): return lax.ppermute(value, 'ctx', [(i, i ^ 2) for i in range(ctx)])]
    pallas_call x61 -> x62, Pallas kernels: 86.6 us -> 86.1 us  [kernel_call(): pl.pallas_call(run, out_shape=out_shape, in_specs=specs, out_specs=out_sp...]
  transfers between devices with their start and end apart: 108 -> 108, of which waited for: 52 -> 51; matrix products, arithmetic and copies ran while one was open for 0% -> 0% of each run, Pallas kernels for 18% -> 19%
where the time goes in v15:
time: 364 us; the launch traced here: 358 us
  waiting for transfers between devices  134 us (37%)
  starting transfers between devices  114 us (31%)
  Pallas kernels  86.1 us (24%)
  between operations  15.9 us (4%)
  local copies, waits for them, and re-layouts  8.52 us (2%)
    pallas_call x62, Pallas kernels, kernel_call(): pl.pallas_call(run, out_shape=out_shape, in_specs=specs, out_specs=out_sp...  86.1 us
    ppermute x43, starting transfers between devices, swap_core(): return lax.ppermute(value, 'ctx', [(i, i ^ 1) for i in range(ctx)])  55.7 us
    ppermute x16, waiting for transfers between devices, swap_xy(): return lax.ppermute(value, ('ctx', 'tp'), pairs)  37.7 us
    ppermute x18, waiting for transfers between devices, swap_x(): return lax.ppermute(value, 'ctx', [(i, i ^ 2) for i in range(ctx)])  28.7 us
    ppermute x6, waiting for transfers between devices, shift_z(): lax.ppermute(value, 'fsdp', [(i, (i + d) % fsdp) for i in range(fsdp)])  20.2 us
    all_gather x2, waiting for transfers between devices, per_device(): mlp_w.append(lax.all_gather(own, 'fsdp', axis=0, tiled=True))  18.5 us
    ppermute x16, starting transfers between devices, swap_xy(): return lax.ppermute(value, ('ctx', 'tp'), pairs)  17.4 us
    ppermute x18, waiting for transfers between devices, swap_y(): return lax.ppermute(value, 'tp', [(i, i ^ 1) for i in range(tp)])  14.8 us
  transfers between devices with their start and end apart: 108, of which 51 were waited for; matrix products, arithmetic and copies ran while one was open for 0% of the time, Pallas kernels for 19%

profile of v15, /device:TPU:9, one launch (start us, length us, event | category | flops | bytes accessed | tf_op | source)
XLA Modules:
  0.0 358.0 jit_solution(6831732970044305197)
XLA Ops:
  15.2 2.3 prep_upstream.1
  45.4 3.4 attn.5
  51.2 2.6 attn.4
  54.0 2.2 collective-permute-start.18
  56.7 3.6 %collective-permute-done.18.refs_1_ = bf16[80,1024]{1,0:T(8,128)(2,1)S(1)} collective-permute-done((bf16[80,1024]{1,0:T(8,128)(2,1)S(1)}, bf16[80,1024]{1,0:T(8,128)(2,1)S(1)}, u32[]{:S(2)}, u32[]{:S(2)}) %collective-permute-start.18) | collective-permute-done | bytes 163872 | tf_op jit(solution)/shard_map/ppermute | solution.py:839
  60.3 3.7 %collective-permute-done.19.refs_2_ = bf16[80,1024]{1,0:T(8,128)(2,1)S(1)} collective-permute-done((bf16[80,1024]{1,0:T(8,128)(2,1)S(1)}, bf16[80,1024]{1,0:T(8,128)(2,1)S(1)}, u32[]{:S(2)}, u32[]{:S(2)}) %collective-permute-start.19) | collective-permute-done | bytes 163872 | tf_op jit(solution)/shard_map/ppermute | solution.py:830
  72.6 2.4 collective-permute-start.26
  78.3 6.8 %all-gather.7.cloned.1.call-done.refs_4_ = bf16[1024,1024]{1,0:T(8,128)(2,1)} async-done(((bf16[256,1024]{1,0:T(8,128)(2,1)}), bf16[1024,1024]{1,0:T(8,128)(2,1)}) %all-gather.7.cloned.1.call-update) | async-done | bytes 2097168 | tf_op jit(solution)/shard_map/all_gather | solution.py:910
  94.1 3.6 collective-permute-done.29.refs_1_
  97.7 3.6 collective-permute-done.30.refs_2_
  110.0 2.3 collective-permute-start.37
  118.9 2.6 attn.7
  122.4 2.6 attn.6
  125.2 2.2 collective-permute-start.40
  127.9 4.2 %collective-permute-done.40.refs_1_ = bf16[80,1024]{1,0:T(8,128)(2,1)S(1)} collective-permute-done((bf16[80,1024]{1,0:T(8,128)(2,1)S(1)}, bf16[80,1024]{1,0:T(8,128)(2,1)S(1)}, u32[]{:S(2)}, u32[]{:S(2)}) %collective-permute-start.40) | collective-permute-done | bytes 163872 | tf_op jit(solution)/shard_map/ppermute | solution.py:839
  132.1 3.4 collective-permute-done.41.refs_2_
  143.9 2.3 collective-permute-start.48
  148.5 11.7 %all-gather.11.cloned.1.call-done.refs_4_ = bf16[1024,1024]{1,0:T(8,128)(2,1)} async-done(((bf16[256,1024]{1,0:T(8,128)(2,1)}), bf16[1024,1024]{1,0:T(8,128)(2,1)}) %all-gather.11.cloned.1.call-update) | async-done | bytes 2097168 | tf_op jit(solution)/shard_map/all_gather | solution.py:910
  160.2 3.6 %mlp.6 = (bf16[320,1024]{1,0:T(8,128)(2,1)S(1)}, bf16[320,1024]{1,0:T(8,128)(2,1)S(1)}, bf16[320,512]{1,0:T(8,128)(2,1)S(1)}, f32[2,320,256]{2,1,0:T(8,128)S(1)}...) custom-call(bf16[80,1024]{1,0:T(8,128)(2,1)S(1)} %collective-permute, ...), custom_call_target="tpu_custom_call" | custom-call | tf_op jit(solution)/shard_map/mlp/pallas_call | solution.py:87
  167.7 3.5 mlp_grad.2
  179.3 7.2 %collective-permute-done.52.refs_1_ = bf16[160,1024]{1,0:T(8,128)(2,1)S(1)} collective-permute-done((bf16[160,1024]{1,0:T(8,128)(2,1)S(1)}, bf16[160,1024]{1,0:T(8,128)(2,1)S(1)}, u32[]{:S(2)}, u32[]{:S(2)}) %collective-permute-start.52) | collective-permute-done | bytes 327712 | tf_op jit(solution)/shard_map/ppermute | solution.py:839
  186.6 7.1 %collective-permute-done.53.refs_2_ = bf16[160,1024]{1,0:T(8,128)(2,1)S(1)} collective-permute-done((bf16[160,1024]{1,0:T(8,128)(2,1)S(1)}, bf16[160,1024]{1,0:T(8,128)(2,1)S(1)}, u32[]{:S(2)}, u32[]{:S(2)}) %collective-permute-start.53) | collective-permute-done | bytes 327712 | tf_op jit(solution)/shard_map/ppermute | solution.py:830
  203.3 2.3 collective-permute-start.61
  208.0 2.5 attn_back.4
  210.5 2.5 attn_back.5
  215.9 2.2 collective-permute-start.64
  218.6 3.9 %collective-permute-done.64.refs_1_ = bf16[80,1024]{1,0:T(8,128)(2,1)S(1)} collective-permute-done((bf16[80,1024]{1,0:T(8,128)(2,1)S(1)}, bf16[80,1024]{1,0:T(8,128)(2,1)S(1)}, u32[]{:S(2)}, u32[]{:S(2)}) %collective-permute-start.64) | collective-permute-done | bytes 163872 | tf_op jit(solution)/shard_map/ppermute | solution.py:839
  222.5 3.6 collective-permute-done.65.refs_2_
  226.9 2.6 attn_grad.2
  236.7 2.3 collective-permute-start.72
  245.1 3.4 mlp_grad.3
  248.7 2.3 collective-permute-done.74.refs_1_
  251.2 2.2 collective-permute-start.75
  253.9 3.9 %collective-permute-done.75.refs_1_ = bf16[80,1024]{1,0:T(8,128)(2,1)S(1)} collective-permute-done((bf16[80,1024]{1,0:T(8,128)(2,1)S(1)}, bf16[80,1024]{1,0:T(8,128)(2,1)S(1)}, u32[]{:S(2)}, u32[]{:S(2)}) %collective-permute-start.75) | collective-permute-done | bytes 163872 | tf_op jit(solution)/shard_map/ppermute | solution.py:839
  257.8 3.6 collective-permute-done.76.refs_2_
  269.8 2.3 collective-permute-start.83
  274.4 2.5 attn_back.6
  276.9 2.5 attn_back.7
  282.3 2.2 collective-permute-start.86
  285.0 3.9 %collective-permute-done.86.refs_1_ = bf16[80,1024]{1,0:T(8,128)(2,1)S(1)} collective-permute-done((bf16[80,1024]{1,0:T(8,128)(2,1)S(1)}, bf16[80,1024]{1,0:T(8,128)(2,1)S(1)}, u32[]{:S(2)}, u32[]{:S(2)}) %collective-permute-start.86) | collective-permute-done | bytes 163872 | tf_op jit(solution)/shard_map/ppermute | solution.py:839
  288.9 3.7 %collective-permute-done.87.refs_2_ = bf16[80,1024]{1,0:T(8,128)(2,1)S(1)} collective-permute-done((bf16[80,1024]{1,0:T(8,128)(2,1)S(1)}, bf16[80,1024]{1,0:T(8,128)(2,1)S(1)}, u32[]{:S(2)}, u32[]{:S(2)}) %collective-permute-start.87) | collective-permute-done | bytes 163872 | tf_op jit(solution)/shard_map/ppermute | solution.py:830
  294.3 2.7 attn_grad.3
  297.0 2.9 reduce-scatter.8.cloned.1.call-done.refs_0_
  304.0 3.0 collective-permute-start.91
  310.7 2.4 collective-permute-start.93
  313.1 17.6 %collective-permute-done.92.refs_4_ = bf16[288,512]{1,0:T(8,128)(2,1)S(1)} collective-permute-done((bf16[288,512]{1,0:T(8,128)(2,1)S(1)}, bf16[288,512]{1,0:T(8,128)(2,1)S(1)}, u32[]{:S(2)}, u32[]{:S(2)}) %collective-permute-start.92) | collective-permute-done | bytes 294944 | tf_op jit(solution)/shard_map/ppermute | solution.py:842
  330.7 2.6 collective-permute-done.93.refs_5_
  340.5 4.3 %place.1 = (f32[2,3,256,512]{3,2,1,0:T(8,128)}, f32[2,512,256]{2,1,0:T(8,128)}, f32[2,256,2048]{2,1,0:T(8,128)}, f32[2,2048,256]{2,1,0:T(8,128)}, f32[8,128]{1,0:T(8,128)S(1)}) custom-call(bf16[2560,512]{1,0:T(8,128)(2,1)S(1)} %get-tuple-element.370.refs_0_, bf16[2560,512]{1,0:T(8,128)(2,1)S(1)} %collective-permute-done.98.refs_1_), custom_call_target="tpu_custom_call" | custom-call | tf_op jit(solution)/shard_map/place/pallas_call | solution.py:87
  (373 shorter events, 165.6 us)
Async XLA Ops:
  7.2 34.1 %all-gather.5.cloned.1.call-start = ((), (), s32[]{:S(2)}) async-start(), calls=%async_computation.3 | async-start | bytes 1310720 | tf_op jit(solution)/shard_map/all_gather | solution.py:908
  9.0 76.0 %all-gather.7.cloned.1.call-start = ((), (), s32[]{:S(2)}) async-start(), calls=%async_computation.4 | async-start | bytes 2621440 | tf_op jit(solution)/shard_map/all_gather | solution.py:910
  11.2 103.8 %all-gather.9.cloned.1.call-start = ((), (), s32[]{:S(2)}) async-start(), calls=%async_computation.5 | async-start | bytes 1310720 | tf_op jit(solution)/shard_map/all_gather | solution.py:908
  11.4 10.9 %collective-permute-start.2 = (bf16[17,256]{1,0:T(8,128)(2,1)S(1)}, bf16[17,256]{1,0:T(8,128)(2,1)S(1)}, u32[]{:S(2)}, u32[]{:S(2)}) collective-permute-start(bf16[17,256]{1,0:T(8,128)(2,1)S(1)} %fusion.1), channel_id=1, source_target_pairs={{0,8},{8,16},{16,24},{24,0},{1,9},{9,17},{17,25},{25,1},{2,10},{10... | collective-permute-start | bytes 26120 | tf_op jit(solution)/shard_map/ppermute | solution.py:842
  12.8 10.8 %collective-permute-start.1 = (bf16[17,256]{1,0:T(8,128)(2,1)S(1)}, bf16[17,256]{1,0:T(8,128)(2,1)S(1)}, u32[]{:S(2)}, u32[]{:S(2)}) collective-permute-start(bf16[17,256]{1,0:T(8,128)(2,1)S(1)} %fusion.1), channel_id=1, source_target_pairs={{0,16},{8,24},{16,0},{24,8},{1,17},{9,25},{17,1},{25,9},{2,18},{10... | collective-permute-start | bytes 26120 | tf_op jit(solution)/shard_map/ppermute | solution.py:842
  13.9 10.0 %collective-permute-start = (bf16[17,256]{1,0:T(8,128)(2,1)S(1)}, bf16[17,256]{1,0:T(8,128)(2,1)S(1)}, u32[]{:S(2)}, u32[]{:S(2)}) collective-permute-start(bf16[17,256]{1,0:T(8,128)(2,1)S(1)} %fusion.1), channel_id=1, source_target_pairs={{0,24},{8,0},{16,8},{24,16},{1,25},{9,1},{17,9},{25,17},{2,26},{10... | collective-permute-start | bytes 26120 | tf_op jit(solution)/shard_map/ppermute | solution.py:842
  17.6 9.2 %collective-permute-start.9 = (bf16[80,1024]{1,0:T(8,128)(2,1)S(1)}, bf16[80,1024]{1,0:T(8,128)(2,1)S(1)}, u32[]{:S(2)}, u32[]{:S(2)}) collective-permute-start(bf16[80,1024]{1,0:T(8,128)(2,1)S(1)} %get-tuple-element.201.refs_0_), channel_id=1, source_target_pairs={{0,2},{2,0},{4,6},{6,4},{1,3},{3,1},{5,7},{7,5},{8,10},{10,8},{12,... | collective-permute-start | bytes 491528 | tf_op jit(solution)/shard_map/ppermute | solution.py:827
  19.1 8.9 %collective-permute-start.8 = (bf16[80,1024]{1,0:T(8,128)(2,1)S(1)}, bf16[80,1024]{1,0:T(8,128)(2,1)S(1)}, u32[]{:S(2)}, u32[]{:S(2)}) collective-permute-start(bf16[80,1024]{1,0:T(8,128)(2,1)S(1)} %get-tuple-element.201.refs_0_), channel_id=1, source_target_pairs={{0,1},{1,0},{2,3},{3,2},{4,5},{5,4},{6,7},{7,6},{8,9},{9,8},{10,11... | collective-permute-start | bytes 491528 | tf_op jit(solution)/shard_map/ppermute | solution.py:833
  22.2 138.0 %all-gather.11.cloned.1.call-start = ((), (), s32[]{:S(2)}) async-start(), calls=%async_computation.6 | async-start | bytes 2621440 | tf_op jit(solution)/shard_map/all_gather | solution.py:910
  25.5 9.0 %collective-permute-start.5 = (bf16[80,1024]{1,0:T(8,128)(2,1)S(1)}, bf16[80,1024]{1,0:T(8,128)(2,1)S(1)}, u32[]{:S(2)}, u32[]{:S(2)}) collective-permute-start(bf16[80,1024]{1,0:T(8,128)(2,1)S(1)} %get-tuple-element.197.refs_0_), channel_id=1, source_target_pairs={{0,1},{1,0},{2,3},{3,2},{4,5},{5,4},{6,7},{7,6},{8,9},{9,8},{10,11... | collective-permute-start | bytes 491528 | tf_op jit(solution)/shard_map/ppermute | solution.py:833
  26.8 8.8 %collective-permute-start.4 = (bf16[80,1024]{1,0:T(8,128)(2,1)S(1)}, bf16[80,1024]{1,0:T(8,128)(2,1)S(1)}, u32[]{:S(2)}, u32[]{:S(2)}) collective-permute-start(bf16[80,1024]{1,0:T(8,128)(2,1)S(1)} %get-tuple-element.197.refs_0_), channel_id=1, source_target_pairs={{0,4},{2,6},{4,0},{6,2},{1,5},{3,7},{5,1},{7,3},{8,12},{10,14},{12... | collective-permute-start | bytes 491528 | tf_op jit(solution)/shard_map/ppermute | solution.py:830
  28.0 10.4 %collective-permute-start.3 = (bf16[80,1024]{1,0:T(8,128)(2,1)S(1)}, bf16[80,1024]{1,0:T(8,128)(2,1)S(1)}, u32[]{:S(2)}, u32[]{:S(2)}) collective-permute-start(bf16[80,1024]{1,0:T(8,128)(2,1)S(1)} %get-tuple-element.197.refs_0_), channel_id=1, source_target_pairs={{0,5},{1,4},{2,7},{3,6},{4,1},{5,0},{6,3},{7,2},{8,13},{9,12},{10,... | collective-permute-start | bytes 491528 | tf_op jit(solution)/shard_map/ppermute | solution.py:839
  28.2 11.3 %collective-permute-start.12 = (bf16[80,1024]{1,0:T(8,128)(2,1)S(1)}, bf16[80,1024]{1,0:T(8,128)(2,1)S(1)}, u32[]{:S(2)}, u32[]{:S(2)}) collective-permute-start(bf16[80,1024]{1,0:T(8,128)(2,1)S(1)} %collective-permute-done.8.refs_3_), channel_id=1, source_target_pairs={{0,2},{2,0},{4,6},{6,4},{1,3},{3,1},{5,7},{7,5},{8,10},{10,8},{12,... | collective-permute-start | bytes 491528 | tf_op jit(solution)/shard_map/ppermute | solution.py:827
  31.3 8.2 %collective-permute-start.11 = (bf16[80,1024]{1,0:T(8,128)(2,1)S(1)}, bf16[80,1024]{1,0:T(8,128)(2,1)S(1)}, u32[]{:S(2)}, u32[]{:S(2)}) collective-permute-start(bf16[80,1024]{1,0:T(8,128)(2,1)S(1)} %collective-permute-done.7.refs_2_), channel_id=1, source_target_pairs={{0,2},{2,0},{4,6},{6,4},{1,3},{3,1},{5,7},{7,5},{8,10},{10,8},{12,... | collective-permute-start | bytes 491528 | tf_op jit(solution)/shard_map/ppermute | solution.py:827
  34.5 8.6 %collective-permute-start.13 = (bf16[80,1024]{1,0:T(8,128)(2,1)S(1)}, bf16[80,1024]{1,0:T(8,128)(2,1)}, u32[]{:S(2)}, u32[]{:S(2)}) collective-permute-start(bf16[80,1024]{1,0:T(8,128)(2,1)S(1)} %get-tuple-element.197.refs_0_), channel_id=1, source_target_pairs={{0,2},{2,0},{4,6},{6,4},{1,3},{3,1},{5,7},{7,5},{8,10},{10,8},{12,... | collective-permute-start | bytes 491528 | tf_op jit(solution)/shard_map/ppermute | solution.py:827
  51.0 178.8 %reduce-scatter.4.cloned.1.call-start = ((), (), s32[]{:S(2)}) async-start(), calls=%async_computation.7 | async-start | bytes 2621440 | tf_op jit(solution)/shard_map/reduce_scatter | solution.py:1087
  56.5 8.2 %collective-permute-start.20 = (bf16[80,1024]{1,0:T(8,128)(2,1)S(1)}, bf16[80,1024]{1,0:T(8,128)(2,1)S(1)}, u32[]{:S(2)}, u32[]{:S(2)}) collective-permute-start(bf16[80,1024]{1,0:T(8,128)(2,1)S(1)} %get-tuple-element.214), channel_id=1, source_target_pairs={{0,1},{1,0},{2,3},{3,2},{4,5},{5,4},{6,7},{7,6},{8,9},{9,8},{10,11... | collective-permute-start | bytes 491528 | tf_op jit(solution)/shard_map/ppermute | solution.py:833
  68.6 8.7 %collective-permute-start.24 = (bf16[80,1024]{1,0:T(8,128)(2,1)S(1)}, bf16[80,1024]{1,0:T(8,128)(2,1)S(1)}, u32[]{:S(2)}, u32[]{:S(2)}) collective-permute-start(bf16[80,1024]{1,0:T(8,128)(2,1)S(1)} %get-tuple-element.216.refs_0_), channel_id=1, source_target_pairs={{0,2},{2,0},{4,6},{6,4},{1,3},{3,1},{5,7},{7,5},{8,10},{10,8},{12,... | collective-permute-start | bytes 491528 | tf_op jit(solution)/shard_map/ppermute | solution.py:827
  93.8 8.2 %collective-permute-start.31 = (bf16[80,1024]{1,0:T(8,128)(2,1)S(1)}, bf16[80,1024]{1,0:T(8,128)(2,1)S(1)}, u32[]{:S(2)}, u32[]{:S(2)}) collective-permute-start(bf16[80,1024]{1,0:T(8,128)(2,1)S(1)} %get-tuple-element.224), channel_id=1, source_target_pairs={{0,1},{1,0},{2,3},{3,2},{4,5},{5,4},{6,7},{7,6},{8,9},{9,8},{10,11... | collective-permute-start | bytes 491528 | tf_op jit(solution)/shard_map/ppermute | solution.py:833
  105.9 10.7 %collective-permute-start.35 = (bf16[80,1024]{1,0:T(8,128)(2,1)S(1)}, bf16[80,1024]{1,0:T(8,128)(2,1)S(1)}, u32[]{:S(2)}, u32[]{:S(2)}) collective-permute-start(bf16[80,1024]{1,0:T(8,128)(2,1)S(1)} %get-tuple-element.226.refs_0_), channel_id=1, source_target_pairs={{0,2},{2,0},{4,6},{6,4},{1,3},{3,1},{5,7},{7,5},{8,10},{10,8},{12,... | collective-permute-start | bytes 491528 | tf_op jit(solution)/shard_map/ppermute | solution.py:827
  127.4 8.2 %collective-permute-start.41 = (bf16[80,1024]{1,0:T(8,128)(2,1)S(1)}, bf16[80,1024]{1,0:T(8,128)(2,1)S(1)}, u32[]{:S(2)}, u32[]{:S(2)}) collective-permute-start(bf16[80,1024]{1,0:T(8,128)(2,1)S(1)} %get-tuple-element.237), channel_id=1, source_target_pairs={{0,4},{2,6},{4,0},{6,2},{1,5},{3,7},{5,1},{7,3},{8,12},{10,14},{12... | collective-permute-start | bytes 491528 | tf_op jit(solution)/shard_map/ppermute | solution.py:830
  127.7 8.3 %collective-permute-start.42 = (bf16[80,1024]{1,0:T(8,128)(2,1)S(1)}, bf16[80,1024]{1,0:T(8,128)(2,1)S(1)}, u32[]{:S(2)}, u32[]{:S(2)}) collective-permute-start(bf16[80,1024]{1,0:T(8,128)(2,1)S(1)} %get-tuple-element.238), channel_id=1, source_target_pairs={{0,1},{1,0},{2,3},{3,2},{4,5},{5,4},{6,7},{7,6},{8,9},{9,8},{10,11... | collective-permute-start | bytes 491528 | tf_op jit(solution)/shard_map/ppermute | solution.py:833
  139.9 20.3 %collective-permute-start.46 = (bf16[80,1024]{1,0:T(8,128)(2,1)S(1)}, bf16[80,1024]{1,0:T(8,128)(2,1)S(1)}, u32[]{:S(2)}, u32[]{:S(2)}) collective-permute-start(bf16[80,1024]{1,0:T(8,128)(2,1)S(1)} %get-tuple-element.240.refs_0_), channel_id=1, source_target_pairs={{0,2},{2,0},{4,6},{6,4},{1,3},{3,1},{5,7},{7,5},{8,10},{10,8},{12,... | collective-permute-start | bytes 491528 | tf_op jit(solution)/shard_map/ppermute | solution.py:827
  142.6 17.6 %collective-permute-start.49 = (bf16[80,1024]{1,0:T(8,128)(2,1)S(1)}, bf16[80,1024]{1,0:T(8,128)(2,1)S(1)}, u32[]{:S(2)}, u32[]{:S(2)}) collective-permute-start(bf16[80,1024]{1,0:T(8,128)(2,1)S(1)} %collective-permute-done.45.refs_3_), channel_id=1, source_target_pairs={{0,2},{2,0},{4,6},{6,4},{1,3},{3,1},{5,7},{7,5},{8,10},{10,8},{12,... | collective-permute-start | bytes 491528 | tf_op jit(solution)/shard_map/ppermute | solution.py:827
  143.9 16.4 %collective-permute-start.48 = (bf16[80,1024]{1,0:T(8,128)(2,1)S(1)}, bf16[80,1024]{1,0:T(8,128)(2,1)}, u32[]{:S(2)}, u32[]{:S(2)}) collective-permute-start(bf16[80,1024]{1,0:T(8,128)(2,1)S(1)} %collective-permute-done.44.refs_2_), channel_id=1, source_target_pairs={{0,2},{2,0},{4,6},{6,4},{1,3},{3,1},{5,7},{7,5},{8,10},{10,8},{12,... | collective-permute-start | bytes 491528 | tf_op jit(solution)/shard_map/ppermute | solution.py:827
  146.9 13.3 %collective-permute-start.47 = (bf16[80,1024]{1,0:T(8,128)(2,1)S(1)}, bf16[80,1024]{1,0:T(8,128)(2,1)}, u32[]{:S(2)}, u32[]{:S(2)}) collective-permute-start(bf16[80,1024]{1,0:T(8,128)(2,1)S(1)} %collective-permute-done.43.refs_1_), channel_id=1, source_target_pairs={{0,2},{2,0},{4,6},{6,4},{1,3},{3,1},{5,7},{7,5},{8,10},{10,8},{12,... | collective-permute-start | bytes 491528 | tf_op jit(solution)/shard_map/ppermute | solution.py:827
  171.3 90.9 %reduce-scatter.6.cloned.1.call-start = ((), (), s32[]{:S(2)}) async-start(), calls=%async_computation.8 | async-start | bytes 1310720 | tf_op jit(solution)/shard_map/reduce_scatter | solution.py:1087
  176.6 9.9 %collective-permute-start.52 = (bf16[160,1024]{1,0:T(8,128)(2,1)S(1)}, bf16[160,1024]{1,0:T(8,128)(2,1)S(1)}, u32[]{:S(2)}, u32[]{:S(2)}) collective-permute-start(bf16[160,1024]{1,0:T(8,128)(2,1)S(1)} %get-tuple-element.268), channel_id=1, source_target_pairs={{0,5},{1,4},{2,7},{3,6},{4,1},{5,0},{6,3},{7,2},{8,13},{9,12},{10,... | collective-permute-start | bytes 983048 | tf_op jit(solution)/shard_map/ppermute | solution.py:839
  178.8 14.9 %collective-permute-start.53 = (bf16[160,1024]{1,0:T(8,128)(2,1)S(1)}, bf16[160,1024]{1,0:T(8,128)(2,1)S(1)}, u32[]{:S(2)}, u32[]{:S(2)}) collective-permute-start(bf16[160,1024]{1,0:T(8,128)(2,1)S(1)} %get-tuple-element.269), channel_id=1, source_target_pairs={{0,4},{2,6},{4,0},{6,2},{1,5},{3,7},{5,1},{7,3},{8,12},{10,14},{12... | collective-permute-start | bytes 983048 | tf_op jit(solution)/shard_map/ppermute | solution.py:830
  179.1 15.3 %collective-permute-start.54 = (bf16[160,1024]{1,0:T(8,128)(2,1)S(1)}, bf16[160,1024]{1,0:T(8,128)(2,1)S(1)}, u32[]{:S(2)}, u32[]{:S(2)}) collective-permute-start(bf16[160,1024]{1,0:T(8,128)(2,1)S(1)} %get-tuple-element.270), channel_id=1, source_target_pairs={{0,1},{1,0},{2,3},{3,2},{4,5},{5,4},{6,7},{7,6},{8,9},{9,8},{10,11... | collective-permute-start | bytes 983048 | tf_op jit(solution)/shard_map/ppermute | solution.py:833
  199.3 11.1 %collective-permute-start.59 = (bf16[80,1024]{1,0:T(8,128)(2,1)S(1)}, bf16[80,1024]{1,0:T(8,128)(2,1)S(1)}, u32[]{:S(2)}, u32[]{:S(2)}) collective-permute-start(bf16[80,1024]{1,0:T(8,128)(2,1)S(1)} %get-tuple-element.289.refs_0_), channel_id=1, source_target_pairs={{0,2},{2,0},{4,6},{6,4},{1,3},{3,1},{5,7},{7,5},{8,10},{10,8},{12,... | collective-permute-start | bytes 491528 | tf_op jit(solution)/shard_map/ppermute | solution.py:827
  202.1 8.4 %collective-permute-start.62 = (bf16[80,1024]{1,0:T(8,128)(2,1)S(1)}, bf16[80,1024]{1,0:T(8,128)(2,1)S(1)}, u32[]{:S(2)}, u32[]{:S(2)}) collective-permute-start(bf16[80,1024]{1,0:T(8,128)(2,1)S(1)} %collective-permute-done.58.refs_3_), channel_id=1, source_target_pairs={{0,2},{2,0},{4,6},{6,4},{1,3},{3,1},{5,7},{7,5},{8,10},{10,8},{12,... | collective-permute-start | bytes 491528 | tf_op jit(solution)/shard_map/ppermute | solution.py:827
  218.3 8.2 %collective-permute-start.66 = (bf16[80,1024]{1,0:T(8,128)(2,1)S(1)}, bf16[80,1024]{1,0:T(8,128)(2,1)S(1)}, u32[]{:S(2)}, u32[]{:S(2)}) collective-permute-start(bf16[80,1024]{1,0:T(8,128)(2,1)S(1)} %get-tuple-element.305), channel_id=1, source_target_pairs={{0,1},{1,0},{2,3},{3,2},{4,5},{5,4},{6,7},{7,6},{8,9},{9,8},{10,11... | collective-permute-start | bytes 491528 | tf_op jit(solution)/shard_map/ppermute | solution.py:833
  229.6 70.4 %reduce-scatter.8.cloned.1.call-start = ((), (), s32[]{:S(2)}) async-start(), calls=%async_computation.9 | async-start | bytes 2621440 | tf_op jit(solution)/shard_map/reduce_scatter | solution.py:1087
  232.6 11.1 %collective-permute-start.70 = (bf16[80,1024]{1,0:T(8,128)(2,1)S(1)}, bf16[80,1024]{1,0:T(8,128)(2,1)S(1)}, u32[]{:S(2)}, u32[]{:S(2)}) collective-permute-start(bf16[80,1024]{1,0:T(8,128)(2,1)S(1)} %settle.2.refs_0_), channel_id=1, source_target_pairs={{0,2},{2,0},{4,6},{6,4},{1,3},{3,1},{5,7},{7,5},{8,10},{10,8},{12,... | collective-permute-start | bytes 491528 | tf_op jit(solution)/shard_map/ppermute | solution.py:827
  235.1 8.6 %collective-permute-start.73 = (bf16[80,1024]{1,0:T(8,128)(2,1)S(1)}, bf16[80,1024]{1,0:T(8,128)(2,1)S(1)}, u32[]{:S(2)}, u32[]{:S(2)}) collective-permute-start(bf16[80,1024]{1,0:T(8,128)(2,1)S(1)} %collective-permute-done.69.refs_3_), channel_id=1, source_target_pairs={{0,2},{2,0},{4,6},{6,4},{1,3},{3,1},{5,7},{7,5},{8,10},{10,8},{12,... | collective-permute-start | bytes 491528 | tf_op jit(solution)/shard_map/ppermute | solution.py:827
  253.6 8.2 %collective-permute-start.77 = (bf16[80,1024]{1,0:T(8,128)(2,1)S(1)}, bf16[80,1024]{1,0:T(8,128)(2,1)S(1)}, u32[]{:S(2)}, u32[]{:S(2)}) collective-permute-start(bf16[80,1024]{1,0:T(8,128)(2,1)S(1)} %get-tuple-element.326), channel_id=1, source_target_pairs={{0,1},{1,0},{2,3},{3,2},{4,5},{5,4},{6,7},{7,6},{8,9},{9,8},{10,11... | collective-permute-start | bytes 491528 | tf_op jit(solution)/shard_map/ppermute | solution.py:833
  265.7 11.2 %collective-permute-start.81 = (bf16[80,1024]{1,0:T(8,128)(2,1)S(1)}, bf16[80,1024]{1,0:T(8,128)(2,1)S(1)}, u32[]{:S(2)}, u32[]{:S(2)}) collective-permute-start(bf16[80,1024]{1,0:T(8,128)(2,1)S(1)} %get-tuple-element.332.refs_0_), channel_id=1, source_target_pairs={{0,2},{2,0},{4,6},{6,4},{1,3},{3,1},{5,7},{7,5},{8,10},{10,8},{12,... | collective-permute-start | bytes 491528 | tf_op jit(solution)/shard_map/ppermute | solution.py:827
  268.3 8.5 %collective-permute-start.84 = (bf16[80,1024]{1,0:T(8,128)(2,1)S(1)}, bf16[80,1024]{1,0:T(8,128)(2,1)S(1)}, u32[]{:S(2)}, u32[]{:S(2)}) collective-permute-start(bf16[80,1024]{1,0:T(8,128)(2,1)S(1)} %collective-permute-done.80.refs_3_), channel_id=1, source_target_pairs={{0,2},{2,0},{4,6},{6,4},{1,3},{3,1},{5,7},{7,5},{8,10},{10,8},{12,... | collective-permute-start | bytes 491528 | tf_op jit(solution)/shard_map/ppermute | solution.py:827
  284.7 8.3 %collective-permute-start.88 = (bf16[80,1024]{1,0:T(8,128)(2,1)S(1)}, bf16[80,1024]{1,0:T(8,128)(2,1)S(1)}, u32[]{:S(2)}, u32[]{:S(2)}) collective-permute-start(bf16[80,1024]{1,0:T(8,128)(2,1)S(1)} %get-tuple-element.348), channel_id=1, source_target_pairs={{0,1},{1,0},{2,3},{3,2},{4,5},{5,4},{6,7},{7,6},{8,9},{9,8},{10,11... | collective-permute-start | bytes 491528 | tf_op jit(solution)/shard_map/ppermute | solution.py:833
  301.3 32.1 %collective-permute-start.90 = (bf16[1280,512]{1,0:T(8,128)(2,1)S(1)}, bf16[1280,512]{1,0:T(8,128)(2,1)S(1)}, u32[]{:S(2)}, u32[]{:S(2)}) collective-permute-start(bf16[1280,512]{1,0:T(8,128)(2,1)S(1)} %fetch.1.refs_1_), channel_id=1, source_target_pairs={{0,4},{2,6},{4,0},{6,2},{1,5},{3,7},{5,1},{7,3},{8,12},{10,14},{12... | collective-permute-start | bytes 3932168 | tf_op jit(solution)/shard_map/ppermute | solution.py:830
  302.5 8.1 %collective-permute-start.55 = (f32[80,1024]{1,0:T(8,128)S(1)}, f32[80,1024]{1,0:T(8,128)S(1)}, u32[]{:S(2)}, u32[]{:S(2)}) collective-permute-start(f32[80,1024]{1,0:T(8,128)S(1)} %copy-done.31), channel_id=1, source_target_pairs={{0,1},{1,0},{2,3},{3,2},{4,5},{5,4},{6,7},{7,6},{8,9},{9,8},{10,11... | collective-permute-start | bytes 983048 | tf_op jit(solution)/shard_map/ppermute | solution.py:833
  303.7 29.6 %collective-permute-start.89 = (f32[80,1024]{1,0:T(8,128)S(1)}, f32[80,1024]{1,0:T(8,128)S(1)}, u32[]{:S(2)}, u32[]{:S(2)}) collective-permute-start(f32[80,1024]{1,0:T(8,128)S(1)} %copy-done.32), channel_id=1, source_target_pairs={{0,1},{1,0},{2,3},{3,2},{4,5},{5,4},{6,7},{7,6},{8,9},{9,8},{10,11... | collective-permute-start | bytes 983048 | tf_op jit(solution)/shard_map/ppermute | solution.py:833
  304.0 9.1 %collective-permute-start.91 = (bf16[288,512]{1,0:T(8,128)(2,1)S(1)}, bf16[288,512]{1,0:T(8,128)(2,1)S(1)}, u32[]{:S(2)}, u32[]{:S(2)}) collective-permute-start(bf16[288,512]{1,0:T(8,128)(2,1)S(1)} %copy-done.51), channel_id=1, source_target_pairs={{0,8},{8,16},{16,24},{24,0},{1,9},{9,17},{17,25},{25,1},{2,10},{10... | collective-permute-start | bytes 884744 | tf_op jit(solution)/shard_map/ppermute | solution.py:842
  307.0 23.8 %collective-permute-start.92 = (bf16[288,512]{1,0:T(8,128)(2,1)S(1)}, bf16[288,512]{1,0:T(8,128)(2,1)S(1)}, u32[]{:S(2)}, u32[]{:S(2)}) collective-permute-start(bf16[288,512]{1,0:T(8,128)(2,1)S(1)} %copy-done.50), channel_id=1, source_target_pairs={{0,16},{8,24},{16,0},{24,8},{1,17},{9,25},{17,1},{25,9},{2,18},{10... | collective-permute-start | bytes 884744 | tf_op jit(solution)/shard_map/ppermute | solution.py:842
  310.7 22.6 %collective-permute-start.93 = (bf16[288,512]{1,0:T(8,128)(2,1)S(1)}, bf16[288,512]{1,0:T(8,128)(2,1)S(1)}, u32[]{:S(2)}, u32[]{:S(2)}) collective-permute-start(bf16[288,512]{1,0:T(8,128)(2,1)S(1)} %copy-done.49), channel_id=1, source_target_pairs={{0,24},{8,0},{16,8},{24,16},{1,25},{9,1},{17,9},{25,17},{2,26},{10... | collective-permute-start | bytes 884744 | tf_op jit(solution)/shard_map/ppermute | solution.py:842
  335.9 9.5 %collective-permute-start.97 = (bf16[256,512]{1,0:T(8,128)(2,1)S(1)}, bf16[256,512]{1,0:T(8,128)(2,1)S(1)}, u32[]{:S(2)}, u32[]{:S(2)}) collective-permute-start(bf16[256,512]{1,0:T(8,128)(2,1)S(1)} %get-tuple-element.369.refs_4_), channel_id=1, source_target_pairs={{0,4},{2,6},{4,0},{6,2},{1,5},{3,7},{5,1},{7,3},{8,12},{10,14},{12... | collective-permute-start | bytes 786440 | tf_op jit(solution)/shard_map/ppermute | solution.py:830
  336.2 8.5 %collective-permute-start.96 = (f32[24,256]{1,0:T(8,128)S(1)}, f32[24,256]{1,0:T(8,128)S(1)}, u32[]{:S(2)}, u32[]{:S(2)}) collective-permute-start(f32[24,256]{1,0:T(8,128)S(1)} %get-tuple-element.368.refs_0_), channel_id=1, source_target_pairs={{0,1},{1,0},{2,3},{3,2},{4,5},{5,4},{6,7},{7,6},{8,9},{9,8},{10,11... | collective-permute-start | bytes 73736 | tf_op jit(solution)/shard_map/ppermute | solution.py:833
  (112 other events, 1082.0 us)
Sparse Core Ops, SparseCore 0:
  10.2 28.8 all-gather.4
  41.2 43.8 all-gather.6
  86.6 28.2 all-gather.8
  116.3 43.8 all-gather.10
  171.4 41.9 reduce-scatter.3
  229.7 25.1 reduce-scatter.5
  257.8 42.1 reduce-scatter.7

commit v16 on v15

--- a/solution.py
+++ b/solution.py
@@ -332,32 +332,35 @@
         copy.wait()
 
 
-def mlp_kernel(hidden, keep_count, saves, load_count, c0, c1, c2, c3, w, bias, *refs):
+def mlp_kernel(hidden, keep_count, saves, load_w, load_count, c0, c1, c2, c3, w, bias, *refs):
     kept, rest = refs[:keep_count], refs[keep_count:]
-    sources, rest = rest[: max(0, load_count - 1)], rest[max(0, load_count - 1) :]
+    sources, rest = rest[:load_count], rest[load_count:]
     partial_ref, x_out, act_out, slope_out, *rest = rest
     kept_hbm, rest = rest[:keep_count], rest[keep_count:]
+    targets, rest = rest[:load_count], rest[load_count:]
     loaded = []
-    if load_count:
-        w_ref, *targets = rest[:load_count]
-        *rest, load_sems, chunk_sems = rest[load_count:]
+    if load_w:
+        w_ref, *rest, w_sems, chunk_sems = rest
         rows = c0.shape[0]
         chunks = start_copies(
             [(c, x_out.at[pl.ds(k * rows, rows), :]) for k, c in enumerate((c0, c1, c2, c3))],
             chunk_sems,
         )
         spans = (pl.ds(0, hidden), pl.ds(hidden, hidden))
-        loaded = start_copies(
-            [(w.at[:, c], w_ref.at[:, c]) for c in spans] + list(zip(sources, targets)), load_sems
-        )
+        loaded = start_copies([(w.at[:, c], w_ref.at[:, c]) for c in spans], w_sems)
         w = w_ref
+    if load_count:
+        *rest, load_sems = rest
+        fetched = start_copies(list(zip(sources, targets)), load_sems)
+    else:
+        fetched = []
     if saves:
         x, act_ref, slope_ref, sems = rest
     else:
         x, act_ref, slope_ref = x_out, act_out, slope_out
         (sems,) = rest
     copies = start_copies(list(zip(kept, kept_hbm)), sems)
-    if load_count:
+    if load_w:
         for chunk in chunks:
             chunk.wait()
     else:
@@ -365,7 +368,7 @@
     if saves:
         copies += start_copies([(x, x_out)], sems.at[pl.ds(keep_count, 1)])
     block = hidden // 2
-    if load_count:
+    if load_w:
         loaded[0].wait()
     for k in range(2):
         span = slice(k * block, (k + 1) * block)
@@ -380,10 +383,10 @@
             )
     if saves:
         copies += start_copies([(act_ref, act_out)], sems.at[pl.ds(3 + keep_count, 1)])
-    if load_count:
+    if load_w:
         loaded[1].wait()
     partial_ref[...] = dot_nt(act_ref[...], w[:, hidden:]).astype(bf16)
-    for copy in copies + loaded[2:]:
+    for copy in copies + fetched:
         copy.wait()
 
 
@@ -1042,30 +1045,35 @@
         for side in (1, 0):
             kept = (middle,) if side == 1 else ()
             saves = l + 1 < depth
-            loads = (mlp_w[l], *upstream_rows) if not saves and side == 1 else ()
+            load_w = not saves and side == 1
+            loads = tuple(upstream_rows) if not saves and side == 0 else ()
             shapes = [
                 ((half, width), bf16),
                 ((half, hidden), bf16),
                 ((2, half, hidden // 2), f32),
             ]
             mlp[side] = kernel_call(
-                functools.partial(mlp_kernel, hidden, len(kept), saves, len(loads)),
+                functools.partial(mlp_kernel, hidden, len(kept), saves, load_w, len(loads)),
                 [partial_out]
                 + [saved(*shape) if saves else shape for shape in shapes]
                 + [saved(k.shape, k.dtype) for k in kept]
-                + [(v.shape, v.dtype) for v in loads],
-                *[Anywhere(c) if loads else c for c in second_chunks[side]],
-                Far(mlp_w[l]) if loads else mlp_w[l],
+                + [(v.shape, v.dtype) for v in loads]
+                + ([(mlp_w[l].shape, bf16)] if load_w else []),
+                *[Anywhere(c) if load_w else c for c in second_chunks[side]],
+                Far(mlp_w[l]) if load_w else mlp_w[l],
                 fc1_all[l],
                 *kept,
-                *[Far(v) for v in loads[1:]],
+                *[Far(v) for v in loads],
                 name="mlp",
                 scratch=[pltpu.VMEM(*shape) for shape in shapes if saves]
                 + [DMA((4 + len(kept),))]
-                + ([DMA((len(loads) + 1,)), DMA((CHIPS,))] if loads else []),
+                + ([DMA((2,)), DMA((CHIPS,))] if load_w else [])
+                + [DMA((len(loads),)) for _ in loads[:1]],
             )
+            if load_w:
+                *mlp[side], mlp_w[l] = mlp[side]
             if loads:
-                *mlp[side], mlp_w[l], near, far = mlp[side]
+                *mlp[side], near, far = mlp[side]
                 upstream_chunks = [(near,), (far,)]
         saved_all.append((attn, pairs if outer > 1 else None, mlp))
         if l + 1 < depth:
@@ -1135,21 +1143,9 @@
             ],
         )
         mlp_parts[l] = scatter_grads(mlp_grad)
-        sums, *output_sums = reduce_rows(*zip(kept[0::2], kept[1::2]))
+        (sums,) = reduce_rows(tuple(kept[:2]))
         if l + 1 == depth:
-            outputs_own, output_token = kernel_call(
-                functools.partial(sum_out_kernel, shift_row(l, 3)),
-                [saved((rows, width), f32), TOKEN],
-                *output_sums[0],
-                Far(mlp[1][4]),
-                vecs,
-                mask,
-                name="sum_out",
-                scratch=[pltpu.VMEM((rows, width), f32)] * 2 + [DMA((2,))],
-            )
-            after = (output_token,)
-        else:
-            after = ()
+            output_pair = tuple(kept[2:])
         unit_sums[l] = (back[0][2], back[1][2])
         grad_middle, middle_b, sums_two = kernel_call(
             functools.partial(norm_back_two_kernel, gain_row(l, 1)),
@@ -1159,7 +1155,6 @@
             upstream,
             vecs,
             name="norm_back_two",
-            after=after,
         )
         if l + 1 < depth:
             middle_b, sums_two, grad_middle = settle(
@@ -1226,7 +1221,10 @@
 
         far_part = project(1, ())
         near_part = project(0, ())
-        (sums,) = reduce_rows((near_part, far_part))
+        pairs_now = [(near_part, far_part)]
+        if l == 0:
+            pairs_now.append(output_pair)
+        sums, *output_sums = reduce_rows(*pairs_now)
         body = functools.partial(norm_back_one_kernel, gain_row(l, 0))
         if l > 0:
             masked = ()
@@ -1318,6 +1316,16 @@
         after=(upstream_b,),
         scratch=[DMA((blocks,))],
     )
+    outputs_own, _ = kernel_call(
+        functools.partial(sum_out_kernel, shift_row(depth - 1, 3)),
+        [saved((rows, width), f32), TOKEN],
+        *output_sums[0],
+        Far(saved_all[depth - 1][2][1][4]),
+        vecs,
+        mask,
+        name="sum_out",
+        scratch=[pltpu.VMEM((rows, width), f32)] * 2 + [DMA((2,))],
+    )
     own_term, *other_terms = attn_grads
     other_terms = [shift_z(term, d + 1) for d, term in enumerate(other_terms)]
     crossed = swap_x(stacked)

time: 364 us -> 360 us (0.989)
  waiting for transfers between devices: 134 us -> 125 us
  transfers between devices with their start and end apart: 108 -> 108, of which waited for: 51 -> 49; matrix products, arithmetic and copies ran while one was open for 0% -> 0% of each run, Pallas kernels for 19% -> 20%
where the time goes in v16:
time: 360 us; the launch traced here: 353 us
  waiting for transfers between devices  125 us (35%)
  starting transfers between devices  114 us (32%)
  Pallas kernels  88.5 us (25%)
  between operations  15.8 us (4%)
  local copies, waits for them, and re-layouts  9.45 us (3%)
    pallas_call x62, Pallas kernels, kernel_call(): pl.pallas_call(run, out_shape=out_shape, in_specs=specs, out_specs=out_sp...  88.5 us
    ppermute x43, starting transfers between devices, swap_core(): return lax.ppermute(value, 'ctx', [(i, i ^ 1) for i in range(ctx)])  56.4 us
    ppermute x16, waiting for transfers between devices, swap_xy(): return lax.ppermute(value, ('ctx', 'tp'), pairs)  37.5 us
    ppermute x18, waiting for transfers between devices, swap_x(): return lax.ppermute(value, 'ctx', [(i, i ^ 2) for i in range(ctx)])  28.6 us
    ppermute x6, waiting for transfers between devices, shift_z(): lax.ppermute(value, 'fsdp', [(i, (i + d) % fsdp) for i in range(fsdp)])  18.5 us
    all_gather x2, waiting for transfers between devices, per_device(): mlp_w.append(lax.all_gather(own, 'fsdp', axis=0, tiled=True))  17.6 us
    ppermute x16, starting transfers between devices, swap_xy(): return lax.ppermute(value, ('ctx', 'tp'), pairs)  17.3 us
    ppermute x18, starting transfers between devices, swap_y(): return lax.ppermute(value, 'tp', [(i, i ^ 1) for i in range(tp)])  14.8 us
  transfers between devices with their start and end apart: 108, of which 49 were waited for; matrix products, arithmetic and copies ran while one was open for 0% of the time, Pallas kernels for 20%

profile of v16, /device:TPU:9, one launch (start us, length us, event | category | flops | bytes accessed | tf_op | source)
XLA Modules:
  0.0 353.3 jit_solution(16391008294370202060)
XLA Ops:
  15.2 2.3 prep_upstream.1
  46.0 3.5 attn.5
  51.9 2.6 attn.4
  54.7 2.2 collective-permute-start.18
  57.4 3.6 %collective-permute-done.18.refs_1_ = bf16[80,1024]{1,0:T(8,128)(2,1)S(1)} collective-permute-done((bf16[80,1024]{1,0:T(8,128)(2,1)S(1)}, bf16[80,1024]{1,0:T(8,128)(2,1)S(1)}, u32[]{:S(2)}, u32[]{:S(2)}) %collective-permute-start.18) | collective-permute-done | bytes 163872 | tf_op jit(solution)/shard_map/ppermute | solution.py:842
  61.0 3.7 %collective-permute-done.19.refs_2_ = bf16[80,1024]{1,0:T(8,128)(2,1)S(1)} collective-permute-done((bf16[80,1024]{1,0:T(8,128)(2,1)S(1)}, bf16[80,1024]{1,0:T(8,128)(2,1)S(1)}, u32[]{:S(2)}, u32[]{:S(2)}) %collective-permute-start.19) | collective-permute-done | bytes 163872 | tf_op jit(solution)/shard_map/ppermute | solution.py:833
  73.2 2.4 collective-permute-start.26
  79.0 6.1 %all-gather.7.cloned.1.call-done.refs_4_ = bf16[1024,1024]{1,0:T(8,128)(2,1)} async-done(((bf16[256,1024]{1,0:T(8,128)(2,1)}), bf16[1024,1024]{1,0:T(8,128)(2,1)}) %all-gather.7.cloned.1.call-update) | async-done | bytes 2097168 | tf_op jit(solution)/shard_map/all_gather | solution.py:913
  91.4 2.2 collective-permute-start.29
  94.1 3.6 %collective-permute-done.29.refs_1_ = bf16[80,1024]{1,0:T(8,128)(2,1)S(1)} collective-permute-done((bf16[80,1024]{1,0:T(8,128)(2,1)S(1)}, bf16[80,1024]{1,0:T(8,128)(2,1)S(1)}, u32[]{:S(2)}, u32[]{:S(2)}) %collective-permute-start.29) | collective-permute-done | bytes 163872 | tf_op jit(solution)/shard_map/ppermute | solution.py:842
  97.7 3.6 %collective-permute-done.30.refs_2_ = bf16[80,1024]{1,0:T(8,128)(2,1)S(1)} collective-permute-done((bf16[80,1024]{1,0:T(8,128)(2,1)S(1)}, bf16[80,1024]{1,0:T(8,128)(2,1)S(1)}, u32[]{:S(2)}, u32[]{:S(2)}) %collective-permute-start.30) | collective-permute-done | bytes 163872 | tf_op jit(solution)/shard_map/ppermute | solution.py:833
  110.0 2.3 collective-permute-start.37
  119.0 2.6 attn.7
  122.6 2.6 attn.6
  125.4 2.2 collective-permute-start.40
  128.1 4.2 %collective-permute-done.40.refs_1_ = bf16[80,1024]{1,0:T(8,128)(2,1)S(1)} collective-permute-done((bf16[80,1024]{1,0:T(8,128)(2,1)S(1)}, bf16[80,1024]{1,0:T(8,128)(2,1)S(1)}, u32[]{:S(2)}, u32[]{:S(2)}) %collective-permute-start.40) | collective-permute-done | bytes 163872 | tf_op jit(solution)/shard_map/ppermute | solution.py:842
  132.3 3.4 collective-permute-done.41.refs_2_
  144.0 2.3 collective-permute-start.48
  148.7 11.6 %all-gather.11.cloned.1.call-done.refs_4_ = bf16[1024,1024]{1,0:T(8,128)(2,1)} async-done(((bf16[256,1024]{1,0:T(8,128)(2,1)}), bf16[1024,1024]{1,0:T(8,128)(2,1)}) %all-gather.11.cloned.1.call-update) | async-done | bytes 2097168 | tf_op jit(solution)/shard_map/all_gather | solution.py:913
  160.3 3.5 mlp.6
  168.1 3.5 mlp_grad.2
  178.6 3.7 %collective-permute-done.51.refs_1_ = bf16[80,1024]{1,0:T(8,128)(2,1)S(1)} collective-permute-done((bf16[80,1024]{1,0:T(8,128)(2,1)S(1)}, bf16[80,1024]{1,0:T(8,128)(2,1)S(1)}, u32[]{:S(2)}, u32[]{:S(2)}) %collective-permute-start.51) | collective-permute-done | bytes 163872 | tf_op jit(solution)/shard_map/ppermute | solution.py:842
  182.3 3.7 %collective-permute-done.52.refs_2_ = bf16[80,1024]{1,0:T(8,128)(2,1)S(1)} collective-permute-done((bf16[80,1024]{1,0:T(8,128)(2,1)S(1)}, bf16[80,1024]{1,0:T(8,128)(2,1)S(1)}, u32[]{:S(2)}, u32[]{:S(2)}) %collective-permute-start.52) | collective-permute-done | bytes 163872 | tf_op jit(solution)/shard_map/ppermute | solution.py:833
  193.8 2.3 collective-permute-start.59
  198.4 2.5 attn_back.4
  201.0 2.5 attn_back.5
  206.3 2.2 collective-permute-start.62
  209.0 3.9 %collective-permute-done.62.refs_1_ = bf16[80,1024]{1,0:T(8,128)(2,1)S(1)} collective-permute-done((bf16[80,1024]{1,0:T(8,128)(2,1)S(1)}, bf16[80,1024]{1,0:T(8,128)(2,1)S(1)}, u32[]{:S(2)}, u32[]{:S(2)}) %collective-permute-start.62) | collective-permute-done | bytes 163872 | tf_op jit(solution)/shard_map/ppermute | solution.py:842
  212.9 3.6 %collective-permute-done.63.refs_2_ = bf16[80,1024]{1,0:T(8,128)(2,1)S(1)} collective-permute-done((bf16[80,1024]{1,0:T(8,128)(2,1)S(1)}, bf16[80,1024]{1,0:T(8,128)(2,1)S(1)}, u32[]{:S(2)}, u32[]{:S(2)}) %collective-permute-start.63) | collective-permute-done | bytes 163872 | tf_op jit(solution)/shard_map/ppermute | solution.py:833
  217.3 2.7 attn_grad.2
  228.8 2.3 collective-permute-start.70
  237.2 3.4 mlp_grad.3
  240.8 2.3 collective-permute-done.72.refs_1_
  246.0 3.9 %collective-permute-done.73.refs_1_ = bf16[80,1024]{1,0:T(8,128)(2,1)S(1)} collective-permute-done((bf16[80,1024]{1,0:T(8,128)(2,1)S(1)}, bf16[80,1024]{1,0:T(8,128)(2,1)S(1)}, u32[]{:S(2)}, u32[]{:S(2)}) %collective-permute-start.73) | collective-permute-done | bytes 163872 | tf_op jit(solution)/shard_map/ppermute | solution.py:842
  249.9 3.6 %collective-permute-done.74.refs_2_ = bf16[80,1024]{1,0:T(8,128)(2,1)S(1)} collective-permute-done((bf16[80,1024]{1,0:T(8,128)(2,1)S(1)}, bf16[80,1024]{1,0:T(8,128)(2,1)S(1)}, u32[]{:S(2)}, u32[]{:S(2)}) %collective-permute-start.74) | collective-permute-done | bytes 163872 | tf_op jit(solution)/shard_map/ppermute | solution.py:833
  261.9 2.3 collective-permute-start.81
  266.5 2.5 attn_back.6
  269.0 2.5 attn_back.7
  274.7 2.2 collective-permute-start.85
  277.4 7.2 %collective-permute-done.85.refs_1_ = bf16[160,1024]{1,0:T(8,128)(2,1)S(1)} collective-permute-done((bf16[160,1024]{1,0:T(8,128)(2,1)S(1)}, bf16[160,1024]{1,0:T(8,128)(2,1)S(1)}, u32[]{:S(2)}, u32[]{:S(2)}) %collective-permute-start.85) | collective-permute-done | bytes 327712 | tf_op jit(solution)/shard_map/ppermute | solution.py:842
  284.6 7.0 %collective-permute-done.86.refs_2_ = bf16[160,1024]{1,0:T(8,128)(2,1)S(1)} collective-permute-done((bf16[160,1024]{1,0:T(8,128)(2,1)S(1)}, bf16[160,1024]{1,0:T(8,128)(2,1)S(1)}, u32[]{:S(2)}, u32[]{:S(2)}) %collective-permute-start.86) | collective-permute-done | bytes 327712 | tf_op jit(solution)/shard_map/ppermute | solution.py:833
  293.6 2.7 attn_grad.3
  301.7 2.4 sum_out.1
  304.4 2.5 collective-permute-start.92
  307.5 3.0 collective-permute-start.93
  310.4 15.5 %collective-permute-done.92.refs_4_ = bf16[288,512]{1,0:T(8,128)(2,1)S(1)} collective-permute-done((bf16[288,512]{1,0:T(8,128)(2,1)S(1)}, bf16[288,512]{1,0:T(8,128)(2,1)S(1)}, u32[]{:S(2)}, u32[]{:S(2)}) %collective-permute-start.92) | collective-permute-done | bytes 294944 | tf_op jit(solution)/shard_map/ppermute | solution.py:845
  326.0 2.5 collective-permute-done.93.refs_5_
  335.7 4.3 %place.1 = (f32[2,3,256,512]{3,2,1,0:T(8,128)}, f32[2,512,256]{2,1,0:T(8,128)}, f32[2,256,2048]{2,1,0:T(8,128)}, f32[2,2048,256]{2,1,0:T(8,128)}, f32[8,128]{1,0:T(8,128)S(1)}) custom-call(bf16[2560,512]{1,0:T(8,128)(2,1)S(1)} %get-tuple-element.368.refs_0_, bf16[2560,512]{1,0:T(8,128)(2,1)S(1)} %collective-permute-done.98.refs_1_), custom_call_target="tpu_custom_call" | custom-call | tf_op jit(solution)/shard_map/place/pallas_call | solution.py:87
  (373 shorter events, 164.7 us)
Async XLA Ops:
  7.2 34.2 %all-gather.5.cloned.1.call-start = ((), (), s32[]{:S(2)}) async-start(), calls=%async_computation.3 | async-start | bytes 1310720 | tf_op jit(solution)/shard_map/all_gather | solution.py:911
  9.0 76.0 %all-gather.7.cloned.1.call-start = ((), (), s32[]{:S(2)}) async-start(), calls=%async_computation.4 | async-start | bytes 2621440 | tf_op jit(solution)/shard_map/all_gather | solution.py:913
  11.2 103.8 %all-gather.9.cloned.1.call-start = ((), (), s32[]{:S(2)}) async-start(), calls=%async_computation.5 | async-start | bytes 1310720 | tf_op jit(solution)/shard_map/all_gather | solution.py:911
  11.4 10.9 %collective-permute-start.2 = (bf16[17,256]{1,0:T(8,128)(2,1)S(1)}, bf16[17,256]{1,0:T(8,128)(2,1)S(1)}, u32[]{:S(2)}, u32[]{:S(2)}) collective-permute-start(bf16[17,256]{1,0:T(8,128)(2,1)S(1)} %fusion.1), channel_id=1, source_target_pairs={{0,8},{8,16},{16,24},{24,0},{1,9},{9,17},{17,25},{25,1},{2,10},{10... | collective-permute-start | bytes 26120 | tf_op jit(solution)/shard_map/ppermute | solution.py:845
  12.8 10.8 %collective-permute-start.1 = (bf16[17,256]{1,0:T(8,128)(2,1)S(1)}, bf16[17,256]{1,0:T(8,128)(2,1)S(1)}, u32[]{:S(2)}, u32[]{:S(2)}) collective-permute-start(bf16[17,256]{1,0:T(8,128)(2,1)S(1)} %fusion.1), channel_id=1, source_target_pairs={{0,16},{8,24},{16,0},{24,8},{1,17},{9,25},{17,1},{25,9},{2,18},{10... | collective-permute-start | bytes 26120 | tf_op jit(solution)/shard_map/ppermute | solution.py:845
  13.9 9.9 %collective-permute-start = (bf16[17,256]{1,0:T(8,128)(2,1)S(1)}, bf16[17,256]{1,0:T(8,128)(2,1)S(1)}, u32[]{:S(2)}, u32[]{:S(2)}) collective-permute-start(bf16[17,256]{1,0:T(8,128)(2,1)S(1)} %fusion.1), channel_id=1, source_target_pairs={{0,24},{8,0},{16,8},{24,16},{1,25},{9,1},{17,9},{25,17},{2,26},{10... | collective-permute-start | bytes 26120 | tf_op jit(solution)/shard_map/ppermute | solution.py:845
  17.5 9.2 %collective-permute-start.9 = (bf16[80,1024]{1,0:T(8,128)(2,1)S(1)}, bf16[80,1024]{1,0:T(8,128)(2,1)S(1)}, u32[]{:S(2)}, u32[]{:S(2)}) collective-permute-start(bf16[80,1024]{1,0:T(8,128)(2,1)S(1)} %get-tuple-element.200.refs_0_), channel_id=1, source_target_pairs={{0,2},{2,0},{4,6},{6,4},{1,3},{3,1},{5,7},{7,5},{8,10},{10,8},{12,... | collective-permute-start | bytes 491528 | tf_op jit(solution)/shard_map/ppermute | solution.py:830
  19.1 8.9 %collective-permute-start.8 = (bf16[80,1024]{1,0:T(8,128)(2,1)S(1)}, bf16[80,1024]{1,0:T(8,128)(2,1)S(1)}, u32[]{:S(2)}, u32[]{:S(2)}) collective-permute-start(bf16[80,1024]{1,0:T(8,128)(2,1)S(1)} %get-tuple-element.200.refs_0_), channel_id=1, source_target_pairs={{0,1},{1,0},{2,3},{3,2},{4,5},{5,4},{6,7},{7,6},{8,9},{9,8},{10,11... | collective-permute-start | bytes 491528 | tf_op jit(solution)/shard_map/ppermute | solution.py:836
  22.2 138.1 %all-gather.11.cloned.1.call-start = ((), (), s32[]{:S(2)}) async-start(), calls=%async_computation.6 | async-start | bytes 2621440 | tf_op jit(solution)/shard_map/all_gather | solution.py:913
  25.5 9.0 %collective-permute-start.5 = (bf16[80,1024]{1,0:T(8,128)(2,1)S(1)}, bf16[80,1024]{1,0:T(8,128)(2,1)}, u32[]{:S(2)}, u32[]{:S(2)}) collective-permute-start(bf16[80,1024]{1,0:T(8,128)(2,1)S(1)} %get-tuple-element.196.refs_0_), channel_id=1, source_target_pairs={{0,1},{1,0},{2,3},{3,2},{4,5},{5,4},{6,7},{7,6},{8,9},{9,8},{10,11... | collective-permute-start | bytes 491528 | tf_op jit(solution)/shard_map/ppermute | solution.py:836
  26.8 8.9 %collective-permute-start.4 = (bf16[80,1024]{1,0:T(8,128)(2,1)S(1)}, bf16[80,1024]{1,0:T(8,128)(2,1)}, u32[]{:S(2)}, u32[]{:S(2)}) collective-permute-start(bf16[80,1024]{1,0:T(8,128)(2,1)S(1)} %get-tuple-element.196.refs_0_), channel_id=1, source_target_pairs={{0,4},{2,6},{4,0},{6,2},{1,5},{3,7},{5,1},{7,3},{8,12},{10,14},{12... | collective-permute-start | bytes 491528 | tf_op jit(solution)/shard_map/ppermute | solution.py:833
  28.0 10.5 %collective-permute-start.3 = (bf16[80,1024]{1,0:T(8,128)(2,1)S(1)}, bf16[80,1024]{1,0:T(8,128)(2,1)}, u32[]{:S(2)}, u32[]{:S(2)}) collective-permute-start(bf16[80,1024]{1,0:T(8,128)(2,1)S(1)} %get-tuple-element.196.refs_0_), channel_id=1, source_target_pairs={{0,5},{1,4},{2,7},{3,6},{4,1},{5,0},{6,3},{7,2},{8,13},{9,12},{10,... | collective-permute-start | bytes 491528 | tf_op jit(solution)/shard_map/ppermute | solution.py:842
  28.2 11.4 %collective-permute-start.12 = (bf16[80,1024]{1,0:T(8,128)(2,1)S(1)}, bf16[80,1024]{1,0:T(8,128)(2,1)S(1)}, u32[]{:S(2)}, u32[]{:S(2)}) collective-permute-start(bf16[80,1024]{1,0:T(8,128)(2,1)S(1)} %collective-permute-done.8.refs_3_), channel_id=1, source_target_pairs={{0,2},{2,0},{4,6},{6,4},{1,3},{3,1},{5,7},{7,5},{8,10},{10,8},{12,... | collective-permute-start | bytes 491528 | tf_op jit(solution)/shard_map/ppermute | solution.py:830
  31.3 8.3 %collective-permute-start.11 = (bf16[80,1024]{1,0:T(8,128)(2,1)S(1)}, bf16[80,1024]{1,0:T(8,128)(2,1)S(1)}, u32[]{:S(2)}, u32[]{:S(2)}) collective-permute-start(bf16[80,1024]{1,0:T(8,128)(2,1)S(1)} %collective-permute-done.7.refs_2_), channel_id=1, source_target_pairs={{0,2},{2,0},{4,6},{6,4},{1,3},{3,1},{5,7},{7,5},{8,10},{10,8},{12,... | collective-permute-start | bytes 491528 | tf_op jit(solution)/shard_map/ppermute | solution.py:830
  34.4 9.9 %collective-permute-start.13 = (bf16[80,1024]{1,0:T(8,128)(2,1)S(1)}, bf16[80,1024]{1,0:T(8,128)(2,1)}, u32[]{:S(2)}, u32[]{:S(2)}) collective-permute-start(bf16[80,1024]{1,0:T(8,128)(2,1)S(1)} %get-tuple-element.196.refs_0_), channel_id=1, source_target_pairs={{0,2},{2,0},{4,6},{6,4},{1,3},{3,1},{5,7},{7,5},{8,10},{10,8},{12,... | collective-permute-start | bytes 491528 | tf_op jit(solution)/shard_map/ppermute | solution.py:830
  51.7 169.3 %reduce-scatter.4.cloned.1.call-start = ((), (), s32[]{:S(2)}) async-start(), calls=%async_computation.7 | async-start | bytes 2621440 | tf_op jit(solution)/shard_map/reduce_scatter | solution.py:1095
  57.2 8.2 %collective-permute-start.20 = (bf16[80,1024]{1,0:T(8,128)(2,1)S(1)}, bf16[80,1024]{1,0:T(8,128)(2,1)S(1)}, u32[]{:S(2)}, u32[]{:S(2)}) collective-permute-start(bf16[80,1024]{1,0:T(8,128)(2,1)S(1)} %get-tuple-element.213), channel_id=1, source_target_pairs={{0,1},{1,0},{2,3},{3,2},{4,5},{5,4},{6,7},{7,6},{8,9},{9,8},{10,11... | collective-permute-start | bytes 491528 | tf_op jit(solution)/shard_map/ppermute | solution.py:836
  69.3 8.7 %collective-permute-start.24 = (bf16[80,1024]{1,0:T(8,128)(2,1)S(1)}, bf16[80,1024]{1,0:T(8,128)(2,1)S(1)}, u32[]{:S(2)}, u32[]{:S(2)}) collective-permute-start(bf16[80,1024]{1,0:T(8,128)(2,1)S(1)} %get-tuple-element.215.refs_0_), channel_id=1, source_target_pairs={{0,2},{2,0},{4,6},{6,4},{1,3},{3,1},{5,7},{7,5},{8,10},{10,8},{12,... | collective-permute-start | bytes 491528 | tf_op jit(solution)/shard_map/ppermute | solution.py:830
  93.8 8.2 %collective-permute-start.31 = (bf16[80,1024]{1,0:T(8,128)(2,1)S(1)}, bf16[80,1024]{1,0:T(8,128)(2,1)S(1)}, u32[]{:S(2)}, u32[]{:S(2)}) collective-permute-start(bf16[80,1024]{1,0:T(8,128)(2,1)S(1)} %get-tuple-element.227), channel_id=1, source_target_pairs={{0,1},{1,0},{2,3},{3,2},{4,5},{5,4},{6,7},{7,6},{8,9},{9,8},{10,11... | collective-permute-start | bytes 491528 | tf_op jit(solution)/shard_map/ppermute | solution.py:836
  105.9 10.8 %collective-permute-start.35 = (bf16[80,1024]{1,0:T(8,128)(2,1)S(1)}, bf16[80,1024]{1,0:T(8,128)(2,1)S(1)}, u32[]{:S(2)}, u32[]{:S(2)}) collective-permute-start(bf16[80,1024]{1,0:T(8,128)(2,1)S(1)} %get-tuple-element.229.refs_0_), channel_id=1, source_target_pairs={{0,2},{2,0},{4,6},{6,4},{1,3},{3,1},{5,7},{7,5},{8,10},{10,8},{12,... | collective-permute-start | bytes 491528 | tf_op jit(solution)/shard_map/ppermute | solution.py:830
  108.6 8.2 %collective-permute-start.38 = (bf16[80,1024]{1,0:T(8,128)(2,1)S(1)}, bf16[80,1024]{1,0:T(8,128)(2,1)}, u32[]{:S(2)}, u32[]{:S(2)}) collective-permute-start(bf16[80,1024]{1,0:T(8,128)(2,1)S(1)} %collective-permute-done.34.refs_3_), channel_id=1, source_target_pairs={{0,2},{2,0},{4,6},{6,4},{1,3},{3,1},{5,7},{7,5},{8,10},{10,8},{12,... | collective-permute-start | bytes 491528 | tf_op jit(solution)/shard_map/ppermute | solution.py:830
  127.6 8.2 %collective-permute-start.41 = (bf16[80,1024]{1,0:T(8,128)(2,1)S(1)}, bf16[80,1024]{1,0:T(8,128)(2,1)S(1)}, u32[]{:S(2)}, u32[]{:S(2)}) collective-permute-start(bf16[80,1024]{1,0:T(8,128)(2,1)S(1)} %get-tuple-element.244), channel_id=1, source_target_pairs={{0,4},{2,6},{4,0},{6,2},{1,5},{3,7},{5,1},{7,3},{8,12},{10,14},{12... | collective-permute-start | bytes 491528 | tf_op jit(solution)/shard_map/ppermute | solution.py:833
  127.8 8.3 %collective-permute-start.42 = (bf16[80,1024]{1,0:T(8,128)(2,1)S(1)}, bf16[80,1024]{1,0:T(8,128)(2,1)S(1)}, u32[]{:S(2)}, u32[]{:S(2)}) collective-permute-start(bf16[80,1024]{1,0:T(8,128)(2,1)S(1)} %get-tuple-element.245), channel_id=1, source_target_pairs={{0,1},{1,0},{2,3},{3,2},{4,5},{5,4},{6,7},{7,6},{8,9},{9,8},{10,11... | collective-permute-start | bytes 491528 | tf_op jit(solution)/shard_map/ppermute | solution.py:836
  140.0 20.2 %collective-permute-start.46 = (bf16[80,1024]{1,0:T(8,128)(2,1)S(1)}, bf16[80,1024]{1,0:T(8,128)(2,1)S(1)}, u32[]{:S(2)}, u32[]{:S(2)}) collective-permute-start(bf16[80,1024]{1,0:T(8,128)(2,1)S(1)} %get-tuple-element.247.refs_0_), channel_id=1, source_target_pairs={{0,2},{2,0},{4,6},{6,4},{1,3},{3,1},{5,7},{7,5},{8,10},{10,8},{12,... | collective-permute-start | bytes 491528 | tf_op jit(solution)/shard_map/ppermute | solution.py:830
  142.8 17.4 %collective-permute-start.49 = (bf16[80,1024]{1,0:T(8,128)(2,1)S(1)}, bf16[80,1024]{1,0:T(8,128)(2,1)}, u32[]{:S(2)}, u32[]{:S(2)}) collective-permute-start(bf16[80,1024]{1,0:T(8,128)(2,1)S(1)} %collective-permute-done.45.refs_3_), channel_id=1, source_target_pairs={{0,2},{2,0},{4,6},{6,4},{1,3},{3,1},{5,7},{7,5},{8,10},{10,8},{12,... | collective-permute-start | bytes 491528 | tf_op jit(solution)/shard_map/ppermute | solution.py:830
  144.0 16.3 %collective-permute-start.48 = (bf16[80,1024]{1,0:T(8,128)(2,1)S(1)}, bf16[80,1024]{1,0:T(8,128)(2,1)}, u32[]{:S(2)}, u32[]{:S(2)}) collective-permute-start(bf16[80,1024]{1,0:T(8,128)(2,1)S(1)} %collective-permute-done.44.refs_2_), channel_id=1, source_target_pairs={{0,2},{2,0},{4,6},{6,4},{1,3},{3,1},{5,7},{7,5},{8,10},{10,8},{12,... | collective-permute-start | bytes 491528 | tf_op jit(solution)/shard_map/ppermute | solution.py:830
  147.1 13.2 %collective-permute-start.47 = (bf16[80,1024]{1,0:T(8,128)(2,1)S(1)}, bf16[80,1024]{1,0:T(8,128)(2,1)}, u32[]{:S(2)}, u32[]{:S(2)}) collective-permute-start(bf16[80,1024]{1,0:T(8,128)(2,1)S(1)} %collective-permute-done.43.refs_1_), channel_id=1, source_target_pairs={{0,2},{2,0},{4,6},{6,4},{1,3},{3,1},{5,7},{7,5},{8,10},{10,8},{12,... | collective-permute-start | bytes 491528 | tf_op jit(solution)/shard_map/ppermute | solution.py:830
  171.7 82.6 %reduce-scatter.6.cloned.1.call-start = ((), (), s32[]{:S(2)}) async-start(), calls=%async_computation.8 | async-start | bytes 1310720 | tf_op jit(solution)/shard_map/reduce_scatter | solution.py:1095
  178.4 8.3 %collective-permute-start.53 = (bf16[80,1024]{1,0:T(8,128)(2,1)S(1)}, bf16[80,1024]{1,0:T(8,128)(2,1)S(1)}, u32[]{:S(2)}, u32[]{:S(2)}) collective-permute-start(bf16[80,1024]{1,0:T(8,128)(2,1)S(1)} %get-tuple-element.275), channel_id=1, source_target_pairs={{0,1},{1,0},{2,3},{3,2},{4,5},{5,4},{6,7},{7,6},{8,9},{9,8},{10,11... | collective-permute-start | bytes 491528 | tf_op jit(solution)/shard_map/ppermute | solution.py:836
  189.8 11.2 %collective-permute-start.57 = (bf16[80,1024]{1,0:T(8,128)(2,1)S(1)}, bf16[80,1024]{1,0:T(8,128)(2,1)S(1)}, u32[]{:S(2)}, u32[]{:S(2)}) collective-permute-start(bf16[80,1024]{1,0:T(8,128)(2,1)S(1)} %get-tuple-element.278.refs_0_), channel_id=1, source_target_pairs={{0,2},{2,0},{4,6},{6,4},{1,3},{3,1},{5,7},{7,5},{8,10},{10,8},{12,... | collective-permute-start | bytes 491528 | tf_op jit(solution)/shard_map/ppermute | solution.py:830
  192.5 8.4 %collective-permute-start.60 = (bf16[80,1024]{1,0:T(8,128)(2,1)S(1)}, bf16[80,1024]{1,0:T(8,128)(2,1)S(1)}, u32[]{:S(2)}, u32[]{:S(2)}) collective-permute-start(bf16[80,1024]{1,0:T(8,128)(2,1)S(1)} %collective-permute-done.56.refs_3_), channel_id=1, source_target_pairs={{0,2},{2,0},{4,6},{6,4},{1,3},{3,1},{5,7},{7,5},{8,10},{10,8},{12,... | collective-permute-start | bytes 491528 | tf_op jit(solution)/shard_map/ppermute | solution.py:830
  220.7 75.6 %reduce-scatter.8.cloned.1.call-start = ((), (), s32[]{:S(2)}) async-start(), calls=%async_computation.9 | async-start | bytes 2621440 | tf_op jit(solution)/shard_map/reduce_scatter | solution.py:1095
  224.7 11.2 %collective-permute-start.68 = (bf16[80,1024]{1,0:T(8,128)(2,1)S(1)}, bf16[80,1024]{1,0:T(8,128)(2,1)S(1)}, u32[]{:S(2)}, u32[]{:S(2)}) collective-permute-start(bf16[80,1024]{1,0:T(8,128)(2,1)S(1)} %settle.2.refs_0_), channel_id=1, source_target_pairs={{0,2},{2,0},{4,6},{6,4},{1,3},{3,1},{5,7},{7,5},{8,10},{10,8},{12,... | collective-permute-start | bytes 491528 | tf_op jit(solution)/shard_map/ppermute | solution.py:830
  227.2 8.6 %collective-permute-start.71 = (bf16[80,1024]{1,0:T(8,128)(2,1)S(1)}, bf16[80,1024]{1,0:T(8,128)(2,1)S(1)}, u32[]{:S(2)}, u32[]{:S(2)}) collective-permute-start(bf16[80,1024]{1,0:T(8,128)(2,1)S(1)} %collective-permute-done.67.refs_3_), channel_id=1, source_target_pairs={{0,2},{2,0},{4,6},{6,4},{1,3},{3,1},{5,7},{7,5},{8,10},{10,8},{12,... | collective-permute-start | bytes 491528 | tf_op jit(solution)/shard_map/ppermute | solution.py:830
  245.7 8.2 %collective-permute-start.75 = (bf16[80,1024]{1,0:T(8,128)(2,1)S(1)}, bf16[80,1024]{1,0:T(8,128)(2,1)S(1)}, u32[]{:S(2)}, u32[]{:S(2)}) collective-permute-start(bf16[80,1024]{1,0:T(8,128)(2,1)S(1)} %get-tuple-element.315), channel_id=1, source_target_pairs={{0,1},{1,0},{2,3},{3,2},{4,5},{5,4},{6,7},{7,6},{8,9},{9,8},{10,11... | collective-permute-start | bytes 491528 | tf_op jit(solution)/shard_map/ppermute | solution.py:836
  257.8 11.2 %collective-permute-start.79 = (bf16[80,1024]{1,0:T(8,128)(2,1)S(1)}, bf16[80,1024]{1,0:T(8,128)(2,1)S(1)}, u32[]{:S(2)}, u32[]{:S(2)}) collective-permute-start(bf16[80,1024]{1,0:T(8,128)(2,1)S(1)} %get-tuple-element.321.refs_0_), channel_id=1, source_target_pairs={{0,2},{2,0},{4,6},{6,4},{1,3},{3,1},{5,7},{7,5},{8,10},{10,8},{12,... | collective-permute-start | bytes 491528 | tf_op jit(solution)/shard_map/ppermute | solution.py:830
  260.4 8.5 %collective-permute-start.82 = (bf16[80,1024]{1,0:T(8,128)(2,1)S(1)}, bf16[80,1024]{1,0:T(8,128)(2,1)S(1)}, u32[]{:S(2)}, u32[]{:S(2)}) collective-permute-start(bf16[80,1024]{1,0:T(8,128)(2,1)S(1)} %collective-permute-done.78.refs_3_), channel_id=1, source_target_pairs={{0,2},{2,0},{4,6},{6,4},{1,3},{3,1},{5,7},{7,5},{8,10},{10,8},{12,... | collective-permute-start | bytes 491528 | tf_op jit(solution)/shard_map/ppermute | solution.py:830
  274.7 9.9 %collective-permute-start.85 = (bf16[160,1024]{1,0:T(8,128)(2,1)S(1)}, bf16[160,1024]{1,0:T(8,128)(2,1)S(1)}, u32[]{:S(2)}, u32[]{:S(2)}) collective-permute-start(bf16[160,1024]{1,0:T(8,128)(2,1)S(1)} %get-tuple-element.337), channel_id=1, source_target_pairs={{0,5},{1,4},{2,7},{3,6},{4,1},{5,0},{6,3},{7,2},{8,13},{9,12},{10,... | collective-permute-start | bytes 983048 | tf_op jit(solution)/shard_map/ppermute | solution.py:842
  276.8 14.8 %collective-permute-start.86 = (bf16[160,1024]{1,0:T(8,128)(2,1)S(1)}, bf16[160,1024]{1,0:T(8,128)(2,1)S(1)}, u32[]{:S(2)}, u32[]{:S(2)}) collective-permute-start(bf16[160,1024]{1,0:T(8,128)(2,1)S(1)} %get-tuple-element.338), channel_id=1, source_target_pairs={{0,4},{2,6},{4,0},{6,2},{1,5},{3,7},{5,1},{7,3},{8,12},{10,14},{12... | collective-permute-start | bytes 983048 | tf_op jit(solution)/shard_map/ppermute | solution.py:833
  277.1 15.2 %collective-permute-start.87 = (bf16[160,1024]{1,0:T(8,128)(2,1)S(1)}, bf16[160,1024]{1,0:T(8,128)(2,1)S(1)}, u32[]{:S(2)}, u32[]{:S(2)}) collective-permute-start(bf16[160,1024]{1,0:T(8,128)(2,1)S(1)} %get-tuple-element.339), channel_id=1, source_target_pairs={{0,1},{1,0},{2,3},{3,2},{4,5},{5,4},{6,7},{7,6},{8,9},{9,8},{10,11... | collective-permute-start | bytes 983048 | tf_op jit(solution)/shard_map/ppermute | solution.py:836
  297.8 30.7 %collective-permute-start.90 = (bf16[1280,512]{1,0:T(8,128)(2,1)S(1)}, bf16[1280,512]{1,0:T(8,128)(2,1)S(1)}, u32[]{:S(2)}, u32[]{:S(2)}) collective-permute-start(bf16[1280,512]{1,0:T(8,128)(2,1)S(1)} %fetch.1.refs_1_), channel_id=1, source_target_pairs={{0,4},{2,6},{4,0},{6,2},{1,5},{3,7},{5,1},{7,3},{8,12},{10,14},{12... | collective-permute-start | bytes 3932168 | tf_op jit(solution)/shard_map/ppermute | solution.py:833
  299.0 8.4 %collective-permute-start.91 = (bf16[288,512]{1,0:T(8,128)(2,1)S(1)}, bf16[288,512]{1,0:T(8,128)(2,1)S(1)}, u32[]{:S(2)}, u32[]{:S(2)}) collective-permute-start(bf16[288,512]{1,0:T(8,128)(2,1)S(1)} %copy-done.51), channel_id=1, source_target_pairs={{0,8},{8,16},{16,24},{24,0},{1,9},{9,17},{17,25},{25,1},{2,10},{10... | collective-permute-start | bytes 884744 | tf_op jit(solution)/shard_map/ppermute | solution.py:845
  300.5 28.0 %collective-permute-start.89 = (f32[80,1024]{1,0:T(8,128)S(1)}, f32[80,1024]{1,0:T(8,128)S(1)}, u32[]{:S(2)}, u32[]{:S(2)}) collective-permute-start(f32[80,1024]{1,0:T(8,128)S(1)} %copy-done.30), channel_id=1, source_target_pairs={{0,1},{1,0},{2,3},{3,2},{4,5},{5,4},{6,7},{7,6},{8,9},{9,8},{10,11... | collective-permute-start | bytes 983048 | tf_op jit(solution)/shard_map/ppermute | solution.py:836
  304.1 24.4 %collective-permute-start.88 = (f32[80,1024]{1,0:T(8,128)}, f32[80,1024]{1,0:T(8,128)S(1)}, u32[]{:S(2)}, u32[]{:S(2)}) collective-permute-start(f32[80,1024]{1,0:T(8,128)} %get-tuple-element.341.refs_0_), channel_id=1, source_target_pairs={{0,1},{1,0},{2,3},{3,2},{4,5},{5,4},{6,7},{7,6},{8,9},{9,8},{10,11... | collective-permute-start | bytes 983048 | tf_op jit(solution)/shard_map/ppermute | solution.py:836
  304.4 21.5 %collective-permute-start.92 = (bf16[288,512]{1,0:T(8,128)(2,1)S(1)}, bf16[288,512]{1,0:T(8,128)(2,1)S(1)}, u32[]{:S(2)}, u32[]{:S(2)}) collective-permute-start(bf16[288,512]{1,0:T(8,128)(2,1)S(1)} %copy-done.50), channel_id=1, source_target_pairs={{0,16},{8,24},{16,0},{24,8},{1,17},{9,25},{17,1},{25,9},{2,18},{10... | collective-permute-start | bytes 884744 | tf_op jit(solution)/shard_map/ppermute | solution.py:845
  307.5 21.0 %collective-permute-start.93 = (bf16[288,512]{1,0:T(8,128)(2,1)S(1)}, bf16[288,512]{1,0:T(8,128)(2,1)S(1)}, u32[]{:S(2)}, u32[]{:S(2)}) collective-permute-start(bf16[288,512]{1,0:T(8,128)(2,1)S(1)} %copy-done.49), channel_id=1, source_target_pairs={{0,24},{8,0},{16,8},{24,16},{1,25},{9,1},{17,9},{25,17},{2,26},{10... | collective-permute-start | bytes 884744 | tf_op jit(solution)/shard_map/ppermute | solution.py:845
  331.2 9.6 %collective-permute-start.97 = (bf16[256,512]{1,0:T(8,128)(2,1)S(1)}, bf16[256,512]{1,0:T(8,128)(2,1)S(1)}, u32[]{:S(2)}, u32[]{:S(2)}) collective-permute-start(bf16[256,512]{1,0:T(8,128)(2,1)S(1)} %get-tuple-element.367.refs_4_), channel_id=1, source_target_pairs={{0,4},{2,6},{4,0},{6,2},{1,5},{3,7},{5,1},{7,3},{8,12},{10,14},{12... | collective-permute-start | bytes 786440 | tf_op jit(solution)/shard_map/ppermute | solution.py:833
  331.5 8.6 %collective-permute-start.96 = (f32[24,256]{1,0:T(8,128)S(1)}, f32[24,256]{1,0:T(8,128)S(1)}, u32[]{:S(2)}, u32[]{:S(2)}) collective-permute-start(f32[24,256]{1,0:T(8,128)S(1)} %get-tuple-element.366.refs_0_), channel_id=1, source_target_pairs={{0,1},{1,0},{2,3},{3,2},{4,5},{5,4},{6,7},{7,6},{8,9},{9,8},{10,11... | collective-permute-start | bytes 73736 | tf_op jit(solution)/shard_map/ppermute | solution.py:836
  (112 other events, 880.0 us)
Sparse Core Ops, SparseCore 0:
  10.2 28.8 all-gather.4
  41.2 43.8 all-gather.6
  86.6 28.3 all-gather.8
  116.4 43.8 all-gather.10
  171.8 42.0 reduce-scatter.3
  220.9 25.2 reduce-scatter.5
  249.0 42.1 reduce-scatter.7

commit v17 on v16

--- a/solution.py
+++ b/solution.py
@@ -390,11 +390,17 @@
         copy.wait()
 
 
-def mlp_back_kernel(hidden, chunk_count, *refs):
+def mlp_back_kernel(hidden, chunk_count, fetches, *refs):
     chunks, (w, slope, *rest) = refs[:chunk_count], refs[chunk_count:]
+    if fetches:
+        *rest, slope_ref, slope_sem = rest
+        fetched = start_copies([(slope, slope_ref)], slope_sem)
+        slope = slope_ref
     partial_ref, grad_ref, sum_hbm, x, sum_ref, sems = rest
     assemble(chunks, x)
     grad = dot(x[...], w[:, hidden:])
+    if fetches:
+        fetched[0].wait()
     block = hidden // 2
     for k in range(2):
         span = slice(k * block, (k + 1) * block)
@@ -534,8 +540,9 @@
     kept_hbm, (packed, sums_ref, *staged, sems) = refs[:keep_count], refs[keep_count:]
     rows = up_near.shape[0]
     used = count + 2
-    sent = start_copies(list(zip(kept, kept_hbm)), sems.at[pl.ds(used, keep_count)])
-    passed_ref[...] = passed[...]
+    sent = start_copies(
+        [(passed, passed_ref), *zip(kept, kept_hbm)], sems.at[pl.ds(used, 1 + keep_count)]
+    )
     packed[:rows, :feats] = gq_near[...].astype(bf16)
     packed[rows:, :feats] = gq_far[...].astype(bf16)
     packed[:, feats : 2 * feats] = gk[...].astype(bf16)
@@ -583,9 +590,7 @@
 def settle_kernel(keep_count, after_count, passed, *refs):
     kept, refs = refs[:keep_count], refs[keep_count + after_count :]
     passed_ref, *kept_hbm, sems = refs
-    copies = start_copies(list(zip(kept, kept_hbm)), sems)
-    passed_ref[...] = passed[...]
-    for copy in copies:
+    for copy in start_copies([(passed, passed_ref), *zip(kept, kept_hbm)], sems):
         copy.wait()
 
 
@@ -663,7 +668,8 @@
         copy.wait()
 
 
-def place_last_kernel(feats, here, sibling, qkv_in, out_in, qkv_hbm, out_hbm, qkv, out, sems):
+def place_last_kernel(feats, vectors, here, sibling, qkv_in, out_in, mine, far, *refs):
+    qkv_hbm, out_hbm, *vector_refs, qkv, out, sems = refs
     ci = lax.rem(lax.axis_index("ctx"), GROUP)
     rows = here.shape[0] // 2
     copies = []
@@ -679,6 +685,7 @@
         copies += start_copies(
             [(out.at[k], out_hbm.at[0, span, :])], sems.at[pl.ds(2 * k + 1, 1)]
         )
+    vectors(mine, far, *vector_refs)
     for copy in copies:
         copy.wait()
 
@@ -788,17 +795,15 @@
                     heads_ref[l, j, c * heads + h : c * heads + h + 1, :] = value
 
 
-def place_rows_kernel(own, other, out_hbm, sems):
-    rows = own.shape[0]
+def place_rows_kernel(count, *refs):
+    terms, outs, sems = refs[: 2 * count], refs[2 * count : 3 * count], refs[-1]
+    rows = terms[0].shape[0]
     start = pl.multiple_of(lax.axis_index("tp") * rows, rows)
-    copies = start_copies(
-        [
-            (own, out_hbm.at[0, pl.ds(start, rows), :]),
-            (other, out_hbm.at[0, pl.ds(pl.multiple_of(rows - start, rows), rows), :]),
-        ],
-        sems,
-    )
-    for copy in copies:
+    places = (pl.ds(start, rows), pl.ds(pl.multiple_of(rows - start, rows), rows))
+    moves = [
+        (terms[2 * k + j], out.at[0, places[j], :]) for k, out in enumerate(outs) for j in range(2)
+    ]
+    for copy in start_copies(moves, sems):
         copy.wait()
 
 
@@ -851,14 +856,15 @@
         return near, tuple(swap_core(chunk) for chunk in near)
 
     def settle(value, there, *kept):
+        shape = value.value if isinstance(value, Far) else value
         return kernel_call(
             functools.partial(settle_kernel, len(kept), 1),
-            [(value.shape, value.dtype)] + [saved(k.shape, k.dtype) for k in kept],
+            [(shape.shape, shape.dtype)] + [saved(k.shape, k.dtype) for k in kept],
             value,
             *kept,
             Far(there),
             name="settle",
-            scratch=[DMA((max(1, len(kept)),))],
+            scratch=[DMA((1 + len(kept),))],
         )
 
     def reduce_rows(*pairs, after=()):
@@ -1106,8 +1112,9 @@
         attn, pairs, mlp = saved_all[l]
         back = [None, None]
         for side in (1, 0):
+            fetches = l + 1 < depth and side == 0
             back[side] = kernel_call(
-                functools.partial(mlp_back_kernel, hidden, len(upstream_chunks[side])),
+                functools.partial(mlp_back_kernel, hidden, len(upstream_chunks[side]), fetches),
                 [
                     partial_out,
                     ((half, hidden), bf16),
@@ -1116,9 +1123,10 @@
                 ],
                 *upstream_chunks[side],
                 mlp_w[l],
-                mlp[side][3],
+                Far(mlp[side][3]) if fetches else mlp[side][3],
                 name="mlp_back",
-                scratch=[pltpu.VMEM((1, hidden), f32), DMA((1,))],
+                scratch=[pltpu.VMEM((1, hidden), f32), DMA((1,))]
+                + ([pltpu.VMEM(mlp[side][3].shape, f32), DMA((1,))] if fetches else []),
             )
         kept = [back[0][0], back[1][0]]
         if l + 1 == depth:
@@ -1273,7 +1281,7 @@
             *kernel_call(
                 functools.partial(attn_grad_kernel, feats, count, len(kept)),
                 [saved((width if l > 0 else width_own + 32, 4 * feats), bf16)] * count
-                + [saved((2, feats), f32), row_bf16]
+                + [saved((2, feats), f32), saved(*row_bf16) if l > 0 else row_bf16]
                 + [saved(k.shape, k.dtype) for k in kept],
                 attn[0][3],
                 attn[1][3],
@@ -1292,7 +1300,7 @@
                     pltpu.VMEM((2, feats), f32),
                 ]
                 + [pltpu.VMEM(*shape) for shape in shapes]
-                + [DMA((count + 2 + len(kept),))],
+                + [DMA((count + 3 + len(kept),))],
             ),
             sums_two,
         ][: count + 5]
@@ -1300,7 +1308,7 @@
             sums_two = sums_kept
         if l > 0:
             attn_parts[l] = scatter_grads(attn_grads[0])
-            (upstream_b,) = settle(upstream_b, mlp_parts[l])
+            (upstream_b,) = settle(Far(upstream_b), mlp_parts[l])
             upstream_chunks = gather_rows(upstream_b)
         row_sums[l] = (sums_one, sums_two)
 
@@ -1374,36 +1382,25 @@
         name="vector_plane",
         after=(place_token,),
     )
-    grad_gains, grad_shifts, grad_fc1_bias, grad_qv_bias = kernel_call(
-        functools.partial(vector_place_kernel, depth, head_dim),
-        [
-            (norm_gains.shape, f32),
-            (shifts.shape, f32),
-            (fc1_bias.shape, f32),
-            (qv_bias.shape, f32),
-        ],
-        mine,
-        swap_core(mine),
-        name="vector_place",
-    )
-    grad_inputs, outputs = (
-        kernel_call(
-            place_rows_kernel,
-            [saved(inputs.shape, f32)],
-            own,
-            other,
-            name="place_rows",
-            scratch=[DMA((2,))],
-        )[0]
-        for own, other in zip((upstream, outputs_own), others)
-    )
-    placed[:2] = kernel_call(
-        functools.partial(place_last_kernel, feats),
-        [saved(v.shape, f32) for v in (w_qkv, w_out)],
+    grad_inputs, outputs = kernel_call(
+        functools.partial(place_rows_kernel, 2),
+        [saved(inputs.shape, f32)] * 2,
+        *(upstream, others[0], outputs_own, others[1]),
+        name="place_rows",
+        scratch=[DMA((4,))],
+    )
+    *placed[:2], grad_gains, grad_shifts, grad_fc1_bias, grad_qv_bias = kernel_call(
+        functools.partial(
+            place_last_kernel, feats, functools.partial(vector_place_kernel, depth, head_dim)
+        ),
+        [saved(v.shape, f32) for v in (w_qkv, w_out)]
+        + [(v.shape, f32) for v in (norm_gains, shifts, fc1_bias, qv_bias)],
         last_pair,
         swap_core(last_pair),
         Far(placed[0]),
         Far(placed[1]),
+        mine,
+        swap_core(mine),
         name="place_last",
         scratch=[
             pltpu.VMEM((GROUP, 3, width_own, feats), f32),

time: 360 us -> 359 us (level)
    unnamed x110 -> x104, local copies, waits for them, and re-layouts: 8.73 us -> 6.05 us
    pallas_call x62 -> x60, Pallas kernels: 88.5 us -> 90 us  [kernel_call(): pl.pallas_call(run, out_shape=out_shape, in_specs=specs, out_specs=out_sp...]
  transfers between devices with their start and end apart: 108 -> 108, of which waited for: 49 -> 50; matrix products, arithmetic and copies ran while one was open for 0% -> 0% of each run, Pallas kernels for 20% -> 21%
where the time goes in v17:
time: 359 us; the launch traced here: 352 us
  waiting for transfers between devices  125 us (35%)
  starting transfers between devices  115 us (32%)
  Pallas kernels  90 us (25%)
  between operations  15.8 us (4%)
  local copies, waits for them, and re-layouts  6.77 us (2%)
    pallas_call x60, Pallas kernels, kernel_call(): pl.pallas_call(run, out_shape=out_shape, in_specs=specs, out_specs=out_sp...  90 us
    ppermute x43, starting transfers between devices, swap_core(): return lax.ppermute(value, 'ctx', [(i, i ^ 1) for i in range(ctx)])  56.6 us
    ppermute x16, waiting for transfers between devices, swap_xy(): return lax.ppermute(value, ('ctx', 'tp'), pairs)  37.4 us
    ppermute x18, waiting for transfers between devices, swap_x(): return lax.ppermute(value, 'ctx', [(i, i ^ 2) for i in range(ctx)])  28.7 us
    ppermute x6, waiting for transfers between devices, shift_z(): lax.ppermute(value, 'fsdp', [(i, (i + d) % fsdp) for i in range(fsdp)])  18.6 us
    all_gather x2, waiting for transfers between devices, per_device(): mlp_w.append(lax.all_gather(own, 'fsdp', axis=0, tiled=True))  17.6 us
    ppermute x16, starting transfers between devices, swap_xy(): return lax.ppermute(value, ('ctx', 'tp'), pairs)  17.5 us
    ppermute x18, starting transfers between devices, swap_y(): return lax.ppermute(value, 'tp', [(i, i ^ 1) for i in range(tp)])  14.6 us
  transfers between devices with their start and end apart: 108, of which 50 were waited for; matrix products, arithmetic and copies ran while one was open for 0% of the time, Pallas kernels for 21%

profile of v17, /device:TPU:9, one launch (start us, length us, event | category | flops | bytes accessed | tf_op | source)
XLA Modules:
  0.0 352.4 jit_solution(6200513917391296526)
XLA Ops:
  15.2 2.3 prep_upstream.1
  46.0 3.5 attn.5
  51.9 2.6 attn.4
  54.7 2.2 collective-permute-start.18
  57.4 3.6 %collective-permute-done.18.refs_1_ = bf16[80,1024]{1,0:T(8,128)(2,1)S(1)} collective-permute-done((bf16[80,1024]{1,0:T(8,128)(2,1)S(1)}, bf16[80,1024]{1,0:T(8,128)(2,1)S(1)}, u32[]{:S(2)}, u32[]{:S(2)}) %collective-permute-start.18) | collective-permute-done | bytes 163872 | tf_op jit(solution)/shard_map/ppermute | solution.py:847
  61.0 3.7 %collective-permute-done.19.refs_2_ = bf16[80,1024]{1,0:T(8,128)(2,1)S(1)} collective-permute-done((bf16[80,1024]{1,0:T(8,128)(2,1)S(1)}, bf16[80,1024]{1,0:T(8,128)(2,1)S(1)}, u32[]{:S(2)}, u32[]{:S(2)}) %collective-permute-start.19) | collective-permute-done | bytes 163872 | tf_op jit(solution)/shard_map/ppermute | solution.py:838
  73.3 2.4 collective-permute-start.26
  79.0 6.0 %all-gather.7.cloned.1.call-done.refs_4_ = bf16[1024,1024]{1,0:T(8,128)(2,1)} async-done(((bf16[256,1024]{1,0:T(8,128)(2,1)}), bf16[1024,1024]{1,0:T(8,128)(2,1)}) %all-gather.7.cloned.1.call-update) | async-done | bytes 2097168 | tf_op jit(solution)/shard_map/all_gather | solution.py:919
  91.4 2.2 collective-permute-start.29
  94.1 3.6 %collective-permute-done.29.refs_1_ = bf16[80,1024]{1,0:T(8,128)(2,1)S(1)} collective-permute-done((bf16[80,1024]{1,0:T(8,128)(2,1)S(1)}, bf16[80,1024]{1,0:T(8,128)(2,1)S(1)}, u32[]{:S(2)}, u32[]{:S(2)}) %collective-permute-start.29) | collective-permute-done | bytes 163872 | tf_op jit(solution)/shard_map/ppermute | solution.py:847
  97.7 3.6 %collective-permute-done.30.refs_2_ = bf16[80,1024]{1,0:T(8,128)(2,1)S(1)} collective-permute-done((bf16[80,1024]{1,0:T(8,128)(2,1)S(1)}, bf16[80,1024]{1,0:T(8,128)(2,1)S(1)}, u32[]{:S(2)}, u32[]{:S(2)}) %collective-permute-start.30) | collective-permute-done | bytes 163872 | tf_op jit(solution)/shard_map/ppermute | solution.py:838
  110.1 2.3 collective-permute-start.37
  119.0 2.6 attn.7
  122.6 2.6 attn.6
  128.1 4.2 %collective-permute-done.40.refs_1_ = bf16[80,1024]{1,0:T(8,128)(2,1)S(1)} collective-permute-done((bf16[80,1024]{1,0:T(8,128)(2,1)S(1)}, bf16[80,1024]{1,0:T(8,128)(2,1)S(1)}, u32[]{:S(2)}, u32[]{:S(2)}) %collective-permute-start.40) | collective-permute-done | bytes 163872 | tf_op jit(solution)/shard_map/ppermute | solution.py:847
  132.3 3.4 collective-permute-done.41.refs_2_
  144.1 2.3 collective-permute-start.48
  148.7 11.6 %all-gather.11.cloned.1.call-done.refs_4_ = bf16[1024,1024]{1,0:T(8,128)(2,1)} async-done(((bf16[256,1024]{1,0:T(8,128)(2,1)}), bf16[1024,1024]{1,0:T(8,128)(2,1)}) %all-gather.11.cloned.1.call-update) | async-done | bytes 2097168 | tf_op jit(solution)/shard_map/all_gather | solution.py:919
  160.3 3.5 mlp.6
  168.2 3.5 mlp_grad.2
  178.6 3.7 %collective-permute-done.51.refs_1_ = bf16[80,1024]{1,0:T(8,128)(2,1)S(1)} collective-permute-done((bf16[80,1024]{1,0:T(8,128)(2,1)S(1)}, bf16[80,1024]{1,0:T(8,128)(2,1)S(1)}, u32[]{:S(2)}, u32[]{:S(2)}) %collective-permute-start.51) | collective-permute-done | bytes 163872 | tf_op jit(solution)/shard_map/ppermute | solution.py:847
  182.3 3.7 %collective-permute-done.52.refs_2_ = bf16[80,1024]{1,0:T(8,128)(2,1)S(1)} collective-permute-done((bf16[80,1024]{1,0:T(8,128)(2,1)S(1)}, bf16[80,1024]{1,0:T(8,128)(2,1)S(1)}, u32[]{:S(2)}, u32[]{:S(2)}) %collective-permute-start.52) | collective-permute-done | bytes 163872 | tf_op jit(solution)/shard_map/ppermute | solution.py:838
  193.8 2.3 collective-permute-start.59
  198.4 2.5 attn_back.4
  201.0 2.5 attn_back.5
  209.1 3.9 %collective-permute-done.62.refs_1_ = bf16[80,1024]{1,0:T(8,128)(2,1)S(1)} collective-permute-done((bf16[80,1024]{1,0:T(8,128)(2,1)S(1)}, bf16[80,1024]{1,0:T(8,128)(2,1)S(1)}, u32[]{:S(2)}, u32[]{:S(2)}) %collective-permute-start.62) | collective-permute-done | bytes 163872 | tf_op jit(solution)/shard_map/ppermute | solution.py:847
  213.0 3.6 %collective-permute-done.63.refs_2_ = bf16[80,1024]{1,0:T(8,128)(2,1)S(1)} collective-permute-done((bf16[80,1024]{1,0:T(8,128)(2,1)S(1)}, bf16[80,1024]{1,0:T(8,128)(2,1)S(1)}, u32[]{:S(2)}, u32[]{:S(2)}) %collective-permute-start.63) | collective-permute-done | bytes 163872 | tf_op jit(solution)/shard_map/ppermute | solution.py:838
  217.4 2.7 attn_grad.2
  228.2 2.3 collective-permute-start.70
  232.7 2.5 mlp_back.6
  236.7 3.4 mlp_grad.3
  240.3 2.3 collective-permute-done.72.refs_1_
  242.7 2.2 collective-permute-start.73
  245.4 3.9 %collective-permute-done.73.refs_1_ = bf16[80,1024]{1,0:T(8,128)(2,1)S(1)} collective-permute-done((bf16[80,1024]{1,0:T(8,128)(2,1)S(1)}, bf16[80,1024]{1,0:T(8,128)(2,1)S(1)}, u32[]{:S(2)}, u32[]{:S(2)}) %collective-permute-start.73) | collective-permute-done | bytes 163872 | tf_op jit(solution)/shard_map/ppermute | solution.py:847
  249.3 3.6 %collective-permute-done.74.refs_2_ = bf16[80,1024]{1,0:T(8,128)(2,1)S(1)} collective-permute-done((bf16[80,1024]{1,0:T(8,128)(2,1)S(1)}, bf16[80,1024]{1,0:T(8,128)(2,1)S(1)}, u32[]{:S(2)}, u32[]{:S(2)}) %collective-permute-start.74) | collective-permute-done | bytes 163872 | tf_op jit(solution)/shard_map/ppermute | solution.py:838
  261.6 2.3 collective-permute-start.81
  266.2 2.5 attn_back.6
  268.7 2.5 attn_back.7
  274.3 2.2 collective-permute-start.85
  277.1 7.2 %collective-permute-done.85.refs_1_ = bf16[160,1024]{1,0:T(8,128)(2,1)S(1)} collective-permute-done((bf16[160,1024]{1,0:T(8,128)(2,1)S(1)}, bf16[160,1024]{1,0:T(8,128)(2,1)S(1)}, u32[]{:S(2)}, u32[]{:S(2)}) %collective-permute-start.85) | collective-permute-done | bytes 327712 | tf_op jit(solution)/shard_map/ppermute | solution.py:847
  284.3 7.1 %collective-permute-done.86.refs_2_ = bf16[160,1024]{1,0:T(8,128)(2,1)S(1)} collective-permute-done((bf16[160,1024]{1,0:T(8,128)(2,1)S(1)}, bf16[160,1024]{1,0:T(8,128)(2,1)S(1)}, u32[]{:S(2)}, u32[]{:S(2)}) %collective-permute-start.86) | collective-permute-done | bytes 327712 | tf_op jit(solution)/shard_map/ppermute | solution.py:838
  293.3 2.7 attn_grad.3
  301.4 2.4 sum_out.1
  304.1 2.5 collective-permute-start.92
  307.2 3.0 collective-permute-start.93
  310.1 15.5 %collective-permute-done.92.refs_4_ = bf16[288,512]{1,0:T(8,128)(2,1)S(1)} collective-permute-done((bf16[288,512]{1,0:T(8,128)(2,1)S(1)}, bf16[288,512]{1,0:T(8,128)(2,1)S(1)}, u32[]{:S(2)}, u32[]{:S(2)}) %collective-permute-start.92) | collective-permute-done | bytes 294944 | tf_op jit(solution)/shard_map/ppermute | solution.py:850
  325.7 2.5 collective-permute-done.93.refs_5_
  335.4 4.3 %place.1 = (f32[2,3,256,512]{3,2,1,0:T(8,128)}, f32[2,512,256]{2,1,0:T(8,128)}, f32[2,256,2048]{2,1,0:T(8,128)}, f32[2,2048,256]{2,1,0:T(8,128)}, f32[8,128]{1,0:T(8,128)S(1)}) custom-call(bf16[2560,512]{1,0:T(8,128)(2,1)S(1)} %get-tuple-element.372.refs_0_, bf16[2560,512]{1,0:T(8,128)(2,1)S(1)} %collective-permute-done.98.refs_1_), custom_call_target="tpu_custom_call" | custom-call | tf_op jit(solution)/shard_map/place/pallas_call | solution.py:87
  (365 shorter events, 163.3 us)
Async XLA Ops:
  7.2 34.2 %all-gather.5.cloned.1.call-start = ((), (), s32[]{:S(2)}) async-start(), calls=%async_computation.3 | async-start | bytes 1310720 | tf_op jit(solution)/shard_map/all_gather | solution.py:917
  9.0 76.0 %all-gather.7.cloned.1.call-start = ((), (), s32[]{:S(2)}) async-start(), calls=%async_computation.4 | async-start | bytes 2621440 | tf_op jit(solution)/shard_map/all_gather | solution.py:919
  11.2 103.8 %all-gather.9.cloned.1.call-start = ((), (), s32[]{:S(2)}) async-start(), calls=%async_computation.5 | async-start | bytes 1310720 | tf_op jit(solution)/shard_map/all_gather | solution.py:917
  11.4 10.9 %collective-permute-start.2 = (bf16[17,256]{1,0:T(8,128)(2,1)S(1)}, bf16[17,256]{1,0:T(8,128)(2,1)S(1)}, u32[]{:S(2)}, u32[]{:S(2)}) collective-permute-start(bf16[17,256]{1,0:T(8,128)(2,1)S(1)} %fusion.1), channel_id=1, source_target_pairs={{0,8},{8,16},{16,24},{24,0},{1,9},{9,17},{17,25},{25,1},{2,10},{10... | collective-permute-start | bytes 26120 | tf_op jit(solution)/shard_map/ppermute | solution.py:850
  12.8 10.8 %collective-permute-start.1 = (bf16[17,256]{1,0:T(8,128)(2,1)S(1)}, bf16[17,256]{1,0:T(8,128)(2,1)S(1)}, u32[]{:S(2)}, u32[]{:S(2)}) collective-permute-start(bf16[17,256]{1,0:T(8,128)(2,1)S(1)} %fusion.1), channel_id=1, source_target_pairs={{0,16},{8,24},{16,0},{24,8},{1,17},{9,25},{17,1},{25,9},{2,18},{10... | collective-permute-start | bytes 26120 | tf_op jit(solution)/shard_map/ppermute | solution.py:850
  13.9 10.0 %collective-permute-start = (bf16[17,256]{1,0:T(8,128)(2,1)S(1)}, bf16[17,256]{1,0:T(8,128)(2,1)S(1)}, u32[]{:S(2)}, u32[]{:S(2)}) collective-permute-start(bf16[17,256]{1,0:T(8,128)(2,1)S(1)} %fusion.1), channel_id=1, source_target_pairs={{0,24},{8,0},{16,8},{24,16},{1,25},{9,1},{17,9},{25,17},{2,26},{10... | collective-permute-start | bytes 26120 | tf_op jit(solution)/shard_map/ppermute | solution.py:850
  17.5 9.3 %collective-permute-start.9 = (bf16[80,1024]{1,0:T(8,128)(2,1)S(1)}, bf16[80,1024]{1,0:T(8,128)(2,1)S(1)}, u32[]{:S(2)}, u32[]{:S(2)}) collective-permute-start(bf16[80,1024]{1,0:T(8,128)(2,1)S(1)} %get-tuple-element.202.refs_0_), channel_id=1, source_target_pairs={{0,2},{2,0},{4,6},{6,4},{1,3},{3,1},{5,7},{7,5},{8,10},{10,8},{12,... | collective-permute-start | bytes 491528 | tf_op jit(solution)/shard_map/ppermute | solution.py:835
  19.1 8.9 %collective-permute-start.8 = (bf16[80,1024]{1,0:T(8,128)(2,1)S(1)}, bf16[80,1024]{1,0:T(8,128)(2,1)S(1)}, u32[]{:S(2)}, u32[]{:S(2)}) collective-permute-start(bf16[80,1024]{1,0:T(8,128)(2,1)S(1)} %get-tuple-element.202.refs_0_), channel_id=1, source_target_pairs={{0,1},{1,0},{2,3},{3,2},{4,5},{5,4},{6,7},{7,6},{8,9},{9,8},{10,11... | collective-permute-start | bytes 491528 | tf_op jit(solution)/shard_map/ppermute | solution.py:841
  22.2 138.1 %all-gather.11.cloned.1.call-start = ((), (), s32[]{:S(2)}) async-start(), calls=%async_computation.6 | async-start | bytes 2621440 | tf_op jit(solution)/shard_map/all_gather | solution.py:919
  25.5 9.0 %collective-permute-start.5 = (bf16[80,1024]{1,0:T(8,128)(2,1)S(1)}, bf16[80,1024]{1,0:T(8,128)(2,1)}, u32[]{:S(2)}, u32[]{:S(2)}) collective-permute-start(bf16[80,1024]{1,0:T(8,128)(2,1)S(1)} %get-tuple-element.198.refs_0_), channel_id=1, source_target_pairs={{0,1},{1,0},{2,3},{3,2},{4,5},{5,4},{6,7},{7,6},{8,9},{9,8},{10,11... | collective-permute-start | bytes 491528 | tf_op jit(solution)/shard_map/ppermute | solution.py:841
  26.8 8.9 %collective-permute-start.4 = (bf16[80,1024]{1,0:T(8,128)(2,1)S(1)}, bf16[80,1024]{1,0:T(8,128)(2,1)}, u32[]{:S(2)}, u32[]{:S(2)}) collective-permute-start(bf16[80,1024]{1,0:T(8,128)(2,1)S(1)} %get-tuple-element.198.refs_0_), channel_id=1, source_target_pairs={{0,4},{2,6},{4,0},{6,2},{1,5},{3,7},{5,1},{7,3},{8,12},{10,14},{12... | collective-permute-start | bytes 491528 | tf_op jit(solution)/shard_map/ppermute | solution.py:838
  28.0 10.5 %collective-permute-start.3 = (bf16[80,1024]{1,0:T(8,128)(2,1)S(1)}, bf16[80,1024]{1,0:T(8,128)(2,1)}, u32[]{:S(2)}, u32[]{:S(2)}) collective-permute-start(bf16[80,1024]{1,0:T(8,128)(2,1)S(1)} %get-tuple-element.198.refs_0_), channel_id=1, source_target_pairs={{0,5},{1,4},{2,7},{3,6},{4,1},{5,0},{6,3},{7,2},{8,13},{9,12},{10,... | collective-permute-start | bytes 491528 | tf_op jit(solution)/shard_map/ppermute | solution.py:847
  28.2 11.4 %collective-permute-start.12 = (bf16[80,1024]{1,0:T(8,128)(2,1)S(1)}, bf16[80,1024]{1,0:T(8,128)(2,1)S(1)}, u32[]{:S(2)}, u32[]{:S(2)}) collective-permute-start(bf16[80,1024]{1,0:T(8,128)(2,1)S(1)} %collective-permute-done.8.refs_3_), channel_id=1, source_target_pairs={{0,2},{2,0},{4,6},{6,4},{1,3},{3,1},{5,7},{7,5},{8,10},{10,8},{12,... | collective-permute-start | bytes 491528 | tf_op jit(solution)/shard_map/ppermute | solution.py:835
  31.3 8.3 %collective-permute-start.11 = (bf16[80,1024]{1,0:T(8,128)(2,1)S(1)}, bf16[80,1024]{1,0:T(8,128)(2,1)S(1)}, u32[]{:S(2)}, u32[]{:S(2)}) collective-permute-start(bf16[80,1024]{1,0:T(8,128)(2,1)S(1)} %collective-permute-done.7.refs_2_), channel_id=1, source_target_pairs={{0,2},{2,0},{4,6},{6,4},{1,3},{3,1},{5,7},{7,5},{8,10},{10,8},{12,... | collective-permute-start | bytes 491528 | tf_op jit(solution)/shard_map/ppermute | solution.py:835
  34.5 9.9 %collective-permute-start.13 = (bf16[80,1024]{1,0:T(8,128)(2,1)S(1)}, bf16[80,1024]{1,0:T(8,128)(2,1)}, u32[]{:S(2)}, u32[]{:S(2)}) collective-permute-start(bf16[80,1024]{1,0:T(8,128)(2,1)S(1)} %get-tuple-element.198.refs_0_), channel_id=1, source_target_pairs={{0,2},{2,0},{4,6},{6,4},{1,3},{3,1},{5,7},{7,5},{8,10},{10,8},{12,... | collective-permute-start | bytes 491528 | tf_op jit(solution)/shard_map/ppermute | solution.py:835
  51.7 168.6 %reduce-scatter.4.cloned.1.call-start = ((), (), s32[]{:S(2)}) async-start(), calls=%async_computation.7 | async-start | bytes 2621440 | tf_op jit(solution)/shard_map/reduce_scatter | solution.py:1101
  57.2 8.1 %collective-permute-start.20 = (bf16[80,1024]{1,0:T(8,128)(2,1)S(1)}, bf16[80,1024]{1,0:T(8,128)(2,1)S(1)}, u32[]{:S(2)}, u32[]{:S(2)}) collective-permute-start(bf16[80,1024]{1,0:T(8,128)(2,1)S(1)} %get-tuple-element.219), channel_id=1, source_target_pairs={{0,1},{1,0},{2,3},{3,2},{4,5},{5,4},{6,7},{7,6},{8,9},{9,8},{10,11... | collective-permute-start | bytes 491528 | tf_op jit(solution)/shard_map/ppermute | solution.py:841
  69.3 8.7 %collective-permute-start.24 = (bf16[80,1024]{1,0:T(8,128)(2,1)S(1)}, bf16[80,1024]{1,0:T(8,128)(2,1)S(1)}, u32[]{:S(2)}, u32[]{:S(2)}) collective-permute-start(bf16[80,1024]{1,0:T(8,128)(2,1)S(1)} %get-tuple-element.221.refs_0_), channel_id=1, source_target_pairs={{0,2},{2,0},{4,6},{6,4},{1,3},{3,1},{5,7},{7,5},{8,10},{10,8},{12,... | collective-permute-start | bytes 491528 | tf_op jit(solution)/shard_map/ppermute | solution.py:835
  93.9 8.2 %collective-permute-start.31 = (bf16[80,1024]{1,0:T(8,128)(2,1)S(1)}, bf16[80,1024]{1,0:T(8,128)(2,1)S(1)}, u32[]{:S(2)}, u32[]{:S(2)}) collective-permute-start(bf16[80,1024]{1,0:T(8,128)(2,1)S(1)} %get-tuple-element.233), channel_id=1, source_target_pairs={{0,1},{1,0},{2,3},{3,2},{4,5},{5,4},{6,7},{7,6},{8,9},{9,8},{10,11... | collective-permute-start | bytes 491528 | tf_op jit(solution)/shard_map/ppermute | solution.py:841
  106.0 10.7 %collective-permute-start.35 = (bf16[80,1024]{1,0:T(8,128)(2,1)S(1)}, bf16[80,1024]{1,0:T(8,128)(2,1)S(1)}, u32[]{:S(2)}, u32[]{:S(2)}) collective-permute-start(bf16[80,1024]{1,0:T(8,128)(2,1)S(1)} %get-tuple-element.235.refs_0_), channel_id=1, source_target_pairs={{0,2},{2,0},{4,6},{6,4},{1,3},{3,1},{5,7},{7,5},{8,10},{10,8},{12,... | collective-permute-start | bytes 491528 | tf_op jit(solution)/shard_map/ppermute | solution.py:835
  127.6 8.2 %collective-permute-start.41 = (bf16[80,1024]{1,0:T(8,128)(2,1)S(1)}, bf16[80,1024]{1,0:T(8,128)(2,1)S(1)}, u32[]{:S(2)}, u32[]{:S(2)}) collective-permute-start(bf16[80,1024]{1,0:T(8,128)(2,1)S(1)} %get-tuple-element.250), channel_id=1, source_target_pairs={{0,4},{2,6},{4,0},{6,2},{1,5},{3,7},{5,1},{7,3},{8,12},{10,14},{12... | collective-permute-start | bytes 491528 | tf_op jit(solution)/shard_map/ppermute | solution.py:838
  127.9 8.3 %collective-permute-start.42 = (bf16[80,1024]{1,0:T(8,128)(2,1)S(1)}, bf16[80,1024]{1,0:T(8,128)(2,1)S(1)}, u32[]{:S(2)}, u32[]{:S(2)}) collective-permute-start(bf16[80,1024]{1,0:T(8,128)(2,1)S(1)} %get-tuple-element.251), channel_id=1, source_target_pairs={{0,1},{1,0},{2,3},{3,2},{4,5},{5,4},{6,7},{7,6},{8,9},{9,8},{10,11... | collective-permute-start | bytes 491528 | tf_op jit(solution)/shard_map/ppermute | solution.py:841
  140.1 20.2 %collective-permute-start.46 = (bf16[80,1024]{1,0:T(8,128)(2,1)S(1)}, bf16[80,1024]{1,0:T(8,128)(2,1)S(1)}, u32[]{:S(2)}, u32[]{:S(2)}) collective-permute-start(bf16[80,1024]{1,0:T(8,128)(2,1)S(1)} %get-tuple-element.253.refs_0_), channel_id=1, source_target_pairs={{0,2},{2,0},{4,6},{6,4},{1,3},{3,1},{5,7},{7,5},{8,10},{10,8},{12,... | collective-permute-start | bytes 491528 | tf_op jit(solution)/shard_map/ppermute | solution.py:835
  142.8 17.4 %collective-permute-start.49 = (bf16[80,1024]{1,0:T(8,128)(2,1)S(1)}, bf16[80,1024]{1,0:T(8,128)(2,1)}, u32[]{:S(2)}, u32[]{:S(2)}) collective-permute-start(bf16[80,1024]{1,0:T(8,128)(2,1)S(1)} %collective-permute-done.45.refs_3_), channel_id=1, source_target_pairs={{0,2},{2,0},{4,6},{6,4},{1,3},{3,1},{5,7},{7,5},{8,10},{10,8},{12,... | collective-permute-start | bytes 491528 | tf_op jit(solution)/shard_map/ppermute | solution.py:835
  144.1 16.2 %collective-permute-start.48 = (bf16[80,1024]{1,0:T(8,128)(2,1)S(1)}, bf16[80,1024]{1,0:T(8,128)(2,1)}, u32[]{:S(2)}, u32[]{:S(2)}) collective-permute-start(bf16[80,1024]{1,0:T(8,128)(2,1)S(1)} %collective-permute-done.44.refs_2_), channel_id=1, source_target_pairs={{0,2},{2,0},{4,6},{6,4},{1,3},{3,1},{5,7},{7,5},{8,10},{10,8},{12,... | collective-permute-start | bytes 491528 | tf_op jit(solution)/shard_map/ppermute | solution.py:835
  147.1 13.2 %collective-permute-start.47 = (bf16[80,1024]{1,0:T(8,128)(2,1)S(1)}, bf16[80,1024]{1,0:T(8,128)(2,1)}, u32[]{:S(2)}, u32[]{:S(2)}) collective-permute-start(bf16[80,1024]{1,0:T(8,128)(2,1)S(1)} %collective-permute-done.43.refs_1_), channel_id=1, source_target_pairs={{0,2},{2,0},{4,6},{6,4},{1,3},{3,1},{5,7},{7,5},{8,10},{10,8},{12,... | collective-permute-start | bytes 491528 | tf_op jit(solution)/shard_map/ppermute | solution.py:835
  171.7 82.1 %reduce-scatter.6.cloned.1.call-start = ((), (), s32[]{:S(2)}) async-start(), calls=%async_computation.8 | async-start | bytes 1310720 | tf_op jit(solution)/shard_map/reduce_scatter | solution.py:1101
  178.4 8.2 %collective-permute-start.53 = (bf16[80,1024]{1,0:T(8,128)(2,1)S(1)}, bf16[80,1024]{1,0:T(8,128)(2,1)S(1)}, u32[]{:S(2)}, u32[]{:S(2)}) collective-permute-start(bf16[80,1024]{1,0:T(8,128)(2,1)S(1)} %get-tuple-element.281), channel_id=1, source_target_pairs={{0,1},{1,0},{2,3},{3,2},{4,5},{5,4},{6,7},{7,6},{8,9},{9,8},{10,11... | collective-permute-start | bytes 491528 | tf_op jit(solution)/shard_map/ppermute | solution.py:841
  189.8 11.2 %collective-permute-start.57 = (bf16[80,1024]{1,0:T(8,128)(2,1)S(1)}, bf16[80,1024]{1,0:T(8,128)(2,1)S(1)}, u32[]{:S(2)}, u32[]{:S(2)}) collective-permute-start(bf16[80,1024]{1,0:T(8,128)(2,1)S(1)} %get-tuple-element.284.refs_0_), channel_id=1, source_target_pairs={{0,2},{2,0},{4,6},{6,4},{1,3},{3,1},{5,7},{7,5},{8,10},{10,8},{12,... | collective-permute-start | bytes 491528 | tf_op jit(solution)/shard_map/ppermute | solution.py:835
  192.5 8.4 %collective-permute-start.60 = (bf16[80,1024]{1,0:T(8,128)(2,1)S(1)}, bf16[80,1024]{1,0:T(8,128)(2,1)S(1)}, u32[]{:S(2)}, u32[]{:S(2)}) collective-permute-start(bf16[80,1024]{1,0:T(8,128)(2,1)S(1)} %collective-permute-done.56.refs_3_), channel_id=1, source_target_pairs={{0,2},{2,0},{4,6},{6,4},{1,3},{3,1},{5,7},{7,5},{8,10},{10,8},{12,... | collective-permute-start | bytes 491528 | tf_op jit(solution)/shard_map/ppermute | solution.py:835
  208.8 8.1 %collective-permute-start.64 = (bf16[80,1024]{1,0:T(8,128)(2,1)S(1)}, bf16[80,1024]{1,0:T(8,128)(2,1)S(1)}, u32[]{:S(2)}, u32[]{:S(2)}) collective-permute-start(bf16[80,1024]{1,0:T(8,128)(2,1)S(1)} %get-tuple-element.300), channel_id=1, source_target_pairs={{0,1},{1,0},{2,3},{3,2},{4,5},{5,4},{6,7},{7,6},{8,9},{9,8},{10,11... | collective-permute-start | bytes 491528 | tf_op jit(solution)/shard_map/ppermute | solution.py:841
  220.1 75.9 %reduce-scatter.8.cloned.1.call-start = ((), (), s32[]{:S(2)}) async-start(), calls=%async_computation.9 | async-start | bytes 2621440 | tf_op jit(solution)/shard_map/reduce_scatter | solution.py:1101
  224.1 11.2 %collective-permute-start.68 = (bf16[80,1024]{1,0:T(8,128)(2,1)S(1)}, bf16[80,1024]{1,0:T(8,128)(2,1)S(1)}, u32[]{:S(2)}, u32[]{:S(2)}) collective-permute-start(bf16[80,1024]{1,0:T(8,128)(2,1)S(1)} %settle.2.refs_0_), channel_id=1, source_target_pairs={{0,2},{2,0},{4,6},{6,4},{1,3},{3,1},{5,7},{7,5},{8,10},{10,8},{12,... | collective-permute-start | bytes 491528 | tf_op jit(solution)/shard_map/ppermute | solution.py:835
  226.6 8.7 %collective-permute-start.71 = (bf16[80,1024]{1,0:T(8,128)(2,1)S(1)}, bf16[80,1024]{1,0:T(8,128)(2,1)S(1)}, u32[]{:S(2)}, u32[]{:S(2)}) collective-permute-start(bf16[80,1024]{1,0:T(8,128)(2,1)S(1)} %collective-permute-done.67.refs_3_), channel_id=1, source_target_pairs={{0,2},{2,0},{4,6},{6,4},{1,3},{3,1},{5,7},{7,5},{8,10},{10,8},{12,... | collective-permute-start | bytes 491528 | tf_op jit(solution)/shard_map/ppermute | solution.py:835
  245.2 8.1 %collective-permute-start.75 = (bf16[80,1024]{1,0:T(8,128)(2,1)S(1)}, bf16[80,1024]{1,0:T(8,128)(2,1)S(1)}, u32[]{:S(2)}, u32[]{:S(2)}) collective-permute-start(bf16[80,1024]{1,0:T(8,128)(2,1)S(1)} %get-tuple-element.321), channel_id=1, source_target_pairs={{0,1},{1,0},{2,3},{3,2},{4,5},{5,4},{6,7},{7,6},{8,9},{9,8},{10,11... | collective-permute-start | bytes 491528 | tf_op jit(solution)/shard_map/ppermute | solution.py:841
  257.5 11.2 %collective-permute-start.79 = (bf16[80,1024]{1,0:T(8,128)(2,1)S(1)}, bf16[80,1024]{1,0:T(8,128)(2,1)S(1)}, u32[]{:S(2)}, u32[]{:S(2)}) collective-permute-start(bf16[80,1024]{1,0:T(8,128)(2,1)S(1)} %get-tuple-element.327.refs_0_), channel_id=1, source_target_pairs={{0,2},{2,0},{4,6},{6,4},{1,3},{3,1},{5,7},{7,5},{8,10},{10,8},{12,... | collective-permute-start | bytes 491528 | tf_op jit(solution)/shard_map/ppermute | solution.py:835
  260.1 8.6 %collective-permute-start.82 = (bf16[80,1024]{1,0:T(8,128)(2,1)S(1)}, bf16[80,1024]{1,0:T(8,128)(2,1)S(1)}, u32[]{:S(2)}, u32[]{:S(2)}) collective-permute-start(bf16[80,1024]{1,0:T(8,128)(2,1)S(1)} %collective-permute-done.78.refs_3_), channel_id=1, source_target_pairs={{0,2},{2,0},{4,6},{6,4},{1,3},{3,1},{5,7},{7,5},{8,10},{10,8},{12,... | collective-permute-start | bytes 491528 | tf_op jit(solution)/shard_map/ppermute | solution.py:835
  274.3 9.9 %collective-permute-start.85 = (bf16[160,1024]{1,0:T(8,128)(2,1)S(1)}, bf16[160,1024]{1,0:T(8,128)(2,1)S(1)}, u32[]{:S(2)}, u32[]{:S(2)}) collective-permute-start(bf16[160,1024]{1,0:T(8,128)(2,1)S(1)} %get-tuple-element.343), channel_id=1, source_target_pairs={{0,5},{1,4},{2,7},{3,6},{4,1},{5,0},{6,3},{7,2},{8,13},{9,12},{10,... | collective-permute-start | bytes 983048 | tf_op jit(solution)/shard_map/ppermute | solution.py:847
  276.5 14.8 %collective-permute-start.86 = (bf16[160,1024]{1,0:T(8,128)(2,1)S(1)}, bf16[160,1024]{1,0:T(8,128)(2,1)S(1)}, u32[]{:S(2)}, u32[]{:S(2)}) collective-permute-start(bf16[160,1024]{1,0:T(8,128)(2,1)S(1)} %get-tuple-element.344), channel_id=1, source_target_pairs={{0,4},{2,6},{4,0},{6,2},{1,5},{3,7},{5,1},{7,3},{8,12},{10,14},{12... | collective-permute-start | bytes 983048 | tf_op jit(solution)/shard_map/ppermute | solution.py:838
  276.8 15.1 %collective-permute-start.87 = (bf16[160,1024]{1,0:T(8,128)(2,1)S(1)}, bf16[160,1024]{1,0:T(8,128)(2,1)S(1)}, u32[]{:S(2)}, u32[]{:S(2)}) collective-permute-start(bf16[160,1024]{1,0:T(8,128)(2,1)S(1)} %get-tuple-element.345), channel_id=1, source_target_pairs={{0,1},{1,0},{2,3},{3,2},{4,5},{5,4},{6,7},{7,6},{8,9},{9,8},{10,11... | collective-permute-start | bytes 983048 | tf_op jit(solution)/shard_map/ppermute | solution.py:841
  297.4 30.8 %collective-permute-start.90 = (bf16[1280,512]{1,0:T(8,128)(2,1)S(1)}, bf16[1280,512]{1,0:T(8,128)(2,1)S(1)}, u32[]{:S(2)}, u32[]{:S(2)}) collective-permute-start(bf16[1280,512]{1,0:T(8,128)(2,1)S(1)} %fetch.1.refs_1_), channel_id=1, source_target_pairs={{0,4},{2,6},{4,0},{6,2},{1,5},{3,7},{5,1},{7,3},{8,12},{10,14},{12... | collective-permute-start | bytes 3932168 | tf_op jit(solution)/shard_map/ppermute | solution.py:838
  298.7 8.4 %collective-permute-start.91 = (bf16[288,512]{1,0:T(8,128)(2,1)S(1)}, bf16[288,512]{1,0:T(8,128)(2,1)S(1)}, u32[]{:S(2)}, u32[]{:S(2)}) collective-permute-start(bf16[288,512]{1,0:T(8,128)(2,1)S(1)} %copy-done.48), channel_id=1, source_target_pairs={{0,8},{8,16},{16,24},{24,0},{1,9},{9,17},{17,25},{25,1},{2,10},{10... | collective-permute-start | bytes 884744 | tf_op jit(solution)/shard_map/ppermute | solution.py:850
  300.2 28.0 %collective-permute-start.88 = (f32[80,1024]{1,0:T(8,128)S(1)}, f32[80,1024]{1,0:T(8,128)S(1)}, u32[]{:S(2)}, u32[]{:S(2)}) collective-permute-start(f32[80,1024]{1,0:T(8,128)S(1)} %copy-done.29), channel_id=1, source_target_pairs={{0,1},{1,0},{2,3},{3,2},{4,5},{5,4},{6,7},{7,6},{8,9},{9,8},{10,11... | collective-permute-start | bytes 983048 | tf_op jit(solution)/shard_map/ppermute | solution.py:841
  303.8 24.4 %collective-permute-start.89 = (f32[80,1024]{1,0:T(8,128)}, f32[80,1024]{1,0:T(8,128)S(1)}, u32[]{:S(2)}, u32[]{:S(2)}) collective-permute-start(f32[80,1024]{1,0:T(8,128)} %get-tuple-element.361.refs_2_), channel_id=1, source_target_pairs={{0,1},{1,0},{2,3},{3,2},{4,5},{5,4},{6,7},{7,6},{8,9},{9,8},{10,11... | collective-permute-start | bytes 983048 | tf_op jit(solution)/shard_map/ppermute | solution.py:841
  304.1 21.6 %collective-permute-start.92 = (bf16[288,512]{1,0:T(8,128)(2,1)S(1)}, bf16[288,512]{1,0:T(8,128)(2,1)S(1)}, u32[]{:S(2)}, u32[]{:S(2)}) collective-permute-start(bf16[288,512]{1,0:T(8,128)(2,1)S(1)} %copy-done.47), channel_id=1, source_target_pairs={{0,16},{8,24},{16,0},{24,8},{1,17},{9,25},{17,1},{25,9},{2,18},{10... | collective-permute-start | bytes 884744 | tf_op jit(solution)/shard_map/ppermute | solution.py:850
  307.2 21.0 %collective-permute-start.93 = (bf16[288,512]{1,0:T(8,128)(2,1)S(1)}, bf16[288,512]{1,0:T(8,128)(2,1)S(1)}, u32[]{:S(2)}, u32[]{:S(2)}) collective-permute-start(bf16[288,512]{1,0:T(8,128)(2,1)S(1)} %copy-done.46), channel_id=1, source_target_pairs={{0,24},{8,0},{16,8},{24,16},{1,25},{9,1},{17,9},{25,17},{2,26},{10... | collective-permute-start | bytes 884744 | tf_op jit(solution)/shard_map/ppermute | solution.py:850
  330.9 9.6 %collective-permute-start.97 = (bf16[256,512]{1,0:T(8,128)(2,1)S(1)}, bf16[256,512]{1,0:T(8,128)(2,1)S(1)}, u32[]{:S(2)}, u32[]{:S(2)}) collective-permute-start(bf16[256,512]{1,0:T(8,128)(2,1)S(1)} %get-tuple-element.371.refs_4_), channel_id=1, source_target_pairs={{0,4},{2,6},{4,0},{6,2},{1,5},{3,7},{5,1},{7,3},{8,12},{10,14},{12... | collective-permute-start | bytes 786440 | tf_op jit(solution)/shard_map/ppermute | solution.py:838
  331.2 8.5 %collective-permute-start.96 = (f32[24,256]{1,0:T(8,128)S(1)}, f32[24,256]{1,0:T(8,128)S(1)}, u32[]{:S(2)}, u32[]{:S(2)}) collective-permute-start(f32[24,256]{1,0:T(8,128)S(1)} %get-tuple-element.370.refs_0_), channel_id=1, source_target_pairs={{0,1},{1,0},{2,3},{3,2},{4,5},{5,4},{6,7},{7,6},{8,9},{9,8},{10,11... | collective-permute-start | bytes 73736 | tf_op jit(solution)/shard_map/ppermute | solution.py:841
  (109 other events, 885.8 us)
Sparse Core Ops, SparseCore 0:
  10.2 28.8 all-gather.4
  41.2 43.8 all-gather.6
  86.6 28.3 all-gather.8
  116.4 43.8 all-gather.10
  171.8 41.9 reduce-scatter.3
  220.2 25.1 reduce-scatter.5
  248.3 42.1 reduce-scatter.7

commit v18 on v17

--- a/solution.py
+++ b/solution.py
@@ -610,17 +610,15 @@
         copy.wait()
 
 
-def shard_sum_kernel(depth, own_hbm, stacked, crossed, *refs):
+def shard_sum_kernel(depth, own_hbm, mine_a, mine_b, cross_a, cross_b, *refs):
     *others, part_ref, mine_ref, pair_ref, own, sems = refs
-    count = stacked.shape[0]
-    first, *copies = start_copies(
-        [
-            (own_hbm, own),
-            (stacked, pair_ref.at[pl.ds(0, count), :]),
-            (crossed, pair_ref.at[pl.ds(count, count), :]),
-        ],
-        sems,
-    )
+    moves = [(own_hbm, own)]
+    row = 0
+    for source in (mine_a, mine_b, cross_a, cross_b):
+        count = source.shape[0]
+        moves.append((source, pair_ref.at[pl.ds(row, count), :]))
+        row += count
+    first, *copies = start_copies(moves, sems)
     first.wait()
     rows, width = part_ref.shape[0], mine_ref.shape[1]
     terms = [ref[...].astype(f32) for ref in (own, *others)]
@@ -1276,6 +1274,7 @@
         shapes = [((width, 3 * feats), bf16), ((width, feats), bf16)]
         if l == 0:
             shapes = [((fsdp, width_own + 32, 4 * feats), bf16)]
+        sums_now = sums_one
         kept = [sums_one, upstream] + ([sums_two] if l + 1 == depth else [])
         *attn_grads, head_sums[l], upstream_b, sums_one, upstream, sums_kept = [
             *kernel_call(
@@ -1312,19 +1311,26 @@
             upstream_chunks = gather_rows(upstream_b)
         row_sums[l] = (sums_one, sums_two)
 
-    sources = [mlp_parts[0]]
-    for l in range(1, depth):
-        sources += [mlp_parts[l], attn_parts[l]]
     blocks = 3 * depth - 1
-    (stacked,) = kernel_call(
-        functools.partial(fetch_kernel, len(sources)),
-        [((blocks * width_own, hidden), bf16)],
-        *[Far(v) for v in sources],
-        name="fetch",
-        after=(upstream_b,),
-        scratch=[DMA((blocks,))],
-    )
-    outputs_own, _ = kernel_call(
+
+    def fetch(sources, after):
+        count = sum(v.shape[1] // hidden for v in sources)
+        return kernel_call(
+            functools.partial(fetch_kernel, len(sources)),
+            [((count * width_own, hidden), bf16)],
+            *[Far(v) for v in sources],
+            name="fetch",
+            after=after,
+            scratch=[DMA((count,))],
+        )[0]
+
+    upper = [v for l in range(1, depth) for v in (mlp_parts[l], attn_parts[l])]
+    stacked = (fetch(mlp_parts[:1], (upstream_b,)), fetch(upper, (sums_now,)))
+    crossed = [swap_x(v) for v in stacked]
+    own_term, *other_terms = attn_grads
+    other_terms = [shift_z(term, d + 1) for d, term in enumerate(other_terms)]
+    inputs_other = swap_y(upstream)
+    outputs_own, output_token = kernel_call(
         functools.partial(sum_out_kernel, shift_row(depth - 1, 3)),
         [saved((rows, width), f32), TOKEN],
         *output_sums[0],
@@ -1332,12 +1338,9 @@
         vecs,
         mask,
         name="sum_out",
+        after=(Anywhere(inputs_other),),
         scratch=[pltpu.VMEM((rows, width), f32)] * 2 + [DMA((2,))],
     )
-    own_term, *other_terms = attn_grads
-    other_terms = [shift_z(term, d + 1) for d, term in enumerate(other_terms)]
-    crossed = swap_x(stacked)
-    others = (swap_y(upstream), swap_y(outputs_own))
     part, mine, pair = kernel_call(
         functools.partial(shard_sum_kernel, depth),
         [
@@ -1346,13 +1349,13 @@
             ((2 * blocks * width_own, hidden), bf16),
         ],
         Far(own_term),
-        stacked,
-        crossed,
+        *[Anywhere(v) for v in (*stacked, *crossed)],
         *other_terms,
         name="shard_sum",
-        after=others,
-        scratch=[pltpu.VMEM(own_term.shape, bf16), DMA((3,))],
-    )
+        after=(output_token,),
+        scratch=[pltpu.VMEM(own_term.shape, bf16), DMA((5,))],
+    )
+    others = (inputs_other, swap_y(outputs_own))
     if outer > 1:
         part = lax.psum(part, "ctx", axis_index_groups=outer_groups)
     *placed, place_token = kernel_call(
@@ -1380,7 +1383,7 @@
         part,
         swap_x(part),
         name="vector_plane",
-        after=(place_token,),
+        after=(place_token, Anywhere(others[1])),
     )
     grad_inputs, outputs = kernel_call(
         functools.partial(place_rows_kernel, 2),

time: 359 us -> 361 us (level)
    unnamed x104 -> x102, local copies, waits for them, and re-layouts: 6.05 us -> 7.64 us
    pallas_call x60 -> x61, Pallas kernels: 90 us -> 90.4 us  [kernel_call(): pl.pallas_call(run, out_shape=out_shape, in_specs=specs, out_specs=out_sp...]
    ppermute x18 -> x19, starting transfers between devices: 14.4 us -> 14.6 us  [swap_x(): return lax.ppermute(value, 'ctx', [(i, i ^ 2) for i in range(ctx)])]
    ppermute x18 -> x19, waiting for transfers between devices: 28.7 us -> 28.7 us  [swap_x(): return lax.ppermute(value, 'ctx', [(i, i ^ 2) for i in range(ctx)])]
  transfers between devices with their start and end apart: 108 -> 109, of which waited for: 50 -> 50; matrix products, arithmetic and copies ran while one was open for 0% -> 0% of each run, Pallas kernels for 21% -> 21%
where the time goes in v18:
time: 361 us; the launch traced here: 356 us
  waiting for transfers between devices  127 us (35%)
  starting transfers between devices  115 us (32%)
  Pallas kernels  90.4 us (25%)
  between operations  15.7 us (4%)
  local copies, waits for them, and re-layouts  8.36 us (2%)
    pallas_call x61, Pallas kernels, kernel_call(): pl.pallas_call(run, out_shape=out_shape, in_specs=specs, out_specs=out_sp...  90.4 us
    ppermute x43, starting transfers between devices, swap_core(): return lax.ppermute(value, 'ctx', [(i, i ^ 1) for i in range(ctx)])  56.7 us
    ppermute x16, waiting for transfers between devices, swap_xy(): return lax.ppermute(value, ('ctx', 'tp'), pairs)  36.6 us
    ppermute x19, waiting for transfers between devices, swap_x(): return lax.ppermute(value, 'ctx', [(i, i ^ 2) for i in range(ctx)])  28.7 us
    ppermute x6, waiting for transfers between devices, shift_z(): lax.ppermute(value, 'fsdp', [(i, (i + d) % fsdp) for i in range(fsdp)])  18.9 us
    ppermute x16, starting transfers between devices, swap_xy(): return lax.ppermute(value, ('ctx', 'tp'), pairs)  18.3 us
    all_gather x2, waiting for transfers between devices, per_device(): mlp_w.append(lax.all_gather(own, 'fsdp', axis=0, tiled=True))  17.6 us
    ppermute x18, starting transfers between devices, swap_y(): return lax.ppermute(value, 'tp', [(i, i ^ 1) for i in range(tp)])  14.8 us
  transfers between devices with their start and end apart: 109, of which 50 were waited for; matrix products, arithmetic and copies ran while one was open for 0% of the time, Pallas kernels for 21%

profile of v18, /device:TPU:9, one launch (start us, length us, event | category | flops | bytes accessed | tf_op | source)
XLA Modules:
  0.0 356.2 jit_solution(14083862442610565006)
XLA Ops:
  15.2 2.3 prep_upstream.1
  46.0 3.5 attn.5
  51.9 2.6 attn.4
  54.7 2.2 collective-permute-start.18
  57.4 3.6 %collective-permute-done.18.refs_1_ = bf16[80,1024]{1,0:T(8,128)(2,1)S(1)} collective-permute-done((bf16[80,1024]{1,0:T(8,128)(2,1)S(1)}, bf16[80,1024]{1,0:T(8,128)(2,1)S(1)}, u32[]{:S(2)}, u32[]{:S(2)}) %collective-permute-start.18) | collective-permute-done | bytes 163872 | tf_op jit(solution)/shard_map/ppermute | solution.py:845
  61.0 3.7 %collective-permute-done.19.refs_2_ = bf16[80,1024]{1,0:T(8,128)(2,1)S(1)} collective-permute-done((bf16[80,1024]{1,0:T(8,128)(2,1)S(1)}, bf16[80,1024]{1,0:T(8,128)(2,1)S(1)}, u32[]{:S(2)}, u32[]{:S(2)}) %collective-permute-start.19) | collective-permute-done | bytes 163872 | tf_op jit(solution)/shard_map/ppermute | solution.py:836
  73.3 2.4 collective-permute-start.26
  79.0 6.0 %all-gather.7.cloned.1.call-done.refs_4_ = bf16[1024,1024]{1,0:T(8,128)(2,1)} async-done(((bf16[256,1024]{1,0:T(8,128)(2,1)}), bf16[1024,1024]{1,0:T(8,128)(2,1)}) %all-gather.7.cloned.1.call-update) | async-done | bytes 2097168 | tf_op jit(solution)/shard_map/all_gather | solution.py:917
  91.4 2.2 collective-permute-start.29
  94.1 3.6 %collective-permute-done.29.refs_1_ = bf16[80,1024]{1,0:T(8,128)(2,1)S(1)} collective-permute-done((bf16[80,1024]{1,0:T(8,128)(2,1)S(1)}, bf16[80,1024]{1,0:T(8,128)(2,1)S(1)}, u32[]{:S(2)}, u32[]{:S(2)}) %collective-permute-start.29) | collective-permute-done | bytes 163872 | tf_op jit(solution)/shard_map/ppermute | solution.py:845
  97.7 3.6 %collective-permute-done.30.refs_2_ = bf16[80,1024]{1,0:T(8,128)(2,1)S(1)} collective-permute-done((bf16[80,1024]{1,0:T(8,128)(2,1)S(1)}, bf16[80,1024]{1,0:T(8,128)(2,1)S(1)}, u32[]{:S(2)}, u32[]{:S(2)}) %collective-permute-start.30) | collective-permute-done | bytes 163872 | tf_op jit(solution)/shard_map/ppermute | solution.py:836
  110.1 2.3 collective-permute-start.37
  119.0 2.6 attn.7
  122.6 2.6 attn.6
  128.1 4.2 %collective-permute-done.40.refs_1_ = bf16[80,1024]{1,0:T(8,128)(2,1)S(1)} collective-permute-done((bf16[80,1024]{1,0:T(8,128)(2,1)S(1)}, bf16[80,1024]{1,0:T(8,128)(2,1)S(1)}, u32[]{:S(2)}, u32[]{:S(2)}) %collective-permute-start.40) | collective-permute-done | bytes 163872 | tf_op jit(solution)/shard_map/ppermute | solution.py:845
  132.3 3.4 collective-permute-done.41.refs_2_
  144.1 2.3 collective-permute-start.48
  148.7 11.6 %all-gather.11.cloned.1.call-done.refs_4_ = bf16[1024,1024]{1,0:T(8,128)(2,1)} async-done(((bf16[256,1024]{1,0:T(8,128)(2,1)}), bf16[1024,1024]{1,0:T(8,128)(2,1)}) %all-gather.11.cloned.1.call-update) | async-done | bytes 2097168 | tf_op jit(solution)/shard_map/all_gather | solution.py:917
  160.3 3.5 mlp.6
  168.2 3.5 mlp_grad.2
  175.9 2.2 collective-permute-start.51
  178.6 3.7 %collective-permute-done.51.refs_1_ = bf16[80,1024]{1,0:T(8,128)(2,1)S(1)} collective-permute-done((bf16[80,1024]{1,0:T(8,128)(2,1)S(1)}, bf16[80,1024]{1,0:T(8,128)(2,1)S(1)}, u32[]{:S(2)}, u32[]{:S(2)}) %collective-permute-start.51) | collective-permute-done | bytes 163872 | tf_op jit(solution)/shard_map/ppermute | solution.py:845
  182.3 3.7 %collective-permute-done.52.refs_2_ = bf16[80,1024]{1,0:T(8,128)(2,1)S(1)} collective-permute-done((bf16[80,1024]{1,0:T(8,128)(2,1)S(1)}, bf16[80,1024]{1,0:T(8,128)(2,1)S(1)}, u32[]{:S(2)}, u32[]{:S(2)}) %collective-permute-start.52) | collective-permute-done | bytes 163872 | tf_op jit(solution)/shard_map/ppermute | solution.py:836
  193.8 2.3 collective-permute-start.59
  198.4 2.5 attn_back.4
  201.0 2.5 attn_back.5
  206.3 2.2 collective-permute-start.62
  209.1 3.9 %collective-permute-done.62.refs_1_ = bf16[80,1024]{1,0:T(8,128)(2,1)S(1)} collective-permute-done((bf16[80,1024]{1,0:T(8,128)(2,1)S(1)}, bf16[80,1024]{1,0:T(8,128)(2,1)S(1)}, u32[]{:S(2)}, u32[]{:S(2)}) %collective-permute-start.62) | collective-permute-done | bytes 163872 | tf_op jit(solution)/shard_map/ppermute | solution.py:845
  213.0 3.6 %collective-permute-done.63.refs_2_ = bf16[80,1024]{1,0:T(8,128)(2,1)S(1)} collective-permute-done((bf16[80,1024]{1,0:T(8,128)(2,1)S(1)}, bf16[80,1024]{1,0:T(8,128)(2,1)S(1)}, u32[]{:S(2)}, u32[]{:S(2)}) %collective-permute-start.63) | collective-permute-done | bytes 163872 | tf_op jit(solution)/shard_map/ppermute | solution.py:836
  217.4 2.7 attn_grad.2
  228.2 2.3 collective-permute-start.70
  232.7 2.5 mlp_back.6
  236.7 3.4 mlp_grad.3
  240.3 2.3 collective-permute-done.72.refs_1_
  242.7 2.2 collective-permute-start.73
  245.4 3.9 %collective-permute-done.73.refs_1_ = bf16[80,1024]{1,0:T(8,128)(2,1)S(1)} collective-permute-done((bf16[80,1024]{1,0:T(8,128)(2,1)S(1)}, bf16[80,1024]{1,0:T(8,128)(2,1)S(1)}, u32[]{:S(2)}, u32[]{:S(2)}) %collective-permute-start.73) | collective-permute-done | bytes 163872 | tf_op jit(solution)/shard_map/ppermute | solution.py:845
  249.3 3.6 %collective-permute-done.74.refs_2_ = bf16[80,1024]{1,0:T(8,128)(2,1)S(1)} collective-permute-done((bf16[80,1024]{1,0:T(8,128)(2,1)S(1)}, bf16[80,1024]{1,0:T(8,128)(2,1)S(1)}, u32[]{:S(2)}, u32[]{:S(2)}) %collective-permute-start.74) | collective-permute-done | bytes 163872 | tf_op jit(solution)/shard_map/ppermute | solution.py:836
  263.2 2.3 collective-permute-start.81
  267.7 2.5 attn_back.6
  270.3 2.5 attn_back.7
  275.9 2.2 collective-permute-start.85
  278.6 7.2 %collective-permute-done.85.refs_1_ = bf16[160,1024]{1,0:T(8,128)(2,1)S(1)} collective-permute-done((bf16[160,1024]{1,0:T(8,128)(2,1)S(1)}, bf16[160,1024]{1,0:T(8,128)(2,1)S(1)}, u32[]{:S(2)}, u32[]{:S(2)}) %collective-permute-start.85) | collective-permute-done | bytes 327712 | tf_op jit(solution)/shard_map/ppermute | solution.py:845
  285.8 7.1 %collective-permute-done.86.refs_2_ = bf16[160,1024]{1,0:T(8,128)(2,1)S(1)} collective-permute-done((bf16[160,1024]{1,0:T(8,128)(2,1)S(1)}, bf16[160,1024]{1,0:T(8,128)(2,1)S(1)}, u32[]{:S(2)}, u32[]{:S(2)}) %collective-permute-start.86) | collective-permute-done | bytes 327712 | tf_op jit(solution)/shard_map/ppermute | solution.py:836
  297.2 2.7 attn_grad.3
  304.1 2.5 collective-permute-start.93
  312.4 15.9 %collective-permute-done.93.refs_6_ = bf16[288,512]{1,0:T(8,128)(2,1)S(1)} collective-permute-done((bf16[288,512]{1,0:T(8,128)(2,1)}, bf16[288,512]{1,0:T(8,128)(2,1)S(1)}, u32[]{:S(2)}, u32[]{:S(2)}) %collective-permute-start.93) | collective-permute-done | bytes 294944 | tf_op jit(solution)/shard_map/ppermute | solution.py:848
  328.3 3.0 collective-permute-done.94.refs_7_
  339.9 4.3 %place.1 = (f32[2,3,256,512]{3,2,1,0:T(8,128)}, f32[2,512,256]{2,1,0:T(8,128)}, f32[2,256,2048]{2,1,0:T(8,128)}, f32[2,2048,256]{2,1,0:T(8,128)}, f32[8,128]{1,0:T(8,128)S(1)}) custom-call(bf16[2560,512]{1,0:T(8,128)(2,1)S(1)} %get-tuple-element.374.refs_0_, bf16[2560,512]{1,0:T(8,128)(2,1)S(1)} %collective-permute-done.99.refs_1_), custom_call_target="tpu_custom_call" | custom-call | tf_op jit(solution)/shard_map/place/pallas_call | solution.py:87
  (366 shorter events, 167.4 us)
Async XLA Ops:
  7.2 34.2 %all-gather.5.cloned.1.call-start = ((), (), s32[]{:S(2)}) async-start(), calls=%async_computation.3 | async-start | bytes 1310720 | tf_op jit(solution)/shard_map/all_gather | solution.py:915
  9.0 76.0 %all-gather.7.cloned.1.call-start = ((), (), s32[]{:S(2)}) async-start(), calls=%async_computation.4 | async-start | bytes 2621440 | tf_op jit(solution)/shard_map/all_gather | solution.py:917
  11.2 103.8 %all-gather.9.cloned.1.call-start = ((), (), s32[]{:S(2)}) async-start(), calls=%async_computation.5 | async-start | bytes 1310720 | tf_op jit(solution)/shard_map/all_gather | solution.py:915
  11.4 10.9 %collective-permute-start.2 = (bf16[17,256]{1,0:T(8,128)(2,1)S(1)}, bf16[17,256]{1,0:T(8,128)(2,1)S(1)}, u32[]{:S(2)}, u32[]{:S(2)}) collective-permute-start(bf16[17,256]{1,0:T(8,128)(2,1)S(1)} %fusion.1), channel_id=1, source_target_pairs={{0,8},{8,16},{16,24},{24,0},{1,9},{9,17},{17,25},{25,1},{2,10},{10... | collective-permute-start | bytes 26120 | tf_op jit(solution)/shard_map/ppermute | solution.py:848
  12.8 10.8 %collective-permute-start.1 = (bf16[17,256]{1,0:T(8,128)(2,1)S(1)}, bf16[17,256]{1,0:T(8,128)(2,1)S(1)}, u32[]{:S(2)}, u32[]{:S(2)}) collective-permute-start(bf16[17,256]{1,0:T(8,128)(2,1)S(1)} %fusion.1), channel_id=1, source_target_pairs={{0,16},{8,24},{16,0},{24,8},{1,17},{9,25},{17,1},{25,9},{2,18},{10... | collective-permute-start | bytes 26120 | tf_op jit(solution)/shard_map/ppermute | solution.py:848
  13.9 10.0 %collective-permute-start = (bf16[17,256]{1,0:T(8,128)(2,1)S(1)}, bf16[17,256]{1,0:T(8,128)(2,1)S(1)}, u32[]{:S(2)}, u32[]{:S(2)}) collective-permute-start(bf16[17,256]{1,0:T(8,128)(2,1)S(1)} %fusion.1), channel_id=1, source_target_pairs={{0,24},{8,0},{16,8},{24,16},{1,25},{9,1},{17,9},{25,17},{2,26},{10... | collective-permute-start | bytes 26120 | tf_op jit(solution)/shard_map/ppermute | solution.py:848
  17.5 9.3 %collective-permute-start.9 = (bf16[80,1024]{1,0:T(8,128)(2,1)S(1)}, bf16[80,1024]{1,0:T(8,128)(2,1)S(1)}, u32[]{:S(2)}, u32[]{:S(2)}) collective-permute-start(bf16[80,1024]{1,0:T(8,128)(2,1)S(1)} %get-tuple-element.203.refs_0_), channel_id=1, source_target_pairs={{0,2},{2,0},{4,6},{6,4},{1,3},{3,1},{5,7},{7,5},{8,10},{10,8},{12,... | collective-permute-start | bytes 491528 | tf_op jit(solution)/shard_map/ppermute | solution.py:833
  19.1 8.9 %collective-permute-start.8 = (bf16[80,1024]{1,0:T(8,128)(2,1)S(1)}, bf16[80,1024]{1,0:T(8,128)(2,1)S(1)}, u32[]{:S(2)}, u32[]{:S(2)}) collective-permute-start(bf16[80,1024]{1,0:T(8,128)(2,1)S(1)} %get-tuple-element.203.refs_0_), channel_id=1, source_target_pairs={{0,1},{1,0},{2,3},{3,2},{4,5},{5,4},{6,7},{7,6},{8,9},{9,8},{10,11... | collective-permute-start | bytes 491528 | tf_op jit(solution)/shard_map/ppermute | solution.py:839
  22.2 138.1 %all-gather.11.cloned.1.call-start = ((), (), s32[]{:S(2)}) async-start(), calls=%async_computation.6 | async-start | bytes 2621440 | tf_op jit(solution)/shard_map/all_gather | solution.py:917
  25.5 9.0 %collective-permute-start.5 = (bf16[80,1024]{1,0:T(8,128)(2,1)S(1)}, bf16[80,1024]{1,0:T(8,128)(2,1)}, u32[]{:S(2)}, u32[]{:S(2)}) collective-permute-start(bf16[80,1024]{1,0:T(8,128)(2,1)S(1)} %get-tuple-element.199.refs_0_), channel_id=1, source_target_pairs={{0,1},{1,0},{2,3},{3,2},{4,5},{5,4},{6,7},{7,6},{8,9},{9,8},{10,11... | collective-permute-start | bytes 491528 | tf_op jit(solution)/shard_map/ppermute | solution.py:839
  26.8 8.9 %collective-permute-start.4 = (bf16[80,1024]{1,0:T(8,128)(2,1)S(1)}, bf16[80,1024]{1,0:T(8,128)(2,1)}, u32[]{:S(2)}, u32[]{:S(2)}) collective-permute-start(bf16[80,1024]{1,0:T(8,128)(2,1)S(1)} %get-tuple-element.199.refs_0_), channel_id=1, source_target_pairs={{0,4},{2,6},{4,0},{6,2},{1,5},{3,7},{5,1},{7,3},{8,12},{10,14},{12... | collective-permute-start | bytes 491528 | tf_op jit(solution)/shard_map/ppermute | solution.py:836
  28.0 10.5 %collective-permute-start.3 = (bf16[80,1024]{1,0:T(8,128)(2,1)S(1)}, bf16[80,1024]{1,0:T(8,128)(2,1)}, u32[]{:S(2)}, u32[]{:S(2)}) collective-permute-start(bf16[80,1024]{1,0:T(8,128)(2,1)S(1)} %get-tuple-element.199.refs_0_), channel_id=1, source_target_pairs={{0,5},{1,4},{2,7},{3,6},{4,1},{5,0},{6,3},{7,2},{8,13},{9,12},{10,... | collective-permute-start | bytes 491528 | tf_op jit(solution)/shard_map/ppermute | solution.py:845
  28.2 11.4 %collective-permute-start.12 = (bf16[80,1024]{1,0:T(8,128)(2,1)S(1)}, bf16[80,1024]{1,0:T(8,128)(2,1)S(1)}, u32[]{:S(2)}, u32[]{:S(2)}) collective-permute-start(bf16[80,1024]{1,0:T(8,128)(2,1)S(1)} %collective-permute-done.8.refs_3_), channel_id=1, source_target_pairs={{0,2},{2,0},{4,6},{6,4},{1,3},{3,1},{5,7},{7,5},{8,10},{10,8},{12,... | collective-permute-start | bytes 491528 | tf_op jit(solution)/shard_map/ppermute | solution.py:833
  31.3 8.3 %collective-permute-start.11 = (bf16[80,1024]{1,0:T(8,128)(2,1)S(1)}, bf16[80,1024]{1,0:T(8,128)(2,1)S(1)}, u32[]{:S(2)}, u32[]{:S(2)}) collective-permute-start(bf16[80,1024]{1,0:T(8,128)(2,1)S(1)} %collective-permute-done.7.refs_2_), channel_id=1, source_target_pairs={{0,2},{2,0},{4,6},{6,4},{1,3},{3,1},{5,7},{7,5},{8,10},{10,8},{12,... | collective-permute-start | bytes 491528 | tf_op jit(solution)/shard_map/ppermute | solution.py:833
  34.5 9.9 %collective-permute-start.13 = (bf16[80,1024]{1,0:T(8,128)(2,1)S(1)}, bf16[80,1024]{1,0:T(8,128)(2,1)}, u32[]{:S(2)}, u32[]{:S(2)}) collective-permute-start(bf16[80,1024]{1,0:T(8,128)(2,1)S(1)} %get-tuple-element.199.refs_0_), channel_id=1, source_target_pairs={{0,2},{2,0},{4,6},{6,4},{1,3},{3,1},{5,7},{7,5},{8,10},{10,8},{12,... | collective-permute-start | bytes 491528 | tf_op jit(solution)/shard_map/ppermute | solution.py:833
  51.7 168.6 %reduce-scatter.4.cloned.1.call-start = ((), (), s32[]{:S(2)}) async-start(), calls=%async_computation.7 | async-start | bytes 2621440 | tf_op jit(solution)/shard_map/reduce_scatter | solution.py:1099
  57.2 8.1 %collective-permute-start.20 = (bf16[80,1024]{1,0:T(8,128)(2,1)S(1)}, bf16[80,1024]{1,0:T(8,128)(2,1)S(1)}, u32[]{:S(2)}, u32[]{:S(2)}) collective-permute-start(bf16[80,1024]{1,0:T(8,128)(2,1)S(1)} %get-tuple-element.220), channel_id=1, source_target_pairs={{0,1},{1,0},{2,3},{3,2},{4,5},{5,4},{6,7},{7,6},{8,9},{9,8},{10,11... | collective-permute-start | bytes 491528 | tf_op jit(solution)/shard_map/ppermute | solution.py:839
  69.3 8.7 %collective-permute-start.24 = (bf16[80,1024]{1,0:T(8,128)(2,1)S(1)}, bf16[80,1024]{1,0:T(8,128)(2,1)S(1)}, u32[]{:S(2)}, u32[]{:S(2)}) collective-permute-start(bf16[80,1024]{1,0:T(8,128)(2,1)S(1)} %get-tuple-element.222.refs_0_), channel_id=1, source_target_pairs={{0,2},{2,0},{4,6},{6,4},{1,3},{3,1},{5,7},{7,5},{8,10},{10,8},{12,... | collective-permute-start | bytes 491528 | tf_op jit(solution)/shard_map/ppermute | solution.py:833
  93.9 8.2 %collective-permute-start.31 = (bf16[80,1024]{1,0:T(8,128)(2,1)S(1)}, bf16[80,1024]{1,0:T(8,128)(2,1)S(1)}, u32[]{:S(2)}, u32[]{:S(2)}) collective-permute-start(bf16[80,1024]{1,0:T(8,128)(2,1)S(1)} %get-tuple-element.234), channel_id=1, source_target_pairs={{0,1},{1,0},{2,3},{3,2},{4,5},{5,4},{6,7},{7,6},{8,9},{9,8},{10,11... | collective-permute-start | bytes 491528 | tf_op jit(solution)/shard_map/ppermute | solution.py:839
  106.0 10.7 %collective-permute-start.35 = (bf16[80,1024]{1,0:T(8,128)(2,1)S(1)}, bf16[80,1024]{1,0:T(8,128)(2,1)S(1)}, u32[]{:S(2)}, u32[]{:S(2)}) collective-permute-start(bf16[80,1024]{1,0:T(8,128)(2,1)S(1)} %get-tuple-element.236.refs_0_), channel_id=1, source_target_pairs={{0,2},{2,0},{4,6},{6,4},{1,3},{3,1},{5,7},{7,5},{8,10},{10,8},{12,... | collective-permute-start | bytes 491528 | tf_op jit(solution)/shard_map/ppermute | solution.py:833
  127.6 8.2 %collective-permute-start.41 = (bf16[80,1024]{1,0:T(8,128)(2,1)S(1)}, bf16[80,1024]{1,0:T(8,128)(2,1)S(1)}, u32[]{:S(2)}, u32[]{:S(2)}) collective-permute-start(bf16[80,1024]{1,0:T(8,128)(2,1)S(1)} %get-tuple-element.251), channel_id=1, source_target_pairs={{0,4},{2,6},{4,0},{6,2},{1,5},{3,7},{5,1},{7,3},{8,12},{10,14},{12... | collective-permute-start | bytes 491528 | tf_op jit(solution)/shard_map/ppermute | solution.py:836
  127.9 8.3 %collective-permute-start.42 = (bf16[80,1024]{1,0:T(8,128)(2,1)S(1)}, bf16[80,1024]{1,0:T(8,128)(2,1)S(1)}, u32[]{:S(2)}, u32[]{:S(2)}) collective-permute-start(bf16[80,1024]{1,0:T(8,128)(2,1)S(1)} %get-tuple-element.252), channel_id=1, source_target_pairs={{0,1},{1,0},{2,3},{3,2},{4,5},{5,4},{6,7},{7,6},{8,9},{9,8},{10,11... | collective-permute-start | bytes 491528 | tf_op jit(solution)/shard_map/ppermute | solution.py:839
  140.1 20.2 %collective-permute-start.46 = (bf16[80,1024]{1,0:T(8,128)(2,1)S(1)}, bf16[80,1024]{1,0:T(8,128)(2,1)S(1)}, u32[]{:S(2)}, u32[]{:S(2)}) collective-permute-start(bf16[80,1024]{1,0:T(8,128)(2,1)S(1)} %get-tuple-element.254.refs_0_), channel_id=1, source_target_pairs={{0,2},{2,0},{4,6},{6,4},{1,3},{3,1},{5,7},{7,5},{8,10},{10,8},{12,... | collective-permute-start | bytes 491528 | tf_op jit(solution)/shard_map/ppermute | solution.py:833
  142.8 17.4 %collective-permute-start.49 = (bf16[80,1024]{1,0:T(8,128)(2,1)S(1)}, bf16[80,1024]{1,0:T(8,128)(2,1)}, u32[]{:S(2)}, u32[]{:S(2)}) collective-permute-start(bf16[80,1024]{1,0:T(8,128)(2,1)S(1)} %collective-permute-done.45.refs_3_), channel_id=1, source_target_pairs={{0,2},{2,0},{4,6},{6,4},{1,3},{3,1},{5,7},{7,5},{8,10},{10,8},{12,... | collective-permute-start | bytes 491528 | tf_op jit(solution)/shard_map/ppermute | solution.py:833
  144.1 16.2 %collective-permute-start.48 = (bf16[80,1024]{1,0:T(8,128)(2,1)S(1)}, bf16[80,1024]{1,0:T(8,128)(2,1)}, u32[]{:S(2)}, u32[]{:S(2)}) collective-permute-start(bf16[80,1024]{1,0:T(8,128)(2,1)S(1)} %collective-permute-done.44.refs_2_), channel_id=1, source_target_pairs={{0,2},{2,0},{4,6},{6,4},{1,3},{3,1},{5,7},{7,5},{8,10},{10,8},{12,... | collective-permute-start | bytes 491528 | tf_op jit(solution)/shard_map/ppermute | solution.py:833
  147.1 13.2 %collective-permute-start.47 = (bf16[80,1024]{1,0:T(8,128)(2,1)S(1)}, bf16[80,1024]{1,0:T(8,128)(2,1)}, u32[]{:S(2)}, u32[]{:S(2)}) collective-permute-start(bf16[80,1024]{1,0:T(8,128)(2,1)S(1)} %collective-permute-done.43.refs_1_), channel_id=1, source_target_pairs={{0,2},{2,0},{4,6},{6,4},{1,3},{3,1},{5,7},{7,5},{8,10},{10,8},{12,... | collective-permute-start | bytes 491528 | tf_op jit(solution)/shard_map/ppermute | solution.py:833
  171.7 82.7 %reduce-scatter.6.cloned.1.call-start = ((), (), s32[]{:S(2)}) async-start(), calls=%async_computation.8 | async-start | bytes 1310720 | tf_op jit(solution)/shard_map/reduce_scatter | solution.py:1099
  178.4 8.2 %collective-permute-start.53 = (bf16[80,1024]{1,0:T(8,128)(2,1)S(1)}, bf16[80,1024]{1,0:T(8,128)(2,1)S(1)}, u32[]{:S(2)}, u32[]{:S(2)}) collective-permute-start(bf16[80,1024]{1,0:T(8,128)(2,1)S(1)} %get-tuple-element.282), channel_id=1, source_target_pairs={{0,1},{1,0},{2,3},{3,2},{4,5},{5,4},{6,7},{7,6},{8,9},{9,8},{10,11... | collective-permute-start | bytes 491528 | tf_op jit(solution)/shard_map/ppermute | solution.py:839
  189.8 11.2 %collective-permute-start.57 = (bf16[80,1024]{1,0:T(8,128)(2,1)S(1)}, bf16[80,1024]{1,0:T(8,128)(2,1)S(1)}, u32[]{:S(2)}, u32[]{:S(2)}) collective-permute-start(bf16[80,1024]{1,0:T(8,128)(2,1)S(1)} %get-tuple-element.285.refs_0_), channel_id=1, source_target_pairs={{0,2},{2,0},{4,6},{6,4},{1,3},{3,1},{5,7},{7,5},{8,10},{10,8},{12,... | collective-permute-start | bytes 491528 | tf_op jit(solution)/shard_map/ppermute | solution.py:833
  192.5 8.4 %collective-permute-start.60 = (bf16[80,1024]{1,0:T(8,128)(2,1)S(1)}, bf16[80,1024]{1,0:T(8,128)(2,1)S(1)}, u32[]{:S(2)}, u32[]{:S(2)}) collective-permute-start(bf16[80,1024]{1,0:T(8,128)(2,1)S(1)} %collective-permute-done.56.refs_3_), channel_id=1, source_target_pairs={{0,2},{2,0},{4,6},{6,4},{1,3},{3,1},{5,7},{7,5},{8,10},{10,8},{12,... | collective-permute-start | bytes 491528 | tf_op jit(solution)/shard_map/ppermute | solution.py:833
  208.8 8.1 %collective-permute-start.64 = (bf16[80,1024]{1,0:T(8,128)(2,1)S(1)}, bf16[80,1024]{1,0:T(8,128)(2,1)S(1)}, u32[]{:S(2)}, u32[]{:S(2)}) collective-permute-start(bf16[80,1024]{1,0:T(8,128)(2,1)S(1)} %get-tuple-element.301), channel_id=1, source_target_pairs={{0,1},{1,0},{2,3},{3,2},{4,5},{5,4},{6,7},{7,6},{8,9},{9,8},{10,11... | collective-permute-start | bytes 491528 | tf_op jit(solution)/shard_map/ppermute | solution.py:839
  220.1 81.1 %reduce-scatter.8.cloned.1.call-start = ((), (), s32[]{:S(2)}) async-start(), calls=%async_computation.9 | async-start | bytes 2621440 | tf_op jit(solution)/shard_map/reduce_scatter | solution.py:1099
  224.1 11.2 %collective-permute-start.68 = (bf16[80,1024]{1,0:T(8,128)(2,1)S(1)}, bf16[80,1024]{1,0:T(8,128)(2,1)S(1)}, u32[]{:S(2)}, u32[]{:S(2)}) collective-permute-start(bf16[80,1024]{1,0:T(8,128)(2,1)S(1)} %settle.2.refs_0_), channel_id=1, source_target_pairs={{0,2},{2,0},{4,6},{6,4},{1,3},{3,1},{5,7},{7,5},{8,10},{10,8},{12,... | collective-permute-start | bytes 491528 | tf_op jit(solution)/shard_map/ppermute | solution.py:833
  226.6 8.7 %collective-permute-start.71 = (bf16[80,1024]{1,0:T(8,128)(2,1)S(1)}, bf16[80,1024]{1,0:T(8,128)(2,1)S(1)}, u32[]{:S(2)}, u32[]{:S(2)}) collective-permute-start(bf16[80,1024]{1,0:T(8,128)(2,1)S(1)} %collective-permute-done.67.refs_3_), channel_id=1, source_target_pairs={{0,2},{2,0},{4,6},{6,4},{1,3},{3,1},{5,7},{7,5},{8,10},{10,8},{12,... | collective-permute-start | bytes 491528 | tf_op jit(solution)/shard_map/ppermute | solution.py:833
  259.0 11.2 %collective-permute-start.79 = (bf16[80,1024]{1,0:T(8,128)(2,1)S(1)}, bf16[80,1024]{1,0:T(8,128)(2,1)S(1)}, u32[]{:S(2)}, u32[]{:S(2)}) collective-permute-start(bf16[80,1024]{1,0:T(8,128)(2,1)S(1)} %get-tuple-element.328.refs_0_), channel_id=1, source_target_pairs={{0,2},{2,0},{4,6},{6,4},{1,3},{3,1},{5,7},{7,5},{8,10},{10,8},{12,... | collective-permute-start | bytes 491528 | tf_op jit(solution)/shard_map/ppermute | solution.py:833
  261.6 8.6 %collective-permute-start.82 = (bf16[80,1024]{1,0:T(8,128)(2,1)S(1)}, bf16[80,1024]{1,0:T(8,128)(2,1)S(1)}, u32[]{:S(2)}, u32[]{:S(2)}) collective-permute-start(bf16[80,1024]{1,0:T(8,128)(2,1)S(1)} %collective-permute-done.78.refs_3_), channel_id=1, source_target_pairs={{0,2},{2,0},{4,6},{6,4},{1,3},{3,1},{5,7},{7,5},{8,10},{10,8},{12,... | collective-permute-start | bytes 491528 | tf_op jit(solution)/shard_map/ppermute | solution.py:833
  275.9 9.9 %collective-permute-start.85 = (bf16[160,1024]{1,0:T(8,128)(2,1)S(1)}, bf16[160,1024]{1,0:T(8,128)(2,1)S(1)}, u32[]{:S(2)}, u32[]{:S(2)}) collective-permute-start(bf16[160,1024]{1,0:T(8,128)(2,1)S(1)} %get-tuple-element.344), channel_id=1, source_target_pairs={{0,5},{1,4},{2,7},{3,6},{4,1},{5,0},{6,3},{7,2},{8,13},{9,12},{10,... | collective-permute-start | bytes 983048 | tf_op jit(solution)/shard_map/ppermute | solution.py:845
  278.0 14.8 %collective-permute-start.86 = (bf16[160,1024]{1,0:T(8,128)(2,1)S(1)}, bf16[160,1024]{1,0:T(8,128)(2,1)S(1)}, u32[]{:S(2)}, u32[]{:S(2)}) collective-permute-start(bf16[160,1024]{1,0:T(8,128)(2,1)S(1)} %get-tuple-element.345), channel_id=1, source_target_pairs={{0,4},{2,6},{4,0},{6,2},{1,5},{3,7},{5,1},{7,3},{8,12},{10,14},{12... | collective-permute-start | bytes 983048 | tf_op jit(solution)/shard_map/ppermute | solution.py:836
  278.3 15.1 %collective-permute-start.87 = (bf16[160,1024]{1,0:T(8,128)(2,1)S(1)}, bf16[160,1024]{1,0:T(8,128)(2,1)S(1)}, u32[]{:S(2)}, u32[]{:S(2)}) collective-permute-start(bf16[160,1024]{1,0:T(8,128)(2,1)S(1)} %get-tuple-element.346), channel_id=1, source_target_pairs={{0,1},{1,0},{2,3},{3,2},{4,5},{5,4},{6,7},{7,6},{8,9},{9,8},{10,11... | collective-permute-start | bytes 983048 | tf_op jit(solution)/shard_map/ppermute | solution.py:839
  295.0 36.3 %collective-permute-start.91 = (bf16[768,512]{1,0:T(8,128)(2,1)S(1)}, bf16[768,512]{1,0:T(8,128)(2,1)}, u32[]{:S(2)}, u32[]{:S(2)}) collective-permute-start(bf16[768,512]{1,0:T(8,128)(2,1)S(1)} %fetch.3.refs_2_), channel_id=1, source_target_pairs={{0,4},{2,6},{4,0},{6,2},{1,5},{3,7},{5,1},{7,3},{8,12},{10,14},{12... | collective-permute-start | bytes 2359304 | tf_op jit(solution)/shard_map/ppermute | solution.py:836
  299.9 8.8 %collective-permute-start.88 = (f32[80,1024]{1,0:T(8,128)}, f32[80,1024]{1,0:T(8,128)S(1)}, u32[]{:S(2)}, u32[]{:S(2)}) collective-permute-start(f32[80,1024]{1,0:T(8,128)} %get-tuple-element.360.refs_0_), channel_id=1, source_target_pairs={{0,1},{1,0},{2,3},{3,2},{4,5},{5,4},{6,7},{7,6},{8,9},{9,8},{10,11... | collective-permute-start | bytes 983048 | tf_op jit(solution)/shard_map/ppermute | solution.py:839
  302.2 29.1 %collective-permute-start.90 = (bf16[512,512]{1,0:T(8,128)(2,1)S(1)}, bf16[512,512]{1,0:T(8,128)(2,1)S(1)}, u32[]{:S(2)}, u32[]{:S(2)}) collective-permute-start(bf16[512,512]{1,0:T(8,128)(2,1)S(1)} %fetch.2.refs_1_), channel_id=1, source_target_pairs={{0,4},{2,6},{4,0},{6,2},{1,5},{3,7},{5,1},{7,3},{8,12},{10,14},{12... | collective-permute-start | bytes 1572872 | tf_op jit(solution)/shard_map/ppermute | solution.py:836
  302.6 9.8 %collective-permute-start.92 = (bf16[288,512]{1,0:T(8,128)(2,1)}, bf16[288,512]{1,0:T(8,128)(2,1)S(1)}, u32[]{:S(2)}, u32[]{:S(2)}) collective-permute-start(bf16[288,512]{1,0:T(8,128)(2,1)} %get-tuple-element.368), channel_id=1, source_target_pairs={{0,8},{8,16},{16,24},{24,0},{1,9},{9,17},{17,25},{25,1},{2,10},{10... | collective-permute-start | bytes 884744 | tf_op jit(solution)/shard_map/ppermute | solution.py:848
  304.1 24.2 %collective-permute-start.93 = (bf16[288,512]{1,0:T(8,128)(2,1)}, bf16[288,512]{1,0:T(8,128)(2,1)S(1)}, u32[]{:S(2)}, u32[]{:S(2)}) collective-permute-start(bf16[288,512]{1,0:T(8,128)(2,1)} %get-tuple-element.369), channel_id=1, source_target_pairs={{0,16},{8,24},{16,0},{24,8},{1,17},{9,25},{17,1},{25,9},{2,18},{10... | collective-permute-start | bytes 884744 | tf_op jit(solution)/shard_map/ppermute | solution.py:848
  308.7 22.6 %collective-permute-start.94 = (bf16[288,512]{1,0:T(8,128)(2,1)}, bf16[288,512]{1,0:T(8,128)(2,1)S(1)}, u32[]{:S(2)}, u32[]{:S(2)}) collective-permute-start(bf16[288,512]{1,0:T(8,128)(2,1)} %get-tuple-element.370), channel_id=1, source_target_pairs={{0,24},{8,0},{16,8},{24,16},{1,25},{9,1},{17,9},{25,17},{2,26},{10... | collective-permute-start | bytes 884744 | tf_op jit(solution)/shard_map/ppermute | solution.py:848
  334.2 10.0 %collective-permute-start.89 = (f32[80,1024]{1,0:T(8,128)S(1)}, f32[80,1024]{1,0:T(8,128)S(1)}, u32[]{:S(2)}, u32[]{:S(2)}) collective-permute-start(f32[80,1024]{1,0:T(8,128)S(1)} %copy-done.31), channel_id=1, source_target_pairs={{0,1},{1,0},{2,3},{3,2},{4,5},{5,4},{6,7},{7,6},{8,9},{9,8},{10,11... | collective-permute-start | bytes 983048 | tf_op jit(solution)/shard_map/ppermute | solution.py:839
  334.6 9.7 %collective-permute-start.98 = (bf16[256,512]{1,0:T(8,128)(2,1)S(1)}, bf16[256,512]{1,0:T(8,128)(2,1)S(1)}, u32[]{:S(2)}, u32[]{:S(2)}) collective-permute-start(bf16[256,512]{1,0:T(8,128)(2,1)S(1)} %get-tuple-element.373.refs_4_), channel_id=1, source_target_pairs={{0,4},{2,6},{4,0},{6,2},{1,5},{3,7},{5,1},{7,3},{8,12},{10,14},{12... | collective-permute-start | bytes 786440 | tf_op jit(solution)/shard_map/ppermute | solution.py:836
  335.7 8.6 %collective-permute-start.97 = (f32[24,256]{1,0:T(8,128)S(1)}, f32[24,256]{1,0:T(8,128)S(1)}, u32[]{:S(2)}, u32[]{:S(2)}) collective-permute-start(f32[24,256]{1,0:T(8,128)S(1)} %get-tuple-element.372.refs_0_), channel_id=1, source_target_pairs={{0,1},{1,0},{2,3},{3,2},{4,5},{5,4},{6,7},{7,6},{8,9},{9,8},{10,11... | collective-permute-start | bytes 73736 | tf_op jit(solution)/shard_map/ppermute | solution.py:839
  (109 other events, 866.7 us)
Sparse Core Ops, SparseCore 0:
  10.2 28.8 all-gather.4
  41.2 43.8 all-gather.6
  86.6 28.3 all-gather.8
  116.4 43.8 all-gather.10
  171.8 41.9 reduce-scatter.3
  220.2 25.1 reduce-scatter.5
  248.3 42.1 reduce-scatter.7

commit v19 on v18

--- a/solution.py
+++ b/solution.py
@@ -1274,7 +1274,7 @@
         shapes = [((width, 3 * feats), bf16), ((width, feats), bf16)]
         if l == 0:
             shapes = [((fsdp, width_own + 32, 4 * feats), bf16)]
-        sums_now = sums_one
+        sums_now, rows_now = sums_one, upstream
         kept = [sums_one, upstream] + ([sums_two] if l + 1 == depth else [])
         *attn_grads, head_sums[l], upstream_b, sums_one, upstream, sums_kept = [
             *kernel_call(
@@ -1329,7 +1329,7 @@
     crossed = [swap_x(v) for v in stacked]
     own_term, *other_terms = attn_grads
     other_terms = [shift_z(term, d + 1) for d, term in enumerate(other_terms)]
-    inputs_other = swap_y(upstream)
+    inputs_other = swap_y(rows_now)
     outputs_own, output_token = kernel_call(
         functools.partial(sum_out_kernel, shift_row(depth - 1, 3)),
         [saved((rows, width), f32), TOKEN],

time: 361 us -> 360 us (level)
    ppermute x6, waiting for transfers between devices: 18.9 us -> 22.8 us  [shift_z(): lax.ppermute(value, 'fsdp', [(i, (i + d) % fsdp) for i in range(fsdp)])]
    unnamed x102 -> x98, local copies, waits for them, and re-layouts: 7.64 us -> 6.01 us
where the time goes in v19:
time: 360 us; the launch traced here: 355 us
  waiting for transfers between devices  129 us (36%)
  starting transfers between devices  113 us (31%)
  Pallas kernels  90.5 us (25%)
  between operations  15.7 us (4%)
  local copies, waits for them, and re-layouts  6.74 us (2%)
    pallas_call x61, Pallas kernels, kernel_call(): pl.pallas_call(run, out_shape=out_shape, in_specs=specs, out_specs=out_sp...  90.5 us
    ppermute x43, starting transfers between devices, swap_core(): return lax.ppermute(value, 'ctx', [(i, i ^ 1) for i in range(ctx)])  56.5 us
    ppermute x16, waiting for transfers between devices, swap_xy(): return lax.ppermute(value, ('ctx', 'tp'), pairs)  36.7 us
    ppermute x19, waiting for transfers between devices, swap_x(): return lax.ppermute(value, 'ctx', [(i, i ^ 2) for i in range(ctx)])  28.7 us
    ppermute x6, waiting for transfers between devices, shift_z(): lax.ppermute(value, 'fsdp', [(i, (i + d) % fsdp) for i in range(fsdp)])  22.8 us
    ppermute x16, starting transfers between devices, swap_xy(): return lax.ppermute(value, ('ctx', 'tp'), pairs)  18.3 us
    all_gather x2, waiting for transfers between devices, per_device(): mlp_w.append(lax.all_gather(own, 'fsdp', axis=0, tiled=True))  17.6 us
    ppermute x18, starting transfers between devices, swap_y(): return lax.ppermute(value, 'tp', [(i, i ^ 1) for i in range(tp)])  14.7 us
  transfers between devices with their start and end apart: 109, of which 50 were waited for; matrix products, arithmetic and copies ran while one was open for 0% of the time, Pallas kernels for 21%

profile of v19, /device:TPU:9, one launch (start us, length us, event | category | flops | bytes accessed | tf_op | source)
XLA Modules:
  0.0 354.7 jit_solution(13968076270092517950)
XLA Ops:
  15.2 2.3 prep_upstream.1
  46.0 3.5 attn.5
  51.9 2.6 attn.4
  54.7 2.2 collective-permute-start.18
  57.4 3.6 %collective-permute-done.18.refs_1_ = bf16[80,1024]{1,0:T(8,128)(2,1)S(1)} collective-permute-done((bf16[80,1024]{1,0:T(8,128)(2,1)S(1)}, bf16[80,1024]{1,0:T(8,128)(2,1)S(1)}, u32[]{:S(2)}, u32[]{:S(2)}) %collective-permute-start.18) | collective-permute-done | bytes 163872 | tf_op jit(solution)/shard_map/ppermute | solution.py:845
  61.0 3.7 %collective-permute-done.19.refs_2_ = bf16[80,1024]{1,0:T(8,128)(2,1)S(1)} collective-permute-done((bf16[80,1024]{1,0:T(8,128)(2,1)S(1)}, bf16[80,1024]{1,0:T(8,128)(2,1)S(1)}, u32[]{:S(2)}, u32[]{:S(2)}) %collective-permute-start.19) | collective-permute-done | bytes 163872 | tf_op jit(solution)/shard_map/ppermute | solution.py:836
  73.2 2.5 collective-permute-start.26
  79.0 6.1 %all-gather.7.cloned.1.call-done.refs_4_ = bf16[1024,1024]{1,0:T(8,128)(2,1)} async-done(((bf16[256,1024]{1,0:T(8,128)(2,1)}), bf16[1024,1024]{1,0:T(8,128)(2,1)}) %all-gather.7.cloned.1.call-update) | async-done | bytes 2097168 | tf_op jit(solution)/shard_map/all_gather | solution.py:917
  94.1 3.6 %collective-permute-done.29.refs_1_ = bf16[80,1024]{1,0:T(8,128)(2,1)S(1)} collective-permute-done((bf16[80,1024]{1,0:T(8,128)(2,1)S(1)}, bf16[80,1024]{1,0:T(8,128)(2,1)S(1)}, u32[]{:S(2)}, u32[]{:S(2)}) %collective-permute-start.29) | collective-permute-done | bytes 163872 | tf_op jit(solution)/shard_map/ppermute | solution.py:845
  97.7 3.6 %collective-permute-done.30.refs_2_ = bf16[80,1024]{1,0:T(8,128)(2,1)S(1)} collective-permute-done((bf16[80,1024]{1,0:T(8,128)(2,1)S(1)}, bf16[80,1024]{1,0:T(8,128)(2,1)S(1)}, u32[]{:S(2)}, u32[]{:S(2)}) %collective-permute-start.30) | collective-permute-done | bytes 163872 | tf_op jit(solution)/shard_map/ppermute | solution.py:836
  110.0 2.3 collective-permute-start.37
  119.0 2.6 attn.7
  122.6 2.6 attn.6
  125.4 2.2 collective-permute-start.40
  128.1 4.2 %collective-permute-done.40.refs_1_ = bf16[80,1024]{1,0:T(8,128)(2,1)S(1)} collective-permute-done((bf16[80,1024]{1,0:T(8,128)(2,1)S(1)}, bf16[80,1024]{1,0:T(8,128)(2,1)S(1)}, u32[]{:S(2)}, u32[]{:S(2)}) %collective-permute-start.40) | collective-permute-done | bytes 163872 | tf_op jit(solution)/shard_map/ppermute | solution.py:845
  132.3 3.4 collective-permute-done.41.refs_2_
  144.0 2.3 collective-permute-start.48
  148.7 11.6 %all-gather.11.cloned.1.call-done.refs_4_ = bf16[1024,1024]{1,0:T(8,128)(2,1)} async-done(((bf16[256,1024]{1,0:T(8,128)(2,1)}), bf16[1024,1024]{1,0:T(8,128)(2,1)}) %all-gather.11.cloned.1.call-update) | async-done | bytes 2097168 | tf_op jit(solution)/shard_map/all_gather | solution.py:917
  160.3 3.5 mlp.6
  168.1 3.5 mlp_grad.2
  178.6 3.7 %collective-permute-done.51.refs_1_ = bf16[80,1024]{1,0:T(8,128)(2,1)S(1)} collective-permute-done((bf16[80,1024]{1,0:T(8,128)(2,1)S(1)}, bf16[80,1024]{1,0:T(8,128)(2,1)S(1)}, u32[]{:S(2)}, u32[]{:S(2)}) %collective-permute-start.51) | collective-permute-done | bytes 163872 | tf_op jit(solution)/shard_map/ppermute | solution.py:845
  182.3 3.7 %collective-permute-done.52.refs_2_ = bf16[80,1024]{1,0:T(8,128)(2,1)S(1)} collective-permute-done((bf16[80,1024]{1,0:T(8,128)(2,1)S(1)}, bf16[80,1024]{1,0:T(8,128)(2,1)S(1)}, u32[]{:S(2)}, u32[]{:S(2)}) %collective-permute-start.52) | collective-permute-done | bytes 163872 | tf_op jit(solution)/shard_map/ppermute | solution.py:836
  193.8 2.3 collective-permute-start.59
  198.4 2.5 attn_back.4
  201.0 2.5 attn_back.5
  206.3 2.2 collective-permute-start.62
  209.0 3.9 %collective-permute-done.62.refs_1_ = bf16[80,1024]{1,0:T(8,128)(2,1)S(1)} collective-permute-done((bf16[80,1024]{1,0:T(8,128)(2,1)S(1)}, bf16[80,1024]{1,0:T(8,128)(2,1)S(1)}, u32[]{:S(2)}, u32[]{:S(2)}) %collective-permute-start.62) | collective-permute-done | bytes 163872 | tf_op jit(solution)/shard_map/ppermute | solution.py:845
  212.9 3.6 %collective-permute-done.63.refs_2_ = bf16[80,1024]{1,0:T(8,128)(2,1)S(1)} collective-permute-done((bf16[80,1024]{1,0:T(8,128)(2,1)S(1)}, bf16[80,1024]{1,0:T(8,128)(2,1)S(1)}, u32[]{:S(2)}, u32[]{:S(2)}) %collective-permute-start.63) | collective-permute-done | bytes 163872 | tf_op jit(solution)/shard_map/ppermute | solution.py:836
  217.3 2.7 attn_grad.2
  228.2 2.3 collective-permute-start.70
  232.7 2.5 mlp_back.6
  236.7 3.4 mlp_grad.3
  240.2 2.3 collective-permute-done.72.refs_1_
  242.7 2.2 collective-permute-start.73
  245.4 3.9 %collective-permute-done.73.refs_1_ = bf16[80,1024]{1,0:T(8,128)(2,1)S(1)} collective-permute-done((bf16[80,1024]{1,0:T(8,128)(2,1)S(1)}, bf16[80,1024]{1,0:T(8,128)(2,1)S(1)}, u32[]{:S(2)}, u32[]{:S(2)}) %collective-permute-start.73) | collective-permute-done | bytes 163872 | tf_op jit(solution)/shard_map/ppermute | solution.py:845
  249.3 3.6 %collective-permute-done.74.refs_2_ = bf16[80,1024]{1,0:T(8,128)(2,1)S(1)} collective-permute-done((bf16[80,1024]{1,0:T(8,128)(2,1)S(1)}, bf16[80,1024]{1,0:T(8,128)(2,1)S(1)}, u32[]{:S(2)}, u32[]{:S(2)}) %collective-permute-start.74) | collective-permute-done | bytes 163872 | tf_op jit(solution)/shard_map/ppermute | solution.py:836
  261.6 2.3 collective-permute-start.81
  266.1 2.5 attn_back.6
  268.7 2.5 attn_back.7
  274.3 2.2 collective-permute-start.85
  277.0 7.2 %collective-permute-done.85.refs_1_ = bf16[160,1024]{1,0:T(8,128)(2,1)S(1)} collective-permute-done((bf16[160,1024]{1,0:T(8,128)(2,1)S(1)}, bf16[160,1024]{1,0:T(8,128)(2,1)S(1)}, u32[]{:S(2)}, u32[]{:S(2)}) %collective-permute-start.85) | collective-permute-done | bytes 327712 | tf_op jit(solution)/shard_map/ppermute | solution.py:845
  284.2 7.1 %collective-permute-done.86.refs_2_ = bf16[160,1024]{1,0:T(8,128)(2,1)S(1)} collective-permute-done((bf16[160,1024]{1,0:T(8,128)(2,1)S(1)}, bf16[160,1024]{1,0:T(8,128)(2,1)S(1)}, u32[]{:S(2)}, u32[]{:S(2)}) %collective-permute-start.86) | collective-permute-done | bytes 327712 | tf_op jit(solution)/shard_map/ppermute | solution.py:836
  296.9 2.7 attn_grad.3
  302.4 2.6 collective-permute-start.93
  307.0 2.2 collective-permute-done.92.refs_5_
  309.2 17.5 %collective-permute-done.93.refs_6_ = bf16[288,512]{1,0:T(8,128)(2,1)S(1)} collective-permute-done((bf16[288,512]{1,0:T(8,128)(2,1)}, bf16[288,512]{1,0:T(8,128)(2,1)S(1)}, u32[]{:S(2)}, u32[]{:S(2)}) %collective-permute-start.93) | collective-permute-done | bytes 294944 | tf_op jit(solution)/shard_map/ppermute | solution.py:848
  326.7 3.1 collective-permute-done.94.refs_7_
  338.4 4.3 %place.1 = (f32[2,3,256,512]{3,2,1,0:T(8,128)}, f32[2,512,256]{2,1,0:T(8,128)}, f32[2,256,2048]{2,1,0:T(8,128)}, f32[2,2048,256]{2,1,0:T(8,128)}, f32[8,128]{1,0:T(8,128)S(1)}) custom-call(bf16[2560,512]{1,0:T(8,128)(2,1)S(1)} %get-tuple-element.374.refs_0_, bf16[2560,512]{1,0:T(8,128)(2,1)S(1)} %collective-permute-done.99.refs_1_), custom_call_target="tpu_custom_call" | custom-call | tf_op jit(solution)/shard_map/place/pallas_call | solution.py:87
  (362 shorter events, 164.0 us)
Async XLA Ops:
  7.2 34.2 %all-gather.5.cloned.1.call-start = ((), (), s32[]{:S(2)}) async-start(), calls=%async_computation.3 | async-start | bytes 1310720 | tf_op jit(solution)/shard_map/all_gather | solution.py:915
  9.0 76.0 %all-gather.7.cloned.1.call-start = ((), (), s32[]{:S(2)}) async-start(), calls=%async_computation.4 | async-start | bytes 2621440 | tf_op jit(solution)/shard_map/all_gather | solution.py:917
  11.2 103.8 %all-gather.9.cloned.1.call-start = ((), (), s32[]{:S(2)}) async-start(), calls=%async_computation.5 | async-start | bytes 1310720 | tf_op jit(solution)/shard_map/all_gather | solution.py:915
  11.4 10.9 %collective-permute-start.2 = (bf16[17,256]{1,0:T(8,128)(2,1)S(1)}, bf16[17,256]{1,0:T(8,128)(2,1)S(1)}, u32[]{:S(2)}, u32[]{:S(2)}) collective-permute-start(bf16[17,256]{1,0:T(8,128)(2,1)S(1)} %fusion.1), channel_id=1, source_target_pairs={{0,8},{8,16},{16,24},{24,0},{1,9},{9,17},{17,25},{25,1},{2,10},{10... | collective-permute-start | bytes 26120 | tf_op jit(solution)/shard_map/ppermute | solution.py:848
  12.8 10.8 %collective-permute-start.1 = (bf16[17,256]{1,0:T(8,128)(2,1)S(1)}, bf16[17,256]{1,0:T(8,128)(2,1)S(1)}, u32[]{:S(2)}, u32[]{:S(2)}) collective-permute-start(bf16[17,256]{1,0:T(8,128)(2,1)S(1)} %fusion.1), channel_id=1, source_target_pairs={{0,16},{8,24},{16,0},{24,8},{1,17},{9,25},{17,1},{25,9},{2,18},{10... | collective-permute-start | bytes 26120 | tf_op jit(solution)/shard_map/ppermute | solution.py:848
  13.9 9.9 %collective-permute-start = (bf16[17,256]{1,0:T(8,128)(2,1)S(1)}, bf16[17,256]{1,0:T(8,128)(2,1)S(1)}, u32[]{:S(2)}, u32[]{:S(2)}) collective-permute-start(bf16[17,256]{1,0:T(8,128)(2,1)S(1)} %fusion.1), channel_id=1, source_target_pairs={{0,24},{8,0},{16,8},{24,16},{1,25},{9,1},{17,9},{25,17},{2,26},{10... | collective-permute-start | bytes 26120 | tf_op jit(solution)/shard_map/ppermute | solution.py:848
  17.5 9.2 %collective-permute-start.9 = (bf16[80,1024]{1,0:T(8,128)(2,1)S(1)}, bf16[80,1024]{1,0:T(8,128)(2,1)S(1)}, u32[]{:S(2)}, u32[]{:S(2)}) collective-permute-start(bf16[80,1024]{1,0:T(8,128)(2,1)S(1)} %get-tuple-element.203.refs_0_), channel_id=1, source_target_pairs={{0,2},{2,0},{4,6},{6,4},{1,3},{3,1},{5,7},{7,5},{8,10},{10,8},{12,... | collective-permute-start | bytes 491528 | tf_op jit(solution)/shard_map/ppermute | solution.py:833
  19.1 8.9 %collective-permute-start.8 = (bf16[80,1024]{1,0:T(8,128)(2,1)S(1)}, bf16[80,1024]{1,0:T(8,128)(2,1)S(1)}, u32[]{:S(2)}, u32[]{:S(2)}) collective-permute-start(bf16[80,1024]{1,0:T(8,128)(2,1)S(1)} %get-tuple-element.203.refs_0_), channel_id=1, source_target_pairs={{0,1},{1,0},{2,3},{3,2},{4,5},{5,4},{6,7},{7,6},{8,9},{9,8},{10,11... | collective-permute-start | bytes 491528 | tf_op jit(solution)/shard_map/ppermute | solution.py:839
  22.2 138.1 %all-gather.11.cloned.1.call-start = ((), (), s32[]{:S(2)}) async-start(), calls=%async_computation.6 | async-start | bytes 2621440 | tf_op jit(solution)/shard_map/all_gather | solution.py:917
  25.5 9.0 %collective-permute-start.5 = (bf16[80,1024]{1,0:T(8,128)(2,1)S(1)}, bf16[80,1024]{1,0:T(8,128)(2,1)}, u32[]{:S(2)}, u32[]{:S(2)}) collective-permute-start(bf16[80,1024]{1,0:T(8,128)(2,1)S(1)} %get-tuple-element.199.refs_0_), channel_id=1, source_target_pairs={{0,1},{1,0},{2,3},{3,2},{4,5},{5,4},{6,7},{7,6},{8,9},{9,8},{10,11... | collective-permute-start | bytes 491528 | tf_op jit(solution)/shard_map/ppermute | solution.py:839
  26.8 8.9 %collective-permute-start.4 = (bf16[80,1024]{1,0:T(8,128)(2,1)S(1)}, bf16[80,1024]{1,0:T(8,128)(2,1)}, u32[]{:S(2)}, u32[]{:S(2)}) collective-permute-start(bf16[80,1024]{1,0:T(8,128)(2,1)S(1)} %get-tuple-element.199.refs_0_), channel_id=1, source_target_pairs={{0,4},{2,6},{4,0},{6,2},{1,5},{3,7},{5,1},{7,3},{8,12},{10,14},{12... | collective-permute-start | bytes 491528 | tf_op jit(solution)/shard_map/ppermute | solution.py:836
  28.0 10.5 %collective-permute-start.3 = (bf16[80,1024]{1,0:T(8,128)(2,1)S(1)}, bf16[80,1024]{1,0:T(8,128)(2,1)}, u32[]{:S(2)}, u32[]{:S(2)}) collective-permute-start(bf16[80,1024]{1,0:T(8,128)(2,1)S(1)} %get-tuple-element.199.refs_0_), channel_id=1, source_target_pairs={{0,5},{1,4},{2,7},{3,6},{4,1},{5,0},{6,3},{7,2},{8,13},{9,12},{10,... | collective-permute-start | bytes 491528 | tf_op jit(solution)/shard_map/ppermute | solution.py:845
  28.2 11.4 %collective-permute-start.12 = (bf16[80,1024]{1,0:T(8,128)(2,1)S(1)}, bf16[80,1024]{1,0:T(8,128)(2,1)S(1)}, u32[]{:S(2)}, u32[]{:S(2)}) collective-permute-start(bf16[80,1024]{1,0:T(8,128)(2,1)S(1)} %collective-permute-done.8.refs_3_), channel_id=1, source_target_pairs={{0,2},{2,0},{4,6},{6,4},{1,3},{3,1},{5,7},{7,5},{8,10},{10,8},{12,... | collective-permute-start | bytes 491528 | tf_op jit(solution)/shard_map/ppermute | solution.py:833
  31.3 8.3 %collective-permute-start.11 = (bf16[80,1024]{1,0:T(8,128)(2,1)S(1)}, bf16[80,1024]{1,0:T(8,128)(2,1)S(1)}, u32[]{:S(2)}, u32[]{:S(2)}) collective-permute-start(bf16[80,1024]{1,0:T(8,128)(2,1)S(1)} %collective-permute-done.7.refs_2_), channel_id=1, source_target_pairs={{0,2},{2,0},{4,6},{6,4},{1,3},{3,1},{5,7},{7,5},{8,10},{10,8},{12,... | collective-permute-start | bytes 491528 | tf_op jit(solution)/shard_map/ppermute | solution.py:833
  34.4 9.9 %collective-permute-start.13 = (bf16[80,1024]{1,0:T(8,128)(2,1)S(1)}, bf16[80,1024]{1,0:T(8,128)(2,1)}, u32[]{:S(2)}, u32[]{:S(2)}) collective-permute-start(bf16[80,1024]{1,0:T(8,128)(2,1)S(1)} %get-tuple-element.199.refs_0_), channel_id=1, source_target_pairs={{0,2},{2,0},{4,6},{6,4},{1,3},{3,1},{5,7},{7,5},{8,10},{10,8},{12,... | collective-permute-start | bytes 491528 | tf_op jit(solution)/shard_map/ppermute | solution.py:833
  51.7 168.6 %reduce-scatter.4.cloned.1.call-start = ((), (), s32[]{:S(2)}) async-start(), calls=%async_computation.7 | async-start | bytes 2621440 | tf_op jit(solution)/shard_map/reduce_scatter | solution.py:1099
  69.3 8.7 %collective-permute-start.24 = (bf16[80,1024]{1,0:T(8,128)(2,1)S(1)}, bf16[80,1024]{1,0:T(8,128)(2,1)S(1)}, u32[]{:S(2)}, u32[]{:S(2)}) collective-permute-start(bf16[80,1024]{1,0:T(8,128)(2,1)S(1)} %get-tuple-element.222.refs_0_), channel_id=1, source_target_pairs={{0,2},{2,0},{4,6},{6,4},{1,3},{3,1},{5,7},{7,5},{8,10},{10,8},{12,... | collective-permute-start | bytes 491528 | tf_op jit(solution)/shard_map/ppermute | solution.py:833
  93.8 8.2 %collective-permute-start.31 = (bf16[80,1024]{1,0:T(8,128)(2,1)S(1)}, bf16[80,1024]{1,0:T(8,128)(2,1)S(1)}, u32[]{:S(2)}, u32[]{:S(2)}) collective-permute-start(bf16[80,1024]{1,0:T(8,128)(2,1)S(1)} %get-tuple-element.234), channel_id=1, source_target_pairs={{0,1},{1,0},{2,3},{3,2},{4,5},{5,4},{6,7},{7,6},{8,9},{9,8},{10,11... | collective-permute-start | bytes 491528 | tf_op jit(solution)/shard_map/ppermute | solution.py:839
  106.0 10.7 %collective-permute-start.35 = (bf16[80,1024]{1,0:T(8,128)(2,1)S(1)}, bf16[80,1024]{1,0:T(8,128)(2,1)S(1)}, u32[]{:S(2)}, u32[]{:S(2)}) collective-permute-start(bf16[80,1024]{1,0:T(8,128)(2,1)S(1)} %get-tuple-element.236.refs_0_), channel_id=1, source_target_pairs={{0,2},{2,0},{4,6},{6,4},{1,3},{3,1},{5,7},{7,5},{8,10},{10,8},{12,... | collective-permute-start | bytes 491528 | tf_op jit(solution)/shard_map/ppermute | solution.py:833
  127.6 8.2 %collective-permute-start.41 = (bf16[80,1024]{1,0:T(8,128)(2,1)S(1)}, bf16[80,1024]{1,0:T(8,128)(2,1)S(1)}, u32[]{:S(2)}, u32[]{:S(2)}) collective-permute-start(bf16[80,1024]{1,0:T(8,128)(2,1)S(1)} %get-tuple-element.251), channel_id=1, source_target_pairs={{0,4},{2,6},{4,0},{6,2},{1,5},{3,7},{5,1},{7,3},{8,12},{10,14},{12... | collective-permute-start | bytes 491528 | tf_op jit(solution)/shard_map/ppermute | solution.py:836
  127.8 8.3 %collective-permute-start.42 = (bf16[80,1024]{1,0:T(8,128)(2,1)S(1)}, bf16[80,1024]{1,0:T(8,128)(2,1)S(1)}, u32[]{:S(2)}, u32[]{:S(2)}) collective-permute-start(bf16[80,1024]{1,0:T(8,128)(2,1)S(1)} %get-tuple-element.252), channel_id=1, source_target_pairs={{0,1},{1,0},{2,3},{3,2},{4,5},{5,4},{6,7},{7,6},{8,9},{9,8},{10,11... | collective-permute-start | bytes 491528 | tf_op jit(solution)/shard_map/ppermute | solution.py:839
  140.0 20.2 %collective-permute-start.46 = (bf16[80,1024]{1,0:T(8,128)(2,1)S(1)}, bf16[80,1024]{1,0:T(8,128)(2,1)S(1)}, u32[]{:S(2)}, u32[]{:S(2)}) collective-permute-start(bf16[80,1024]{1,0:T(8,128)(2,1)S(1)} %get-tuple-element.254.refs_0_), channel_id=1, source_target_pairs={{0,2},{2,0},{4,6},{6,4},{1,3},{3,1},{5,7},{7,5},{8,10},{10,8},{12,... | collective-permute-start | bytes 491528 | tf_op jit(solution)/shard_map/ppermute | solution.py:833
  142.8 17.4 %collective-permute-start.49 = (bf16[80,1024]{1,0:T(8,128)(2,1)S(1)}, bf16[80,1024]{1,0:T(8,128)(2,1)}, u32[]{:S(2)}, u32[]{:S(2)}) collective-permute-start(bf16[80,1024]{1,0:T(8,128)(2,1)S(1)} %collective-permute-done.45.refs_3_), channel_id=1, source_target_pairs={{0,2},{2,0},{4,6},{6,4},{1,3},{3,1},{5,7},{7,5},{8,10},{10,8},{12,... | collective-permute-start | bytes 491528 | tf_op jit(solution)/shard_map/ppermute | solution.py:833
  144.0 16.2 %collective-permute-start.48 = (bf16[80,1024]{1,0:T(8,128)(2,1)S(1)}, bf16[80,1024]{1,0:T(8,128)(2,1)}, u32[]{:S(2)}, u32[]{:S(2)}) collective-permute-start(bf16[80,1024]{1,0:T(8,128)(2,1)S(1)} %collective-permute-done.44.refs_2_), channel_id=1, source_target_pairs={{0,2},{2,0},{4,6},{6,4},{1,3},{3,1},{5,7},{7,5},{8,10},{10,8},{12,... | collective-permute-start | bytes 491528 | tf_op jit(solution)/shard_map/ppermute | solution.py:833
  147.1 13.2 %collective-permute-start.47 = (bf16[80,1024]{1,0:T(8,128)(2,1)S(1)}, bf16[80,1024]{1,0:T(8,128)(2,1)}, u32[]{:S(2)}, u32[]{:S(2)}) collective-permute-start(bf16[80,1024]{1,0:T(8,128)(2,1)S(1)} %collective-permute-done.43.refs_1_), channel_id=1, source_target_pairs={{0,2},{2,0},{4,6},{6,4},{1,3},{3,1},{5,7},{7,5},{8,10},{10,8},{12,... | collective-permute-start | bytes 491528 | tf_op jit(solution)/shard_map/ppermute | solution.py:833
  171.7 82.1 %reduce-scatter.6.cloned.1.call-start = ((), (), s32[]{:S(2)}) async-start(), calls=%async_computation.8 | async-start | bytes 1310720 | tf_op jit(solution)/shard_map/reduce_scatter | solution.py:1099
  178.3 8.3 %collective-permute-start.53 = (bf16[80,1024]{1,0:T(8,128)(2,1)S(1)}, bf16[80,1024]{1,0:T(8,128)(2,1)S(1)}, u32[]{:S(2)}, u32[]{:S(2)}) collective-permute-start(bf16[80,1024]{1,0:T(8,128)(2,1)S(1)} %get-tuple-element.282), channel_id=1, source_target_pairs={{0,1},{1,0},{2,3},{3,2},{4,5},{5,4},{6,7},{7,6},{8,9},{9,8},{10,11... | collective-permute-start | bytes 491528 | tf_op jit(solution)/shard_map/ppermute | solution.py:839
  189.7 11.2 %collective-permute-start.57 = (bf16[80,1024]{1,0:T(8,128)(2,1)S(1)}, bf16[80,1024]{1,0:T(8,128)(2,1)S(1)}, u32[]{:S(2)}, u32[]{:S(2)}) collective-permute-start(bf16[80,1024]{1,0:T(8,128)(2,1)S(1)} %get-tuple-element.285.refs_0_), channel_id=1, source_target_pairs={{0,2},{2,0},{4,6},{6,4},{1,3},{3,1},{5,7},{7,5},{8,10},{10,8},{12,... | collective-permute-start | bytes 491528 | tf_op jit(solution)/shard_map/ppermute | solution.py:833
  192.5 8.4 %collective-permute-start.60 = (bf16[80,1024]{1,0:T(8,128)(2,1)S(1)}, bf16[80,1024]{1,0:T(8,128)(2,1)S(1)}, u32[]{:S(2)}, u32[]{:S(2)}) collective-permute-start(bf16[80,1024]{1,0:T(8,128)(2,1)S(1)} %collective-permute-done.56.refs_3_), channel_id=1, source_target_pairs={{0,2},{2,0},{4,6},{6,4},{1,3},{3,1},{5,7},{7,5},{8,10},{10,8},{12,... | collective-permute-start | bytes 491528 | tf_op jit(solution)/shard_map/ppermute | solution.py:833
  208.8 8.1 %collective-permute-start.64 = (bf16[80,1024]{1,0:T(8,128)(2,1)S(1)}, bf16[80,1024]{1,0:T(8,128)(2,1)S(1)}, u32[]{:S(2)}, u32[]{:S(2)}) collective-permute-start(bf16[80,1024]{1,0:T(8,128)(2,1)S(1)} %get-tuple-element.301), channel_id=1, source_target_pairs={{0,1},{1,0},{2,3},{3,2},{4,5},{5,4},{6,7},{7,6},{8,9},{9,8},{10,11... | collective-permute-start | bytes 491528 | tf_op jit(solution)/shard_map/ppermute | solution.py:839
  220.1 79.5 %reduce-scatter.8.cloned.1.call-start = ((), (), s32[]{:S(2)}) async-start(), calls=%async_computation.9 | async-start | bytes 2621440 | tf_op jit(solution)/shard_map/reduce_scatter | solution.py:1099
  224.0 11.2 %collective-permute-start.68 = (bf16[80,1024]{1,0:T(8,128)(2,1)S(1)}, bf16[80,1024]{1,0:T(8,128)(2,1)S(1)}, u32[]{:S(2)}, u32[]{:S(2)}) collective-permute-start(bf16[80,1024]{1,0:T(8,128)(2,1)S(1)} %settle.2.refs_0_), channel_id=1, source_target_pairs={{0,2},{2,0},{4,6},{6,4},{1,3},{3,1},{5,7},{7,5},{8,10},{10,8},{12,... | collective-permute-start | bytes 491528 | tf_op jit(solution)/shard_map/ppermute | solution.py:833
  226.6 8.7 %collective-permute-start.71 = (bf16[80,1024]{1,0:T(8,128)(2,1)S(1)}, bf16[80,1024]{1,0:T(8,128)(2,1)S(1)}, u32[]{:S(2)}, u32[]{:S(2)}) collective-permute-start(bf16[80,1024]{1,0:T(8,128)(2,1)S(1)} %collective-permute-done.67.refs_3_), channel_id=1, source_target_pairs={{0,2},{2,0},{4,6},{6,4},{1,3},{3,1},{5,7},{7,5},{8,10},{10,8},{12,... | collective-permute-start | bytes 491528 | tf_op jit(solution)/shard_map/ppermute | solution.py:833
  245.2 8.1 %collective-permute-start.75 = (bf16[80,1024]{1,0:T(8,128)(2,1)S(1)}, bf16[80,1024]{1,0:T(8,128)(2,1)S(1)}, u32[]{:S(2)}, u32[]{:S(2)}) collective-permute-start(bf16[80,1024]{1,0:T(8,128)(2,1)S(1)} %get-tuple-element.322), channel_id=1, source_target_pairs={{0,1},{1,0},{2,3},{3,2},{4,5},{5,4},{6,7},{7,6},{8,9},{9,8},{10,11... | collective-permute-start | bytes 491528 | tf_op jit(solution)/shard_map/ppermute | solution.py:839
  257.5 11.2 %collective-permute-start.79 = (bf16[80,1024]{1,0:T(8,128)(2,1)S(1)}, bf16[80,1024]{1,0:T(8,128)(2,1)S(1)}, u32[]{:S(2)}, u32[]{:S(2)}) collective-permute-start(bf16[80,1024]{1,0:T(8,128)(2,1)S(1)} %get-tuple-element.328.refs_0_), channel_id=1, source_target_pairs={{0,2},{2,0},{4,6},{6,4},{1,3},{3,1},{5,7},{7,5},{8,10},{10,8},{12,... | collective-permute-start | bytes 491528 | tf_op jit(solution)/shard_map/ppermute | solution.py:833
  260.1 8.5 %collective-permute-start.82 = (bf16[80,1024]{1,0:T(8,128)(2,1)S(1)}, bf16[80,1024]{1,0:T(8,128)(2,1)S(1)}, u32[]{:S(2)}, u32[]{:S(2)}) collective-permute-start(bf16[80,1024]{1,0:T(8,128)(2,1)S(1)} %collective-permute-done.78.refs_3_), channel_id=1, source_target_pairs={{0,2},{2,0},{4,6},{6,4},{1,3},{3,1},{5,7},{7,5},{8,10},{10,8},{12,... | collective-permute-start | bytes 491528 | tf_op jit(solution)/shard_map/ppermute | solution.py:833
  274.3 9.9 %collective-permute-start.85 = (bf16[160,1024]{1,0:T(8,128)(2,1)S(1)}, bf16[160,1024]{1,0:T(8,128)(2,1)S(1)}, u32[]{:S(2)}, u32[]{:S(2)}) collective-permute-start(bf16[160,1024]{1,0:T(8,128)(2,1)S(1)} %get-tuple-element.344), channel_id=1, source_target_pairs={{0,5},{1,4},{2,7},{3,6},{4,1},{5,0},{6,3},{7,2},{8,13},{9,12},{10,... | collective-permute-start | bytes 983048 | tf_op jit(solution)/shard_map/ppermute | solution.py:845
  276.5 14.8 %collective-permute-start.86 = (bf16[160,1024]{1,0:T(8,128)(2,1)S(1)}, bf16[160,1024]{1,0:T(8,128)(2,1)S(1)}, u32[]{:S(2)}, u32[]{:S(2)}) collective-permute-start(bf16[160,1024]{1,0:T(8,128)(2,1)S(1)} %get-tuple-element.345), channel_id=1, source_target_pairs={{0,4},{2,6},{4,0},{6,2},{1,5},{3,7},{5,1},{7,3},{8,12},{10,14},{12... | collective-permute-start | bytes 983048 | tf_op jit(solution)/shard_map/ppermute | solution.py:836
  276.8 15.2 %collective-permute-start.87 = (bf16[160,1024]{1,0:T(8,128)(2,1)S(1)}, bf16[160,1024]{1,0:T(8,128)(2,1)S(1)}, u32[]{:S(2)}, u32[]{:S(2)}) collective-permute-start(bf16[160,1024]{1,0:T(8,128)(2,1)S(1)} %get-tuple-element.346), channel_id=1, source_target_pairs={{0,1},{1,0},{2,3},{3,2},{4,5},{5,4},{6,7},{7,6},{8,9},{9,8},{10,11... | collective-permute-start | bytes 983048 | tf_op jit(solution)/shard_map/ppermute | solution.py:839
  293.5 36.3 %collective-permute-start.91 = (bf16[768,512]{1,0:T(8,128)(2,1)S(1)}, bf16[768,512]{1,0:T(8,128)(2,1)}, u32[]{:S(2)}, u32[]{:S(2)}) collective-permute-start(bf16[768,512]{1,0:T(8,128)(2,1)S(1)} %fetch.3.refs_2_), channel_id=1, source_target_pairs={{0,4},{2,6},{4,0},{6,2},{1,5},{3,7},{5,1},{7,3},{8,12},{10,14},{12... | collective-permute-start | bytes 2359304 | tf_op jit(solution)/shard_map/ppermute | solution.py:836
  294.7 10.3 %collective-permute-start.88 = (f32[80,1024]{1,0:T(8,128)S(1)}, f32[80,1024]{1,0:T(8,128)S(1)}, u32[]{:S(2)}, u32[]{:S(2)}) collective-permute-start(f32[80,1024]{1,0:T(8,128)S(1)} %get-tuple-element.359.refs_13_), channel_id=1, source_target_pairs={{0,1},{1,0},{2,3},{3,2},{4,5},{5,4},{6,7},{7,6},{8,9},{9,8},{10,11... | collective-permute-start | bytes 983048 | tf_op jit(solution)/shard_map/ppermute | solution.py:839
  300.6 29.2 %collective-permute-start.90 = (bf16[512,512]{1,0:T(8,128)(2,1)S(1)}, bf16[512,512]{1,0:T(8,128)(2,1)S(1)}, u32[]{:S(2)}, u32[]{:S(2)}) collective-permute-start(bf16[512,512]{1,0:T(8,128)(2,1)S(1)} %fetch.2.refs_1_), channel_id=1, source_target_pairs={{0,4},{2,6},{4,0},{6,2},{1,5},{3,7},{5,1},{7,3},{8,12},{10,14},{12... | collective-permute-start | bytes 1572872 | tf_op jit(solution)/shard_map/ppermute | solution.py:836
  301.0 8.2 %collective-permute-start.92 = (bf16[288,512]{1,0:T(8,128)(2,1)}, bf16[288,512]{1,0:T(8,128)(2,1)S(1)}, u32[]{:S(2)}, u32[]{:S(2)}) collective-permute-start(bf16[288,512]{1,0:T(8,128)(2,1)} %get-tuple-element.368), channel_id=1, source_target_pairs={{0,8},{8,16},{16,24},{24,0},{1,9},{9,17},{17,25},{25,1},{2,10},{10... | collective-permute-start | bytes 884744 | tf_op jit(solution)/shard_map/ppermute | solution.py:848
  302.4 24.2 %collective-permute-start.93 = (bf16[288,512]{1,0:T(8,128)(2,1)}, bf16[288,512]{1,0:T(8,128)(2,1)S(1)}, u32[]{:S(2)}, u32[]{:S(2)}) collective-permute-start(bf16[288,512]{1,0:T(8,128)(2,1)} %get-tuple-element.369), channel_id=1, source_target_pairs={{0,16},{8,24},{16,0},{24,8},{1,17},{9,25},{17,1},{25,9},{2,18},{10... | collective-permute-start | bytes 884744 | tf_op jit(solution)/shard_map/ppermute | solution.py:848
  305.0 24.8 %collective-permute-start.94 = (bf16[288,512]{1,0:T(8,128)(2,1)}, bf16[288,512]{1,0:T(8,128)(2,1)S(1)}, u32[]{:S(2)}, u32[]{:S(2)}) collective-permute-start(bf16[288,512]{1,0:T(8,128)(2,1)} %get-tuple-element.370), channel_id=1, source_target_pairs={{0,24},{8,0},{16,8},{24,16},{1,25},{9,1},{17,9},{25,17},{2,26},{10... | collective-permute-start | bytes 884744 | tf_op jit(solution)/shard_map/ppermute | solution.py:848
  332.7 10.0 %collective-permute-start.89 = (f32[80,1024]{1,0:T(8,128)S(1)}, f32[80,1024]{1,0:T(8,128)S(1)}, u32[]{:S(2)}, u32[]{:S(2)}) collective-permute-start(f32[80,1024]{1,0:T(8,128)S(1)} %copy-done.31), channel_id=1, source_target_pairs={{0,1},{1,0},{2,3},{3,2},{4,5},{5,4},{6,7},{7,6},{8,9},{9,8},{10,11... | collective-permute-start | bytes 983048 | tf_op jit(solution)/shard_map/ppermute | solution.py:839
  332.9 9.8 %collective-permute-start.98 = (bf16[256,512]{1,0:T(8,128)(2,1)S(1)}, bf16[256,512]{1,0:T(8,128)(2,1)S(1)}, u32[]{:S(2)}, u32[]{:S(2)}) collective-permute-start(bf16[256,512]{1,0:T(8,128)(2,1)S(1)} %get-tuple-element.373.refs_4_), channel_id=1, source_target_pairs={{0,4},{2,6},{4,0},{6,2},{1,5},{3,7},{5,1},{7,3},{8,12},{10,14},{12... | collective-permute-start | bytes 786440 | tf_op jit(solution)/shard_map/ppermute | solution.py:836
  334.2 8.6 %collective-permute-start.97 = (f32[24,256]{1,0:T(8,128)S(1)}, f32[24,256]{1,0:T(8,128)S(1)}, u32[]{:S(2)}, u32[]{:S(2)}) collective-permute-start(f32[24,256]{1,0:T(8,128)S(1)} %get-tuple-element.372.refs_0_), channel_id=1, source_target_pairs={{0,1},{1,0},{2,3},{3,2},{4,5},{5,4},{6,7},{7,6},{8,9},{9,8},{10,11... | collective-permute-start | bytes 73736 | tf_op jit(solution)/shard_map/ppermute | solution.py:839
  (107 other events, 863.3 us)
Sparse Core Ops, SparseCore 0:
  10.2 28.8 all-gather.4
  41.2 43.8 all-gather.6
  86.6 28.3 all-gather.8
  116.4 43.8 all-gather.10
  171.8 42.0 reduce-scatter.3
  220.2 25.2 reduce-scatter.5
  248.4 42.1 reduce-scatter.7
